TPU v7x, 32 devices: a whole 2x2x4 slice. The times are simulated.
32 devices in a mesh: seq: 8 (over y, x, core), head: 4 (over z).
Axes of the slice: x: 2, y: 2, z: 4, core: 2. Of those that a mesh axis runs over, the one named last changes fastest.
Arguments:
- tokens: bfloat16 [2, 4096, 2048], P(None, 'seq'), may hold values from -6 to 6
- gain_attn: float32 [2048], replicated, may hold values from 0.5 to 1.5
- w_query: bfloat16 [2048, 2048], P(None, 'head'), may hold values from -0.125 to 0.125
- w_key: bfloat16 [2048, 2048], P(None, 'head'), may hold values from -0.125 to 0.125
- w_value: bfloat16 [2048, 2048], P(None, 'head'), may hold values from -0.125 to 0.125
- w_forget: bfloat16 [2048, 256], P(None, 'head'), may hold values from -0.0625 to 0.0625
- forget_bias: float32 [256], P('head')
- w_out: bfloat16 [2048, 2048], P('head'), may hold values from -8 to 8
- gain_ffn: float32 [2048], replicated, may hold values from 0.5 to 1.5
- w_gate: bfloat16 [2048, 5632], P('seq', 'head'), may hold values from -0.125 to 0.125
- w_up: bfloat16 [2048, 5632], P('seq', 'head'), may hold values from -0.125 to 0.125
- w_down: bfloat16 [5632, 2048], P('head', 'seq'), may hold values from -0.078125 to 0.078125
- cotangent: bfloat16 [2, 4096, 2048], P(None, 'seq'), may hold values from -6 to 6
Outputs:
- out: bfloat16 [2, 4096, 2048], P(None, 'seq')
- in_grad: float32 [2, 4096, 2048], P(None, 'seq')
- grad_gain_attn: float32 [2048], P('seq')
- grad_w_query: float32 [2048, 2048], P('seq', 'head')
- grad_w_key: float32 [2048, 2048], P('seq', 'head')
- grad_w_value: float32 [2048, 2048], P('seq', 'head')
- grad_w_forget: float32 [2048, 256], P('seq', 'head')
- grad_forget_bias: float32 [256], P('head')
- grad_w_out: float32 [2048, 2048], P('head', 'seq')
- grad_gain_ffn: float32 [2048], P('seq')
- grad_w_gate: float32 [2048, 5632], P('seq', 'head')
- grad_w_up: float32 [2048, 5632], P('seq', 'head')
- grad_w_down: float32 [5632, 2048], P('head', 'seq')
All inputs are finite; a program needn't handle non-finite values.
Results may differ from a plain program's by a relative error of at most 0.025.
Values may be sent and summed in bfloat16 or wider, within the bound.
No kernel may reach another device: no remote copies, remote signals or barrier semaphores. Data moves between devices by JAX's collectives and lax.ppermute only.
A program may use at most 320 MiB of HBM per device.

v0:
```python
import jax
import jax.numpy as jnp
from jax import lax
from jax.sharding import PartitionSpec as P

DH = 512
BLK = 128


norm_eps = 1e-06
rate_bound = 0.5
highest = lax.Precision.HIGHEST


def prefix(shard, axis, join, neutral):
    place = lax.axis_index(axis)
    gathered = jax.tree.map(
        lambda a, kind: lax.all_gather(a.astype(kind), axis), shard, (jnp.bfloat16, jnp.bfloat16)
    )
    state = jax.tree.map(lambda a, e: jnp.zeros_like(a) + jnp.asarray(e, a.dtype), shard, neutral)

    def one(hop, state):
        return join(
            state,
            jax.tree.map(
                lambda a, own: lax.dynamic_index_in_dim(a, hop, 0, False).astype(own.dtype),
                gathered,
                shard,
            ),
        )

    return lax.fori_loop(0, place, one, state)


def shortened(shard):

    def short(part):
        return part.astype(jnp.bfloat16) if part.dtype == jnp.float32 else part

    return jax.tree.map(short, shard)


def spread(value, axis, source):
    kept = jnp.where(lax.axis_index(axis) == source, value, 0).astype(value.dtype)
    return lax.psum(kept, axis)


def entering_2(shard, axis, combine, identity):
    peers, mine = (lax.axis_size(axis), lax.axis_index(axis))
    everything = jax.tree.map(
        lambda part, kind: lax.all_gather(part.astype(kind), axis),
        shard,
        jax.tree.map(lambda a: jnp.bfloat16 if a.dtype == jnp.float32 else a.dtype, shard),
    )
    start = jax.tree.map(
        lambda part, zero: jnp.broadcast_to(jnp.asarray(zero, part.dtype), part.shape),
        shard,
        identity,
    )

    def hop(k, before):
        at = peers - 1 - k
        reached = at > mine
        new = combine(
            before, jax.tree.map(lambda part, own: part[at].astype(own.dtype), everything, shard)
        )
        return jax.tree.map(lambda a, b: jnp.where(reached, a, b), new, before)

    return lax.fori_loop(0, peers, hop, start)


def product(left, right):
    return jnp.dot(left, right, preferred_element_type=jnp.float32)


def precise(left, right):
    return jnp.dot(left, right, precision=highest)


def norm_scale(token_rows):
    return lax.rsqrt(jnp.mean(token_rows * token_rows, axis=-1, keepdims=True) + norm_eps)


def norm_back(grad_normed, token_rows, norm_factor, gain):
    weighted = grad_normed * gain
    cubed = norm_factor * norm_factor * norm_factor
    return norm_factor * weighted - token_rows * cubed * jnp.mean(
        weighted * token_rows, axis=-1, keepdims=True
    )


def block_core(query_rows, key_rows, value_rows, log_keep, slot_state):
    block_rows = query_rows.shape[0]
    head_width = query_rows.shape[1]
    causal = jnp.arange(block_rows)[:, None] >= jnp.arange(block_rows)[None, :]
    cumulative = jnp.cumsum(log_keep, axis=0)
    growth = jnp.exp(cumulative)
    inflow = jnp.exp(-cumulative) * -jnp.expm1(log_keep)
    pair_scores = jnp.where(causal, precise(query_rows, key_rows.T), 0.0)
    scores = growth * (
        precise(query_rows, slot_state[:, :head_width].T) + precise(pair_scores, inflow)
    )
    slot_probs = jax.nn.softmax(scores, axis=-1)
    weights = slot_probs * growth
    mixing = jnp.where(causal, precise(weights, inflow.T), 0.0)
    output = precise(weights, slot_state[:, head_width:]) + precise(mixing, value_rows)
    joined = jnp.concatenate([key_rows, value_rows], 1)
    new_state = jnp.exp(cumulative[-1])[:, None] * (slot_state + precise(inflow.T, joined))
    return (output, new_state)


def block_state(key_rows, value_rows, log_keep, slot_state):
    cumulative = jnp.cumsum(log_keep, axis=0)
    inflow = jnp.exp(-cumulative) * -jnp.expm1(log_keep)
    joined = jnp.concatenate([key_rows, value_rows], 1)
    return jnp.exp(cumulative[-1])[:, None] * (slot_state + precise(inflow.T, joined))


def split_blocks(member):
    return member.reshape(member.shape[0] // BLK, BLK, member.shape[1])


def span_readout(query_rows, key_rows, value_rows, log_keep, entering):

    def advance(slot_state, pieces):
        output, new_state = block_core(pieces[0], pieces[1], pieces[2], pieces[3], slot_state)
        return (new_state, output)

    pieces_all = (
        split_blocks(query_rows),
        split_blocks(key_rows),
        split_blocks(value_rows),
        split_blocks(log_keep),
    )
    unused, outputs = lax.scan(advance, entering, pieces_all)
    return outputs.reshape(query_rows.shape[0], query_rows.shape[1])


def span_transform(key_rows, value_rows, log_keep):

    def advance(slot_state, pieces):
        return (block_state(pieces[0], pieces[1], pieces[2], slot_state), 0.0)

    start_state = jnp.zeros((log_keep.shape[1], 2 * key_rows.shape[1]), jnp.float32)
    final_state, unused = lax.scan(
        advance,
        start_state,
        (split_blocks(key_rows), split_blocks(value_rows), split_blocks(log_keep)),
    )
    return (jnp.exp(jnp.sum(log_keep, axis=0)), final_state)


def combine_maps(earlier, later):
    return (earlier[0] * later[0], later[1] + later[0][..., None] * earlier[1])


def head_inputs(query_rows, key_rows, value_rows, log_keep):
    return (
        query_rows.astype(jnp.float32),
        key_rows.astype(jnp.float32),
        value_rows.astype(jnp.float32),
        log_keep,
    )


def ffn_forward(hidden, gain_ffn, full_weights, hidden_units):
    factor_ffn = norm_scale(hidden)
    normed_ffn = (hidden * factor_ffn * gain_ffn).astype(jnp.bfloat16)
    gate_up = product(normed_ffn, full_weights[:, : 2 * hidden_units])
    gate_rows = gate_up[:, :hidden_units]
    act_rows = (jax.nn.silu(gate_rows) * gate_up[:, hidden_units:]).astype(jnp.bfloat16)
    branch_part = jnp.einsum(
        "rf,df->rd",
        act_rows,
        full_weights[:, 2 * hidden_units :],
        preferred_element_type=jnp.float32,
    )
    return (branch_part, normed_ffn, factor_ffn, gate_up, act_rows)


def ffn_backward(grad_out, gate_up, full_weights, hidden_units):
    grad_act = product(grad_out, full_weights[:, 2 * hidden_units :])
    gate_rows = gate_up[:, :hidden_units]
    up_rows = gate_up[:, hidden_units:]
    gate_sigmoid = jax.nn.sigmoid(gate_rows)
    grad_gate = grad_act * up_rows * gate_sigmoid * (1.0 + gate_rows * (1.0 - gate_sigmoid))
    grad_up = grad_act * gate_rows * gate_sigmoid
    grad_pair = jnp.concatenate([grad_gate, grad_up], 1).astype(jnp.bfloat16)
    grad_normed_part = jnp.einsum(
        "rf,df->rd",
        grad_pair,
        full_weights[:, : 2 * hidden_units],
        preferred_element_type=jnp.float32,
    )
    return (grad_pair, grad_normed_part)


def weight_terms(entries):
    term_total = None
    for normed_ffn, grad_pair, grad_out, act_rows in entries:
        row_term = jnp.concatenate(
            [
                jnp.einsum("rc,rf->cf", normed_ffn, grad_pair, preferred_element_type=jnp.float32),
                jnp.einsum("rc,rf->cf", grad_out, act_rows, preferred_element_type=jnp.float32),
            ],
            1,
        )
        term_total = row_term
    return term_total


def term_maker(entries):
    return weight_terms(entries)


def on_device(
    tokens,
    gain_attn,
    w_query,
    w_key,
    w_value,
    w_forget,
    forget_bias,
    w_out,
    gain_ffn,
    w_gate,
    w_up,
    w_down,
    cotangent,
):
    micro_count = tokens.shape[0]
    model_width = tokens.shape[2]
    head_width = DH
    local_heads = w_query.shape[1] // head_width
    slot_count = w_forget.shape[1] // local_heads
    hidden_units = w_gate.shape[1]
    width_rows = w_gate.shape[0]
    seq_count = lax.axis_size("seq")
    incoming = jnp.zeros((local_heads, slot_count, 2 * head_width), jnp.float32)
    saved_attn = []
    saved_hidden = []
    for micro_pos in range(micro_count):
        token_rows = tokens[micro_pos].astype(jnp.float32)
        norm_factor = norm_scale(token_rows)
        normed = (token_rows * norm_factor * gain_attn).astype(jnp.bfloat16)
        query_rows = product(normed, w_query).astype(jnp.bfloat16)
        key_rows = product(normed, w_key).astype(jnp.bfloat16)
        value_rows = product(normed, w_value).astype(jnp.bfloat16)
        forget_logit = product(normed, w_forget) + forget_bias
        log_keep = -rate_bound * jax.nn.sigmoid(-forget_logit)
        head_parts = [head_inputs(query_rows, key_rows, value_rows, log_keep)]
        span_maps = [
            span_transform(head_part[1], head_part[2], head_part[3]) for head_part in head_parts
        ]
        span_decay = jnp.stack([span_map[0] for span_map in span_maps])
        local_state = jnp.stack([span_map[1] for span_map in span_maps])
        prefix_decay, prefix_state = prefix(
            (span_decay, local_state),
            "seq",
            combine_maps,
            (jnp.ones_like(span_decay), jnp.zeros_like(local_state)),
        )
        entering = prefix_decay[..., None] * incoming + prefix_state
        if micro_pos + 1 < micro_count:
            incoming = spread(
                shortened(span_decay[..., None] * entering + local_state), "seq", seq_count - 1
            )
        head_outputs = [
            span_readout(head_part[0], head_part[1], head_part[2], head_part[3], entering[head_pos])
            for head_pos, head_part in enumerate(head_parts)
        ]
        mixed_heads = head_outputs[0].astype(jnp.bfloat16)
        attended = lax.psum(product(mixed_heads, w_out).astype(jnp.bfloat16), "head").astype(
            jnp.float32
        )
        saved_hidden.append(token_rows + attended)
        saved_attn.append(
            (
                token_rows,
                norm_factor,
                normed,
                head_parts,
                forget_logit,
                span_decay,
                entering,
                mixed_heads,
            )
        )
    stacked = jnp.concatenate([w_gate, w_up, w_down.T], 1)

    def fetch_weights():
        return lax.all_gather(stacked, "seq", axis=0, tiled=True)

    out_rows = []
    saved_ffn = []
    for micro_pos in range(micro_count):
        hidden = saved_hidden[micro_pos]
        branch_part, normed_ffn, factor_ffn, gate_up, act_rows = ffn_forward(
            hidden, gain_ffn, fetch_weights(), hidden_units
        )
        ffn_rows = lax.psum(branch_part.astype(jnp.bfloat16), "head").astype(jnp.float32)
        out_rows.append((hidden + ffn_rows).astype(jnp.bfloat16))
        saved_ffn.append((normed_ffn, factor_ffn, gate_up, act_rows))
    grad_ffn_w = jnp.zeros((width_rows, 3 * hidden_units), jnp.float32)
    grad_gain_ffn = jnp.zeros((model_width,), jnp.float32)
    grad_hidden_all = []
    ffn_entries = []
    for micro_pos in range(micro_count):
        grad_out = cotangent[micro_pos]
        hidden = saved_hidden[micro_pos]
        normed_ffn, factor_ffn, gate_up, act_rows = saved_ffn[micro_pos]
        grad_pair, grad_normed_part = ffn_backward(grad_out, gate_up, fetch_weights(), hidden_units)
        grad_normed = lax.psum(grad_normed_part.astype(jnp.bfloat16), "head").astype(jnp.float32)
        grad_gain_ffn = grad_gain_ffn + jnp.sum(grad_normed * hidden * factor_ffn, axis=0)
        grad_hidden_all.append(
            grad_out.astype(jnp.float32) + norm_back(grad_normed, hidden, factor_ffn, gain_ffn)
        )
        ffn_entry = (normed_ffn, grad_pair, grad_out, act_rows)
        ffn_entries.append(ffn_entry)
        grad_ffn_w = grad_ffn_w + lax.psum_scatter(
            term_maker([ffn_entry]).astype(jnp.bfloat16), "seq", scatter_dimension=0, tiled=True
        ).astype(jnp.float32)
    grad_query_w = jnp.zeros(w_query.shape, jnp.float32)
    grad_key_w = jnp.zeros(w_key.shape, jnp.float32)
    grad_value_w = jnp.zeros(w_value.shape, jnp.float32)
    grad_forget_w = jnp.zeros(w_forget.shape, jnp.float32)
    grad_out_t = jnp.zeros((model_width, w_out.shape[0]), jnp.float32)
    grad_bias = jnp.zeros(forget_bias.shape, jnp.float32)
    grad_gain_attn = jnp.zeros((model_width,), jnp.float32)
    in_grads = [None] * micro_count
    outgoing = jnp.zeros_like(incoming)
    for micro_pos in reversed(range(micro_count)):
        (
            token_rows,
            norm_factor,
            normed,
            head_parts,
            forget_logit,
            span_decay,
            entering,
            mixed_heads,
        ) = saved_attn[micro_pos]
        grad_att = grad_hidden_all[micro_pos].astype(jnp.bfloat16)
        grad_out_t = grad_out_t + jnp.einsum(
            "rd,rk->dk", grad_att, mixed_heads, preferred_element_type=jnp.float32
        )
        grad_mixed = jnp.einsum("rd,kd->rk", grad_att, w_out, preferred_element_type=jnp.float32)
        read_grads = []
        for head_pos, head_part in enumerate(head_parts):
            unused, pull_read = jax.vjp(
                span_readout,
                head_part[0],
                head_part[1],
                head_part[2],
                head_part[3],
                entering[head_pos],
            )
            read_grads.append(pull_read(grad_mixed))
        local_grad = jnp.stack([read_grad[4] for read_grad in read_grads])
        suffix_decay, suffix_state = entering_2(
            (span_decay, local_grad),
            "seq",
            combine_maps,
            (jnp.ones_like(span_decay), jnp.zeros_like(local_grad)),
        )
        leaving_grad = suffix_decay[..., None] * outgoing + suffix_state
        if micro_pos > 0:
            outgoing = spread(
                shortened(local_grad + span_decay[..., None] * leaving_grad), "seq", 0
            )
        query_grads = []
        key_grads = []
        value_grads = []
        keep_grads = []
        for head_pos, head_part in enumerate(head_parts):
            unused, pull_map = jax.vjp(span_transform, head_part[1], head_part[2], head_part[3])
            map_grads = pull_map(
                (
                    jnp.sum(leaving_grad[head_pos] * entering[head_pos], axis=-1),
                    leaving_grad[head_pos],
                )
            )
            read_grad = read_grads[head_pos]
            query_grads.append(read_grad[0])
            key_grads.append(read_grad[1] + map_grads[0])
            value_grads.append(read_grad[2] + map_grads[1])
            keep_grads.append(read_grad[3] + map_grads[2])
        grad_query = query_grads[0].astype(jnp.bfloat16)
        grad_key = key_grads[0].astype(jnp.bfloat16)
        grad_value = value_grads[0].astype(jnp.bfloat16)
        forget_rate = jax.nn.sigmoid(-forget_logit)
        grad_logit = (keep_grads[0] * rate_bound * forget_rate * (1.0 - forget_rate)).astype(
            jnp.bfloat16
        )
        grad_query_w = grad_query_w + jnp.einsum(
            "rd,rk->dk", normed, grad_query, preferred_element_type=jnp.float32
        )
        grad_key_w = grad_key_w + jnp.einsum(
            "rd,rk->dk", normed, grad_key, preferred_element_type=jnp.float32
        )
        grad_value_w = grad_value_w + jnp.einsum(
            "rd,rk->dk", normed, grad_value, preferred_element_type=jnp.float32
        )
        grad_forget_w = grad_forget_w + jnp.einsum(
            "rd,rk->dk", normed, grad_logit, preferred_element_type=jnp.float32
        )
        grad_bias = grad_bias + jnp.sum(grad_logit.astype(jnp.float32), axis=0)
        grad_normed_part = jnp.einsum(
            "rk,dk->rd", grad_query, w_query, preferred_element_type=jnp.float32
        )
        grad_normed_part = grad_normed_part + jnp.einsum(
            "rk,dk->rd", grad_key, w_key, preferred_element_type=jnp.float32
        )
        grad_normed_part = grad_normed_part + jnp.einsum(
            "rk,dk->rd", grad_value, w_value, preferred_element_type=jnp.float32
        )
        grad_normed_part = grad_normed_part + jnp.einsum(
            "rk,dk->rd", grad_logit, w_forget, preferred_element_type=jnp.float32
        )
        grad_normed = lax.psum(grad_normed_part.astype(jnp.bfloat16), "head").astype(jnp.float32)
        grad_gain_attn = grad_gain_attn + jnp.sum(grad_normed * token_rows * norm_factor, axis=0)
        in_grads[micro_pos] = grad_hidden_all[micro_pos] + norm_back(
            grad_normed, token_rows, norm_factor, gain_attn
        )
    shares = (
        lax.psum_scatter(
            grad_query_w.astype(jnp.bfloat16), "seq", scatter_dimension=0, tiled=True
        ).astype(jnp.float32),
        lax.psum_scatter(
            grad_key_w.astype(jnp.bfloat16), "seq", scatter_dimension=0, tiled=True
        ).astype(jnp.float32),
        lax.psum_scatter(
            grad_value_w.astype(jnp.bfloat16), "seq", scatter_dimension=0, tiled=True
        ).astype(jnp.float32),
        lax.psum_scatter(
            grad_forget_w.astype(jnp.bfloat16), "seq", scatter_dimension=0, tiled=True
        ).astype(jnp.float32),
        lax.psum_scatter(
            grad_out_t.astype(jnp.bfloat16), "seq", scatter_dimension=0, tiled=True
        ).astype(jnp.float32),
        lax.psum_scatter(
            grad_gain_attn.astype(jnp.bfloat16), "seq", scatter_dimension=0, tiled=True
        ).astype(jnp.float32),
        lax.psum_scatter(
            grad_gain_ffn.astype(jnp.bfloat16), "seq", scatter_dimension=0, tiled=True
        ).astype(jnp.float32),
    )
    bias_total = lax.psum(grad_bias, "seq")
    return (
        jnp.stack(out_rows),
        jnp.stack(in_grads),
        shares[5],
        shares[0],
        shares[1],
        shares[2],
        shares[3],
        bias_total,
        shares[4].T,
        shares[6],
        grad_ffn_w[:, :hidden_units],
        grad_ffn_w[:, hidden_units : 2 * hidden_units],
        grad_ffn_w[:, 2 * hidden_units :].T,
    )


def solution(mesh):
    return jax.shard_map(
        on_device,
        mesh=mesh,
        in_specs=(
            P(None, "seq", None),
            P(),
            P(None, "head"),
            P(None, "head"),
            P(None, "head"),
            P(None, "head"),
            P("head"),
            P("head", None),
            P(),
            P("seq", "head"),
            P("seq", "head"),
            P("head", "seq"),
            P(None, "seq", None),
        ),
        out_specs=(
            P(None, "seq", None),
            P(None, "seq", None),
            P("seq"),
            P("seq", "head"),
            P("seq", "head"),
            P("seq", "head"),
            P("seq", "head"),
            P("head"),
            P("head", "seq"),
            P("seq"),
            P("seq", "head"),
            P("seq", "head"),
            P("head", "seq"),
        ),
        check_vma=False,
    )
```

profile of v0, /device:TPU:0, one launch (start us, length us, event | category | flops | bytes accessed | tf_op | source)
XLA Modules:
  0.0 1988.5 jit_solution(14475797748775304369)
XLA Ops:
  7.3 3.3 fusion.358
  11.2 3.8 broadcast_multiply_fusion.6
  15.8 3.7 convolution_convert_fusion.8
  22.0 21.5 %while.375 = (s32[]{:T(128)}, f32[64,1024]{1,0:T(8,128)}, f32[4,128,64]{2,1,0:T(8,128)}, f32[4,128,512]{2,1,0:T(8,128)}, f32[4,128,512]{2,1,0:T(8,128)S(1)}, /*index=5*/s32[]{:T(128)}, f32[]{:T(128)}, s32[]{:T(128)}) while((s32[]{:T(128)}, f32[64,1024]{1,0:T(8,128)}, f32[4,128,64]{2,1,0:T(8,128)}, f32[4,128,512]{2,1,0:T(8,128)}, ...), condition=%wide.region_19.20_spmd.clone, body=%wide.region_17.19_spmd.clone.sunk | while | flops 102055936 | bytes 2294643 | solution.py:145
  45.5 4.0 broadcast_multiply_fusion.7
  49.4 3.8 convolution_convert_fusion.11
  59.6 21.5 %while.374 = (s32[]{:T(128)}, f32[64,1024]{1,0:T(8,128)}, f32[4,128,64]{2,1,0:T(8,128)}, f32[4,128,512]{2,1,0:T(8,128)}, f32[4,128,512]{2,1,0:T(8,128)S(1)}, /*index=5*/s32[]{:T(128)}, f32[]{:T(128)}, s32[]{:T(128)}) while((s32[]{:T(128)}, f32[64,1024]{1,0:T(8,128)}, f32[4,128,64]{2,1,0:T(8,128)}, f32[4,128,512]{2,1,0:T(8,128)}, ...), condition=%wide.region_4.5_spmd.clone, body=%wide.region_2.0_spmd.clone.sunk | while | flops 102055936 | bytes 2294643 | solution.py:145
  87.5 4.5 convolution_convert_fusion.6
  96.6 15.2 all-reduce.13
  120.3 42.0 %while.367 = (s32[]{:T(128)}, f32[64,1024]{1,0:T(8,128)S(1)}, bf16[4,128,512]{2,1,0:T(8,128)(2,1)}, f32[4,128,64]{2,1,0:T(8,128)}, f32[4,128,512]{2,1,0:T(8,128)...) while((s32[]{:T(128)}, f32[64,1024]{1,0:T(8,128)S(1)}, ...), condition=%wide.region_11.12_spmd, body=%wide.region_7.11_spmd.sunk | while | flops 429416192 | bytes 9345453 | solution.py:135
  162.3 3.7 convolution_convert_fusion.5
  166.0 19.7 all-reduce.23.cloned.1.call-done
  187.4 46.3 %while.369 = (s32[]{:T(128)}, f32[64,1024]{1,0:T(8,128)S(1)}, bf16[4,128,512]{2,1,0:T(8,128)(2,1)}, f32[4,128,64]{2,1,0:T(8,128)}, f32[4,128,512]{2,1,0:T(8,128)...) while((s32[]{:T(128)}, f32[64,1024]{1,0:T(8,128)S(1)}, ...), condition=%wide.region_27.28_spmd, body=%wide.region_23.27_spmd.sunk | while | flops 429416192 | bytes 9345453 | solution.py:135
  233.8 3.6 convolution_convert_fusion.4
  242.0 3.5 pad_maximum_fusion.14
  253.0 61.9 %while.379 = (s32[]{:T(128)}, f32[64,1024]{1,0:T(8,128)}, f32[4,128,64]{1,2,0:T(8,128)}, f32[4,128,64]{1,2,0:T(8,128)}, f32[4,128,64]{1,2,0:T(8,128)}, /*index=5...) while((s32[]{:T(128)}, f32[64,1024]{1,0:T(8,128)}, ...), condition=%wide.region_72.73_spmd.clone, body=%wide.region_70.72_spmd.clone.sunk | while | flops 102219776 | bytes 4852431 | solution.py:145
  321.4 69.0 %while.378 = (s32[]{:T(128)}, f32[64,1024]{1,0:T(8,128)}, f32[4,128,64]{1,2,0:T(8,128)}, f32[4,128,64]{1,2,0:T(8,128)}, f32[4,128,64]{1,2,0:T(8,128)}, /*index=5...) while((s32[]{:T(128)}, f32[64,1024]{1,0:T(8,128)}, ...), condition=%wide.region_62.63_spmd.clone, body=%wide.region_60.62_spmd.clone.sunk | while | flops 102219776 | bytes 4852175 | solution.py:145
  405.7 155.4 %while.372 = (s32[]{:T(128)}, f32[64,1024]{1,0:T(8,128)}, f32[4,128,64]{1,2,0:T(8,128)}, f32[4,128,64]{1,2,0:T(8,128)}, f32[4,128,64]{1,2,0:T(8,128)}, /*index=5...) while((s32[]{:T(128)}, f32[64,1024]{1,0:T(8,128)}, ...), condition=%wide.region_37.38_spmd.clone.clone, body=%wide.region_33.37_spmd.clone.clone.sunk | while | flops 278462464 | bytes 9118837 | solution.py:135
  562.9 4.9 multiply_reduce_fusion.1
  569.1 13.4 fusion.318
  582.5 11.4 fusion.320
  593.9 11.5 multiply_convert_fusion.3
  605.4 9.4 multiply_convert_fusion.5
  614.8 9.1 fusion.393
  624.0 7.7 fusion.390
  647.5 157.7 %while.373 = (s32[]{:T(128)}, f32[64,1024]{1,0:T(8,128)}, f32[4,128,64]{1,2,0:T(8,128)}, f32[4,128,64]{1,2,0:T(8,128)}, f32[4,128,64]{1,2,0:T(8,128)}, /*index=5...) while((s32[]{:T(128)}, f32[64,1024]{1,0:T(8,128)}, ...), condition=%wide.region_51.52_spmd.clone.clone, body=%wide.region_47.51_spmd.clone.clone.sunk | while | flops 278462464 | bytes 9118837 | solution.py:135
  805.2 7.0 fusion.355
  813.5 6.7 fusion.352
  825.5 114.9 %while.381 = (s32[]{:T(128)}, f32[64,1024]{1,0:T(8,128)S(1)}, bf16[4,128,512]{2,1,0:T(8,128)(2,1)}, f32[4,128,512]{2,1,0:T(8,128)}, f32[4,128,512]{2,1,0:T(8,128...) while((s32[]{:T(128)}, f32[64,1024]{1,0:T(8,128)S(1)}, ...), condition=%wide.region_56.57_spmd.clone.clone, body=%wide.region_52.56_spmd.clone.clone.sunk | while | flops 857833472 | bytes 13290421 | solution.py:135
  941.2 4.6 fusion.426
  947.7 98.9 %while.380 = (s32[]{:T(128)}, f32[64,1024]{1,0:T(8,128)S(1)}, bf16[4,128,512]{2,1,0:T(8,128)(2,1)}, f32[4,128,512]{2,1,0:T(8,128)S(1)}, f32[4,128,512]{2,1,0:T(8...) while((s32[]{:T(128)}, f32[64,1024]{1,0:T(8,128)S(1)}, ...), condition=%wide.region_42.43_spmd.clone.clone, body=%wide.region_38.42_spmd.clone.clone.sunk | while | flops 857833472 | bytes 13290421 | solution.py:135
  1047.7 5.7 fusion.421
  1053.5 18.6 while.377
  1073.7 35.4 %while.371 = (s32[]{:T(128)}, f32[64,1024]{1,0:T(8,128)S(1)}, f32[4,128,512]{2,1,0:T(8,128)S(1)}, f32[4,128,512]{2,1,0:T(8,128)}, f32[4,128,64]{1,0,2:T(4,128)S(...) while((s32[]{:T(128)}, f32[64,1024]{1,0:T(8,128)S(1)}, ...), condition=%wide.region_76.77_spmd, body=%wide.region_73.76_spmd.sunk | while | flops 202629120 | bytes 4002513 | solution.py:145
  1109.2 18.6 while.376
  1129.5 3.1 fusion.462
  1132.6 48.5 %all-reduce.25.cloned.1.call-done = bf16[1,64,1024]{2,1,0:T(8,128)(2,1)} async-done(((bf16[1,64,1024]{2,1,0:T(8,128)(2,1)}), bf16[1,64,1024]{2,1,0:T(8,128)(2,1)}) %all-reduce.25.cloned.1.call-update) | async-done | bytes 131088 | tf_op jit(solution)/shard_map/psum | solution.py:45
  1183.6 35.4 %while.370 = (s32[]{:T(128)}, f32[64,1024]{1,0:T(8,128)S(1)}, f32[4,128,512]{2,1,0:T(8,128)S(1)}, f32[4,128,512]{2,1,0:T(8,128)}, f32[4,128,64]{1,0,2:T(4,128)S(...) while((s32[]{:T(128)}, f32[64,1024]{1,0:T(8,128)S(1)}, ...), condition=%wide.region_66.67_spmd, body=%wide.region_63.66_spmd.sunk | while | flops 202629120 | bytes 4002513 | solution.py:145
  1220.8 3.2 fusion.402
  1224.0 6.3 add_convert_fusion
  1230.5 3.2 fusion.455
  1233.7 2.9 add_convert_fusion.3
  1237.0 3.2 fusion.453
  1240.6 2.8 add_convert_fusion.2
  1244.0 7.9 fusion.399
  1251.9 7.4 fusion.396
  1259.3 3.3 fusion.481
  1265.2 2.9 add_convert_fusion.1
  1282.1 8.2 fusion.323
  1290.3 8.3 convolution_convert_fusion
  1298.6 9.7 pad_maximum_fusion.9
  1308.7 8.3 fusion.322
  1317.0 8.7 convolution_convert_fusion.1
  1325.7 9.8 pad_maximum_fusion.8
  1336.3 12.4 psum.87
  1353.9 37.4 %reduce-scatter.10.cloned.1.call-done = bf16[256,512]{1,0:T(8,128)(2,1)} async-done(((bf16[2048,512]{1,0:T(8,128)(2,1)}), bf16[256,512]{1,0:T(8,128)(2,1)}) %reduce-scatter.10.cloned.1.call-update) | async-done | bytes 262160 | tf_op jit(solution)/shard_map/reduce_scatter | solution.py:429
  1393.1 42.6 %reduce-scatter.12.cloned.1.call-done = bf16[256,512]{1,0:T(8,128)(2,1)} async-done(((bf16[2048,512]{1,0:T(8,128)(2,1)}), bf16[256,512]{1,0:T(8,128)(2,1)}) %reduce-scatter.12.cloned.1.call-update) | async-done | bytes 262160 | tf_op jit(solution)/shard_map/reduce_scatter | solution.py:432
  1437.5 294.1 %all-reduce.27.cloned.1.call-done = (bf16[512,2048]{1,0:T(8,128)(2,1)}, bf16[512,2048]{1,0:T(8,128)(2,1)}, bf16[512,2048]{1,0:T(8,128)(2,1)}, bf16[512,2048]{1,0:T(8,128)(2,1)}) async-done(((bf16[512,2048]{1,0:T(8,128)(2,1)}, bf16[512,2048]{1,0:T(8,128)(2,1)}, bf16[512,2048]{1,0:T(8,128)(2,1)}, bf16[512,2048]{1,0:T(8,128)(2,1)}), (bf16[512,2048]{1,0:T(8,128)(2,1)}, bf16[512,2048]{1,0:T(8,128)(2,1)}, ...) | async-done | bytes 8388624 | tf_op jit(solution)/shard_map/psum | solution.py:301
  1731.6 5.2 fusion.373
  1736.8 14.2 all-reduce.12
  1752.3 13.2 fusion.347
  1767.8 4.1 pad_maximum_fusion.10
  1771.9 81.2 %reduce-scatter.20.cloned.1.call-done = bf16[256,4224]{1,0:T(8,128)(2,1)} async-done(((bf16[2048,4224]{1,0:T(8,128)(2,1)}), bf16[256,4224]{1,0:T(8,128)(2,1)}) %reduce-scatter.20.cloned.1.call-update) | async-done | bytes 2162704 | tf_op jit(solution)/shard_map/reduce_scatter | solution.py:320
  1853.1 122.1 %reduce-scatter.18.cloned.1.call-done = bf16[256,4224]{1,0:T(8,128)(2,1)} async-done(((bf16[2048,4224]{1,0:T(8,128)(2,1)}), bf16[256,4224]{1,0:T(8,128)(2,1)}) %reduce-scatter.18.cloned.1.call-update) | async-done | bytes 2162704 | tf_op jit(solution)/shard_map/reduce_scatter | solution.py:320
  (1435 shorter events, 1033.6 us)
Async XLA Ops:
  7.2 155.1 %copy-start = (bf16[512,2048]{1,0:T(8,128)(2,1)S(1)}, bf16[512,2048]{1,0:T(8,128)(2,1)}, u32[]{:S(2)}) copy-start(bf16[512,2048]{1,0:T(8,128)(2,1)} %param.52) | copy-start | bytes 6291460
  7.2 108.1 %all-gather.16.cloned.1.call-start = ((), (), s32[]{:S(2)}) async-start(), calls=%async_computation.18 | async-start | bytes 1179648 | tf_op jit(solution)/shard_map/all_gather | solution.py:18
  11.1 76.4 %copy-start.94 = (f32[512]{0:T(512)}, f32[512]{0:T(512)S(1)}, u32[]{:S(2)}) copy-start(f32[512]{0:T(512)S(1)} %get-tuple-element.5386) | copy-start | bytes 6148
  11.2 80.9 %copy-start.96 = (f32[512]{0:T(512)}, f32[512]{0:T(512)S(1)}, u32[]{:S(2)}) copy-start(f32[512]{0:T(512)S(1)} %get-tuple-element.5399) | copy-start | bytes 6148
  43.6 9.7 copy-start.19
  45.4 70.1 %all-gather.14.cloned.1.call-start = ((), (), s32[]{:S(2)}) async-start(), calls=%async_computation.17 | async-start | bytes 1179648 | tf_op jit(solution)/shard_map/all_gather | solution.py:18
  81.1 10.9 copy-start.18
  82.9 102.8 %all-reduce.23.cloned.1.call-start = ((), (), s32[]{:S(2)}) async-start(), calls=%async_computation.8 | async-start | bytes 262144 | tf_op jit(solution)/shard_map/psum | solution.py:45
  119.3 443.7 %all-reduce.31.cloned.1.call-start = ((), (), s32[]{:S(2)}) async-start(), calls=%async_computation.23 | async-start | bytes 8388608 | tf_op jit(solution)/shard_map/psum | solution.py:273
  162.3 23.4 %copy-start.34 = (f32[1,64,1024]{2,1,0:T(8,128)S(1)}, f32[1,64,1024]{2,1,0:T(8,128)}, u32[]{:S(2)}) copy-start(f32[1,64,1024]{2,1,0:T(8,128)} %copy-done.33) | copy-start | bytes 786436
  237.4 331.6 %all-gather.12.cloned.1.call-start = ((), (), s32[]{:S(2)}) async-start(), calls=%async_computation.7 | async-start | bytes 19464192 | tf_op jit(solution)/shard_map/all_gather | solution.py:292
  245.4 559.7 %all-reduce.29.cloned.1.call-start = ((), (), s32[]{:S(2)}) async-start(), calls=%async_computation.22 | async-start | bytes 8388608 | tf_op jit(solution)/shard_map/psum | solution.py:313
  568.4 14.0 copy-start.90
  569.0 13.4 copy-start.87
  569.1 13.4 copy-start.5
  569.1 13.4 copy-start.24
  593.9 11.5 copy-start.59
  593.9 20.9 %slice-start = ((s8[17301504]{0:T(1024)(128)(4,1)}), s8[4194304]{0:T(1024)(128)(4,1)S(1)}, s32[]{:S(2)}) async-start(s8[17301504]{0:T(1024)(128)(4,1)} %bitcast.1432), calls=%async_computation.24 | async-start | bytes 8388608
  593.9 20.9 %slice-start.1 = ((s8[17301504]{0:T(1024)(128)(4,1)}), s8[4194304]{0:T(1024)(128)(4,1)S(1)}, s32[]{:S(2)}) async-start(s8[17301504]{0:T(1024)(128)(4,1)} %bitcast.1432), calls=%async_computation.25 | async-start | bytes 8388608
  593.9 20.9 %slice-start.2 = ((s8[17301504]{0:T(1024)(128)(4,1)}), s8[4194304]{0:T(1024)(128)(4,1)S(1)}, s32[]{:S(2)}) async-start(s8[17301504]{0:T(1024)(128)(4,1)} %bitcast.1432), calls=%async_computation.26 | async-start | bytes 8388608
  605.4 9.4 slice-start.3
  605.4 9.5 slice-start.4
  614.8 9.2 copy-start.118
  614.8 9.1 copy-start.119
  631.7 15.8 copy-start.14
  631.7 421.8 %all-gather.20.cloned.1.call-start = ((), (), s32[]{:S(2)}) async-start(), calls=%async_computation.20 | async-start | bytes 1179648 | tf_op jit(solution)/shard_map/all_gather | solution.py:51
  826.4 14.1 copy-start.30
  855.0 14.1 copy-start.30
  883.7 14.1 copy-start.30
  912.4 14.1 copy-start.30
  941.2 168.0 %all-gather.18.cloned.1.call-start = ((), (), s32[]{:S(2)}) async-start(), calls=%async_computation.19 | async-start | bytes 1179648 | tf_op jit(solution)/shard_map/all_gather | solution.py:51
  948.5 13.5 copy-start.64
  973.3 13.4 copy-start.64
  998.0 13.4 copy-start.64
  1022.6 13.4 copy-start.64
  1047.7 24.4 %copy-start.58 = (f32[64,1024]{1,0:T(8,128)S(1)}, f32[64,1024]{1,0:T(8,128)}, u32[]{:S(2)}) copy-start(f32[64,1024]{1,0:T(8,128)} %copy-done.57) | copy-start | bytes 786436
  1053.4 20.3 %copy-start.72 = (f32[4,128,64]{1,2,0:T(8,128)S(1)}, f32[4,128,64]{1,2,0:T(8,128)}, u32[]{:S(2)}) copy-start(f32[4,128,64]{1,2,0:T(8,128)} %get-tuple-element.7368) | copy-start | bytes 393220
  1053.4 127.7 %all-reduce.25.cloned.1.call-start = ((), (), s32[]{:S(2)}) async-start(), calls=%async_computation.9 | async-start | bytes 262144 | tf_op jit(solution)/shard_map/psum | solution.py:45
  1073.7 35.5 %copy-start.116 = (f32[64]{0:T(128)S(1)}, f32[64]{0:T(128)}, u32[]{:S(2)}) copy-start(f32[64]{0:T(128)} %get-tuple-element.5382) | copy-start | bytes 772
  1073.7 35.5 %copy-start.36 = (f32[1,64,1024]{2,1,0:T(8,128)S(1)}, f32[1,64,1024]{2,1,0:T(8,128)}, u32[]{:S(2)}) copy-start(f32[1,64,1024]{2,1,0:T(8,128)} %custom-call.3) | copy-start | bytes 786436
  1073.7 35.5 %copy-start.93 = (f32[1,64]{1,0:T(1,128)S(1)}, f32[1,64]{1,0:T(1,128)}, u32[]{:S(2)}) copy-start(f32[1,64]{1,0:T(1,128)} %custom-call.2) | copy-start | bytes 772
  1073.7 54.2 %copy-start.17 = (f32[64,1024]{1,0:T(8,128)S(1)}, f32[64,1024]{1,0:T(8,128)}, u32[]{:S(2)}) copy-start(f32[64,1024]{1,0:T(8,128)} %copy-done.16) | copy-start | bytes 786436
  1073.7 54.2 %copy-start.111 = (f32[64]{0:T(128)S(1)}, f32[64]{0:T(128)}, u32[]{:S(2)}) copy-start(f32[64]{0:T(128)} %get-tuple-element.5393) | copy-start | bytes 772
  1109.1 19.6 copy-start.76
  1109.1 19.6 copy-start.78
  1109.1 20.3 %copy-start.84 = (f32[2048]{0:T(1024)S(1)}, f32[2048]{0:T(1024)}, u32[]{:S(2)}) copy-start(f32[2048]{0:T(1024)} %param.46) | copy-start | bytes 24580
  1109.1 20.3 %copy-start.95 = (f32[512]{0:T(512)S(1)}, f32[512]{0:T(512)}, u32[]{:S(2)}) copy-start(f32[512]{0:T(512)} %copy-done.94) | copy-start | bytes 6148
  1109.2 71.9 %copy-start.29 = (f32[1,64,1024]{2,1,0:T(8,128)S(1)}, f32[1,64,1024]{2,1,0:T(8,128)}, u32[]{:S(2)}) copy-start(f32[1,64,1024]{2,1,0:T(8,128)} %copy-done.28) | copy-start | bytes 786436
  1109.2 71.9 %copy-start.105 = (f32[64]{0:T(128)S(1)}, f32[64]{0:T(128)}, u32[]{:S(2)}) copy-start(f32[64]{0:T(128)} %copy-done.104) | copy-start | bytes 772
  1128.6 54.9 %copy-start.73 = (f32[4,128,64]{1,2,0:T(8,128)S(1)}, f32[4,128,64]{1,2,0:T(8,128)}, u32[]{:S(2)}) copy-start(f32[4,128,64]{1,2,0:T(8,128)} %get-tuple-element.7689) | copy-start | bytes 393220
  1128.7 220.1 %reduce-scatter.14.cloned.1.call-start = ((), (), s32[]{:S(2)}) async-start(), calls=%async_computation.13 | async-start | bytes 294912 | tf_op jit(solution)/shard_map/reduce_scatter | solution.py:435
  1183.5 35.5 %copy-start.114 = (f32[64]{0:T(128)S(1)}, f32[64]{0:T(128)}, u32[]{:S(2)}) copy-start(f32[64]{0:T(128)} %get-tuple-element.5380) | copy-start | bytes 772
  1183.5 35.5 %copy-start.77 = (f32[4,128,64]{1,0,2:T(4,128)S(1)}, f32[4,128,64]{1,0,2:T(4,128)}, u32[]{:S(2)}) copy-start(f32[4,128,64]{1,0,2:T(4,128)} %get-tuple-element.3366) | copy-start | bytes 393220
  1183.5 37.3 %copy-start.97 = (f32[512]{0:T(512)S(1)}, f32[512]{0:T(512)}, u32[]{:S(2)}) copy-start(f32[512]{0:T(512)} %copy-done.96) | copy-start | bytes 6148
  1219.0 11.4 copy-start.54
  1224.0 126.1 %reduce-scatter.16.cloned.1.call-start = ((), (), s32[]{:S(2)}) async-start(), calls=%async_computation.14 | async-start | bytes 2359296 | tf_op jit(solution)/shard_map/reduce_scatter | solution.py:438
  1230.4 121.7 %reduce-scatter.8.cloned.1.call-start = ((), (), s32[]{:S(2)}) async-start(), calls=%async_computation.10 | async-start | bytes 2359296 | tf_op jit(solution)/shard_map/reduce_scatter | solution.py:426
  1236.6 154.7 %reduce-scatter.10.cloned.1.call-start = ((), (), s32[]{:S(2)}) async-start(), calls=%async_computation.11 | async-start | bytes 2359296 | tf_op jit(solution)/shard_map/reduce_scatter | solution.py:429
  1243.4 192.3 %reduce-scatter.12.cloned.1.call-start = ((), (), s32[]{:S(2)}) async-start(), calls=%async_computation.12 | async-start | bytes 2359296 | tf_op jit(solution)/shard_map/reduce_scatter | solution.py:432
  1268.1 463.5 %all-reduce.27.cloned.1.call-start = ((), (), s32[]{:S(2)}) async-start(), calls=%async_computation.21 | async-start | bytes 16777216 | tf_op jit(solution)/shard_map/psum | solution.py:301
  1281.8 571.3 %reduce-scatter.20.cloned.1.call-start = ((), (), s32[]{:S(2)}) async-start(), calls=%async_computation.16 | async-start | bytes 19464192 | tf_op jit(solution)/shard_map/reduce_scatter | solution.py:320
  1308.4 666.8 %reduce-scatter.18.cloned.1.call-start = ((), (), s32[]{:S(2)}) async-start(), calls=%async_computation.15 | async-start | bytes 19464192 | tf_op jit(solution)/shard_map/reduce_scatter | solution.py:320
  1731.6 20.7 %copy-start.102 = (f32[512]{0:T(512)S(1)}, f32[512]{0:T(512)}, u32[]{:S(2)}) copy-start(f32[512]{0:T(512)} %get-tuple-element.5385) | copy-start | bytes 6148
  1731.6 20.7 %copy-start.103 = (f32[512]{0:T(512)S(1)}, f32[512]{0:T(512)}, u32[]{:S(2)}) copy-start(f32[512]{0:T(512)} %get-tuple-element.5400) | copy-start | bytes 6148
  (109 other events, 446.2 us)
Sparse Core Ops, SparseCore 0:
  45.5 26.1 all-gather.15
  83.0 26.2 all-gather.13
  119.4 66.3 all-reduce.22
  237.5 154.7 all-reduce.30
  394.6 94.4 all-gather.11
  631.8 154.5 all-reduce.28
  941.3 22.7 all-gather.19
  1053.5 22.8 all-gather.17
  1128.8 52.2 all-reduce.24
  1224.1 32.9 reduce-scatter.13
  1260.8 41.1 reduce-scatter.15
  1305.1 41.2 reduce-scatter.7
  1350.1 41.2 reduce-scatter.9
  1394.5 41.1 reduce-scatter.11
  1438.7 292.8 all-reduce.26
  1735.5 117.5 reduce-scatter.19
  1856.6 118.5 reduce-scatter.17
where the time goes:
time: 2020 us; the launch traced here: 1990 us
  waiting for transfers between devices  646 us (32%)
  matrix products  534 us (26%)
  local copies, waits for them, and re-layouts  448 us (22%)
  other arithmetic  295 us (15%)
  blocking collectives  41.9 us (2%)
    dot_general x240, matrix products, precise(): return jnp.dot(left, right, precision=highest)  334 us
    psum x1, waiting for transfers between devices, on_device(): lax.psum(branch_part.astype(jnp.bfloat16), 'head').astype(jnp.float32)  294 us
    dynamic_update_slice x208, local copies, waits for them, and re-layouts, span_readout(): unused, outputs = lax.scan(advance, entering, pieces_all)  221 us
    reduce_scatter x2, waiting for transfers between devices, on_device(): lax.psum_scatter(term_maker([ffn_entry]).astype(jnp.bfloat16), 'seq', sca...  203 us
    dot_general x14, matrix products, product(): return jnp.dot(left, right, preferred_element_type=jnp.float32)  78.3 us
    psum x2, waiting for transfers between devices, spread(): return lax.psum(kept, axis)  68.2 us
    dynamic_update_slice x40, other arithmetic, span_readout(): unused, outputs = lax.scan(advance, entering, pieces_all)  57.2 us
    squeeze x48, local copies, waits for them, and re-layouts, span_transform(): lax.scan(advance, start_state, (split_blocks(key_rows), split_blocks(valu...  56.5 us
  transfers between devices with their start and end apart: 17, of which 7 were waited for; matrix products, arithmetic and copies ran while one was open for 46% of the time, Pallas kernels for 0%

commit v1 on v0

v1 whole, which is shorter than its diff:
```python
import functools

import jax
import jax.numpy as jnp
from jax import lax
from jax.experimental import pallas as pl
from jax.experimental.pallas import tpu as pltpu
from jax.sharding import PartitionSpec as P

CHUNK = 128
TILE = 256
EPS = 1e-06
RATE = 0.5
MIB = 2**20
f32 = jnp.float32
bf16 = jnp.bfloat16
highest = lax.Precision.HIGHEST


def nn(a, b):
    return lax.dot_general(a, b, (((1,), (0,)), ((), ())), preferred_element_type=f32)


def nt(a, b):
    return lax.dot_general(a, b, (((1,), (1,)), ((), ())), preferred_element_type=f32)


def tn(a, b):
    return lax.dot_general(a, b, (((0,), (0,)), ((), ())), preferred_element_type=f32)


def exact(a, b, dims):
    return lax.dot_general(a, b, (dims, ((), ())), precision=highest, preferred_element_type=f32)


def halves(a):
    high = a.astype(bf16)
    return high, (a - high.astype(f32)).astype(bf16)


def call(name, kernel, grid, in_specs, out_specs, out_shape, scratch=(), vmem=48, cost=None):
    return pl.pallas_call(
        kernel,
        name=name,
        grid=grid,
        in_specs=in_specs,
        out_specs=out_specs,
        out_shape=out_shape,
        scratch_shapes=scratch,
        compiler_params=pltpu.CompilerParams(
            dimension_semantics=("arbitrary",) * len(grid), vmem_limit_bytes=vmem * MIB
        ),
        cost_estimate=cost,
    )


def cost(flops, data):
    return pl.CostEstimate(flops=int(flops), bytes_accessed=int(data), transcendentals=0)


def fixed(shape):
    zeros = (0,) * len(shape)
    return pl.BlockSpec(shape, lambda *_: zeros, pipeline_mode=pl.Buffered(1))


def shaped(shape, dtype):
    return jax.ShapeDtypeStruct(shape, dtype)


def triangle(lower):
    r = lax.broadcasted_iota(jnp.int32, (CHUNK, CHUNK), 0)
    c = lax.broadcasted_iota(jnp.int32, (CHUNK, CHUNK), 1)
    return r >= c if lower else r <= c


def gates(z):
    la = -RATE * lax.logistic(-z)
    y = -la
    taken = jnp.ones_like(y)
    for n in range(9, 1, -1):
        taken = 1.0 - y * (1.0 / n) * taken
    taken = y * taken
    cum = exact(triangle(True).astype(f32), la, ((1,), (0,)))
    total = exact(la, jnp.ones((CHUNK, 128), f32), ((0,), (0,)))
    return la, cum, jnp.exp(-cum) * taken, total


def project_kernel(per_part, x_ref, gain_ref, wq_ref, wk_ref, wv_ref, wf_ref, bias_ref,
                   xn_ref, q_ref, k_ref, v_ref, z_ref, s_ref, d_ref, state, decay):
    @pl.when(lax.rem(pl.program_id(0), per_part) == 0)
    def _():
        state[...] = jnp.zeros_like(state)
        decay[...] = jnp.zeros_like(decay)

    x = x_ref[...].astype(f32)
    r1 = lax.rsqrt(jnp.mean(x * x, axis=-1, keepdims=True) + EPS)
    xn = (x * r1 * gain_ref[...]).astype(bf16)
    xn_ref[...] = xn
    q_ref[...] = nn(xn, wq_ref[...]).astype(bf16)
    k_ref[...] = nn(xn, wk_ref[...]).astype(bf16)
    v_ref[...] = nn(xn, wv_ref[...]).astype(bf16)
    z_ref[...] = nn(xn, wf_ref[...]) + bias_ref[...]
    width = k_ref.shape[1]
    for c in range(x_ref.shape[0] // CHUNK):
        rows = pl.ds(c * CHUNK, CHUNK)
        _, _, inflow, total = gates(z_ref[rows, :])
        spread = inflow.astype(bf16)
        keep = jnp.exp(total[:, :1])
        state[:, :width] = keep * (state[:, :width] + tn(spread, k_ref[rows, :]))
        state[:, width:] = keep * (state[:, width:] + tn(spread, v_ref[rows, :]))
        decay[...] += total
    s_ref[0] = state[...]
    d_ref[0] = decay[...]


def read_kernel(per_part, q_ref, k_ref, v_ref, z_ref, e0_ref, o_ref, p_ref, sc_ref, e_ref, state):
    @pl.when(lax.rem(pl.program_id(0), per_part) == 0)
    def _():
        state[...] = e0_ref[0]

    width = q_ref.shape[1]
    lower = triangle(True)
    for c in range(q_ref.shape[0] // CHUNK):
        rows = pl.ds(c * CHUNK, CHUNK)
        q, k, v = q_ref[rows, :], k_ref[rows, :], v_ref[rows, :]
        _, cum, inflow, total = gates(z_ref[rows, :])
        growth = jnp.exp(cum)
        e_ref[c] = state[...]
        i_hi, i_lo = halves(inflow)
        a_hi, a_lo = halves(jnp.where(lower, nt(q, k), 0.0))
        e_hi, e_lo = halves(state[:, :width])
        scores = growth * (
            nt(q, e_hi) + nt(q, e_lo) + nn(a_hi, i_hi) + (nn(a_hi, i_lo) + nn(a_lo, i_hi))
        )
        top = jnp.exp(scores - jnp.max(scores, axis=-1, keepdims=True))
        p = top / jnp.sum(top, axis=-1, keepdims=True)
        w = (p * growth).astype(bf16)
        mixing = jnp.where(lower, nt(w, i_hi), 0.0).astype(bf16)
        o_ref[rows, :] = (nn(w, state[:, width:].astype(bf16)) + nn(mixing, v)).astype(bf16)
        p_ref[rows, :] = p
        sc_ref[rows, :] = scores
        keep = jnp.exp(total[:, :1])
        state[:, :width] = keep * (state[:, :width] + tn(i_hi, k))
        state[:, width:] = keep * (state[:, width:] + tn(i_hi, v))


def back_kernel(per_part, dhn_ref, hid_ref, cot_ref, gain_ref, wo_ref, q_ref, k_ref, v_ref, z_ref, p_ref, sc_ref, e_ref,
                dhid_ref, datt_ref, dq_ref, dkl_ref, dvl_ref, h_ref, x1_ref, g_ref, s_ref, gg_ref, state):
    step = pl.program_id(0)

    @pl.when(lax.rem(step, per_part) == 0)
    def _():
        state[...] = jnp.zeros_like(state)

    @pl.when(step == 0)
    def _():
        gg_ref[...] = jnp.zeros_like(gg_ref)

    hidden = hid_ref[...]
    dhn = dhn_ref[...].astype(f32)
    r2 = lax.rsqrt(jnp.mean(hidden * hidden, axis=-1, keepdims=True) + EPS)
    gg_ref[...] += jnp.sum((dhn * hidden * r2).reshape(-1, 8, hidden.shape[1]), axis=0)
    u2 = gain_ref[...] * dhn
    dhid = (
        cot_ref[...].astype(f32)
        + r2 * u2
        - hidden * (r2 * r2 * r2) * jnp.mean(u2 * hidden, axis=-1, keepdims=True)
    )
    dhid_ref[...] = dhid
    datt_ref[...] = dhid.astype(bf16)
    width = q_ref.shape[1]
    do_all = nt(datt_ref[...], wo_ref[...]).astype(bf16)
    lower, upper = triangle(True), triangle(False)
    for c in reversed(range(q_ref.shape[0] // CHUNK)):
        rows = pl.ds(c * CHUNK, CHUNK)
        q, k, v = q_ref[rows, :], k_ref[rows, :], v_ref[rows, :]
        do = do_all[c * CHUNK : (c + 1) * CHUNK]
        _, cum, inflow, total = gates(z_ref[rows, :])
        growth = jnp.exp(cum)
        p = p_ref[rows, :]
        i_hi, i_lo = halves(inflow)
        b_hi, b_lo = halves(jnp.where(lower, nt(do, v), 0.0))
        ev_hi, ev_lo = halves(e_ref[c, :, width:])
        dp = growth * (
            nt(do, ev_hi) + nt(do, ev_lo) + nn(b_hi, i_hi) + (nn(b_hi, i_lo) + nn(b_lo, i_hi))
        )
        ds = p * (dp - jnp.sum(p * dp, axis=-1, keepdims=True))
        w = (p * growth).astype(bf16)
        gds = (growth * ds).astype(bf16)
        n = jnp.where(lower, nt(gds, i_hi), 0.0).astype(bf16)
        dq_ref[rows, :] = (nn(gds, e_ref[c, :, :width].astype(bf16)) + nn(n, k)).astype(bf16)
        n_t = jnp.where(upper, nt(i_hi, gds), 0.0).astype(bf16)
        m_t = jnp.where(upper, nt(i_hi, w), 0.0).astype(bf16)
        dkl_ref[rows, :] = nn(n_t, q)
        dvl_ref[rows, :] = nn(m_t, do)
        h_ref[rows, :] = ds * sc_ref[rows, :] + p * dp
        a_t = jnp.where(upper, nt(k, q), 0.0).astype(bf16)
        b_t = jnp.where(upper, nt(v, do), 0.0).astype(bf16)
        x1_ref[rows, :] = nn(a_t, gds) + nn(b_t, w)
        keep = jnp.exp(total[:, :1])
        g_k, g_v = tn(gds, q), tn(w, do)
        g_ref[c, :, :width] = g_k
        g_ref[c, :, width:] = g_v
        state[:, :width] = g_k + keep * state[:, :width]
        state[:, width:] = g_v + keep * state[:, width:]
    s_ref[0] = state[...]


def last_kernel(per_part, l0_ref, k_ref, v_ref, z_ref, e_ref, g_ref, dkl_ref, dvl_ref, h_ref, x1_ref, dq_ref, x_ref,
                wq_ref, wk_ref, wv_ref, wf_ref, dk_ref, dv_ref, dz_ref, dxn_ref, bias_ref, gg_ref, state):
    step = pl.program_id(0)

    @pl.when(lax.rem(step, per_part) == 0)
    def _():
        state[...] = l0_ref[0]

    @pl.when(step == 0)
    def _():
        gg_ref[...] = jnp.zeros_like(gg_ref)
        bias_ref[...] = jnp.zeros_like(bias_ref)

    width = k_ref.shape[1]
    low, up = triangle(True).astype(f32), triangle(False).astype(f32)
    for c in reversed(range(k_ref.shape[0] // CHUNK)):
        rows = pl.ds(c * CHUNK, CHUNK)
        k, v = k_ref[rows, :], v_ref[rows, :]
        z = z_ref[rows, :]
        _, cum, inflow, total = gates(z)
        i_hi = inflow.astype(bf16)
        keep = jnp.exp(total[:, :1])
        lg = keep * state[...]
        lg_k, lg_v = lg[:, :width].astype(bf16), lg[:, width:].astype(bf16)
        dk_ref[rows, :] = (dkl_ref[rows, :] + nn(i_hi, lg_k)).astype(bf16)
        dv_ref[rows, :] = (dvl_ref[rows, :] + nn(i_hi, lg_v)).astype(bf16)
        x1 = x1_ref[rows, :]
        x2 = nt(k, lg_k) + nt(v, lg_v)
        met = exact(jnp.ones((8, 2 * width), f32), lg * e_ref[c], ((1,), (1,)))
        h, r1 = h_ref[rows, :], inflow * x1
        dla = (
            exact(up, h - r1, ((1,), (0,)))
            + r1
            + exact(low, inflow * x2, ((1,), (0,)))
            + met[:1]
            - jnp.exp(-cum) * (x1 + x2)
        )
        rate = lax.logistic(-z)
        dz = (dla * RATE * rate * (1.0 - rate)).astype(bf16)
        dz_ref[rows, :] = dz
        bias_ref[...] += jnp.sum(dz.astype(f32).reshape(-1, 8, dz.shape[1]), axis=0)
        state[...] = g_ref[c] + lg
    dxn = (
        nt(dq_ref[...], wq_ref[...])
        + nt(dk_ref[...], wk_ref[...])
        + nt(dv_ref[...], wv_ref[...])
        + nt(dz_ref[...], wf_ref[...])
    )
    dxn_ref[...] = dxn.astype(bf16)
    x = x_ref[...].astype(f32)
    r1 = lax.rsqrt(jnp.mean(x * x, axis=-1, keepdims=True) + EPS)
    gg_ref[...] += jnp.sum((dxn * x * r1).reshape(-1, 8, x.shape[1]), axis=0)


def hidden_kernel(n_head, place_ref, *refs):
    o_refs, (x_ref, gain_ref), w_refs = refs[:n_head], refs[n_head : n_head + 2], refs[n_head + 2 : n_head + 7]
    hid_ref, hn_ref, blocks, weights, sems = refs[n_head + 7 :]
    quarter = w_refs[1].shape[1]
    copies = [pltpu.make_async_copy(w_refs[0], weights.at[0], sems.at[0])]
    for d in range(1, n_head):
        for i in range(4):
            rows = pl.ds(pl.multiple_of(place_ref[1 + i] * quarter, quarter), quarter)
            copies.append(
                pltpu.make_async_copy(w_refs[1 + i].at[d - 1], weights.at[d, rows, :], sems.at[len(copies)])
            )

    @pl.when(pl.program_id(0) == 0)
    def _():
        for copy in copies:
            copy.start()
        for copy in copies:
            copy.wait()

    for d in range(n_head):
        blocks[d] = o_refs[d][...]
    me = place_ref[0]
    attended = None
    for h in range(n_head):
        away = lax.rem(me - h + n_head, n_head)
        term = nn(blocks[away], weights[away])
        attended = term if attended is None else attended + term
    hidden = x_ref[...].astype(f32) + attended
    hid_ref[...] = hidden
    r2 = lax.rsqrt(jnp.mean(hidden * hidden, axis=-1, keepdims=True) + EPS)
    hn_ref[...] = (hidden * r2 * gain_ref[...]).astype(bf16)


def flat(ref):
    block = ref[...]
    return block.reshape(block.shape[0] * block.shape[1], block.shape[2])


def units_kernel(hn_ref, cot_ref, wg_ref, wu_ref, wd_ref, act_ref, dg_ref, du_ref):
    gate = nn(hn_ref[...], flat(wg_ref))
    up = nn(hn_ref[...], flat(wu_ref))
    dact = nn(cot_ref[...], flat(wd_ref))
    s = lax.logistic(gate)
    silu = gate * s
    act_ref[...] = (silu * up).astype(bf16)
    dg_ref[...] = (dact * up * s * (1.0 + gate * (1.0 - s))).astype(bf16)
    du_ref[...] = (dact * silu).astype(bf16)


def wide_kernel(pairs, *refs):
    outs = refs[2 * pairs :]
    total = nt(refs[0][...], flat(refs[pairs]))
    for i in range(1, pairs):
        total = total + nt(refs[i][...], flat(refs[pairs + i]))
    total = total.astype(bf16)
    for t, out in enumerate(outs):
        out[...] = total[t * TILE : (t + 1) * TILE]


def summed(pairs):
    total = tn(*pairs[0])
    for pair in pairs[1:]:
        total = total + tn(*pair)
    return total.astype(bf16)


def ffn_grad_kernel(*refs):
    cot_ref, out_ref = refs[(len(refs) - 2) // 4], refs[-1]
    parts = cot_ref.shape[0]
    hn, dg, du, act = refs[:parts], *(refs[i * parts + 1 : (i + 1) * parts + 1] for i in (1, 2, 3))
    blocks, _, width, units = out_ref.shape
    for i, grads in enumerate((dg, du)):
        block = summed([(hn[m][...], grads[m][...]) for m in range(parts)])
        out_ref[:, i] = block.reshape(blocks, width, units)
    block = summed([(cot_ref[m], act[m][...]) for m in range(parts)])
    out_ref[:, 2] = block.reshape(blocks, width, units)


def attn_grad_kernel(*refs):
    out_ref, dzw_ref = refs[-2:]
    xn_ref = refs[0]
    parts = (len(refs) - 3) // 6
    datt, dq, dk, dv, o, dz = (refs[1 + i * parts : 1 + (i + 1) * parts] for i in range(6))
    rows, width = dq[0].shape
    xn = [xn_ref[m * rows : (m + 1) * rows, :] for m in range(parts)]
    for i, grads in enumerate((dq, dk, dv)):
        out_ref[:, i * width : (i + 1) * width] = summed([(xn[m], grads[m][...]) for m in range(parts)])
    out_ref[:, 3 * width :] = summed([(datt[m][...], o[m][...]) for m in range(parts)])
    dzw_ref[...] = summed([(xn[m], dz[m][...]) for m in range(parts)])


def packed(decay, state):
    high = decay.astype(bf16)
    low = (decay - high.astype(f32)).astype(bf16)
    lane = lax.broadcasted_iota(jnp.int32, decay.shape[:-1] + (128,), decay.ndim - 1)
    return jnp.concatenate([state.astype(bf16), jnp.where(lane == 0, high, low)], -1)


def unpacked(arrived):
    tail = arrived[..., -128:].astype(f32)
    return tail[..., 0:1] + tail[..., 1:2], arrived[..., :-128].astype(f32)


def scan_states(decay, state, after, behind=()):
    n, me = lax.axis_size("seq"), lax.axis_index("seq")
    part = (jnp.ones_like(decay), jnp.zeros_like(state))
    whole = (decay, state)
    bit, arrivals = 1, []
    while bit < n:
        message = packed(*whole)
        if len(arrivals) < len(behind):
            message = behind_of(message, behind[len(arrivals)])
        arrivals.append(lax.ppermute(message, "seq", [(i, i ^ bit) for i in range(n)]))
        there = unpacked(arrivals[-1])
        first = (me & bit) == 0
        takes = first if after else jnp.logical_not(first)
        d, s = whole
        part = (
            jnp.where(takes, there[0] * part[0], part[0]),
            jnp.where(takes, part[1] + part[0] * there[1], part[1]),
        )
        whole = (
            d * there[0],
            jnp.where(takes, s + d * there[1], there[1] + there[0] * s),
        )
        bit *= 2
    return part, whole, arrivals


def chained(part, whole, parts):
    arriving = jnp.zeros_like(part[1][0])
    found = {}
    for m in parts:
        found[m] = part[1][m] + part[0][m] * arriving
        arriving = whole[1][m] + whole[0][m] * arriving
    return jnp.stack([found[m] for m in sorted(found)])


def turned(block, n):
    return [lax.ppermute(block, "head", [(i, (i + d) % n) for i in range(n)]) for d in range(1, n)]


def behind_of(value, *first):
    return lax.optimization_barrier((value,) + first)[0]


def added(a, b):
    return (a.astype(f32) + b.astype(f32)).astype(bf16)


class Line:
    INWARD, OUTWARD, MIDDLE = [(0, 1), (3, 2)], [(1, 0), (2, 3)], [(1, 2), (2, 1)]

    def __init__(self):
        me = lax.axis_index("head")
        self.end = (me == 0) | (me == 3)
        self.pair = self.total = None

    def step(self, piece=None, inputs=()):
        pair, total = self.pair, self.total
        sends = []
        if piece is not None and total is not None:
            sends.append((jnp.where(self.end, piece, total), self.INWARD + self.OUTWARD))
        elif piece is not None:
            sends.append((piece, self.INWARD))
        elif total is not None:
            sends.append((total, self.OUTWARD))
        if pair is not None:
            sends.append((pair, self.MIDDLE))
        values = [s[0] for s in sends] + list(inputs)
        gated = list(lax.optimization_barrier(tuple(values)))
        arrived = [lax.ppermute(g, "head", way) for g, (_, way) in zip(gated, sends)]
        outer = arrived[0] if piece is not None or total is not None else None
        self.pair = added(piece, outer) if piece is not None else None
        self.total = added(pair, arrived[-1]) if pair is not None else None
        done = jnp.where(self.end, outer, total) if total is not None else None
        return done, gated[len(sends) :]


def on_device(tokens, gain_attn, w_query, w_key, w_value, w_forget, forget_bias, w_out, gain_ffn, w_gate, w_up, w_down,
              cotangent):
    parts, part_rows, width = tokens.shape
    rows = parts * part_rows
    head = w_query.shape[1]
    slots = w_forget.shape[1]
    units = w_gate.shape[1]
    n_seq, n_head = lax.axis_size("seq"), lax.axis_size("head")
    span = w_gate.shape[0]
    steps = rows // TILE
    per_part = part_rows // TILE
    chunks = TILE // CHUNK

    gain1 = gain_attn.reshape(1, width)
    gain2 = gain_ffn.reshape(1, width)
    state_scratch = pltpu.VMEM((slots, 2 * head), f32)

    def tiled(columns, back=False):
        return pl.BlockSpec((TILE, columns), (lambda i: (per_part - 1 - i, 0)) if back else (lambda i: (i, 0)))

    def at(m, columns, back=False):
        return pl.BlockSpec(
            (TILE, columns),
            (lambda i: (m * per_part + per_part - 1 - i, 0)) if back else (lambda i: (m * per_part + i, 0)),
        )

    def part_at(m, columns, back=False):
        return pl.BlockSpec(
            (None, TILE, columns), (lambda i: (m, per_part - 1 - i, 0)) if back else (lambda i: (m, i, 0))
        )

    def chunked(back=False):
        return pl.BlockSpec(
            (chunks, slots, 2 * head), (lambda i: (per_part - 1 - i, 0, 0)) if back else (lambda i: (i, 0, 0))
        )

    def state_of(m, columns):
        return pl.BlockSpec((1, slots, columns), lambda i: (m, 0, 0))

    one_state = pl.BlockSpec((1, slots, 2 * head), lambda i: (0, 0, 0))
    per_chunk = shaped((part_rows // CHUNK, slots, 2 * head), f32)

    stacked = jnp.stack([w_gate, w_up, w_down.T])
    x = tokens.reshape(rows, width)
    place = lax.axis_index("seq")
    low_bit, high_bit = place & 1, (place & 2) // 2
    quarter = head // 4
    share = lax.dynamic_slice_in_dim(w_out, (2 * high_bit + low_bit) * quarter, quarter, 0)
    x, stacked, share = lax.optimization_barrier((x, stacked, share))
    full = lax.all_gather(stacked, "seq")
    shares = turned(share, n_head)
    all_rows = lambda c: pl.BlockSpec((TILE, c), lambda i: (i, 0))
    by_part = lambda c: pl.BlockSpec((1, slots, c), lambda i: (i // per_part, 0, 0))
    xn, q, k, v, z, local, decay_sum = call(
        "project",
        functools.partial(project_kernel, per_part),
        (steps,),
        [all_rows(width), fixed((1, width))] + [fixed((width, head))] * 3 + [fixed((width, slots)), fixed((1, slots))],
        [all_rows(width), all_rows(head), all_rows(head), all_rows(head), all_rows(slots), by_part(2 * head), by_part(128)],
        [shaped((rows, width), bf16)] + [shaped((rows, head), bf16)] * 3
        + [shaped((rows, slots), f32), shaped((parts, slots, 2 * head), f32), shaped((parts, slots, 128), f32)],
        [state_scratch, pltpu.VMEM((slots, 128), f32)],
        cost=cost(2 * rows * width * (3 * head + slots), 2 * rows * width * 3 + 2 * width * 3 * head),
    )(x, gain1, w_query, w_key, w_value, w_forget, forget_bias.reshape(1, slots))
    decay = jnp.exp(decay_sum[:, :, :1])
    before, everything, arrivals = scan_states(decay, local, False, shares[:2])
    entering = chained(before, everything, range(parts))

    held = jnp.stack(shares)
    held = behind_of(held, arrivals[1] if len(arrivals) > 1 else arrivals[0])
    across = lax.ppermute(held, "seq", [(i, i ^ 2) for i in range(n_seq)])
    beside = lax.ppermute(held, "seq", [(i, i ^ 1) for i in range(n_seq)])

    o, p, scores, e_chunks = [], [], [], []
    for m in range(parts):
        o_m, p_m, s_m, e_m = call(
            "read",
            functools.partial(read_kernel, per_part),
            (per_part,),
            [at(m, head)] * 3 + [at(m, slots), state_of(m, 2 * head)],
            [tiled(head), tiled(slots), tiled(slots), chunked()],
            [shaped((part_rows, head), bf16), shaped((part_rows, slots), f32), shaped((part_rows, slots), f32), per_chunk],
            [state_scratch],
            cost=cost(2 * part_rows * head * 600, 2 * part_rows * head * 4 + part_rows * slots * 64),
        )(q, k, v, z, entering)
        o.append(o_m)
        p.append(p_m)
        scores.append(s_m)
        e_chunks.append(e_m)

    turns = [turned(o_m, n_head) for o_m in o]
    beside_across = lax.ppermute(behind_of(across, turns[0][0]), "seq", [(i, i ^ 1) for i in range(n_seq)])
    low_place, high_place = 2 * high_bit, 2 * (1 - high_bit)
    places = jnp.stack(
        [lax.axis_index("head"), low_place + low_bit, high_place + low_bit, low_place + 1 - low_bit,
         high_place + 1 - low_bit]
    ).astype(jnp.int32)

    def project_out(m, own):
        return call(
            "hidden",
            functools.partial(hidden_kernel, n_head),
            (per_part,),
            [pl.BlockSpec(memory_space=pltpu.SMEM)] + [tiled(head)] * n_head + [at(m, width), fixed((1, width))]
            + [pl.BlockSpec(memory_space=pl.ANY)] * 5,
            [tiled(width), tiled(width)],
            [shaped((part_rows, width), f32), shaped((part_rows, width), bf16)],
            [pltpu.VMEM((n_head, TILE, head), bf16), pltpu.VMEM((n_head, head, width), bf16),
             pltpu.SemaphoreType.DMA((4 * n_head - 3,))],
            cost=cost(2 * part_rows * width * width, part_rows * width * 10 + 2 * width * width),
        )(places, own, *turns[m], x, gain2, w_out, held, across, beside, beside_across)

    unit_tile = 256
    unit_steps = pl.cdiv(units, unit_tile)

    def weight_tile(which):
        return pl.BlockSpec((n_seq, None, span, unit_tile), lambda j: (0, which, 0, j))

    def feed(m, hn):
        unit_out = pl.BlockSpec((part_rows, unit_tile), lambda j: (0, j))
        return call(
            "units",
            units_kernel,
            (unit_steps,),
            [fixed((part_rows, width)),
             pl.BlockSpec((None, part_rows, width), lambda j: (m, 0, 0), pipeline_mode=pl.Buffered(1)),
             weight_tile(0), weight_tile(1), weight_tile(2)],
            [unit_out] * 3,
            [shaped((part_rows, units), bf16)] * 3,
            cost=cost(6 * part_rows * width * units, 4 * part_rows * width + 6 * part_rows * units + 6 * width * units),
        )(hn, cotangent, full, full, full)

    group = max(1, TILE // span)
    wide = group * span
    pieces = part_rows // TILE

    def weight_rows(which):
        return pl.BlockSpec((group, None, span, units), lambda j: (j, which, 0, 0))

    def widened(name, sources, which):
        count = len(sources)
        return call(
            name,
            functools.partial(wide_kernel, count),
            (width // wide,),
            [fixed((part_rows, units))] * count + [weight_rows(i) for i in which],
            [pl.BlockSpec((TILE, wide), lambda j: (0, j))] * pieces,
            [shaped((TILE, width), bf16)] * pieces,
            cost=cost(2 * count * part_rows * width * units,
                      2 * count * (part_rows + width) * units + 2 * part_rows * width),
        )(*sources, *([full] * count))

    def back(m, dhn, hidden):
        return call(
            "back",
            functools.partial(back_kernel, per_part),
            (per_part,),
            [tiled(width, True), tiled(width, True), part_at(m, width, True), fixed((1, width)), fixed((head, width))]
            + [at(m, head, True)] * 3 + [at(m, slots, True)] + [tiled(slots, True)] * 2 + [chunked(True)],
            [tiled(width, True), tiled(width, True), tiled(head, True), tiled(head, True), tiled(head, True),
             tiled(slots, True), tiled(slots, True), chunked(True), one_state,
             pl.BlockSpec((8, width), lambda i: (0, 0))],
            [shaped((part_rows, width), f32), shaped((part_rows, width), bf16), shaped((part_rows, head), bf16),
             shaped((part_rows, head), f32), shaped((part_rows, head), f32), shaped((part_rows, slots), f32),
             shaped((part_rows, slots), f32), per_chunk, shaped((1, slots, 2 * head), f32), shaped((8, width), f32)],
            [state_scratch],
            cost=cost(2 * part_rows * width * head + 2 * part_rows * head * 1500,
                      part_rows * width * 14 + part_rows * head * 20),
        )(dhn, hidden, cotangent, gain2, w_out, q, k, v, z, p[m], scores[m], e_chunks[m])

    def last(m, leaving, saved):
        dq, dk_local, dv_local, h_sum, x_local, g_chunks = saved
        return call(
            "last",
            functools.partial(last_kernel, per_part),
            (per_part,),
            [state_of(m, 2 * head), at(m, head, True), at(m, head, True), at(m, slots, True), chunked(True), chunked(True),
             tiled(head, True), tiled(head, True), tiled(slots, True), tiled(slots, True), tiled(head, True),
             at(m, width, True)] + [fixed((width, head))] * 3 + [fixed((width, slots))],
            [tiled(head, True), tiled(head, True), tiled(slots, True), tiled(width, True),
             pl.BlockSpec((8, slots), lambda i: (0, 0)), pl.BlockSpec((8, width), lambda i: (0, 0))],
            [shaped((part_rows, head), bf16), shaped((part_rows, head), bf16), shaped((part_rows, slots), bf16),
             shaped((part_rows, width), bf16), shaped((8, slots), f32), shaped((8, width), f32)],
            [state_scratch],
            cost=cost(2 * part_rows * width * (3 * head + slots),
                      part_rows * width * 8 + part_rows * head * 20 + width * head * 6),
        )(leaving, k, v, z, e_chunks[m], g_chunks, dk_local, dv_local, h_sum, x_local, dq, x,
          w_query, w_key, w_value, w_forget)

    def ffn_grads(normed, gates, ups, acts):
        return call(
            "ffn_grads",
            ffn_grad_kernel,
            (width // wide,),
            [pl.BlockSpec((part_rows, wide), lambda j: (0, j))] * parts
            + [pl.BlockSpec((parts, part_rows, wide), lambda j: (0, 0, j))]
            + [fixed((part_rows, units))] * (3 * parts),
            pl.BlockSpec((group, 3, span, units), lambda j: (j, 0, 0, 0)),
            shaped((n_seq, 3, span, units), bf16),
            cost=cost(6 * rows * width * units, 4 * rows * width + 6 * rows * units + 6 * width * units),
            vmem=56,
        )(*normed, cotangent, *gates, *ups, *acts)

    line = Line()
    sums, order, live = {}, [], {}

    def advance(key=None, piece=None):
        names = list(live)
        done, gated = line.step(piece, [live[n] for n in names])
        live.update(zip(names, gated))
        order.append(key)
        if done is not None:
            sums[order[-3]] = done

    def joined(kind, m):
        return jnp.concatenate([sums[kind, m, t] for t in range(pieces)], 0)

    hidden, hn, act, dgate, dup, backs, lasts = ([None] * parts for _ in range(7))

    def forward(m, own):
        live["hidden", m], live["hn", m] = project_out(m, own)
        live["act", m], live["dgate", m], live["dup", m] = feed(m, live["hn", m])

    forward(0, o[0])
    dhn_parts = widened("dhn", (live["dgate", 0], live["dup", 0]), (0, 1))
    live["o", 1] = o[1]
    advance(("dhn", 0, 0), dhn_parts[0])

    forward(1, live["o", 1])
    live["later"] = dhn_parts[1]
    advance(("dhn", 0, 1), live.pop("later"))

    dhn_parts = widened("dhn", (live["dgate", 1], live["dup", 1]), (0, 1))
    ffn_a = widened("ffn", (live["act", 0],), (2,))
    live["later"], live["ffn", 0], live["ffn", 1] = dhn_parts[1], *ffn_a
    advance(("dhn", 1, 0), dhn_parts[0])

    live["ffn", 2], live["ffn", 3] = widened("ffn", (live["act", 1],), (2,))
    advance(("dhn", 1, 1), live.pop("later"))

    grads = ffn_grads(*([live[n, m] for m in range(parts)] for n in ("hn", "dgate", "dup", "act")))
    for n in ("hn", "dgate", "dup", "act"):
        for m in range(parts):
            del live[n, m]
    live["ffn_grads"] = grads
    advance(("ffn", 0, 0), live.pop(("ffn", 0)))

    ffn_shares = lax.psum_scatter(live.pop("ffn_grads"), "seq", scatter_dimension=0)
    backs[0] = back(0, joined("dhn", 0), live["hidden", 0])
    live["back", 0] = backs[0][8]
    advance(("ffn", 0, 1), live.pop(("ffn", 1)))

    advance(("ffn", 1, 0), live.pop(("ffn", 2)))

    backs[1] = back(1, joined("dhn", 1), live["hidden", 1])
    live["back", 1] = backs[1][8]
    advance(("ffn", 1, 1), live.pop(("ffn", 3)))

    local_back = jnp.concatenate([live.pop(("back", m)) for m in range(parts)], 0)
    behind, everything, _ = scan_states(decay, local_back, True)
    live["leaving"] = chained(behind, everything, reversed(range(parts)))
    live["ffn_shares"] = ffn_shares
    advance()

    lasts[0] = last(0, live["leaving"], backs[0][2:8])
    live["dxn", 0], live["dxn", 1] = lasts[0][3][:TILE], lasts[0][3][TILE:]
    ffn_shares = live.pop("ffn_shares")
    advance(("dxn", 0, 0), live.pop(("dxn", 0)))

    lasts[1] = last(1, live.pop("leaving"), backs[1][2:8])
    live["dxn", 2], live["dxn", 3], live["xn"] = lasts[1][3][:TILE], lasts[1][3][TILE:], xn
    advance(("dxn", 0, 1), live.pop(("dxn", 1)))
    xn = live.pop("xn")

    attn_grads, forget_grads = call(
        "attn_grads",
        attn_grad_kernel,
        (width // TILE,),
        [pl.BlockSpec((rows, TILE), lambda j: (0, j))] + [pl.BlockSpec((part_rows, TILE), lambda j: (0, j))] * parts
        + [fixed((part_rows, head))] * (4 * parts) + [fixed((part_rows, slots))] * parts,
        [pl.BlockSpec((TILE, 4 * head), lambda j: (j, 0)), pl.BlockSpec((TILE, slots), lambda j: (j, 0))],
        [shaped((width, 4 * head), bf16), shaped((width, slots), bf16)],
        cost=cost(2 * rows * width * (4 * head + slots), 4 * rows * width + 8 * rows * head + 8 * width * head),
    )(xn, *[b[1] for b in backs], *[b[2] for b in backs], *[n[0] for n in lasts], *[n[1] for n in lasts], *o,
      *[n[2] for n in lasts])
    live["attn_grads"] = attn_grads
    bias_sum = sum(jnp.sum(n[4], 0) for n in lasts)
    gain1_sum = sum(jnp.sum(n[5], 0) for n in lasts)
    gain2_sum = sum(jnp.sum(b[9], 0) for b in backs)
    small = jnp.concatenate(
        [
            forget_grads,
            gain2_sum.astype(bf16)[:, None],
            gain1_sum.astype(bf16)[:, None],
            jnp.zeros((width, 128 - 2 - slots % 128), bf16),
        ],
        1,
    ).reshape(n_seq, span, -1)
    bias_row = jnp.pad(jnp.stack(halves(bias_sum)), ((0, 14), (0, small.shape[2] - slots)))
    small = jnp.concatenate([small, jnp.broadcast_to(bias_row, (n_seq,) + bias_row.shape)], 1)
    live["small"] = small
    outs, in_grads = [], []

    def finish_out(m):
        outs.append((live.pop(("hidden", m)) + joined("ffn", m).astype(f32)).astype(bf16))

    def finish_grad(m):
        dxn = joined("dxn", m)
        xf = tokens[m].astype(f32)
        r1 = lax.rsqrt(jnp.mean(xf * xf, axis=-1, keepdims=True) + EPS)
        u1 = gain1 * dxn.astype(f32)
        in_grads.append(backs[m][0] + r1 * u1 - xf * (r1 * r1 * r1) * jnp.mean(u1 * xf, axis=-1, keepdims=True))

    advance(("dxn", 1, 0), live.pop(("dxn", 2)))
    small_shares = lax.psum_scatter(live.pop("small"), "seq", scatter_dimension=0).astype(f32)
    attn_shares = lax.psum_scatter(live.pop("attn_grads"), "seq", scatter_dimension=0, tiled=True).astype(f32)
    bias_total = small_shares[span, :slots] + small_shares[span + 1, :slots]
    gain1_total = small_shares[:span, slots + 1]
    bit = 1
    while bit < n_head:
        gain1_total = gain1_total + lax.ppermute(gain1_total, "head", [(i, i ^ bit) for i in range(n_head)])
        bit *= 2

    finish_out(0)
    live["out", 0] = outs[0]
    advance(("dxn", 1, 1), live.pop(("dxn", 3)))
    finish_out(1)
    live["out", 1] = outs[1]
    advance()
    finish_grad(0)
    live["in_grad"] = in_grads[0]
    advance()
    finish_grad(1)
    outs, in_grads[0] = [live["out", m] for m in range(parts)], live["in_grad"]

    return (
        jnp.stack(outs),
        jnp.stack(in_grads),
        gain1_total,
        attn_shares[:, :head],
        attn_shares[:, head : 2 * head],
        attn_shares[:, 2 * head : 3 * head],
        small_shares[:span, :slots],
        bias_total,
        attn_shares[:, 3 * head :].T,
        small_shares[:span, slots],
        ffn_shares[0].astype(f32),
        ffn_shares[1].astype(f32),
        ffn_shares[2].astype(f32).T,
    )


def solution(mesh):
    rows, both = P(None, "seq", None), P("seq", "head")
    by_head, down = P(None, "head"), P("head", "seq")
    return jax.shard_map(
        on_device,
        mesh=mesh,
        in_specs=(rows, P(), by_head, by_head, by_head, by_head, P("head"), P("head", None), P(), both, both, down, rows),
        out_specs=(rows, rows, P("seq"), both, both, both, both, P("head"), down, P("seq"), both, both, down),
        check_vma=False,
    )
```

time: 2020 us -> 761 us (0.38); the launches traced: 1990 us -> 751 us
  matrix products: 534 us -> 0 us
  local copies, waits for them, and re-layouts: 448 us -> 43.1 us
  waiting for transfers between devices: 646 us -> 265 us
  Pallas kernels: 0 us -> 215 us
  other arithmetic: 295 us -> 108 us
  starting transfers between devices: 1.98 us -> 104 us
  blocking collectives: 41.9 us -> 0 us
    dot_general x282 -> x0, matrix products: 534 us -> none  [the longest x240 334 us: precise(): return jnp.dot(left, right, precision=highest)]
    psum x5 -> x0, waiting for transfers between devices: 362 us -> none  [the longest x1 294 us: on_device(): lax.psum(branch_part.astype(jnp.bfloat16), 'head').astype(jnp.float32)]
    reduce_scatter x7 -> x3, waiting for transfers between devices: 283 us -> 2.01 us  [the longest x1 2.01 us: on_device(): lax.psum_scatter(live.pop('ffn_grads'), 'seq', scatter_dimension=0)]
    ppermute x0 -> x47, waiting for transfers between devices: none -> 263 us  [the longest x27 132 us: step(): lax.ppermute(g, 'head', way)]
    dynamic_update_slice x208 -> x0, local copies, waits for them, and re-layouts: 221 us -> none  [span_readout(): unused, outputs = lax.scan(advance, entering, pieces_all)]
    pallas_call x0 -> x17, Pallas kernels: none -> 215 us  [the longest x4 37.8 us: widened(): call(name, functools.partial(wide_kernel, count), (width // wide,), [fixe...]
    ppermute x0 -> x47, starting transfers between devices: none -> 104 us  [the longest x27 56.4 us: step(): lax.ppermute(g, 'head', way)]
    another operation x106 -> x1, local copies, waits for them, and re-layouts: 62.5 us -> 0.08 us  [on_device(): jnp.stack([lax.axis_index('head'), low_place + low_bit, high_place + low_...]
  transfers between devices with their start and end apart: 17 -> 51, of which waited for: 7 -> 22; matrix products, arithmetic and copies ran while one was open for 46% -> 13% of each run, Pallas kernels for 0% -> 27%
where the time goes in v1:
time: 761 us; the launch traced here: 751 us
  waiting for transfers between devices  265 us (35%)
  Pallas kernels  215 us (28%)
  other arithmetic  108 us (14%)
  starting transfers between devices  104 us (14%)
  local copies, waits for them, and re-layouts  43.1 us (6%)
  between operations  16.2 us (2%)
    ppermute x27, waiting for transfers between devices, step(): lax.ppermute(g, 'head', way)  132 us
    ppermute x9, waiting for transfers between devices, turned(): lax.ppermute(block, 'head', [(i, (i + d) % n) for i in range(n)])  57.5 us
    ppermute x27, starting transfers between devices, step(): lax.ppermute(g, 'head', way)  56.4 us
    ppermute x6, waiting for transfers between devices, scan_states(): lax.ppermute(message, 'seq', [(i, i ^ bit) for i in range(n)])  41.4 us
    ppermute x9, starting transfers between devices, turned(): lax.ppermute(block, 'head', [(i, (i + d) % n) for i in range(n)])  38.2 us
    pallas_call x4, Pallas kernels, widened(): call(name, functools.partial(wide_kernel, count), (width // wide,), [fixe...  37.8 us
    unnamed x246, local copies, waits for them, and re-layouts  34.4 us
    pallas_call x2, Pallas kernels, feed(): call('units', units_kernel, (unit_steps,), [fixed((part_rows, width)), pl...  30.5 us
  transfers between devices with their start and end apart: 51, of which 22 were waited for; matrix products, arithmetic and copies ran while one was open for 13% of the time, Pallas kernels for 27%

profile of v1, /device:TPU:0, one launch (start us, length us, event | category | flops | bytes accessed | tf_op | source)
XLA Modules:
  0.0 751.3 jit_solution(16155560581567649999)
XLA Ops:
  12.4 3.1 collective-permute-start
  15.8 16.1 %project.1 = (bf16[1024,2048]{1,0:T(8,128)(2,1)}, bf16[1024,512]{1,0:T(8,128)(2,1)S(1)}, bf16[1024,512]{1,0:T(8,128)(2,1)S(1)}, bf16[1024,512]{1,0:T(8,128)(2,1)...) custom-call(bf16[1024,2048]{1,0:T(8,128)(2,1)} %bitcast.79, ...), custom_call_target="tpu_custom_call" | custom-call | flops 6710886400 | bytes 18874368 | tf_op jit(solution)/shard_map/project/pallas_call | solution.py:495
  34.7 2.7 collective-permute-start.2
  41.9 19.6 %collective-permute-done.2 = bf16[128,2048]{1,0:T(8,128)(2,1)} collective-permute-done((bf16[128,2048]{1,0:T(8,128)(2,1)}, bf16[128,2048]{1,0:T(8,128)(2,1)}, u32[]{:S(2)}, u32[]{:S(2)}) %collective-permute-start.2) | collective-permute-done | bytes 524320 | tf_op jit(solution)/shard_map/ppermute | solution.py:402
  63.0 2.8 collective-permute-start.8
  65.9 11.7 %collective-permute-done.3 = bf16[2,64,1152]{2,1,0:T(8,128)(2,1)} collective-permute-done((bf16[2,64,1152]{2,1,0:T(8,128)(2,1)}, bf16[2,64,1152]{2,1,0:T(8,128)(2,1)}, u32[]{:S(2)}, u32[]{:S(2)}) %collective-permute-start.3) | collective-permute-done | bytes 294944 | tf_op jit(solution)/shard_map/ppermute | solution.py:375
  84.5 2.7 pad_maximum_fusion.7.refs_7_
  88.7 10.2 %collective-permute-done.4 = bf16[2,64,1152]{2,1,0:T(8,128)(2,1)} collective-permute-done((bf16[2,64,1152]{2,1,0:T(8,128)(2,1)}, bf16[2,64,1152]{2,1,0:T(8,128)(2,1)}, u32[]{:S(2)}, u32[]{:S(2)}) %collective-permute-start.4) | collective-permute-done | bytes 294944 | tf_op jit(solution)/shard_map/ppermute | solution.py:375
  105.0 5.6 read.2
  113.1 14.4 %collective-permute-done.5.refs_1_ = bf16[512,512]{1,0:T(8,128)(2,1)S(1)} collective-permute-done((bf16[512,512]{1,0:T(8,128)(2,1)}, bf16[512,512]{1,0:T(8,128)(2,1)S(1)}, u32[]{:S(2)}, u32[]{:S(2)}) %collective-permute-start.5) | collective-permute-done | bytes 524320 | tf_op jit(solution)/shard_map/ppermute | solution.py:402
  128.3 16.5 %collective-permute-done.9.refs_8_ = bf16[3,128,2048]{2,1,0:T(8,128)(2,1)} collective-permute-done((bf16[3,128,2048]{2,1,0:T(8,128)(2,1)}, bf16[3,128,2048]{2,1,0:T(8,128)(2,1)}, u32[]{:S(2)}, u32[]{:S(2)}) %collective-permute-start.9) | collective-permute-done | bytes 1572896 | tf_op jit(solution)/shard_map/ppermute | solution.py:512
  144.8 3.3 collective-permute-start.7
  149.3 5.5 read.3
  158.3 2.5 collective-permute-done.7.refs_3_
  162.3 21.0 %collective-permute-done.6.refs_2_ = bf16[512,512]{1,0:T(8,128)(2,1)} collective-permute-done((bf16[512,512]{1,0:T(8,128)(2,1)}, bf16[512,512]{1,0:T(8,128)(2,1)}, u32[]{:S(2)}, u32[]{:S(2)}) %collective-permute-start.6) | collective-permute-done | bytes 524320 | tf_op jit(solution)/shard_map/ppermute | solution.py:402
  183.3 23.7 %collective-permute-start.13 = (bf16[512,512]{1,0:T(8,128)(2,1)}, bf16[512,512]{1,0:T(8,128)(2,1)}, u32[]{:S(2)}, u32[]{:S(2)}) collective-permute-start(bf16[512,512]{1,0:T(8,128)(2,1)} %get-tuple-element.229.refs_0_.refs_10_), channel_id=1, source_target_pairs={{0,1},{1,2},{2,3},{3,0},{4,5},{5,6},{6,7},{7,4},{8,9},{9,10},{10,1... | collective-permute-start | bytes 1572872 | tf_op jit(solution)/shard_map/ppermute | solution.py:402
  207.0 12.0 %hidden.2 = (f32[512,2048]{1,0:T(8,128)}, bf16[512,2048]{1,0:T(8,128)(2,1)}) custom-call(s32[5]{0:T(128)S(1)} %stack.80.place_ref, bf16[512,512]{1,0:T(8,128)(2,1)} %get-tuple-element.211.refs_0_.refs_9_, bf16[512,512]{1,0:T(8,128)(2,1)S(1)} %copy-done.65, bf16[512,512]{1,0:T(8,128)(2,1)} %collective-permute-done.6.refs_2_, ...), custom_call_target="tpu_custom_call" | custom-call | flops 4294967296 | bytes 18874368 | tf_op jit(solution)/shard_map/hidden/pallas_call | solution.py:541
  219.0 15.2 %units.2 = (bf16[512,1408]{1,0:T(8,128)(2,1)S(1)}, bf16[512,1408]{1,0:T(8,128)(2,1)S(1)}, bf16[512,1408]{1,0:T(8,128)(2,1)S(1)}) custom-call(bf16[512,2048]{1,0:T(8,128)(2,1)} %get-tuple-element.276.hn_ref.refs_0_, bf16[2,512,2048]{2,1,0:T(8,128)(2,1)} %cot_ref.7, bf16[8,3,256,1408]{3,2,1,0:T(8,128)(2,1)} %bitcast.67, bf16[8,3,256,1408]{3,2,1,0:T(8,128)(2,1)} %bitcast.68, ...), custom_call_target="tpu_custom_call" | custom-call | flops 8858370048 | bytes 25821184 | tf_op jit(solution)/shard_map/units/pallas_call | solution.py:562
  234.3 11.7 %dhn.2 = (bf16[256,2048]{1,0:T(8,128)(2,1)S(1)}, bf16[256,2048]{1,0:T(8,128)(2,1)S(1)}) custom-call(bf16[512,1408]{1,0:T(8,128)(2,1)S(1)} %get-tuple-element.278.refs_0_.refs_3_, bf16[512,1408]{1,0:T(8,128)(2,1)S(1)} %get-tuple-element.280.refs_1_.refs_5_, bf16[8,3,256,1408]{3,2,1,0:T(8,128)(2,1)} %bitcast.70, bf16[8,3,256,1408]{3,2,1,0:T(8,128)(2,1)} %bitcast.71), custom_call_target="tpu_custom_call" | custom-call | flops 5905580032 | bytes 16515072 | tf_op jit(solution)/shard_map/dhn/pallas_call | solution.py:583
  248.0 11.9 %hidden.3 = (f32[512,2048]{1,0:T(8,128)}, bf16[512,2048]{1,0:T(8,128)(2,1)}) custom-call(s32[5]{0:T(128)S(1)} %stack.80.place_ref, bf16[512,512]{1,0:T(8,128)(2,1)} %get-tuple-element.229.refs_0_.refs_10_, bf16[512,512]{1,0:T(8,128)(2,1)} %collective-permute-done.13.refs_1_, bf16[512,512]{1,0:T(8,128)(2,1)S(1)} %collective-permute-done.14.refs_2_, ...), custom_call_target="tpu_custom_call" | custom-call | flops 4294967296 | bytes 18874368 | tf_op jit(solution)/shard_map/hidden/pallas_call | solution.py:541
  259.9 15.2 %units.3 = (bf16[512,1408]{1,0:T(8,128)(2,1)S(1)}, bf16[512,1408]{1,0:T(8,128)(2,1)S(1)}, bf16[512,1408]{1,0:T(8,128)(2,1)S(1)}) custom-call(bf16[512,2048]{1,0:T(8,128)(2,1)} %get-tuple-element.277.hn_ref.refs_1_, bf16[2,512,2048]{2,1,0:T(8,128)(2,1)} %cot_ref.7, bf16[8,3,256,1408]{3,2,1,0:T(8,128)(2,1)} %bitcast.72, bf16[8,3,256,1408]{3,2,1,0:T(8,128)(2,1)} %bitcast.73, ...), custom_call_target="tpu_custom_call" | custom-call | flops 8858370048 | bytes 25821184 | tf_op jit(solution)/shard_map/units/pallas_call | solution.py:562
  283.3 7.8 %ffn.2 = (bf16[256,2048]{1,0:T(8,128)(2,1)S(1)}, bf16[256,2048]{1,0:T(8,128)(2,1)S(1)}) custom-call(bf16[512,1408]{1,0:T(8,128)(2,1)S(1)} %copy-done.26, bf16[8,3,256,1408]{3,2,1,0:T(8,128)(2,1)} %bitcast.75), custom_call_target="tpu_custom_call" | custom-call | flops 2952790016 | bytes 9306112 | tf_op jit(solution)/shard_map/ffn/pallas_call | solution.py:583
  293.1 10.6 %dhn.3 = (bf16[256,2048]{1,0:T(8,128)(2,1)S(1)}, bf16[256,2048]{1,0:T(8,128)(2,1)S(1)}) custom-call(bf16[512,1408]{1,0:T(8,128)(2,1)S(1)} %get-tuple-element.279.refs_0_.refs_4_, bf16[512,1408]{1,0:T(8,128)(2,1)S(1)} %copy-done.24, bf16[8,3,256,1408]{3,2,1,0:T(8,128)(2,1)} %bitcast.76, bf16[8,3,256,1408]{3,2,1,0:T(8,128)(2,1)} %bitcast.77), custom_call_target="tpu_custom_call" | custom-call | flops 5905580032 | bytes 16515072 | tf_op jit(solution)/shard_map/dhn/pallas_call | solution.py:583
  306.7 3.5 collective-permute-start.19
  311.3 7.8 %ffn.3 = (bf16[256,2048]{1,0:T(8,128)(2,1)S(1)}, bf16[256,2048]{1,0:T(8,128)(2,1)S(1)}) custom-call(bf16[512,1408]{1,0:T(8,128)(2,1)S(1)} %copy-done.28, bf16[8,3,256,1408]{3,2,1,0:T(8,128)(2,1)} %bitcast.78), custom_call_target="tpu_custom_call" | custom-call | flops 2952790016 | bytes 9306112 | tf_op jit(solution)/shard_map/ffn/pallas_call | solution.py:583
  319.1 12.6 %collective-permute-done.19 = bf16[256,2048]{1,0:T(8,128)(2,1)S(1)} collective-permute-done((bf16[256,2048]{1,0:T(8,128)(2,1)S(1)}, bf16[256,2048]{1,0:T(8,128)(2,1)S(1)}, u32[]{:S(2)}, u32[]{:S(2)}) %collective-permute-start.19) | collective-permute-done | bytes 1048608 | tf_op jit(solution)/shard_map/ppermute | solution.py:434
  336.4 4.8 collective-permute-start.21
  341.1 26.6 %ffn_grads.1 = bf16[8,3,256,1408]{3,2,1,0:T(8,128)(2,1)} custom-call(bf16[512,2048]{1,0:T(8,128)(2,1)} %get-tuple-element.276.hn_ref.refs_0_, bf16[512,2048]{1,0:T(8,128)(2,1)} %get-tuple-element.277.hn_ref.refs_1_, bf16[2,512,2048]{2,1,0:T(8,128)(2,1)} %cot_ref.7, bf16[512,1408]{1,0:T(8,128)(2,1)} %copy-done.20, bf16[512,1408]{1,0:T(8,128)(2,1)} %copy-done.22, ...), custom_call_target="tpu_custom_call" | custom-call | flops 17716740096 | bytes 34340864 | tf_op jit(solution)/shard_map/ffn_grads/pallas_call | solution.py:632
  367.8 3.0 add_convert_fusion.19
  370.8 3.1 broadcast_select_fusion.18
  374.1 2.6 broadcast_select_fusion.16
  380.9 15.2 %back.2 = (f32[512,2048]{1,0:T(8,128)}, bf16[512,2048]{1,0:T(8,128)(2,1)}, bf16[512,512]{1,0:T(8,128)(2,1)S(1)}, f32[512,512]{1,0:T(8,128)S(1)}, f32[512,512]{1,...) custom-call(bf16[512,2048]{1,0:T(8,128)(2,1)} %pad_maximum_fusion.3., ...), custom_call_target="tpu_custom_call" | custom-call | flops 1860173824 | bytes 19922944 | tf_op jit(solution)/shard_map/back/pallas_call | solution.py:595
  399.0 2.9 collective-permute-start.25
  402.8 17.6 %collective-permute-done.25 = bf16[256,2048]{1,0:T(8,128)(2,1)S(1)} collective-permute-done((bf16[256,2048]{1,0:T(8,128)(2,1)S(1)}, bf16[256,2048]{1,0:T(8,128)(2,1)S(1)}, u32[]{:S(2)}, u32[]{:S(2)}) %collective-permute-start.25) | collective-permute-done | bytes 1048608 | tf_op jit(solution)/shard_map/ppermute | solution.py:434
  422.5 3.1 collective-permute-start.26
  425.6 2.3 broadcast_select_fusion.12
  430.8 13.8 %back.3 = (f32[512,2048]{1,0:T(8,128)}, bf16[512,2048]{1,0:T(8,128)(2,1)}, bf16[512,512]{1,0:T(8,128)(2,1)S(1)}, f32[512,512]{1,0:T(8,128)S(1)}, f32[512,512]{1,...) custom-call(bf16[512,2048]{1,0:T(8,128)(2,1)} %pad_maximum_fusion.4., ...), custom_call_target="tpu_custom_call" | custom-call | flops 1860173824 | bytes 19922944 | tf_op jit(solution)/shard_map/back/pallas_call | solution.py:595
  451.6 11.5 %collective-permute-done.31 = bf16[2,64,1152]{2,1,0:T(8,128)(2,1)S(1)} collective-permute-done((bf16[2,64,1152]{2,1,0:T(8,128)(2,1)S(1)}, bf16[2,64,1152]{2,1,0:T(8,128)(2,1)S(1)}, u32[]{:S(2)}, u32[]{:S(2)}) %collective-permute-start.31) | collective-permute-done | bytes 294944 | tf_op jit(solution)/shard_map/ppermute | solution.py:375
  466.3 4.2 collective-permute-start.29
  470.5 6.4 collective-permute-done.32
  480.0 13.1 %collective-permute-done.29 = bf16[256,2048]{1,0:T(8,128)(2,1)S(1)} collective-permute-done((bf16[256,2048]{1,0:T(8,128)(2,1)S(1)}, bf16[256,2048]{1,0:T(8,128)(2,1)S(1)}, u32[]{:S(2)}, u32[]{:S(2)}) %collective-permute-start.29) | collective-permute-done | bytes 1048608 | tf_op jit(solution)/shard_map/ppermute | solution.py:434
  503.1 12.9 %last.2 = (bf16[512,512]{1,0:T(8,128)(2,1)S(1)}, bf16[512,512]{1,0:T(8,128)(2,1)S(1)}, bf16[512,64]{1,0:T(8,128)(2,1)S(1)}, bf16[512,2048]{1,0:T(8,128)(2,1)}, f...) custom-call(f32[2,64,1024]{2,1,0:T(8,128)S(1)} %copy-done.5, bf16[1024,512]{1,0:T(8,128)(2,1)S(1)} %copy-done.1, ...), custom_call_target="tpu_custom_call" | custom-call | flops 3355443200 | bytes 19922944 | tf_op jit(solution)/shard_map/last/pallas_call | solution.py:614
  518.4 4.2 fusion.53
  522.6 13.0 %last.3 = (bf16[512,512]{1,0:T(8,128)(2,1)S(1)}, bf16[512,512]{1,0:T(8,128)(2,1)S(1)}, bf16[512,64]{1,0:T(8,128)(2,1)S(1)}, bf16[512,2048]{1,0:T(8,128)(2,1)}, f...) custom-call(f32[2,64,1024]{2,1,0:T(8,128)S(1)} %copy-done.6, bf16[1024,512]{1,0:T(8,128)(2,1)S(1)} %copy-done.1, ...), custom_call_target="tpu_custom_call" | custom-call | flops 3355443200 | bytes 19922944 | tf_op jit(solution)/shard_map/last/pallas_call | solution.py:614
  537.2 7.9 %collective-permute-start.34 = (bf16[256,2048]{1,0:T(8,128)(2,1)}, bf16[256,2048]{1,0:T(8,128)(2,1)S(1)}, u32[]{:S(2)}, u32[]{:S(2)}) collective-permute-start(bf16[256,2048]{1,0:T(8,128)(2,1)} %get-tuple-element.331), channel_id=1, source_target_pairs={{0,1},{3,2},{1,0},{2,3},{4,5},{7,6},{5,4},{6,7},{8,9},{11,10},{9,8... | collective-permute-start | bytes 3145736 | tf_op jit(solution)/shard_map/ppermute | solution.py:434
  545.4 3.3 fusion.52
  548.7 19.2 %collective-permute-done.34 = bf16[256,2048]{1,0:T(8,128)(2,1)S(1)} collective-permute-done((bf16[256,2048]{1,0:T(8,128)(2,1)}, bf16[256,2048]{1,0:T(8,128)(2,1)S(1)}, u32[]{:S(2)}, u32[]{:S(2)}) %collective-permute-start.34) | collective-permute-done | bytes 1048608 | tf_op jit(solution)/shard_map/ppermute | solution.py:434
  569.9 6.4 collective-permute-start.36
  576.4 14.1 %attn_grads.1 = (bf16[2048,2048]{1,0:T(8,128)(2,1)}, bf16[2048,64]{1,0:T(8,128)(2,1)S(1)}) custom-call(bf16[1024,2048]{1,0:T(8,128)(2,1)} %get-tuple-element.349.refs_0_, bf16[512,2048]{1,0:T(8,128)(2,1)} %get-tuple-element.350.refs_1_, bf16[512,2048]{1,0:T(8,128)(2,1)} %get-tuple-element.351.refs_2_, bf16[512,512]{1,0:T(8,128)(2,1)S(1)} %copy-done.39, ...), custom_call_target="tpu_custom_call" | custom-call | flops 8858370048 | bytes 20971520 | tf_op jit(solution)/shard_map/attn_grads/pallas_call | solution.py:716
  591.8 4.1 collective-permute-done.36
  597.8 3.1 broadcast_select_fusion.9
  601.1 3.1 broadcast_select_fusion.7
  605.9 3.3 broadcast_select_fusion.6
  611.3 2.9 copy.57
  614.2 14.3 %collective-permute-done.41 = bf16[256,2048]{1,0:T(8,128)(2,1)} collective-permute-done((bf16[256,2048]{1,0:T(8,128)(2,1)}, bf16[256,2048]{1,0:T(8,128)(2,1)}, u32[]{:S(2)}, u32[]{:S(2)}) %collective-permute-start.41) | collective-permute-done | bytes 1048608 | tf_op jit(solution)/shard_map/ppermute | solution.py:434
  628.6 2.3 broadcast_select_fusion.5
  630.9 2.7 broadcast_select_fusion.4
  638.1 3.5 add_convert_fusion.1
  641.6 14.3 %collective-permute-done.45 = f32[256]{0:T(256)S(1)} collective-permute-done((f32[256]{0:T(256)S(1)}, f32[256]{0:T(256)S(1)}, u32[]{:S(2)}, u32[]{:S(2)}) %collective-permute-start.45) | collective-permute-done | bytes 1056 | tf_op jit(solution)/shard_map/ppermute | solution.py:762
  668.6 14.1 %collective-permute-done.39 = bf16[256,2048]{1,0:T(8,128)(2,1)S(1)} collective-permute-done((bf16[256,2048]{1,0:T(8,128)(2,1)S(1)}, bf16[256,2048]{1,0:T(8,128)(2,1)S(1)}, u32[]{:S(2)}, u32[]{:S(2)}) %collective-permute-start.39) | collective-permute-done | bytes 1048608 | tf_op jit(solution)/shard_map/ppermute | solution.py:434
  692.4 2.4 pad_maximum_fusion.1
  694.8 20.7 %collective-permute-done.43 = bf16[256,2048]{1,0:T(8,128)(2,1)S(1)} collective-permute-done((bf16[256,2048]{1,0:T(8,128)(2,1)S(1)}, bf16[256,2048]{1,0:T(8,128)(2,1)S(1)}, u32[]{:S(2)}, u32[]{:S(2)}) %collective-permute-start.43) | collective-permute-done | bytes 1048608 | tf_op jit(solution)/shard_map/ppermute | solution.py:434
  715.6 16.5 %collective-permute-done.44 = bf16[256,2048]{1,0:T(8,128)(2,1)S(1)} collective-permute-done((bf16[256,2048]{1,0:T(8,128)(2,1)S(1)}, bf16[256,2048]{1,0:T(8,128)(2,1)S(1)}, u32[]{:S(2)}, u32[]{:S(2)}) %collective-permute-start.44) | collective-permute-done | bytes 1048608 | tf_op jit(solution)/shard_map/ppermute | solution.py:434
  736.5 4.0 pad_maximum_fusion
  (446 shorter events, 142.9 us)
Async XLA Ops:
  7.2 211.8 %all-gather.3.cloned.1.call-start = ((), (), s32[]{:S(2)}) async-start(), calls=%async_computation.6 | async-start | bytes 19464192 | tf_op jit(solution)/shard_map/all_gather | solution.py:491
  12.4 485.1 %reduce-scatter.4.cloned.1.call-start = ((), (), s32[]{:S(2)}) async-start(), calls=%async_computation.3 | async-start | bytes 19464192 | tf_op jit(solution)/shard_map/reduce_scatter | solution.py:689
  12.4 22.3 %collective-permute-start = (bf16[128,2048]{1,0:T(8,128)(2,1)}, bf16[128,2048]{1,0:T(8,128)(2,1)}, u32[]{:S(2)}, u32[]{:S(2)}) collective-permute-start(bf16[128,2048]{1,0:T(8,128)(2,1)} %constant_dynamic-slice_fusion), channel_id=1, source_target_pairs={{0,1},{1,2},{2,3},{3,0},{4,5},{5,6},{6,7},{7,4},{8,9},{9,10},{10,1... | collective-permute-start | bytes 1572872 | tf_op jit(solution)/shard_map/ppermute | solution.py:402
  32.9 46.6 %copy-start.35 = (f32[2,64,128]{2,1,0:T(8,128)}, f32[2,64,128]{2,1,0:T(8,128)S(1)}, u32[]{:S(2)}) copy-start(f32[2,64,128]{2,1,0:T(8,128)S(1)} %get-tuple-element.207) | copy-start | bytes 196612
  32.9 115.3 %copy-start = (bf16[1024,512]{1,0:T(8,128)(2,1)}, bf16[1024,512]{1,0:T(8,128)(2,1)S(1)}, u32[]{:S(2)}) copy-start(bf16[1024,512]{1,0:T(8,128)(2,1)S(1)} %get-tuple-element.203.k_ref) | copy-start | bytes 3145732
  32.9 115.3 %copy-start.4 = (bf16[1024,512]{1,0:T(8,128)(2,1)}, bf16[1024,512]{1,0:T(8,128)(2,1)S(1)}, u32[]{:S(2)}) copy-start(bf16[1024,512]{1,0:T(8,128)(2,1)S(1)} %get-tuple-element.202.q_ref) | copy-start | bytes 3145732
  33.9 71.1 %copy-start.118 = (pred[128]{0:T(512)(128)(4,1)}, pred[128]{0:T(512)(128)(4,1)S(1)}, u32[]{:S(2)}) copy-start(pred[128]{0:T(512)(128)(4,1)S(1)} %iota_compare_fusion) | copy-start | bytes 388
  34.7 2.7 collective-permute-start.1
  34.7 26.8 %collective-permute-start.2 = (bf16[128,2048]{1,0:T(8,128)(2,1)}, bf16[128,2048]{1,0:T(8,128)(2,1)}, u32[]{:S(2)}, u32[]{:S(2)}) collective-permute-start(bf16[128,2048]{1,0:T(8,128)(2,1)} %constant_dynamic-slice_fusion), channel_id=1, source_target_pairs={{0,2},{1,3},{2,0},{3,1},{4,6},{5,7},{6,4},{7,5},{8,10},{9,11},{10,... | collective-permute-start | bytes 1572872 | tf_op jit(solution)/shard_map/ppermute | solution.py:402
  61.5 16.0 %collective-permute-start.3 = (bf16[2,64,1152]{2,1,0:T(8,128)(2,1)}, bf16[2,64,1152]{2,1,0:T(8,128)(2,1)}, u32[]{:S(2)}, u32[]{:S(2)}) collective-permute-start(bf16[2,64,1152]{2,1,0:T(8,128)(2,1)} %pad_maximum_fusion.13), channel_id=1, source_target_pairs={{0,8},{4,12},{8,0},{12,4},{16,24},{20,28},{24,16},{28,20},{1,9},{5... | collective-permute-start | bytes 884744 | tf_op jit(solution)/shard_map/ppermute | solution.py:375
  63.0 21.5 %collective-permute-start.8 = (bf16[128,2048]{1,0:T(8,128)(2,1)}, bf16[128,2048]{1,0:T(8,128)(2,1)}, u32[]{:S(2)}, u32[]{:S(2)}) collective-permute-start(bf16[128,2048]{1,0:T(8,128)(2,1)} %constant_dynamic-slice_fusion), channel_id=1, source_target_pairs={{0,3},{1,0},{2,1},{3,2},{4,7},{5,4},{6,5},{7,6},{8,11},{9,8},{10,9... | collective-permute-start | bytes 1572872 | tf_op jit(solution)/shard_map/ppermute | solution.py:402
  83.0 16.0 %collective-permute-start.4 = (bf16[2,64,1152]{2,1,0:T(8,128)(2,1)}, bf16[2,64,1152]{2,1,0:T(8,128)(2,1)}, u32[]{:S(2)}, u32[]{:S(2)}) collective-permute-start(bf16[2,64,1152]{2,1,0:T(8,128)(2,1)} %pad_maximum_fusion.14), channel_id=1, source_target_pairs={{0,16},{4,20},{8,24},{12,28},{16,0},{20,4},{24,8},{28,12},{1,17},{... | collective-permute-start | bytes 884744 | tf_op jit(solution)/shard_map/ppermute | solution.py:375
  87.2 57.6 %collective-permute-start.9 = (bf16[3,128,2048]{2,1,0:T(8,128)(2,1)}, bf16[3,128,2048]{2,1,0:T(8,128)(2,1)}, u32[]{:S(2)}, u32[]{:S(2)}) collective-permute-start(bf16[3,128,2048]{2,1,0:T(8,128)(2,1)} %pad_maximum_fusion.7.refs_7_), channel_id=1, source_target_pairs={{0,8},{4,12},{8,0},{12,4},{16,24},{20,28},{24,16},{28,20},{1,9},{5... | collective-permute-start | bytes 4718600 | tf_op jit(solution)/shard_map/ppermute | solution.py:512
  113.1 14.4 %collective-permute-start.5 = (bf16[512,512]{1,0:T(8,128)(2,1)}, bf16[512,512]{1,0:T(8,128)(2,1)S(1)}, u32[]{:S(2)}, u32[]{:S(2)}) collective-permute-start(bf16[512,512]{1,0:T(8,128)(2,1)} %get-tuple-element.211.refs_0_.refs_9_), channel_id=1, source_target_pairs={{0,1},{1,2},{2,3},{3,0},{4,5},{5,6},{6,7},{7,4},{8,9},{9,10},{10,1... | collective-permute-start | bytes 1572872 | tf_op jit(solution)/shard_map/ppermute | solution.py:402
  113.1 93.9 %collective-permute-start.10 = (bf16[3,128,2048]{2,1,0:T(8,128)(2,1)}, bf16[3,128,2048]{2,1,0:T(8,128)(2,1)}, u32[]{:S(2)}, u32[]{:S(2)}) collective-permute-start(bf16[3,128,2048]{2,1,0:T(8,128)(2,1)} %pad_maximum_fusion.7.refs_7_), channel_id=1, source_target_pairs={{0,4},{4,0},{8,12},{12,8},{16,20},{20,16},{24,28},{28,24},{1,5},{5... | collective-permute-start | bytes 4718600 | tf_op jit(solution)/shard_map/ppermute | solution.py:513
  144.8 62.2 %collective-permute-start.11 = (bf16[3,128,2048]{2,1,0:T(8,128)(2,1)}, bf16[3,128,2048]{2,1,0:T(8,128)(2,1)}, u32[]{:S(2)}, u32[]{:S(2)}) collective-permute-start(bf16[3,128,2048]{2,1,0:T(8,128)(2,1)} %collective-permute-done.9.refs_8_), channel_id=1, source_target_pairs={{0,4},{4,0},{8,12},{12,8},{16,20},{20,16},{24,28},{28,24},{1,5},{5... | collective-permute-start | bytes 4718600 | tf_op jit(solution)/shard_map/ppermute | solution.py:533
  144.8 15.9 %collective-permute-start.7 = (bf16[512,512]{1,0:T(8,128)(2,1)}, bf16[512,512]{1,0:T(8,128)(2,1)}, u32[]{:S(2)}, u32[]{:S(2)}) collective-permute-start(bf16[512,512]{1,0:T(8,128)(2,1)} %get-tuple-element.211.refs_0_.refs_9_), channel_id=1, source_target_pairs={{0,3},{1,0},{2,1},{3,2},{4,7},{5,4},{6,5},{7,6},{8,11},{9,8},{10,9... | collective-permute-start | bytes 1572872 | tf_op jit(solution)/shard_map/ppermute | solution.py:402
  148.2 35.1 %collective-permute-start.6 = (bf16[512,512]{1,0:T(8,128)(2,1)}, bf16[512,512]{1,0:T(8,128)(2,1)}, u32[]{:S(2)}, u32[]{:S(2)}) collective-permute-start(bf16[512,512]{1,0:T(8,128)(2,1)} %get-tuple-element.211.refs_0_.refs_9_), channel_id=1, source_target_pairs={{0,2},{1,3},{2,0},{3,1},{4,6},{5,7},{6,4},{7,5},{8,10},{9,11},{10,... | collective-permute-start | bytes 1572872 | tf_op jit(solution)/shard_map/ppermute | solution.py:402
  149.3 57.7 %copy-start.59 = (f32[2048]{0:T(1024)S(1)}, f32[2048]{0:T(1024)}, u32[]{:S(2)}) copy-start(f32[2048]{0:T(1024)} %param.21) | copy-start | bytes 24580
  149.3 57.7 %copy-start.65 = (bf16[512,512]{1,0:T(8,128)(2,1)S(1)}, bf16[512,512]{1,0:T(8,128)(2,1)}, u32[]{:S(2)}) copy-start(bf16[512,512]{1,0:T(8,128)(2,1)} %copy-done.64) | copy-start | bytes 1572868
  157.2 90.8 %collective-permute-start.15 = (bf16[512,512]{1,0:T(8,128)(2,1)}, bf16[512,512]{1,0:T(8,128)(2,1)S(1)}, u32[]{:S(2)}, u32[]{:S(2)}) collective-permute-start(bf16[512,512]{1,0:T(8,128)(2,1)} %get-tuple-element.229.refs_0_.refs_10_), channel_id=1, source_target_pairs={{0,3},{1,0},{2,1},{3,2},{4,7},{5,4},{6,5},{7,6},{8,11},{9,8},{10,9... | collective-permute-start | bytes 1572872 | tf_op jit(solution)/shard_map/ppermute | solution.py:402
  160.8 87.2 %collective-permute-start.14 = (bf16[512,512]{1,0:T(8,128)(2,1)}, bf16[512,512]{1,0:T(8,128)(2,1)S(1)}, u32[]{:S(2)}, u32[]{:S(2)}) collective-permute-start(bf16[512,512]{1,0:T(8,128)(2,1)} %get-tuple-element.229.refs_0_.refs_10_), channel_id=1, source_target_pairs={{0,2},{1,3},{2,0},{3,1},{4,6},{5,7},{6,4},{7,5},{8,10},{9,11},{10,... | collective-permute-start | bytes 1572872 | tf_op jit(solution)/shard_map/ppermute | solution.py:402
  183.3 64.7 %collective-permute-start.13 = (bf16[512,512]{1,0:T(8,128)(2,1)}, bf16[512,512]{1,0:T(8,128)(2,1)}, u32[]{:S(2)}, u32[]{:S(2)}) collective-permute-start(bf16[512,512]{1,0:T(8,128)(2,1)} %get-tuple-element.229.refs_0_.refs_10_), channel_id=1, source_target_pairs={{0,1},{1,2},{2,3},{3,0},{4,5},{5,6},{6,7},{7,4},{8,9},{9,10},{10,1... | collective-permute-start | bytes 1572872 | tf_op jit(solution)/shard_map/ppermute | solution.py:402
  246.0 31.4 %collective-permute-start.12 = (bf16[256,2048]{1,0:T(8,128)(2,1)S(1)}, bf16[256,2048]{1,0:T(8,128)(2,1)S(1)}, u32[]{:S(2)}, u32[]{:S(2)}) collective-permute-start(bf16[256,2048]{1,0:T(8,128)(2,1)S(1)} %get-tuple-element.223), channel_id=1, source_target_pairs={{0,1},{3,2},{4,5},{7,6},{8,9},{11,10},{12,13},{15,14},{16,17},{19,... | collective-permute-start | bytes 3145736 | tf_op jit(solution)/shard_map/ppermute | solution.py:434
  278.8 24.8 %collective-permute-start.17 = (bf16[256,2048]{1,0:T(8,128)(2,1)S(1)}, bf16[256,2048]{1,0:T(8,128)(2,1)}, u32[]{:S(2)}, u32[]{:S(2)}) collective-permute-start(bf16[256,2048]{1,0:T(8,128)(2,1)S(1)} %get-tuple-element.239), channel_id=1, source_target_pairs={{0,1},{3,2},{4,5},{7,6},{8,9},{11,10},{12,13},{15,14},{16,17},{19,... | collective-permute-start | bytes 3145736 | tf_op jit(solution)/shard_map/ppermute | solution.py:434
  281.1 24.6 %collective-permute-start.16 = (bf16[256,2048]{1,0:T(8,128)(2,1)}, bf16[256,2048]{1,0:T(8,128)(2,1)S(1)}, u32[]{:S(2)}, u32[]{:S(2)}) collective-permute-start(bf16[256,2048]{1,0:T(8,128)(2,1)} %add_convert_fusion.25), channel_id=1, source_target_pairs={{1,2},{2,1},{5,6},{6,5},{9,10},{10,9},{13,14},{14,13},{17,18},{18,... | collective-permute-start | bytes 3145736 | tf_op jit(solution)/shard_map/ppermute | solution.py:434
  303.6 29.4 %copy-start.19 = (bf16[256,2048]{1,0:T(8,128)(2,1)}, bf16[256,2048]{1,0:T(8,128)(2,1)S(1)}, u32[]{:S(2)}) copy-start(bf16[256,2048]{1,0:T(8,128)(2,1)S(1)} %get-tuple-element.251) | copy-start | bytes 3145732
  306.7 25.0 %collective-permute-start.19 = (bf16[256,2048]{1,0:T(8,128)(2,1)S(1)}, bf16[256,2048]{1,0:T(8,128)(2,1)S(1)}, u32[]{:S(2)}, u32[]{:S(2)}) collective-permute-start(bf16[256,2048]{1,0:T(8,128)(2,1)S(1)} %broadcast_select_fusion.20), channel_id=1, source_target_pairs={{0,1},{3,2},{1,0},{2,3},{4,5},{7,6},{5,4},{6,7},{8,9},{11,10},{9,8... | collective-permute-start | bytes 3145736 | tf_op jit(solution)/shard_map/ppermute | solution.py:434
  310.2 22.9 %collective-permute-start.18 = (bf16[256,2048]{1,0:T(8,128)(2,1)S(1)}, bf16[256,2048]{1,0:T(8,128)(2,1)S(1)}, u32[]{:S(2)}, u32[]{:S(2)}) collective-permute-start(bf16[256,2048]{1,0:T(8,128)(2,1)S(1)} %add_convert_fusion.23), channel_id=1, source_target_pairs={{1,2},{2,1},{5,6},{6,5},{9,10},{10,9},{13,14},{14,13},{17,18},{18,... | collective-permute-start | bytes 3145736 | tf_op jit(solution)/shard_map/ppermute | solution.py:434
  319.1 128.1 %copy-start.12 = (bf16[256,2048]{1,0:T(8,128)(2,1)}, bf16[256,2048]{1,0:T(8,128)(2,1)S(1)}, u32[]{:S(2)}) copy-start(bf16[256,2048]{1,0:T(8,128)(2,1)S(1)} %get-tuple-element.303) | copy-start | bytes 3145732
  334.7 36.0 %collective-permute-start.20 = (bf16[256,2048]{1,0:T(8,128)(2,1)}, bf16[256,2048]{1,0:T(8,128)(2,1)}, u32[]{:S(2)}, u32[]{:S(2)}) collective-permute-start(bf16[256,2048]{1,0:T(8,128)(2,1)} %add_convert_fusion.21), channel_id=1, source_target_pairs={{1,2},{2,1},{5,6},{6,5},{9,10},{10,9},{13,14},{14,13},{17,18},{18,... | collective-permute-start | bytes 3145736 | tf_op jit(solution)/shard_map/ppermute | solution.py:434
  336.4 31.4 %collective-permute-start.21 = (bf16[256,2048]{1,0:T(8,128)(2,1)}, bf16[256,2048]{1,0:T(8,128)(2,1)}, u32[]{:S(2)}, u32[]{:S(2)}) collective-permute-start(bf16[256,2048]{1,0:T(8,128)(2,1)} %broadcast_select_fusion.19), channel_id=1, source_target_pairs={{0,1},{3,2},{1,0},{2,3},{4,5},{7,6},{5,4},{6,7},{8,9},{11,10},{9,8... | collective-permute-start | bytes 3145736 | tf_op jit(solution)/shard_map/ppermute | solution.py:434
  373.9 261.7 %reduce-scatter.6.cloned.1.call-start = ((), (), s32[]{:S(2)}) async-start(), calls=%async_computation.4 | async-start | bytes 884736 | tf_op jit(solution)/shard_map/reduce_scatter | solution.py:756
  373.9 22.3 %collective-permute-start.23 = (bf16[256,2048]{1,0:T(8,128)(2,1)}, bf16[256,2048]{1,0:T(8,128)(2,1)S(1)}, u32[]{:S(2)}, u32[]{:S(2)}) collective-permute-start(bf16[256,2048]{1,0:T(8,128)(2,1)} %broadcast_select_fusion.18), channel_id=1, source_target_pairs={{0,1},{3,2},{1,0},{2,3},{4,5},{7,6},{5,4},{6,7},{8,9},{11,10},{9,8... | collective-permute-start | bytes 3145736 | tf_op jit(solution)/shard_map/ppermute | solution.py:434
  376.7 20.0 %collective-permute-start.22 = (bf16[256,2048]{1,0:T(8,128)(2,1)S(1)}, bf16[256,2048]{1,0:T(8,128)(2,1)S(1)}, u32[]{:S(2)}, u32[]{:S(2)}) collective-permute-start(bf16[256,2048]{1,0:T(8,128)(2,1)S(1)} %copy-done.81), channel_id=1, source_target_pairs={{1,2},{2,1},{5,6},{6,5},{9,10},{10,9},{13,14},{14,13},{17,18},{18,... | collective-permute-start | bytes 3145736 | tf_op jit(solution)/shard_map/ppermute | solution.py:434
  399.0 21.4 %collective-permute-start.25 = (bf16[256,2048]{1,0:T(8,128)(2,1)S(1)}, bf16[256,2048]{1,0:T(8,128)(2,1)S(1)}, u32[]{:S(2)}, u32[]{:S(2)}) collective-permute-start(bf16[256,2048]{1,0:T(8,128)(2,1)S(1)} %broadcast_select_fusion.17), channel_id=1, source_target_pairs={{0,1},{3,2},{1,0},{2,3},{4,5},{7,6},{5,4},{6,7},{8,9},{11,10},{9,8... | collective-permute-start | bytes 3145736 | tf_op jit(solution)/shard_map/ppermute | solution.py:434
  401.9 18.9 %collective-permute-start.24 = (bf16[256,2048]{1,0:T(8,128)(2,1)S(1)}, bf16[256,2048]{1,0:T(8,128)(2,1)S(1)}, u32[]{:S(2)}, u32[]{:S(2)}) collective-permute-start(bf16[256,2048]{1,0:T(8,128)(2,1)S(1)} %add_convert_fusion.17), channel_id=1, source_target_pairs={{1,2},{2,1},{5,6},{6,5},{9,10},{10,9},{13,14},{14,13},{17,18},{18,... | collective-permute-start | bytes 3145736 | tf_op jit(solution)/shard_map/ppermute | solution.py:434
  422.5 22.9 %collective-permute-start.26 = (bf16[256,2048]{1,0:T(8,128)(2,1)}, bf16[256,2048]{1,0:T(8,128)(2,1)S(1)}, u32[]{:S(2)}, u32[]{:S(2)}) collective-permute-start(bf16[256,2048]{1,0:T(8,128)(2,1)} %broadcast_select_fusion.14), channel_id=1, source_target_pairs={{0,1},{3,2},{1,0},{2,3},{4,5},{7,6},{5,4},{6,7},{8,9},{11,10},{9,8... | collective-permute-start | bytes 3145736 | tf_op jit(solution)/shard_map/ppermute | solution.py:434
  428.0 19.2 %collective-permute-start.27 = (bf16[256,2048]{1,0:T(8,128)(2,1)S(1)}, bf16[256,2048]{1,0:T(8,128)(2,1)S(1)}, u32[]{:S(2)}, u32[]{:S(2)}) collective-permute-start(bf16[256,2048]{1,0:T(8,128)(2,1)S(1)} %add_convert_fusion.15), channel_id=1, source_target_pairs={{1,2},{2,1},{5,6},{6,5},{9,10},{10,9},{13,14},{14,13},{17,18},{18,... | collective-permute-start | bytes 3145736 | tf_op jit(solution)/shard_map/ppermute | solution.py:434
  448.9 1.6 collective-permute-start.30
  451.3 11.8 %collective-permute-start.31 = (bf16[2,64,1152]{2,1,0:T(8,128)(2,1)S(1)}, bf16[2,64,1152]{2,1,0:T(8,128)(2,1)S(1)}, u32[]{:S(2)}, u32[]{:S(2)}) collective-permute-start(bf16[2,64,1152]{2,1,0:T(8,128)(2,1)S(1)} %pad_maximum_fusion.15), channel_id=1, source_target_pairs={{0,8},{4,12},{8,0},{12,4},{16,24},{20,28},{24,16},{28,20},{1,9},{5... | collective-permute-start | bytes 884744 | tf_op jit(solution)/shard_map/ppermute | solution.py:375
  464.0 12.9 %collective-permute-start.32 = (bf16[2,64,1152]{2,1,0:T(8,128)(2,1)S(1)}, bf16[2,64,1152]{2,1,0:T(8,128)(2,1)S(1)}, u32[]{:S(2)}, u32[]{:S(2)}) collective-permute-start(bf16[2,64,1152]{2,1,0:T(8,128)(2,1)S(1)} %pad_maximum_fusion.16), channel_id=1, source_target_pairs={{0,16},{4,20},{8,24},{12,28},{16,0},{20,4},{24,8},{28,12},{1,17},{... | collective-permute-start | bytes 884744 | tf_op jit(solution)/shard_map/ppermute | solution.py:375
  465.5 13.1 %collective-permute-start.28 = (bf16[256,2048]{1,0:T(8,128)(2,1)S(1)}, bf16[256,2048]{1,0:T(8,128)(2,1)S(1)}, u32[]{:S(2)}, u32[]{:S(2)}) collective-permute-start(bf16[256,2048]{1,0:T(8,128)(2,1)S(1)} %copy-done.92), channel_id=1, source_target_pairs={{1,2},{2,1},{5,6},{6,5},{9,10},{10,9},{13,14},{14,13},{17,18},{18,... | collective-permute-start | bytes 3145736 | tf_op jit(solution)/shard_map/ppermute | solution.py:434
  466.3 26.8 %collective-permute-start.29 = (bf16[256,2048]{1,0:T(8,128)(2,1)S(1)}, bf16[256,2048]{1,0:T(8,128)(2,1)S(1)}, u32[]{:S(2)}, u32[]{:S(2)}) collective-permute-start(bf16[256,2048]{1,0:T(8,128)(2,1)S(1)} %copy-done.106), channel_id=1, source_target_pairs={{0,1},{3,2},{1,0},{2,3},{4,5},{7,6},{5,4},{6,7},{8,9},{11,10},{9,8... | collective-permute-start | bytes 3145736 | tf_op jit(solution)/shard_map/ppermute | solution.py:434
  497.5 20.8 %collective-permute-start.33 = (bf16[256,2048]{1,0:T(8,128)(2,1)}, bf16[256,2048]{1,0:T(8,128)(2,1)}, u32[]{:S(2)}, u32[]{:S(2)}) collective-permute-start(bf16[256,2048]{1,0:T(8,128)(2,1)} %add_convert_fusion.11), channel_id=1, source_target_pairs={{1,2},{2,1},{5,6},{6,5},{9,10},{10,9},{13,14},{14,13},{17,18},{18,... | collective-permute-start | bytes 3145736 | tf_op jit(solution)/shard_map/ppermute | solution.py:434
  537.2 30.6 %collective-permute-start.34 = (bf16[256,2048]{1,0:T(8,128)(2,1)}, bf16[256,2048]{1,0:T(8,128)(2,1)S(1)}, u32[]{:S(2)}, u32[]{:S(2)}) collective-permute-start(bf16[256,2048]{1,0:T(8,128)(2,1)} %get-tuple-element.331), channel_id=1, source_target_pairs={{0,1},{3,2},{1,0},{2,3},{4,5},{7,6},{5,4},{6,7},{8,9},{11,10},{9,8... | collective-permute-start | bytes 3145736 | tf_op jit(solution)/shard_map/ppermute | solution.py:434
  545.3 31.0 %copy-start.71 = (bf16[512,64]{1,0:T(8,128)(2,1)S(1)}, bf16[512,64]{1,0:T(8,128)(2,1)}, u32[]{:S(2)}) copy-start(bf16[512,64]{1,0:T(8,128)(2,1)} %copy-done.70) | copy-start | bytes 196612
  548.6 27.7 %copy-start.61 = (bf16[512,512]{1,0:T(8,128)(2,1)S(1)}, bf16[512,512]{1,0:T(8,128)(2,1)}, u32[]{:S(2)}) copy-start(bf16[512,512]{1,0:T(8,128)(2,1)} %copy-done.60) | copy-start | bytes 1572868
  548.6 27.7 %copy-start.63 = (bf16[512,512]{1,0:T(8,128)(2,1)S(1)}, bf16[512,512]{1,0:T(8,128)(2,1)}, u32[]{:S(2)}) copy-start(bf16[512,512]{1,0:T(8,128)(2,1)} %copy-done.62) | copy-start | bytes 1572868
  548.6 27.7 %copy-start.67 = (bf16[512,512]{1,0:T(8,128)(2,1)S(1)}, bf16[512,512]{1,0:T(8,128)(2,1)}, u32[]{:S(2)}) copy-start(bf16[512,512]{1,0:T(8,128)(2,1)} %copy-done.66) | copy-start | bytes 1572868
  548.7 27.7 %copy-start.69 = (bf16[512,512]{1,0:T(8,128)(2,1)S(1)}, bf16[512,512]{1,0:T(8,128)(2,1)}, u32[]{:S(2)}) copy-start(bf16[512,512]{1,0:T(8,128)(2,1)} %copy-done.68) | copy-start | bytes 1572868
  568.2 29.6 %collective-permute-start.35 = (bf16[256,2048]{1,0:T(8,128)(2,1)S(1)}, bf16[256,2048]{1,0:T(8,128)(2,1)}, u32[]{:S(2)}, u32[]{:S(2)}) collective-permute-start(bf16[256,2048]{1,0:T(8,128)(2,1)S(1)} %add_convert_fusion.9), channel_id=1, source_target_pairs={{1,2},{2,1},{5,6},{6,5},{9,10},{10,9},{13,14},{14,13},{17,18},{18,... | collective-permute-start | bytes 3145736 | tf_op jit(solution)/shard_map/ppermute | solution.py:434
  569.9 26.0 %collective-permute-start.36 = (bf16[256,2048]{1,0:T(8,128)(2,1)S(1)}, bf16[256,2048]{1,0:T(8,128)(2,1)}, u32[]{:S(2)}, u32[]{:S(2)}) collective-permute-start(bf16[256,2048]{1,0:T(8,128)(2,1)S(1)} %copy-done.95), channel_id=1, source_target_pairs={{0,1},{3,2},{4,5},{7,6},{8,9},{11,10},{12,13},{15,14},{16,17},{19,... | collective-permute-start | bytes 3145736 | tf_op jit(solution)/shard_map/ppermute | solution.py:434
  601.0 139.5 %reduce-scatter.8.cloned.1.call-start = ((), (), s32[]{:S(2)}) async-start(), calls=%async_computation.5 | async-start | bytes 9437184 | tf_op jit(solution)/shard_map/reduce_scatter | solution.py:757
  604.1 24.4 %collective-permute-start.41 = (bf16[256,2048]{1,0:T(8,128)(2,1)}, bf16[256,2048]{1,0:T(8,128)(2,1)}, u32[]{:S(2)}, u32[]{:S(2)}) collective-permute-start(bf16[256,2048]{1,0:T(8,128)(2,1)} %add_convert_fusion.12), channel_id=1, source_target_pairs={{1,0},{2,3},{5,4},{6,7},{9,8},{10,11},{13,12},{14,15},{17,16},{18,... | collective-permute-start | bytes 3145736 | tf_op jit(solution)/shard_map/ppermute | solution.py:434
  633.6 29.2 %collective-permute-start.37 = (bf16[256,2048]{1,0:T(8,128)(2,1)S(1)}, bf16[256,2048]{1,0:T(8,128)(2,1)S(1)}, u32[]{:S(2)}, u32[]{:S(2)}) collective-permute-start(bf16[256,2048]{1,0:T(8,128)(2,1)S(1)} %add_convert_fusion.7), channel_id=1, source_target_pairs={{1,2},{2,1},{5,6},{6,5},{9,10},{10,9},{13,14},{14,13},{17,18},{18,... | collective-permute-start | bytes 3145736 | tf_op jit(solution)/shard_map/ppermute | solution.py:434
  634.4 26.7 %collective-permute-start.38 = (bf16[256,2048]{1,0:T(8,128)(2,1)}, bf16[256,2048]{1,0:T(8,128)(2,1)}, u32[]{:S(2)}, u32[]{:S(2)}) collective-permute-start(bf16[256,2048]{1,0:T(8,128)(2,1)} %broadcast_select_fusion.9), channel_id=1, source_target_pairs={{0,1},{3,2},{1,0},{2,3},{4,5},{7,6},{5,4},{6,7},{8,9},{11,10},{9,8... | collective-permute-start | bytes 3145736 | tf_op jit(solution)/shard_map/ppermute | solution.py:434
  637.0 18.9 %collective-permute-start.45 = (f32[256]{0:T(256)S(1)}, f32[256]{0:T(256)S(1)}, u32[]{:S(2)}, u32[]{:S(2)}) collective-permute-start(f32[256]{0:T(256)S(1)} %bitcast.91), channel_id=1, source_target_pairs={{0,1},{1,0},{2,3},{3,2},{4,5},{5,4},{6,7},{7,6},{8,9},{9,8},{10,11... | collective-permute-start | bytes 3080 | tf_op jit(solution)/shard_map/ppermute | solution.py:762
  656.0 4.5 collective-permute-start.46
  663.3 19.3 %collective-permute-start.39 = (bf16[256,2048]{1,0:T(8,128)(2,1)S(1)}, bf16[256,2048]{1,0:T(8,128)(2,1)S(1)}, u32[]{:S(2)}, u32[]{:S(2)}) collective-permute-start(bf16[256,2048]{1,0:T(8,128)(2,1)S(1)} %broadcast_select_fusion.8), channel_id=1, source_target_pairs={{0,1},{3,2},{1,0},{2,3},{4,5},{7,6},{5,4},{6,7},{8,9},{11,10},{9,8... | collective-permute-start | bytes 3145736 | tf_op jit(solution)/shard_map/ppermute | solution.py:434
  664.2 18.9 %collective-permute-start.40 = (bf16[256,2048]{1,0:T(8,128)(2,1)S(1)}, bf16[256,2048]{1,0:T(8,128)(2,1)S(1)}, u32[]{:S(2)}, u32[]{:S(2)}) collective-permute-start(bf16[256,2048]{1,0:T(8,128)(2,1)S(1)} %add_convert_fusion.5), channel_id=1, source_target_pairs={{1,2},{2,1},{5,6},{6,5},{9,10},{10,9},{13,14},{14,13},{17,18},{18,... | collective-permute-start | bytes 3145736 | tf_op jit(solution)/shard_map/ppermute | solution.py:434
  683.5 6.9 collective-permute-start.42
  686.9 28.6 %collective-permute-start.43 = (bf16[256,2048]{1,0:T(8,128)(2,1)S(1)}, bf16[256,2048]{1,0:T(8,128)(2,1)S(1)}, u32[]{:S(2)}, u32[]{:S(2)}) collective-permute-start(bf16[256,2048]{1,0:T(8,128)(2,1)S(1)} %add_convert_fusion.3), channel_id=1, source_target_pairs={{1,0},{2,3},{5,4},{6,7},{9,8},{10,11},{13,12},{14,15},{17,16},{18,... | collective-permute-start | bytes 3145736 | tf_op jit(solution)/shard_map/ppermute | solution.py:434
  690.8 41.3 %collective-permute-start.44 = (bf16[256,2048]{1,0:T(8,128)(2,1)S(1)}, bf16[256,2048]{1,0:T(8,128)(2,1)S(1)}, u32[]{:S(2)}, u32[]{:S(2)}) collective-permute-start(bf16[256,2048]{1,0:T(8,128)(2,1)S(1)} %add_convert_fusion.2), channel_id=1, source_target_pairs={{1,0},{2,3},{5,4},{6,7},{9,8},{10,11},{13,12},{14,15},{17,16},{18,... | collective-permute-start | bytes 3145736 | tf_op jit(solution)/shard_map/ppermute | solution.py:434
  (107 other events, 653.3 us)
Sparse Core Ops, SparseCore 0:
  12.5 121.8 all-gather.2
  374.0 123.4 reduce-scatter.3
  601.1 33.9 reduce-scatter.5
  638.8 71.2 reduce-scatter.7

commit v2 on v1

v2 whole, which is shorter than its diff:
```python
import functools

import jax
import jax.numpy as jnp
from jax import lax
from jax.experimental import pallas as pl
from jax.experimental.pallas import tpu as pltpu
from jax.sharding import PartitionSpec as P

CHUNK = 128
TILE = 256
EPS = 1e-06
RATE = 0.5
MIB = 2**20
f32 = jnp.float32
bf16 = jnp.bfloat16
highest = lax.Precision.HIGHEST


def nn(a, b):
    return lax.dot_general(a, b, (((1,), (0,)), ((), ())), preferred_element_type=f32)


def nt(a, b):
    return lax.dot_general(a, b, (((1,), (1,)), ((), ())), preferred_element_type=f32)


def tn(a, b):
    return lax.dot_general(a, b, (((0,), (0,)), ((), ())), preferred_element_type=f32)


def exact(a, b, dims):
    return lax.dot_general(a, b, (dims, ((), ())), precision=highest, preferred_element_type=f32)


def halves(a):
    high = a.astype(bf16)
    return high, (a - high.astype(f32)).astype(bf16)


def call(name, kernel, grid, in_specs, out_specs, out_shape, scratch=(), vmem=48, cost=None):
    return pl.pallas_call(
        kernel,
        name=name,
        grid=grid,
        in_specs=in_specs,
        out_specs=out_specs,
        out_shape=out_shape,
        scratch_shapes=scratch,
        compiler_params=pltpu.CompilerParams(
            dimension_semantics=("arbitrary",) * len(grid), vmem_limit_bytes=vmem * MIB
        ),
        cost_estimate=cost,
    )


def cost(flops, data):
    return pl.CostEstimate(flops=int(flops), bytes_accessed=int(data), transcendentals=0)


def fixed(shape):
    zeros = (0,) * len(shape)
    return pl.BlockSpec(shape, lambda *_: zeros, pipeline_mode=pl.Buffered(1))


def shaped(shape, dtype):
    return jax.ShapeDtypeStruct(shape, dtype)


def triangle(lower):
    r = lax.broadcasted_iota(jnp.int32, (CHUNK, CHUNK), 0)
    c = lax.broadcasted_iota(jnp.int32, (CHUNK, CHUNK), 1)
    return r >= c if lower else r <= c


def gates(z):
    la = -RATE * lax.logistic(-z)
    y = -la
    taken = jnp.ones_like(y)
    for n in range(9, 1, -1):
        taken = 1.0 - y * (1.0 / n) * taken
    taken = y * taken
    cum = exact(triangle(True).astype(f32), la, ((1,), (0,)))
    total = exact(la, jnp.ones((CHUNK, 128), f32), ((0,), (0,)))
    return la, cum, jnp.exp(-cum) * taken, total


def project_kernel(per_part, x_ref, gain_ref, wq_ref, wk_ref, wv_ref, wf_ref, bias_ref,
                   xn_ref, q_ref, k_ref, v_ref, z_ref, s_ref, d_ref, sent_ref, state, decay):
    @pl.when(lax.rem(pl.program_id(0), per_part) == 0)
    def _():
        state[...] = jnp.zeros_like(state)
        decay[...] = jnp.zeros_like(decay)

    x = x_ref[...].astype(f32)
    r1 = lax.rsqrt(jnp.mean(x * x, axis=-1, keepdims=True) + EPS)
    xn = (x * r1 * gain_ref[...]).astype(bf16)
    xn_ref[...] = xn
    q_ref[...] = nn(xn, wq_ref[...]).astype(bf16)
    k_ref[...] = nn(xn, wk_ref[...]).astype(bf16)
    v_ref[...] = nn(xn, wv_ref[...]).astype(bf16)
    z_ref[...] = nn(xn, wf_ref[...]) + bias_ref[...]
    width = k_ref.shape[1]
    for c in range(x_ref.shape[0] // CHUNK):
        rows = pl.ds(c * CHUNK, CHUNK)
        _, _, inflow, total = gates(z_ref[rows, :])
        spread = inflow.astype(bf16)
        keep = jnp.exp(total[:, :1])
        state[:, :width] = keep * (state[:, :width] + tn(spread, k_ref[rows, :]))
        state[:, width:] = keep * (state[:, width:] + tn(spread, v_ref[rows, :]))
        decay[...] += total
    s_ref[0] = state[...]
    d_ref[0] = jnp.exp(decay[...])
    pack(sent_ref, 0, jnp.exp(decay[...]), state[...])


def read_kernel(per_part, q_ref, k_ref, v_ref, z_ref, e0_ref, o_ref, p_ref, sc_ref, e_ref, state):
    @pl.when(lax.rem(pl.program_id(0), per_part) == 0)
    def _():
        state[...] = e0_ref[0]

    width = q_ref.shape[1]
    lower = triangle(True)
    for c in range(q_ref.shape[0] // CHUNK):
        rows = pl.ds(c * CHUNK, CHUNK)
        q, k, v = q_ref[rows, :], k_ref[rows, :], v_ref[rows, :]
        _, cum, inflow, total = gates(z_ref[rows, :])
        growth = jnp.exp(cum)
        e_ref[c] = state[...]
        i_hi, i_lo = halves(inflow)
        a_hi, a_lo = halves(jnp.where(lower, nt(q, k), 0.0))
        e_hi, e_lo = halves(state[:, :width])
        scores = growth * (
            nt(q, e_hi) + nt(q, e_lo) + nn(a_hi, i_hi) + (nn(a_hi, i_lo) + nn(a_lo, i_hi))
        )
        top = jnp.exp(scores - jnp.max(scores, axis=-1, keepdims=True))
        p = top / jnp.sum(top, axis=-1, keepdims=True)
        w = (p * growth).astype(bf16)
        mixing = jnp.where(lower, nt(w, i_hi), 0.0).astype(bf16)
        o_ref[rows, :] = (nn(w, state[:, width:].astype(bf16)) + nn(mixing, v)).astype(bf16)
        p_ref[rows, :] = p
        sc_ref[rows, :] = scores
        keep = jnp.exp(total[:, :1])
        state[:, :width] = keep * (state[:, :width] + tn(i_hi, k))
        state[:, width:] = keep * (state[:, width:] + tn(i_hi, v))


def back_kernel(dhn_ref, hid_ref, cot_ref, gain_ref, wo_ref, q_ref, k_ref, v_ref, z_ref, p_ref, sc_ref, e_ref,
                dhid_ref, datt_ref, dq_ref, dkl_ref, dvl_ref, h_ref, x1_ref, g_ref, s_ref, d_ref, gg_ref, state, decay):
    step = pl.program_id(0)

    @pl.when(step == 0)
    def _():
        state[...] = jnp.zeros_like(state)
        decay[...] = jnp.zeros_like(decay)
        gg_ref[...] = jnp.zeros_like(gg_ref)

    hidden = hid_ref[...]
    dhn = dhn_ref[...].astype(f32)
    r2 = lax.rsqrt(jnp.mean(hidden * hidden, axis=-1, keepdims=True) + EPS)
    gg_ref[...] += jnp.sum((dhn * hidden * r2).reshape(-1, 8, hidden.shape[1]), axis=0)
    u2 = gain_ref[...] * dhn
    dhid = (
        cot_ref[...].astype(f32)
        + r2 * u2
        - hidden * (r2 * r2 * r2) * jnp.mean(u2 * hidden, axis=-1, keepdims=True)
    )
    dhid_ref[...] = dhid
    datt = dhid.astype(bf16)
    datt_ref[...] = datt
    width = q_ref.shape[1]
    do = nt(datt, wo_ref[...]).astype(bf16)
    lower, upper = triangle(True), triangle(False)
    q, k, v = q_ref[...], k_ref[...], v_ref[...]
    _, cum, inflow, total = gates(z_ref[...])
    growth = jnp.exp(cum)
    p = p_ref[...]
    i_hi, i_lo = halves(inflow)
    b_hi, b_lo = halves(jnp.where(lower, nt(do, v), 0.0))
    ev_hi, ev_lo = halves(e_ref[0, :, width:])
    dp = growth * (nt(do, ev_hi) + nt(do, ev_lo) + nn(b_hi, i_hi) + (nn(b_hi, i_lo) + nn(b_lo, i_hi)))
    ds = p * (dp - jnp.sum(p * dp, axis=-1, keepdims=True))
    w = (p * growth).astype(bf16)
    gds = (growth * ds).astype(bf16)
    n = jnp.where(lower, nt(gds, i_hi), 0.0).astype(bf16)
    dq_ref[...] = (nn(gds, e_ref[0, :, :width].astype(bf16)) + nn(n, k)).astype(bf16)
    n_t = jnp.where(upper, nt(i_hi, gds), 0.0).astype(bf16)
    m_t = jnp.where(upper, nt(i_hi, w), 0.0).astype(bf16)
    dkl_ref[...] = nn(n_t, q)
    dvl_ref[...] = nn(m_t, do)
    h_ref[...] = ds * sc_ref[...] + p * dp
    a_t = jnp.where(upper, nt(k, q), 0.0).astype(bf16)
    b_t = jnp.where(upper, nt(v, do), 0.0).astype(bf16)
    x1_ref[...] = nn(a_t, gds) + nn(b_t, w)
    keep = jnp.exp(total[:, :1])
    g_k, g_v = tn(gds, q), tn(w, do)
    g_ref[0, :, :width] = g_k
    g_ref[0, :, width:] = g_v
    state[:, :width] = g_k + keep * state[:, :width]
    state[:, width:] = g_v + keep * state[:, width:]
    decay[...] += total
    s_ref[...] = state[...]
    d_ref[...] = jnp.exp(decay[...])


def last_kernel(l0_ref, k_ref, v_ref, z_ref, e_ref, g_ref, dkl_ref, dvl_ref, h_ref, x1_ref, dq_ref, x_ref,
                wq_ref, wk_ref, wv_ref, wf_ref, dk_ref, dv_ref, dz_ref, dxn_ref, bias_ref, gg_ref, state):
    step = pl.program_id(0)

    @pl.when(step == 0)
    def _():
        state[...] = l0_ref[...]
        gg_ref[...] = jnp.zeros_like(gg_ref)
        bias_ref[...] = jnp.zeros_like(bias_ref)

    width = k_ref.shape[1]
    low, up = triangle(True).astype(f32), triangle(False).astype(f32)
    k, v, z = k_ref[...], v_ref[...], z_ref[...]
    _, cum, inflow, total = gates(z)
    i_hi = inflow.astype(bf16)
    keep = jnp.exp(total[:, :1])
    lg = keep * state[...]
    lg_k, lg_v = lg[:, :width].astype(bf16), lg[:, width:].astype(bf16)
    dk = (dkl_ref[...] + nn(i_hi, lg_k)).astype(bf16)
    dv = (dvl_ref[...] + nn(i_hi, lg_v)).astype(bf16)
    dk_ref[...] = dk
    dv_ref[...] = dv
    x1 = x1_ref[...]
    x2 = nt(k, lg_k) + nt(v, lg_v)
    met = exact(jnp.ones((8, 2 * width), f32), lg * e_ref[0], ((1,), (1,)))
    h, r1 = h_ref[...], inflow * x1
    dla = (
        exact(up, h - r1, ((1,), (0,)))
        + r1
        + exact(low, inflow * x2, ((1,), (0,)))
        + met[:1]
        - jnp.exp(-cum) * (x1 + x2)
    )
    rate = lax.logistic(-z)
    dz = (dla * RATE * rate * (1.0 - rate)).astype(bf16)
    dz_ref[...] = dz
    bias_ref[...] += jnp.sum(dz.astype(f32).reshape(-1, 8, dz.shape[1]), axis=0)
    state[...] = g_ref[0] + lg
    dxn = nt(dq_ref[...], wq_ref[...]) + nt(dk, wk_ref[...]) + nt(dv, wv_ref[...]) + nt(dz, wf_ref[...])
    dxn_ref[...] = dxn.astype(bf16)
    x = x_ref[...].astype(f32)
    r1 = lax.rsqrt(jnp.mean(x * x, axis=-1, keepdims=True) + EPS)
    gg_ref[...] += jnp.sum((dxn * x * r1).reshape(-1, 8, x.shape[1]), axis=0)


def hidden_kernel(n_head, place_ref, *refs):
    o_refs, (x_ref, gain_ref), w_refs = refs[:n_head], refs[n_head : n_head + 2], refs[n_head + 2 : n_head + 7]
    hid_ref, hn_ref, blocks, weights, sems = refs[n_head + 7 :]
    quarter = w_refs[1].shape[1]
    copies = [pltpu.make_async_copy(w_refs[0], weights.at[0], sems.at[0])]
    for d in range(1, n_head):
        for i in range(4):
            rows = pl.ds(pl.multiple_of(place_ref[1 + i] * quarter, quarter), quarter)
            copies.append(
                pltpu.make_async_copy(w_refs[1 + i].at[d - 1], weights.at[d, rows, :], sems.at[len(copies)])
            )

    @pl.when(pl.program_id(0) == 0)
    def _():
        for copy in copies:
            copy.start()
        for copy in copies:
            copy.wait()

    for d in range(n_head):
        blocks[d] = o_refs[d][...]
    me = place_ref[0]
    attended = None
    for h in range(n_head):
        away = lax.rem(me - h + n_head, n_head)
        term = nn(blocks[away], weights[away])
        attended = term if attended is None else attended + term
    hidden = x_ref[...].astype(f32) + attended
    hid_ref[...] = hidden
    r2 = lax.rsqrt(jnp.mean(hidden * hidden, axis=-1, keepdims=True) + EPS)
    hn_ref[...] = (hidden * r2 * gain_ref[...]).astype(bf16)


def out_kernel(hid_ref, ffn_ref, *refs):
    refs[-1][0] = (hid_ref[...] + ffn_ref[...].astype(f32)).astype(bf16)


def in_grad_kernel(dhid_ref, dxn_ref, x_ref, gain_ref, *refs):
    x = x_ref[...].astype(f32)
    r1 = lax.rsqrt(jnp.mean(x * x, axis=-1, keepdims=True) + EPS)
    u1 = gain_ref[...] * dxn_ref[...].astype(f32)
    refs[-1][0] = dhid_ref[...] + r1 * u1 - x * (r1 * r1 * r1) * jnp.mean(u1 * x, axis=-1, keepdims=True)


def flat(ref):
    block = ref[...]
    return block.reshape(block.shape[0] * block.shape[1], block.shape[2])


def units_kernel(hn_ref, cot_ref, wg_ref, wu_ref, wd_ref, act_ref, dg_ref, du_ref):
    gate = nn(hn_ref[...], flat(wg_ref))
    up = nn(hn_ref[...], flat(wu_ref))
    dact = nn(cot_ref[...], flat(wd_ref))
    s = lax.logistic(gate)
    silu = gate * s
    act_ref[...] = (silu * up).astype(bf16)
    dg_ref[...] = (dact * up * s * (1.0 + gate * (1.0 - s))).astype(bf16)
    du_ref[...] = (dact * silu).astype(bf16)


def wide_kernel(pairs, *refs):
    outs = refs[2 * pairs :]
    total = nt(refs[0][...], flat(refs[pairs]))
    for i in range(1, pairs):
        total = total + nt(refs[i][...], flat(refs[pairs + i]))
    total = total.astype(bf16)
    for t, out in enumerate(outs):
        out[...] = total[t * TILE : (t + 1) * TILE]


def summed(pairs):
    total = tn(*pairs[0])
    for pair in pairs[1:]:
        total = total + tn(*pair)
    return total.astype(bf16)


def down_grad_kernel(*refs):
    cot_ref, act, out_ref = refs[0], refs[1:-1], refs[-1]
    block = summed([(cot_ref[m], a[...]) for m, a in enumerate(act)])
    out_ref[...] = block.reshape(out_ref.shape)


def wide_grad_kernel(*refs):
    out_ref = refs[-1]
    parts = (len(refs) - 2) // 3
    hn, dg, du = refs[:parts], refs[parts : 2 * parts], refs[2 * parts : 3 * parts]
    blocks, _, width, units = out_ref.shape
    for i, grads in enumerate((dg, du)):
        block = summed([(hn[m][...], grads[m][...]) for m in range(parts)])
        out_ref[:, i] = block.reshape(blocks, width, units)


def attn_grad_kernel(count, parts, *refs):
    out_ref, dzw_ref = refs[-2:]
    xn_ref = refs[0]
    datt, dq, dk, dv, dz = (refs[1 + i * count : 1 + (i + 1) * count] for i in range(5))
    o = refs[1 + 5 * count : 1 + 5 * count + parts]
    rows, width = dq[0].shape
    xn = [xn_ref[i * rows : (i + 1) * rows, :] for i in range(count)]
    for i, grads in enumerate((dq, dk, dv)):
        out_ref[:, i * width : (i + 1) * width] = summed([(x, g[...]) for x, g in zip(xn, grads)])
    each = count // parts
    o_rows = [o[i // each][(i % each) * rows : (i % each + 1) * rows, :] for i in range(count)]
    out_ref[:, 3 * width :] = summed([(d[...], r) for d, r in zip(datt, o_rows)])
    dzw_ref[...] = summed([(x, g[...]) for x, g in zip(xn, dz)])


def pack(ref, m, decay, state):
    high, low = halves(decay)
    lane = lax.broadcasted_iota(jnp.int32, decay.shape, 1)
    width = state.shape[1]
    ref[m, :, :width] = state.astype(bf16)
    ref[m, :, width:] = jnp.where(lane == 0, high.astype(f32), low.astype(f32)).astype(bf16)


def fold_kernel(parts, pieces, *refs):
    s_refs, d_refs, (s_out, d_out, sent) = refs[: parts * pieces], refs[parts * pieces : -3], refs[-3:]
    for m in range(parts):
        s, d = s_refs[m * pieces + pieces - 1][...], d_refs[m * pieces + pieces - 1][...]
        for t in reversed(range(pieces - 1)):
            here = d_refs[m * pieces + t][...]
            s, d = s_refs[m * pieces + t][...] + here[:, :1] * s, here * d
        s_out[m], d_out[m] = s, d
        pack(sent, m, d, s)


def hop_kernel(bit, after, first, final, parts, pieces, *refs):
    refs = list(refs)
    s_ref, d_ref, got_ref = refs[:3]
    refs = refs[3:]
    if not first:
        part_s_ref, part_d_ref = refs[:2]
        refs = refs[2:]
    early = (lax.axis_index("seq") & bit) == 0
    takes = early if after else jnp.logical_not(early)
    width = s_ref.shape[2]
    found = []
    for m in range(parts):
        tail = got_ref[m, :, width:].astype(f32)
        there_d, there_s = tail[:, :1] + tail[:, 1:2], got_ref[m, :, :width].astype(f32)
        s, d = s_ref[m], d_ref[m]
        there_wide = jnp.broadcast_to(there_d, d.shape)
        new_s = jnp.where(takes, s + d[:, :1] * there_s, there_s + there_d * s)
        if first:
            part_s, part_d = jnp.where(takes, there_s, 0.0), jnp.where(takes, there_wide, 1.0)
        else:
            part_s, part_d = part_s_ref[m], part_d_ref[m]
            part_s = jnp.where(takes, part_s + part_d[:, :1] * there_s, part_s)
            part_d = jnp.where(takes, part_d * there_wide, part_d)
        found.append((new_s, d * there_wide, part_s, part_d))
    if not final:
        s_out, d_out, part_s_out, part_d_out, sent = refs
        for m, (s, d, part_s, part_d) in enumerate(found):
            s_out[m], d_out[m], part_s_out[m], part_d_out[m] = s, d, part_s, part_d
            pack(sent, m, d, s)
        return
    *own, out = refs
    arriving = jnp.zeros_like(found[0][0])
    for m in reversed(range(parts)) if after else range(parts):
        s, d, part_s, part_d = found[m]
        enters = part_s + part_d[:, :1] * arriving
        arriving = s + d[:, :1] * arriving
        for t in reversed(range(pieces)) if after else range(1):
            out[m * pieces + t if after else m] = enters
            if after and t:
                here = m * pieces + t
                enters = own[here][...] + own[parts * pieces + here][:, :1] * enters


def in_vmem(name, kernel, operands, shapes):
    return pl.pallas_call(
        kernel,
        name=name,
        in_specs=[pl.BlockSpec(memory_space=pltpu.VMEM)] * len(operands),
        out_specs=[pl.BlockSpec(memory_space=pltpu.VMEM)] * len(shapes),
        out_shape=shapes,
        compiler_params=pltpu.CompilerParams(vmem_limit_bytes=48 * MIB),
        cost_estimate=cost(0, 6 * MIB),
    )(*operands)


def scan_states(n, state, decay, sent, after, own=(), pieces=1, behind=()):
    parts, slots, width = state.shape
    part, bit, hops = [], 1, 0
    while bit < n:
        if hops < len(behind):
            sent = behind_of(sent, *behind[hops])
        got = lax.ppermute(sent, "seq", [(i, i ^ bit) for i in range(n)])
        final = 2 * bit == n
        shapes = [shaped(state.shape, f32), shaped(decay.shape, f32)] * 2 + [shaped(sent.shape, bf16)]
        if final:
            shapes = [shaped((parts * pieces, slots, width), f32)]
        results = in_vmem(
            "hop",
            functools.partial(hop_kernel, bit, after, not part, final, parts, pieces),
            [state, decay, got, *part, *(own if final else ())],
            shapes,
        )
        if final:
            return results[0]
        state, decay, *part, sent = results
        bit, hops = 2 * bit, hops + 1


def turned(block, n):
    return [lax.ppermute(block, "head", [(i, (i + d) % n) for i in range(n)]) for d in range(1, n)]


def behind_of(value, *first):
    return lax.optimization_barrier((value,) + first)[0]


def join_kernel(has, *refs):
    refs = iter(refs)
    piece, outer, pair, middle, total, coming = (next(refs) if h else None for h in has)
    makes = (piece is not None, pair is not None or coming is not None, total is not None)
    new_pair, new_total, done = (next(refs) if m else None for m in makes)
    me = lax.axis_index("head")
    end = (me == 0) | (me == 3)

    def each(work):
        @pl.loop(0, TILE // 32)
        def _(i):
            work(pl.ds(pl.multiple_of(i * 32, 32), 32))

    def both(a, b, rows):
        return (a[rows, :].astype(f32) + b[rows, :].astype(f32)).astype(bf16)

    @pl.when(end)
    def _():
        def work(rows):
            if coming is not None:
                new_total[rows, :] = coming[rows, :]
            if done is not None:
                done[rows, :] = outer[rows, :]

        each(work)

    @pl.when(jnp.logical_not(end))
    def _():
        def work(rows):
            if piece is not None:
                new_pair[rows, :] = both(piece, outer, rows)
            if pair is not None:
                new_total[rows, :] = both(pair, middle, rows)
            if done is not None:
                done[rows, :] = total[rows, :]

        each(work)


class Line:
    INWARD, OUTWARD, MIDDLE = [(0, 1), (3, 2)], [(1, 0), (2, 3)], [(1, 2), (2, 1)]

    def __init__(self):
        self.piece = self.pair = self.payload = None
        self.returns = False

    def load(self, piece):
        self.piece = self.payload = piece

    def step(self, inputs):
        piece, pair, payload, returns = self.piece, self.pair, self.payload, self.returns
        values = [v for v in (payload, pair) if v is not None] + inputs
        values = list(lax.optimization_barrier(tuple(values)))
        outer = middle = None
        if payload is not None:
            payload = values.pop(0)
            way = (self.INWARD if piece is not None else []) + (self.OUTWARD if returns else [])
            outer = lax.ppermute(payload, "head", way)
        if pair is not None:
            pair = values.pop(0)
            middle = lax.ppermute(pair, "head", self.MIDDLE)
        self.waiting = (piece, outer, pair, middle, payload if returns else None)
        return values

    def join(self, coming=None):
        piece, outer, pair, middle, total = self.waiting
        if piece is None and total is None:
            outer = None
        operands = [piece, outer, pair, middle, total, coming]
        makes = [piece is not None, pair is not None or coming is not None, total is not None]
        arrays = [o for o in operands if o is not None]
        results = in_vmem(
            "join",
            functools.partial(join_kernel, [o is not None for o in operands]),
            arrays,
            [shaped(arrays[0].shape, bf16)] * sum(makes),
        )
        results = iter(results)
        self.pair, self.payload, done = (next(results) if m else None for m in makes)
        self.returns = pair is not None
        self.piece = coming
        return done


def on_device(tokens, gain_attn, w_query, w_key, w_value, w_forget, forget_bias, w_out, gain_ffn, w_gate, w_up, w_down,
              cotangent):
    parts, part_rows, width = tokens.shape
    rows = parts * part_rows
    head = w_query.shape[1]
    slots = w_forget.shape[1]
    units = w_gate.shape[1]
    n_seq, n_head = lax.axis_size("seq"), lax.axis_size("head")
    span = w_gate.shape[0]
    steps = rows // TILE
    per_part = part_rows // TILE
    chunks = TILE // CHUNK

    gain1 = gain_attn.reshape(1, width)
    gain2 = gain_ffn.reshape(1, width)
    state_scratch = pltpu.VMEM((slots, 2 * head), f32)

    def tiled(columns, back=False):
        return pl.BlockSpec((TILE, columns), (lambda i: (per_part - 1 - i, 0)) if back else (lambda i: (i, 0)))

    def at(m, columns, back=False):
        return pl.BlockSpec(
            (TILE, columns),
            (lambda i: (m * per_part + per_part - 1 - i, 0)) if back else (lambda i: (m * per_part + i, 0)),
        )

    def part_at(m, columns, back=False):
        return pl.BlockSpec(
            (None, TILE, columns), (lambda i: (m, per_part - 1 - i, 0)) if back else (lambda i: (m, i, 0))
        )

    def chunked(back=False):
        return pl.BlockSpec(
            (chunks, slots, 2 * head), (lambda i: (per_part - 1 - i, 0, 0)) if back else (lambda i: (i, 0, 0))
        )

    def state_of(m, columns):
        return pl.BlockSpec((1, slots, columns), lambda i: (m, 0, 0))

    one_state = pl.BlockSpec((1, slots, 2 * head), lambda i: (0, 0, 0))
    per_chunk = shaped((part_rows // CHUNK, slots, 2 * head), f32)

    stacked = jnp.stack([w_gate, w_up, w_down.T])
    x = tokens.reshape(rows, width)
    place = lax.axis_index("seq")
    low_bit, high_bit = place & 1, (place & 2) // 2
    quarter = head // 4
    share = lax.dynamic_slice_in_dim(w_out, (2 * high_bit + low_bit) * quarter, quarter, 0)
    x, stacked, share = lax.optimization_barrier((x, stacked, share))
    full = lax.all_gather(stacked, "seq")
    shares = turned(share, n_head)
    all_rows = lambda c: pl.BlockSpec((TILE, c), lambda i: (i, 0))
    by_part = lambda c: pl.BlockSpec((1, slots, c), lambda i: (i // per_part, 0, 0))
    xn, q, k, v, z, local, decay, sent = call(
        "project",
        functools.partial(project_kernel, per_part),
        (steps,),
        [all_rows(width), fixed((1, width))] + [fixed((width, head))] * 3 + [fixed((width, slots)), fixed((1, slots))],
        [all_rows(width), all_rows(head), all_rows(head), all_rows(head), all_rows(slots), by_part(2 * head), by_part(128),
         by_part(2 * head + 128)],
        [shaped((rows, width), bf16)] + [shaped((rows, head), bf16)] * 3
        + [shaped((rows, slots), f32), shaped((parts, slots, 2 * head), f32), shaped((parts, slots, 128), f32),
           shaped((parts, slots, 2 * head + 128), bf16)],
        [state_scratch, pltpu.VMEM((slots, 128), f32)],
        cost=cost(2 * rows * width * (3 * head + slots), 2 * rows * width * 3 + 2 * width * 3 * head),
    )(x, gain1, w_query, w_key, w_value, w_forget, forget_bias.reshape(1, slots))
    entering = scan_states(n_seq, local, decay, sent, False, behind=[(shares[0], shares[-1])])

    o, p, scores, e_chunks = [], [], [], []
    for m in range(parts):
        o_m, p_m, s_m, e_m = call(
            "read",
            functools.partial(read_kernel, per_part),
            (per_part,),
            [at(m, head)] * 3 + [at(m, slots), state_of(m, 2 * head)],
            [tiled(head), tiled(slots), tiled(slots), chunked()],
            [shaped((part_rows, head), bf16), shaped((part_rows, slots), f32), shaped((part_rows, slots), f32), per_chunk],
            [state_scratch],
            cost=cost(2 * part_rows * head * 600, 2 * part_rows * head * 4 + part_rows * slots * 64),
        )(q, k, v, z, entering)
        o.append(o_m)
        p.append(p_m)
        scores.append(s_m)
        e_chunks.append(e_m)

    turns = [turned(o_m, n_head) for o_m in o]
    held = jnp.stack(list(lax.optimization_barrier((*shares, o[0]))[: n_head - 1]))
    across = lax.ppermute(held, "seq", [(i, i ^ 2) for i in range(n_seq)])
    beside = lax.ppermute(held, "seq", [(i, i ^ 1) for i in range(n_seq)])
    beside_across = lax.ppermute(behind_of(across, *turns[0], o[1]), "seq", [(i, i ^ 1) for i in range(n_seq)])
    low_place, high_place = 2 * high_bit, 2 * (1 - high_bit)
    places = jnp.stack(
        [lax.axis_index("head"), low_place + low_bit, high_place + low_bit, low_place + 1 - low_bit,
         high_place + 1 - low_bit]
    ).astype(jnp.int32)

    def project_out(m, own):
        return call(
            "hidden",
            functools.partial(hidden_kernel, n_head),
            (per_part,),
            [pl.BlockSpec(memory_space=pltpu.SMEM)] + [tiled(head)] * n_head + [at(m, width), fixed((1, width))]
            + [pl.BlockSpec(memory_space=pl.ANY)] * 5,
            [tiled(width), tiled(width)],
            [shaped((part_rows, width), f32), shaped((part_rows, width), bf16)],
            [pltpu.VMEM((n_head, TILE, head), bf16), pltpu.VMEM((n_head, head, width), bf16),
             pltpu.SemaphoreType.DMA((4 * n_head - 3,))],
            cost=cost(2 * part_rows * width * width, part_rows * width * 10 + 2 * width * width),
        )(places, own, *turns[m], x, gain2, w_out, held, across, beside, beside_across)

    unit_tile = 256
    unit_steps = pl.cdiv(units, unit_tile)

    def weight_tile(which):
        return pl.BlockSpec((n_seq, None, span, unit_tile), lambda j: (0, which, 0, j))

    def feed(m, hn):
        unit_out = pl.BlockSpec((part_rows, unit_tile), lambda j: (0, j))
        return call(
            "units",
            units_kernel,
            (unit_steps,),
            [fixed((part_rows, width)),
             pl.BlockSpec((None, part_rows, width), lambda j: (m, 0, 0), pipeline_mode=pl.Buffered(1)),
             weight_tile(0), weight_tile(1), weight_tile(2)],
            [unit_out] * 3,
            [shaped((part_rows, units), bf16)] * 3,
            cost=cost(6 * part_rows * width * units, 4 * part_rows * width + 6 * part_rows * units + 6 * width * units),
        )(hn, cotangent, full, full, full)

    group = max(1, TILE // span)
    wide = group * span
    pieces = part_rows // TILE

    def weight_rows(which):
        return pl.BlockSpec((group, None, span, units), lambda j: (j, which, 0, 0))

    def widened(name, sources, which):
        count = len(sources)
        return call(
            name,
            functools.partial(wide_kernel, count),
            (width // wide,),
            [fixed((part_rows, units))] * count + [weight_rows(i) for i in which],
            [pl.BlockSpec((TILE, wide), lambda j: (0, j))] * pieces,
            [shaped((TILE, width), bf16)] * pieces,
            cost=cost(2 * count * part_rows * width * units,
                      2 * count * (part_rows + width) * units + 2 * part_rows * width),
        )(*sources, *([full] * count))

    def chunk_rows(m, t, columns, within=False):
        start = (0 if within else m * part_rows // CHUNK) + t * chunks
        return pl.BlockSpec((CHUNK, columns), lambda i: (start + chunks - 1 - i, 0))

    def chunk_state(t):
        return pl.BlockSpec((1, slots, 2 * head), lambda i: (t * chunks + chunks - 1 - i, 0, 0))

    def own_rows(columns):
        return pl.BlockSpec((CHUNK, columns), lambda i: (chunks - 1 - i, 0))

    def whole(shape):
        return pl.BlockSpec(shape, lambda i: (0,) * len(shape))

    def back(m, t, dhn, hidden):
        return call(
            "back",
            back_kernel,
            (chunks,),
            [own_rows(width), chunk_rows(m, t, width, True),
             pl.BlockSpec((None, CHUNK, width), lambda i: (m, t * chunks + chunks - 1 - i, 0)),
             fixed((1, width)), fixed((head, width))]
            + [chunk_rows(m, t, head)] * 3 + [chunk_rows(m, t, slots)] + [chunk_rows(m, t, slots, True)] * 2
            + [chunk_state(t)],
            [own_rows(width), own_rows(width), own_rows(head), own_rows(head), own_rows(head), own_rows(slots),
             own_rows(slots), chunk_state(0), whole((slots, 2 * head)), whole((slots, 128)), whole((8, width))],
            [shaped((TILE, width), f32), shaped((TILE, width), bf16), shaped((TILE, head), bf16),
             shaped((TILE, head), f32), shaped((TILE, head), f32), shaped((TILE, slots), f32),
             shaped((TILE, slots), f32), shaped((chunks, slots, 2 * head), f32), shaped((slots, 2 * head), f32),
             shaped((slots, 128), f32), shaped((8, width), f32)],
            [state_scratch, pltpu.VMEM((slots, 128), f32)],
            cost=cost(2 * TILE * width * head + 2 * TILE * head * 1500, TILE * width * 14 + TILE * head * 20),
        )(dhn, hidden, cotangent, gain2, w_out, q, k, v, z, p[m], scores[m], e_chunks[m])

    def last(m, t, leaving, saved):
        dq, dk_local, dv_local, h_sum, x_local, g_chunks = saved
        here = m * pieces + t
        return call(
            "last",
            last_kernel,
            (chunks,),
            [pl.BlockSpec((None, slots, 2 * head), lambda i: (here, 0, 0)), chunk_rows(m, t, head),
             chunk_rows(m, t, head), chunk_rows(m, t, slots), chunk_state(t), chunk_state(0), own_rows(head),
             own_rows(head), own_rows(slots), own_rows(slots), own_rows(head), chunk_rows(m, t, width)]
            + [fixed((width, head))] * 3 + [fixed((width, slots))],
            [own_rows(head), own_rows(head), own_rows(slots), own_rows(width), whole((8, slots)), whole((8, width))],
            [shaped((TILE, head), bf16), shaped((TILE, head), bf16), shaped((TILE, slots), bf16),
             shaped((TILE, width), bf16), shaped((8, slots), f32), shaped((8, width), f32)],
            [state_scratch],
            cost=cost(2 * TILE * width * (3 * head + slots), TILE * width * 8 + TILE * head * 20 + width * head * 6),
        )(leaving, k, v, z, e_chunks[m], g_chunks, dk_local, dv_local, h_sum, x_local, dq, x,
          w_query, w_key, w_value, w_forget)

    grads_shape = shaped((n_seq, 3, span, units), bf16)

    def down_grads(acts):
        return call(
            "down_grads",
            down_grad_kernel,
            (width // wide,),
            [pl.BlockSpec((parts, part_rows, wide), lambda j: (0, 0, j))] + [fixed((part_rows, units))] * parts,
            pl.BlockSpec((group, 1, span, units), lambda j: (j, 2, 0, 0)),
            grads_shape,
            cost=cost(2 * rows * width * units, 2 * (rows * width + rows * units + width * units)),
        )(cotangent, *acts)

    def wide_grads(normed, gates, ups, held_grads):
        return pl.pallas_call(
            wide_grad_kernel,
            name="wide_grads",
            grid=(width // wide,),
            in_specs=[pl.BlockSpec((part_rows, wide), lambda j: (0, j))] * parts
            + [fixed((part_rows, units))] * (2 * parts) + [pl.BlockSpec(memory_space=pl.ANY)],
            out_specs=pl.BlockSpec((group, 2, span, units), lambda j: (j, 0, 0, 0)),
            out_shape=grads_shape,
            input_output_aliases={3 * parts: 0},
            compiler_params=pltpu.CompilerParams(dimension_semantics=("arbitrary",), vmem_limit_bytes=48 * MIB),
            cost_estimate=cost(4 * rows * width * units, 2 * (rows * width + 2 * rows * units + 2 * width * units)),
        )(*normed, *gates, *ups, held_grads)

    line = Line()
    live = {}

    def start():
        names = list(live)
        live.update(zip(names, line.step([live[n] for n in names])))

    def end(coming=None, done=None):
        total = line.join(coming)
        if done is not None:
            live[done] = total

    backs, lasts = {}, {}
    outs, in_grads = [None], [None]
    quarter_rows = TILE // 2

    def piece_rows(m, t):
        first = m * 2 * per_part + 2 * t
        return lambda i: ((first + i) // (2 * per_part), (first + i) % (2 * per_part), 0)

    def into(name, kernel, m, t, kept, dtype, inputs, specs):
        spec = pl.BlockSpec((1, quarter_rows, width), piece_rows(m, t))
        old = [] if kept[0] is None else [kept[0]]
        kept[0] = pl.pallas_call(
            kernel,
            name=name,
            grid=(2,),
            in_specs=specs + [pl.BlockSpec(memory_space=pl.ANY)] * len(old),
            out_specs=spec,
            out_shape=shaped(tokens.shape, dtype),
            input_output_aliases={len(specs): 0} if old else {},
            compiler_params=pltpu.CompilerParams(dimension_semantics=("arbitrary",), vmem_limit_bytes=32 * MIB),
            cost_estimate=cost(0, TILE * width * 10),
        )(*inputs, *old)

    piece_spec = pl.BlockSpec((quarter_rows, width), lambda i: (i, 0))

    def finish_out(m, t):
        held_rows = pl.BlockSpec((quarter_rows, width), lambda i: (2 * t + i, 0))
        into("out", out_kernel, m, t, outs, bf16, [live["hidden", m], live.pop(("ffn", m, t))], [held_rows, piece_spec])

    def finish_grad(m, t):
        x_rows = pl.BlockSpec((quarter_rows, width), lambda i: (m * 2 * per_part + 2 * t + i, 0))
        into("in_grad", in_grad_kernel, m, t, in_grads, f32, [backs[m, t][0], live.pop(("dxn", m, t)), x, gain1],
             [piece_spec, piece_spec, x_rows, pl.BlockSpec((1, width), lambda i: (0, 0))])

    def go_back(m, t):
        backs[m, t] = back(m, t, live.pop(("dhn", m, t)), live["hidden", m])
        live["back", m, t] = backs[m, t][8]

    def go_last(m, t):
        lasts[m, t] = last(m, t, live["leaving"], backs[m, t][2:8])
        live["dxn_part", m, t] = lasts[m, t][3]

    def forward(m, own):
        live["hidden", m], live["hn", m] = project_out(m, own)
        live["act", m], live["dgate", m], live["dup", m] = feed(m, live["hn", m])

    forward(0, o[0])
    dhn_a = widened("dhn", (live["dgate", 0], live["dup", 0]), (0, 1))
    live["o", 1] = o[1]
    live["dhn_a"] = dhn_a[1]
    line.load(dhn_a[0])
    start()
    forward(1, live.pop(("o", 1)))
    end(live.pop("dhn_a"))
    start()
    live["dhn_b"], live["dhn_c"] = widened("dhn", (live["dgate", 1], live["dup", 1]), (0, 1))
    live["ffn_a"], live["ffn_b"] = widened("ffn", (live["act", 0],), (2,))
    end(live.pop("dhn_b"))
    start()
    live["ffn_c"], live["ffn_d"] = widened("ffn", (live["act", 1],), (2,))
    live["grads"] = down_grads([live["act", m] for m in range(parts)])
    end(live.pop("dhn_c"), ("dhn", 0, 0))
    start()
    live["grads"] = wide_grads(*([live[n, m] for m in range(parts)] for n in ("hn", "dgate", "dup")), live["grads"])
    for n in ("hn", "dgate", "dup", "act"):
        for m in range(parts):
            del live[n, m]
    end(live.pop("ffn_a"), ("dhn", 0, 1))
    start()
    ffn_shares = lax.psum_scatter(live.pop("grads"), "seq", scatter_dimension=0)
    go_back(0, 0)
    go_back(0, 1)
    end(live.pop("ffn_b"), ("dhn", 1, 0))
    start()
    go_back(1, 0)
    end(live.pop("ffn_c"), ("dhn", 1, 1))
    start()
    go_back(1, 1)
    every = [(m, t) for m in range(parts) for t in range(pieces)]
    for key in every:
        live.pop(("back", *key))
    own = [backs[key][8] for key in every] + [backs[key][9] for key in every]
    folded = in_vmem(
        "fold",
        functools.partial(fold_kernel, parts, pieces),
        own,
        [shaped(local.shape, f32), shaped(decay.shape, f32), shaped(sent.shape, bf16)],
    )
    live["folded"] = folded[2]
    end(live.pop("ffn_d"), ("ffn", 0, 0))
    start()
    live["leaving"] = scan_states(n_seq, folded[0], folded[1], live.pop("folded"), True, own, pieces)
    go_last(0, 0)
    end(live.pop(("dxn_part", 0, 0)), ("ffn", 0, 1))
    start()
    go_last(0, 1)
    go_last(1, 0)
    live["ffn_shares"] = ffn_shares
    end(live.pop(("dxn_part", 0, 1)), ("ffn", 1, 0))
    start()
    ffn_shares = live.pop("ffn_shares")
    go_last(1, 1)
    live.pop("leaving")
    attn_grads, forget_grads = call(
        "attn_grads",
        functools.partial(attn_grad_kernel, len(every), parts),
        (width // TILE,),
        [pl.BlockSpec((rows, TILE), lambda j: (0, j))] + [pl.BlockSpec((TILE, TILE), lambda j: (0, j))] * len(every)
        + [fixed((TILE, head))] * (3 * len(every)) + [fixed((TILE, slots))] * len(every)
        + [fixed((part_rows, head))] * parts,
        [pl.BlockSpec((TILE, 4 * head), lambda j: (j, 0)), pl.BlockSpec((TILE, slots), lambda j: (j, 0))],
        [shaped((width, 4 * head), bf16), shaped((width, slots), bf16)],
        cost=cost(2 * rows * width * (4 * head + slots), 4 * rows * width + 8 * rows * head + 8 * width * head),
    )(xn, *[backs[key][1] for key in every], *[backs[key][2] for key in every],
      *[lasts[key][i] for i in range(3) for key in every], *o)
    live["attn_grads"] = attn_grads
    bias_sum = sum(jnp.sum(n[4], 0) for n in lasts.values())
    gain1_sum = sum(jnp.sum(n[5], 0) for n in lasts.values())
    gain2_sum = sum(jnp.sum(n[10], 0) for n in backs.values())
    small = jnp.concatenate(
        [
            forget_grads,
            gain2_sum.astype(bf16)[:, None],
            gain1_sum.astype(bf16)[:, None],
            jnp.zeros((width, 128 - 2 - slots % 128), bf16),
        ],
        1,
    ).reshape(n_seq, span, -1)
    bias_row = jnp.pad(jnp.stack(halves(bias_sum)), ((0, 14), (0, small.shape[2] - slots)))
    live["small"] = jnp.concatenate([small, jnp.broadcast_to(bias_row, (n_seq,) + bias_row.shape)], 1)
    end(live.pop(("dxn_part", 1, 0)), ("ffn", 1, 1))
    start()
    small_shares = lax.psum_scatter(live.pop("small"), "seq", scatter_dimension=0).astype(f32)
    attn_shares = lax.psum_scatter(live.pop("attn_grads"), "seq", scatter_dimension=0, tiled=True).astype(f32)
    bias_total = small_shares[span, :slots] + small_shares[span + 1, :slots]
    gain1_total = small_shares[:span, slots + 1]
    bit = 1
    while bit < n_head:
        gain1_total = gain1_total + lax.ppermute(gain1_total, "head", [(i, i ^ bit) for i in range(n_head)])
        bit *= 2
    for t in range(pieces):
        finish_out(0, t)
    live["out"] = outs[0]
    end(live.pop(("dxn_part", 1, 1)), ("dxn", 0, 0))
    start()
    outs[0] = live.pop("out")
    for t in range(pieces):
        finish_out(1, t)
    finish_grad(0, 0)
    live["out"], live["in_grad"] = outs[0], in_grads[0]
    end(None, ("dxn", 0, 1))
    start()
    in_grads[0] = live.pop("in_grad")
    finish_grad(0, 1)
    live["in_grad"] = in_grads[0]
    end(None, ("dxn", 1, 0))
    start()
    in_grads[0] = live.pop("in_grad")
    finish_grad(1, 0)
    live["in_grad"] = in_grads[0]
    end(None, ("dxn", 1, 1))
    finish_grad(1, 1)

    return (
        live["out"],
        in_grads[0],
        gain1_total,
        attn_shares[:, :head],
        attn_shares[:, head : 2 * head],
        attn_shares[:, 2 * head : 3 * head],
        small_shares[:span, :slots],
        bias_total,
        attn_shares[:, 3 * head :].T,
        small_shares[:span, slots],
        ffn_shares[0].astype(f32),
        ffn_shares[1].astype(f32),
        ffn_shares[2].astype(f32).T,
    )


def solution(mesh):
    rows, both = P(None, "seq", None), P("seq", "head")
    by_head, down = P(None, "head"), P("head", "seq")
    return jax.shard_map(
        on_device,
        mesh=mesh,
        in_specs=(rows, P(), by_head, by_head, by_head, by_head, P("head"), P("head", None), P(), both, both, down, rows),
        out_specs=(rows, rows, P("seq"), both, both, both, both, P("head"), down, P("seq"), both, both, down),
        check_vma=False,
    )
```

time: 761 us -> 718 us (0.943)
  other arithmetic: 108 us -> 19.3 us
  local copies, waits for them, and re-layouts: 43.1 us -> 109 us
  waiting for transfers between devices: 265 us -> 200 us
  Pallas kernels: 215 us -> 279 us
  starting transfers between devices: 104 us -> 84.5 us
    unnamed x246 -> x403, local copies, waits for them, and re-layouts: 34.4 us -> 103 us
    pallas_call x6 -> x40, Pallas kernels: 95.5 us -> 163 us  [the longest x4 37.5 us: last(): call('last', last_kernel, (chunks,), [pl.BlockSpec((None, slots, 2 * head...]
    ppermute x34 -> x33, waiting for transfers between devices: 174 us -> 125 us  [the longest x14 73.3 us: step(): outer = lax.ppermute(payload, 'head', way)]
    select_n x29 -> x0, other arithmetic: 37 us -> none  [the longest x12 21.6 us: step(): done = jnp.where(self.end, outer, total) if total is not None else None]
    ppermute x9, waiting for transfers between devices: 57.5 us -> 26.9 us  [turned(): lax.ppermute(block, 'head', [(i, (i + d) % n) for i in range(n)])]
    convert_element_type x36 -> x0, other arithmetic: 29.8 us -> none  [the longest x15 18.3 us: added(): return (a.astype(f32) + b.astype(f32)).astype(bf16)]
    ppermute x9, starting transfers between devices: 38.2 us -> 17.2 us  [turned(): lax.ppermute(block, 'head', [(i, (i + d) % n) for i in range(n)])]
    ppermute x1, waiting for transfers between devices: 16.5 us -> 32.6 us  [on_device(): across = lax.ppermute(held, 'seq', [(i, i ^ 2) for i in range(n_seq)])]
  transfers between devices with their start and end apart: 51 -> 50, of which waited for: 22 -> 18; matrix products, arithmetic and copies ran while one was open for 13% -> 3% of each run, Pallas kernels for 27% -> 38%
where the time goes in v2:
time: 718 us; the launch traced here: 708 us
  Pallas kernels  279 us (39%)
  waiting for transfers between devices  200 us (28%)
  local copies, waits for them, and re-layouts  109 us (15%)
  starting transfers between devices  84.5 us (12%)
  other arithmetic  19.3 us (3%)
  between operations  16 us (2%)
    unnamed x403, local copies, waits for them, and re-layouts  103 us
    ppermute x14, waiting for transfers between devices, step(): outer = lax.ppermute(payload, 'head', way)  73.3 us
    ppermute x6, waiting for transfers between devices, scan_states(): got = lax.ppermute(sent, 'seq', [(i, i ^ bit) for i in range(n)])  52.1 us
    ppermute x14, starting transfers between devices, step(): outer = lax.ppermute(payload, 'head', way)  41.1 us
    pallas_call x4, Pallas kernels, last(): call('last', last_kernel, (chunks,), [pl.BlockSpec((None, slots, 2 * head...  37.5 us
    pallas_call x4, Pallas kernels, widened(): call(name, functools.partial(wide_kernel, count), (width // wide,), [fixe...  37.1 us
    pallas_call x4, Pallas kernels, back(): call('back', back_kernel, (chunks,), [own_rows(width), chunk_rows(m, t, w...  36.7 us
    pallas_call x21, Pallas kernels, in_vmem(): pl.pallas_call(kernel, name=name, in_specs=[pl.BlockSpec(memory_space=plt...  35.1 us
  transfers between devices with their start and end apart: 50, of which 18 were waited for; matrix products, arithmetic and copies ran while one was open for 3% of the time, Pallas kernels for 38%

profile of v2, /device:TPU:0, one launch (start us, length us, event | category | flops | bytes accessed | tf_op | source)
XLA Modules:
  0.0 708.4 jit_solution(10089592760011222385)
XLA Ops:
  11.6 3.1 collective-permute-start
  17.1 16.2 %project.1 = (bf16[1024,2048]{1,0:T(8,128)(2,1)}, bf16[1024,512]{1,0:T(8,128)(2,1)S(1)}, bf16[1024,512]{1,0:T(8,128)(2,1)S(1)}, bf16[1024,512]{1,0:T(8,128)(2,1)...) custom-call(bf16[1024,2048]{1,0:T(8,128)(2,1)} %bitcast.45, ...), custom_call_target="tpu_custom_call" | custom-call | flops 6710886400 | bytes 18874368 | tf_op jit(solution)/shard_map/project/pallas_call | solution.py:601
  34.2 5.1 collective-permute-done.1
  44.0 11.7 %collective-permute-done.3.refs_2_ = bf16[2,64,1152]{2,1,0:T(8,128)(2,1)S(1)} collective-permute-done((bf16[2,64,1152]{2,1,0:T(8,128)(2,1)S(1)}, bf16[2,64,1152]{2,1,0:T(8,128)(2,1)S(1)}, u32[]{:S(2)}, u32[]{:S(2)}) %collective-permute-start.3) | collective-permute-done | bytes 294944 | tf_op jit(solution)/shard_map/ppermute | solution.py:439
  57.5 9.9 %collective-permute-done.4.refs_2_ = bf16[2,64,1152]{2,1,0:T(8,128)(2,1)S(1)} collective-permute-done((bf16[2,64,1152]{2,1,0:T(8,128)(2,1)S(1)}, bf16[2,64,1152]{2,1,0:T(8,128)(2,1)S(1)}, u32[]{:S(2)}, u32[]{:S(2)}) %collective-permute-start.4) | collective-permute-done | bytes 294944 | tf_op jit(solution)/shard_map/ppermute | solution.py:439
  67.8 4.9 read.2
  75.6 2.3 collective-permute-start.6
  79.3 4.8 read.3
  86.6 4.4 collective-permute-done.5.refs_1_
  91.8 17.4 %collective-permute-done.6.refs_2_ = bf16[512,512]{1,0:T(8,128)(2,1)S(1)} collective-permute-done((bf16[512,512]{1,0:T(8,128)(2,1)S(1)}, bf16[512,512]{1,0:T(8,128)(2,1)S(1)}, u32[]{:S(2)}, u32[]{:S(2)}) %collective-permute-start.6) | collective-permute-done | bytes 524320 | tf_op jit(solution)/shard_map/ppermute | solution.py:457
  110.8 32.6 %collective-permute-done.9.refs_8_ = bf16[3,128,2048]{2,1,0:T(8,128)(2,1)S(1)} collective-permute-done((bf16[3,128,2048]{2,1,0:T(8,128)(2,1)}, bf16[3,128,2048]{2,1,0:T(8,128)(2,1)S(1)}, u32[]{:S(2)}, u32[]{:S(2)}) %collective-permute-start.9) | collective-permute-done | bytes 1572896 | tf_op jit(solution)/shard_map/ppermute | solution.py:635
  145.0 2.4 collective-permute-start.14
  152.4 11.2 %hidden.2 = (f32[512,2048]{1,0:T(8,128)}, bf16[512,2048]{1,0:T(8,128)(2,1)}) custom-call(s32[5]{0:T(128)S(1)} %stack.52.place_ref, bf16[512,512]{1,0:T(8,128)(2,1)S(1)} %get-tuple-element.328.refs_0_.refs_21_, bf16[512,512]{1,0:T(8,128)(2,1)S(1)} %copy-done.156, bf16[512,512]{1,0:T(8,128)(2,1)S(1)} %copy-done.158, bf16[512,512]{1,0:T(8,128)(2,1)S(1)} %copy-done.160, ...), custom_call_target="tpu_custom_call" | custom-call | flops 4294967296 | bytes 18874368 | tf_op jit(solution)/shard_map/hidden/pallas_call | solution.py:645
  163.6 15.2 %units.2 = (bf16[512,1408]{1,0:T(8,128)(2,1)S(1)}, bf16[512,1408]{1,0:T(8,128)(2,1)S(1)}, bf16[512,1408]{1,0:T(8,128)(2,1)S(1)}) custom-call(bf16[512,2048]{1,0:T(8,128)(2,1)} %get-tuple-element.405.hn_ref.refs_0_, bf16[2,512,2048]{2,1,0:T(8,128)(2,1)} %cot_ref.11, bf16[8,3,256,1408]{3,2,1,0:T(8,128)(2,1)} %bitcast.69, bf16[8,3,256,1408]{3,2,1,0:T(8,128)(2,1)} %bitcast.70, ...), custom_call_target="tpu_custom_call" | custom-call | flops 8858370048 | bytes 25821184 | tf_op jit(solution)/shard_map/units/pallas_call | solution.py:666
  178.9 10.6 %dhn.2 = (bf16[256,2048]{1,0:T(8,128)(2,1)S(1)}, bf16[256,2048]{1,0:T(8,128)(2,1)S(1)}) custom-call(bf16[512,1408]{1,0:T(8,128)(2,1)S(1)} %get-tuple-element.407.refs_0_.refs_2_, bf16[512,1408]{1,0:T(8,128)(2,1)S(1)} %get-tuple-element.409.refs_1_.refs_4_, bf16[8,3,256,1408]{3,2,1,0:T(8,128)(2,1)} %bitcast.72, bf16[8,3,256,1408]{3,2,1,0:T(8,128)(2,1)} %bitcast.73), custom_call_target="tpu_custom_call" | custom-call | flops 5905580032 | bytes 16515072 | tf_op jit(solution)/shard_map/dhn/pallas_call | solution.py:687
  189.5 3.5 collective-permute-start.12
  193.1 11.4 %hidden.3 = (f32[512,2048]{1,0:T(8,128)}, bf16[512,2048]{1,0:T(8,128)(2,1)}) custom-call(s32[5]{0:T(128)S(1)} %stack.52.place_ref, bf16[512,512]{1,0:T(8,128)(2,1)S(1)} %copy-done.153, bf16[512,512]{1,0:T(8,128)(2,1)} %collective-permute-done.13.refs_1_, bf16[512,512]{1,0:T(8,128)(2,1)} %collective-permute-done.14.refs_2_, ...), custom_call_target="tpu_custom_call" | custom-call | flops 4294967296 | bytes 18874368 | tf_op jit(solution)/shard_map/hidden/pallas_call | solution.py:645
  204.5 15.2 %units.3 = (bf16[512,1408]{1,0:T(8,128)(2,1)S(1)}, bf16[512,1408]{1,0:T(8,128)(2,1)S(1)}, bf16[512,1408]{1,0:T(8,128)(2,1)S(1)}) custom-call(bf16[512,2048]{1,0:T(8,128)(2,1)} %get-tuple-element.406.hn_ref.refs_1_, bf16[2,512,2048]{2,1,0:T(8,128)(2,1)} %cot_ref.11, bf16[8,3,256,1408]{3,2,1,0:T(8,128)(2,1)} %bitcast.74, bf16[8,3,256,1408]{3,2,1,0:T(8,128)(2,1)} %bitcast.75, ...), custom_call_target="tpu_custom_call" | custom-call | flops 8858370048 | bytes 25821184 | tf_op jit(solution)/shard_map/units/pallas_call | solution.py:666
  222.1 3.3 collective-permute-start.16
  227.2 7.8 %ffn.2 = (bf16[256,2048]{1,0:T(8,128)(2,1)S(1)}, bf16[256,2048]{1,0:T(8,128)(2,1)S(1)}) custom-call(bf16[512,1408]{1,0:T(8,128)(2,1)S(1)} %get-tuple-element.382.refs_0_.refs_1_, bf16[8,3,256,1408]{3,2,1,0:T(8,128)(2,1)} %bitcast.77), custom_call_target="tpu_custom_call" | custom-call | flops 2952790016 | bytes 9306112 | tf_op jit(solution)/shard_map/ffn/pallas_call | solution.py:687
  235.9 11.0 %dhn.3 = (bf16[256,2048]{1,0:T(8,128)(2,1)S(1)}, bf16[256,2048]{1,0:T(8,128)(2,1)S(1)}) custom-call(bf16[512,1408]{1,0:T(8,128)(2,1)S(1)} %get-tuple-element.408.refs_0_.refs_3_, bf16[512,1408]{1,0:T(8,128)(2,1)S(1)} %get-tuple-element.410.refs_1_.refs_5_, bf16[8,3,256,1408]{3,2,1,0:T(8,128)(2,1)} %bitcast.78, bf16[8,3,256,1408]{3,2,1,0:T(8,128)(2,1)} %bitcast.79), custom_call_target="tpu_custom_call" | custom-call | flops 5905580032 | bytes 16515072 | tf_op jit(solution)/shard_map/dhn/pallas_call | solution.py:687
  251.7 3.5 collective-permute-start.18
  258.3 7.8 %ffn.3 = (bf16[256,2048]{1,0:T(8,128)(2,1)S(1)}, bf16[256,2048]{1,0:T(8,128)(2,1)S(1)}) custom-call(bf16[512,1408]{1,0:T(8,128)(2,1)S(1)} %copy-done.11, bf16[8,3,256,1408]{3,2,1,0:T(8,128)(2,1)} %bitcast.80), custom_call_target="tpu_custom_call" | custom-call | flops 2952790016 | bytes 9306112 | tf_op jit(solution)/shard_map/ffn/pallas_call | solution.py:687
  267.1 11.4 %down_grads.1.refs_6_ = bf16[8,3,256,1408]{3,2,1,0:T(8,128)(2,1)} custom-call(bf16[2,512,2048]{2,1,0:T(8,128)(2,1)} %cot_ref.11, bf16[512,1408]{1,0:T(8,128)(2,1)S(1)} %get-tuple-element.382.refs_0_.refs_1_, bf16[512,1408]{1,0:T(8,128)(2,1)S(1)} %copy-done.11), custom_call_target="tpu_custom_call" | custom-call | flops 5905580032 | bytes 12845056 | tf_op jit(solution)/shard_map/down_grads/pallas_call | solution.py:753
  280.7 3.6 join.16
  285.3 2.4 collective-permute-start.20
  289.5 16.9 %wide_grads.1 = bf16[8,3,256,1408]{3,2,1,0:T(8,128)(2,1)} custom-call(bf16[512,2048]{1,0:T(8,128)(2,1)} %get-tuple-element.405.hn_ref.refs_0_, bf16[512,2048]{1,0:T(8,128)(2,1)} %get-tuple-element.406.hn_ref.refs_1_, bf16[512,1408]{1,0:T(8,128)(2,1)S(1)} %get-tuple-element.407.refs_0_.refs_2_, ...), custom_call_target="tpu_custom_call", output_to_operand_aliasing={{}: (6, {})} | custom-call | flops 11811160064 | bytes 21495808 | tf_op jit(solution)/shard_map/wide_grads/pallas_call | solution.py:764
  306.4 3.1 collective-permute-done.20.refs_1_
  309.5 3.6 join.17
  314.2 4.3 collective-permute-start.22
  319.3 9.2 %back.4 = (f32[256,2048]{1,0:T(8,128)}, bf16[256,2048]{1,0:T(8,128)(2,1)S(1)}, bf16[256,512]{1,0:T(8,128)(2,1)S(1)}, f32[256,512]{1,0:T(8,128)S(1)}, f32[256,512...) custom-call(bf16[256,2048]{1,0:T(8,128)(2,1)S(1)} %copy-done.70, ...), custom_call_target="tpu_custom_call" | custom-call | flops 930086912 | bytes 9961472 | tf_op jit(solution)/shard_map/back/pallas_call | solution.py:712
  331.7 9.9 %back.5 = (f32[256,2048]{1,0:T(8,128)}, bf16[256,2048]{1,0:T(8,128)(2,1)S(1)}, bf16[256,512]{1,0:T(8,128)(2,1)S(1)}, f32[256,512]{1,0:T(8,128)S(1)}, f32[256,512...) custom-call(bf16[256,2048]{1,0:T(8,128)(2,1)S(1)} %copy-done.72, ...), custom_call_target="tpu_custom_call" | custom-call | flops 930086912 | bytes 9961472 | tf_op jit(solution)/shard_map/back/pallas_call | solution.py:712
  343.6 2.6 join.18
  346.3 2.7 collective-permute-start.24
  349.7 8.9 %back.6 = (f32[256,2048]{1,0:T(8,128)}, bf16[256,2048]{1,0:T(8,128)(2,1)S(1)}, bf16[256,512]{1,0:T(8,128)(2,1)S(1)}, f32[256,512]{1,0:T(8,128)S(1)}, f32[256,512...) custom-call(bf16[256,2048]{1,0:T(8,128)(2,1)S(1)} %get-tuple-element, ...), custom_call_target="tpu_custom_call" | custom-call | flops 930086912 | bytes 9961472 | tf_op jit(solution)/shard_map/back/pallas_call | solution.py:712
  358.7 10.9 %collective-permute-done.24.refs_1_ = bf16[256,2048]{1,0:T(8,128)(2,1)S(1)} collective-permute-done((bf16[256,2048]{1,0:T(8,128)(2,1)S(1)}, bf16[256,2048]{1,0:T(8,128)(2,1)S(1)}, u32[]{:S(2)}, u32[]{:S(2)}) %collective-permute-start.24) | collective-permute-done | bytes 1048608 | tf_op jit(solution)/shard_map/ppermute | solution.py:521
  370.6 2.3 join.19
  373.1 4.3 collective-permute-start.26
  378.1 8.8 %back.7 = (f32[256,2048]{1,0:T(8,128)}, bf16[256,2048]{1,0:T(8,128)(2,1)S(1)}, bf16[256,512]{1,0:T(8,128)(2,1)S(1)}, f32[256,512]{1,0:T(8,128)S(1)}, f32[256,512...) custom-call(bf16[256,2048]{1,0:T(8,128)(2,1)S(1)} %get-tuple-element, ...), custom_call_target="tpu_custom_call" | custom-call | flops 930086912 | bytes 9961472 | tf_op jit(solution)/shard_map/back/pallas_call | solution.py:712
  387.6 9.6 %collective-permute-done.26.refs_1_ = bf16[256,2048]{1,0:T(8,128)(2,1)S(1)} collective-permute-done((bf16[256,2048]{1,0:T(8,128)(2,1)S(1)}, bf16[256,2048]{1,0:T(8,128)(2,1)S(1)}, u32[]{:S(2)}, u32[]{:S(2)}) %collective-permute-start.26) | collective-permute-done | bytes 1048608 | tf_op jit(solution)/shard_map/ppermute | solution.py:521
  398.2 2.4 join.20
  401.6 4.3 collective-permute-start.28
  410.0 14.7 %collective-permute-done.31.refs_2_ = bf16[2,64,1152]{2,1,0:T(8,128)(2,1)S(1)} collective-permute-done((bf16[2,64,1152]{2,1,0:T(8,128)(2,1)S(1)}, bf16[2,64,1152]{2,1,0:T(8,128)(2,1)S(1)}, u32[]{:S(2)}, u32[]{:S(2)}) %collective-permute-start.31) | collective-permute-done | bytes 294944 | tf_op jit(solution)/shard_map/ppermute | solution.py:439
  426.6 12.6 %collective-permute-done.32.refs_2_ = bf16[2,64,1152]{2,1,0:T(8,128)(2,1)S(1)} collective-permute-done((bf16[2,64,1152]{2,1,0:T(8,128)(2,1)S(1)}, bf16[2,64,1152]{2,1,0:T(8,128)(2,1)S(1)}, u32[]{:S(2)}, u32[]{:S(2)}) %collective-permute-start.32) | collective-permute-done | bytes 294944 | tf_op jit(solution)/shard_map/ppermute | solution.py:439
  439.6 9.4 %last.4 = (bf16[256,512]{1,0:T(8,128)(2,1)S(1)}, bf16[256,512]{1,0:T(8,128)(2,1)S(1)}, bf16[256,64]{1,0:T(8,128)(2,1)S(1)}, bf16[256,2048]{1,0:T(8,128)(2,1)S(1)...) custom-call(f32[4,64,1024]{2,1,0:T(8,128)S(1)} %hop.11.l0_ref, bf16[1024,512]{1,0:T(8,128)(2,1)} %copy-done.3, ...), custom_call_target="tpu_custom_call" | custom-call | flops 1677721600 | bytes 13107200 | tf_op jit(solution)/shard_map/last/pallas_call | solution.py:734
  453.1 3.7 join.21
  469.8 9.3 %last.6 = (bf16[256,512]{1,0:T(8,128)(2,1)S(1)}, bf16[256,512]{1,0:T(8,128)(2,1)S(1)}, bf16[256,64]{1,0:T(8,128)(2,1)S(1)}, bf16[256,2048]{1,0:T(8,128)(2,1)S(1)...) custom-call(f32[4,64,1024]{2,1,0:T(8,128)S(1)} %hop.11.l0_ref, bf16[1024,512]{1,0:T(8,128)(2,1)} %copy-done.3, ...), custom_call_target="tpu_custom_call" | custom-call | flops 1677721600 | bytes 13107200 | tf_op jit(solution)/shard_map/last/pallas_call | solution.py:734
  487.3 9.4 %last.5 = (bf16[256,512]{1,0:T(8,128)(2,1)S(1)}, bf16[256,512]{1,0:T(8,128)(2,1)S(1)}, bf16[256,64]{1,0:T(8,128)(2,1)S(1)}, bf16[256,2048]{1,0:T(8,128)(2,1)S(1)...) custom-call(f32[4,64,1024]{2,1,0:T(8,128)S(1)} %hop.11.l0_ref, bf16[1024,512]{1,0:T(8,128)(2,1)} %copy-done.3, ...), custom_call_target="tpu_custom_call" | custom-call | flops 1677721600 | bytes 13107200 | tf_op jit(solution)/shard_map/last/pallas_call | solution.py:734
  503.7 2.7 join.22
  509.4 2.7 collective-permute-start.35
  519.0 9.3 %last.7 = (bf16[256,512]{1,0:T(8,128)(2,1)S(1)}, bf16[256,512]{1,0:T(8,128)(2,1)S(1)}, bf16[256,64]{1,0:T(8,128)(2,1)S(1)}, bf16[256,2048]{1,0:T(8,128)(2,1)S(1)...) custom-call(f32[4,64,1024]{2,1,0:T(8,128)S(1)} %hop.11.l0_ref, bf16[1024,512]{1,0:T(8,128)(2,1)} %copy-done.3, ...), custom_call_target="tpu_custom_call" | custom-call | flops 1677721600 | bytes 13107200 | tf_op jit(solution)/shard_map/last/pallas_call | solution.py:734
  552.2 13.7 %attn_grads.1 = (bf16[2048,2048]{1,0:T(8,128)(2,1)}, bf16[2048,64]{1,0:T(8,128)(2,1)S(1)}) custom-call(bf16[1024,2048]{1,0:T(8,128)(2,1)} %get-tuple-element.531.refs_0_, bf16[256,2048]{1,0:T(8,128)(2,1)S(1)} %copy-done.146, bf16[256,2048]{1,0:T(8,128)(2,1)} %copy-done.147, bf16[256,2048]{1,0:T(8,128)(2,1)} %copy-done.148, bf16[256,2048]{1,0:T(8,128)(2,1)} %copy-done.149, ...), custom_call_target="tpu_custom_call" | custom-call | flops 8858370048 | bytes 20971520 | tf_op jit(solution)/shard_map/attn_grads/pallas_call | solution.py:892
  568.9 2.3 join.23
  578.5 2.2 copy-done.5
  583.5 15.3 %collective-permute-done.37.refs_1_ = bf16[256,2048]{1,0:T(8,128)(2,1)S(1)} collective-permute-done((bf16[256,2048]{1,0:T(8,128)(2,1)S(1)}, bf16[256,2048]{1,0:T(8,128)(2,1)S(1)}, u32[]{:S(2)}, u32[]{:S(2)}) %collective-permute-start.37) | collective-permute-done | bytes 1048608 | tf_op jit(solution)/shard_map/ppermute | solution.py:521
  598.8 2.3 join.24
  601.2 4.4 collective-permute-start.39
  612.6 13.7 %collective-permute-done.39.refs_1_ = bf16[256,2048]{1,0:T(8,128)(2,1)S(1)} collective-permute-done((bf16[256,2048]{1,0:T(8,128)(2,1)S(1)}, bf16[256,2048]{1,0:T(8,128)(2,1)S(1)}, u32[]{:S(2)}, u32[]{:S(2)}) %collective-permute-start.39) | collective-permute-done | bytes 1048608 | tf_op jit(solution)/shard_map/ppermute | solution.py:521
  635.5 20.7 %collective-permute-done.41.refs_0_ = bf16[256,2048]{1,0:T(8,128)(2,1)S(1)} collective-permute-done((bf16[256,2048]{1,0:T(8,128)(2,1)S(1)}, bf16[256,2048]{1,0:T(8,128)(2,1)S(1)}, u32[]{:S(2)}, u32[]{:S(2)}) %collective-permute-start.41) | collective-permute-done | bytes 1048608 | tf_op jit(solution)/shard_map/ppermute | solution.py:521
  661.3 4.9 collective-permute-start.44
  668.3 3.3 copy.70
  671.6 11.5 %collective-permute-done.44 = f32[256]{0:T(256)S(1)} collective-permute-done((f32[256]{0:T(256)S(1)}, f32[256]{0:T(256)S(1)}, u32[]{:S(2)}, u32[]{:S(2)}) %collective-permute-start.44) | collective-permute-done | bytes 1056 | tf_op jit(solution)/shard_map/ppermute | solution.py:927
  684.8 2.8 collective-permute-done.45
  688.2 2.2 copy-done.1
  (533 shorter events, 182.8 us)
Async XLA Ops:
  7.2 156.4 %all-gather.3.cloned.1.call-start = ((), (), s32[]{:S(2)}) async-start(), calls=%async_computation.6 | async-start | bytes 19464192 | tf_op jit(solution)/shard_map/all_gather | solution.py:597
  11.6 497.8 %reduce-scatter.4.cloned.1.call-start = ((), (), s32[]{:S(2)}) async-start(), calls=%async_computation.3 | async-start | bytes 19464192 | tf_op jit(solution)/shard_map/reduce_scatter | solution.py:858
  11.6 22.6 %collective-permute-start = (bf16[128,2048]{1,0:T(8,128)(2,1)S(1)}, bf16[128,2048]{1,0:T(8,128)(2,1)S(1)}, u32[]{:S(2)}, u32[]{:S(2)}) collective-permute-start(bf16[128,2048]{1,0:T(8,128)(2,1)S(1)} %constant_dynamic-slice_fusion), channel_id=1, source_target_pairs={{0,1},{1,2},{2,3},{3,0},{4,5},{5,6},{6,7},{7,4},{8,9},{9,10},{10,1... | collective-permute-start | bytes 1572872 | tf_op jit(solution)/shard_map/ppermute | solution.py:457
  14.7 24.6 %collective-permute-start.1 = (bf16[128,2048]{1,0:T(8,128)(2,1)S(1)}, bf16[128,2048]{1,0:T(8,128)(2,1)S(1)}, u32[]{:S(2)}, u32[]{:S(2)}) collective-permute-start(bf16[128,2048]{1,0:T(8,128)(2,1)S(1)} %constant_dynamic-slice_fusion), channel_id=1, source_target_pairs={{0,3},{1,0},{2,1},{3,2},{4,7},{5,4},{6,5},{7,6},{8,11},{9,8},{10,9... | collective-permute-start | bytes 1572872 | tf_op jit(solution)/shard_map/ppermute | solution.py:457
  34.2 45.1 %copy-start.3 = (bf16[1024,512]{1,0:T(8,128)(2,1)}, bf16[1024,512]{1,0:T(8,128)(2,1)S(1)}, u32[]{:S(2)}) copy-start(bf16[1024,512]{1,0:T(8,128)(2,1)S(1)} %get-tuple-element.310.k_ref) | copy-start | bytes 3145732
  34.2 45.1 %copy-start.7 = (bf16[1024,512]{1,0:T(8,128)(2,1)}, bf16[1024,512]{1,0:T(8,128)(2,1)S(1)}, u32[]{:S(2)}) copy-start(bf16[1024,512]{1,0:T(8,128)(2,1)S(1)} %get-tuple-element.309.q_ref) | copy-start | bytes 3145732
  39.3 28.5 %copy-start.195 = (bf16[128,2048]{1,0:T(8,128)(2,1)}, bf16[128,2048]{1,0:T(8,128)(2,1)S(1)}, u32[]{:S(2)}) copy-start(bf16[128,2048]{1,0:T(8,128)(2,1)S(1)} %collective-permute-done.1) | copy-start | bytes 1572868
  39.3 1.6 collective-permute-start.2
  41.1 14.6 %collective-permute-start.3 = (bf16[2,64,1152]{2,1,0:T(8,128)(2,1)S(1)}, bf16[2,64,1152]{2,1,0:T(8,128)(2,1)S(1)}, u32[]{:S(2)}, u32[]{:S(2)}) collective-permute-start(bf16[2,64,1152]{2,1,0:T(8,128)(2,1)S(1)} %get-tuple-element.320), channel_id=1, source_target_pairs={{0,8},{4,12},{8,0},{12,4},{16,24},{20,28},{24,16},{28,20},{1,9},{5... | collective-permute-start | bytes 884744 | tf_op jit(solution)/shard_map/ppermute | solution.py:439
  42.7 30.0 %collective-permute-start.8 = (bf16[128,2048]{1,0:T(8,128)(2,1)S(1)}, bf16[128,2048]{1,0:T(8,128)(2,1)S(1)}, u32[]{:S(2)}, u32[]{:S(2)}) collective-permute-start(bf16[128,2048]{1,0:T(8,128)(2,1)S(1)} %constant_dynamic-slice_fusion), channel_id=1, source_target_pairs={{0,2},{1,3},{2,0},{3,1},{4,6},{5,7},{6,4},{7,5},{8,10},{9,11},{10,... | collective-permute-start | bytes 1572872 | tf_op jit(solution)/shard_map/ppermute | solution.py:457
  56.0 11.5 %collective-permute-start.4 = (bf16[2,64,1152]{2,1,0:T(8,128)(2,1)S(1)}, bf16[2,64,1152]{2,1,0:T(8,128)(2,1)S(1)}, u32[]{:S(2)}, u32[]{:S(2)}) collective-permute-start(bf16[2,64,1152]{2,1,0:T(8,128)(2,1)S(1)} %get-tuple-element.325), channel_id=1, source_target_pairs={{0,16},{4,20},{8,24},{12,28},{16,0},{20,4},{24,8},{28,12},{1,17},{... | collective-permute-start | bytes 884744 | tf_op jit(solution)/shard_map/ppermute | solution.py:439
  72.7 76.5 %copy-start.150 = (bf16[512,512]{1,0:T(8,128)(2,1)}, bf16[512,512]{1,0:T(8,128)(2,1)S(1)}, u32[]{:S(2)}) copy-start(bf16[512,512]{1,0:T(8,128)(2,1)S(1)} %get-tuple-element.328.refs_0_.refs_21_) | copy-start | bytes 1572868
  74.3 74.9 %copy-start.130 = (f32[2048]{0:T(1024)S(1)}, f32[2048]{0:T(1024)}, u32[]{:S(2)}) copy-start(f32[2048]{0:T(1024)} %param.21) | copy-start | bytes 24580
  74.3 69.1 %collective-permute-start.9 = (bf16[3,128,2048]{2,1,0:T(8,128)(2,1)}, bf16[3,128,2048]{2,1,0:T(8,128)(2,1)S(1)}, u32[]{:S(2)}, u32[]{:S(2)}) collective-permute-start(bf16[3,128,2048]{2,1,0:T(8,128)(2,1)} %pad_maximum_fusion.1.refs_7_), channel_id=1, source_target_pairs={{0,8},{4,12},{8,0},{12,4},{16,24},{20,28},{24,16},{28,20},{1,9},{5... | collective-permute-start | bytes 4718600 | tf_op jit(solution)/shard_map/ppermute | solution.py:635
  74.3 16.7 %collective-permute-start.5 = (bf16[512,512]{1,0:T(8,128)(2,1)S(1)}, bf16[512,512]{1,0:T(8,128)(2,1)S(1)}, u32[]{:S(2)}, u32[]{:S(2)}) collective-permute-start(bf16[512,512]{1,0:T(8,128)(2,1)S(1)} %get-tuple-element.328.refs_0_.refs_21_), channel_id=1, source_target_pairs={{0,1},{1,2},{2,3},{3,0},{4,5},{5,6},{6,7},{7,4},{8,9},{9,10},{10,1... | collective-permute-start | bytes 1572872 | tf_op jit(solution)/shard_map/ppermute | solution.py:457
  75.6 33.5 %collective-permute-start.6 = (bf16[512,512]{1,0:T(8,128)(2,1)S(1)}, bf16[512,512]{1,0:T(8,128)(2,1)S(1)}, u32[]{:S(2)}, u32[]{:S(2)}) collective-permute-start(bf16[512,512]{1,0:T(8,128)(2,1)S(1)} %get-tuple-element.328.refs_0_.refs_21_), channel_id=1, source_target_pairs={{0,2},{1,3},{2,0},{3,1},{4,6},{5,7},{6,4},{7,5},{8,10},{9,11},{10,... | collective-permute-start | bytes 1572872 | tf_op jit(solution)/shard_map/ppermute | solution.py:457
  77.9 32.0 %collective-permute-start.7 = (bf16[512,512]{1,0:T(8,128)(2,1)S(1)}, bf16[512,512]{1,0:T(8,128)(2,1)S(1)}, u32[]{:S(2)}, u32[]{:S(2)}) collective-permute-start(bf16[512,512]{1,0:T(8,128)(2,1)S(1)} %get-tuple-element.328.refs_0_.refs_21_), channel_id=1, source_target_pairs={{0,3},{1,0},{2,1},{3,2},{4,7},{5,4},{6,5},{7,6},{8,11},{9,8},{10,9... | collective-permute-start | bytes 1572872 | tf_op jit(solution)/shard_map/ppermute | solution.py:457
  79.3 69.9 %collective-permute-start.10 = (bf16[3,128,2048]{2,1,0:T(8,128)(2,1)}, bf16[3,128,2048]{2,1,0:T(8,128)(2,1)}, u32[]{:S(2)}, u32[]{:S(2)}) collective-permute-start(bf16[3,128,2048]{2,1,0:T(8,128)(2,1)} %pad_maximum_fusion.1.refs_7_), channel_id=1, source_target_pairs={{0,4},{4,0},{8,12},{12,8},{16,20},{20,16},{24,28},{28,24},{1,5},{5... | collective-permute-start | bytes 4718600 | tf_op jit(solution)/shard_map/ppermute | solution.py:636
  143.4 5.8 collective-permute-start.11
  143.5 49.6 %collective-permute-start.13 = (bf16[512,512]{1,0:T(8,128)(2,1)}, bf16[512,512]{1,0:T(8,128)(2,1)}, u32[]{:S(2)}, u32[]{:S(2)}) collective-permute-start(bf16[512,512]{1,0:T(8,128)(2,1)} %copy-done.152), channel_id=1, source_target_pairs={{0,1},{1,2},{2,3},{3,0},{4,5},{5,6},{6,7},{7,4},{8,9},{9,10},{10,1... | collective-permute-start | bytes 1572872 | tf_op jit(solution)/shard_map/ppermute | solution.py:457
  145.0 48.1 %collective-permute-start.14 = (bf16[512,512]{1,0:T(8,128)(2,1)}, bf16[512,512]{1,0:T(8,128)(2,1)}, u32[]{:S(2)}, u32[]{:S(2)}) collective-permute-start(bf16[512,512]{1,0:T(8,128)(2,1)} %copy-done.152), channel_id=1, source_target_pairs={{0,2},{1,3},{2,0},{3,1},{4,6},{5,7},{6,4},{7,5},{8,10},{9,11},{10,... | collective-permute-start | bytes 1572872 | tf_op jit(solution)/shard_map/ppermute | solution.py:457
  147.4 45.7 %collective-permute-start.15 = (bf16[512,512]{1,0:T(8,128)(2,1)}, bf16[512,512]{1,0:T(8,128)(2,1)}, u32[]{:S(2)}, u32[]{:S(2)}) collective-permute-start(bf16[512,512]{1,0:T(8,128)(2,1)} %copy-done.152), channel_id=1, source_target_pairs={{0,3},{1,0},{2,1},{3,2},{4,7},{5,4},{6,5},{7,6},{8,11},{9,8},{10,9... | collective-permute-start | bytes 1572872 | tf_op jit(solution)/shard_map/ppermute | solution.py:457
  189.5 31.3 %collective-permute-start.12 = (bf16[256,2048]{1,0:T(8,128)(2,1)S(1)}, bf16[256,2048]{1,0:T(8,128)(2,1)}, u32[]{:S(2)}, u32[]{:S(2)}) collective-permute-start(bf16[256,2048]{1,0:T(8,128)(2,1)S(1)} %get-tuple-element.343.refs_0_), channel_id=1, source_target_pairs={{0,1},{3,2},{4,5},{7,6},{8,9},{11,10},{12,13},{15,14},{16,17},{19,... | collective-permute-start | bytes 3145736 | tf_op jit(solution)/shard_map/ppermute | solution.py:521
  222.1 26.7 %collective-permute-start.16 = (bf16[256,2048]{1,0:T(8,128)(2,1)S(1)}, bf16[256,2048]{1,0:T(8,128)(2,1)S(1)}, u32[]{:S(2)}, u32[]{:S(2)}) collective-permute-start(bf16[256,2048]{1,0:T(8,128)(2,1)S(1)} %get-tuple-element.357), channel_id=1, source_target_pairs={{0,1},{3,2},{4,5},{7,6},{8,9},{11,10},{12,13},{15,14},{16,17},{19,... | collective-permute-start | bytes 3145736 | tf_op jit(solution)/shard_map/ppermute | solution.py:521
  225.5 23.4 %collective-permute-start.17 = (bf16[256,2048]{1,0:T(8,128)(2,1)S(1)}, bf16[256,2048]{1,0:T(8,128)(2,1)}, u32[]{:S(2)}, u32[]{:S(2)}) collective-permute-start(bf16[256,2048]{1,0:T(8,128)(2,1)S(1)} %get-tuple-element.358.refs_2_), channel_id=1, source_target_pairs={{1,2},{2,1},{5,6},{6,5},{9,10},{10,9},{13,14},{14,13},{17,18},{18,... | collective-permute-start | bytes 3145736 | tf_op jit(solution)/shard_map/ppermute | solution.py:524
  251.7 26.8 %collective-permute-start.18 = (bf16[256,2048]{1,0:T(8,128)(2,1)S(1)}, bf16[256,2048]{1,0:T(8,128)(2,1)S(1)}, u32[]{:S(2)}, u32[]{:S(2)}) collective-permute-start(bf16[256,2048]{1,0:T(8,128)(2,1)S(1)} %get-tuple-element.376.refs_4_), channel_id=1, source_target_pairs={{0,1},{3,2},{1,0},{2,3},{4,5},{7,6},{5,4},{6,7},{8,9},{11,10},{9,8... | collective-permute-start | bytes 3145736 | tf_op jit(solution)/shard_map/ppermute | solution.py:521
  255.2 24.2 %collective-permute-start.19 = (bf16[256,2048]{1,0:T(8,128)(2,1)S(1)}, bf16[256,2048]{1,0:T(8,128)(2,1)}, u32[]{:S(2)}, u32[]{:S(2)}) collective-permute-start(bf16[256,2048]{1,0:T(8,128)(2,1)S(1)} %get-tuple-element.377.refs_2_), channel_id=1, source_target_pairs={{1,2},{2,1},{5,6},{6,5},{9,10},{10,9},{13,14},{14,13},{17,18},{18,... | collective-permute-start | bytes 3145736 | tf_op jit(solution)/shard_map/ppermute | solution.py:524
  285.3 24.2 %copy-start.31 = (bf16[256,2048]{1,0:T(8,128)(2,1)S(1)}, bf16[256,2048]{1,0:T(8,128)(2,1)}, u32[]{:S(2)}) copy-start(bf16[256,2048]{1,0:T(8,128)(2,1)} %copy-done.30) | copy-start | bytes 3145732
  285.3 24.2 %collective-permute-start.20 = (bf16[256,2048]{1,0:T(8,128)(2,1)}, bf16[256,2048]{1,0:T(8,128)(2,1)S(1)}, u32[]{:S(2)}, u32[]{:S(2)}) collective-permute-start(bf16[256,2048]{1,0:T(8,128)(2,1)} %get-tuple-element.395.refs_4_), channel_id=1, source_target_pairs={{0,1},{3,2},{1,0},{2,3},{4,5},{7,6},{5,4},{6,7},{8,9},{11,10},{9,8... | collective-permute-start | bytes 3145736 | tf_op jit(solution)/shard_map/ppermute | solution.py:521
  287.7 21.8 %collective-permute-start.21 = (bf16[256,2048]{1,0:T(8,128)(2,1)}, bf16[256,2048]{1,0:T(8,128)(2,1)}, u32[]{:S(2)}, u32[]{:S(2)}) collective-permute-start(bf16[256,2048]{1,0:T(8,128)(2,1)} %get-tuple-element.396.refs_2_), channel_id=1, source_target_pairs={{1,2},{2,1},{5,6},{6,5},{9,10},{10,9},{13,14},{14,13},{17,18},{18,... | collective-permute-start | bytes 3145736 | tf_op jit(solution)/shard_map/ppermute | solution.py:524
  314.2 345.7 %reduce-scatter.6.cloned.1.call-start = ((), (), s32[]{:S(2)}) async-start(), calls=%async_computation.4 | async-start | bytes 884736 | tf_op jit(solution)/shard_map/reduce_scatter | solution.py:921
  314.2 28.4 %collective-permute-start.22 = (bf16[256,2048]{1,0:T(8,128)(2,1)}, bf16[256,2048]{1,0:T(8,128)(2,1)S(1)}, u32[]{:S(2)}, u32[]{:S(2)}) collective-permute-start(bf16[256,2048]{1,0:T(8,128)(2,1)} %get-tuple-element.415.refs_4_), channel_id=1, source_target_pairs={{0,1},{3,2},{1,0},{2,3},{4,5},{7,6},{5,4},{6,7},{8,9},{11,10},{9,8... | collective-permute-start | bytes 3145736 | tf_op jit(solution)/shard_map/ppermute | solution.py:521
  318.5 24.1 %collective-permute-start.23 = (bf16[256,2048]{1,0:T(8,128)(2,1)}, bf16[256,2048]{1,0:T(8,128)(2,1)S(1)}, u32[]{:S(2)}, u32[]{:S(2)}) collective-permute-start(bf16[256,2048]{1,0:T(8,128)(2,1)} %get-tuple-element.416.refs_2_), channel_id=1, source_target_pairs={{1,2},{2,1},{5,6},{6,5},{9,10},{10,9},{13,14},{14,13},{17,18},{18,... | collective-permute-start | bytes 3145736 | tf_op jit(solution)/shard_map/ppermute | solution.py:524
  331.7 107.8 %copy-start.105 = (bf16[256,512]{1,0:T(8,128)(2,1)}, bf16[256,512]{1,0:T(8,128)(2,1)S(1)}, u32[]{:S(2)}) copy-start(bf16[256,512]{1,0:T(8,128)(2,1)S(1)} %get-tuple-element.480.dq_ref.refs_5_) | copy-start | bytes 786436
  346.3 23.3 %collective-permute-start.24 = (bf16[256,2048]{1,0:T(8,128)(2,1)S(1)}, bf16[256,2048]{1,0:T(8,128)(2,1)S(1)}, u32[]{:S(2)}, u32[]{:S(2)}) collective-permute-start(bf16[256,2048]{1,0:T(8,128)(2,1)S(1)} %get-tuple-element.431.refs_4_), channel_id=1, source_target_pairs={{0,1},{3,2},{1,0},{2,3},{4,5},{7,6},{5,4},{6,7},{8,9},{11,10},{9,8... | collective-permute-start | bytes 3145736 | tf_op jit(solution)/shard_map/ppermute | solution.py:521
  349.0 20.6 %collective-permute-start.25 = (bf16[256,2048]{1,0:T(8,128)(2,1)S(1)}, bf16[256,2048]{1,0:T(8,128)(2,1)S(1)}, u32[]{:S(2)}, u32[]{:S(2)}) collective-permute-start(bf16[256,2048]{1,0:T(8,128)(2,1)S(1)} %get-tuple-element.432.refs_2_), channel_id=1, source_target_pairs={{1,2},{2,1},{5,6},{6,5},{9,10},{10,9},{13,14},{14,13},{17,18},{18,... | collective-permute-start | bytes 3145736 | tf_op jit(solution)/shard_map/ppermute | solution.py:524
  358.7 28.7 %copy-start.131 = (f32[64,128]{1,0:T(8,128)}, f32[64,128]{1,0:T(8,128)S(1)}, u32[]{:S(2)}) copy-start(f32[64,128]{1,0:T(8,128)S(1)} %get-tuple-element.456.refs_6_.refs_11_) | copy-start | bytes 98308
  373.1 25.1 %copy-start.21 = (bf16[256,2048]{1,0:T(8,128)(2,1)S(1)}, bf16[256,2048]{1,0:T(8,128)(2,1)}, u32[]{:S(2)}) copy-start(bf16[256,2048]{1,0:T(8,128)(2,1)} %copy-done.20) | copy-start | bytes 3145732
  373.1 24.1 %collective-permute-start.26 = (bf16[256,2048]{1,0:T(8,128)(2,1)S(1)}, bf16[256,2048]{1,0:T(8,128)(2,1)S(1)}, u32[]{:S(2)}, u32[]{:S(2)}) collective-permute-start(bf16[256,2048]{1,0:T(8,128)(2,1)S(1)} %get-tuple-element.446.refs_4_), channel_id=1, source_target_pairs={{0,1},{3,2},{1,0},{2,3},{4,5},{7,6},{5,4},{6,7},{8,9},{11,10},{9,8... | collective-permute-start | bytes 3145736 | tf_op jit(solution)/shard_map/ppermute | solution.py:521
  377.3 19.9 %collective-permute-start.27 = (bf16[256,2048]{1,0:T(8,128)(2,1)S(1)}, bf16[256,2048]{1,0:T(8,128)(2,1)S(1)}, u32[]{:S(2)}, u32[]{:S(2)}) collective-permute-start(bf16[256,2048]{1,0:T(8,128)(2,1)S(1)} %get-tuple-element.447.refs_2_), channel_id=1, source_target_pairs={{1,2},{2,1},{5,6},{6,5},{9,10},{10,9},{13,14},{14,13},{17,18},{18,... | collective-permute-start | bytes 3145736 | tf_op jit(solution)/shard_map/ppermute | solution.py:524
  401.6 37.9 %copy-start.48 = (bf16[256,2048]{1,0:T(8,128)(2,1)}, bf16[256,2048]{1,0:T(8,128)(2,1)S(1)}, u32[]{:S(2)}) copy-start(bf16[256,2048]{1,0:T(8,128)(2,1)S(1)} %get-tuple-element.461.refs_2_) | copy-start | bytes 3145732
  401.6 37.9 %copy-start.49 = (bf16[256,2048]{1,0:T(8,128)(2,1)}, bf16[256,2048]{1,0:T(8,128)(2,1)S(1)}, u32[]{:S(2)}) copy-start(bf16[256,2048]{1,0:T(8,128)(2,1)S(1)} %get-tuple-element.460.refs_4_) | copy-start | bytes 3145732
  401.6 37.5 %copy-start.132 = (f32[64,128]{1,0:T(8,128)S(1)}, f32[64,128]{1,0:T(8,128)}, u32[]{:S(2)}) copy-start(f32[64,128]{1,0:T(8,128)} %copy-done.131) | copy-start | bytes 98308
  401.6 50.4 %collective-permute-start.28 = (bf16[256,2048]{1,0:T(8,128)(2,1)S(1)}, bf16[256,2048]{1,0:T(8,128)(2,1)S(1)}, u32[]{:S(2)}, u32[]{:S(2)}) collective-permute-start(bf16[256,2048]{1,0:T(8,128)(2,1)S(1)} %get-tuple-element.460.refs_4_), channel_id=1, source_target_pairs={{0,1},{3,2},{1,0},{2,3},{4,5},{7,6},{5,4},{6,7},{8,9},{11,10},{9,8... | collective-permute-start | bytes 3145736 | tf_op jit(solution)/shard_map/ppermute | solution.py:521
  405.9 46.2 %collective-permute-start.29 = (bf16[256,2048]{1,0:T(8,128)(2,1)S(1)}, bf16[256,2048]{1,0:T(8,128)(2,1)S(1)}, u32[]{:S(2)}, u32[]{:S(2)}) collective-permute-start(bf16[256,2048]{1,0:T(8,128)(2,1)S(1)} %get-tuple-element.461.refs_2_), channel_id=1, source_target_pairs={{1,2},{2,1},{5,6},{6,5},{9,10},{10,9},{13,14},{14,13},{17,18},{18,... | collective-permute-start | bytes 3145736 | tf_op jit(solution)/shard_map/ppermute | solution.py:524
  406.8 1.6 collective-permute-start.30
  408.7 16.0 %collective-permute-start.31 = (bf16[2,64,1152]{2,1,0:T(8,128)(2,1)S(1)}, bf16[2,64,1152]{2,1,0:T(8,128)(2,1)S(1)}, u32[]{:S(2)}, u32[]{:S(2)}) collective-permute-start(bf16[2,64,1152]{2,1,0:T(8,128)(2,1)S(1)} %get-tuple-element.467), channel_id=1, source_target_pairs={{0,8},{4,12},{8,0},{12,4},{16,24},{20,28},{24,16},{28,20},{1,9},{5... | collective-permute-start | bytes 884744 | tf_op jit(solution)/shard_map/ppermute | solution.py:439
  425.0 14.2 %collective-permute-start.32 = (bf16[2,64,1152]{2,1,0:T(8,128)(2,1)S(1)}, bf16[2,64,1152]{2,1,0:T(8,128)(2,1)S(1)}, u32[]{:S(2)}, u32[]{:S(2)}) collective-permute-start(bf16[2,64,1152]{2,1,0:T(8,128)(2,1)S(1)} %get-tuple-element.472), channel_id=1, source_target_pairs={{0,16},{4,20},{8,24},{12,28},{16,0},{20,4},{24,8},{28,12},{1,17},{... | collective-permute-start | bytes 884744 | tf_op jit(solution)/shard_map/ppermute | solution.py:439
  457.7 46.0 %collective-permute-start.33 = (bf16[256,2048]{1,0:T(8,128)(2,1)}, bf16[256,2048]{1,0:T(8,128)(2,1)}, u32[]{:S(2)}, u32[]{:S(2)}) collective-permute-start(bf16[256,2048]{1,0:T(8,128)(2,1)} %get-tuple-element.496.refs_4_), channel_id=1, source_target_pairs={{0,1},{3,2},{1,0},{2,3},{4,5},{7,6},{5,4},{6,7},{8,9},{11,10},{9,8... | collective-permute-start | bytes 3145736 | tf_op jit(solution)/shard_map/ppermute | solution.py:521
  459.4 44.3 %collective-permute-start.34 = (bf16[256,2048]{1,0:T(8,128)(2,1)}, bf16[256,2048]{1,0:T(8,128)(2,1)}, u32[]{:S(2)}, u32[]{:S(2)}) collective-permute-start(bf16[256,2048]{1,0:T(8,128)(2,1)} %get-tuple-element.497.refs_2_), channel_id=1, source_target_pairs={{1,2},{2,1},{5,6},{6,5},{9,10},{10,9},{13,14},{14,13},{17,18},{18,... | collective-permute-start | bytes 3145736 | tf_op jit(solution)/shard_map/ppermute | solution.py:524
  509.4 59.5 %collective-permute-start.35 = (bf16[256,2048]{1,0:T(8,128)(2,1)}, bf16[256,2048]{1,0:T(8,128)(2,1)S(1)}, u32[]{:S(2)}, u32[]{:S(2)}) collective-permute-start(bf16[256,2048]{1,0:T(8,128)(2,1)} %copy-done.47), channel_id=1, source_target_pairs={{0,1},{3,2},{1,0},{2,3},{4,5},{7,6},{5,4},{6,7},{8,9},{11,10},{9,8... | collective-permute-start | bytes 3145736 | tf_op jit(solution)/shard_map/ppermute | solution.py:521
  512.1 56.8 %collective-permute-start.36 = (bf16[256,2048]{1,0:T(8,128)(2,1)}, bf16[256,2048]{1,0:T(8,128)(2,1)}, u32[]{:S(2)}, u32[]{:S(2)}) collective-permute-start(bf16[256,2048]{1,0:T(8,128)(2,1)} %copy-done.46), channel_id=1, source_target_pairs={{1,2},{2,1},{5,6},{6,5},{9,10},{10,9},{13,14},{14,13},{17,18},{18,... | collective-permute-start | bytes 3145736 | tf_op jit(solution)/shard_map/ppermute | solution.py:524
  574.2 123.5 %reduce-scatter.8.cloned.1.call-start = ((), (), s32[]{:S(2)}) async-start(), calls=%async_computation.5 | async-start | bytes 9437184 | tf_op jit(solution)/shard_map/reduce_scatter | solution.py:922
  575.4 23.4 %collective-permute-start.37 = (bf16[256,2048]{1,0:T(8,128)(2,1)S(1)}, bf16[256,2048]{1,0:T(8,128)(2,1)S(1)}, u32[]{:S(2)}, u32[]{:S(2)}) collective-permute-start(bf16[256,2048]{1,0:T(8,128)(2,1)S(1)} %copy-done.53), channel_id=1, source_target_pairs={{0,1},{3,2},{1,0},{2,3},{4,5},{7,6},{5,4},{6,7},{8,9},{11,10},{9,8... | collective-permute-start | bytes 3145736 | tf_op jit(solution)/shard_map/ppermute | solution.py:521
  576.9 21.9 %collective-permute-start.38 = (bf16[256,2048]{1,0:T(8,128)(2,1)S(1)}, bf16[256,2048]{1,0:T(8,128)(2,1)}, u32[]{:S(2)}, u32[]{:S(2)}) collective-permute-start(bf16[256,2048]{1,0:T(8,128)(2,1)S(1)} %copy-done.51), channel_id=1, source_target_pairs={{1,2},{2,1},{5,6},{6,5},{9,10},{10,9},{13,14},{14,13},{17,18},{18,... | collective-permute-start | bytes 3145736 | tf_op jit(solution)/shard_map/ppermute | solution.py:524
  583.5 22.9 %copy-start.66 = (bf16[256,2048]{1,0:T(8,128)(2,1)S(1)}, bf16[256,2048]{1,0:T(8,128)(2,1)}, u32[]{:S(2)}) copy-start(bf16[256,2048]{1,0:T(8,128)(2,1)} %copy-done.65) | copy-start | bytes 3145732
  601.2 25.2 %collective-permute-start.39 = (bf16[256,2048]{1,0:T(8,128)(2,1)S(1)}, bf16[256,2048]{1,0:T(8,128)(2,1)S(1)}, u32[]{:S(2)}, u32[]{:S(2)}) collective-permute-start(bf16[256,2048]{1,0:T(8,128)(2,1)S(1)} %get-tuple-element.575.refs_4_), channel_id=1, source_target_pairs={{0,1},{3,2},{1,0},{2,3},{4,5},{7,6},{5,4},{6,7},{8,9},{11,10},{9,8... | collective-permute-start | bytes 3145736 | tf_op jit(solution)/shard_map/ppermute | solution.py:521
  605.6 21.7 %collective-permute-start.40 = (bf16[256,2048]{1,0:T(8,128)(2,1)S(1)}, bf16[256,2048]{1,0:T(8,128)(2,1)S(1)}, u32[]{:S(2)}, u32[]{:S(2)}) collective-permute-start(bf16[256,2048]{1,0:T(8,128)(2,1)S(1)} %get-tuple-element.576.refs_2_), channel_id=1, source_target_pairs={{1,2},{2,1},{5,6},{6,5},{9,10},{10,9},{13,14},{14,13},{17,18},{18,... | collective-permute-start | bytes 3145736 | tf_op jit(solution)/shard_map/ppermute | solution.py:524
  631.5 24.7 %collective-permute-start.41 = (bf16[256,2048]{1,0:T(8,128)(2,1)S(1)}, bf16[256,2048]{1,0:T(8,128)(2,1)S(1)}, u32[]{:S(2)}, u32[]{:S(2)}) collective-permute-start(bf16[256,2048]{1,0:T(8,128)(2,1)S(1)} %get-tuple-element.586.refs_3_), channel_id=1, source_target_pairs={{1,0},{2,3},{5,4},{6,7},{9,8},{10,11},{13,12},{14,15},{17,16},{18,... | collective-permute-start | bytes 3145736 | tf_op jit(solution)/shard_map/ppermute | solution.py:521
  632.8 23.4 %collective-permute-start.42 = (bf16[256,2048]{1,0:T(8,128)(2,1)S(1)}, bf16[256,2048]{1,0:T(8,128)(2,1)S(1)}, u32[]{:S(2)}, u32[]{:S(2)}) collective-permute-start(bf16[256,2048]{1,0:T(8,128)(2,1)S(1)} %get-tuple-element.587.refs_1_), channel_id=1, source_target_pairs={{1,2},{2,1},{5,6},{6,5},{9,10},{10,9},{13,14},{14,13},{17,18},{18,... | collective-permute-start | bytes 3145736 | tf_op jit(solution)/shard_map/ppermute | solution.py:524
  635.5 30.7 %copy-start.187 = (bf16[1,3,256,1408]{3,2,1,0:T(8,128)(2,1)S(1)}, bf16[1,3,256,1408]{3,2,1,0:T(8,128)(2,1)}, u32[]{:S(2)}) copy-start(bf16[1,3,256,1408]{3,2,1,0:T(8,128)(2,1)} %reduce-scatter.4.cloned.1.call-done) | copy-start | bytes 6488068
  658.5 35.1 %collective-permute-start.43 = (bf16[256,2048]{1,0:T(8,128)(2,1)S(1)}, bf16[256,2048]{1,0:T(8,128)(2,1)}, u32[]{:S(2)}, u32[]{:S(2)}) collective-permute-start(bf16[256,2048]{1,0:T(8,128)(2,1)S(1)} %get-tuple-element.596.refs_1_), channel_id=1, source_target_pairs={{1,0},{2,3},{5,4},{6,7},{9,8},{10,11},{13,12},{14,15},{17,16},{18,... | collective-permute-start | bytes 3145736 | tf_op jit(solution)/shard_map/ppermute | solution.py:521
  661.3 21.8 %collective-permute-start.44 = (f32[256]{0:T(256)S(1)}, f32[256]{0:T(256)S(1)}, u32[]{:S(2)}, u32[]{:S(2)}) collective-permute-start(f32[256]{0:T(256)S(1)} %bitcast.88), channel_id=1, source_target_pairs={{0,1},{1,0},{2,3},{3,2},{4,5},{5,4},{6,7},{7,6},{8,9},{9,8},{10,11... | collective-permute-start | bytes 3080 | tf_op jit(solution)/shard_map/ppermute | solution.py:927
  683.2 4.5 collective-permute-start.45
  (185 other events, 959.6 us)
Sparse Core Ops, SparseCore 0:
  11.7 135.3 all-gather.2
  314.3 126.1 reduce-scatter.3
  574.3 34.1 reduce-scatter.5
  612.2 71.2 reduce-scatter.7

commit v3 on v2

v3 whole, which is shorter than its diff:
```python
import functools

import jax
import jax.numpy as jnp
from jax import lax
from jax.experimental import pallas as pl
from jax.experimental.pallas import tpu as pltpu
from jax.sharding import PartitionSpec as P

CHUNK = 128
TILE = 256
EPS = 1e-06
RATE = 0.5
MIB = 2**20
f32 = jnp.float32
bf16 = jnp.bfloat16
highest = lax.Precision.HIGHEST


def nn(a, b):
    return lax.dot_general(a, b, (((1,), (0,)), ((), ())), preferred_element_type=f32)


def nt(a, b):
    return lax.dot_general(a, b, (((1,), (1,)), ((), ())), preferred_element_type=f32)


def tn(a, b):
    return lax.dot_general(a, b, (((0,), (0,)), ((), ())), preferred_element_type=f32)


def exact(a, b, dims):
    return lax.dot_general(a, b, (dims, ((), ())), precision=highest, preferred_element_type=f32)


def halves(a):
    high = a.astype(bf16)
    return high, (a - high.astype(f32)).astype(bf16)


def call(name, kernel, grid, in_specs, out_specs, out_shape, scratch=(), vmem=48, cost=None, loose=(), loose_out=(),
         aliases=None):
    single = not isinstance(out_shape, list)
    shapes = [out_shape] if single else out_shape
    shapes = [s if i in loose_out else pltpu.HBM(s.shape, s.dtype) for i, s in enumerate(shapes)]
    function = pl.pallas_call(
        kernel,
        name=name,
        grid=grid,
        in_specs=in_specs,
        out_specs=out_specs,
        out_shape=shapes[0] if single else shapes,
        scratch_shapes=scratch,
        input_output_aliases=aliases or {},
        compiler_params=pltpu.CompilerParams(
            dimension_semantics=("arbitrary",) * len(grid), vmem_limit_bytes=vmem * MIB
        ),
        cost_estimate=cost,
    )

    def run(*operands):
        return function(*[
            o if i in loose or spec.memory_space == pltpu.SMEM else pltpu.with_memory_space_constraint(o, pltpu.HBM)
            for i, (o, spec) in enumerate(zip(operands, in_specs))
        ])

    return run


def cost(flops, data):
    return pl.CostEstimate(flops=int(flops), bytes_accessed=int(data), transcendentals=0)


def fixed(shape):
    zeros = (0,) * len(shape)
    return pl.BlockSpec(shape, lambda *_: zeros, pipeline_mode=pl.Buffered(1))


def shaped(shape, dtype):
    return jax.ShapeDtypeStruct(shape, dtype)


def triangle(lower):
    r = lax.broadcasted_iota(jnp.int32, (CHUNK, CHUNK), 0)
    c = lax.broadcasted_iota(jnp.int32, (CHUNK, CHUNK), 1)
    return r >= c if lower else r <= c


def gates(z):
    la = -RATE * lax.logistic(-z)
    y = -la
    taken = jnp.ones_like(y)
    for n in range(9, 1, -1):
        taken = 1.0 - y * (1.0 / n) * taken
    taken = y * taken
    cum = exact(triangle(True).astype(f32), la, ((1,), (0,)))
    total = exact(la, jnp.ones((CHUNK, 128), f32), ((0,), (0,)))
    return la, cum, jnp.exp(-cum) * taken, total


def project_kernel(per_part, x_ref, gain_ref, wq_ref, wk_ref, wv_ref, wf_ref, bias_ref,
                   xn_ref, q_ref, k_ref, v_ref, z_ref, s_ref, d_ref, sent_ref, state, decay):
    @pl.when(lax.rem(pl.program_id(0), per_part) == 0)
    def _():
        state[...] = jnp.zeros_like(state)
        decay[...] = jnp.zeros_like(decay)

    x = x_ref[...].astype(f32)
    r1 = lax.rsqrt(jnp.mean(x * x, axis=-1, keepdims=True) + EPS)
    xn = (x * r1 * gain_ref[...]).astype(bf16)
    xn_ref[...] = xn
    q_ref[...] = nn(xn, wq_ref[...]).astype(bf16)
    k_ref[...] = nn(xn, wk_ref[...]).astype(bf16)
    v_ref[...] = nn(xn, wv_ref[...]).astype(bf16)
    z_ref[...] = nn(xn, wf_ref[...]) + bias_ref[...]
    width = k_ref.shape[1]
    for c in range(x_ref.shape[0] // CHUNK):
        rows = pl.ds(c * CHUNK, CHUNK)
        _, _, inflow, total = gates(z_ref[rows, :])
        spread = inflow.astype(bf16)
        keep = jnp.exp(total[:, :1])
        state[:, :width] = keep * (state[:, :width] + tn(spread, k_ref[rows, :]))
        state[:, width:] = keep * (state[:, width:] + tn(spread, v_ref[rows, :]))
        decay[...] += total
    s_ref[0] = state[...]
    d_ref[0] = jnp.exp(decay[...])
    pack(sent_ref, 0, jnp.exp(decay[...]), state[...])


def read_kernel(q_ref, k_ref, v_ref, z_ref, e0_ref, wo_ref, o_ref, p_ref, sc_ref, e_ref, left_ref, att_ref, state):
    @pl.when(pl.program_id(0) == 0)
    def _():
        state[...] = e0_ref[...]

    width = q_ref.shape[1]
    lower = triangle(True)
    q, k, v = q_ref[...], k_ref[...], v_ref[...]
    _, cum, inflow, total = gates(z_ref[...])
    growth = jnp.exp(cum)
    e_ref[0] = state[...]
    i_hi, i_lo = halves(inflow)
    a_hi, a_lo = halves(jnp.where(lower, nt(q, k), 0.0))
    e_hi, e_lo = halves(state[:, :width])
    scores = growth * (nt(q, e_hi) + nt(q, e_lo) + nn(a_hi, i_hi) + (nn(a_hi, i_lo) + nn(a_lo, i_hi)))
    top = jnp.exp(scores - jnp.max(scores, axis=-1, keepdims=True))
    p = top / jnp.sum(top, axis=-1, keepdims=True)
    w = (p * growth).astype(bf16)
    mixing = jnp.where(lower, nt(w, i_hi), 0.0).astype(bf16)
    o = (nn(w, state[:, width:].astype(bf16)) + nn(mixing, v)).astype(bf16)
    o_ref[...] = o
    att_ref[...] = nn(o, wo_ref[...]).astype(bf16)
    p_ref[...] = p
    sc_ref[...] = scores
    keep = jnp.exp(total[:, :1])
    state[:, :width] = keep * (state[:, :width] + tn(i_hi, k))
    state[:, width:] = keep * (state[:, width:] + tn(i_hi, v))
    left_ref[...] = state[...]


def back_kernel(dhn_ref, hid_ref, cot_ref, gain_ref, wo_ref, q_ref, k_ref, v_ref, z_ref, p_ref, sc_ref, e_ref,
                dhid_ref, datt_ref, dq_ref, dkl_ref, dvl_ref, h_ref, x1_ref, g_ref, s_ref, d_ref, gg_ref, state, decay):
    step = pl.program_id(0)

    @pl.when(step == 0)
    def _():
        state[...] = jnp.zeros_like(state)
        decay[...] = jnp.zeros_like(decay)
        gg_ref[...] = jnp.zeros_like(gg_ref)

    hidden = hid_ref[...]
    dhn = dhn_ref[...].astype(f32)
    r2 = lax.rsqrt(jnp.mean(hidden * hidden, axis=-1, keepdims=True) + EPS)
    gg_ref[...] += jnp.sum((dhn * hidden * r2).reshape(-1, 8, hidden.shape[1]), axis=0)
    u2 = gain_ref[...] * dhn
    dhid = (
        cot_ref[...].astype(f32)
        + r2 * u2
        - hidden * (r2 * r2 * r2) * jnp.mean(u2 * hidden, axis=-1, keepdims=True)
    )
    dhid_ref[...] = dhid
    datt = dhid.astype(bf16)
    datt_ref[...] = datt
    width = q_ref.shape[1]
    do = nt(datt, wo_ref[...]).astype(bf16)
    lower, upper = triangle(True), triangle(False)
    q, k, v = q_ref[...], k_ref[...], v_ref[...]
    _, cum, inflow, total = gates(z_ref[...])
    growth = jnp.exp(cum)
    p = p_ref[...]
    i_hi, i_lo = halves(inflow)
    b_hi, b_lo = halves(jnp.where(lower, nt(do, v), 0.0))
    ev_hi, ev_lo = halves(e_ref[0, :, width:])
    dp = growth * (nt(do, ev_hi) + nt(do, ev_lo) + nn(b_hi, i_hi) + (nn(b_hi, i_lo) + nn(b_lo, i_hi)))
    ds = p * (dp - jnp.sum(p * dp, axis=-1, keepdims=True))
    w = (p * growth).astype(bf16)
    gds = (growth * ds).astype(bf16)
    n = jnp.where(lower, nt(gds, i_hi), 0.0).astype(bf16)
    dq_ref[...] = (nn(gds, e_ref[0, :, :width].astype(bf16)) + nn(n, k)).astype(bf16)
    n_t = jnp.where(upper, nt(i_hi, gds), 0.0).astype(bf16)
    m_t = jnp.where(upper, nt(i_hi, w), 0.0).astype(bf16)
    dkl_ref[...] = nn(n_t, q)
    dvl_ref[...] = nn(m_t, do)
    h_ref[...] = ds * sc_ref[...] + p * dp
    a_t = jnp.where(upper, nt(k, q), 0.0).astype(bf16)
    b_t = jnp.where(upper, nt(v, do), 0.0).astype(bf16)
    x1_ref[...] = nn(a_t, gds) + nn(b_t, w)
    keep = jnp.exp(total[:, :1])
    g_k, g_v = tn(gds, q), tn(w, do)
    g_ref[0, :, :width] = g_k
    g_ref[0, :, width:] = g_v
    state[:, :width] = g_k + keep * state[:, :width]
    state[:, width:] = g_v + keep * state[:, width:]
    decay[...] += total
    s_ref[...] = state[...]
    d_ref[...] = jnp.exp(decay[...])


def last_kernel(l0_ref, k_ref, v_ref, z_ref, e_ref, g_ref, dkl_ref, dvl_ref, h_ref, x1_ref, dq_ref, x_ref,
                wq_ref, wk_ref, wv_ref, wf_ref, dk_ref, dv_ref, dz_ref, dxn_ref, bias_ref, gg_ref, state):
    step = pl.program_id(0)

    @pl.when(step == 0)
    def _():
        state[...] = l0_ref[...]
        gg_ref[...] = jnp.zeros_like(gg_ref)
        bias_ref[...] = jnp.zeros_like(bias_ref)

    width = k_ref.shape[1]
    low, up = triangle(True).astype(f32), triangle(False).astype(f32)
    k, v, z = k_ref[...], v_ref[...], z_ref[...]
    _, cum, inflow, total = gates(z)
    i_hi = inflow.astype(bf16)
    keep = jnp.exp(total[:, :1])
    lg = keep * state[...]
    lg_k, lg_v = lg[:, :width].astype(bf16), lg[:, width:].astype(bf16)
    dk = (dkl_ref[...] + nn(i_hi, lg_k)).astype(bf16)
    dv = (dvl_ref[...] + nn(i_hi, lg_v)).astype(bf16)
    dk_ref[...] = dk
    dv_ref[...] = dv
    x1 = x1_ref[...]
    x2 = nt(k, lg_k) + nt(v, lg_v)
    met = exact(jnp.ones((8, 2 * width), f32), lg * e_ref[0], ((1,), (1,)))
    h, r1 = h_ref[...], inflow * x1
    dla = (
        exact(up, h - r1, ((1,), (0,)))
        + r1
        + exact(low, inflow * x2, ((1,), (0,)))
        + met[:1]
        - jnp.exp(-cum) * (x1 + x2)
    )
    rate = lax.logistic(-z)
    dz = (dla * RATE * rate * (1.0 - rate)).astype(bf16)
    dz_ref[...] = dz
    bias_ref[...] += jnp.sum(dz.astype(f32).reshape(-1, 8, dz.shape[1]), axis=0)
    state[...] = g_ref[0] + lg
    dxn = nt(dq_ref[...], wq_ref[...]) + nt(dk, wk_ref[...]) + nt(dv, wv_ref[...]) + nt(dz, wf_ref[...])
    dxn_ref[...] = dxn.astype(bf16)
    x = x_ref[...].astype(f32)
    r1 = lax.rsqrt(jnp.mean(x * x, axis=-1, keepdims=True) + EPS)
    gg_ref[...] += jnp.sum((dxn * x * r1).reshape(-1, 8, x.shape[1]), axis=0)


def out_kernel(hid_ref, ffn_ref, *refs):
    refs[-1][0] = (hid_ref[...] + ffn_ref[...].astype(f32)).astype(bf16)


def in_grad_kernel(dhid_ref, dxn_ref, x_ref, gain_ref, *refs):
    x = x_ref[...].astype(f32)
    r1 = lax.rsqrt(jnp.mean(x * x, axis=-1, keepdims=True) + EPS)
    u1 = gain_ref[...] * dxn_ref[...].astype(f32)
    refs[-1][0] = dhid_ref[...] + r1 * u1 - x * (r1 * r1 * r1) * jnp.mean(u1 * x, axis=-1, keepdims=True)


def feed_kernel(first_row, x_ref, att_ref, gain_ref, cot_ref, full_ref, hid_ref, hn_ref, act_ref, dg_ref, du_ref,
                ffn_ref, dhn_ref, weights, x, cot, hid, hn, act, dg, du, ffn, in_sems, out_sems, weight_sems):
    rows, width = x.shape
    units = act.shape[1]
    blocks, _, span, _ = weights.shape
    tiles = [(u, min(TILE, units - u)) for u in range(0, units, TILE)]
    here = pl.ds(first_row, rows)
    reads = [pltpu.make_async_copy(source.at[here, :], target, in_sems.at[i])
             for i, (source, target) in enumerate(((x_ref, x), (cot_ref, cot)))]
    loads = [pltpu.make_async_copy(full_ref.at[:, :, :, pl.ds(u, size)], weights.at[:, :, :, pl.ds(u, size)],
                                   weight_sems.at[i]) for i, (u, size) in enumerate(tiles)]
    writes = [pltpu.make_async_copy(source, target, out_sems.at[i])
              for i, (source, target) in enumerate(
                  ((hid, hid_ref), (hn, hn_ref), (act, act_ref), (dg, dg_ref), (du, du_ref), (ffn, ffn_ref)))]
    for copy in reads + loads:
        copy.start()
    for copy in reads:
        copy.wait()
    hidden = x[...].astype(f32) + att_ref[...].astype(f32)
    hid[...] = hidden
    r2 = lax.rsqrt(jnp.mean(hidden * hidden, axis=-1, keepdims=True) + EPS)
    hn[...] = (hidden * r2 * gain_ref[...]).astype(bf16)
    writes[0].start()
    writes[1].start()
    for (u, size), load in zip(tiles, loads):
        load.wait()
        gate, up, dact = (
            nn(left[...], weights[:, i, :, u : u + size].reshape(width, size))
            for i, left in enumerate((hn, hn, cot))
        )
        s = lax.logistic(gate)
        silu = gate * s
        act[:, u : u + size] = (silu * up).astype(bf16)
        dg[:, u : u + size] = (dact * up * s * (1.0 + gate * (1.0 - s))).astype(bf16)
        du[:, u : u + size] = (dact * silu).astype(bf16)
    for write in writes[2:5]:
        write.start()
    group = max(1, TILE // span)
    for b in range(0, blocks, group):
        columns = slice(b * span, (b + group) * span)
        w_gate, w_up, w_down = (weights[b : b + group, i].reshape(group * span, units) for i in range(3))
        ffn[:, columns] = nt(act[...], w_down).astype(bf16)
        dhn_ref[:, columns] = (nt(dg[...], w_gate) + nt(du[...], w_up)).astype(bf16)
    writes[5].start()
    for write in writes:
        write.wait()


def summed(pairs):
    total = tn(*pairs[0])
    for pair in pairs[1:]:
        total = total + tn(*pair)
    return total.astype(bf16)


def down_grad_kernel(*refs):
    cot_ref, act, out_ref = refs[0], refs[1:-1], refs[-1]
    rows = act[0].shape[0]
    block = summed([(cot_ref[i * rows : (i + 1) * rows, :], a[...]) for i, a in enumerate(act)])
    out_ref[...] = block.reshape(out_ref.shape)


def wide_grad_kernel(*refs):
    out_ref = refs[-1]
    count = (len(refs) - 2) // 3
    hn, dg, du = refs[:count], refs[count : 2 * count], refs[2 * count : 3 * count]
    blocks, _, width, units = out_ref.shape
    for i, grads in enumerate((dg, du)):
        block = summed([(h[...], g[...]) for h, g in zip(hn, grads)])
        out_ref[:, i] = block.reshape(blocks, width, units)


def attn_grad_kernel(count, *refs):
    out_ref, dzw_ref = refs[-2:]
    xn_ref = refs[0]
    datt, dq, dk, dv, dz, o = (refs[1 + i * count : 1 + (i + 1) * count] for i in range(6))
    rows, width = dq[0].shape
    xn = [xn_ref[i * rows : (i + 1) * rows, :] for i in range(count)]
    for i, grads in enumerate((dq, dk, dv)):
        out_ref[:, i * width : (i + 1) * width] = summed([(x, g[...]) for x, g in zip(xn, grads)])
    out_ref[:, 3 * width :] = summed([(d[...], r[...]) for d, r in zip(datt, o)])
    dzw_ref[...] = summed([(x, g[...]) for x, g in zip(xn, dz)])


def pack(ref, m, decay, state):
    high, low = halves(decay)
    lane = lax.broadcasted_iota(jnp.int32, decay.shape, 1)
    width = state.shape[1]
    ref[m, :, :width] = state.astype(bf16)
    ref[m, :, width:] = jnp.where(lane == 0, high.astype(f32), low.astype(f32)).astype(bf16)


def fold_kernel(parts, pieces, *refs):
    s_refs, d_refs, (s_out, d_out, sent) = refs[: parts * pieces], refs[parts * pieces : -3], refs[-3:]
    for m in range(parts):
        s, d = s_refs[m * pieces + pieces - 1][...], d_refs[m * pieces + pieces - 1][...]
        for t in reversed(range(pieces - 1)):
            here = d_refs[m * pieces + t][...]
            s, d = s_refs[m * pieces + t][...] + here[:, :1] * s, here * d
        s_out[m], d_out[m] = s, d
        pack(sent, m, d, s)


def hop_kernel(bit, after, first, final, parts, pieces, *refs):
    refs = list(refs)
    s_ref, d_ref, got_ref = refs[:3]
    refs = refs[3:]
    if not first:
        part_s_ref, part_d_ref = refs[:2]
        refs = refs[2:]
    early = (lax.axis_index("seq") & bit) == 0
    takes = early if after else jnp.logical_not(early)
    width = s_ref.shape[2]
    found = []
    for m in range(parts):
        tail = got_ref[m, :, width:].astype(f32)
        there_d, there_s = tail[:, :1] + tail[:, 1:2], got_ref[m, :, :width].astype(f32)
        s, d = s_ref[m], d_ref[m]
        there_wide = jnp.broadcast_to(there_d, d.shape)
        new_s = jnp.where(takes, s + d[:, :1] * there_s, there_s + there_d * s)
        if first:
            part_s, part_d = jnp.where(takes, there_s, 0.0), jnp.where(takes, there_wide, 1.0)
        else:
            part_s, part_d = part_s_ref[m], part_d_ref[m]
            part_s = jnp.where(takes, part_s + part_d[:, :1] * there_s, part_s)
            part_d = jnp.where(takes, part_d * there_wide, part_d)
        found.append((new_s, d * there_wide, part_s, part_d))
    if not final:
        s_out, d_out, part_s_out, part_d_out, sent = refs
        for m, (s, d, part_s, part_d) in enumerate(found):
            s_out[m], d_out[m], part_s_out[m], part_d_out[m] = s, d, part_s, part_d
            pack(sent, m, d, s)
        return
    *own, out = refs
    arriving = jnp.zeros_like(found[0][0])
    for m in reversed(range(parts)) if after else range(parts):
        s, d, part_s, part_d = found[m]
        enters = part_s + part_d[:, :1] * arriving
        arriving = s + d[:, :1] * arriving
        for t in reversed(range(pieces)) if after else range(1):
            out[m * pieces + t if after else m] = enters
            if after and t:
                here = m * pieces + t
                enters = own[here][...] + own[parts * pieces + here][:, :1] * enters


def in_vmem(name, kernel, operands, shapes):
    return pl.pallas_call(
        kernel,
        name=name,
        in_specs=[pl.BlockSpec(memory_space=pltpu.VMEM)] * len(operands),
        out_specs=[pl.BlockSpec(memory_space=pltpu.VMEM)] * len(shapes),
        out_shape=shapes,
        compiler_params=pltpu.CompilerParams(vmem_limit_bytes=48 * MIB),
        cost_estimate=cost(0, 6 * MIB),
    )(*operands)


def scan_states(n, state, decay, sent, after, own=(), pieces=1, tie=None):
    parts, slots, width = state.shape
    part, bit, hops = [], 1, 0
    while bit < n:
        got = lax.ppermute(sent, "seq", [(i, i ^ bit) for i in range(n)])
        final = 2 * bit == n
        shapes = [shaped(state.shape, f32), shaped(decay.shape, f32)] * 2 + [shaped(sent.shape, bf16)]
        if final:
            shapes = [shaped((parts * pieces, slots, width), f32)]
        results = in_vmem(
            "hop",
            functools.partial(hop_kernel, bit, after, not part, final, parts, pieces),
            [state, decay, got, *part, *(own if final else ())],
            shapes,
        )
        if final:
            return results[0]
        state, decay, *part, sent = results
        if tie is not None and not hops:
            sent = tie(sent)
        bit, hops = 2 * bit, hops + 1


def behind_of(value, *first):
    return lax.optimization_barrier((value,) + first)[0]


def join_kernel(has, *refs):
    refs = iter(refs)
    piece, outer, pair, middle, total, coming = (next(refs) if h else None for h in has)
    makes = (piece is not None, pair is not None or coming is not None, total is not None)
    new_pair, new_total, done = (next(refs) if m else None for m in makes)
    me = lax.axis_index("head")
    end = (me == 0) | (me == 3)

    def each(work):
        @pl.loop(0, TILE // 32)
        def _(i):
            work(pl.ds(pl.multiple_of(i * 32, 32), 32))

    def both(a, b, rows):
        return (a[rows, :].astype(f32) + b[rows, :].astype(f32)).astype(bf16)

    @pl.when(end)
    def _():
        def work(rows):
            if coming is not None:
                new_total[rows, :] = coming[rows, :]
            if done is not None:
                done[rows, :] = outer[rows, :]

        each(work)

    @pl.when(jnp.logical_not(end))
    def _():
        def work(rows):
            if piece is not None:
                new_pair[rows, :] = both(piece, outer, rows)
            if pair is not None:
                new_total[rows, :] = both(pair, middle, rows)
            if done is not None:
                done[rows, :] = total[rows, :]

        each(work)


class Line:
    INWARD, OUTWARD, MIDDLE = [(0, 1), (3, 2)], [(1, 0), (2, 3)], [(1, 2), (2, 1)]

    def __init__(self):
        self.piece = self.pair = self.payload = None
        self.returns = False

    def load(self, piece):
        self.piece = self.payload = piece

    def step(self, inputs):
        piece, pair, payload, returns = self.piece, self.pair, self.payload, self.returns
        values = [v for v in (payload, pair) if v is not None] + inputs
        values = list(lax.optimization_barrier(tuple(values)))
        outer = middle = None
        if payload is not None:
            payload = values.pop(0)
            way = (self.INWARD if piece is not None else []) + (self.OUTWARD if returns else [])
            outer = lax.ppermute(payload, "head", way)
        if pair is not None:
            pair = values.pop(0)
            middle = lax.ppermute(pair, "head", self.MIDDLE)
        self.waiting = (piece, outer, pair, middle, payload if returns else None)
        return values

    def join(self, coming=None):
        piece, outer, pair, middle, total = self.waiting
        if piece is None and total is None:
            outer = None
        operands = [piece, outer, pair, middle, total, coming]
        makes = [piece is not None, pair is not None or coming is not None, total is not None]
        arrays = [o for o in operands if o is not None]
        results = in_vmem(
            "join",
            functools.partial(join_kernel, [o is not None for o in operands]),
            arrays,
            [shaped(arrays[0].shape, bf16)] * sum(makes),
        )
        results = iter(results)
        self.pair, self.payload, done = (next(results) if m else None for m in makes)
        self.returns = pair is not None
        self.piece = coming
        return done


def on_device(tokens, gain_attn, w_query, w_key, w_value, w_forget, forget_bias, w_out, gain_ffn, w_gate, w_up, w_down,
              cotangent):
    parts, part_rows, width = tokens.shape
    rows = parts * part_rows
    head = w_query.shape[1]
    slots = w_forget.shape[1]
    units = w_gate.shape[1]
    n_seq, n_head = lax.axis_size("seq"), lax.axis_size("head")
    span = w_gate.shape[0]
    per_part = pieces = part_rows // TILE
    chunks = TILE // CHUNK
    every = [(m, t) for m in range(parts) for t in range(pieces)]

    x = tokens.reshape(rows, width)
    cot = cotangent.reshape(rows, width)
    gain1 = gain_attn.reshape(1, width)
    gain2 = gain_ffn.reshape(1, width)
    state_scratch = pltpu.VMEM((slots, 2 * head), f32)
    decay_scratch = pltpu.VMEM((slots, 128), f32)
    anywhere = pl.BlockSpec(memory_space=pl.ANY)
    in_place = pl.BlockSpec(memory_space=pltpu.VMEM)

    stacked = jnp.stack([w_gate, w_up, w_down.T])
    x, stacked = lax.optimization_barrier((x, stacked))
    full = lax.all_gather(stacked, "seq")

    all_rows = lambda c: pl.BlockSpec((TILE, c), lambda i: (i, 0))
    by_part = lambda c: pl.BlockSpec((1, slots, c), lambda i: (i // per_part, 0, 0))
    xn, q, k, v, z, local, decay, sent = call(
        "project",
        functools.partial(project_kernel, per_part),
        (rows // TILE,),
        [all_rows(width), fixed((1, width))] + [fixed((width, head))] * 3 + [fixed((width, slots)), fixed((1, slots))],
        [all_rows(width), all_rows(head), all_rows(head), all_rows(head), all_rows(slots), by_part(2 * head), by_part(128),
         by_part(2 * head + 128)],
        [shaped((rows, width), bf16)] + [shaped((rows, head), bf16)] * 3
        + [shaped((rows, slots), f32), shaped((parts, slots, 2 * head), f32), shaped((parts, slots, 128), f32),
           shaped((parts, slots, 2 * head + 128), bf16)],
        [state_scratch, decay_scratch],
        cost=cost(2 * rows * width * (3 * head + slots), 2 * rows * width * 3 + 2 * width * 3 * head),
        loose_out=(5, 6, 7),
    )(x, gain1, w_query, w_key, w_value, w_forget, forget_bias.reshape(1, slots))
    entering = scan_states(n_seq, local, decay, sent, False)

    def chunk_rows(m, t, columns, back):
        start = (m * pieces + t) * chunks
        return pl.BlockSpec((CHUNK, columns), lambda i: (start + (chunks - 1 - i if back else i), 0))

    def own_rows(columns, back):
        return pl.BlockSpec((CHUNK, columns), lambda i: (chunks - 1 - i if back else i, 0))

    def chunk_state(back):
        return pl.BlockSpec((1, slots, 2 * head), lambda i: (chunks - 1 - i if back else i, 0, 0))

    def whole(shape):
        return pl.BlockSpec(shape, lambda i: (0,) * len(shape))

    def state_of(m):
        return pl.BlockSpec((None, slots, 2 * head), lambda i: (m, 0, 0))

    states_shape = shaped((chunks, slots, 2 * head), f32)

    def read(m, t, entering, which):
        return call(
            "read",
            read_kernel,
            (chunks,),
            [chunk_rows(m, t, head, False)] * 3 + [chunk_rows(m, t, slots, False), state_of(which), fixed((head, width))],
            [own_rows(head, False), own_rows(slots, False), own_rows(slots, False), chunk_state(False),
             pl.BlockSpec((None, slots, 2 * head), lambda i: (0, 0, 0)), own_rows(width, False)],
            [shaped((TILE, head), bf16), shaped((TILE, slots), f32), shaped((TILE, slots), f32), states_shape,
             shaped((1, slots, 2 * head), f32), shaped((TILE, width), bf16)],
            [state_scratch],
            cost=cost(2 * TILE * head * (600 + width), 2 * TILE * (head * 4 + width) + 2 * head * width),
            loose=(4,),
            loose_out=(4, 5),
        )(q, k, v, z, entering, w_out)

    def feed(m, t, attended):
        tile_count = pl.cdiv(units, TILE)
        vmem = pltpu.VMEM
        return call(
            "feed",
            functools.partial(feed_kernel, (m * pieces + t) * TILE),
            (),
            [anywhere, in_place, in_place, anywhere, anywhere],
            [anywhere] * 6 + [in_place],
            [shaped((TILE, width), f32), shaped((TILE, width), bf16)] + [shaped((TILE, units), bf16)] * 3
            + [shaped((TILE, width), bf16)] * 2,
            [vmem((n_seq, 3, span, units), bf16), vmem((TILE, width), bf16), vmem((TILE, width), bf16),
             vmem((TILE, width), f32), vmem((TILE, width), bf16)] + [vmem((TILE, units), bf16)] * 3
            + [vmem((TILE, width), bf16), pltpu.SemaphoreType.DMA((2,)), pltpu.SemaphoreType.DMA((6,)),
               pltpu.SemaphoreType.DMA((tile_count,))],
            cost=cost(12 * TILE * width * units, 6 * width * units + TILE * width * 14),
            loose=(1, 2),
            loose_out=(6,),
        )(x, attended, gain2, cot, full)

    group = max(1, TILE // span)
    wide = group * span
    grads_shape = shaped((n_seq, 3, span, units), bf16)

    def down_grads(acts):
        return call(
            "down_grads",
            down_grad_kernel,
            (width // wide,),
            [pl.BlockSpec((rows, wide), lambda j: (0, j))] + [fixed((TILE, units))] * len(acts),
            pl.BlockSpec((group, 1, span, units), lambda j: (j, 2, 0, 0)),
            grads_shape,
            cost=cost(2 * rows * width * units, 2 * (rows * width + rows * units + width * units)),
        )(cot, *acts)

    def wide_grads(normed, gates, ups, held_grads):
        count = len(normed)
        return call(
            "wide_grads",
            wide_grad_kernel,
            (width // wide,),
            [pl.BlockSpec((TILE, wide), lambda j: (0, j))] * count
            + [fixed((TILE, units))] * (2 * count) + [anywhere],
            pl.BlockSpec((group, 2, span, units), lambda j: (j, 0, 0, 0)),
            grads_shape,
            cost=cost(4 * rows * width * units, 2 * (rows * width + 2 * rows * units + 2 * width * units)),
            aliases={3 * count: 0},
        )(*normed, *gates, *ups, held_grads)

    def back(m, t, dhn, hidden):
        o, p, scores, e_chunks = reads[m, t][:4]
        return call(
            "back",
            back_kernel,
            (chunks,),
            [own_rows(width, True), own_rows(width, True), chunk_rows(m, t, width, True), fixed((1, width)),
             fixed((head, width))]
            + [chunk_rows(m, t, head, True)] * 3 + [chunk_rows(m, t, slots, True)] + [own_rows(slots, True)] * 2
            + [chunk_state(True)],
            [own_rows(width, True)] * 2 + [own_rows(head, True)] * 3 + [own_rows(slots, True)] * 2
            + [chunk_state(True), whole((slots, 2 * head)), whole((slots, 128)), whole((8, width))],
            [shaped((TILE, width), f32), shaped((TILE, width), bf16), shaped((TILE, head), bf16),
             shaped((TILE, head), f32), shaped((TILE, head), f32), shaped((TILE, slots), f32),
             shaped((TILE, slots), f32), states_shape, shaped((slots, 2 * head), f32), shaped((slots, 128), f32),
             shaped((8, width), f32)],
            [state_scratch, decay_scratch],
            cost=cost(2 * TILE * width * head + 2 * TILE * head * 1500, TILE * width * 14 + TILE * head * 20),
            loose=(0,),
            loose_out=(8, 9),
        )(dhn, hidden, cot, gain2, w_out, q, k, v, z, p, scores, e_chunks)

    def last(m, t, leaving, saved):
        dq, dk_local, dv_local, h_sum, x_local, g_chunks = saved
        return call(
            "last",
            last_kernel,
            (chunks,),
            [state_of(m * pieces + t), chunk_rows(m, t, head, True), chunk_rows(m, t, head, True),
             chunk_rows(m, t, slots, True), chunk_state(True), chunk_state(True), own_rows(head, True),
             own_rows(head, True), own_rows(slots, True), own_rows(slots, True), own_rows(head, True),
             chunk_rows(m, t, width, True)] + [fixed((width, head))] * 3 + [fixed((width, slots))],
            [own_rows(head, True), own_rows(head, True), own_rows(slots, True), own_rows(width, True), whole((8, slots)),
             whole((8, width))],
            [shaped((TILE, head), bf16), shaped((TILE, head), bf16), shaped((TILE, slots), bf16),
             shaped((TILE, width), bf16), shaped((8, slots), f32), shaped((8, width), f32)],
            [state_scratch],
            cost=cost(2 * TILE * width * (3 * head + slots), TILE * width * 8 + TILE * head * 20 + width * head * 6),
            loose=(0,),
            loose_out=(3,),
        )(leaving, k, v, z, reads[m, t][3], g_chunks, dk_local, dv_local, h_sum, x_local, dq, x,
          w_query, w_key, w_value, w_forget)

    line = Line()
    live = {}

    def start():
        names = list(live)
        live.update(zip(names, line.step([live[n] for n in names])))

    def end(coming=None, done=None):
        total = line.join(coming)
        if done is not None:
            live[done] = total

    reads, backs, lasts = {}, {}, {}
    outs, in_grads = [None], [None]
    eighth = TILE // 2

    def into(name, kernel, m, t, kept, dtype, inputs, specs):
        spec = pl.BlockSpec((1, eighth, width), lambda i: (m, 2 * t + i, 0))
        old = [] if kept[0] is None else [kept[0]]
        kept[0] = call(
            name,
            kernel,
            (2,),
            specs + [anywhere] * len(old),
            spec,
            shaped(tokens.shape, dtype),
            cost=cost(0, TILE * width * 10),
            loose=(1,),
            aliases={len(specs): 0} if old else None,
        )(*inputs, *old)

    piece_spec = pl.BlockSpec((eighth, width), lambda i: (i, 0))

    def finish_out(m, t):
        into("out", out_kernel, m, t, outs, bf16, [live.pop(("hidden", m, t)), live.pop(("ffn", m, t))],
             [piece_spec, piece_spec])

    def finish_grad(m, t):
        x_rows = pl.BlockSpec((eighth, width), lambda i: (2 * (m * pieces + t) + i, 0))
        into("in_grad", in_grad_kernel, m, t, in_grads, f32, [backs[m, t][0], live.pop(("dxn", m, t)), x, gain1],
             [piece_spec, piece_spec, x_rows, pl.BlockSpec((1, width), lambda i: (0, 0))])

    def go_read(m, t):
        before = live["entering"] if t == 0 else live.pop("left")
        reads[m, t] = read(m, t, before, m if t == 0 else 0)
        if t + 1 < pieces:
            live["left"] = reads[m, t][4]
        return reads[m, t][5]

    def go_feed(m, t):
        made = feed(m, t, live.pop(("att", m, t)))
        for name, value in zip(("hidden", "hn", "act", "dgate", "dup", "ffn_part"), made):
            live[name, m, t] = value
        return made[6]

    def go_back(m, t):
        backs[m, t] = back(m, t, live.pop(("dhn", m, t)), live["hidden", m, t])
        live["back", m, t] = backs[m, t][8]

    def go_last(m, t):
        lasts[m, t] = last(m, t, live["leaving"], backs[m, t][2:8])
        live["dxn_part", m, t] = lasts[m, t][3]

    def taken(name):
        return [live.pop((name, *key)) for key in every]

    live["entering"] = entering
    line.load(go_read(0, 0))
    start()
    end(go_read(0, 1))
    start()
    end(go_read(1, 0))
    start()
    end(go_read(1, 1), ("att", 0, 0))
    live.pop("entering")
    start()
    end(go_feed(0, 0), ("att", 0, 1))
    start()
    end(go_feed(0, 1), ("att", 1, 0))
    start()
    end(go_feed(1, 0), ("att", 1, 1))
    start()
    end(go_feed(1, 1), ("dhn", 0, 0))
    start()
    live["grads"] = down_grads(taken("act"))
    go_back(0, 0)
    end(live.pop(("ffn_part", 0, 0)), ("dhn", 0, 1))
    start()
    live["grads"] = wide_grads(taken("hn"), taken("dgate"), taken("dup"), live["grads"])
    end(live.pop(("ffn_part", 0, 1)), ("dhn", 1, 0))
    start()
    ffn_shares = lax.psum_scatter(live.pop("grads"), "seq", scatter_dimension=0)
    go_back(0, 1)
    go_back(1, 0)
    end(live.pop(("ffn_part", 1, 0)), ("dhn", 1, 1))
    start()
    go_back(1, 1)
    taken("back")
    own = [backs[key][8] for key in every] + [backs[key][9] for key in every]
    folded = in_vmem(
        "fold",
        functools.partial(fold_kernel, parts, pieces),
        own,
        [shaped(local.shape, f32), shaped(decay.shape, f32), shaped(sent.shape, bf16)],
    )

    def next_step(sent):
        live["sent"] = sent
        end(live.pop(("ffn_part", 1, 1)), ("ffn", 0, 0))
        start()
        return live.pop("sent")

    live["leaving"] = scan_states(n_seq, *folded, True, own, pieces, next_step)
    go_last(0, 0)
    end(live.pop(("dxn_part", 0, 0)), ("ffn", 0, 1))
    start()
    go_last(0, 1)
    go_last(1, 0)
    end(live.pop(("dxn_part", 0, 1)), ("ffn", 1, 0))
    start()
    go_last(1, 1)
    live.pop("leaving")
    attn_grads, forget_grads = call(
        "attn_grads",
        functools.partial(attn_grad_kernel, len(every)),
        (width // TILE,),
        [pl.BlockSpec((rows, TILE), lambda j: (0, j))] + [pl.BlockSpec((TILE, TILE), lambda j: (0, j))] * len(every)
        + [fixed((TILE, head))] * (3 * len(every)) + [fixed((TILE, slots))] * len(every)
        + [fixed((TILE, head))] * len(every),
        [pl.BlockSpec((TILE, 4 * head), lambda j: (j, 0)), pl.BlockSpec((TILE, slots), lambda j: (j, 0))],
        [shaped((width, 4 * head), bf16), shaped((width, slots), bf16)],
        cost=cost(2 * rows * width * (4 * head + slots), 4 * rows * width + 8 * rows * head + 8 * width * head),
    )(xn, *[backs[key][1] for key in every], *[backs[key][2] for key in every],
      *[lasts[key][i] for i in range(3) for key in every], *[reads[key][0] for key in every])
    live["attn_grads"] = attn_grads
    bias_sum = jnp.sum(sum(n[4] for n in lasts.values()), 0)
    gain1_sum = jnp.sum(sum(n[5] for n in lasts.values()), 0)
    gain2_sum = jnp.sum(sum(n[10] for n in backs.values()), 0)
    small = jnp.concatenate(
        [
            forget_grads,
            gain2_sum.astype(bf16)[:, None],
            gain1_sum.astype(bf16)[:, None],
            jnp.zeros((width, 128 - 2 - slots % 128), bf16),
        ],
        1,
    ).reshape(n_seq, span, -1)
    bias_row = jnp.pad(jnp.stack(halves(bias_sum)), ((0, 14), (0, small.shape[2] - slots)))
    live["small"] = jnp.concatenate([small, jnp.broadcast_to(bias_row, (n_seq,) + bias_row.shape)], 1)
    end(live.pop(("dxn_part", 1, 0)), ("ffn", 1, 1))
    start()
    small_shares = lax.psum_scatter(live.pop("small"), "seq", scatter_dimension=0)
    attn_shares = lax.psum_scatter(live.pop("attn_grads"), "seq", scatter_dimension=0, tiled=True)
    finish_out(0, 0)
    finish_out(0, 1)
    live["out"], live["ffn_shares"] = outs[0], ffn_shares
    end(live.pop(("dxn_part", 1, 1)), ("dxn", 0, 0))
    start()
    outs[0], ffn_shares = live.pop("out"), live.pop("ffn_shares")
    finish_out(1, 0)
    finish_out(1, 1)
    finish_grad(0, 0)
    live["out"], live["in_grad"] = outs[0], in_grads[0]
    end(None, ("dxn", 0, 1))
    start()
    in_grads[0] = live.pop("in_grad")
    finish_grad(0, 1)
    live["in_grad"], live["small"] = in_grads[0], small_shares
    end(None, ("dxn", 1, 0))
    start()
    in_grads[0], small_shares = live.pop("in_grad"), live.pop("small").astype(f32)
    gain1_total = small_shares[:span, slots + 1]
    bit = 1
    while bit < n_head:
        gain1_total = gain1_total + lax.ppermute(gain1_total, "head", [(i, i ^ bit) for i in range(n_head)])
        bit *= 2
    finish_grad(1, 0)
    end(None, ("dxn", 1, 1))
    live["dxn", 1, 1], attn_shares = lax.optimization_barrier((live["dxn", 1, 1], attn_shares))
    attn_shares = attn_shares.astype(f32)
    finish_grad(1, 1)

    return (
        live["out"],
        in_grads[0],
        gain1_total,
        attn_shares[:, :head],
        attn_shares[:, head : 2 * head],
        attn_shares[:, 2 * head : 3 * head],
        small_shares[:span, :slots],
        small_shares[span, :slots] + small_shares[span + 1, :slots],
        attn_shares[:, 3 * head :].T,
        small_shares[:span, slots],
        ffn_shares[0].astype(f32),
        ffn_shares[1].astype(f32),
        ffn_shares[2].astype(f32).T,
    )


def solution(mesh):
    rows, both = P(None, "seq", None), P("seq", "head")
    by_head, down = P(None, "head"), P("head", "seq")
    return jax.shard_map(
        on_device,
        mesh=mesh,
        in_specs=(rows, P(), by_head, by_head, by_head, by_head, P("head"), P("head", None), P(), both, both, down, rows),
        out_specs=(rows, rows, P("seq"), both, both, both, both, P("head"), down, P("seq"), both, both, down),
        check_vma=False,
    )
```

time: 718 us -> 618 us (0.86)
  local copies, waits for them, and re-layouts: 109 us -> 40.6 us
  waiting for transfers between devices: 200 us -> 151 us
  Pallas kernels: 279 us -> 308 us
    unnamed x403 -> x177, local copies, waits for them, and re-layouts: 103 us -> 36 us
    ppermute x12 -> x0, waiting for transfers between devices: 59.5 us -> none  [the longest x1 32.6 us: on_device(): across = lax.ppermute(held, 'seq', [(i, i ^ 2) for i in range(n_seq)])]
    pallas_call x30 -> x28, Pallas kernels: 244 us -> 266 us  [run(): function(*[o if i in loose or spec.memory_space == pltpu.SMEM else pltpu....]
    reduce_scatter x1, waiting for transfers between devices: 0.01 us -> 18.3 us  [on_device(): lax.psum_scatter(live.pop('attn_grads'), 'seq', scatter_dimension=0, tile...]
    ppermute x12 -> x0, starting transfers between devices: 17.2 us -> none  [the longest x9 17.2 us: turned(): lax.ppermute(block, 'head', [(i, (i + d) % n) for i in range(n)])]
    ppermute x14 -> x18, starting transfers between devices: 41.1 us -> 54 us  [step(): outer = lax.ppermute(payload, 'head', way)]
    ppermute x2, waiting for transfers between devices: 14.4 us -> 6.28 us  [on_device(): lax.ppermute(gain1_total, 'head', [(i, i ^ bit) for i in range(n_head)])]
    pallas_call x21 -> x25, Pallas kernels: 35.1 us -> 41.8 us  [in_vmem(): pl.pallas_call(kernel, name=name, in_specs=[pl.BlockSpec(memory_space=plt...]
  transfers between devices with their start and end apart: 50 -> 46, of which waited for: 18 -> 15; matrix products, arithmetic and copies ran while one was open for 3% -> 2% of each run, Pallas kernels for 38% -> 47%
where the time goes in v3:
time: 618 us; the launch traced here: 609 us
  Pallas kernels  308 us (50%)
  waiting for transfers between devices  151 us (24%)
  starting transfers between devices  82.5 us (13%)
  local copies, waits for them, and re-layouts  40.6 us (7%)
  between operations  15.5 us (3%)
  other arithmetic  12.2 us (2%)
    pallas_call x28, Pallas kernels, run(): function(*[o if i in loose or spec.memory_space == pltpu.SMEM else pltpu....  266 us
    ppermute x18, waiting for transfers between devices, step(): outer = lax.ppermute(payload, 'head', way)  77.7 us
    ppermute x18, starting transfers between devices, step(): outer = lax.ppermute(payload, 'head', way)  54 us
    ppermute x6, waiting for transfers between devices, scan_states(): got = lax.ppermute(sent, 'seq', [(i, i ^ bit) for i in range(n)])  47.6 us
    pallas_call x25, Pallas kernels, in_vmem(): pl.pallas_call(kernel, name=name, in_specs=[pl.BlockSpec(memory_space=plt...  41.8 us
    unnamed x177, local copies, waits for them, and re-layouts  36 us
    reduce_scatter x1, waiting for transfers between devices, on_device(): lax.psum_scatter(live.pop('attn_grads'), 'seq', scatter_dimension=0, tile...  18.3 us
    ppermute x16, starting transfers between devices, step(): middle = lax.ppermute(pair, 'head', self.MIDDLE)  16.9 us
  transfers between devices with their start and end apart: 46, of which 15 were waited for; matrix products, arithmetic and copies ran while one was open for 2% of the time, Pallas kernels for 47%

profile of v3, /device:TPU:0, one launch (start us, length us, event | category | flops | bytes accessed | tf_op | source)
XLA Modules:
  0.0 609.3 jit_solution(8659434072305503071)
XLA Ops:
  8.7 2.9 pad_maximum_fusion
  13.6 16.6 %project.1 = (bf16[1024,2048]{1,0:T(8,128)(2,1)}, bf16[1024,512]{1,0:T(8,128)(2,1)}, bf16[1024,512]{1,0:T(8,128)(2,1)}, bf16[1024,512]{1,0:T(8,128)(2,1)}, f32[1...) custom-call(bf16[1024,2048]{1,0:T(8,128)(2,1)} %bitcast.44, ...), custom_call_target="tpu_custom_call" | custom-call | flops 6710886400 | bytes 18874368 | tf_op jit(solution)/shard_map/project/pallas_call | solution.py:62
  32.2 2.9 collective-permute-start.1
  35.1 14.0 %collective-permute-done.1.refs_2_ = bf16[2,64,1152]{2,1,0:T(8,128)(2,1)S(1)} collective-permute-done((bf16[2,64,1152]{2,1,0:T(8,128)(2,1)S(1)}, bf16[2,64,1152]{2,1,0:T(8,128)(2,1)S(1)}, u32[]{:S(2)}, u32[]{:S(2)}) %collective-permute-start.1) | collective-permute-done | bytes 294944 | tf_op jit(solution)/shard_map/ppermute | solution.py:436
  51.4 6.6 %collective-permute-done.2.refs_2_ = bf16[2,64,1152]{2,1,0:T(8,128)(2,1)S(1)} collective-permute-done((bf16[2,64,1152]{2,1,0:T(8,128)(2,1)S(1)}, bf16[2,64,1152]{2,1,0:T(8,128)(2,1)S(1)}, u32[]{:S(2)}, u32[]{:S(2)}) %collective-permute-start.2) | collective-permute-done | bytes 294944 | tf_op jit(solution)/shard_map/ppermute | solution.py:436
  58.3 5.5 read.4
  63.8 3.7 collective-permute-start.3
  67.5 5.6 read.5
  73.1 15.4 %collective-permute-done.3.refs_1_ = bf16[256,2048]{1,0:T(8,128)(2,1)S(1)} collective-permute-done((bf16[256,2048]{1,0:T(8,128)(2,1)S(1)}, bf16[256,2048]{1,0:T(8,128)(2,1)S(1)}, u32[]{:S(2)}, u32[]{:S(2)}) %collective-permute-start.3) | collective-permute-done | bytes 1048608 | tf_op jit(solution)/shard_map/ppermute | solution.py:516
  88.6 4.6 collective-permute-start.4
  93.9 5.5 read.6
  100.4 13.0 %collective-permute-done.4.refs_1_ = bf16[256,2048]{1,0:T(8,128)(2,1)S(1)} collective-permute-done((bf16[256,2048]{1,0:T(8,128)(2,1)S(1)}, bf16[256,2048]{1,0:T(8,128)(2,1)S(1)}, u32[]{:S(2)}, u32[]{:S(2)}) %collective-permute-start.4) | collective-permute-done | bytes 1048608 | tf_op jit(solution)/shard_map/ppermute | solution.py:516
  116.0 4.3 collective-permute-start.6
  121.0 5.6 read.7
  127.6 12.7 %collective-permute-done.6.refs_1_ = bf16[256,2048]{1,0:T(8,128)(2,1)S(1)} collective-permute-done((bf16[256,2048]{1,0:T(8,128)(2,1)S(1)}, bf16[256,2048]{1,0:T(8,128)(2,1)S(1)}, u32[]{:S(2)}, u32[]{:S(2)}) %collective-permute-start.6) | collective-permute-done | bytes 1048608 | tf_op jit(solution)/shard_map/ppermute | solution.py:516
  144.7 4.3 collective-permute-start.8
  152.3 19.4 %feed.4 = (f32[256,2048]{1,0:T(8,128)}, bf16[256,2048]{1,0:T(8,128)(2,1)}, bf16[256,1408]{1,0:T(8,128)(2,1)}, bf16[256,1408]{1,0:T(8,128)(2,1)}, bf16[256,1408]{...) custom-call(bf16[1024,2048]{1,0:T(8,128)(2,1)} %bitcast.45, ...), custom_call_target="tpu_custom_call" | custom-call | flops 8858370048 | bytes 24641536 | tf_op jit(solution)/shard_map/feed/pallas_call | solution.py:62
  178.3 19.4 %feed.5 = (f32[256,2048]{1,0:T(8,128)}, bf16[256,2048]{1,0:T(8,128)(2,1)}, bf16[256,1408]{1,0:T(8,128)(2,1)}, bf16[256,1408]{1,0:T(8,128)(2,1)}, bf16[256,1408]{...) custom-call(bf16[1024,2048]{1,0:T(8,128)(2,1)} %bitcast.46, ...), custom_call_target="tpu_custom_call" | custom-call | flops 8858370048 | bytes 24641536 | tf_op jit(solution)/shard_map/feed/pallas_call | solution.py:62
  202.1 3.0 collective-permute-start.12
  206.0 19.3 %feed.6 = (f32[256,2048]{1,0:T(8,128)}, bf16[256,2048]{1,0:T(8,128)(2,1)}, bf16[256,1408]{1,0:T(8,128)(2,1)}, bf16[256,1408]{1,0:T(8,128)(2,1)}, bf16[256,1408]{...) custom-call(bf16[1024,2048]{1,0:T(8,128)(2,1)} %bitcast.47, ...), custom_call_target="tpu_custom_call" | custom-call | flops 8858370048 | bytes 24641536 | tf_op jit(solution)/shard_map/feed/pallas_call | solution.py:62
  229.8 2.8 collective-permute-start.14
  233.7 19.3 %feed.7 = (f32[256,2048]{1,0:T(8,128)}, bf16[256,2048]{1,0:T(8,128)(2,1)}, bf16[256,1408]{1,0:T(8,128)(2,1)}, bf16[256,1408]{1,0:T(8,128)(2,1)}, bf16[256,1408]{...) custom-call(bf16[1024,2048]{1,0:T(8,128)(2,1)} %bitcast.48, ...), custom_call_target="tpu_custom_call" | custom-call | flops 8858370048 | bytes 24641536 | tf_op jit(solution)/shard_map/feed/pallas_call | solution.py:62
  257.4 3.0 collective-permute-start.16
  261.4 8.6 %back.4 = (f32[256,2048]{1,0:T(8,128)}, bf16[256,2048]{1,0:T(8,128)(2,1)}, bf16[256,512]{1,0:T(8,128)(2,1)}, f32[256,512]{1,0:T(8,128)}, f32[256,512]{1,0:T(8,12...) custom-call(bf16[256,2048]{1,0:T(8,128)(2,1)S(1)} %get-tuple-element, ...), custom_call_target="tpu_custom_call" | custom-call | flops 930086912 | bytes 9961472 | tf_op jit(solution)/shard_map/back/pallas_call | solution.py:62
  270.0 12.0 %down_grads.1.refs_12_ = bf16[8,3,256,1408]{3,2,1,0:T(8,128)(2,1)} custom-call(bf16[1024,2048]{1,0:T(8,128)(2,1)} %bitcast.62, bf16[256,1408]{1,0:T(8,128)(2,1)} %get-tuple-element.555.refs_1_, bf16[256,1408]{1,0:T(8,128)(2,1)} %get-tuple-element.556.refs_2_, bf16[256,1408]{1,0:T(8,128)(2,1)} %get-tuple-element.557.refs_3_, ...), custom_call_target="tpu_custom_call" | custom-call | flops 5905580032 | bytes 12845056 | tf_op jit(solution)/shard_map/down_grads/pallas_call | solution.py:62
  283.1 3.3 join.25
  286.5 2.4 collective-permute-start.18
  290.6 19.0 %wide_grads.1 = bf16[8,3,256,1408]{3,2,1,0:T(8,128)(2,1)} custom-call(bf16[256,2048]{1,0:T(8,128)(2,1)} %get-tuple-element.576.refs_0_, bf16[256,2048]{1,0:T(8,128)(2,1)} %get-tuple-element.577.refs_1_, bf16[256,2048]{1,0:T(8,128)(2,1)} %get-tuple-element.578.refs_2_, bf16[256,2048]{1,0:T(8,128)(2,1)} %get-tuple-element.579.refs_3_, ...), custom_call_target="tpu_custom_call", output_to_operand_aliasing={{}: (12, {})} | custom-call | flops 11811160064 | bytes 21495808 | tf_op jit(solution)/shard_map/wide_grads/pallas_call | solution.py:62
  309.6 2.6 join.26
  317.0 8.6 %back.6 = (f32[256,2048]{1,0:T(8,128)}, bf16[256,2048]{1,0:T(8,128)(2,1)}, bf16[256,512]{1,0:T(8,128)(2,1)}, f32[256,512]{1,0:T(8,128)}, f32[256,512]{1,0:T(8,12...) custom-call(bf16[256,2048]{1,0:T(8,128)(2,1)S(1)} %get-tuple-element, ...), custom_call_target="tpu_custom_call" | custom-call | flops 930086912 | bytes 9961472 | tf_op jit(solution)/shard_map/back/pallas_call | solution.py:62
  325.6 9.6 %back.5 = (f32[256,2048]{1,0:T(8,128)}, bf16[256,2048]{1,0:T(8,128)(2,1)}, bf16[256,512]{1,0:T(8,128)(2,1)}, f32[256,512]{1,0:T(8,128)}, f32[256,512]{1,0:T(8,12...) custom-call(bf16[256,2048]{1,0:T(8,128)(2,1)S(1)} %get-tuple-element, ...), custom_call_target="tpu_custom_call" | custom-call | flops 930086912 | bytes 9961472 | tf_op jit(solution)/shard_map/back/pallas_call | solution.py:62
  336.2 3.1 join.27
  339.4 4.3 collective-permute-start.22
  344.4 8.6 %back.7 = (f32[256,2048]{1,0:T(8,128)}, bf16[256,2048]{1,0:T(8,128)(2,1)}, bf16[256,512]{1,0:T(8,128)(2,1)}, f32[256,512]{1,0:T(8,128)}, f32[256,512]{1,0:T(8,12...) custom-call(bf16[256,2048]{1,0:T(8,128)(2,1)S(1)} %get-tuple-element, ...), custom_call_target="tpu_custom_call" | custom-call | flops 930086912 | bytes 9961472 | tf_op jit(solution)/shard_map/back/pallas_call | solution.py:62
  355.0 5.0 collective-permute-done.22.refs_1_
  363.4 4.1 collective-permute-start.25
  370.0 12.3 %collective-permute-done.27.refs_2_ = bf16[2,64,1152]{2,1,0:T(8,128)(2,1)S(1)} collective-permute-done((bf16[2,64,1152]{2,1,0:T(8,128)(2,1)S(1)}, bf16[2,64,1152]{2,1,0:T(8,128)(2,1)S(1)}, u32[]{:S(2)}, u32[]{:S(2)}) %collective-permute-start.27) | collective-permute-done | bytes 294944 | tf_op jit(solution)/shard_map/ppermute | solution.py:436
  384.1 12.0 %collective-permute-done.28.refs_2_ = bf16[2,64,1152]{2,1,0:T(8,128)(2,1)S(1)} collective-permute-done((bf16[2,64,1152]{2,1,0:T(8,128)(2,1)S(1)}, bf16[2,64,1152]{2,1,0:T(8,128)(2,1)S(1)}, u32[]{:S(2)}, u32[]{:S(2)}) %collective-permute-start.28) | collective-permute-done | bytes 294944 | tf_op jit(solution)/shard_map/ppermute | solution.py:436
  396.4 10.6 %last.4 = (bf16[256,512]{1,0:T(8,128)(2,1)}, bf16[256,512]{1,0:T(8,128)(2,1)}, bf16[256,64]{1,0:T(8,128)(2,1)}, bf16[256,2048]{1,0:T(8,128)(2,1)S(1)}, f32[8,64]{1,0:T(8,128)}, /*index=5*/f32[8,2048]{1,0:T(8,128)}) custom-call(f32[4,64,1024]{2,1,0:T(8,128)S(1)} %hop.11.l0_ref, bf16[1024,512]{1,0:T(8,128)(2,1)} %get-tuple-element.404.k_ref, ...), custom_call_target="tpu_custom_call" | custom-call | flops 1677721600 | bytes 13107200 | tf_op jit(solution)/shard_map/last/pallas_call | solution.py:62
  409.1 3.7 join.29
  413.8 2.5 collective-permute-start.29
  418.0 10.8 %last.6 = (bf16[256,512]{1,0:T(8,128)(2,1)}, bf16[256,512]{1,0:T(8,128)(2,1)}, bf16[256,64]{1,0:T(8,128)(2,1)}, bf16[256,2048]{1,0:T(8,128)(2,1)S(1)}, f32[8,64]{1,0:T(8,128)}, /*index=5*/f32[8,2048]{1,0:T(8,128)}) custom-call(f32[4,64,1024]{2,1,0:T(8,128)S(1)} %hop.11.l0_ref, bf16[1024,512]{1,0:T(8,128)(2,1)} %get-tuple-element.404.k_ref, ...), custom_call_target="tpu_custom_call" | custom-call | flops 1677721600 | bytes 13107200 | tf_op jit(solution)/shard_map/last/pallas_call | solution.py:62
  428.8 11.0 %last.5 = (bf16[256,512]{1,0:T(8,128)(2,1)}, bf16[256,512]{1,0:T(8,128)(2,1)}, bf16[256,64]{1,0:T(8,128)(2,1)}, bf16[256,2048]{1,0:T(8,128)(2,1)S(1)}, f32[8,64]{1,0:T(8,128)}, /*index=5*/f32[8,2048]{1,0:T(8,128)}) custom-call(f32[4,64,1024]{2,1,0:T(8,128)S(1)} %hop.11.l0_ref, bf16[1024,512]{1,0:T(8,128)(2,1)} %get-tuple-element.404.k_ref, ...), custom_call_target="tpu_custom_call" | custom-call | flops 1677721600 | bytes 13107200 | tf_op jit(solution)/shard_map/last/pallas_call | solution.py:62
  440.8 2.6 join.30
  443.5 11.6 %last.7 = (bf16[256,512]{1,0:T(8,128)(2,1)}, bf16[256,512]{1,0:T(8,128)(2,1)}, bf16[256,64]{1,0:T(8,128)(2,1)}, bf16[256,2048]{1,0:T(8,128)(2,1)S(1)}, f32[8,64]{1,0:T(8,128)}, /*index=5*/f32[8,2048]{1,0:T(8,128)}) custom-call(f32[4,64,1024]{2,1,0:T(8,128)S(1)} %hop.11.l0_ref, bf16[1024,512]{1,0:T(8,128)(2,1)} %get-tuple-element.404.k_ref, ...), custom_call_target="tpu_custom_call" | custom-call | flops 1677721600 | bytes 13107200 | tf_op jit(solution)/shard_map/last/pallas_call | solution.py:62
  461.2 15.5 %attn_grads.1 = (bf16[2048,2048]{1,0:T(8,128)(2,1)}, bf16[2048,64]{1,0:T(8,128)(2,1)}) custom-call(bf16[1024,2048]{1,0:T(8,128)(2,1)} %get-tuple-element.708.refs_0_, bf16[256,2048]{1,0:T(8,128)(2,1)} %get-tuple-element.709.refs_1_, bf16[256,2048]{1,0:T(8,128)(2,1)} %get-tuple-element.710.refs_2_, bf16[256,2048]{1,0:T(8,128)(2,1)} %get-tuple-element.711.refs_3_, ...), custom_call_target="tpu_custom_call" | custom-call | flops 8858370048 | bytes 20971520 | tf_op jit(solution)/shard_map/attn_grads/pallas_call | solution.py:62
  479.2 2.9 join.31
  489.1 2.4 out.4.refs_0_
  491.5 2.6 out.5.refs_0_
  494.1 10.1 %collective-permute-done.33.refs_1_ = bf16[256,2048]{1,0:T(8,128)(2,1)S(1)} collective-permute-done((bf16[256,2048]{1,0:T(8,128)(2,1)S(1)}, bf16[256,2048]{1,0:T(8,128)(2,1)S(1)}, u32[]{:S(2)}, u32[]{:S(2)}) %collective-permute-start.33) | collective-permute-done | bytes 1048608 | tf_op jit(solution)/shard_map/ppermute | solution.py:516
  507.6 4.4 collective-permute-start.35
  512.7 3.4 in_grad.4.refs_0_
  516.1 2.5 out.6.refs_0_
  518.6 2.5 out.7
  521.2 5.5 collective-permute-done.35.refs_1_
  532.0 3.9 in_grad.5.refs_0_
  535.9 16.0 %collective-permute-done.37.refs_0_ = bf16[256,2048]{1,0:T(8,128)(2,1)S(1)} collective-permute-done((bf16[256,2048]{1,0:T(8,128)(2,1)S(1)}, bf16[256,2048]{1,0:T(8,128)(2,1)S(1)}, u32[]{:S(2)}, u32[]{:S(2)}) %collective-permute-start.37) | collective-permute-done | bytes 1048608 | tf_op jit(solution)/shard_map/ppermute | solution.py:516
  555.9 2.7 collective-permute-start.40
  558.6 3.7 convert_bitcast_fusion
  562.2 2.9 copy.70
  565.2 6.3 %collective-permute-done.40 = f32[256]{0:T(256)S(1)} collective-permute-done((f32[256]{0:T(256)S(1)}, f32[256]{0:T(256)S(1)}, u32[]{:S(2)}, u32[]{:S(2)}) %collective-permute-start.40) | collective-permute-done | bytes 1056 | tf_op jit(solution)/shard_map/ppermute | solution.py:887
  573.0 3.3 in_grad.6.refs_0_
  576.9 18.3 %reduce-scatter.8.cloned.1.call-done = bf16[256,2048]{1,0:T(8,128)(2,1)} async-done(((bf16[2048,2048]{1,0:T(8,128)(2,1)}), bf16[256,2048]{1,0:T(8,128)(2,1)}) %reduce-scatter.8.cloned.1.call-update) | async-done | bytes 1048592 | tf_op jit(solution)/shard_map/reduce_scatter | solution.py:865
  599.0 3.3 in_grad.7
  (287 shorter events, 103.7 us)
Async XLA Ops:
  7.2 143.9 %all-gather.3.cloned.1.call-start = ((), (), s32[]{:S(2)}) async-start(), calls=%async_computation.6 | async-start | bytes 19464192 | tf_op jit(solution)/shard_map/all_gather | solution.py:567
  11.7 495.9 %reduce-scatter.4.cloned.1.call-start = ((), (), s32[]{:S(2)}) async-start(), calls=%async_computation.3 | async-start | bytes 19464192 | tf_op jit(solution)/shard_map/reduce_scatter | solution.py:804
  30.2 1.7 collective-permute-start
  32.2 16.9 %collective-permute-start.1 = (bf16[2,64,1152]{2,1,0:T(8,128)(2,1)S(1)}, bf16[2,64,1152]{2,1,0:T(8,128)(2,1)S(1)}, u32[]{:S(2)}, u32[]{:S(2)}) collective-permute-start(bf16[2,64,1152]{2,1,0:T(8,128)(2,1)S(1)} %get-tuple-element.412), channel_id=1, source_target_pairs={{0,8},{4,12},{8,0},{12,4},{16,24},{20,28},{24,16},{28,20},{1,9},{5... | collective-permute-start | bytes 884744 | tf_op jit(solution)/shard_map/ppermute | solution.py:436
  49.4 8.7 %collective-permute-start.2 = (bf16[2,64,1152]{2,1,0:T(8,128)(2,1)S(1)}, bf16[2,64,1152]{2,1,0:T(8,128)(2,1)S(1)}, u32[]{:S(2)}, u32[]{:S(2)}) collective-permute-start(bf16[2,64,1152]{2,1,0:T(8,128)(2,1)S(1)} %get-tuple-element.417), channel_id=1, source_target_pairs={{0,16},{4,20},{8,24},{12,28},{16,0},{20,4},{24,8},{28,12},{1,17},{... | collective-permute-start | bytes 884744 | tf_op jit(solution)/shard_map/ppermute | solution.py:436
  63.8 24.7 %collective-permute-start.3 = (bf16[256,2048]{1,0:T(8,128)(2,1)S(1)}, bf16[256,2048]{1,0:T(8,128)(2,1)S(1)}, u32[]{:S(2)}, u32[]{:S(2)}) collective-permute-start(bf16[256,2048]{1,0:T(8,128)(2,1)S(1)} %get-tuple-element.424.refs_0_), channel_id=1, source_target_pairs={{0,1},{3,2},{4,5},{7,6},{8,9},{11,10},{12,13},{15,14},{16,17},{19,... | collective-permute-start | bytes 3145736 | tf_op jit(solution)/shard_map/ppermute | solution.py:516
  88.6 24.8 %collective-permute-start.4 = (bf16[256,2048]{1,0:T(8,128)(2,1)S(1)}, bf16[256,2048]{1,0:T(8,128)(2,1)S(1)}, u32[]{:S(2)}, u32[]{:S(2)}) collective-permute-start(bf16[256,2048]{1,0:T(8,128)(2,1)S(1)} %get-tuple-element.428), channel_id=1, source_target_pairs={{0,1},{3,2},{4,5},{7,6},{8,9},{11,10},{12,13},{15,14},{16,17},{19,... | collective-permute-start | bytes 3145736 | tf_op jit(solution)/shard_map/ppermute | solution.py:516
  93.2 20.1 %collective-permute-start.5 = (bf16[256,2048]{1,0:T(8,128)(2,1)S(1)}, bf16[256,2048]{1,0:T(8,128)(2,1)S(1)}, u32[]{:S(2)}, u32[]{:S(2)}) collective-permute-start(bf16[256,2048]{1,0:T(8,128)(2,1)S(1)} %get-tuple-element.429.refs_2_), channel_id=1, source_target_pairs={{1,2},{2,1},{5,6},{6,5},{9,10},{10,9},{13,14},{14,13},{17,18},{18,... | collective-permute-start | bytes 3145736 | tf_op jit(solution)/shard_map/ppermute | solution.py:519
  116.0 25.3 %copy-start.3 = (bf16[256,2048]{1,0:T(8,128)(2,1)S(1)}, bf16[256,2048]{1,0:T(8,128)(2,1)}, u32[]{:S(2)}) copy-start(bf16[256,2048]{1,0:T(8,128)(2,1)} %copy-done.2) | copy-start | bytes 3145732
  116.0 24.3 %collective-permute-start.6 = (bf16[256,2048]{1,0:T(8,128)(2,1)S(1)}, bf16[256,2048]{1,0:T(8,128)(2,1)S(1)}, u32[]{:S(2)}, u32[]{:S(2)}) collective-permute-start(bf16[256,2048]{1,0:T(8,128)(2,1)S(1)} %get-tuple-element.437.refs_4_), channel_id=1, source_target_pairs={{0,1},{3,2},{1,0},{2,3},{4,5},{7,6},{5,4},{6,7},{8,9},{11,10},{9,8... | collective-permute-start | bytes 3145736 | tf_op jit(solution)/shard_map/ppermute | solution.py:516
  120.3 20.0 %collective-permute-start.7 = (bf16[256,2048]{1,0:T(8,128)(2,1)S(1)}, bf16[256,2048]{1,0:T(8,128)(2,1)S(1)}, u32[]{:S(2)}, u32[]{:S(2)}) collective-permute-start(bf16[256,2048]{1,0:T(8,128)(2,1)S(1)} %get-tuple-element.438.refs_2_), channel_id=1, source_target_pairs={{1,2},{2,1},{5,6},{6,5},{9,10},{10,9},{13,14},{14,13},{17,18},{18,... | collective-permute-start | bytes 3145736 | tf_op jit(solution)/shard_map/ppermute | solution.py:519
  144.7 27.1 %copy-start.42 = (bf16[256,2048]{1,0:T(8,128)(2,1)}, bf16[256,2048]{1,0:T(8,128)(2,1)S(1)}, u32[]{:S(2)}) copy-start(bf16[256,2048]{1,0:T(8,128)(2,1)S(1)} %get-tuple-element.443.refs_2_) | copy-start | bytes 3145732
  144.7 27.1 %copy-start.43 = (bf16[256,2048]{1,0:T(8,128)(2,1)}, bf16[256,2048]{1,0:T(8,128)(2,1)S(1)}, u32[]{:S(2)}) copy-start(bf16[256,2048]{1,0:T(8,128)(2,1)S(1)} %get-tuple-element.442.refs_4_) | copy-start | bytes 3145732
  144.7 28.1 %collective-permute-start.8 = (bf16[256,2048]{1,0:T(8,128)(2,1)S(1)}, bf16[256,2048]{1,0:T(8,128)(2,1)S(1)}, u32[]{:S(2)}, u32[]{:S(2)}) collective-permute-start(bf16[256,2048]{1,0:T(8,128)(2,1)S(1)} %get-tuple-element.442.refs_4_), channel_id=1, source_target_pairs={{0,1},{3,2},{1,0},{2,3},{4,5},{7,6},{5,4},{6,7},{8,9},{11,10},{9,8... | collective-permute-start | bytes 3145736 | tf_op jit(solution)/shard_map/ppermute | solution.py:516
  148.9 23.9 %collective-permute-start.9 = (bf16[256,2048]{1,0:T(8,128)(2,1)S(1)}, bf16[256,2048]{1,0:T(8,128)(2,1)}, u32[]{:S(2)}, u32[]{:S(2)}) collective-permute-start(bf16[256,2048]{1,0:T(8,128)(2,1)S(1)} %get-tuple-element.443.refs_2_), channel_id=1, source_target_pairs={{1,2},{2,1},{5,6},{6,5},{9,10},{10,9},{13,14},{14,13},{17,18},{18,... | collective-permute-start | bytes 3145736 | tf_op jit(solution)/shard_map/ppermute | solution.py:519
  152.3 20.5 %copy-start.17 = (bf16[256,2048]{1,0:T(8,128)(2,1)S(1)}, bf16[256,2048]{1,0:T(8,128)(2,1)}, u32[]{:S(2)}) copy-start(bf16[256,2048]{1,0:T(8,128)(2,1)} %copy-done.16) | copy-start | bytes 3145732
  175.1 22.6 %copy-start.46 = (bf16[256,2048]{1,0:T(8,128)(2,1)}, bf16[256,2048]{1,0:T(8,128)(2,1)S(1)}, u32[]{:S(2)}) copy-start(bf16[256,2048]{1,0:T(8,128)(2,1)S(1)} %get-tuple-element.459.refs_2_) | copy-start | bytes 3145732
  175.2 22.6 %copy-start.47 = (bf16[256,2048]{1,0:T(8,128)(2,1)}, bf16[256,2048]{1,0:T(8,128)(2,1)S(1)}, u32[]{:S(2)}) copy-start(bf16[256,2048]{1,0:T(8,128)(2,1)S(1)} %get-tuple-element.458.refs_4_) | copy-start | bytes 3145732
  175.2 24.5 %copy-start.21 = (bf16[256,2048]{1,0:T(8,128)(2,1)S(1)}, bf16[256,2048]{1,0:T(8,128)(2,1)}, u32[]{:S(2)}) copy-start(bf16[256,2048]{1,0:T(8,128)(2,1)} %copy-done.20) | copy-start | bytes 3145732
  175.2 23.5 %collective-permute-start.10 = (bf16[256,2048]{1,0:T(8,128)(2,1)S(1)}, bf16[256,2048]{1,0:T(8,128)(2,1)S(1)}, u32[]{:S(2)}, u32[]{:S(2)}) collective-permute-start(bf16[256,2048]{1,0:T(8,128)(2,1)S(1)} %get-tuple-element.458.refs_4_), channel_id=1, source_target_pairs={{0,1},{3,2},{1,0},{2,3},{4,5},{7,6},{5,4},{6,7},{8,9},{11,10},{9,8... | collective-permute-start | bytes 3145736 | tf_op jit(solution)/shard_map/ppermute | solution.py:516
  177.4 21.3 %collective-permute-start.11 = (bf16[256,2048]{1,0:T(8,128)(2,1)S(1)}, bf16[256,2048]{1,0:T(8,128)(2,1)S(1)}, u32[]{:S(2)}, u32[]{:S(2)}) collective-permute-start(bf16[256,2048]{1,0:T(8,128)(2,1)S(1)} %get-tuple-element.459.refs_2_), channel_id=1, source_target_pairs={{1,2},{2,1},{5,6},{6,5},{9,10},{10,9},{13,14},{14,13},{17,18},{18,... | collective-permute-start | bytes 3145736 | tf_op jit(solution)/shard_map/ppermute | solution.py:519
  202.0 23.4 %copy-start.48 = (bf16[256,2048]{1,0:T(8,128)(2,1)}, bf16[256,2048]{1,0:T(8,128)(2,1)S(1)}, u32[]{:S(2)}) copy-start(bf16[256,2048]{1,0:T(8,128)(2,1)S(1)} %get-tuple-element.476.refs_2_) | copy-start | bytes 3145732
  202.0 23.4 %copy-start.49 = (bf16[256,2048]{1,0:T(8,128)(2,1)}, bf16[256,2048]{1,0:T(8,128)(2,1)S(1)}, u32[]{:S(2)}) copy-start(bf16[256,2048]{1,0:T(8,128)(2,1)S(1)} %get-tuple-element.475.refs_4_) | copy-start | bytes 3145732
  202.1 25.4 %copy-start.23 = (bf16[256,2048]{1,0:T(8,128)(2,1)S(1)}, bf16[256,2048]{1,0:T(8,128)(2,1)}, u32[]{:S(2)}) copy-start(bf16[256,2048]{1,0:T(8,128)(2,1)} %copy-done.22) | copy-start | bytes 3145732
  202.1 24.4 %collective-permute-start.12 = (bf16[256,2048]{1,0:T(8,128)(2,1)S(1)}, bf16[256,2048]{1,0:T(8,128)(2,1)S(1)}, u32[]{:S(2)}, u32[]{:S(2)}) collective-permute-start(bf16[256,2048]{1,0:T(8,128)(2,1)S(1)} %get-tuple-element.475.refs_4_), channel_id=1, source_target_pairs={{0,1},{3,2},{1,0},{2,3},{4,5},{7,6},{5,4},{6,7},{8,9},{11,10},{9,8... | collective-permute-start | bytes 3145736 | tf_op jit(solution)/shard_map/ppermute | solution.py:516
  205.1 21.3 %collective-permute-start.13 = (bf16[256,2048]{1,0:T(8,128)(2,1)S(1)}, bf16[256,2048]{1,0:T(8,128)(2,1)S(1)}, u32[]{:S(2)}, u32[]{:S(2)}) collective-permute-start(bf16[256,2048]{1,0:T(8,128)(2,1)S(1)} %get-tuple-element.476.refs_2_), channel_id=1, source_target_pairs={{1,2},{2,1},{5,6},{6,5},{9,10},{10,9},{13,14},{14,13},{17,18},{18,... | collective-permute-start | bytes 3145736 | tf_op jit(solution)/shard_map/ppermute | solution.py:519
  229.8 23.3 %copy-start.44 = (bf16[256,2048]{1,0:T(8,128)(2,1)}, bf16[256,2048]{1,0:T(8,128)(2,1)S(1)}, u32[]{:S(2)}) copy-start(bf16[256,2048]{1,0:T(8,128)(2,1)S(1)} %get-tuple-element.503.refs_2_) | copy-start | bytes 3145732
  229.8 23.3 %copy-start.45 = (bf16[256,2048]{1,0:T(8,128)(2,1)}, bf16[256,2048]{1,0:T(8,128)(2,1)S(1)}, u32[]{:S(2)}) copy-start(bf16[256,2048]{1,0:T(8,128)(2,1)S(1)} %get-tuple-element.502.refs_4_) | copy-start | bytes 3145732
  229.8 25.3 %copy-start.19 = (bf16[256,2048]{1,0:T(8,128)(2,1)S(1)}, bf16[256,2048]{1,0:T(8,128)(2,1)}, u32[]{:S(2)}) copy-start(bf16[256,2048]{1,0:T(8,128)(2,1)} %copy-done.18) | copy-start | bytes 3145732
  229.8 24.3 %collective-permute-start.14 = (bf16[256,2048]{1,0:T(8,128)(2,1)S(1)}, bf16[256,2048]{1,0:T(8,128)(2,1)S(1)}, u32[]{:S(2)}, u32[]{:S(2)}) collective-permute-start(bf16[256,2048]{1,0:T(8,128)(2,1)S(1)} %get-tuple-element.502.refs_4_), channel_id=1, source_target_pairs={{0,1},{3,2},{1,0},{2,3},{4,5},{7,6},{5,4},{6,7},{8,9},{11,10},{9,8... | collective-permute-start | bytes 3145736 | tf_op jit(solution)/shard_map/ppermute | solution.py:516
  232.6 21.5 %collective-permute-start.15 = (bf16[256,2048]{1,0:T(8,128)(2,1)S(1)}, bf16[256,2048]{1,0:T(8,128)(2,1)S(1)}, u32[]{:S(2)}, u32[]{:S(2)}) collective-permute-start(bf16[256,2048]{1,0:T(8,128)(2,1)S(1)} %get-tuple-element.503.refs_2_), channel_id=1, source_target_pairs={{1,2},{2,1},{5,6},{6,5},{9,10},{10,9},{13,14},{14,13},{17,18},{18,... | collective-permute-start | bytes 3145736 | tf_op jit(solution)/shard_map/ppermute | solution.py:519
  257.4 24.6 %collective-permute-start.16 = (bf16[256,2048]{1,0:T(8,128)(2,1)S(1)}, bf16[256,2048]{1,0:T(8,128)(2,1)S(1)}, u32[]{:S(2)}, u32[]{:S(2)}) collective-permute-start(bf16[256,2048]{1,0:T(8,128)(2,1)S(1)} %get-tuple-element.531.refs_4_), channel_id=1, source_target_pairs={{0,1},{3,2},{1,0},{2,3},{4,5},{7,6},{5,4},{6,7},{8,9},{11,10},{9,8... | collective-permute-start | bytes 3145736 | tf_op jit(solution)/shard_map/ppermute | solution.py:516
  260.5 21.6 %collective-permute-start.17 = (bf16[256,2048]{1,0:T(8,128)(2,1)S(1)}, bf16[256,2048]{1,0:T(8,128)(2,1)S(1)}, u32[]{:S(2)}, u32[]{:S(2)}) collective-permute-start(bf16[256,2048]{1,0:T(8,128)(2,1)S(1)} %get-tuple-element.532.refs_2_), channel_id=1, source_target_pairs={{1,2},{2,1},{5,6},{6,5},{9,10},{10,9},{13,14},{14,13},{17,18},{18,... | collective-permute-start | bytes 3145736 | tf_op jit(solution)/shard_map/ppermute | solution.py:519
  286.5 23.1 %copy-start.41 = (bf16[256,2048]{1,0:T(8,128)(2,1)}, bf16[256,2048]{1,0:T(8,128)(2,1)S(1)}, u32[]{:S(2)}) copy-start(bf16[256,2048]{1,0:T(8,128)(2,1)S(1)} %get-tuple-element.567.refs_2_) | copy-start | bytes 3145732
  286.5 23.2 %copy-start.7 = (bf16[256,2048]{1,0:T(8,128)(2,1)S(1)}, bf16[256,2048]{1,0:T(8,128)(2,1)}, u32[]{:S(2)}) copy-start(bf16[256,2048]{1,0:T(8,128)(2,1)} %get-tuple-element.533.refs_5_.refs_0_) | copy-start | bytes 3145732
  286.5 23.1 %collective-permute-start.18 = (bf16[256,2048]{1,0:T(8,128)(2,1)}, bf16[256,2048]{1,0:T(8,128)(2,1)}, u32[]{:S(2)}, u32[]{:S(2)}) collective-permute-start(bf16[256,2048]{1,0:T(8,128)(2,1)} %get-tuple-element.566.refs_4_), channel_id=1, source_target_pairs={{0,1},{3,2},{1,0},{2,3},{4,5},{7,6},{5,4},{6,7},{8,9},{11,10},{9,8... | collective-permute-start | bytes 3145736 | tf_op jit(solution)/shard_map/ppermute | solution.py:516
  288.9 20.7 %collective-permute-start.19 = (bf16[256,2048]{1,0:T(8,128)(2,1)S(1)}, bf16[256,2048]{1,0:T(8,128)(2,1)}, u32[]{:S(2)}, u32[]{:S(2)}) collective-permute-start(bf16[256,2048]{1,0:T(8,128)(2,1)S(1)} %get-tuple-element.567.refs_2_), channel_id=1, source_target_pairs={{1,2},{2,1},{5,6},{6,5},{9,10},{10,9},{13,14},{14,13},{17,18},{18,... | collective-permute-start | bytes 3145736 | tf_op jit(solution)/shard_map/ppermute | solution.py:519
  314.3 238.9 %reduce-scatter.6.cloned.1.call-start = ((), (), s32[]{:S(2)}) async-start(), calls=%async_computation.4 | async-start | bytes 884736 | tf_op jit(solution)/shard_map/reduce_scatter | solution.py:864
  314.4 20.8 %collective-permute-start.20 = (bf16[256,2048]{1,0:T(8,128)(2,1)}, bf16[256,2048]{1,0:T(8,128)(2,1)S(1)}, u32[]{:S(2)}, u32[]{:S(2)}) collective-permute-start(bf16[256,2048]{1,0:T(8,128)(2,1)} %copy-done.32), channel_id=1, source_target_pairs={{0,1},{3,2},{1,0},{2,3},{4,5},{7,6},{5,4},{6,7},{8,9},{11,10},{9,8... | collective-permute-start | bytes 3145736 | tf_op jit(solution)/shard_map/ppermute | solution.py:516
  316.3 18.9 %collective-permute-start.21 = (bf16[256,2048]{1,0:T(8,128)(2,1)S(1)}, bf16[256,2048]{1,0:T(8,128)(2,1)S(1)}, u32[]{:S(2)}, u32[]{:S(2)}) collective-permute-start(bf16[256,2048]{1,0:T(8,128)(2,1)S(1)} %copy-done.31), channel_id=1, source_target_pairs={{1,2},{2,1},{5,6},{6,5},{9,10},{10,9},{13,14},{14,13},{17,18},{18,... | collective-permute-start | bytes 3145736 | tf_op jit(solution)/shard_map/ppermute | solution.py:519
  339.4 20.7 %collective-permute-start.22 = (bf16[256,2048]{1,0:T(8,128)(2,1)S(1)}, bf16[256,2048]{1,0:T(8,128)(2,1)S(1)}, u32[]{:S(2)}, u32[]{:S(2)}) collective-permute-start(bf16[256,2048]{1,0:T(8,128)(2,1)S(1)} %get-tuple-element.613.refs_4_), channel_id=1, source_target_pairs={{0,1},{3,2},{1,0},{2,3},{4,5},{7,6},{5,4},{6,7},{8,9},{11,10},{9,8... | collective-permute-start | bytes 3145736 | tf_op jit(solution)/shard_map/ppermute | solution.py:516
  343.6 16.4 %collective-permute-start.23 = (bf16[256,2048]{1,0:T(8,128)(2,1)S(1)}, bf16[256,2048]{1,0:T(8,128)(2,1)S(1)}, u32[]{:S(2)}, u32[]{:S(2)}) collective-permute-start(bf16[256,2048]{1,0:T(8,128)(2,1)S(1)} %get-tuple-element.614.refs_2_), channel_id=1, source_target_pairs={{1,2},{2,1},{5,6},{6,5},{9,10},{10,9},{13,14},{14,13},{17,18},{18,... | collective-permute-start | bytes 3145736 | tf_op jit(solution)/shard_map/ppermute | solution.py:519
  353.1 1.6 collective-permute-start.24
  363.3 33.1 %copy-start.28 = (bf16[256,2048]{1,0:T(8,128)(2,1)}, bf16[256,2048]{1,0:T(8,128)(2,1)S(1)}, u32[]{:S(2)}) copy-start(bf16[256,2048]{1,0:T(8,128)(2,1)S(1)} %get-tuple-element.636.refs_2_) | copy-start | bytes 3145732
  363.4 33.1 %copy-start.29 = (bf16[256,2048]{1,0:T(8,128)(2,1)}, bf16[256,2048]{1,0:T(8,128)(2,1)S(1)}, u32[]{:S(2)}) copy-start(bf16[256,2048]{1,0:T(8,128)(2,1)S(1)} %get-tuple-element.635.refs_4_) | copy-start | bytes 3145732
  363.4 44.7 %collective-permute-start.25 = (bf16[256,2048]{1,0:T(8,128)(2,1)S(1)}, bf16[256,2048]{1,0:T(8,128)(2,1)S(1)}, u32[]{:S(2)}, u32[]{:S(2)}) collective-permute-start(bf16[256,2048]{1,0:T(8,128)(2,1)S(1)} %get-tuple-element.635.refs_4_), channel_id=1, source_target_pairs={{0,1},{3,2},{1,0},{2,3},{4,5},{7,6},{5,4},{6,7},{8,9},{11,10},{9,8... | collective-permute-start | bytes 3145736 | tf_op jit(solution)/shard_map/ppermute | solution.py:516
  367.5 40.5 %collective-permute-start.26 = (bf16[256,2048]{1,0:T(8,128)(2,1)S(1)}, bf16[256,2048]{1,0:T(8,128)(2,1)S(1)}, u32[]{:S(2)}, u32[]{:S(2)}) collective-permute-start(bf16[256,2048]{1,0:T(8,128)(2,1)S(1)} %get-tuple-element.636.refs_2_), channel_id=1, source_target_pairs={{1,2},{2,1},{5,6},{6,5},{9,10},{10,9},{13,14},{14,13},{17,18},{18,... | collective-permute-start | bytes 3145736 | tf_op jit(solution)/shard_map/ppermute | solution.py:519
  368.4 13.8 %collective-permute-start.27 = (bf16[2,64,1152]{2,1,0:T(8,128)(2,1)S(1)}, bf16[2,64,1152]{2,1,0:T(8,128)(2,1)S(1)}, u32[]{:S(2)}, u32[]{:S(2)}) collective-permute-start(bf16[2,64,1152]{2,1,0:T(8,128)(2,1)S(1)} %get-tuple-element.639), channel_id=1, source_target_pairs={{0,8},{4,12},{8,0},{12,4},{16,24},{20,28},{24,16},{28,20},{1,9},{5... | collective-permute-start | bytes 884744 | tf_op jit(solution)/shard_map/ppermute | solution.py:436
  382.5 13.5 %collective-permute-start.28 = (bf16[2,64,1152]{2,1,0:T(8,128)(2,1)S(1)}, bf16[2,64,1152]{2,1,0:T(8,128)(2,1)S(1)}, u32[]{:S(2)}, u32[]{:S(2)}) collective-permute-start(bf16[2,64,1152]{2,1,0:T(8,128)(2,1)S(1)} %get-tuple-element.644), channel_id=1, source_target_pairs={{0,16},{4,20},{8,24},{12,28},{16,0},{20,4},{24,8},{28,12},{1,17},{... | collective-permute-start | bytes 884744 | tf_op jit(solution)/shard_map/ppermute | solution.py:436
  413.8 27.0 %collective-permute-start.29 = (bf16[256,2048]{1,0:T(8,128)(2,1)}, bf16[256,2048]{1,0:T(8,128)(2,1)}, u32[]{:S(2)}, u32[]{:S(2)}) collective-permute-start(bf16[256,2048]{1,0:T(8,128)(2,1)} %get-tuple-element.670.refs_4_), channel_id=1, source_target_pairs={{0,1},{3,2},{1,0},{2,3},{4,5},{7,6},{5,4},{6,7},{8,9},{11,10},{9,8... | collective-permute-start | bytes 3145736 | tf_op jit(solution)/shard_map/ppermute | solution.py:516
  416.2 24.5 %collective-permute-start.30 = (bf16[256,2048]{1,0:T(8,128)(2,1)}, bf16[256,2048]{1,0:T(8,128)(2,1)}, u32[]{:S(2)}, u32[]{:S(2)}) collective-permute-start(bf16[256,2048]{1,0:T(8,128)(2,1)} %get-tuple-element.671.refs_2_), channel_id=1, source_target_pairs={{1,2},{2,1},{5,6},{6,5},{9,10},{10,9},{13,14},{14,13},{17,18},{18,... | collective-permute-start | bytes 3145736 | tf_op jit(solution)/shard_map/ppermute | solution.py:519
  443.5 16.2 %copy-start.26 = (bf16[256,2048]{1,0:T(8,128)(2,1)}, bf16[256,2048]{1,0:T(8,128)(2,1)S(1)}, u32[]{:S(2)}) copy-start(bf16[256,2048]{1,0:T(8,128)(2,1)S(1)} %get-tuple-element.689.refs_2_) | copy-start | bytes 3145732
  457.9 21.3 %collective-permute-start.31 = (bf16[256,2048]{1,0:T(8,128)(2,1)}, bf16[256,2048]{1,0:T(8,128)(2,1)}, u32[]{:S(2)}, u32[]{:S(2)}) collective-permute-start(bf16[256,2048]{1,0:T(8,128)(2,1)} %copy-done.27), channel_id=1, source_target_pairs={{0,1},{3,2},{1,0},{2,3},{4,5},{7,6},{5,4},{6,7},{8,9},{11,10},{9,8... | collective-permute-start | bytes 3145736 | tf_op jit(solution)/shard_map/ppermute | solution.py:516
  459.6 19.5 %collective-permute-start.32 = (bf16[256,2048]{1,0:T(8,128)(2,1)S(1)}, bf16[256,2048]{1,0:T(8,128)(2,1)}, u32[]{:S(2)}, u32[]{:S(2)}) collective-permute-start(bf16[256,2048]{1,0:T(8,128)(2,1)S(1)} %get-tuple-element.689.refs_2_), channel_id=1, source_target_pairs={{1,2},{2,1},{5,6},{6,5},{9,10},{10,9},{13,14},{14,13},{17,18},{18,... | collective-permute-start | bytes 3145736 | tf_op jit(solution)/shard_map/ppermute | solution.py:519
  485.0 110.2 %reduce-scatter.8.cloned.1.call-start = ((), (), s32[]{:S(2)}) async-start(), calls=%async_computation.5 | async-start | bytes 9437184 | tf_op jit(solution)/shard_map/reduce_scatter | solution.py:865
  486.2 18.0 %collective-permute-start.33 = (bf16[256,2048]{1,0:T(8,128)(2,1)S(1)}, bf16[256,2048]{1,0:T(8,128)(2,1)S(1)}, u32[]{:S(2)}, u32[]{:S(2)}) collective-permute-start(bf16[256,2048]{1,0:T(8,128)(2,1)S(1)} %copy-done.38), channel_id=1, source_target_pairs={{0,1},{3,2},{1,0},{2,3},{4,5},{7,6},{5,4},{6,7},{8,9},{11,10},{9,8... | collective-permute-start | bytes 3145736 | tf_op jit(solution)/shard_map/ppermute | solution.py:516
  488.3 15.9 %collective-permute-start.34 = (bf16[256,2048]{1,0:T(8,128)(2,1)S(1)}, bf16[256,2048]{1,0:T(8,128)(2,1)S(1)}, u32[]{:S(2)}, u32[]{:S(2)}) collective-permute-start(bf16[256,2048]{1,0:T(8,128)(2,1)S(1)} %copy-done.36), channel_id=1, source_target_pairs={{1,2},{2,1},{5,6},{6,5},{9,10},{10,9},{13,14},{14,13},{17,18},{18,... | collective-permute-start | bytes 3145736 | tf_op jit(solution)/shard_map/ppermute | solution.py:519
  507.6 19.1 %collective-permute-start.35 = (bf16[256,2048]{1,0:T(8,128)(2,1)S(1)}, bf16[256,2048]{1,0:T(8,128)(2,1)S(1)}, u32[]{:S(2)}, u32[]{:S(2)}) collective-permute-start(bf16[256,2048]{1,0:T(8,128)(2,1)S(1)} %get-tuple-element.759.refs_4_), channel_id=1, source_target_pairs={{0,1},{3,2},{1,0},{2,3},{4,5},{7,6},{5,4},{6,7},{8,9},{11,10},{9,8... | collective-permute-start | bytes 3145736 | tf_op jit(solution)/shard_map/ppermute | solution.py:516
  512.0 14.7 %collective-permute-start.36 = (bf16[256,2048]{1,0:T(8,128)(2,1)S(1)}, bf16[256,2048]{1,0:T(8,128)(2,1)S(1)}, u32[]{:S(2)}, u32[]{:S(2)}) collective-permute-start(bf16[256,2048]{1,0:T(8,128)(2,1)S(1)} %get-tuple-element.760.refs_2_), channel_id=1, source_target_pairs={{1,2},{2,1},{5,6},{6,5},{9,10},{10,9},{13,14},{14,13},{17,18},{18,... | collective-permute-start | bytes 3145736 | tf_op jit(solution)/shard_map/ppermute | solution.py:519
  530.0 21.9 %collective-permute-start.37 = (bf16[256,2048]{1,0:T(8,128)(2,1)S(1)}, bf16[256,2048]{1,0:T(8,128)(2,1)S(1)}, u32[]{:S(2)}, u32[]{:S(2)}) collective-permute-start(bf16[256,2048]{1,0:T(8,128)(2,1)S(1)} %get-tuple-element.771.refs_3_), channel_id=1, source_target_pairs={{1,0},{2,3},{5,4},{6,7},{9,8},{10,11},{13,12},{14,15},{17,16},{18,... | collective-permute-start | bytes 3145736 | tf_op jit(solution)/shard_map/ppermute | solution.py:516
  531.3 20.6 %collective-permute-start.38 = (bf16[256,2048]{1,0:T(8,128)(2,1)S(1)}, bf16[256,2048]{1,0:T(8,128)(2,1)S(1)}, u32[]{:S(2)}, u32[]{:S(2)}) collective-permute-start(bf16[256,2048]{1,0:T(8,128)(2,1)S(1)} %get-tuple-element.772.refs_1_), channel_id=1, source_target_pairs={{1,2},{2,1},{5,6},{6,5},{9,10},{10,9},{13,14},{14,13},{17,18},{18,... | collective-permute-start | bytes 3145736 | tf_op jit(solution)/shard_map/ppermute | solution.py:519
  553.2 23.6 %collective-permute-start.39 = (bf16[256,2048]{1,0:T(8,128)(2,1)S(1)}, bf16[256,2048]{1,0:T(8,128)(2,1)S(1)}, u32[]{:S(2)}, u32[]{:S(2)}) collective-permute-start(bf16[256,2048]{1,0:T(8,128)(2,1)S(1)} %get-tuple-element.782.refs_1_), channel_id=1, source_target_pairs={{1,0},{2,3},{5,4},{6,7},{9,8},{10,11},{13,12},{14,15},{17,16},{18,... | collective-permute-start | bytes 3145736 | tf_op jit(solution)/shard_map/ppermute | solution.py:516
  555.9 15.6 %collective-permute-start.40 = (f32[256]{0:T(256)S(1)}, f32[256]{0:T(256)S(1)}, u32[]{:S(2)}, u32[]{:S(2)}) collective-permute-start(f32[256]{0:T(256)S(1)} %bitcast.79), channel_id=1, source_target_pairs={{0,1},{1,0},{2,3},{3,2},{4,5},{5,4},{6,7},{7,6},{8,9},{9,8},{10,11... | collective-permute-start | bytes 3080 | tf_op jit(solution)/shard_map/ppermute | solution.py:887
  571.5 4.7 collective-permute-start.41
  (68 other events, 387.3 us)
Sparse Core Ops, SparseCore 0:
  11.8 100.6 all-gather.2
  314.4 124.8 reduce-scatter.3
  485.1 35.0 reduce-scatter.5
  523.9 71.2 reduce-scatter.7

commit v4 on v3

--- a/solution.py
+++ b/solution.py
@@ -94,12 +94,22 @@
         taken = 1.0 - y * (1.0 / n) * taken
     taken = y * taken
     cum = exact(triangle(True).astype(f32), la, ((1,), (0,)))
-    total = exact(la, jnp.ones((CHUNK, 128), f32), ((0,), (0,)))
-    return la, cum, jnp.exp(-cum) * taken, total
+    return cum, jnp.exp(-cum) * taken
+
+
+def turned_last(cum):
+    return jnp.broadcast_to(cum[CHUNK - 1 :, :], cum.shape).T
+
+
+def halves_sum(ones, values):
+    high, low = halves(values)
+    both = nn(ones.astype(bf16), jnp.concatenate([high, low], 1))
+    width = values.shape[1]
+    return both[:, :width] + both[:, width:]
 
 
 def project_kernel(per_part, x_ref, gain_ref, wq_ref, wk_ref, wv_ref, wf_ref, bias_ref,
-                   xn_ref, q_ref, k_ref, v_ref, z_ref, s_ref, d_ref, sent_ref, state, decay):
+                   xn_ref, q_ref, k_ref, v_ref, z_ref, cum_ref, in_ref, s_ref, d_ref, sent_ref, state, decay):
     @pl.when(lax.rem(pl.program_id(0), per_part) == 0)
     def _():
         state[...] = jnp.zeros_like(state)
@@ -116,7 +126,10 @@
     width = k_ref.shape[1]
     for c in range(x_ref.shape[0] // CHUNK):
         rows = pl.ds(c * CHUNK, CHUNK)
-        _, _, inflow, total = gates(z_ref[rows, :])
+        cum, inflow = gates(z_ref[rows, :])
+        cum_ref[rows, :] = cum
+        in_ref[rows, :] = inflow
+        total = turned_last(cum)
         spread = inflow.astype(bf16)
         keep = jnp.exp(total[:, :1])
         state[:, :width] = keep * (state[:, :width] + tn(spread, k_ref[rows, :]))
@@ -127,7 +140,7 @@
     pack(sent_ref, 0, jnp.exp(decay[...]), state[...])
 
 
-def read_kernel(q_ref, k_ref, v_ref, z_ref, e0_ref, wo_ref, o_ref, p_ref, sc_ref, e_ref, left_ref, att_ref, state):
+def read_kernel(q_ref, k_ref, v_ref, cum_ref, in_ref, e0_ref, wo_ref, o_ref, p_ref, sc_ref, e_ref, left_ref, att_ref, state):
     @pl.when(pl.program_id(0) == 0)
     def _():
         state[...] = e0_ref[...]
@@ -135,7 +148,8 @@
     width = q_ref.shape[1]
     lower = triangle(True)
     q, k, v = q_ref[...], k_ref[...], v_ref[...]
-    _, cum, inflow, total = gates(z_ref[...])
+    cum, inflow = cum_ref[...], in_ref[...]
+    total = turned_last(cum)
     growth = jnp.exp(cum)
     e_ref[0] = state[...]
     i_hi, i_lo = halves(inflow)
@@ -157,8 +171,8 @@
     left_ref[...] = state[...]
 
 
-def back_kernel(dhn_ref, hid_ref, cot_ref, gain_ref, wo_ref, q_ref, k_ref, v_ref, z_ref, p_ref, sc_ref, e_ref,
-                dhid_ref, datt_ref, dq_ref, dkl_ref, dvl_ref, h_ref, x1_ref, g_ref, s_ref, d_ref, gg_ref, state, decay):
+def back_kernel(dhn_ref, hid_ref, cot_ref, gain_ref, wo_ref, q_ref, k_ref, v_ref, cum_ref, in_ref, p_ref, sc_ref,
+                e_ref, dhid_ref, datt_ref, dq_ref, dkl_ref, dvl_ref, h_ref, x1_ref, g_ref, s_ref, d_ref, gg_ref, state, decay):
     step = pl.program_id(0)
 
     @pl.when(step == 0)
@@ -184,7 +198,8 @@
     do = nt(datt, wo_ref[...]).astype(bf16)
     lower, upper = triangle(True), triangle(False)
     q, k, v = q_ref[...], k_ref[...], v_ref[...]
-    _, cum, inflow, total = gates(z_ref[...])
+    cum, inflow = cum_ref[...], in_ref[...]
+    total = turned_last(cum)
     growth = jnp.exp(cum)
     p = p_ref[...]
     i_hi, i_lo = halves(inflow)
@@ -215,7 +230,7 @@
     d_ref[...] = jnp.exp(decay[...])
 
 
-def last_kernel(l0_ref, k_ref, v_ref, z_ref, e_ref, g_ref, dkl_ref, dvl_ref, h_ref, x1_ref, dq_ref, x_ref,
+def last_kernel(l0_ref, k_ref, v_ref, z_ref, cum_ref, in_ref, e_ref, g_ref, dkl_ref, dvl_ref, h_ref, x1_ref, dq_ref, x_ref,
                 wq_ref, wk_ref, wv_ref, wf_ref, dk_ref, dv_ref, dz_ref, dxn_ref, bias_ref, gg_ref, state):
     step = pl.program_id(0)
 
@@ -226,9 +241,9 @@
         bias_ref[...] = jnp.zeros_like(bias_ref)
 
     width = k_ref.shape[1]
-    low, up = triangle(True).astype(f32), triangle(False).astype(f32)
     k, v, z = k_ref[...], v_ref[...], z_ref[...]
-    _, cum, inflow, total = gates(z)
+    cum, inflow = cum_ref[...], in_ref[...]
+    total = turned_last(cum)
     i_hi = inflow.astype(bf16)
     keep = jnp.exp(total[:, :1])
     lg = keep * state[...]
@@ -239,13 +254,13 @@
     dv_ref[...] = dv
     x1 = x1_ref[...]
     x2 = nt(k, lg_k) + nt(v, lg_v)
-    met = exact(jnp.ones((8, 2 * width), f32), lg * e_ref[0], ((1,), (1,)))
+    met = jnp.broadcast_to(jnp.sum(lg * e_ref[0], axis=1, keepdims=True), (lg.shape[0], CHUNK)).T
     h, r1 = h_ref[...], inflow * x1
     dla = (
-        exact(up, h - r1, ((1,), (0,)))
+        halves_sum(triangle(False), h - r1)
         + r1
-        + exact(low, inflow * x2, ((1,), (0,)))
-        + met[:1]
+        + halves_sum(triangle(True), inflow * x2)
+        + met
         - jnp.exp(-cum) * (x1 + x2)
     )
     rate = lax.logistic(-z)
@@ -343,16 +358,54 @@
         out_ref[:, i] = block.reshape(blocks, width, units)
 
 
-def attn_grad_kernel(count, *refs):
-    out_ref, dzw_ref = refs[-2:]
-    xn_ref = refs[0]
-    datt, dq, dk, dv, dz, o = (refs[1 + i * count : 1 + (i + 1) * count] for i in range(6))
+def query_grad_kernel(count, *refs):
+    xn_ref, out_ref = refs[0], refs[-1]
+    datt, dq, o = (refs[1 + i * count : 1 + (i + 1) * count] for i in range(3))
     rows, width = dq[0].shape
     xn = [xn_ref[i * rows : (i + 1) * rows, :] for i in range(count)]
-    for i, grads in enumerate((dq, dk, dv)):
-        out_ref[:, i * width : (i + 1) * width] = summed([(x, g[...]) for x, g in zip(xn, grads)])
-    out_ref[:, 3 * width :] = summed([(d[...], r[...]) for d, r in zip(datt, o)])
-    dzw_ref[...] = summed([(x, g[...]) for x, g in zip(xn, dz)])
+    out_ref[:, :width] = summed([(x, g[...]) for x, g in zip(xn, dq)])
+    out_ref[:, width:] = summed([(d[...], r[...]) for d, r in zip(datt, o)])
+
+
+def state_grad_kernel(count, *refs):
+    xn_ref, out_ref = refs[0], refs[-1]
+    dk, dv, dz, bias, gain1, gain2 = (refs[1 + i * count : 1 + (i + 1) * count] for i in range(6))
+    rows, width = dk[0].shape
+    slots = dz[0].shape[1]
+    groups, high, _ = out_ref.shape
+    span = high - 16
+    xn = [xn_ref[i * rows : (i + 1) * rows, :] for i in range(count)]
+    for i, grads in enumerate((dk, dv)):
+        block = summed([(x, g[...]) for x, g in zip(xn, grads)])
+        out_ref[:, :span, i * width : (i + 1) * width] = block.reshape(groups, span, width)
+    forget = tn(xn[0], dz[0][...])
+    for x, g in zip(xn[1:], dz[1:]):
+        forget = forget + tn(x, g[...])
+    pad = 128 - slots % 128
+
+    def padded(values):
+        return jnp.concatenate([values, jnp.zeros((values.shape[0], pad), f32)], 1)
+
+    def column(parts):
+        total = parts[0][...]
+        for part in parts[1:]:
+            total = total + part[...]
+        return jnp.sum(total.T, axis=1, keepdims=True)
+
+    small = padded(forget)
+    lane = lax.broadcasted_iota(jnp.int32, small.shape, 1)
+    small = jnp.where(lane == slots, column(gain2), jnp.where(lane == slots + 1, column(gain1), small))
+    out_ref[:, :span, 2 * width :] = small.astype(bf16).reshape(groups, span, slots + pad)
+    total = bias[0][...]
+    for part in bias[1:]:
+        total = total + part[...]
+    total = padded(jnp.broadcast_to(jnp.sum(total, axis=0, keepdims=True), (16, slots)))
+    upper = total.astype(bf16).astype(f32)
+    row = lax.broadcasted_iota(jnp.int32, total.shape, 0)
+    tail = jnp.where(row == 0, upper, jnp.where(row == 1, total - upper, 0.0)).astype(bf16)
+    for g in range(groups):
+        out_ref[g, span:, : 2 * width] = jnp.zeros((16, 2 * width), bf16)
+        out_ref[g, span:, 2 * width :] = tail
 
 
 def pack(ref, m, decay, state):
@@ -470,7 +523,7 @@
             work(pl.ds(pl.multiple_of(i * 32, 32), 32))
 
     def both(a, b, rows):
-        return (a[rows, :].astype(f32) + b[rows, :].astype(f32)).astype(bf16)
+        return a[rows, :] + b[rows, :]
 
     @pl.when(end)
     def _():
@@ -562,27 +615,31 @@
     anywhere = pl.BlockSpec(memory_space=pl.ANY)
     in_place = pl.BlockSpec(memory_space=pltpu.VMEM)
 
-    stacked = jnp.stack([w_gate, w_up, w_down.T])
-    x, stacked = lax.optimization_barrier((x, stacked))
-    full = lax.all_gather(stacked, "seq")
-
     all_rows = lambda c: pl.BlockSpec((TILE, c), lambda i: (i, 0))
     by_part = lambda c: pl.BlockSpec((1, slots, c), lambda i: (i // per_part, 0, 0))
-    xn, q, k, v, z, local, decay, sent = call(
+    xn, q, k, v, z, cum, inflow, local, decay, sent = call(
         "project",
         functools.partial(project_kernel, per_part),
         (rows // TILE,),
         [all_rows(width), fixed((1, width))] + [fixed((width, head))] * 3 + [fixed((width, slots)), fixed((1, slots))],
-        [all_rows(width), all_rows(head), all_rows(head), all_rows(head), all_rows(slots), by_part(2 * head), by_part(128),
-         by_part(2 * head + 128)],
+        [all_rows(width), all_rows(head), all_rows(head), all_rows(head)] + [all_rows(slots)] * 3
+        + [by_part(2 * head), by_part(128), by_part(2 * head + 128)],
         [shaped((rows, width), bf16)] + [shaped((rows, head), bf16)] * 3
-        + [shaped((rows, slots), f32), shaped((parts, slots, 2 * head), f32), shaped((parts, slots, 128), f32),
-           shaped((parts, slots, 2 * head + 128), bf16)],
+        + [shaped((rows, slots), f32)] * 3 + [shaped((parts, slots, 2 * head), f32), shaped((parts, slots, 128), f32),
+                                             shaped((parts, slots, 2 * head + 128), bf16)],
         [state_scratch, decay_scratch],
         cost=cost(2 * rows * width * (3 * head + slots), 2 * rows * width * 3 + 2 * width * 3 * head),
-        loose_out=(5, 6, 7),
+        loose_out=(7, 8, 9),
     )(x, gain1, w_query, w_key, w_value, w_forget, forget_bias.reshape(1, slots))
-    entering = scan_states(n_seq, local, decay, sent, False)
+    stacked = []
+
+    def stack_weights(sent):
+        gate, down, sent = lax.optimization_barrier((w_gate, w_down, sent))
+        stacked.append(jnp.stack([gate, w_up, down.T]))
+        return sent
+
+    entering = scan_states(n_seq, local, decay, sent, False, tie=stack_weights)
+    full = lax.all_gather(stacked[0], "seq")
 
     def chunk_rows(m, t, columns, back):
         start = (m * pieces + t) * chunks
@@ -607,16 +664,17 @@
             "read",
             read_kernel,
             (chunks,),
-            [chunk_rows(m, t, head, False)] * 3 + [chunk_rows(m, t, slots, False), state_of(which), fixed((head, width))],
+            [chunk_rows(m, t, head, False)] * 3 + [chunk_rows(m, t, slots, False)] * 2
+            + [state_of(which), fixed((head, width))],
             [own_rows(head, False), own_rows(slots, False), own_rows(slots, False), chunk_state(False),
              pl.BlockSpec((None, slots, 2 * head), lambda i: (0, 0, 0)), own_rows(width, False)],
             [shaped((TILE, head), bf16), shaped((TILE, slots), f32), shaped((TILE, slots), f32), states_shape,
              shaped((1, slots, 2 * head), f32), shaped((TILE, width), bf16)],
             [state_scratch],
             cost=cost(2 * TILE * head * (600 + width), 2 * TILE * (head * 4 + width) + 2 * head * width),
-            loose=(4,),
+            loose=(5,),
             loose_out=(4, 5),
-        )(q, k, v, z, entering, w_out)
+        )(q, k, v, cum, inflow, entering, w_out)
 
     def feed(m, t, attended):
         tile_count = pl.cdiv(units, TILE)
@@ -675,7 +733,7 @@
             (chunks,),
             [own_rows(width, True), own_rows(width, True), chunk_rows(m, t, width, True), fixed((1, width)),
              fixed((head, width))]
-            + [chunk_rows(m, t, head, True)] * 3 + [chunk_rows(m, t, slots, True)] + [own_rows(slots, True)] * 2
+            + [chunk_rows(m, t, head, True)] * 3 + [chunk_rows(m, t, slots, True)] * 2 + [own_rows(slots, True)] * 2
             + [chunk_state(True)],
             [own_rows(width, True)] * 2 + [own_rows(head, True)] * 3 + [own_rows(slots, True)] * 2
             + [chunk_state(True), whole((slots, 2 * head)), whole((slots, 128)), whole((8, width))],
@@ -687,7 +745,7 @@
             cost=cost(2 * TILE * width * head + 2 * TILE * head * 1500, TILE * width * 14 + TILE * head * 20),
             loose=(0,),
             loose_out=(8, 9),
-        )(dhn, hidden, cot, gain2, w_out, q, k, v, z, p, scores, e_chunks)
+        )(dhn, hidden, cot, gain2, w_out, q, k, v, cum, inflow, p, scores, e_chunks)
 
     def last(m, t, leaving, saved):
         dq, dk_local, dv_local, h_sum, x_local, g_chunks = saved
@@ -696,7 +754,7 @@
             last_kernel,
             (chunks,),
             [state_of(m * pieces + t), chunk_rows(m, t, head, True), chunk_rows(m, t, head, True),
-             chunk_rows(m, t, slots, True), chunk_state(True), chunk_state(True), own_rows(head, True),
+             *[chunk_rows(m, t, slots, True)] * 3, chunk_state(True), chunk_state(True), own_rows(head, True),
              own_rows(head, True), own_rows(slots, True), own_rows(slots, True), own_rows(head, True),
              chunk_rows(m, t, width, True)] + [fixed((width, head))] * 3 + [fixed((width, slots))],
             [own_rows(head, True), own_rows(head, True), own_rows(slots, True), own_rows(width, True), whole((8, slots)),
@@ -707,7 +765,7 @@
             cost=cost(2 * TILE * width * (3 * head + slots), TILE * width * 8 + TILE * head * 20 + width * head * 6),
             loose=(0,),
             loose_out=(3,),
-        )(leaving, k, v, z, reads[m, t][3], g_chunks, dk_local, dv_local, h_sum, x_local, dq, x,
+        )(leaving, k, v, z, cum, inflow, reads[m, t][3], g_chunks, dk_local, dv_local, h_sum, x_local, dq, x,
           w_query, w_key, w_value, w_forget)
 
     line = Line()
@@ -817,52 +875,49 @@
     )
 
     def next_step(sent):
-        live["sent"] = sent
+        live["sent"], live["xn"] = sent, xn
         end(live.pop(("ffn_part", 1, 1)), ("ffn", 0, 0))
         start()
         return live.pop("sent")
 
     live["leaving"] = scan_states(n_seq, *folded, True, own, pieces, next_step)
+    xn_started = live.pop("xn")
+    grad_columns = [pl.BlockSpec((rows, TILE), lambda j: (0, j))]
+    piece_columns = [pl.BlockSpec((TILE, TILE), lambda j: (0, j))] * len(every)
+    piece_whole = [fixed((TILE, head))] * len(every)
+    live["query_grads"] = call(
+        "query_grads",
+        functools.partial(query_grad_kernel, len(every)),
+        (width // TILE,),
+        grad_columns + piece_columns + piece_whole * 2,
+        pl.BlockSpec((TILE, 2 * head), lambda j: (j, 0)),
+        shaped((width, 2 * head), bf16),
+        cost=cost(4 * rows * width * head, 4 * rows * width + 4 * rows * head + 4 * width * head),
+    )(xn_started, *[backs[key][1] for key in every], *[backs[key][2] for key in every], *[reads[key][0] for key in every])
     go_last(0, 0)
     end(live.pop(("dxn_part", 0, 0)), ("ffn", 0, 1))
     start()
+    query_shares = lax.psum_scatter(live.pop("query_grads"), "seq", scatter_dimension=0, tiled=True)
     go_last(0, 1)
     go_last(1, 0)
+    go_last(1, 1)
+    live["xn"] = xn
     end(live.pop(("dxn_part", 0, 1)), ("ffn", 1, 0))
     start()
-    go_last(1, 1)
     live.pop("leaving")
-    attn_grads, forget_grads = call(
-        "attn_grads",
-        functools.partial(attn_grad_kernel, len(every)),
+    few = [pl.BlockSpec((8, TILE), lambda j: (0, j))] * len(every)
+    live["state_grads"] = call(
+        "state_grads",
+        functools.partial(state_grad_kernel, len(every)),
         (width // TILE,),
-        [pl.BlockSpec((rows, TILE), lambda j: (0, j))] + [pl.BlockSpec((TILE, TILE), lambda j: (0, j))] * len(every)
-        + [fixed((TILE, head))] * (3 * len(every)) + [fixed((TILE, slots))] * len(every)
-        + [fixed((TILE, head))] * len(every),
-        [pl.BlockSpec((TILE, 4 * head), lambda j: (j, 0)), pl.BlockSpec((TILE, slots), lambda j: (j, 0))],
-        [shaped((width, 4 * head), bf16), shaped((width, slots), bf16)],
-        cost=cost(2 * rows * width * (4 * head + slots), 4 * rows * width + 8 * rows * head + 8 * width * head),
-    )(xn, *[backs[key][1] for key in every], *[backs[key][2] for key in every],
-      *[lasts[key][i] for i in range(3) for key in every], *[reads[key][0] for key in every])
-    live["attn_grads"] = attn_grads
-    bias_sum = jnp.sum(sum(n[4] for n in lasts.values()), 0)
-    gain1_sum = jnp.sum(sum(n[5] for n in lasts.values()), 0)
-    gain2_sum = jnp.sum(sum(n[10] for n in backs.values()), 0)
-    small = jnp.concatenate(
-        [
-            forget_grads,
-            gain2_sum.astype(bf16)[:, None],
-            gain1_sum.astype(bf16)[:, None],
-            jnp.zeros((width, 128 - 2 - slots % 128), bf16),
-        ],
-        1,
-    ).reshape(n_seq, span, -1)
-    bias_row = jnp.pad(jnp.stack(halves(bias_sum)), ((0, 14), (0, small.shape[2] - slots)))
-    live["small"] = jnp.concatenate([small, jnp.broadcast_to(bias_row, (n_seq,) + bias_row.shape)], 1)
+        grad_columns + piece_whole * 2 + [fixed((TILE, slots))] * len(every) + [fixed((8, slots))] * len(every) + few * 2,
+        pl.BlockSpec((group, span + 16, 2 * head + 128), lambda j: (j, 0, 0)),
+        shaped((n_seq, span + 16, 2 * head + 128), bf16),
+        cost=cost(4 * rows * width * head, 2 * rows * width + 4 * rows * head + 4 * width * head),
+    )(live.pop("xn"), *[lasts[key][i] for i in (0, 1, 2, 4, 5) for key in every], *[backs[key][10] for key in every])
     end(live.pop(("dxn_part", 1, 0)), ("ffn", 1, 1))
     start()
-    small_shares = lax.psum_scatter(live.pop("small"), "seq", scatter_dimension=0)
-    attn_shares = lax.psum_scatter(live.pop("attn_grads"), "seq", scatter_dimension=0, tiled=True)
+    state_shares = lax.psum_scatter(live.pop("state_grads"), "seq", scatter_dimension=0)
     finish_out(0, 0)
     finish_out(0, 1)
     live["out"], live["ffn_shares"] = outs[0], ffn_shares
@@ -877,31 +932,32 @@
     start()
     in_grads[0] = live.pop("in_grad")
     finish_grad(0, 1)
-    live["in_grad"], live["small"] = in_grads[0], small_shares
+    live["in_grad"] = in_grads[0]
     end(None, ("dxn", 1, 0))
     start()
-    in_grads[0], small_shares = live.pop("in_grad"), live.pop("small").astype(f32)
-    gain1_total = small_shares[:span, slots + 1]
+    in_grads[0] = live.pop("in_grad")
+    gain1_total = state_shares[:span, 2 * head + slots + 1].astype(f32)
     bit = 1
     while bit < n_head:
         gain1_total = gain1_total + lax.ppermute(gain1_total, "head", [(i, i ^ bit) for i in range(n_head)])
         bit *= 2
     finish_grad(1, 0)
     end(None, ("dxn", 1, 1))
-    live["dxn", 1, 1], attn_shares = lax.optimization_barrier((live["dxn", 1, 1], attn_shares))
-    attn_shares = attn_shares.astype(f32)
     finish_grad(1, 1)
+    query_shares = query_shares.astype(f32)
+    state_shares = state_shares.astype(f32)
+    small_shares = state_shares[:, 2 * head :]
 
     return (
         live["out"],
         in_grads[0],
         gain1_total,
-        attn_shares[:, :head],
-        attn_shares[:, head : 2 * head],
-        attn_shares[:, 2 * head : 3 * head],
+        query_shares[:, :head],
+        state_shares[:span, :head],
+        state_shares[:span, head : 2 * head],
         small_shares[:span, :slots],
         small_shares[span, :slots] + small_shares[span + 1, :slots],
-        attn_shares[:, 3 * head :].T,
+        query_shares[:, head:].T,
         small_shares[:span, slots],
         ffn_shares[0].astype(f32),
         ffn_shares[1].astype(f32),

time: 618 us -> 601 us (0.972)
  waiting for transfers between devices: 151 us -> 114 us
  local copies, waits for them, and re-layouts: 40.6 us -> 50.1 us
    ppermute x6, waiting for transfers between devices: 47.6 us -> 36.2 us  [scan_states(): got = lax.ppermute(sent, 'seq', [(i, i ^ bit) for i in range(n)])]
    ppermute x18, waiting for transfers between devices: 77.7 us -> 66.7 us  [step(): outer = lax.ppermute(payload, 'head', way)]
    unnamed x177 -> x166, local copies, waits for them, and re-layouts: 36 us -> 45.3 us
    reduce_scatter x2, waiting for transfers between devices: 18.3 us -> 11.3 us  [the longest x1 11.3 us: on_device(): lax.psum_scatter(live.pop('state_grads'), 'seq', scatter_dimension=0)]
    ppermute x2, waiting for transfers between devices: 6.28 us -> 0.08 us  [on_device(): lax.ppermute(gain1_total, 'head', [(i, i ^ bit) for i in range(n_head)])]
    pallas_call x28 -> x29, Pallas kernels: 266 us -> 268 us  [run(): function(*[o if i in loose or spec.memory_space == pltpu.SMEM else pltpu....]
  transfers between devices with their start and end apart: 46 -> 46, of which waited for: 15 -> 16; matrix products, arithmetic and copies ran while one was open for 2% -> 3% of each run, Pallas kernels for 47% -> 47%
where the time goes in v4:
time: 601 us; the launch traced here: 592 us
  Pallas kernels  313 us (52%)
  waiting for transfers between devices  114 us (19%)
  starting transfers between devices  87.9 us (15%)
  local copies, waits for them, and re-layouts  50.1 us (8%)
  between operations  15.1 us (3%)
  other arithmetic  11 us (2%)
    pallas_call x29, Pallas kernels, run(): function(*[o if i in loose or spec.memory_space == pltpu.SMEM else pltpu....  268 us
    ppermute x18, waiting for transfers between devices, step(): outer = lax.ppermute(payload, 'head', way)  66.7 us
    ppermute x18, starting transfers between devices, step(): outer = lax.ppermute(payload, 'head', way)  53.4 us
    unnamed x166, local copies, waits for them, and re-layouts  45.3 us
    pallas_call x25, Pallas kernels, in_vmem(): pl.pallas_call(kernel, name=name, in_specs=[pl.BlockSpec(memory_space=plt...  45.2 us
    ppermute x6, waiting for transfers between devices, scan_states(): got = lax.ppermute(sent, 'seq', [(i, i ^ bit) for i in range(n)])  36.2 us
    ppermute x16, starting transfers between devices, step(): middle = lax.ppermute(pair, 'head', self.MIDDLE)  17.2 us
  transfers between devices with their start and end apart: 46, of which 16 were waited for; matrix products, arithmetic and copies ran while one was open for 3% of the time, Pallas kernels for 47%

profile of v4, /device:TPU:0, one launch (start us, length us, event | category | flops | bytes accessed | tf_op | source)
XLA Modules:
  0.0 592.0 jit_solution(6529016265289648742)
XLA Ops:
  9.2 16.9 %project.1 = (bf16[1024,2048]{1,0:T(8,128)(2,1)}, bf16[1024,512]{1,0:T(8,128)(2,1)}, bf16[1024,512]{1,0:T(8,128)(2,1)}, bf16[1024,512]{1,0:T(8,128)(2,1)}, f32[1...) custom-call(bf16[1024,2048]{1,0:T(8,128)(2,1)} %bitcast.37, ...), custom_call_target="tpu_custom_call" | custom-call | flops 6710886400 | bytes 18874368 | tf_op jit(solution)/shard_map/project/pallas_call | solution.py:62
  28.4 2.9 pad_maximum_fusion
  31.4 2.9 collective-permute-start.1
  34.3 7.3 %collective-permute-done.1.refs_2_ = bf16[2,64,1152]{2,1,0:T(8,128)(2,1)S(1)} collective-permute-done((bf16[2,64,1152]{2,1,0:T(8,128)(2,1)S(1)}, bf16[2,64,1152]{2,1,0:T(8,128)(2,1)S(1)}, u32[]{:S(2)}, u32[]{:S(2)}) %collective-permute-start.1) | collective-permute-done | bytes 294944 | tf_op jit(solution)/shard_map/ppermute | solution.py:489
  43.8 12.3 %collective-permute-done.2.refs_2_ = bf16[2,64,1152]{2,1,0:T(8,128)(2,1)S(1)} collective-permute-done((bf16[2,64,1152]{2,1,0:T(8,128)(2,1)S(1)}, bf16[2,64,1152]{2,1,0:T(8,128)(2,1)S(1)}, u32[]{:S(2)}, u32[]{:S(2)}) %collective-permute-start.2) | collective-permute-done | bytes 294944 | tf_op jit(solution)/shard_map/ppermute | solution.py:489
  56.3 5.3 read.4
  61.6 3.8 collective-permute-start.3
  65.4 5.3 read.5
  70.7 13.4 %collective-permute-done.3.refs_1_ = bf16[256,2048]{1,0:T(8,128)(2,1)S(1)} collective-permute-done((bf16[256,2048]{1,0:T(8,128)(2,1)S(1)}, bf16[256,2048]{1,0:T(8,128)(2,1)S(1)}, u32[]{:S(2)}, u32[]{:S(2)}) %collective-permute-start.3) | collective-permute-done | bytes 1048608 | tf_op jit(solution)/shard_map/ppermute | solution.py:569
  84.2 4.5 collective-permute-start.4
  89.5 5.2 read.6
  95.7 10.5 %collective-permute-done.4.refs_1_ = bf16[256,2048]{1,0:T(8,128)(2,1)S(1)} collective-permute-done((bf16[256,2048]{1,0:T(8,128)(2,1)S(1)}, bf16[256,2048]{1,0:T(8,128)(2,1)S(1)}, u32[]{:S(2)}, u32[]{:S(2)}) %collective-permute-start.4) | collective-permute-done | bytes 1048608 | tf_op jit(solution)/shard_map/ppermute | solution.py:569
  108.9 3.8 collective-permute-start.6
  113.4 5.3 read.7
  119.8 10.3 %collective-permute-done.6.refs_1_ = bf16[256,2048]{1,0:T(8,128)(2,1)S(1)} collective-permute-done((bf16[256,2048]{1,0:T(8,128)(2,1)S(1)}, bf16[256,2048]{1,0:T(8,128)(2,1)S(1)}, u32[]{:S(2)}, u32[]{:S(2)}) %collective-permute-start.6) | collective-permute-done | bytes 1048608 | tf_op jit(solution)/shard_map/ppermute | solution.py:569
  131.1 3.3 join.20
  134.4 4.1 collective-permute-start.8
  139.6 19.4 %feed.4 = (f32[256,2048]{1,0:T(8,128)}, bf16[256,2048]{1,0:T(8,128)(2,1)}, bf16[256,1408]{1,0:T(8,128)(2,1)}, bf16[256,1408]{1,0:T(8,128)(2,1)}, bf16[256,1408]{...) custom-call(bf16[1024,2048]{1,0:T(8,128)(2,1)} %bitcast.38, ...), custom_call_target="tpu_custom_call" | custom-call | flops 8858370048 | bytes 24641536 | tf_op jit(solution)/shard_map/feed/pallas_call | solution.py:62
  161.0 2.6 join.21
  163.7 3.1 collective-permute-start.10
  168.1 19.3 %feed.5 = (f32[256,2048]{1,0:T(8,128)}, bf16[256,2048]{1,0:T(8,128)(2,1)}, bf16[256,1408]{1,0:T(8,128)(2,1)}, bf16[256,1408]{1,0:T(8,128)(2,1)}, bf16[256,1408]{...) custom-call(bf16[1024,2048]{1,0:T(8,128)(2,1)} %bitcast.39, ...), custom_call_target="tpu_custom_call" | custom-call | flops 8858370048 | bytes 24641536 | tf_op jit(solution)/shard_map/feed/pallas_call | solution.py:62
  195.0 19.4 %feed.6 = (f32[256,2048]{1,0:T(8,128)}, bf16[256,2048]{1,0:T(8,128)(2,1)}, bf16[256,1408]{1,0:T(8,128)(2,1)}, bf16[256,1408]{1,0:T(8,128)(2,1)}, bf16[256,1408]{...) custom-call(bf16[1024,2048]{1,0:T(8,128)(2,1)} %bitcast.40, ...), custom_call_target="tpu_custom_call" | custom-call | flops 8858370048 | bytes 24641536 | tf_op jit(solution)/shard_map/feed/pallas_call | solution.py:62
  218.8 3.2 collective-permute-start.14
  222.9 19.4 %feed.7 = (f32[256,2048]{1,0:T(8,128)}, bf16[256,2048]{1,0:T(8,128)(2,1)}, bf16[256,1408]{1,0:T(8,128)(2,1)}, bf16[256,1408]{1,0:T(8,128)(2,1)}, bf16[256,1408]{...) custom-call(bf16[1024,2048]{1,0:T(8,128)(2,1)} %bitcast.41, ...), custom_call_target="tpu_custom_call" | custom-call | flops 8858370048 | bytes 24641536 | tf_op jit(solution)/shard_map/feed/pallas_call | solution.py:62
  249.9 8.7 %back.4 = (f32[256,2048]{1,0:T(8,128)}, bf16[256,2048]{1,0:T(8,128)(2,1)}, bf16[256,512]{1,0:T(8,128)(2,1)}, f32[256,512]{1,0:T(8,128)}, f32[256,512]{1,0:T(8,12...) custom-call(bf16[256,2048]{1,0:T(8,128)(2,1)S(1)} %get-tuple-element, ...), custom_call_target="tpu_custom_call" | custom-call | flops 930086912 | bytes 9961472 | tf_op jit(solution)/shard_map/back/pallas_call | solution.py:62
  258.7 12.1 %down_grads.1.refs_12_ = bf16[8,3,256,1408]{3,2,1,0:T(8,128)(2,1)} custom-call(bf16[1024,2048]{1,0:T(8,128)(2,1)} %bitcast.55, bf16[256,1408]{1,0:T(8,128)(2,1)} %get-tuple-element.557.refs_1_, bf16[256,1408]{1,0:T(8,128)(2,1)} %get-tuple-element.558.refs_2_, bf16[256,1408]{1,0:T(8,128)(2,1)} %get-tuple-element.559.refs_3_, ...), custom_call_target="tpu_custom_call" | custom-call | flops 5905580032 | bytes 12845056 | tf_op jit(solution)/shard_map/down_grads/pallas_call | solution.py:62
  271.8 3.6 join.25
  275.4 2.8 collective-permute-start.18
  279.9 19.0 %wide_grads.1 = bf16[8,3,256,1408]{3,2,1,0:T(8,128)(2,1)} custom-call(bf16[256,2048]{1,0:T(8,128)(2,1)} %get-tuple-element.578.refs_0_, bf16[256,2048]{1,0:T(8,128)(2,1)} %get-tuple-element.579.refs_1_, bf16[256,2048]{1,0:T(8,128)(2,1)} %get-tuple-element.580.refs_2_, bf16[256,2048]{1,0:T(8,128)(2,1)} %get-tuple-element.581.refs_3_, ...), custom_call_target="tpu_custom_call", output_to_operand_aliasing={{}: (12, {})} | custom-call | flops 11811160064 | bytes 21495808 | tf_op jit(solution)/shard_map/wide_grads/pallas_call | solution.py:62
  298.9 2.6 join.26
  306.6 8.8 %back.5 = (f32[256,2048]{1,0:T(8,128)}, bf16[256,2048]{1,0:T(8,128)(2,1)}, bf16[256,512]{1,0:T(8,128)(2,1)}, f32[256,512]{1,0:T(8,128)}, f32[256,512]{1,0:T(8,12...) custom-call(bf16[256,2048]{1,0:T(8,128)(2,1)S(1)} %get-tuple-element, ...), custom_call_target="tpu_custom_call" | custom-call | flops 930086912 | bytes 9961472 | tf_op jit(solution)/shard_map/back/pallas_call | solution.py:62
  315.4 9.9 %back.6 = (f32[256,2048]{1,0:T(8,128)}, bf16[256,2048]{1,0:T(8,128)(2,1)}, bf16[256,512]{1,0:T(8,128)(2,1)}, f32[256,512]{1,0:T(8,128)}, f32[256,512]{1,0:T(8,12...) custom-call(bf16[256,2048]{1,0:T(8,128)(2,1)S(1)} %copy-done.25, ...), custom_call_target="tpu_custom_call" | custom-call | flops 930086912 | bytes 9961472 | tf_op jit(solution)/shard_map/back/pallas_call | solution.py:62
  326.3 3.1 join.27
  329.4 3.9 collective-permute-start.22
  334.0 9.0 %back.7 = (f32[256,2048]{1,0:T(8,128)}, bf16[256,2048]{1,0:T(8,128)(2,1)}, bf16[256,512]{1,0:T(8,128)(2,1)}, f32[256,512]{1,0:T(8,128)}, f32[256,512]{1,0:T(8,12...) custom-call(bf16[256,2048]{1,0:T(8,128)(2,1)S(1)} %get-tuple-element, ...), custom_call_target="tpu_custom_call" | custom-call | flops 930086912 | bytes 9961472 | tf_op jit(solution)/shard_map/back/pallas_call | solution.py:62
  347.8 3.7 join.28
  351.5 3.9 collective-permute-start.25
  359.0 13.0 %collective-permute-done.27.refs_2_ = bf16[2,64,1152]{2,1,0:T(8,128)(2,1)S(1)} collective-permute-done((bf16[2,64,1152]{2,1,0:T(8,128)(2,1)S(1)}, bf16[2,64,1152]{2,1,0:T(8,128)(2,1)S(1)}, u32[]{:S(2)}, u32[]{:S(2)}) %collective-permute-start.27) | collective-permute-done | bytes 294944 | tf_op jit(solution)/shard_map/ppermute | solution.py:489
  375.0 4.9 collective-permute-start.28
  379.9 11.2 %query_grads.1 = bf16[2048,1024]{1,0:T(8,128)(2,1)} custom-call(bf16[1024,2048]{1,0:T(8,128)(2,1)} %get-tuple-element.721.refs_0_, bf16[256,2048]{1,0:T(8,128)(2,1)} %get-tuple-element.666.refs_1_, bf16[256,2048]{1,0:T(8,128)(2,1)} %get-tuple-element.667.refs_2_, bf16[256,2048]{1,0:T(8,128)(2,1)} %get-tuple-element.668.refs_3_, ...), custom_call_target="tpu_custom_call" | custom-call | flops 4294967296 | bytes 14680064 | tf_op jit(solution)/shard_map/query_grads/pallas_call | solution.py:62
  396.9 9.7 %last.4 = (bf16[256,512]{1,0:T(8,128)(2,1)}, bf16[256,512]{1,0:T(8,128)(2,1)}, bf16[256,64]{1,0:T(8,128)(2,1)}, bf16[256,2048]{1,0:T(8,128)(2,1)S(1)}, f32[8,64]{1,0:T(8,128)}, /*index=5*/f32[8,2048]{1,0:T(8,128)}) custom-call(f32[4,64,1024]{2,1,0:T(8,128)S(1)} %hop.11.l0_ref, bf16[1024,512]{1,0:T(8,128)(2,1)} %get-tuple-element.403.k_ref, ...), custom_call_target="tpu_custom_call" | custom-call | flops 1677721600 | bytes 13107200 | tf_op jit(solution)/shard_map/last/pallas_call | solution.py:62
  407.6 2.6 join.29
  414.8 9.9 %last.7 = (bf16[256,512]{1,0:T(8,128)(2,1)}, bf16[256,512]{1,0:T(8,128)(2,1)}, bf16[256,64]{1,0:T(8,128)(2,1)}, bf16[256,2048]{1,0:T(8,128)(2,1)S(1)}, f32[8,64]{1,0:T(8,128)}, /*index=5*/f32[8,2048]{1,0:T(8,128)}) custom-call(f32[4,64,1024]{2,1,0:T(8,128)S(1)} %hop.11.l0_ref, bf16[1024,512]{1,0:T(8,128)(2,1)} %get-tuple-element.403.k_ref, ...), custom_call_target="tpu_custom_call" | custom-call | flops 1677721600 | bytes 13107200 | tf_op jit(solution)/shard_map/last/pallas_call | solution.py:62
  424.7 10.0 %last.6 = (bf16[256,512]{1,0:T(8,128)(2,1)}, bf16[256,512]{1,0:T(8,128)(2,1)}, bf16[256,64]{1,0:T(8,128)(2,1)}, bf16[256,2048]{1,0:T(8,128)(2,1)S(1)}, f32[8,64]{1,0:T(8,128)}, /*index=5*/f32[8,2048]{1,0:T(8,128)}) custom-call(f32[4,64,1024]{2,1,0:T(8,128)S(1)} %hop.11.l0_ref, bf16[1024,512]{1,0:T(8,128)(2,1)} %get-tuple-element.403.k_ref, ...), custom_call_target="tpu_custom_call" | custom-call | flops 1677721600 | bytes 13107200 | tf_op jit(solution)/shard_map/last/pallas_call | solution.py:62
  435.7 9.6 %last.5 = (bf16[256,512]{1,0:T(8,128)(2,1)}, bf16[256,512]{1,0:T(8,128)(2,1)}, bf16[256,64]{1,0:T(8,128)(2,1)}, bf16[256,2048]{1,0:T(8,128)(2,1)S(1)}, f32[8,64]{1,0:T(8,128)}, /*index=5*/f32[8,2048]{1,0:T(8,128)}) custom-call(f32[4,64,1024]{2,1,0:T(8,128)S(1)} %hop.11.l0_ref, bf16[1024,512]{1,0:T(8,128)(2,1)} %get-tuple-element.403.k_ref, ...), custom_call_target="tpu_custom_call" | custom-call | flops 1677721600 | bytes 13107200 | tf_op jit(solution)/shard_map/last/pallas_call | solution.py:62
  447.2 3.6 join.30
  451.8 2.8 collective-permute-start.31
  456.3 11.5 %state_grads.1 = bf16[8,272,1152]{2,1,0:T(8,128)(2,1)} custom-call(bf16[1024,2048]{1,0:T(8,128)(2,1)} %get-tuple-element.721.refs_0_, bf16[256,512]{1,0:T(8,128)(2,1)} %get-tuple-element.722.refs_1_, bf16[256,512]{1,0:T(8,128)(2,1)} %get-tuple-element.723.refs_2_, bf16[256,512]{1,0:T(8,128)(2,1)} %get-tuple-element.724.refs_3_, ...), custom_call_target="tpu_custom_call" | custom-call | flops 4294967296 | bytes 10485760 | tf_op jit(solution)/shard_map/state_grads/pallas_call | solution.py:62
  467.8 4.9 collective-permute-done.31.refs_1_
  472.7 2.7 join.31
  479.1 3.4 collective-permute-start.33
  488.2 11.2 %collective-permute-done.33.refs_1_ = bf16[256,2048]{1,0:T(8,128)(2,1)S(1)} collective-permute-done((bf16[256,2048]{1,0:T(8,128)(2,1)S(1)}, bf16[256,2048]{1,0:T(8,128)(2,1)S(1)}, u32[]{:S(2)}, u32[]{:S(2)}) %collective-permute-start.33) | collective-permute-done | bytes 1048608 | tf_op jit(solution)/shard_map/ppermute | solution.py:569
  500.4 2.8 join.32
  503.3 3.9 collective-permute-start.35
  508.2 3.4 in_grad.4.refs_0_
  516.6 6.6 %collective-permute-done.35.refs_1_ = bf16[256,2048]{1,0:T(8,128)(2,1)S(1)} collective-permute-done((bf16[256,2048]{1,0:T(8,128)(2,1)S(1)}, bf16[256,2048]{1,0:T(8,128)(2,1)S(1)}, u32[]{:S(2)}, u32[]{:S(2)}) %collective-permute-start.35) | collective-permute-done | bytes 1048608 | tf_op jit(solution)/shard_map/ppermute | solution.py:569
  535.0 11.3 %reduce-scatter.6.cloned.1.call-done = bf16[1,272,1152]{2,1,0:T(8,128)(2,1)} async-done(((bf16[8,272,1152]{2,1,0:T(8,128)(2,1)}), bf16[1,272,1152]{2,1,0:T(8,128)(2,1)}) %reduce-scatter.6.cloned.1.call-update) | async-done | bytes 626704 | tf_op jit(solution)/shard_map/reduce_scatter | solution.py:920
  550.1 3.3 in_grad.5.refs_0_
  558.3 3.6 collective-permute-start.41
  564.0 3.7 convert_bitcast_fusion
  567.7 2.9 copy.63
  570.6 3.3 in_grad.6.refs_0_
  573.9 8.0 %collective-permute-done.39.refs_0_ = bf16[256,2048]{1,0:T(8,128)(2,1)S(1)} collective-permute-done((bf16[256,2048]{1,0:T(8,128)(2,1)S(1)}, bf16[256,2048]{1,0:T(8,128)(2,1)S(1)}, u32[]{:S(2)}, u32[]{:S(2)}) %collective-permute-start.39) | collective-permute-done | bytes 1048608 | tf_op jit(solution)/shard_map/ppermute | solution.py:569
  582.0 3.3 in_grad.7
  (266 shorter events, 114.9 us)
Async XLA Ops:
  7.2 132.4 %all-gather.3.cloned.1.call-start = ((), (), s32[]{:S(2)}) async-start(), calls=%async_computation.6 | async-start | bytes 19464192 | tf_op jit(solution)/shard_map/all_gather | solution.py:642
  9.2 18.9 %copy-start.80 = (bf16[1408,256]{1,0:T(8,128)(2,1)S(1)}, bf16[1408,256]{1,0:T(8,128)(2,1)}, u32[]{:S(2)}) copy-start(bf16[1408,256]{1,0:T(8,128)(2,1)} %param.24) | copy-start | bytes 2162692
  26.1 1.7 collective-permute-start
  31.4 471.9 %reduce-scatter.4.cloned.1.call-start = ((), (), s32[]{:S(2)}) async-start(), calls=%async_computation.3 | async-start | bytes 19464192 | tf_op jit(solution)/shard_map/reduce_scatter | solution.py:862
  31.4 10.2 %collective-permute-start.1 = (bf16[2,64,1152]{2,1,0:T(8,128)(2,1)S(1)}, bf16[2,64,1152]{2,1,0:T(8,128)(2,1)S(1)}, u32[]{:S(2)}, u32[]{:S(2)}) collective-permute-start(bf16[2,64,1152]{2,1,0:T(8,128)(2,1)S(1)} %get-tuple-element.413), channel_id=1, source_target_pairs={{0,8},{4,12},{8,0},{12,4},{16,24},{20,28},{24,16},{28,20},{1,9},{5... | collective-permute-start | bytes 884744 | tf_op jit(solution)/shard_map/ppermute | solution.py:489
  41.9 14.1 %collective-permute-start.2 = (bf16[2,64,1152]{2,1,0:T(8,128)(2,1)S(1)}, bf16[2,64,1152]{2,1,0:T(8,128)(2,1)S(1)}, u32[]{:S(2)}, u32[]{:S(2)}) collective-permute-start(bf16[2,64,1152]{2,1,0:T(8,128)(2,1)S(1)} %get-tuple-element.418), channel_id=1, source_target_pairs={{0,16},{4,20},{8,24},{12,28},{16,0},{20,4},{24,8},{28,12},{1,17},{... | collective-permute-start | bytes 884744 | tf_op jit(solution)/shard_map/ppermute | solution.py:489
  61.6 22.5 %collective-permute-start.3 = (bf16[256,2048]{1,0:T(8,128)(2,1)S(1)}, bf16[256,2048]{1,0:T(8,128)(2,1)S(1)}, u32[]{:S(2)}, u32[]{:S(2)}) collective-permute-start(bf16[256,2048]{1,0:T(8,128)(2,1)S(1)} %get-tuple-element.425.refs_0_), channel_id=1, source_target_pairs={{0,1},{3,2},{4,5},{7,6},{8,9},{11,10},{12,13},{15,14},{16,17},{19,... | collective-permute-start | bytes 3145736 | tf_op jit(solution)/shard_map/ppermute | solution.py:569
  84.2 22.0 %collective-permute-start.4 = (bf16[256,2048]{1,0:T(8,128)(2,1)S(1)}, bf16[256,2048]{1,0:T(8,128)(2,1)S(1)}, u32[]{:S(2)}, u32[]{:S(2)}) collective-permute-start(bf16[256,2048]{1,0:T(8,128)(2,1)S(1)} %get-tuple-element.429), channel_id=1, source_target_pairs={{0,1},{3,2},{4,5},{7,6},{8,9},{11,10},{12,13},{15,14},{16,17},{19,... | collective-permute-start | bytes 3145736 | tf_op jit(solution)/shard_map/ppermute | solution.py:569
  88.7 17.5 %collective-permute-start.5 = (bf16[256,2048]{1,0:T(8,128)(2,1)S(1)}, bf16[256,2048]{1,0:T(8,128)(2,1)S(1)}, u32[]{:S(2)}, u32[]{:S(2)}) collective-permute-start(bf16[256,2048]{1,0:T(8,128)(2,1)S(1)} %get-tuple-element.430.refs_2_), channel_id=1, source_target_pairs={{1,2},{2,1},{5,6},{6,5},{9,10},{10,9},{13,14},{14,13},{17,18},{18,... | collective-permute-start | bytes 3145736 | tf_op jit(solution)/shard_map/ppermute | solution.py:572
  108.9 22.2 %copy-start.3 = (bf16[256,2048]{1,0:T(8,128)(2,1)S(1)}, bf16[256,2048]{1,0:T(8,128)(2,1)}, u32[]{:S(2)}) copy-start(bf16[256,2048]{1,0:T(8,128)(2,1)} %copy-done.2) | copy-start | bytes 3145732
  108.9 21.2 %collective-permute-start.6 = (bf16[256,2048]{1,0:T(8,128)(2,1)S(1)}, bf16[256,2048]{1,0:T(8,128)(2,1)S(1)}, u32[]{:S(2)}, u32[]{:S(2)}) collective-permute-start(bf16[256,2048]{1,0:T(8,128)(2,1)S(1)} %get-tuple-element.438.refs_4_), channel_id=1, source_target_pairs={{0,1},{3,2},{1,0},{2,3},{4,5},{7,6},{5,4},{6,7},{8,9},{11,10},{9,8... | collective-permute-start | bytes 3145736 | tf_op jit(solution)/shard_map/ppermute | solution.py:569
  112.7 17.3 %collective-permute-start.7 = (bf16[256,2048]{1,0:T(8,128)(2,1)S(1)}, bf16[256,2048]{1,0:T(8,128)(2,1)S(1)}, u32[]{:S(2)}, u32[]{:S(2)}) collective-permute-start(bf16[256,2048]{1,0:T(8,128)(2,1)S(1)} %get-tuple-element.439.refs_2_), channel_id=1, source_target_pairs={{1,2},{2,1},{5,6},{6,5},{9,10},{10,9},{13,14},{14,13},{17,18},{18,... | collective-permute-start | bytes 3145736 | tf_op jit(solution)/shard_map/ppermute | solution.py:572
  134.4 24.7 %copy-start.42 = (bf16[256,2048]{1,0:T(8,128)(2,1)}, bf16[256,2048]{1,0:T(8,128)(2,1)S(1)}, u32[]{:S(2)}) copy-start(bf16[256,2048]{1,0:T(8,128)(2,1)S(1)} %get-tuple-element.444.refs_2_) | copy-start | bytes 3145732
  134.4 25.7 %collective-permute-start.8 = (bf16[256,2048]{1,0:T(8,128)(2,1)}, bf16[256,2048]{1,0:T(8,128)(2,1)}, u32[]{:S(2)}, u32[]{:S(2)}) collective-permute-start(bf16[256,2048]{1,0:T(8,128)(2,1)} %get-tuple-element.443.refs_4_), channel_id=1, source_target_pairs={{0,1},{3,2},{1,0},{2,3},{4,5},{7,6},{5,4},{6,7},{8,9},{11,10},{9,8... | collective-permute-start | bytes 3145736 | tf_op jit(solution)/shard_map/ppermute | solution.py:569
  138.5 21.5 %collective-permute-start.9 = (bf16[256,2048]{1,0:T(8,128)(2,1)S(1)}, bf16[256,2048]{1,0:T(8,128)(2,1)S(1)}, u32[]{:S(2)}, u32[]{:S(2)}) collective-permute-start(bf16[256,2048]{1,0:T(8,128)(2,1)S(1)} %get-tuple-element.444.refs_2_), channel_id=1, source_target_pairs={{1,2},{2,1},{5,6},{6,5},{9,10},{10,9},{13,14},{14,13},{17,18},{18,... | collective-permute-start | bytes 3145736 | tf_op jit(solution)/shard_map/ppermute | solution.py:572
  139.6 21.5 %copy-start.17 = (bf16[256,2048]{1,0:T(8,128)(2,1)S(1)}, bf16[256,2048]{1,0:T(8,128)(2,1)}, u32[]{:S(2)}) copy-start(bf16[256,2048]{1,0:T(8,128)(2,1)} %copy-done.16) | copy-start | bytes 3145732
  163.7 23.8 %copy-start.45 = (bf16[256,2048]{1,0:T(8,128)(2,1)}, bf16[256,2048]{1,0:T(8,128)(2,1)S(1)}, u32[]{:S(2)}) copy-start(bf16[256,2048]{1,0:T(8,128)(2,1)S(1)} %get-tuple-element.461.refs_2_) | copy-start | bytes 3145732
  163.7 23.8 %copy-start.46 = (bf16[256,2048]{1,0:T(8,128)(2,1)}, bf16[256,2048]{1,0:T(8,128)(2,1)S(1)}, u32[]{:S(2)}) copy-start(bf16[256,2048]{1,0:T(8,128)(2,1)S(1)} %get-tuple-element.460.refs_4_) | copy-start | bytes 3145732
  163.7 25.8 %copy-start.21 = (bf16[256,2048]{1,0:T(8,128)(2,1)S(1)}, bf16[256,2048]{1,0:T(8,128)(2,1)}, u32[]{:S(2)}) copy-start(bf16[256,2048]{1,0:T(8,128)(2,1)} %copy-done.20) | copy-start | bytes 3145732
  163.7 24.8 %collective-permute-start.10 = (bf16[256,2048]{1,0:T(8,128)(2,1)S(1)}, bf16[256,2048]{1,0:T(8,128)(2,1)S(1)}, u32[]{:S(2)}, u32[]{:S(2)}) collective-permute-start(bf16[256,2048]{1,0:T(8,128)(2,1)S(1)} %get-tuple-element.460.refs_4_), channel_id=1, source_target_pairs={{0,1},{3,2},{1,0},{2,3},{4,5},{7,6},{5,4},{6,7},{8,9},{11,10},{9,8... | collective-permute-start | bytes 3145736 | tf_op jit(solution)/shard_map/ppermute | solution.py:569
  166.8 21.7 %collective-permute-start.11 = (bf16[256,2048]{1,0:T(8,128)(2,1)S(1)}, bf16[256,2048]{1,0:T(8,128)(2,1)S(1)}, u32[]{:S(2)}, u32[]{:S(2)}) collective-permute-start(bf16[256,2048]{1,0:T(8,128)(2,1)S(1)} %get-tuple-element.461.refs_2_), channel_id=1, source_target_pairs={{1,2},{2,1},{5,6},{6,5},{9,10},{10,9},{13,14},{14,13},{17,18},{18,... | collective-permute-start | bytes 3145736 | tf_op jit(solution)/shard_map/ppermute | solution.py:572
  191.8 22.6 %copy-start.47 = (bf16[256,2048]{1,0:T(8,128)(2,1)}, bf16[256,2048]{1,0:T(8,128)(2,1)S(1)}, u32[]{:S(2)}) copy-start(bf16[256,2048]{1,0:T(8,128)(2,1)S(1)} %get-tuple-element.478.refs_2_) | copy-start | bytes 3145732
  191.8 22.6 %copy-start.48 = (bf16[256,2048]{1,0:T(8,128)(2,1)}, bf16[256,2048]{1,0:T(8,128)(2,1)S(1)}, u32[]{:S(2)}) copy-start(bf16[256,2048]{1,0:T(8,128)(2,1)S(1)} %get-tuple-element.477.refs_4_) | copy-start | bytes 3145732
  191.9 24.6 %copy-start.23 = (bf16[256,2048]{1,0:T(8,128)(2,1)S(1)}, bf16[256,2048]{1,0:T(8,128)(2,1)}, u32[]{:S(2)}) copy-start(bf16[256,2048]{1,0:T(8,128)(2,1)} %copy-done.22) | copy-start | bytes 3145732
  191.9 23.5 %collective-permute-start.12 = (bf16[256,2048]{1,0:T(8,128)(2,1)S(1)}, bf16[256,2048]{1,0:T(8,128)(2,1)S(1)}, u32[]{:S(2)}, u32[]{:S(2)}) collective-permute-start(bf16[256,2048]{1,0:T(8,128)(2,1)S(1)} %get-tuple-element.477.refs_4_), channel_id=1, source_target_pairs={{0,1},{3,2},{1,0},{2,3},{4,5},{7,6},{5,4},{6,7},{8,9},{11,10},{9,8... | collective-permute-start | bytes 3145736 | tf_op jit(solution)/shard_map/ppermute | solution.py:569
  194.1 21.3 %collective-permute-start.13 = (bf16[256,2048]{1,0:T(8,128)(2,1)S(1)}, bf16[256,2048]{1,0:T(8,128)(2,1)S(1)}, u32[]{:S(2)}, u32[]{:S(2)}) collective-permute-start(bf16[256,2048]{1,0:T(8,128)(2,1)S(1)} %get-tuple-element.478.refs_2_), channel_id=1, source_target_pairs={{1,2},{2,1},{5,6},{6,5},{9,10},{10,9},{13,14},{14,13},{17,18},{18,... | collective-permute-start | bytes 3145736 | tf_op jit(solution)/shard_map/ppermute | solution.py:572
  218.8 23.5 %copy-start.43 = (bf16[256,2048]{1,0:T(8,128)(2,1)}, bf16[256,2048]{1,0:T(8,128)(2,1)S(1)}, u32[]{:S(2)}) copy-start(bf16[256,2048]{1,0:T(8,128)(2,1)S(1)} %get-tuple-element.505.refs_2_) | copy-start | bytes 3145732
  218.8 23.5 %copy-start.44 = (bf16[256,2048]{1,0:T(8,128)(2,1)}, bf16[256,2048]{1,0:T(8,128)(2,1)S(1)}, u32[]{:S(2)}) copy-start(bf16[256,2048]{1,0:T(8,128)(2,1)S(1)} %get-tuple-element.504.refs_4_) | copy-start | bytes 3145732
  218.8 25.5 %copy-start.19 = (bf16[256,2048]{1,0:T(8,128)(2,1)S(1)}, bf16[256,2048]{1,0:T(8,128)(2,1)}, u32[]{:S(2)}) copy-start(bf16[256,2048]{1,0:T(8,128)(2,1)} %copy-done.18) | copy-start | bytes 3145732
  218.8 24.5 %collective-permute-start.14 = (bf16[256,2048]{1,0:T(8,128)(2,1)S(1)}, bf16[256,2048]{1,0:T(8,128)(2,1)S(1)}, u32[]{:S(2)}, u32[]{:S(2)}) collective-permute-start(bf16[256,2048]{1,0:T(8,128)(2,1)S(1)} %get-tuple-element.504.refs_4_), channel_id=1, source_target_pairs={{0,1},{3,2},{1,0},{2,3},{4,5},{7,6},{5,4},{6,7},{8,9},{11,10},{9,8... | collective-permute-start | bytes 3145736 | tf_op jit(solution)/shard_map/ppermute | solution.py:569
  222.0 21.3 %collective-permute-start.15 = (bf16[256,2048]{1,0:T(8,128)(2,1)S(1)}, bf16[256,2048]{1,0:T(8,128)(2,1)S(1)}, u32[]{:S(2)}, u32[]{:S(2)}) collective-permute-start(bf16[256,2048]{1,0:T(8,128)(2,1)S(1)} %get-tuple-element.505.refs_2_), channel_id=1, source_target_pairs={{1,2},{2,1},{5,6},{6,5},{9,10},{10,9},{13,14},{14,13},{17,18},{18,... | collective-permute-start | bytes 3145736 | tf_op jit(solution)/shard_map/ppermute | solution.py:572
  246.6 24.2 %collective-permute-start.16 = (bf16[256,2048]{1,0:T(8,128)(2,1)S(1)}, bf16[256,2048]{1,0:T(8,128)(2,1)S(1)}, u32[]{:S(2)}, u32[]{:S(2)}) collective-permute-start(bf16[256,2048]{1,0:T(8,128)(2,1)S(1)} %get-tuple-element.533.refs_4_), channel_id=1, source_target_pairs={{0,1},{3,2},{1,0},{2,3},{4,5},{7,6},{5,4},{6,7},{8,9},{11,10},{9,8... | collective-permute-start | bytes 3145736 | tf_op jit(solution)/shard_map/ppermute | solution.py:569
  248.8 21.9 %collective-permute-start.17 = (bf16[256,2048]{1,0:T(8,128)(2,1)S(1)}, bf16[256,2048]{1,0:T(8,128)(2,1)S(1)}, u32[]{:S(2)}, u32[]{:S(2)}) collective-permute-start(bf16[256,2048]{1,0:T(8,128)(2,1)S(1)} %get-tuple-element.534.refs_2_), channel_id=1, source_target_pairs={{1,2},{2,1},{5,6},{6,5},{9,10},{10,9},{13,14},{14,13},{17,18},{18,... | collective-permute-start | bytes 3145736 | tf_op jit(solution)/shard_map/ppermute | solution.py:572
  275.4 23.5 %copy-start.7 = (bf16[256,2048]{1,0:T(8,128)(2,1)S(1)}, bf16[256,2048]{1,0:T(8,128)(2,1)}, u32[]{:S(2)}) copy-start(bf16[256,2048]{1,0:T(8,128)(2,1)} %get-tuple-element.535.refs_5_.refs_0_) | copy-start | bytes 3145732
  275.4 23.5 %collective-permute-start.18 = (bf16[256,2048]{1,0:T(8,128)(2,1)}, bf16[256,2048]{1,0:T(8,128)(2,1)}, u32[]{:S(2)}, u32[]{:S(2)}) collective-permute-start(bf16[256,2048]{1,0:T(8,128)(2,1)} %get-tuple-element.568.refs_4_), channel_id=1, source_target_pairs={{0,1},{3,2},{1,0},{2,3},{4,5},{7,6},{5,4},{6,7},{8,9},{11,10},{9,8... | collective-permute-start | bytes 3145736 | tf_op jit(solution)/shard_map/ppermute | solution.py:569
  278.3 20.6 %collective-permute-start.19 = (bf16[256,2048]{1,0:T(8,128)(2,1)}, bf16[256,2048]{1,0:T(8,128)(2,1)}, u32[]{:S(2)}, u32[]{:S(2)}) collective-permute-start(bf16[256,2048]{1,0:T(8,128)(2,1)} %get-tuple-element.569.refs_2_), channel_id=1, source_target_pairs={{1,2},{2,1},{5,6},{6,5},{9,10},{10,9},{13,14},{14,13},{17,18},{18,... | collective-permute-start | bytes 3145736 | tf_op jit(solution)/shard_map/ppermute | solution.py:572
  304.5 224.6 %reduce-scatter.8.cloned.1.call-start = ((), (), s32[]{:S(2)}) async-start(), calls=%async_computation.5 | async-start | bytes 4718592 | tf_op jit(solution)/shard_map/reduce_scatter | solution.py:900
  304.6 20.7 %collective-permute-start.20 = (bf16[256,2048]{1,0:T(8,128)(2,1)}, bf16[256,2048]{1,0:T(8,128)(2,1)S(1)}, u32[]{:S(2)}, u32[]{:S(2)}) collective-permute-start(bf16[256,2048]{1,0:T(8,128)(2,1)} %copy-done.32), channel_id=1, source_target_pairs={{0,1},{3,2},{1,0},{2,3},{4,5},{7,6},{5,4},{6,7},{8,9},{11,10},{9,8... | collective-permute-start | bytes 3145736 | tf_op jit(solution)/shard_map/ppermute | solution.py:569
  305.9 19.4 %collective-permute-start.21 = (bf16[256,2048]{1,0:T(8,128)(2,1)S(1)}, bf16[256,2048]{1,0:T(8,128)(2,1)S(1)}, u32[]{:S(2)}, u32[]{:S(2)}) collective-permute-start(bf16[256,2048]{1,0:T(8,128)(2,1)S(1)} %copy-done.31), channel_id=1, source_target_pairs={{1,2},{2,1},{5,6},{6,5},{9,10},{10,9},{13,14},{14,13},{17,18},{18,... | collective-permute-start | bytes 3145736 | tf_op jit(solution)/shard_map/ppermute | solution.py:572
  329.4 13.6 %copy-start.33 = (bf16[256,2048]{1,0:T(8,128)(2,1)}, bf16[256,2048]{1,0:T(8,128)(2,1)S(1)}, u32[]{:S(2)}) copy-start(bf16[256,2048]{1,0:T(8,128)(2,1)S(1)} %get-tuple-element.616.refs_2_) | copy-start | bytes 3145732
  329.4 17.4 %collective-permute-start.22 = (bf16[256,2048]{1,0:T(8,128)(2,1)S(1)}, bf16[256,2048]{1,0:T(8,128)(2,1)S(1)}, u32[]{:S(2)}, u32[]{:S(2)}) collective-permute-start(bf16[256,2048]{1,0:T(8,128)(2,1)S(1)} %get-tuple-element.615.refs_4_), channel_id=1, source_target_pairs={{0,1},{3,2},{1,0},{2,3},{4,5},{7,6},{5,4},{6,7},{8,9},{11,10},{9,8... | collective-permute-start | bytes 3145736 | tf_op jit(solution)/shard_map/ppermute | solution.py:569
  333.3 13.6 %collective-permute-start.23 = (bf16[256,2048]{1,0:T(8,128)(2,1)S(1)}, bf16[256,2048]{1,0:T(8,128)(2,1)S(1)}, u32[]{:S(2)}, u32[]{:S(2)}) collective-permute-start(bf16[256,2048]{1,0:T(8,128)(2,1)S(1)} %get-tuple-element.616.refs_2_), channel_id=1, source_target_pairs={{1,2},{2,1},{5,6},{6,5},{9,10},{10,9},{13,14},{14,13},{17,18},{18,... | collective-permute-start | bytes 3145736 | tf_op jit(solution)/shard_map/ppermute | solution.py:572
  343.2 1.6 collective-permute-start.24
  351.5 56.1 %collective-permute-start.25 = (bf16[256,2048]{1,0:T(8,128)(2,1)}, bf16[256,2048]{1,0:T(8,128)(2,1)}, u32[]{:S(2)}, u32[]{:S(2)}) collective-permute-start(bf16[256,2048]{1,0:T(8,128)(2,1)} %get-tuple-element.638.refs_4_), channel_id=1, source_target_pairs={{0,1},{3,2},{1,0},{2,3},{4,5},{7,6},{5,4},{6,7},{8,9},{11,10},{9,8... | collective-permute-start | bytes 3145736 | tf_op jit(solution)/shard_map/ppermute | solution.py:569
  355.5 52.1 %collective-permute-start.26 = (bf16[256,2048]{1,0:T(8,128)(2,1)}, bf16[256,2048]{1,0:T(8,128)(2,1)}, u32[]{:S(2)}, u32[]{:S(2)}) collective-permute-start(bf16[256,2048]{1,0:T(8,128)(2,1)} %get-tuple-element.639.refs_2_), channel_id=1, source_target_pairs={{1,2},{2,1},{5,6},{6,5},{9,10},{10,9},{13,14},{14,13},{17,18},{18,... | collective-permute-start | bytes 3145736 | tf_op jit(solution)/shard_map/ppermute | solution.py:572
  357.3 14.7 %collective-permute-start.27 = (bf16[2,64,1152]{2,1,0:T(8,128)(2,1)S(1)}, bf16[2,64,1152]{2,1,0:T(8,128)(2,1)S(1)}, u32[]{:S(2)}, u32[]{:S(2)}) collective-permute-start(bf16[2,64,1152]{2,1,0:T(8,128)(2,1)S(1)} %get-tuple-element.642), channel_id=1, source_target_pairs={{0,8},{4,12},{8,0},{12,4},{16,24},{20,28},{24,16},{28,20},{1,9},{5... | collective-permute-start | bytes 884744 | tf_op jit(solution)/shard_map/ppermute | solution.py:489
  375.0 17.0 %collective-permute-start.28 = (bf16[2,64,1152]{2,1,0:T(8,128)(2,1)S(1)}, bf16[2,64,1152]{2,1,0:T(8,128)(2,1)S(1)}, u32[]{:S(2)}, u32[]{:S(2)}) collective-permute-start(bf16[2,64,1152]{2,1,0:T(8,128)(2,1)S(1)} %get-tuple-element.647), channel_id=1, source_target_pairs={{0,16},{4,20},{8,24},{12,28},{16,0},{20,4},{24,8},{28,12},{1,17},{... | collective-permute-start | bytes 884744 | tf_op jit(solution)/shard_map/ppermute | solution.py:489
  412.3 134.1 %reduce-scatter.6.cloned.1.call-start = ((), (), s32[]{:S(2)}) async-start(), calls=%async_computation.4 | async-start | bytes 5640192 | tf_op jit(solution)/shard_map/reduce_scatter | solution.py:920
  412.3 33.9 %collective-permute-start.29 = (bf16[256,2048]{1,0:T(8,128)(2,1)}, bf16[256,2048]{1,0:T(8,128)(2,1)S(1)}, u32[]{:S(2)}, u32[]{:S(2)}) collective-permute-start(bf16[256,2048]{1,0:T(8,128)(2,1)} %copy-done.29), channel_id=1, source_target_pairs={{0,1},{3,2},{1,0},{2,3},{4,5},{7,6},{5,4},{6,7},{8,9},{11,10},{9,8... | collective-permute-start | bytes 3145736 | tf_op jit(solution)/shard_map/ppermute | solution.py:569
  414.1 32.2 %collective-permute-start.30 = (bf16[256,2048]{1,0:T(8,128)(2,1)S(1)}, bf16[256,2048]{1,0:T(8,128)(2,1)S(1)}, u32[]{:S(2)}, u32[]{:S(2)}) collective-permute-start(bf16[256,2048]{1,0:T(8,128)(2,1)S(1)} %get-tuple-element.686.refs_2_), channel_id=1, source_target_pairs={{1,2},{2,1},{5,6},{6,5},{9,10},{10,9},{13,14},{14,13},{17,18},{18,... | collective-permute-start | bytes 3145736 | tf_op jit(solution)/shard_map/ppermute | solution.py:572
  451.8 16.0 %copy-start.35 = (bf16[256,2048]{1,0:T(8,128)(2,1)}, bf16[256,2048]{1,0:T(8,128)(2,1)S(1)}, u32[]{:S(2)}) copy-start(bf16[256,2048]{1,0:T(8,128)(2,1)S(1)} %get-tuple-element.709.refs_2_) | copy-start | bytes 3145732
  451.8 20.9 %collective-permute-start.31 = (bf16[256,2048]{1,0:T(8,128)(2,1)}, bf16[256,2048]{1,0:T(8,128)(2,1)}, u32[]{:S(2)}, u32[]{:S(2)}) collective-permute-start(bf16[256,2048]{1,0:T(8,128)(2,1)} %get-tuple-element.708.refs_4_), channel_id=1, source_target_pairs={{0,1},{3,2},{1,0},{2,3},{4,5},{7,6},{5,4},{6,7},{8,9},{11,10},{9,8... | collective-permute-start | bytes 3145736 | tf_op jit(solution)/shard_map/ppermute | solution.py:569
  454.6 18.1 %collective-permute-start.32 = (bf16[256,2048]{1,0:T(8,128)(2,1)S(1)}, bf16[256,2048]{1,0:T(8,128)(2,1)}, u32[]{:S(2)}, u32[]{:S(2)}) collective-permute-start(bf16[256,2048]{1,0:T(8,128)(2,1)S(1)} %get-tuple-element.709.refs_2_), channel_id=1, source_target_pairs={{1,2},{2,1},{5,6},{6,5},{9,10},{10,9},{13,14},{14,13},{17,18},{18,... | collective-permute-start | bytes 3145736 | tf_op jit(solution)/shard_map/ppermute | solution.py:572
  456.3 16.5 %copy-start.13 = (bf16[256,2048]{1,0:T(8,128)(2,1)S(1)}, bf16[256,2048]{1,0:T(8,128)(2,1)}, u32[]{:S(2)}) copy-start(bf16[256,2048]{1,0:T(8,128)(2,1)} %copy-done.12) | copy-start | bytes 3145732
  479.1 20.4 %collective-permute-start.33 = (bf16[256,2048]{1,0:T(8,128)(2,1)S(1)}, bf16[256,2048]{1,0:T(8,128)(2,1)S(1)}, u32[]{:S(2)}, u32[]{:S(2)}) collective-permute-start(bf16[256,2048]{1,0:T(8,128)(2,1)S(1)} %copy-done.41), channel_id=1, source_target_pairs={{0,1},{3,2},{1,0},{2,3},{4,5},{7,6},{5,4},{6,7},{8,9},{11,10},{9,8... | collective-permute-start | bytes 3145736 | tf_op jit(solution)/shard_map/ppermute | solution.py:569
  482.5 16.9 %collective-permute-start.34 = (bf16[256,2048]{1,0:T(8,128)(2,1)S(1)}, bf16[256,2048]{1,0:T(8,128)(2,1)S(1)}, u32[]{:S(2)}, u32[]{:S(2)}) collective-permute-start(bf16[256,2048]{1,0:T(8,128)(2,1)S(1)} %get-tuple-element.749.refs_2_), channel_id=1, source_target_pairs={{1,2},{2,1},{5,6},{6,5},{9,10},{10,9},{13,14},{14,13},{17,18},{18,... | collective-permute-start | bytes 3145736 | tf_op jit(solution)/shard_map/ppermute | solution.py:572
  485.7 14.8 %copy-start.9 = (bf16[256,2048]{1,0:T(8,128)(2,1)S(1)}, bf16[256,2048]{1,0:T(8,128)(2,1)}, u32[]{:S(2)}) copy-start(bf16[256,2048]{1,0:T(8,128)(2,1)} %copy-done.8) | copy-start | bytes 3145732
  503.3 20.0 %collective-permute-start.35 = (bf16[256,2048]{1,0:T(8,128)(2,1)S(1)}, bf16[256,2048]{1,0:T(8,128)(2,1)S(1)}, u32[]{:S(2)}, u32[]{:S(2)}) collective-permute-start(bf16[256,2048]{1,0:T(8,128)(2,1)S(1)} %get-tuple-element.762.refs_4_), channel_id=1, source_target_pairs={{0,1},{3,2},{1,0},{2,3},{4,5},{7,6},{5,4},{6,7},{8,9},{11,10},{9,8... | collective-permute-start | bytes 3145736 | tf_op jit(solution)/shard_map/ppermute | solution.py:569
  507.2 16.0 %collective-permute-start.36 = (bf16[256,2048]{1,0:T(8,128)(2,1)S(1)}, bf16[256,2048]{1,0:T(8,128)(2,1)S(1)}, u32[]{:S(2)}, u32[]{:S(2)}) collective-permute-start(bf16[256,2048]{1,0:T(8,128)(2,1)S(1)} %get-tuple-element.763.refs_2_), channel_id=1, source_target_pairs={{1,2},{2,1},{5,6},{6,5},{9,10},{10,9},{13,14},{14,13},{17,18},{18,... | collective-permute-start | bytes 3145736 | tf_op jit(solution)/shard_map/ppermute | solution.py:572
  526.2 27.2 %collective-permute-start.37 = (bf16[256,2048]{1,0:T(8,128)(2,1)S(1)}, bf16[256,2048]{1,0:T(8,128)(2,1)}, u32[]{:S(2)}, u32[]{:S(2)}) collective-permute-start(bf16[256,2048]{1,0:T(8,128)(2,1)S(1)} %get-tuple-element.774.refs_3_), channel_id=1, source_target_pairs={{1,0},{2,3},{5,4},{6,7},{9,8},{10,11},{13,12},{14,15},{17,16},{18,... | collective-permute-start | bytes 3145736 | tf_op jit(solution)/shard_map/ppermute | solution.py:569
  527.5 25.9 %collective-permute-start.38 = (bf16[256,2048]{1,0:T(8,128)(2,1)S(1)}, bf16[256,2048]{1,0:T(8,128)(2,1)}, u32[]{:S(2)}, u32[]{:S(2)}) collective-permute-start(bf16[256,2048]{1,0:T(8,128)(2,1)S(1)} %get-tuple-element.775.refs_1_), channel_id=1, source_target_pairs={{1,2},{2,1},{5,6},{6,5},{9,10},{10,9},{13,14},{14,13},{17,18},{18,... | collective-permute-start | bytes 3145736 | tf_op jit(solution)/shard_map/ppermute | solution.py:572
  547.4 10.9 %collective-permute-start.40 = (f32[256]{0:T(256)S(1)}, f32[256]{0:T(256)S(1)}, u32[]{:S(2)}, u32[]{:S(2)}) collective-permute-start(f32[256]{0:T(256)S(1)} %convert_reduce_fusion), channel_id=1, source_target_pairs={{0,1},{1,0},{2,3},{3,2},{4,5},{5,4},{6,7},{7,6},{8,9},{9,8},{10,11... | collective-permute-start | bytes 3080 | tf_op jit(solution)/shard_map/ppermute | solution.py:942
  555.3 26.5 %collective-permute-start.39 = (bf16[256,2048]{1,0:T(8,128)(2,1)S(1)}, bf16[256,2048]{1,0:T(8,128)(2,1)S(1)}, u32[]{:S(2)}, u32[]{:S(2)}) collective-permute-start(bf16[256,2048]{1,0:T(8,128)(2,1)S(1)} %get-tuple-element.784.refs_1_), channel_id=1, source_target_pairs={{1,0},{2,3},{5,4},{6,7},{9,8},{10,11},{13,12},{14,15},{17,16},{18,... | collective-permute-start | bytes 3145736 | tf_op jit(solution)/shard_map/ppermute | solution.py:569
  558.3 5.2 collective-permute-start.41
  (63 other events, 249.3 us)
Sparse Core Ops, SparseCore 0:
  31.5 99.9 all-gather.2
  304.7 127.4 reduce-scatter.3
  435.9 51.2 reduce-scatter.7
  490.6 55.7 reduce-scatter.5

commit v5 on v4

--- a/solution.py
+++ b/solution.py
@@ -38,7 +38,7 @@
     return high, (a - high.astype(f32)).astype(bf16)
 
 
-def call(name, kernel, grid, in_specs, out_specs, out_shape, scratch=(), vmem=48, cost=None, loose=(), loose_out=(),
+def call(name, kernel, grid, in_specs, out_specs, out_shape, scratch=(), vmem=24, cost=None, loose=(), loose_out=(),
          aliases=None):
     single = not isinstance(out_shape, list)
     shapes = [out_shape] if single else out_shape
@@ -231,13 +231,17 @@
 
 
 def last_kernel(l0_ref, k_ref, v_ref, z_ref, cum_ref, in_ref, e_ref, g_ref, dkl_ref, dvl_ref, h_ref, x1_ref, dq_ref, x_ref,
-                wq_ref, wk_ref, wv_ref, wf_ref, dk_ref, dv_ref, dz_ref, dxn_ref, bias_ref, gg_ref, state):
-    step = pl.program_id(0)
+                wq_ref, wk_ref, wv_ref, wf_ref, dk_ref, dv_ref, dz_ref, dxn_ref, bias_ref, gg_ref,
+                state, wq, wk, wv, wf, sems):
+    step, steps = pl.program_id(0), pl.num_programs(0)
+    loads = [pltpu.make_async_copy(source, target, sems.at[i])
+             for i, (source, target) in enumerate(((wq_ref, wq), (wk_ref, wk), (wv_ref, wv), (wf_ref, wf)))]
 
     @pl.when(step == 0)
     def _():
+        for load in loads:
+            load.start()
         state[...] = l0_ref[...]
-        gg_ref[...] = jnp.zeros_like(gg_ref)
         bias_ref[...] = jnp.zeros_like(bias_ref)
 
     width = k_ref.shape[1]
@@ -248,10 +252,9 @@
     keep = jnp.exp(total[:, :1])
     lg = keep * state[...]
     lg_k, lg_v = lg[:, :width].astype(bf16), lg[:, width:].astype(bf16)
-    dk = (dkl_ref[...] + nn(i_hi, lg_k)).astype(bf16)
-    dv = (dvl_ref[...] + nn(i_hi, lg_v)).astype(bf16)
-    dk_ref[...] = dk
-    dv_ref[...] = dv
+    rows = pl.ds(pl.multiple_of((steps - 1 - step) * CHUNK, CHUNK), CHUNK)
+    dk_ref[rows, :] = (dkl_ref[...] + nn(i_hi, lg_k)).astype(bf16)
+    dv_ref[rows, :] = (dvl_ref[...] + nn(i_hi, lg_v)).astype(bf16)
     x1 = x1_ref[...]
     x2 = nt(k, lg_k) + nt(v, lg_v)
     met = jnp.broadcast_to(jnp.sum(lg * e_ref[0], axis=1, keepdims=True), (lg.shape[0], CHUNK)).T
@@ -265,14 +268,19 @@
     )
     rate = lax.logistic(-z)
     dz = (dla * RATE * rate * (1.0 - rate)).astype(bf16)
-    dz_ref[...] = dz
+    dz_ref[rows, :] = dz
     bias_ref[...] += jnp.sum(dz.astype(f32).reshape(-1, 8, dz.shape[1]), axis=0)
     state[...] = g_ref[0] + lg
-    dxn = nt(dq_ref[...], wq_ref[...]) + nt(dk, wk_ref[...]) + nt(dv, wv_ref[...]) + nt(dz, wf_ref[...])
-    dxn_ref[...] = dxn.astype(bf16)
-    x = x_ref[...].astype(f32)
-    r1 = lax.rsqrt(jnp.mean(x * x, axis=-1, keepdims=True) + EPS)
-    gg_ref[...] += jnp.sum((dxn * x * r1).reshape(-1, 8, x.shape[1]), axis=0)
+
+    @pl.when(step == steps - 1)
+    def _():
+        for load in loads:
+            load.wait()
+        dxn = nt(dq_ref[...], wq[...]) + nt(dk_ref[...], wk[...]) + nt(dv_ref[...], wv[...]) + nt(dz_ref[...], wf[...])
+        dxn_ref[...] = dxn.astype(bf16)
+        x = x_ref[...].astype(f32)
+        r1 = lax.rsqrt(jnp.mean(x * x, axis=-1, keepdims=True) + EPS)
+        gg_ref[...] = jnp.sum((dxn * x * r1).reshape(-1, 8, x.shape[1]), axis=0)
 
 
 def out_kernel(hid_ref, ffn_ref, *refs):
@@ -350,7 +358,7 @@
 
 def wide_grad_kernel(*refs):
     out_ref = refs[-1]
-    count = (len(refs) - 2) // 3
+    count = (len(refs) - 1) // 3
     hn, dg, du = refs[:count], refs[count : 2 * count], refs[2 * count : 3 * count]
     blocks, _, width, units = out_ref.shape
     for i, grads in enumerate((dg, du)):
@@ -368,7 +376,7 @@
 
 
 def state_grad_kernel(count, *refs):
-    xn_ref, out_ref = refs[0], refs[-1]
+    xn_ref, query_ref, out_ref = refs[0], refs[-2], refs[-1]
     dk, dv, dz, bias, gain1, gain2 = (refs[1 + i * count : 1 + (i + 1) * count] for i in range(6))
     rows, width = dk[0].shape
     slots = dz[0].shape[1]
@@ -377,7 +385,8 @@
     xn = [xn_ref[i * rows : (i + 1) * rows, :] for i in range(count)]
     for i, grads in enumerate((dk, dv)):
         block = summed([(x, g[...]) for x, g in zip(xn, grads)])
-        out_ref[:, :span, i * width : (i + 1) * width] = block.reshape(groups, span, width)
+        out_ref[:, :span, (2 + i) * width : (3 + i) * width] = block.reshape(groups, span, width)
+    out_ref[:, :span, : 2 * width] = query_ref[...].reshape(groups, span, 2 * width)
     forget = tn(xn[0], dz[0][...])
     for x, g in zip(xn[1:], dz[1:]):
         forget = forget + tn(x, g[...])
@@ -395,7 +404,7 @@
     small = padded(forget)
     lane = lax.broadcasted_iota(jnp.int32, small.shape, 1)
     small = jnp.where(lane == slots, column(gain2), jnp.where(lane == slots + 1, column(gain1), small))
-    out_ref[:, :span, 2 * width :] = small.astype(bf16).reshape(groups, span, slots + pad)
+    out_ref[:, :span, 4 * width :] = small.astype(bf16).reshape(groups, span, slots + pad)
     total = bias[0][...]
     for part in bias[1:]:
         total = total + part[...]
@@ -404,8 +413,8 @@
     row = lax.broadcasted_iota(jnp.int32, total.shape, 0)
     tail = jnp.where(row == 0, upper, jnp.where(row == 1, total - upper, 0.0)).astype(bf16)
     for g in range(groups):
-        out_ref[g, span:, : 2 * width] = jnp.zeros((16, 2 * width), bf16)
-        out_ref[g, span:, 2 * width :] = tail
+        out_ref[g, span:, : 4 * width] = jnp.zeros((16, 4 * width), bf16)
+        out_ref[g, span:, 4 * width :] = tail
 
 
 def pack(ref, m, decay, state):
@@ -477,12 +486,12 @@
         in_specs=[pl.BlockSpec(memory_space=pltpu.VMEM)] * len(operands),
         out_specs=[pl.BlockSpec(memory_space=pltpu.VMEM)] * len(shapes),
         out_shape=shapes,
-        compiler_params=pltpu.CompilerParams(vmem_limit_bytes=48 * MIB),
+        compiler_params=pltpu.CompilerParams(vmem_limit_bytes=12 * MIB),
         cost_estimate=cost(0, 6 * MIB),
     )(*operands)
 
 
-def scan_states(n, state, decay, sent, after, own=(), pieces=1, tie=None):
+def scan_states(n, state, decay, sent, after, own=(), pieces=1, tie=None, last_tie=None):
     parts, slots, width = state.shape
     part, bit, hops = [], 1, 0
     while bit < n:
@@ -491,6 +500,8 @@
         shapes = [shaped(state.shape, f32), shaped(decay.shape, f32)] * 2 + [shaped(sent.shape, bf16)]
         if final:
             shapes = [shaped((parts * pieces, slots, width), f32)]
+        if final and last_tie is not None:
+            state = behind_of(state, last_tie)
         results = in_vmem(
             "hop",
             functools.partial(hop_kernel, bit, after, not part, final, parts, pieces),
@@ -692,38 +703,36 @@
             + [vmem((TILE, width), bf16), pltpu.SemaphoreType.DMA((2,)), pltpu.SemaphoreType.DMA((6,)),
                pltpu.SemaphoreType.DMA((tile_count,))],
             cost=cost(12 * TILE * width * units, 6 * width * units + TILE * width * 14),
+            vmem=44,
             loose=(1, 2),
             loose_out=(6,),
         )(x, attended, gain2, cot, full)
 
     group = max(1, TILE // span)
-    wide = group * span
-    grads_shape = shaped((n_seq, 3, span, units), bf16)
-
+    columns = group * span
     def down_grads(acts):
         return call(
             "down_grads",
             down_grad_kernel,
-            (width // wide,),
-            [pl.BlockSpec((rows, wide), lambda j: (0, j))] + [fixed((TILE, units))] * len(acts),
-            pl.BlockSpec((group, 1, span, units), lambda j: (j, 2, 0, 0)),
-            grads_shape,
+            (width // columns,),
+            [pl.BlockSpec((rows, columns), lambda j: (0, j))] + [fixed((TILE, units))] * len(acts),
+            pl.BlockSpec((group, span, units), lambda j: (j, 0, 0)),
+            shaped((n_seq, span, units), bf16),
             cost=cost(2 * rows * width * units, 2 * (rows * width + rows * units + width * units)),
         )(cot, *acts)
 
-    def wide_grads(normed, gates, ups, held_grads):
+    def wide_grads(normed, gates, ups):
         count = len(normed)
         return call(
             "wide_grads",
             wide_grad_kernel,
-            (width // wide,),
-            [pl.BlockSpec((TILE, wide), lambda j: (0, j))] * count
-            + [fixed((TILE, units))] * (2 * count) + [anywhere],
+            (width // columns,),
+            [pl.BlockSpec((TILE, columns), lambda j: (0, j))] * count
+            + [fixed((TILE, units))] * (2 * count),
             pl.BlockSpec((group, 2, span, units), lambda j: (j, 0, 0, 0)),
-            grads_shape,
+            shaped((n_seq, 2, span, units), bf16),
             cost=cost(4 * rows * width * units, 2 * (rows * width + 2 * rows * units + 2 * width * units)),
-            aliases={3 * count: 0},
-        )(*normed, *gates, *ups, held_grads)
+        )(*normed, *gates, *ups)
 
     def back(m, t, dhn, hidden):
         o, p, scores, e_chunks = reads[m, t][:4]
@@ -749,19 +758,21 @@
 
     def last(m, t, leaving, saved):
         dq, dk_local, dv_local, h_sum, x_local, g_chunks = saved
+        here = m * pieces + t
         return call(
             "last",
             last_kernel,
             (chunks,),
-            [state_of(m * pieces + t), chunk_rows(m, t, head, True), chunk_rows(m, t, head, True),
+            [state_of(here), chunk_rows(m, t, head, True), chunk_rows(m, t, head, True),
              *[chunk_rows(m, t, slots, True)] * 3, chunk_state(True), chunk_state(True), own_rows(head, True),
-             own_rows(head, True), own_rows(slots, True), own_rows(slots, True), own_rows(head, True),
-             chunk_rows(m, t, width, True)] + [fixed((width, head))] * 3 + [fixed((width, slots))],
-            [own_rows(head, True), own_rows(head, True), own_rows(slots, True), own_rows(width, True), whole((8, slots)),
+             own_rows(head, True), own_rows(slots, True), own_rows(slots, True), whole((TILE, head)),
+             pl.BlockSpec((TILE, width), lambda i: (here, 0))] + [anywhere] * 4,
+            [whole((TILE, head)), whole((TILE, head)), whole((TILE, slots)), whole((TILE, width)), whole((8, slots)),
              whole((8, width))],
             [shaped((TILE, head), bf16), shaped((TILE, head), bf16), shaped((TILE, slots), bf16),
              shaped((TILE, width), bf16), shaped((8, slots), f32), shaped((8, width), f32)],
-            [state_scratch],
+            [state_scratch] + [pltpu.VMEM((width, head), bf16)] * 3
+            + [pltpu.VMEM((width, slots), bf16), pltpu.SemaphoreType.DMA((4,))],
             cost=cost(2 * TILE * width * (3 * head + slots), TILE * width * 8 + TILE * head * 20 + width * head * 6),
             loose=(0,),
             loose_out=(3,),
@@ -852,14 +863,15 @@
     start()
     end(go_feed(1, 1), ("dhn", 0, 0))
     start()
-    live["grads"] = down_grads(taken("act"))
+    live["down_grads"] = down_grads(taken("act"))
     go_back(0, 0)
     end(live.pop(("ffn_part", 0, 0)), ("dhn", 0, 1))
     start()
-    live["grads"] = wide_grads(taken("hn"), taken("dgate"), taken("dup"), live["grads"])
+    down_shares = lax.psum_scatter(live.pop("down_grads"), "seq", scatter_dimension=0)
+    live["wide_grads"] = wide_grads(taken("hn"), taken("dgate"), taken("dup"))
     end(live.pop(("ffn_part", 0, 1)), ("dhn", 1, 0))
     start()
-    ffn_shares = lax.psum_scatter(live.pop("grads"), "seq", scatter_dimension=0)
+    wide = live.pop("wide_grads")
     go_back(0, 1)
     go_back(1, 0)
     end(live.pop(("ffn_part", 1, 0)), ("dhn", 1, 1))
@@ -874,30 +886,28 @@
         [shaped(local.shape, f32), shaped(decay.shape, f32), shaped(sent.shape, bf16)],
     )
 
-    def next_step(sent):
-        live["sent"], live["xn"] = sent, xn
-        end(live.pop(("ffn_part", 1, 1)), ("ffn", 0, 0))
-        start()
-        return live.pop("sent")
-
-    live["leaving"] = scan_states(n_seq, *folded, True, own, pieces, next_step)
-    xn_started = live.pop("xn")
-    grad_columns = [pl.BlockSpec((rows, TILE), lambda j: (0, j))]
+    live["xn"] = xn
+    end(live.pop(("ffn_part", 1, 1)), ("ffn", 0, 0))
+    start()
+    xn_columns = [pl.BlockSpec((rows, TILE), lambda j: (0, j))]
     piece_columns = [pl.BlockSpec((TILE, TILE), lambda j: (0, j))] * len(every)
     piece_whole = [fixed((TILE, head))] * len(every)
-    live["query_grads"] = call(
+    query_grads = call(
         "query_grads",
         functools.partial(query_grad_kernel, len(every)),
         (width // TILE,),
-        grad_columns + piece_columns + piece_whole * 2,
+        xn_columns + piece_columns + piece_whole * 2,
         pl.BlockSpec((TILE, 2 * head), lambda j: (j, 0)),
         shaped((width, 2 * head), bf16),
         cost=cost(4 * rows * width * head, 4 * rows * width + 4 * rows * head + 4 * width * head),
-    )(xn_started, *[backs[key][1] for key in every], *[backs[key][2] for key in every], *[reads[key][0] for key in every])
+    )(live.pop("xn"), *[backs[key][1] for key in every], *[backs[key][2] for key in every],
+      *[reads[key][0] for key in every])
+    live["leaving"] = scan_states(n_seq, *folded, True, own, pieces, last_tie=query_grads)
+    live["query_grads"], live["wide"] = query_grads, wide
     go_last(0, 0)
     end(live.pop(("dxn_part", 0, 0)), ("ffn", 0, 1))
     start()
-    query_shares = lax.psum_scatter(live.pop("query_grads"), "seq", scatter_dimension=0, tiled=True)
+    wide_shares = lax.psum_scatter(live.pop("wide"), "seq", scatter_dimension=0)
     go_last(0, 1)
     go_last(1, 0)
     go_last(1, 1)
@@ -910,20 +920,22 @@
         "state_grads",
         functools.partial(state_grad_kernel, len(every)),
         (width // TILE,),
-        grad_columns + piece_whole * 2 + [fixed((TILE, slots))] * len(every) + [fixed((8, slots))] * len(every) + few * 2,
-        pl.BlockSpec((group, span + 16, 2 * head + 128), lambda j: (j, 0, 0)),
-        shaped((n_seq, span + 16, 2 * head + 128), bf16),
+        xn_columns + piece_whole * 2 + [fixed((TILE, slots))] * len(every) + [fixed((8, slots))] * len(every) + few * 2
+        + [pl.BlockSpec((TILE, 2 * head), lambda j: (j, 0))],
+        pl.BlockSpec((group, span + 16, 4 * head + 128), lambda j: (j, 0, 0)),
+        shaped((n_seq, span + 16, 4 * head + 128), bf16),
         cost=cost(4 * rows * width * head, 2 * rows * width + 4 * rows * head + 4 * width * head),
-    )(live.pop("xn"), *[lasts[key][i] for i in (0, 1, 2, 4, 5) for key in every], *[backs[key][10] for key in every])
+    )(live.pop("xn"), *[lasts[key][i] for i in (0, 1, 2, 4, 5) for key in every], *[backs[key][10] for key in every],
+      live.pop("query_grads"))
     end(live.pop(("dxn_part", 1, 0)), ("ffn", 1, 1))
     start()
-    state_shares = lax.psum_scatter(live.pop("state_grads"), "seq", scatter_dimension=0)
+    attn_shares = lax.psum_scatter(live.pop("state_grads"), "seq", scatter_dimension=0)
     finish_out(0, 0)
     finish_out(0, 1)
-    live["out"], live["ffn_shares"] = outs[0], ffn_shares
+    live["out"], live["down"], live["wide"] = outs[0], down_shares, wide_shares
     end(live.pop(("dxn_part", 1, 1)), ("dxn", 0, 0))
     start()
-    outs[0], ffn_shares = live.pop("out"), live.pop("ffn_shares")
+    outs[0], down_shares, wide_shares = live.pop("out"), live.pop("down"), live.pop("wide")
     finish_out(1, 0)
     finish_out(1, 1)
     finish_grad(0, 0)
@@ -932,11 +944,11 @@
     start()
     in_grads[0] = live.pop("in_grad")
     finish_grad(0, 1)
-    live["in_grad"] = in_grads[0]
+    live["in_grad"], live["attn"] = in_grads[0], attn_shares
     end(None, ("dxn", 1, 0))
     start()
-    in_grads[0] = live.pop("in_grad")
-    gain1_total = state_shares[:span, 2 * head + slots + 1].astype(f32)
+    in_grads[0], late = live.pop("in_grad"), live.pop("attn").astype(f32)
+    gain1_total = late[:span, 4 * head + slots + 1]
     bit = 1
     while bit < n_head:
         gain1_total = gain1_total + lax.ppermute(gain1_total, "head", [(i, i ^ bit) for i in range(n_head)])
@@ -944,24 +956,22 @@
     finish_grad(1, 0)
     end(None, ("dxn", 1, 1))
     finish_grad(1, 1)
-    query_shares = query_shares.astype(f32)
-    state_shares = state_shares.astype(f32)
-    small_shares = state_shares[:, 2 * head :]
+    small_shares = late[:, 4 * head :]
 
     return (
         live["out"],
         in_grads[0],
         gain1_total,
-        query_shares[:, :head],
-        state_shares[:span, :head],
-        state_shares[:span, head : 2 * head],
+        late[:span, :head],
+        late[:span, 2 * head : 3 * head],
+        late[:span, 3 * head : 4 * head],
         small_shares[:span, :slots],
         small_shares[span, :slots] + small_shares[span + 1, :slots],
-        query_shares[:, head:].T,
+        late[:span, head : 2 * head].T,
         small_shares[:span, slots],
-        ffn_shares[0].astype(f32),
-        ffn_shares[1].astype(f32),
-        ffn_shares[2].astype(f32).T,
+        wide_shares[0].astype(f32),
+        wide_shares[1].astype(f32),
+        down_shares.astype(f32).T,
     )
 
 

time: 601 us -> 590 us (0.982)
  waiting for transfers between devices: 114 us -> 167 us
  Pallas kernels: 313 us -> 285 us
  local copies, waits for them, and re-layouts: 50.1 us -> 26.8 us
  starting transfers between devices: 87.9 us -> 77.8 us
    pallas_call x25, Pallas kernels: 45.2 us -> 17.8 us  [in_vmem(): pl.pallas_call(kernel, name=name, in_specs=[pl.BlockSpec(memory_space=plt...]
    ppermute x18, waiting for transfers between devices: 66.7 us -> 89.3 us  [step(): outer = lax.ppermute(payload, 'head', way)]
    unnamed x166 -> x72, local copies, waits for them, and re-layouts: 45.3 us -> 23.5 us
    reduce_scatter x1, waiting for transfers between devices: 11.3 us -> 31.4 us  [on_device(): lax.psum_scatter(live.pop('state_grads'), 'seq', scatter_dimension=0)]
    ppermute x2, waiting for transfers between devices: 0.08 us -> 13.3 us  [on_device(): lax.ppermute(gain1_total, 'head', [(i, i ^ bit) for i in range(n_head)])]
    ppermute x6, waiting for transfers between devices: 36.2 us -> 26.1 us  [scan_states(): got = lax.ppermute(sent, 'seq', [(i, i ^ bit) for i in range(n)])]
    reduce_scatter x2, waiting for transfers between devices: 0.02 us -> 6.91 us  [the longest x1 6.91 us: on_device(): wide_shares = lax.psum_scatter(live.pop('wide'), 'seq', scatter_dimension=0)]
  transfers between devices with their start and end apart: 46 -> 46, of which waited for: 16 -> 14; matrix products, arithmetic and copies ran while one was open for 3% -> 3% of each run, Pallas kernels for 47% -> 45%
where the time goes in v5:
time: 590 us; the launch traced here: 581 us
  Pallas kernels  285 us (48%)
  waiting for transfers between devices  167 us (28%)
  starting transfers between devices  77.8 us (13%)
  local copies, waits for them, and re-layouts  26.8 us (5%)
  between operations  14.8 us (3%)
  other arithmetic  9.64 us (2%)
    pallas_call x29, Pallas kernels, run(): function(*[o if i in loose or spec.memory_space == pltpu.SMEM else pltpu....  267 us
    ppermute x18, waiting for transfers between devices, step(): outer = lax.ppermute(payload, 'head', way)  89.3 us
    ppermute x18, starting transfers between devices, step(): outer = lax.ppermute(payload, 'head', way)  47.5 us
    reduce_scatter x1, waiting for transfers between devices, on_device(): lax.psum_scatter(live.pop('state_grads'), 'seq', scatter_dimension=0)  31.4 us
    ppermute x6, waiting for transfers between devices, scan_states(): got = lax.ppermute(sent, 'seq', [(i, i ^ bit) for i in range(n)])  26.1 us
    unnamed x72, local copies, waits for them, and re-layouts  23.5 us
    pallas_call x25, Pallas kernels, in_vmem(): pl.pallas_call(kernel, name=name, in_specs=[pl.BlockSpec(memory_space=plt...  17.8 us
    ppermute x16, starting transfers between devices, step(): middle = lax.ppermute(pair, 'head', self.MIDDLE)  17.2 us
  transfers between devices with their start and end apart: 46, of which 14 were waited for; matrix products, arithmetic and copies ran while one was open for 3% of the time, Pallas kernels for 45%

profile of v5, /device:TPU:0, one launch (start us, length us, event | category | flops | bytes accessed | tf_op | source)
XLA Modules:
  0.0 581.2 jit_solution(16969178547358039365)
XLA Ops:
  9.2 16.9 %project.1 = (bf16[1024,2048]{1,0:T(8,128)(2,1)}, bf16[1024,512]{1,0:T(8,128)(2,1)}, bf16[1024,512]{1,0:T(8,128)(2,1)}, bf16[1024,512]{1,0:T(8,128)(2,1)}, f32[1...) custom-call(bf16[1024,2048]{1,0:T(8,128)(2,1)} %bitcast.34, ...), custom_call_target="tpu_custom_call" | custom-call | flops 6710886400 | bytes 18874368 | tf_op jit(solution)/shard_map/project/pallas_call | solution.py:62
  28.4 2.9 pad_maximum_fusion
  31.4 2.9 collective-permute-start.1
  34.3 7.3 %collective-permute-done.1.refs_2_ = bf16[2,64,1152]{2,1,0:T(8,128)(2,1)S(1)} collective-permute-done((bf16[2,64,1152]{2,1,0:T(8,128)(2,1)S(1)}, bf16[2,64,1152]{2,1,0:T(8,128)(2,1)S(1)}, u32[]{:S(2)}, u32[]{:S(2)}) %collective-permute-start.1) | collective-permute-done | bytes 294944 | tf_op jit(solution)/shard_map/ppermute | solution.py:498
  43.8 12.3 %collective-permute-done.2.refs_2_ = bf16[2,64,1152]{2,1,0:T(8,128)(2,1)S(1)} collective-permute-done((bf16[2,64,1152]{2,1,0:T(8,128)(2,1)S(1)}, bf16[2,64,1152]{2,1,0:T(8,128)(2,1)S(1)}, u32[]{:S(2)}, u32[]{:S(2)}) %collective-permute-start.2) | collective-permute-done | bytes 294944 | tf_op jit(solution)/shard_map/ppermute | solution.py:498
  56.3 5.3 read.4
  61.6 3.8 collective-permute-start.3
  65.4 5.3 read.5
  70.7 13.4 %collective-permute-done.3.refs_1_ = bf16[256,2048]{1,0:T(8,128)(2,1)S(1)} collective-permute-done((bf16[256,2048]{1,0:T(8,128)(2,1)S(1)}, bf16[256,2048]{1,0:T(8,128)(2,1)S(1)}, u32[]{:S(2)}, u32[]{:S(2)}) %collective-permute-start.3) | collective-permute-done | bytes 1048608 | tf_op jit(solution)/shard_map/ppermute | solution.py:580
  84.2 4.5 collective-permute-start.4
  89.4 5.3 read.6
  94.7 13.3 %collective-permute-done.4.refs_1_ = bf16[256,2048]{1,0:T(8,128)(2,1)S(1)} collective-permute-done((bf16[256,2048]{1,0:T(8,128)(2,1)S(1)}, bf16[256,2048]{1,0:T(8,128)(2,1)S(1)}, u32[]{:S(2)}, u32[]{:S(2)}) %collective-permute-start.4) | collective-permute-done | bytes 1048608 | tf_op jit(solution)/shard_map/ppermute | solution.py:580
  108.1 3.0 collective-permute-start.6
  111.9 5.4 read.7
  117.3 12.9 %collective-permute-done.6.refs_1_ = bf16[256,2048]{1,0:T(8,128)(2,1)S(1)} collective-permute-done((bf16[256,2048]{1,0:T(8,128)(2,1)S(1)}, bf16[256,2048]{1,0:T(8,128)(2,1)S(1)}, u32[]{:S(2)}, u32[]{:S(2)}) %collective-permute-start.6) | collective-permute-done | bytes 1048608 | tf_op jit(solution)/shard_map/ppermute | solution.py:580
  131.3 3.1 collective-permute-start.8
  137.6 19.3 %feed.4 = (f32[256,2048]{1,0:T(8,128)}, bf16[256,2048]{1,0:T(8,128)(2,1)}, bf16[256,1408]{1,0:T(8,128)(2,1)}, bf16[256,1408]{1,0:T(8,128)(2,1)}, bf16[256,1408]{...) custom-call(bf16[1024,2048]{1,0:T(8,128)(2,1)} %bitcast.35, ...), custom_call_target="tpu_custom_call" | custom-call | flops 8858370048 | bytes 24641536 | tf_op jit(solution)/shard_map/feed/pallas_call | solution.py:62
  158.7 2.2 collective-permute-start.10
  162.1 19.3 %feed.5 = (f32[256,2048]{1,0:T(8,128)}, bf16[256,2048]{1,0:T(8,128)(2,1)}, bf16[256,1408]{1,0:T(8,128)(2,1)}, bf16[256,1408]{1,0:T(8,128)(2,1)}, bf16[256,1408]{...) custom-call(bf16[1024,2048]{1,0:T(8,128)(2,1)} %bitcast.36, ...), custom_call_target="tpu_custom_call" | custom-call | flops 8858370048 | bytes 24641536 | tf_op jit(solution)/shard_map/feed/pallas_call | solution.py:62
  181.7 3.0 collective-permute-start.12
  185.6 19.4 %feed.6 = (f32[256,2048]{1,0:T(8,128)}, bf16[256,2048]{1,0:T(8,128)(2,1)}, bf16[256,1408]{1,0:T(8,128)(2,1)}, bf16[256,1408]{1,0:T(8,128)(2,1)}, bf16[256,1408]{...) custom-call(bf16[1024,2048]{1,0:T(8,128)(2,1)} %bitcast.37, ...), custom_call_target="tpu_custom_call" | custom-call | flops 8858370048 | bytes 24641536 | tf_op jit(solution)/shard_map/feed/pallas_call | solution.py:62
  205.2 2.9 collective-permute-start.14
  209.0 19.3 %feed.7 = (f32[256,2048]{1,0:T(8,128)}, bf16[256,2048]{1,0:T(8,128)(2,1)}, bf16[256,1408]{1,0:T(8,128)(2,1)}, bf16[256,1408]{1,0:T(8,128)(2,1)}, bf16[256,1408]{...) custom-call(bf16[1024,2048]{1,0:T(8,128)(2,1)} %bitcast.38, ...), custom_call_target="tpu_custom_call" | custom-call | flops 8858370048 | bytes 24641536 | tf_op jit(solution)/shard_map/feed/pallas_call | solution.py:62
  231.8 2.1 collective-permute-start.17
  233.9 8.7 %back.4 = (f32[256,2048]{1,0:T(8,128)}, bf16[256,2048]{1,0:T(8,128)(2,1)}, bf16[256,512]{1,0:T(8,128)(2,1)}, f32[256,512]{1,0:T(8,128)}, f32[256,512]{1,0:T(8,12...) custom-call(bf16[256,2048]{1,0:T(8,128)(2,1)S(1)} %get-tuple-element, ...), custom_call_target="tpu_custom_call" | custom-call | flops 930086912 | bytes 9961472 | tf_op jit(solution)/shard_map/back/pallas_call | solution.py:62
  242.6 12.0 %down_grads.1 = bf16[8,256,1408]{2,1,0:T(8,128)(2,1)} custom-call(bf16[1024,2048]{1,0:T(8,128)(2,1)} %bitcast.52, bf16[256,1408]{1,0:T(8,128)(2,1)} %get-tuple-element.561.refs_1_, bf16[256,1408]{1,0:T(8,128)(2,1)} %get-tuple-element.562.refs_2_, bf16[256,1408]{1,0:T(8,128)(2,1)} %get-tuple-element.563.refs_3_, bf16[256,1408]{1,0:T(8,128)(2,1)} %get-tuple-element.564.refs_4_), custom_call_target="tpu_custom_call" | custom-call | flops 5905580032 | bytes 12845056 | tf_op jit(solution)/shard_map/down_grads/pallas_call | solution.py:62
  254.7 2.3 join.25
  262.5 19.5 %wide_grads.1 = bf16[8,2,256,1408]{3,2,1,0:T(8,128)(2,1)} custom-call(bf16[256,2048]{1,0:T(8,128)(2,1)} %get-tuple-element.583.refs_0_, bf16[256,2048]{1,0:T(8,128)(2,1)} %get-tuple-element.584.refs_1_, bf16[256,2048]{1,0:T(8,128)(2,1)} %get-tuple-element.585.refs_2_, bf16[256,2048]{1,0:T(8,128)(2,1)} %get-tuple-element.586.refs_3_, ...), custom_call_target="tpu_custom_call" | custom-call | flops 11811160064 | bytes 21495808 | tf_op jit(solution)/shard_map/wide_grads/pallas_call | solution.py:62
  286.5 2.2 collective-permute-start.20
  289.4 8.8 %back.5 = (f32[256,2048]{1,0:T(8,128)}, bf16[256,2048]{1,0:T(8,128)(2,1)}, bf16[256,512]{1,0:T(8,128)(2,1)}, f32[256,512]{1,0:T(8,128)}, f32[256,512]{1,0:T(8,12...) custom-call(bf16[256,2048]{1,0:T(8,128)(2,1)S(1)} %get-tuple-element, ...), custom_call_target="tpu_custom_call" | custom-call | flops 930086912 | bytes 9961472 | tf_op jit(solution)/shard_map/back/pallas_call | solution.py:62
  298.3 8.8 %back.6 = (f32[256,2048]{1,0:T(8,128)}, bf16[256,2048]{1,0:T(8,128)(2,1)}, bf16[256,512]{1,0:T(8,128)(2,1)}, f32[256,512]{1,0:T(8,128)}, f32[256,512]{1,0:T(8,12...) custom-call(bf16[256,2048]{1,0:T(8,128)(2,1)S(1)} %get-tuple-element, ...), custom_call_target="tpu_custom_call" | custom-call | flops 930086912 | bytes 9961472 | tf_op jit(solution)/shard_map/back/pallas_call | solution.py:62
  307.3 2.2 collective-permute-start.22
  310.2 8.8 %back.7 = (f32[256,2048]{1,0:T(8,128)}, bf16[256,2048]{1,0:T(8,128)(2,1)}, bf16[256,512]{1,0:T(8,128)(2,1)}, f32[256,512]{1,0:T(8,128)}, f32[256,512]{1,0:T(8,12...) custom-call(bf16[256,2048]{1,0:T(8,128)(2,1)S(1)} %get-tuple-element, ...), custom_call_target="tpu_custom_call" | custom-call | flops 930086912 | bytes 9961472 | tf_op jit(solution)/shard_map/back/pallas_call | solution.py:62
  319.2 8.7 %collective-permute-done.22.refs_1_ = bf16[256,2048]{1,0:T(8,128)(2,1)S(1)} collective-permute-done((bf16[256,2048]{1,0:T(8,128)(2,1)S(1)}, bf16[256,2048]{1,0:T(8,128)(2,1)S(1)}, u32[]{:S(2)}, u32[]{:S(2)}) %collective-permute-start.22) | collective-permute-done | bytes 1048608 | tf_op jit(solution)/shard_map/ppermute | solution.py:580
  329.0 3.8 collective-permute-start.24
  335.5 5.3 collective-permute-done.27.refs_2_
  343.0 11.0 %query_grads.1.refs_25_ = bf16[2048,1024]{1,0:T(8,128)(2,1)} custom-call(bf16[1024,2048]{1,0:T(8,128)(2,1)} %get-tuple-element.726.refs_0_, bf16[256,2048]{1,0:T(8,128)(2,1)} %get-tuple-element.649.refs_1_, bf16[256,2048]{1,0:T(8,128)(2,1)} %get-tuple-element.650.refs_2_, bf16[256,2048]{1,0:T(8,128)(2,1)} %get-tuple-element.651.refs_3_, ...), custom_call_target="tpu_custom_call" | custom-call | flops 4294967296 | bytes 14680064 | tf_op jit(solution)/shard_map/query_grads/pallas_call | solution.py:62
  354.4 8.1 %last.4 = (bf16[256,512]{1,0:T(8,128)(2,1)}, bf16[256,512]{1,0:T(8,128)(2,1)}, bf16[256,64]{1,0:T(8,128)(2,1)}, bf16[256,2048]{1,0:T(8,128)(2,1)S(1)}, f32[8,64]{1,0:T(8,128)}, /*index=5*/f32[8,2048]{1,0:T(8,128)}) custom-call(f32[4,64,1024]{2,1,0:T(8,128)S(1)} %hop.11.l0_ref, bf16[1024,512]{1,0:T(8,128)(2,1)} %get-tuple-element.407.k_ref, ...), custom_call_target="tpu_custom_call" | custom-call | flops 1677721600 | bytes 13107200 | tf_op jit(solution)/shard_map/last/pallas_call | solution.py:62
  365.2 2.4 collective-permute-start.29
  368.3 10.4 %last.7 = (bf16[256,512]{1,0:T(8,128)(2,1)}, bf16[256,512]{1,0:T(8,128)(2,1)}, bf16[256,64]{1,0:T(8,128)(2,1)}, bf16[256,2048]{1,0:T(8,128)(2,1)S(1)}, f32[8,64]{1,0:T(8,128)}, /*index=5*/f32[8,2048]{1,0:T(8,128)}) custom-call(f32[4,64,1024]{2,1,0:T(8,128)S(1)} %hop.11.l0_ref, bf16[1024,512]{1,0:T(8,128)(2,1)} %get-tuple-element.407.k_ref, ...), custom_call_target="tpu_custom_call" | custom-call | flops 1677721600 | bytes 13107200 | tf_op jit(solution)/shard_map/last/pallas_call | solution.py:62
  378.7 9.4 %last.6 = (bf16[256,512]{1,0:T(8,128)(2,1)}, bf16[256,512]{1,0:T(8,128)(2,1)}, bf16[256,64]{1,0:T(8,128)(2,1)}, bf16[256,2048]{1,0:T(8,128)(2,1)S(1)}, f32[8,64]{1,0:T(8,128)}, /*index=5*/f32[8,2048]{1,0:T(8,128)}) custom-call(f32[4,64,1024]{2,1,0:T(8,128)S(1)} %hop.11.l0_ref, bf16[1024,512]{1,0:T(8,128)(2,1)} %get-tuple-element.407.k_ref, ...), custom_call_target="tpu_custom_call" | custom-call | flops 1677721600 | bytes 13107200 | tf_op jit(solution)/shard_map/last/pallas_call | solution.py:62
  388.1 9.1 %last.5 = (bf16[256,512]{1,0:T(8,128)(2,1)}, bf16[256,512]{1,0:T(8,128)(2,1)}, bf16[256,64]{1,0:T(8,128)(2,1)}, bf16[256,2048]{1,0:T(8,128)(2,1)S(1)}, f32[8,64]{1,0:T(8,128)}, /*index=5*/f32[8,2048]{1,0:T(8,128)}) custom-call(f32[4,64,1024]{2,1,0:T(8,128)S(1)} %hop.11.l0_ref, bf16[1024,512]{1,0:T(8,128)(2,1)} %get-tuple-element.407.k_ref, ...), custom_call_target="tpu_custom_call" | custom-call | flops 1677721600 | bytes 13107200 | tf_op jit(solution)/shard_map/last/pallas_call | solution.py:62
  397.3 3.4 join.30
  401.7 2.6 collective-permute-start.31
  405.9 13.8 %state_grads.1 = bf16[8,272,2176]{2,1,0:T(8,128)(2,1)} custom-call(bf16[1024,2048]{1,0:T(8,128)(2,1)} %get-tuple-element.726.refs_0_, bf16[256,512]{1,0:T(8,128)(2,1)} %get-tuple-element.727.refs_1_, bf16[256,512]{1,0:T(8,128)(2,1)} %get-tuple-element.728.refs_2_, bf16[256,512]{1,0:T(8,128)(2,1)} %get-tuple-element.729.refs_3_, ...), custom_call_target="tpu_custom_call" | custom-call | flops 4294967296 | bytes 10485760 | tf_op jit(solution)/shard_map/state_grads/pallas_call | solution.py:62
  419.7 2.3 join.31
  425.0 4.1 collective-permute-start.33
  430.0 2.4 out.4.refs_0_
  432.5 2.6 out.5.refs_0_
  435.1 7.0 %collective-permute-done.33.refs_1_ = bf16[256,2048]{1,0:T(8,128)(2,1)S(1)} collective-permute-done((bf16[256,2048]{1,0:T(8,128)(2,1)}, bf16[256,2048]{1,0:T(8,128)(2,1)S(1)}, u32[]{:S(2)}, u32[]{:S(2)}) %collective-permute-start.33) | collective-permute-done | bytes 1048608 | tf_op jit(solution)/shard_map/ppermute | solution.py:580
  444.2 6.9 %reduce-scatter.6.cloned.1.call-done = bf16[1,2,256,1408]{3,2,1,0:T(8,128)(2,1)} async-done(((bf16[8,2,256,1408]{3,2,1,0:T(8,128)(2,1)}), bf16[1,2,256,1408]{3,2,1,0:T(8,128)(2,1)}) %reduce-scatter.6.cloned.1.call-update) | async-done | bytes 1441808 | tf_op jit(solution)/shard_map/reduce_scatter | solution.py:910
  454.5 3.4 in_grad.4.refs_0_
  457.9 2.5 out.6.refs_0_
  460.4 2.6 out.7
  463.0 13.2 %collective-permute-done.35.refs_1_ = bf16[256,2048]{1,0:T(8,128)(2,1)S(1)} collective-permute-done((bf16[256,2048]{1,0:T(8,128)(2,1)}, bf16[256,2048]{1,0:T(8,128)(2,1)S(1)}, u32[]{:S(2)}, u32[]{:S(2)}) %collective-permute-start.35) | collective-permute-done | bytes 1048608 | tf_op jit(solution)/shard_map/ppermute | solution.py:580
  480.1 3.3 in_grad.5.refs_0_
  483.4 20.8 %collective-permute-done.37.refs_0_ = bf16[256,2048]{1,0:T(8,128)(2,1)S(1)} collective-permute-done((bf16[256,2048]{1,0:T(8,128)(2,1)S(1)}, bf16[256,2048]{1,0:T(8,128)(2,1)S(1)}, u32[]{:S(2)}, u32[]{:S(2)}) %collective-permute-start.37) | collective-permute-done | bytes 1048608 | tf_op jit(solution)/shard_map/ppermute | solution.py:580
  504.3 31.4 %reduce-scatter.8.cloned.1.call-done = bf16[1,272,2176]{2,1,0:T(8,128)(2,1)} async-done(((bf16[8,272,2176]{2,1,0:T(8,128)(2,1)}), bf16[1,272,2176]{2,1,0:T(8,128)(2,1)}) %reduce-scatter.8.cloned.1.call-update) | async-done | bytes 1183760 | tf_op jit(solution)/shard_map/reduce_scatter | solution.py:932
  537.0 2.3 convert_bitcast_fusion
  539.3 2.9 copy.62
  544.5 2.7 collective-permute-start.40
  549.3 13.3 %collective-permute-done.40 = f32[256]{0:T(256)S(1)} collective-permute-done((f32[256]{0:T(256)S(1)}, f32[256]{0:T(256)S(1)}, u32[]{:S(2)}, u32[]{:S(2)}) %collective-permute-start.40) | collective-permute-done | bytes 1056 | tf_op jit(solution)/shard_map/ppermute | solution.py:954
  567.2 3.3 in_grad.6.refs_0_
  571.1 3.3 in_grad.7
  (170 shorter events, 69.8 us)
Async XLA Ops:
  7.2 129.2 %all-gather.3.cloned.1.call-start = ((), (), s32[]{:S(2)}) async-start(), calls=%async_computation.6 | async-start | bytes 19464192 | tf_op jit(solution)/shard_map/all_gather | solution.py:653
  9.2 18.9 %copy-start.33 = (bf16[1408,256]{1,0:T(8,128)(2,1)S(1)}, bf16[1408,256]{1,0:T(8,128)(2,1)}, u32[]{:S(2)}) copy-start(bf16[1408,256]{1,0:T(8,128)(2,1)} %param.24) | copy-start | bytes 2162692
  26.1 1.7 collective-permute-start
  31.4 412.8 %reduce-scatter.4.cloned.1.call-start = ((), (), s32[]{:S(2)}) async-start(), calls=%async_computation.3 | async-start | bytes 6488064 | tf_op jit(solution)/shard_map/reduce_scatter | solution.py:870
  31.4 10.2 %collective-permute-start.1 = (bf16[2,64,1152]{2,1,0:T(8,128)(2,1)S(1)}, bf16[2,64,1152]{2,1,0:T(8,128)(2,1)S(1)}, u32[]{:S(2)}, u32[]{:S(2)}) collective-permute-start(bf16[2,64,1152]{2,1,0:T(8,128)(2,1)S(1)} %get-tuple-element.417), channel_id=1, source_target_pairs={{0,8},{4,12},{8,0},{12,4},{16,24},{20,28},{24,16},{28,20},{1,9},{5... | collective-permute-start | bytes 884744 | tf_op jit(solution)/shard_map/ppermute | solution.py:498
  41.9 14.1 %collective-permute-start.2 = (bf16[2,64,1152]{2,1,0:T(8,128)(2,1)S(1)}, bf16[2,64,1152]{2,1,0:T(8,128)(2,1)S(1)}, u32[]{:S(2)}, u32[]{:S(2)}) collective-permute-start(bf16[2,64,1152]{2,1,0:T(8,128)(2,1)S(1)} %get-tuple-element.422), channel_id=1, source_target_pairs={{0,16},{4,20},{8,24},{12,28},{16,0},{20,4},{24,8},{28,12},{1,17},{... | collective-permute-start | bytes 884744 | tf_op jit(solution)/shard_map/ppermute | solution.py:498
  61.6 22.5 %collective-permute-start.3 = (bf16[256,2048]{1,0:T(8,128)(2,1)S(1)}, bf16[256,2048]{1,0:T(8,128)(2,1)S(1)}, u32[]{:S(2)}, u32[]{:S(2)}) collective-permute-start(bf16[256,2048]{1,0:T(8,128)(2,1)S(1)} %get-tuple-element.429.refs_0_), channel_id=1, source_target_pairs={{0,1},{3,2},{4,5},{7,6},{8,9},{11,10},{12,13},{15,14},{16,17},{19,... | collective-permute-start | bytes 3145736 | tf_op jit(solution)/shard_map/ppermute | solution.py:580
  84.2 23.8 %collective-permute-start.4 = (bf16[256,2048]{1,0:T(8,128)(2,1)S(1)}, bf16[256,2048]{1,0:T(8,128)(2,1)S(1)}, u32[]{:S(2)}, u32[]{:S(2)}) collective-permute-start(bf16[256,2048]{1,0:T(8,128)(2,1)S(1)} %get-tuple-element.433), channel_id=1, source_target_pairs={{0,1},{3,2},{4,5},{7,6},{8,9},{11,10},{12,13},{15,14},{16,17},{19,... | collective-permute-start | bytes 3145736 | tf_op jit(solution)/shard_map/ppermute | solution.py:580
  88.7 19.3 %collective-permute-start.5 = (bf16[256,2048]{1,0:T(8,128)(2,1)S(1)}, bf16[256,2048]{1,0:T(8,128)(2,1)S(1)}, u32[]{:S(2)}, u32[]{:S(2)}) collective-permute-start(bf16[256,2048]{1,0:T(8,128)(2,1)S(1)} %get-tuple-element.434.refs_2_), channel_id=1, source_target_pairs={{1,2},{2,1},{5,6},{6,5},{9,10},{10,9},{13,14},{14,13},{17,18},{18,... | collective-permute-start | bytes 3145736 | tf_op jit(solution)/shard_map/ppermute | solution.py:583
  108.1 22.1 %collective-permute-start.6 = (bf16[256,2048]{1,0:T(8,128)(2,1)S(1)}, bf16[256,2048]{1,0:T(8,128)(2,1)S(1)}, u32[]{:S(2)}, u32[]{:S(2)}) collective-permute-start(bf16[256,2048]{1,0:T(8,128)(2,1)S(1)} %get-tuple-element.442.refs_4_), channel_id=1, source_target_pairs={{0,1},{3,2},{1,0},{2,3},{4,5},{7,6},{5,4},{6,7},{8,9},{11,10},{9,8... | collective-permute-start | bytes 3145736 | tf_op jit(solution)/shard_map/ppermute | solution.py:580
  111.2 19.0 %collective-permute-start.7 = (bf16[256,2048]{1,0:T(8,128)(2,1)S(1)}, bf16[256,2048]{1,0:T(8,128)(2,1)S(1)}, u32[]{:S(2)}, u32[]{:S(2)}) collective-permute-start(bf16[256,2048]{1,0:T(8,128)(2,1)S(1)} %get-tuple-element.443.refs_2_), channel_id=1, source_target_pairs={{1,2},{2,1},{5,6},{6,5},{9,10},{10,9},{13,14},{14,13},{17,18},{18,... | collective-permute-start | bytes 3145736 | tf_op jit(solution)/shard_map/ppermute | solution.py:583
  130.2 6.2 %copy-start.28 = (f32[2048]{0:T(1024)S(1)}, f32[2048]{0:T(1024)}, u32[]{:S(2)}) copy-start(f32[2048]{0:T(1024)} %param.21) | copy-start | bytes 24580
  131.3 25.6 %collective-permute-start.8 = (bf16[256,2048]{1,0:T(8,128)(2,1)S(1)}, bf16[256,2048]{1,0:T(8,128)(2,1)}, u32[]{:S(2)}, u32[]{:S(2)}) collective-permute-start(bf16[256,2048]{1,0:T(8,128)(2,1)S(1)} %get-tuple-element.447.refs_4_), channel_id=1, source_target_pairs={{0,1},{3,2},{1,0},{2,3},{4,5},{7,6},{5,4},{6,7},{8,9},{11,10},{9,8... | collective-permute-start | bytes 3145736 | tf_op jit(solution)/shard_map/ppermute | solution.py:580
  134.4 22.5 %collective-permute-start.9 = (bf16[256,2048]{1,0:T(8,128)(2,1)S(1)}, bf16[256,2048]{1,0:T(8,128)(2,1)}, u32[]{:S(2)}, u32[]{:S(2)}) collective-permute-start(bf16[256,2048]{1,0:T(8,128)(2,1)S(1)} %get-tuple-element.448.refs_2_), channel_id=1, source_target_pairs={{1,2},{2,1},{5,6},{6,5},{9,10},{10,9},{13,14},{14,13},{17,18},{18,... | collective-permute-start | bytes 3145736 | tf_op jit(solution)/shard_map/ppermute | solution.py:583
  158.7 22.8 %collective-permute-start.10 = (bf16[256,2048]{1,0:T(8,128)(2,1)S(1)}, bf16[256,2048]{1,0:T(8,128)(2,1)S(1)}, u32[]{:S(2)}, u32[]{:S(2)}) collective-permute-start(bf16[256,2048]{1,0:T(8,128)(2,1)S(1)} %get-tuple-element.464.refs_4_), channel_id=1, source_target_pairs={{0,1},{3,2},{1,0},{2,3},{4,5},{7,6},{5,4},{6,7},{8,9},{11,10},{9,8... | collective-permute-start | bytes 3145736 | tf_op jit(solution)/shard_map/ppermute | solution.py:580
  160.8 20.6 %collective-permute-start.11 = (bf16[256,2048]{1,0:T(8,128)(2,1)S(1)}, bf16[256,2048]{1,0:T(8,128)(2,1)S(1)}, u32[]{:S(2)}, u32[]{:S(2)}) collective-permute-start(bf16[256,2048]{1,0:T(8,128)(2,1)S(1)} %get-tuple-element.465.refs_2_), channel_id=1, source_target_pairs={{1,2},{2,1},{5,6},{6,5},{9,10},{10,9},{13,14},{14,13},{17,18},{18,... | collective-permute-start | bytes 3145736 | tf_op jit(solution)/shard_map/ppermute | solution.py:583
  181.7 23.3 %collective-permute-start.12 = (bf16[256,2048]{1,0:T(8,128)(2,1)S(1)}, bf16[256,2048]{1,0:T(8,128)(2,1)S(1)}, u32[]{:S(2)}, u32[]{:S(2)}) collective-permute-start(bf16[256,2048]{1,0:T(8,128)(2,1)S(1)} %get-tuple-element.481.refs_4_), channel_id=1, source_target_pairs={{0,1},{3,2},{1,0},{2,3},{4,5},{7,6},{5,4},{6,7},{8,9},{11,10},{9,8... | collective-permute-start | bytes 3145736 | tf_op jit(solution)/shard_map/ppermute | solution.py:580
  184.7 20.3 %collective-permute-start.13 = (bf16[256,2048]{1,0:T(8,128)(2,1)S(1)}, bf16[256,2048]{1,0:T(8,128)(2,1)S(1)}, u32[]{:S(2)}, u32[]{:S(2)}) collective-permute-start(bf16[256,2048]{1,0:T(8,128)(2,1)S(1)} %get-tuple-element.482.refs_2_), channel_id=1, source_target_pairs={{1,2},{2,1},{5,6},{6,5},{9,10},{10,9},{13,14},{14,13},{17,18},{18,... | collective-permute-start | bytes 3145736 | tf_op jit(solution)/shard_map/ppermute | solution.py:583
  205.2 23.1 %collective-permute-start.14 = (bf16[256,2048]{1,0:T(8,128)(2,1)S(1)}, bf16[256,2048]{1,0:T(8,128)(2,1)S(1)}, u32[]{:S(2)}, u32[]{:S(2)}) collective-permute-start(bf16[256,2048]{1,0:T(8,128)(2,1)S(1)} %get-tuple-element.508.refs_4_), channel_id=1, source_target_pairs={{0,1},{3,2},{1,0},{2,3},{4,5},{7,6},{5,4},{6,7},{8,9},{11,10},{9,8... | collective-permute-start | bytes 3145736 | tf_op jit(solution)/shard_map/ppermute | solution.py:580
  208.0 20.3 %collective-permute-start.15 = (bf16[256,2048]{1,0:T(8,128)(2,1)S(1)}, bf16[256,2048]{1,0:T(8,128)(2,1)S(1)}, u32[]{:S(2)}, u32[]{:S(2)}) collective-permute-start(bf16[256,2048]{1,0:T(8,128)(2,1)S(1)} %get-tuple-element.509.refs_2_), channel_id=1, source_target_pairs={{1,2},{2,1},{5,6},{6,5},{9,10},{10,9},{13,14},{14,13},{17,18},{18,... | collective-permute-start | bytes 3145736 | tf_op jit(solution)/shard_map/ppermute | solution.py:583
  229.9 24.8 %collective-permute-start.16 = (bf16[256,2048]{1,0:T(8,128)(2,1)}, bf16[256,2048]{1,0:T(8,128)(2,1)}, u32[]{:S(2)}, u32[]{:S(2)}) collective-permute-start(bf16[256,2048]{1,0:T(8,128)(2,1)} %get-tuple-element.537.refs_4_), channel_id=1, source_target_pairs={{0,1},{3,2},{1,0},{2,3},{4,5},{7,6},{5,4},{6,7},{8,9},{11,10},{9,8... | collective-permute-start | bytes 3145736 | tf_op jit(solution)/shard_map/ppermute | solution.py:580
  231.8 22.8 %collective-permute-start.17 = (bf16[256,2048]{1,0:T(8,128)(2,1)}, bf16[256,2048]{1,0:T(8,128)(2,1)}, u32[]{:S(2)}, u32[]{:S(2)}) collective-permute-start(bf16[256,2048]{1,0:T(8,128)(2,1)} %get-tuple-element.538.refs_2_), channel_id=1, source_target_pairs={{1,2},{2,1},{5,6},{6,5},{9,10},{10,9},{13,14},{14,13},{17,18},{18,... | collective-permute-start | bytes 3145736 | tf_op jit(solution)/shard_map/ppermute | solution.py:583
  242.6 12.0 %copy-start.3 = (bf16[256,2048]{1,0:T(8,128)(2,1)S(1)}, bf16[256,2048]{1,0:T(8,128)(2,1)}, u32[]{:S(2)}) copy-start(bf16[256,2048]{1,0:T(8,128)(2,1)} %get-tuple-element.539.refs_5_.refs_0_) | copy-start | bytes 3145732
  259.0 23.1 %copy-start.2 = (bf16[256,2048]{1,0:T(8,128)(2,1)S(1)}, bf16[256,2048]{1,0:T(8,128)(2,1)}, u32[]{:S(2)}) copy-start(bf16[256,2048]{1,0:T(8,128)(2,1)} %get-tuple-element.571.refs_5_.refs_0_) | copy-start | bytes 3145732
  259.0 192.1 %reduce-scatter.6.cloned.1.call-start = ((), (), s32[]{:S(2)}) async-start(), calls=%async_computation.4 | async-start | bytes 12976128 | tf_op jit(solution)/shard_map/reduce_scatter | solution.py:910
  259.0 23.0 %collective-permute-start.18 = (bf16[256,2048]{1,0:T(8,128)(2,1)}, bf16[256,2048]{1,0:T(8,128)(2,1)}, u32[]{:S(2)}, u32[]{:S(2)}) collective-permute-start(bf16[256,2048]{1,0:T(8,128)(2,1)} %copy-done.16), channel_id=1, source_target_pairs={{0,1},{3,2},{1,0},{2,3},{4,5},{7,6},{5,4},{6,7},{8,9},{11,10},{9,8... | collective-permute-start | bytes 3145736 | tf_op jit(solution)/shard_map/ppermute | solution.py:580
  260.9 21.2 %collective-permute-start.19 = (bf16[256,2048]{1,0:T(8,128)(2,1)}, bf16[256,2048]{1,0:T(8,128)(2,1)}, u32[]{:S(2)}, u32[]{:S(2)}) collective-permute-start(bf16[256,2048]{1,0:T(8,128)(2,1)} %copy-done.14), channel_id=1, source_target_pairs={{1,2},{2,1},{5,6},{6,5},{9,10},{10,9},{13,14},{14,13},{17,18},{18,... | collective-permute-start | bytes 3145736 | tf_op jit(solution)/shard_map/ppermute | solution.py:583
  286.5 20.6 %collective-permute-start.20 = (bf16[256,2048]{1,0:T(8,128)(2,1)S(1)}, bf16[256,2048]{1,0:T(8,128)(2,1)S(1)}, u32[]{:S(2)}, u32[]{:S(2)}) collective-permute-start(bf16[256,2048]{1,0:T(8,128)(2,1)S(1)} %get-tuple-element.596.refs_4_), channel_id=1, source_target_pairs={{0,1},{3,2},{1,0},{2,3},{4,5},{7,6},{5,4},{6,7},{8,9},{11,10},{9,8... | collective-permute-start | bytes 3145736 | tf_op jit(solution)/shard_map/ppermute | solution.py:580
  288.7 18.4 %collective-permute-start.21 = (bf16[256,2048]{1,0:T(8,128)(2,1)S(1)}, bf16[256,2048]{1,0:T(8,128)(2,1)S(1)}, u32[]{:S(2)}, u32[]{:S(2)}) collective-permute-start(bf16[256,2048]{1,0:T(8,128)(2,1)S(1)} %get-tuple-element.597.refs_2_), channel_id=1, source_target_pairs={{1,2},{2,1},{5,6},{6,5},{9,10},{10,9},{13,14},{14,13},{17,18},{18,... | collective-permute-start | bytes 3145736 | tf_op jit(solution)/shard_map/ppermute | solution.py:583
  298.3 8.8 %copy-start.1 = (bf16[256,2048]{1,0:T(8,128)(2,1)S(1)}, bf16[256,2048]{1,0:T(8,128)(2,1)}, u32[]{:S(2)}) copy-start(bf16[256,2048]{1,0:T(8,128)(2,1)} %get-tuple-element.598.refs_5_.refs_0_) | copy-start | bytes 3145732
  307.3 20.6 %collective-permute-start.22 = (bf16[256,2048]{1,0:T(8,128)(2,1)S(1)}, bf16[256,2048]{1,0:T(8,128)(2,1)S(1)}, u32[]{:S(2)}, u32[]{:S(2)}) collective-permute-start(bf16[256,2048]{1,0:T(8,128)(2,1)S(1)} %get-tuple-element.618.refs_4_), channel_id=1, source_target_pairs={{0,1},{3,2},{1,0},{2,3},{4,5},{7,6},{5,4},{6,7},{8,9},{11,10},{9,8... | collective-permute-start | bytes 3145736 | tf_op jit(solution)/shard_map/ppermute | solution.py:580
  309.5 18.4 %collective-permute-start.23 = (bf16[256,2048]{1,0:T(8,128)(2,1)S(1)}, bf16[256,2048]{1,0:T(8,128)(2,1)S(1)}, u32[]{:S(2)}, u32[]{:S(2)}) collective-permute-start(bf16[256,2048]{1,0:T(8,128)(2,1)S(1)} %get-tuple-element.619.refs_2_), channel_id=1, source_target_pairs={{1,2},{2,1},{5,6},{6,5},{9,10},{10,9},{13,14},{14,13},{17,18},{18,... | collective-permute-start | bytes 3145736 | tf_op jit(solution)/shard_map/ppermute | solution.py:583
  310.2 17.7 %copy-start = (bf16[256,2048]{1,0:T(8,128)(2,1)S(1)}, bf16[256,2048]{1,0:T(8,128)(2,1)}, u32[]{:S(2)}) copy-start(bf16[256,2048]{1,0:T(8,128)(2,1)} %get-tuple-element.617.refs_5_.refs_0_) | copy-start | bytes 3145732
  319.1 14.6 %collective-permute-start.26 = (bf16[2,64,1152]{2,1,0:T(8,128)(2,1)S(1)}, bf16[2,64,1152]{2,1,0:T(8,128)(2,1)S(1)}, u32[]{:S(2)}, u32[]{:S(2)}) collective-permute-start(bf16[2,64,1152]{2,1,0:T(8,128)(2,1)S(1)} %get-tuple-element.641), channel_id=1, source_target_pairs={{0,4},{4,0},{8,12},{12,8},{16,20},{20,16},{24,28},{28,24},{1,5},{5... | collective-permute-start | bytes 884744 | tf_op jit(solution)/shard_map/ppermute | solution.py:498
  329.0 33.5 %collective-permute-start.24 = (bf16[256,2048]{1,0:T(8,128)(2,1)S(1)}, bf16[256,2048]{1,0:T(8,128)(2,1)S(1)}, u32[]{:S(2)}, u32[]{:S(2)}) collective-permute-start(bf16[256,2048]{1,0:T(8,128)(2,1)S(1)} %get-tuple-element.628.refs_4_), channel_id=1, source_target_pairs={{0,1},{3,2},{1,0},{2,3},{4,5},{7,6},{5,4},{6,7},{8,9},{11,10},{9,8... | collective-permute-start | bytes 3145736 | tf_op jit(solution)/shard_map/ppermute | solution.py:580
  332.8 29.7 %collective-permute-start.25 = (bf16[256,2048]{1,0:T(8,128)(2,1)S(1)}, bf16[256,2048]{1,0:T(8,128)(2,1)S(1)}, u32[]{:S(2)}, u32[]{:S(2)}) collective-permute-start(bf16[256,2048]{1,0:T(8,128)(2,1)S(1)} %get-tuple-element.629.refs_2_), channel_id=1, source_target_pairs={{1,2},{2,1},{5,6},{6,5},{9,10},{10,9},{13,14},{14,13},{17,18},{18,... | collective-permute-start | bytes 3145736 | tf_op jit(solution)/shard_map/ppermute | solution.py:583
  334.0 6.8 %collective-permute-start.27 = (bf16[2,64,1152]{2,1,0:T(8,128)(2,1)S(1)}, bf16[2,64,1152]{2,1,0:T(8,128)(2,1)S(1)}, u32[]{:S(2)}, u32[]{:S(2)}) collective-permute-start(bf16[2,64,1152]{2,1,0:T(8,128)(2,1)S(1)} %get-tuple-element.644), channel_id=1, source_target_pairs={{0,8},{4,12},{8,0},{12,4},{16,24},{20,28},{24,16},{28,20},{1,9},{5... | collective-permute-start | bytes 884744 | tf_op jit(solution)/shard_map/ppermute | solution.py:498
  341.1 12.9 %collective-permute-start.28 = (bf16[2,64,1152]{2,1,0:T(8,128)(2,1)S(1)}, bf16[2,64,1152]{2,1,0:T(8,128)(2,1)S(1)}, u32[]{:S(2)}, u32[]{:S(2)}) collective-permute-start(bf16[2,64,1152]{2,1,0:T(8,128)(2,1)S(1)} %get-tuple-element.663), channel_id=1, source_target_pairs={{0,16},{4,20},{8,24},{12,28},{16,0},{20,4},{24,8},{28,12},{1,17},{... | collective-permute-start | bytes 884744 | tf_op jit(solution)/shard_map/ppermute | solution.py:498
  365.1 170.5 %reduce-scatter.8.cloned.1.call-start = ((), (), s32[]{:S(2)}) async-start(), calls=%async_computation.5 | async-start | bytes 10653696 | tf_op jit(solution)/shard_map/reduce_scatter | solution.py:932
  365.2 32.1 %collective-permute-start.29 = (bf16[256,2048]{1,0:T(8,128)(2,1)}, bf16[256,2048]{1,0:T(8,128)(2,1)S(1)}, u32[]{:S(2)}, u32[]{:S(2)}) collective-permute-start(bf16[256,2048]{1,0:T(8,128)(2,1)} %get-tuple-element.689.refs_4_), channel_id=1, source_target_pairs={{0,1},{3,2},{1,0},{2,3},{4,5},{7,6},{5,4},{6,7},{8,9},{11,10},{9,8... | collective-permute-start | bytes 3145736 | tf_op jit(solution)/shard_map/ppermute | solution.py:580
  367.5 29.7 %collective-permute-start.30 = (bf16[256,2048]{1,0:T(8,128)(2,1)}, bf16[256,2048]{1,0:T(8,128)(2,1)S(1)}, u32[]{:S(2)}, u32[]{:S(2)}) collective-permute-start(bf16[256,2048]{1,0:T(8,128)(2,1)} %get-tuple-element.690.refs_2_), channel_id=1, source_target_pairs={{1,2},{2,1},{5,6},{6,5},{9,10},{10,9},{13,14},{14,13},{17,18},{18,... | collective-permute-start | bytes 3145736 | tf_op jit(solution)/shard_map/ppermute | solution.py:583
  388.1 9.2 %copy-start.5 = (bf16[256,2048]{1,0:T(8,128)(2,1)S(1)}, bf16[256,2048]{1,0:T(8,128)(2,1)}, u32[]{:S(2)}) copy-start(bf16[256,2048]{1,0:T(8,128)(2,1)} %copy-done.4) | copy-start | bytes 3145732
  397.3 3.4 copy-start.6
  401.7 18.0 %collective-permute-start.31 = (bf16[256,2048]{1,0:T(8,128)(2,1)}, bf16[256,2048]{1,0:T(8,128)(2,1)}, u32[]{:S(2)}, u32[]{:S(2)}) collective-permute-start(bf16[256,2048]{1,0:T(8,128)(2,1)} %get-tuple-element.713.refs_4_), channel_id=1, source_target_pairs={{0,1},{3,2},{1,0},{2,3},{4,5},{7,6},{5,4},{6,7},{8,9},{11,10},{9,8... | collective-permute-start | bytes 3145736 | tf_op jit(solution)/shard_map/ppermute | solution.py:580
  404.3 15.4 %collective-permute-start.32 = (bf16[256,2048]{1,0:T(8,128)(2,1)}, bf16[256,2048]{1,0:T(8,128)(2,1)}, u32[]{:S(2)}, u32[]{:S(2)}) collective-permute-start(bf16[256,2048]{1,0:T(8,128)(2,1)} %get-tuple-element.714.refs_2_), channel_id=1, source_target_pairs={{1,2},{2,1},{5,6},{6,5},{9,10},{10,9},{13,14},{14,13},{17,18},{18,... | collective-permute-start | bytes 3145736 | tf_op jit(solution)/shard_map/ppermute | solution.py:583
  405.9 13.8 %copy-start.7 = (bf16[256,2048]{1,0:T(8,128)(2,1)S(1)}, bf16[256,2048]{1,0:T(8,128)(2,1)}, u32[]{:S(2)}) copy-start(bf16[256,2048]{1,0:T(8,128)(2,1)} %copy-done.6) | copy-start | bytes 3145732
  425.0 5.0 copy-start.9
  425.0 7.5 %copy-start.23 = (bf16[256,2048]{1,0:T(8,128)(2,1)S(1)}, bf16[256,2048]{1,0:T(8,128)(2,1)}, u32[]{:S(2)}) copy-start(bf16[256,2048]{1,0:T(8,128)(2,1)} %copy-done.22) | copy-start | bytes 3145732
  425.0 17.1 %collective-permute-start.33 = (bf16[256,2048]{1,0:T(8,128)(2,1)}, bf16[256,2048]{1,0:T(8,128)(2,1)S(1)}, u32[]{:S(2)}, u32[]{:S(2)}) collective-permute-start(bf16[256,2048]{1,0:T(8,128)(2,1)} %copy-done.20), channel_id=1, source_target_pairs={{0,1},{3,2},{1,0},{2,3},{4,5},{7,6},{5,4},{6,7},{8,9},{11,10},{9,8... | collective-permute-start | bytes 3145736 | tf_op jit(solution)/shard_map/ppermute | solution.py:580
  429.1 13.0 %collective-permute-start.34 = (bf16[256,2048]{1,0:T(8,128)(2,1)}, bf16[256,2048]{1,0:T(8,128)(2,1)S(1)}, u32[]{:S(2)}, u32[]{:S(2)}) collective-permute-start(bf16[256,2048]{1,0:T(8,128)(2,1)} %copy-done.18), channel_id=1, source_target_pairs={{1,2},{2,1},{5,6},{6,5},{9,10},{10,9},{13,14},{14,13},{17,18},{18,... | collective-permute-start | bytes 3145736 | tf_op jit(solution)/shard_map/ppermute | solution.py:583
  432.5 9.6 %copy-start.19 = (bf16[256,2048]{1,0:T(8,128)(2,1)S(1)}, bf16[256,2048]{1,0:T(8,128)(2,1)}, u32[]{:S(2)}) copy-start(bf16[256,2048]{1,0:T(8,128)(2,1)} %copy-done.18) | copy-start | bytes 3145732
  432.5 9.6 %copy-start.21 = (bf16[256,2048]{1,0:T(8,128)(2,1)S(1)}, bf16[256,2048]{1,0:T(8,128)(2,1)}, u32[]{:S(2)}) copy-start(bf16[256,2048]{1,0:T(8,128)(2,1)} %copy-done.20) | copy-start | bytes 3145732
  451.1 25.1 %collective-permute-start.35 = (bf16[256,2048]{1,0:T(8,128)(2,1)}, bf16[256,2048]{1,0:T(8,128)(2,1)S(1)}, u32[]{:S(2)}, u32[]{:S(2)}) collective-permute-start(bf16[256,2048]{1,0:T(8,128)(2,1)} %copy-done.10), channel_id=1, source_target_pairs={{0,1},{3,2},{1,0},{2,3},{4,5},{7,6},{5,4},{6,7},{8,9},{11,10},{9,8... | collective-permute-start | bytes 3145736 | tf_op jit(solution)/shard_map/ppermute | solution.py:580
  452.6 23.6 %collective-permute-start.36 = (bf16[256,2048]{1,0:T(8,128)(2,1)S(1)}, bf16[256,2048]{1,0:T(8,128)(2,1)S(1)}, u32[]{:S(2)}, u32[]{:S(2)}) collective-permute-start(bf16[256,2048]{1,0:T(8,128)(2,1)S(1)} %get-tuple-element.770.refs_2_), channel_id=1, source_target_pairs={{1,2},{2,1},{5,6},{6,5},{9,10},{10,9},{13,14},{14,13},{17,18},{18,... | collective-permute-start | bytes 3145736 | tf_op jit(solution)/shard_map/ppermute | solution.py:583
  454.5 3.4 copy-start.25
  457.9 2.5 copy-start.27
  460.4 15.8 %copy-start.11 = (bf16[256,2048]{1,0:T(8,128)(2,1)S(1)}, bf16[256,2048]{1,0:T(8,128)(2,1)}, u32[]{:S(2)}) copy-start(bf16[256,2048]{1,0:T(8,128)(2,1)} %copy-done.10) | copy-start | bytes 3145732
  463.0 15.3 %copy-start.32 = (bf16[1,2,256,1408]{3,2,1,0:T(8,128)(2,1)S(1)}, bf16[1,2,256,1408]{3,2,1,0:T(8,128)(2,1)}, u32[]{:S(2)}) copy-start(bf16[1,2,256,1408]{3,2,1,0:T(8,128)(2,1)} %reduce-scatter.6.cloned.1.call-done) | copy-start | bytes 4325380
  476.3 27.9 %collective-permute-start.37 = (bf16[256,2048]{1,0:T(8,128)(2,1)S(1)}, bf16[256,2048]{1,0:T(8,128)(2,1)S(1)}, u32[]{:S(2)}, u32[]{:S(2)}) collective-permute-start(bf16[256,2048]{1,0:T(8,128)(2,1)S(1)} %get-tuple-element.781.refs_3_), channel_id=1, source_target_pairs={{1,0},{2,3},{5,4},{6,7},{9,8},{10,11},{13,12},{14,15},{17,16},{18,... | collective-permute-start | bytes 3145736 | tf_op jit(solution)/shard_map/ppermute | solution.py:580
  477.6 26.6 %collective-permute-start.38 = (bf16[256,2048]{1,0:T(8,128)(2,1)S(1)}, bf16[256,2048]{1,0:T(8,128)(2,1)S(1)}, u32[]{:S(2)}, u32[]{:S(2)}) collective-permute-start(bf16[256,2048]{1,0:T(8,128)(2,1)S(1)} %get-tuple-element.782.refs_1_), channel_id=1, source_target_pairs={{1,2},{2,1},{5,6},{6,5},{9,10},{10,9},{13,14},{14,13},{17,18},{18,... | collective-permute-start | bytes 3145736 | tf_op jit(solution)/shard_map/ppermute | solution.py:583
  535.7 35.4 %collective-permute-start.39 = (bf16[256,2048]{1,0:T(8,128)(2,1)S(1)}, bf16[256,2048]{1,0:T(8,128)(2,1)S(1)}, u32[]{:S(2)}, u32[]{:S(2)}) collective-permute-start(bf16[256,2048]{1,0:T(8,128)(2,1)S(1)} %get-tuple-element.792.refs_1_), channel_id=1, source_target_pairs={{1,0},{2,3},{5,4},{6,7},{9,8},{10,11},{13,12},{14,15},{17,16},{18,... | collective-permute-start | bytes 3145736 | tf_op jit(solution)/shard_map/ppermute | solution.py:580
  542.2 5.0 copy-start.31
  544.5 18.1 %collective-permute-start.40 = (f32[256]{0:T(256)S(1)}, f32[256]{0:T(256)S(1)}, u32[]{:S(2)}, u32[]{:S(2)}) collective-permute-start(f32[256]{0:T(256)S(1)} %get-tuple-element.839), channel_id=1, source_target_pairs={{0,1},{1,0},{2,3},{3,2},{4,5},{5,4},{6,7},{7,6},{8,9},{9,8},{10,11... | collective-permute-start | bytes 3080 | tf_op jit(solution)/shard_map/ppermute | solution.py:954
  562.5 7.9 %collective-permute-start.41 = (f32[256]{0:T(256)S(1)}, f32[256]{0:T(256)S(1)}, u32[]{:S(2)}, u32[]{:S(2)}) collective-permute-start(f32[256]{0:T(256)S(1)} %add.18), channel_id=1, source_target_pairs={{0,2},{1,3},{2,0},{3,1},{4,6},{5,7},{6,4},{7,5},{8,10},{9,11},{10,... | collective-permute-start | bytes 3080 | tf_op jit(solution)/shard_map/ppermute | solution.py:954
  (16 other events, 17.6 us)
Sparse Core Ops, SparseCore 0:
  31.5 99.9 all-gather.2
  259.1 59.6 reduce-scatter.3
  365.3 85.7 reduce-scatter.5
  454.9 80.7 reduce-scatter.7

commit v6 on v5

--- a/solution.py
+++ b/solution.py
@@ -108,8 +108,8 @@
     return both[:, :width] + both[:, width:]
 
 
-def project_kernel(per_part, x_ref, gain_ref, wq_ref, wk_ref, wv_ref, wf_ref, bias_ref,
-                   xn_ref, q_ref, k_ref, v_ref, z_ref, cum_ref, in_ref, s_ref, d_ref, sent_ref, state, decay):
+def project_kernel(per_part, x_ref, gain_ref, wk_ref, wv_ref, wf_ref, bias_ref,
+                   xn_ref, k_ref, v_ref, z_ref, cum_ref, in_ref, s_ref, d_ref, sent_ref, state, decay):
     @pl.when(lax.rem(pl.program_id(0), per_part) == 0)
     def _():
         state[...] = jnp.zeros_like(state)
@@ -119,10 +119,9 @@
     r1 = lax.rsqrt(jnp.mean(x * x, axis=-1, keepdims=True) + EPS)
     xn = (x * r1 * gain_ref[...]).astype(bf16)
     xn_ref[...] = xn
-    q_ref[...] = nn(xn, wq_ref[...]).astype(bf16)
     k_ref[...] = nn(xn, wk_ref[...]).astype(bf16)
     v_ref[...] = nn(xn, wv_ref[...]).astype(bf16)
-    z_ref[...] = nn(xn, wf_ref[...]) + bias_ref[...]
+    z_ref[...] = nt(xn, wf_ref[...]) + bias_ref[...]
     width = k_ref.shape[1]
     for c in range(x_ref.shape[0] // CHUNK):
         rows = pl.ds(c * CHUNK, CHUNK)
@@ -138,6 +137,10 @@
     s_ref[0] = state[...]
     d_ref[0] = jnp.exp(decay[...])
     pack(sent_ref, 0, jnp.exp(decay[...]), state[...])
+
+
+def query_kernel(xn_ref, wq_ref, q_ref):
+    q_ref[...] = nn(xn_ref[...], wq_ref[...]).astype(bf16)
 
 
 def read_kernel(q_ref, k_ref, v_ref, cum_ref, in_ref, e0_ref, wo_ref, o_ref, p_ref, sc_ref, e_ref, left_ref, att_ref, state):
@@ -172,7 +175,7 @@
 
 
 def back_kernel(dhn_ref, hid_ref, cot_ref, gain_ref, wo_ref, q_ref, k_ref, v_ref, cum_ref, in_ref, p_ref, sc_ref,
-                e_ref, dhid_ref, datt_ref, dq_ref, dkl_ref, dvl_ref, h_ref, x1_ref, g_ref, s_ref, d_ref, gg_ref, state, decay):
+                e_ref, datt_ref, dq_ref, dkl_ref, dvl_ref, h_ref, x1_ref, g_ref, s_ref, d_ref, gg_ref, state, decay):
     step = pl.program_id(0)
 
     @pl.when(step == 0)
@@ -181,7 +184,7 @@
         decay[...] = jnp.zeros_like(decay)
         gg_ref[...] = jnp.zeros_like(gg_ref)
 
-    hidden = hid_ref[...]
+    hidden = hid_ref[...].astype(f32)
     dhn = dhn_ref[...].astype(f32)
     r2 = lax.rsqrt(jnp.mean(hidden * hidden, axis=-1, keepdims=True) + EPS)
     gg_ref[...] += jnp.sum((dhn * hidden * r2).reshape(-1, 8, hidden.shape[1]), axis=0)
@@ -191,7 +194,6 @@
         + r2 * u2
         - hidden * (r2 * r2 * r2) * jnp.mean(u2 * hidden, axis=-1, keepdims=True)
     )
-    dhid_ref[...] = dhid
     datt = dhid.astype(bf16)
     datt_ref[...] = datt
     width = q_ref.shape[1]
@@ -276,7 +278,7 @@
     def _():
         for load in loads:
             load.wait()
-        dxn = nt(dq_ref[...], wq[...]) + nt(dk_ref[...], wk[...]) + nt(dv_ref[...], wv[...]) + nt(dz_ref[...], wf[...])
+        dxn = nt(dq_ref[...], wq[...]) + nt(dk_ref[...], wk[...]) + nt(dv_ref[...], wv[...]) + nn(dz_ref[...], wf[...])
         dxn_ref[...] = dxn.astype(bf16)
         x = x_ref[...].astype(f32)
         r1 = lax.rsqrt(jnp.mean(x * x, axis=-1, keepdims=True) + EPS)
@@ -284,14 +286,14 @@
 
 
 def out_kernel(hid_ref, ffn_ref, *refs):
-    refs[-1][0] = (hid_ref[...] + ffn_ref[...].astype(f32)).astype(bf16)
+    refs[-1][0] = (hid_ref[...].astype(f32) + ffn_ref[...].astype(f32)).astype(bf16)
 
 
 def in_grad_kernel(dhid_ref, dxn_ref, x_ref, gain_ref, *refs):
     x = x_ref[...].astype(f32)
     r1 = lax.rsqrt(jnp.mean(x * x, axis=-1, keepdims=True) + EPS)
     u1 = gain_ref[...] * dxn_ref[...].astype(f32)
-    refs[-1][0] = dhid_ref[...] + r1 * u1 - x * (r1 * r1 * r1) * jnp.mean(u1 * x, axis=-1, keepdims=True)
+    refs[-1][0] = dhid_ref[...].astype(f32) + r1 * u1 - x * (r1 * r1 * r1) * jnp.mean(u1 * x, axis=-1, keepdims=True)
 
 
 def feed_kernel(first_row, x_ref, att_ref, gain_ref, cot_ref, full_ref, hid_ref, hn_ref, act_ref, dg_ref, du_ref,
@@ -313,7 +315,7 @@
     for copy in reads:
         copy.wait()
     hidden = x[...].astype(f32) + att_ref[...].astype(f32)
-    hid[...] = hidden
+    hid[...] = hidden.astype(bf16)
     r2 = lax.rsqrt(jnp.mean(hidden * hidden, axis=-1, keepdims=True) + EPS)
     hn[...] = (hidden * r2 * gain_ref[...]).astype(bf16)
     writes[0].start()
@@ -501,7 +503,7 @@
         if final:
             shapes = [shaped((parts * pieces, slots, width), f32)]
         if final and last_tie is not None:
-            state = behind_of(state, last_tie)
+            state = behind_of(state, *last_tie)
         results = in_vmem(
             "hop",
             functools.partial(hop_kernel, bit, after, not part, final, parts, pieces),
@@ -628,20 +630,30 @@
 
     all_rows = lambda c: pl.BlockSpec((TILE, c), lambda i: (i, 0))
     by_part = lambda c: pl.BlockSpec((1, slots, c), lambda i: (i // per_part, 0, 0))
-    xn, q, k, v, z, cum, inflow, local, decay, sent = call(
+    forget_rows = w_forget.T
+    xn, k, v, z, cum, inflow, local, decay, sent = call(
         "project",
         functools.partial(project_kernel, per_part),
         (rows // TILE,),
-        [all_rows(width), fixed((1, width))] + [fixed((width, head))] * 3 + [fixed((width, slots)), fixed((1, slots))],
-        [all_rows(width), all_rows(head), all_rows(head), all_rows(head)] + [all_rows(slots)] * 3
+        [all_rows(width), fixed((1, width))] + [fixed((width, head))] * 2 + [fixed((slots, width)), fixed((1, slots))],
+        [all_rows(width), all_rows(head), all_rows(head)] + [all_rows(slots)] * 3
         + [by_part(2 * head), by_part(128), by_part(2 * head + 128)],
-        [shaped((rows, width), bf16)] + [shaped((rows, head), bf16)] * 3
+        [shaped((rows, width), bf16)] + [shaped((rows, head), bf16)] * 2
         + [shaped((rows, slots), f32)] * 3 + [shaped((parts, slots, 2 * head), f32), shaped((parts, slots, 128), f32),
                                              shaped((parts, slots, 2 * head + 128), bf16)],
         [state_scratch, decay_scratch],
-        cost=cost(2 * rows * width * (3 * head + slots), 2 * rows * width * 3 + 2 * width * 3 * head),
-        loose_out=(7, 8, 9),
-    )(x, gain1, w_query, w_key, w_value, w_forget, forget_bias.reshape(1, slots))
+        cost=cost(2 * rows * width * (2 * head + slots), 2 * rows * width * 3 + 2 * width * 2 * head),
+        loose_out=(6, 7, 8),
+    )(x, gain1, w_key, w_value, forget_rows, forget_bias.reshape(1, slots))
+    q = call(
+        "query",
+        query_kernel,
+        (rows // TILE,),
+        [all_rows(width), fixed((width, head))],
+        all_rows(head),
+        shaped((rows, head), bf16),
+        cost=cost(2 * rows * width * head, 2 * rows * (width + head) + 2 * width * head),
+    )(xn, w_query)
     stacked = []
 
     def stack_weights(sent):
@@ -696,10 +708,10 @@
             (),
             [anywhere, in_place, in_place, anywhere, anywhere],
             [anywhere] * 6 + [in_place],
-            [shaped((TILE, width), f32), shaped((TILE, width), bf16)] + [shaped((TILE, units), bf16)] * 3
+            [shaped((TILE, width), bf16)] * 2 + [shaped((TILE, units), bf16)] * 3
             + [shaped((TILE, width), bf16)] * 2,
             [vmem((n_seq, 3, span, units), bf16), vmem((TILE, width), bf16), vmem((TILE, width), bf16),
-             vmem((TILE, width), f32), vmem((TILE, width), bf16)] + [vmem((TILE, units), bf16)] * 3
+             vmem((TILE, width), bf16), vmem((TILE, width), bf16)] + [vmem((TILE, units), bf16)] * 3
             + [vmem((TILE, width), bf16), pltpu.SemaphoreType.DMA((2,)), pltpu.SemaphoreType.DMA((6,)),
                pltpu.SemaphoreType.DMA((tile_count,))],
             cost=cost(12 * TILE * width * units, 6 * width * units + TILE * width * 14),
@@ -714,9 +726,9 @@
         return call(
             "down_grads",
             down_grad_kernel,
-            (width // columns,),
-            [pl.BlockSpec((rows, columns), lambda j: (0, j))] + [fixed((TILE, units))] * len(acts),
-            pl.BlockSpec((group, span, units), lambda j: (j, 0, 0)),
+            (width // columns // 2,),
+            [pl.BlockSpec((rows, 2 * columns), lambda j: (0, j))] + [fixed((TILE, units))] * len(acts),
+            pl.BlockSpec((2 * group, span, units), lambda j: (j, 0, 0)),
             shaped((n_seq, span, units), bf16),
             cost=cost(2 * rows * width * units, 2 * (rows * width + rows * units + width * units)),
         )(cot, *acts)
@@ -744,16 +756,16 @@
              fixed((head, width))]
             + [chunk_rows(m, t, head, True)] * 3 + [chunk_rows(m, t, slots, True)] * 2 + [own_rows(slots, True)] * 2
             + [chunk_state(True)],
-            [own_rows(width, True)] * 2 + [own_rows(head, True)] * 3 + [own_rows(slots, True)] * 2
+            [own_rows(width, True)] + [own_rows(head, True)] * 3 + [own_rows(slots, True)] * 2
             + [chunk_state(True), whole((slots, 2 * head)), whole((slots, 128)), whole((8, width))],
-            [shaped((TILE, width), f32), shaped((TILE, width), bf16), shaped((TILE, head), bf16),
+            [shaped((TILE, width), bf16), shaped((TILE, head), bf16),
              shaped((TILE, head), f32), shaped((TILE, head), f32), shaped((TILE, slots), f32),
              shaped((TILE, slots), f32), states_shape, shaped((slots, 2 * head), f32), shaped((slots, 128), f32),
              shaped((8, width), f32)],
             [state_scratch, decay_scratch],
             cost=cost(2 * TILE * width * head + 2 * TILE * head * 1500, TILE * width * 14 + TILE * head * 20),
             loose=(0,),
-            loose_out=(8, 9),
+            loose_out=(7, 8),
         )(dhn, hidden, cot, gain2, w_out, q, k, v, cum, inflow, p, scores, e_chunks)
 
     def last(m, t, leaving, saved):
@@ -772,12 +784,12 @@
             [shaped((TILE, head), bf16), shaped((TILE, head), bf16), shaped((TILE, slots), bf16),
              shaped((TILE, width), bf16), shaped((8, slots), f32), shaped((8, width), f32)],
             [state_scratch] + [pltpu.VMEM((width, head), bf16)] * 3
-            + [pltpu.VMEM((width, slots), bf16), pltpu.SemaphoreType.DMA((4,))],
+            + [pltpu.VMEM((slots, width), bf16), pltpu.SemaphoreType.DMA((4,))],
             cost=cost(2 * TILE * width * (3 * head + slots), TILE * width * 8 + TILE * head * 20 + width * head * 6),
             loose=(0,),
             loose_out=(3,),
         )(leaving, k, v, z, cum, inflow, reads[m, t][3], g_chunks, dk_local, dv_local, h_sum, x_local, dq, x,
-          w_query, w_key, w_value, w_forget)
+          w_query, w_key, w_value, forget_rows)
 
     line = Line()
     live = {}
@@ -836,10 +848,10 @@
 
     def go_back(m, t):
         backs[m, t] = back(m, t, live.pop(("dhn", m, t)), live["hidden", m, t])
-        live["back", m, t] = backs[m, t][8]
+        live["back", m, t] = backs[m, t][7]
 
     def go_last(m, t):
-        lasts[m, t] = last(m, t, live["leaving"], backs[m, t][2:8])
+        lasts[m, t] = last(m, t, live["leaving"], backs[m, t][1:7])
         live["dxn_part", m, t] = lasts[m, t][3]
 
     def taken(name):
@@ -863,22 +875,22 @@
     start()
     end(go_feed(1, 1), ("dhn", 0, 0))
     start()
+    live["wide_grads"] = wide_grads(taken("hn"), taken("dgate"), taken("dup"))
+    end(live.pop(("ffn_part", 0, 0)), ("dhn", 0, 1))
+    start()
+    wide_shares = lax.psum_scatter(live.pop("wide_grads"), "seq", scatter_dimension=0)
+    go_back(0, 0)
     live["down_grads"] = down_grads(taken("act"))
-    go_back(0, 0)
-    end(live.pop(("ffn_part", 0, 0)), ("dhn", 0, 1))
+    end(live.pop(("ffn_part", 0, 1)), ("dhn", 1, 0))
     start()
     down_shares = lax.psum_scatter(live.pop("down_grads"), "seq", scatter_dimension=0)
-    live["wide_grads"] = wide_grads(taken("hn"), taken("dgate"), taken("dup"))
-    end(live.pop(("ffn_part", 0, 1)), ("dhn", 1, 0))
-    start()
-    wide = live.pop("wide_grads")
     go_back(0, 1)
     go_back(1, 0)
     end(live.pop(("ffn_part", 1, 0)), ("dhn", 1, 1))
     start()
     go_back(1, 1)
     taken("back")
-    own = [backs[key][8] for key in every] + [backs[key][9] for key in every]
+    own = [backs[key][7] for key in every] + [backs[key][8] for key in every]
     folded = in_vmem(
         "fold",
         functools.partial(fold_kernel, parts, pieces),
@@ -886,13 +898,19 @@
         [shaped(local.shape, f32), shaped(decay.shape, f32), shaped(sent.shape, bf16)],
     )
 
-    live["xn"] = xn
-    end(live.pop(("ffn_part", 1, 1)), ("ffn", 0, 0))
-    start()
     xn_columns = [pl.BlockSpec((rows, TILE), lambda j: (0, j))]
     piece_columns = [pl.BlockSpec((TILE, TILE), lambda j: (0, j))] * len(every)
     piece_whole = [fixed((TILE, head))] * len(every)
-    query_grads = call(
+    made = []
+
+    def next_step(sent):
+        live["xn"] = xn
+        end(behind_of(live.pop(("ffn_part", 1, 1)), sent), ("ffn", 0, 0))
+        start()
+        made.append(query_gradients(live.pop("xn")))
+        return sent
+
+    query_gradients = lambda xn: call(
         "query_grads",
         functools.partial(query_grad_kernel, len(every)),
         (width // TILE,),
@@ -900,14 +918,14 @@
         pl.BlockSpec((TILE, 2 * head), lambda j: (j, 0)),
         shaped((width, 2 * head), bf16),
         cost=cost(4 * rows * width * head, 4 * rows * width + 4 * rows * head + 4 * width * head),
-    )(live.pop("xn"), *[backs[key][1] for key in every], *[backs[key][2] for key in every],
+    )(xn, *[backs[key][0] for key in every], *[backs[key][1] for key in every],
       *[reads[key][0] for key in every])
-    live["leaving"] = scan_states(n_seq, *folded, True, own, pieces, last_tie=query_grads)
-    live["query_grads"], live["wide"] = query_grads, wide
+    live["leaving"] = scan_states(n_seq, *folded, True, own, pieces, next_step, made)
+    live["query_grads"], live["wide"] = made[0], wide_shares
     go_last(0, 0)
     end(live.pop(("dxn_part", 0, 0)), ("ffn", 0, 1))
     start()
-    wide_shares = lax.psum_scatter(live.pop("wide"), "seq", scatter_dimension=0)
+    wide_shares = live.pop("wide")
     go_last(0, 1)
     go_last(1, 0)
     go_last(1, 1)
@@ -925,17 +943,19 @@
         pl.BlockSpec((group, span + 16, 4 * head + 128), lambda j: (j, 0, 0)),
         shaped((n_seq, span + 16, 4 * head + 128), bf16),
         cost=cost(4 * rows * width * head, 2 * rows * width + 4 * rows * head + 4 * width * head),
-    )(live.pop("xn"), *[lasts[key][i] for i in (0, 1, 2, 4, 5) for key in every], *[backs[key][10] for key in every],
+    )(live.pop("xn"), *[lasts[key][i] for i in (0, 1, 2, 4, 5) for key in every], *[backs[key][9] for key in every],
       live.pop("query_grads"))
+    live["down"] = down_shares
     end(live.pop(("dxn_part", 1, 0)), ("ffn", 1, 1))
     start()
+    down_shares = live.pop("down")
     attn_shares = lax.psum_scatter(live.pop("state_grads"), "seq", scatter_dimension=0)
     finish_out(0, 0)
     finish_out(0, 1)
-    live["out"], live["down"], live["wide"] = outs[0], down_shares, wide_shares
+    live["out"] = outs[0]
     end(live.pop(("dxn_part", 1, 1)), ("dxn", 0, 0))
     start()
-    outs[0], down_shares, wide_shares = live.pop("out"), live.pop("down"), live.pop("wide")
+    outs[0] = live.pop("out")
     finish_out(1, 0)
     finish_out(1, 1)
     finish_grad(0, 0)
@@ -949,10 +969,8 @@
     start()
     in_grads[0], late = live.pop("in_grad"), live.pop("attn").astype(f32)
     gain1_total = late[:span, 4 * head + slots + 1]
-    bit = 1
-    while bit < n_head:
-        gain1_total = gain1_total + lax.ppermute(gain1_total, "head", [(i, i ^ bit) for i in range(n_head)])
-        bit *= 2
+    others = [lax.ppermute(gain1_total, "head", [(i, i ^ d) for i in range(n_head)]) for d in (1, 2, 3)]
+    gain1_total = (gain1_total + others[0]) + (others[1] + others[2])
     finish_grad(1, 0)
     end(None, ("dxn", 1, 1))
     finish_grad(1, 1)

time: 590 us -> 556 us (0.942)
  waiting for transfers between devices: 167 us -> 125 us
    reduce_scatter x1, waiting for transfers between devices: 31.4 us -> 13.8 us  [on_device(): lax.psum_scatter(live.pop('state_grads'), 'seq', scatter_dimension=0)]
    ppermute x18, waiting for transfers between devices: 89.3 us -> 73.9 us  [step(): outer = lax.ppermute(payload, 'head', way)]
    reduce_scatter x1, waiting for transfers between devices: 6.91 us -> 0.01 us  [on_device(): lax.psum_scatter(live.pop('wide_grads'), 'seq', scatter_dimension=0)]
    unnamed x72 -> x89, local copies, waits for them, and re-layouts: 23.5 us -> 28.1 us
    ppermute x2 -> x3, waiting for transfers between devices: 13.3 us -> 9.74 us  [on_device(): lax.ppermute(gain1_total, 'head', [(i, i ^ d) for i in range(n_head)])]
    pallas_call x29 -> x30, Pallas kernels: 267 us -> 265 us  [run(): function(*[o if i in loose or spec.memory_space == pltpu.SMEM else pltpu....]
  transfers between devices with their start and end apart: 46 -> 47, of which waited for: 14 -> 15; matrix products, arithmetic and copies ran while one was open for 3% -> 3% of each run, Pallas kernels for 45% -> 48%
where the time goes in v6:
time: 556 us; the launch traced here: 548 us
  Pallas kernels  286 us (51%)
  waiting for transfers between devices  125 us (22%)
  starting transfers between devices  81.4 us (15%)
  local copies, waits for them, and re-layouts  31.3 us (6%)
  between operations  14.8 us (3%)
  other arithmetic  8.45 us (2%)
    pallas_call x30, Pallas kernels, run(): function(*[o if i in loose or spec.memory_space == pltpu.SMEM else pltpu....  265 us
    ppermute x18, waiting for transfers between devices, step(): outer = lax.ppermute(payload, 'head', way)  73.9 us
    ppermute x18, starting transfers between devices, step(): outer = lax.ppermute(payload, 'head', way)  50 us
    unnamed x89, local copies, waits for them, and re-layouts  28.1 us
    ppermute x6, waiting for transfers between devices, scan_states(): got = lax.ppermute(sent, 'seq', [(i, i ^ bit) for i in range(n)])  27.6 us
    pallas_call x25, Pallas kernels, in_vmem(): pl.pallas_call(kernel, name=name, in_specs=[pl.BlockSpec(memory_space=plt...  21.1 us
    ppermute x16, starting transfers between devices, step(): middle = lax.ppermute(pair, 'head', self.MIDDLE)  18.1 us
    reduce_scatter x1, waiting for transfers between devices, on_device(): lax.psum_scatter(live.pop('state_grads'), 'seq', scatter_dimension=0)  13.8 us
  transfers between devices with their start and end apart: 47, of which 15 were waited for; matrix products, arithmetic and copies ran while one was open for 3% of the time, Pallas kernels for 48%

profile of v6, /device:TPU:0, one launch (start us, length us, event | category | flops | bytes accessed | tf_op | source)
XLA Modules:
  0.0 547.6 jit_solution(185725943556795757)
XLA Ops:
  7.2 14.8 %project.1 = (bf16[1024,2048]{1,0:T(8,128)(2,1)}, bf16[1024,512]{1,0:T(8,128)(2,1)}, bf16[1024,512]{1,0:T(8,128)(2,1)}, f32[1024,64]{1,0:T(8,128)}, f32[1024,64]...) custom-call(bf16[1024,2048]{1,0:T(8,128)(2,1)} %bitcast.35, ...), custom_call_target="tpu_custom_call" | custom-call | flops 4563402752 | bytes 16777216 | tf_op jit(solution)/shard_map/project/pallas_call | solution.py:62
  24.3 2.9 pad_maximum_fusion
  27.4 2.9 collective-permute-start.1
  30.3 7.3 %collective-permute-done.1.refs_2_ = bf16[2,64,1152]{2,1,0:T(8,128)(2,1)S(1)} collective-permute-done((bf16[2,64,1152]{2,1,0:T(8,128)(2,1)S(1)}, bf16[2,64,1152]{2,1,0:T(8,128)(2,1)S(1)}, u32[]{:S(2)}, u32[]{:S(2)}) %collective-permute-start.1) | collective-permute-done | bytes 294944 | tf_op jit(solution)/shard_map/ppermute | solution.py:500
  39.7 6.6 %query.1.q_ref = bf16[1024,512]{1,0:T(8,128)(2,1)} custom-call(bf16[1024,2048]{1,0:T(8,128)(2,1)} %get-tuple-element.707.xn_ref.refs_0_, bf16[2048,512]{1,0:T(8,128)(2,1)} %wq_ref.9), custom_call_target="tpu_custom_call" | custom-call | flops 2147483648 | bytes 7340032 | tf_op jit(solution)/shard_map/query/pallas_call | solution.py:62
  46.3 5.7 %collective-permute-done.2.refs_2_ = bf16[2,64,1152]{2,1,0:T(8,128)(2,1)S(1)} collective-permute-done((bf16[2,64,1152]{2,1,0:T(8,128)(2,1)S(1)}, bf16[2,64,1152]{2,1,0:T(8,128)(2,1)S(1)}, u32[]{:S(2)}, u32[]{:S(2)}) %collective-permute-start.2) | collective-permute-done | bytes 294944 | tf_op jit(solution)/shard_map/ppermute | solution.py:500
  52.3 5.2 read.4
  57.5 3.8 collective-permute-start.3
  61.3 5.3 read.5
  66.7 13.4 %collective-permute-done.3.refs_1_ = bf16[256,2048]{1,0:T(8,128)(2,1)S(1)} collective-permute-done((bf16[256,2048]{1,0:T(8,128)(2,1)S(1)}, bf16[256,2048]{1,0:T(8,128)(2,1)S(1)}, u32[]{:S(2)}, u32[]{:S(2)}) %collective-permute-start.3) | collective-permute-done | bytes 1048608 | tf_op jit(solution)/shard_map/ppermute | solution.py:582
  80.1 4.5 collective-permute-start.4
  85.4 5.2 read.6
  90.6 13.4 %collective-permute-done.4.refs_1_ = bf16[256,2048]{1,0:T(8,128)(2,1)S(1)} collective-permute-done((bf16[256,2048]{1,0:T(8,128)(2,1)S(1)}, bf16[256,2048]{1,0:T(8,128)(2,1)S(1)}, u32[]{:S(2)}, u32[]{:S(2)}) %collective-permute-start.4) | collective-permute-done | bytes 1048608 | tf_op jit(solution)/shard_map/ppermute | solution.py:582
  104.1 3.0 collective-permute-start.6
  107.8 5.4 read.7
  113.3 12.9 %collective-permute-done.6.refs_1_ = bf16[256,2048]{1,0:T(8,128)(2,1)S(1)} collective-permute-done((bf16[256,2048]{1,0:T(8,128)(2,1)S(1)}, bf16[256,2048]{1,0:T(8,128)(2,1)S(1)}, u32[]{:S(2)}, u32[]{:S(2)}) %collective-permute-start.6) | collective-permute-done | bytes 1048608 | tf_op jit(solution)/shard_map/ppermute | solution.py:582
  127.3 3.0 collective-permute-start.8
  133.6 19.4 %feed.4 = (bf16[256,2048]{1,0:T(8,128)(2,1)}, bf16[256,2048]{1,0:T(8,128)(2,1)}, bf16[256,1408]{1,0:T(8,128)(2,1)}, bf16[256,1408]{1,0:T(8,128)(2,1)}, bf16[256,...) custom-call(bf16[1024,2048]{1,0:T(8,128)(2,1)} %bitcast.36, ...), custom_call_target="tpu_custom_call" | custom-call | flops 8858370048 | bytes 24641536 | tf_op jit(solution)/shard_map/feed/pallas_call | solution.py:62
  154.7 2.2 collective-permute-start.10
  158.2 19.6 %feed.5 = (bf16[256,2048]{1,0:T(8,128)(2,1)}, bf16[256,2048]{1,0:T(8,128)(2,1)}, bf16[256,1408]{1,0:T(8,128)(2,1)}, bf16[256,1408]{1,0:T(8,128)(2,1)}, bf16[256,...) custom-call(bf16[1024,2048]{1,0:T(8,128)(2,1)} %bitcast.37, ...), custom_call_target="tpu_custom_call" | custom-call | flops 8858370048 | bytes 24641536 | tf_op jit(solution)/shard_map/feed/pallas_call | solution.py:62
  177.9 3.0 collective-permute-start.12
  181.8 19.5 %feed.6 = (bf16[256,2048]{1,0:T(8,128)(2,1)}, bf16[256,2048]{1,0:T(8,128)(2,1)}, bf16[256,1408]{1,0:T(8,128)(2,1)}, bf16[256,1408]{1,0:T(8,128)(2,1)}, bf16[256,...) custom-call(bf16[1024,2048]{1,0:T(8,128)(2,1)} %bitcast.38, ...), custom_call_target="tpu_custom_call" | custom-call | flops 8858370048 | bytes 24641536 | tf_op jit(solution)/shard_map/feed/pallas_call | solution.py:62
  201.5 2.6 collective-permute-start.14
  205.1 19.5 %feed.7 = (bf16[256,2048]{1,0:T(8,128)(2,1)}, bf16[256,2048]{1,0:T(8,128)(2,1)}, bf16[256,1408]{1,0:T(8,128)(2,1)}, bf16[256,1408]{1,0:T(8,128)(2,1)}, bf16[256,...) custom-call(bf16[1024,2048]{1,0:T(8,128)(2,1)} %bitcast.39, ...), custom_call_target="tpu_custom_call" | custom-call | flops 8858370048 | bytes 24641536 | tf_op jit(solution)/shard_map/feed/pallas_call | solution.py:62
  226.7 2.2 collective-permute-start.16
  230.5 19.1 %wide_grads.1 = bf16[8,2,256,1408]{3,2,1,0:T(8,128)(2,1)} custom-call(bf16[256,2048]{1,0:T(8,128)(2,1)} %get-tuple-element.542.refs_0_, bf16[256,2048]{1,0:T(8,128)(2,1)} %get-tuple-element.543.refs_1_, bf16[256,2048]{1,0:T(8,128)(2,1)} %get-tuple-element.544.refs_2_, bf16[256,2048]{1,0:T(8,128)(2,1)} %get-tuple-element.545.refs_3_, ...), custom_call_target="tpu_custom_call" | custom-call | flops 11811160064 | bytes 21495808 | tf_op jit(solution)/shard_map/wide_grads/pallas_call | solution.py:62
  256.7 2.0 collective-permute-start.19
  258.8 8.7 %back.4 = (bf16[256,2048]{1,0:T(8,128)(2,1)}, bf16[256,512]{1,0:T(8,128)(2,1)}, f32[256,512]{1,0:T(8,128)}, f32[256,512]{1,0:T(8,128)}, f32[256,64]{1,0:T(8,128)...) custom-call(bf16[256,2048]{1,0:T(8,128)(2,1)S(1)} %copy-done.13, ...), custom_call_target="tpu_custom_call" | custom-call | flops 930086912 | bytes 9961472 | tf_op jit(solution)/shard_map/back/pallas_call | solution.py:62
  267.5 11.6 %down_grads.1 = bf16[8,256,1408]{2,1,0:T(8,128)(2,1)} custom-call(bf16[1024,2048]{1,0:T(8,128)(2,1)} %bitcast.53, bf16[256,1408]{1,0:T(8,128)(2,1)} %get-tuple-element.572.refs_1_, bf16[256,1408]{1,0:T(8,128)(2,1)} %get-tuple-element.573.refs_2_, bf16[256,1408]{1,0:T(8,128)(2,1)} %get-tuple-element.574.refs_3_, bf16[256,1408]{1,0:T(8,128)(2,1)} %get-tuple-element.575.refs_4_), custom_call_target="tpu_custom_call" | custom-call | flops 5905580032 | bytes 12845056 | tf_op jit(solution)/shard_map/down_grads/pallas_call | solution.py:62
  281.6 3.0 join.26
  288.3 8.3 %back.5 = (bf16[256,2048]{1,0:T(8,128)(2,1)}, bf16[256,512]{1,0:T(8,128)(2,1)}, f32[256,512]{1,0:T(8,128)}, f32[256,512]{1,0:T(8,128)}, f32[256,64]{1,0:T(8,128)...) custom-call(bf16[256,2048]{1,0:T(8,128)(2,1)S(1)} %get-tuple-element, ...), custom_call_target="tpu_custom_call" | custom-call | flops 930086912 | bytes 9961472 | tf_op jit(solution)/shard_map/back/pallas_call | solution.py:62
  296.6 8.5 %back.6 = (bf16[256,2048]{1,0:T(8,128)(2,1)}, bf16[256,512]{1,0:T(8,128)(2,1)}, f32[256,512]{1,0:T(8,128)}, f32[256,512]{1,0:T(8,128)}, f32[256,64]{1,0:T(8,128)...) custom-call(bf16[256,2048]{1,0:T(8,128)(2,1)S(1)} %copy-done.17, ...), custom_call_target="tpu_custom_call" | custom-call | flops 930086912 | bytes 9961472 | tf_op jit(solution)/shard_map/back/pallas_call | solution.py:62
  306.8 3.4 collective-permute-start.23
  311.0 8.3 %back.7 = (bf16[256,2048]{1,0:T(8,128)(2,1)}, bf16[256,512]{1,0:T(8,128)(2,1)}, f32[256,512]{1,0:T(8,128)}, f32[256,512]{1,0:T(8,128)}, f32[256,64]{1,0:T(8,128)...) custom-call(bf16[256,2048]{1,0:T(8,128)(2,1)S(1)} %get-tuple-element, ...), custom_call_target="tpu_custom_call" | custom-call | flops 930086912 | bytes 9961472 | tf_op jit(solution)/shard_map/back/pallas_call | solution.py:62
  321.3 6.2 %collective-permute-done.23.refs_1_ = bf16[256,2048]{1,0:T(8,128)(2,1)S(1)} collective-permute-done((bf16[256,2048]{1,0:T(8,128)(2,1)S(1)}, bf16[256,2048]{1,0:T(8,128)(2,1)S(1)}, u32[]{:S(2)}, u32[]{:S(2)}) %collective-permute-start.23) | collective-permute-done | bytes 1048608 | tf_op jit(solution)/shard_map/ppermute | solution.py:582
  328.7 4.2 collective-permute-start.25
  335.2 11.9 %collective-permute-done.27.refs_2_ = bf16[2,64,1152]{2,1,0:T(8,128)(2,1)S(1)} collective-permute-done((bf16[2,64,1152]{2,1,0:T(8,128)(2,1)S(1)}, bf16[2,64,1152]{2,1,0:T(8,128)(2,1)S(1)}, u32[]{:S(2)}, u32[]{:S(2)}) %collective-permute-start.27) | collective-permute-done | bytes 294944 | tf_op jit(solution)/shard_map/ppermute | solution.py:500
  348.6 11.0 %query_grads.1.refs_25_ = bf16[2048,1024]{1,0:T(8,128)(2,1)} custom-call(bf16[1024,2048]{1,0:T(8,128)(2,1)} %get-tuple-element.707.xn_ref.refs_0_, bf16[256,2048]{1,0:T(8,128)(2,1)} %get-tuple-element.630.refs_1_.dhid_ref, bf16[256,2048]{1,0:T(8,128)(2,1)} %get-tuple-element.631.refs_2_.dhid_ref, bf16[256,2048]{1,0:T(8,128)(2,1)} %get-tuple-element.632.refs_3_.dhid_ref, ...), custom_call_target="tpu_custom_call" | custom-call | flops 4294967296 | bytes 14680064 | tf_op jit(solution)/shard_map/query_grads/pallas_call | solution.py:62
  360.0 9.6 %last.4 = (bf16[256,512]{1,0:T(8,128)(2,1)}, bf16[256,512]{1,0:T(8,128)(2,1)}, bf16[256,64]{1,0:T(8,128)(2,1)}, bf16[256,2048]{1,0:T(8,128)(2,1)S(1)}, f32[8,64]{1,0:T(8,128)}, /*index=5*/f32[8,2048]{1,0:T(8,128)}) custom-call(f32[4,64,1024]{2,1,0:T(8,128)S(1)} %hop.11.l0_ref, bf16[1024,512]{1,0:T(8,128)(2,1)} %get-tuple-element.395.k_ref, ...), custom_call_target="tpu_custom_call" | custom-call | flops 1677721600 | bytes 13107200 | tf_op jit(solution)/shard_map/last/pallas_call | solution.py:62
  375.6 8.7 %last.7 = (bf16[256,512]{1,0:T(8,128)(2,1)}, bf16[256,512]{1,0:T(8,128)(2,1)}, bf16[256,64]{1,0:T(8,128)(2,1)}, bf16[256,2048]{1,0:T(8,128)(2,1)S(1)}, f32[8,64]{1,0:T(8,128)}, /*index=5*/f32[8,2048]{1,0:T(8,128)}) custom-call(f32[4,64,1024]{2,1,0:T(8,128)S(1)} %hop.11.l0_ref, bf16[1024,512]{1,0:T(8,128)(2,1)} %get-tuple-element.395.k_ref, ...), custom_call_target="tpu_custom_call" | custom-call | flops 1677721600 | bytes 13107200 | tf_op jit(solution)/shard_map/last/pallas_call | solution.py:62
  384.3 8.2 %last.6 = (bf16[256,512]{1,0:T(8,128)(2,1)}, bf16[256,512]{1,0:T(8,128)(2,1)}, bf16[256,64]{1,0:T(8,128)(2,1)}, bf16[256,2048]{1,0:T(8,128)(2,1)S(1)}, f32[8,64]{1,0:T(8,128)}, /*index=5*/f32[8,2048]{1,0:T(8,128)}) custom-call(f32[4,64,1024]{2,1,0:T(8,128)S(1)} %hop.11.l0_ref, bf16[1024,512]{1,0:T(8,128)(2,1)} %get-tuple-element.395.k_ref, ...), custom_call_target="tpu_custom_call" | custom-call | flops 1677721600 | bytes 13107200 | tf_op jit(solution)/shard_map/last/pallas_call | solution.py:62
  392.5 8.2 %last.5 = (bf16[256,512]{1,0:T(8,128)(2,1)}, bf16[256,512]{1,0:T(8,128)(2,1)}, bf16[256,64]{1,0:T(8,128)(2,1)}, bf16[256,2048]{1,0:T(8,128)(2,1)S(1)}, f32[8,64]{1,0:T(8,128)}, /*index=5*/f32[8,2048]{1,0:T(8,128)}) custom-call(f32[4,64,1024]{2,1,0:T(8,128)S(1)} %hop.11.l0_ref, bf16[1024,512]{1,0:T(8,128)(2,1)} %get-tuple-element.395.k_ref, ...), custom_call_target="tpu_custom_call" | custom-call | flops 1677721600 | bytes 13107200 | tf_op jit(solution)/shard_map/last/pallas_call | solution.py:62
  400.8 3.4 join.30
  405.1 2.1 collective-permute-start.31
  408.8 13.2 %state_grads.1 = bf16[8,272,2176]{2,1,0:T(8,128)(2,1)} custom-call(bf16[1024,2048]{1,0:T(8,128)(2,1)} %get-tuple-element.707.xn_ref.refs_0_, bf16[256,512]{1,0:T(8,128)(2,1)} %get-tuple-element.708.refs_1_, bf16[256,512]{1,0:T(8,128)(2,1)} %get-tuple-element.709.refs_2_, bf16[256,512]{1,0:T(8,128)(2,1)} %get-tuple-element.710.refs_3_, ...), custom_call_target="tpu_custom_call" | custom-call | flops 4294967296 | bytes 10485760 | tf_op jit(solution)/shard_map/state_grads/pallas_call | solution.py:62
  422.6 2.3 join.31
  427.9 3.8 collective-permute-start.33
  432.6 2.1 out.4.refs_0_
  434.8 2.3 out.5.refs_0_
  437.1 14.0 %collective-permute-done.33.refs_1_ = bf16[256,2048]{1,0:T(8,128)(2,1)S(1)} collective-permute-done((bf16[256,2048]{1,0:T(8,128)(2,1)}, bf16[256,2048]{1,0:T(8,128)(2,1)S(1)}, u32[]{:S(2)}, u32[]{:S(2)}) %collective-permute-start.33) | collective-permute-done | bytes 1048608 | tf_op jit(solution)/shard_map/ppermute | solution.py:582
  451.3 4.0 collective-permute-start.35
  455.9 3.2 in_grad.4.refs_0_
  459.1 2.2 out.6.refs_0_
  461.3 2.1 out.7
  463.5 8.6 %collective-permute-done.35.refs_1_ = bf16[256,2048]{1,0:T(8,128)(2,1)S(1)} collective-permute-done((bf16[256,2048]{1,0:T(8,128)(2,1)S(1)}, bf16[256,2048]{1,0:T(8,128)(2,1)S(1)}, u32[]{:S(2)}, u32[]{:S(2)}) %collective-permute-start.35) | collective-permute-done | bytes 1048608 | tf_op jit(solution)/shard_map/ppermute | solution.py:582
  479.2 2.9 copy.47
  483.4 3.2 in_grad.5.refs_0_
  486.5 4.8 collective-permute-done.37.refs_0_
  496.2 13.8 %reduce-scatter.8.cloned.1.call-done = bf16[1,272,2176]{2,1,0:T(8,128)(2,1)} async-done(((bf16[8,272,2176]{2,1,0:T(8,128)(2,1)}), bf16[1,272,2176]{2,1,0:T(8,128)(2,1)}) %reduce-scatter.8.cloned.1.call-update) | async-done | bytes 1183760 | tf_op jit(solution)/shard_map/reduce_scatter | solution.py:952
  513.6 3.3 collective-permute-start.42
  522.1 2.0 copy.46
  524.1 3.2 in_grad.6.refs_0_
  527.3 9.7 %collective-permute-done.40 = f32[256]{0:T(256)S(1)} collective-permute-done((f32[256]{0:T(256)S(1)}, f32[256]{0:T(256)S(1)}, u32[]{:S(2)}, u32[]{:S(2)}) %collective-permute-start.40) | collective-permute-done | bytes 1056 | tf_op jit(solution)/shard_map/ppermute | solution.py:972
  537.7 3.2 in_grad.7
  (189 shorter events, 78.9 us)
Async XLA Ops:
  7.2 125.1 %all-gather.3.cloned.1.call-start = ((), (), s32[]{:S(2)}) async-start(), calls=%async_computation.6 | async-start | bytes 19464192 | tf_op jit(solution)/shard_map/all_gather | solution.py:665
  7.2 16.8 %copy-start.41 = (bf16[1408,256]{1,0:T(8,128)(2,1)S(1)}, bf16[1408,256]{1,0:T(8,128)(2,1)}, u32[]{:S(2)}) copy-start(bf16[1408,256]{1,0:T(8,128)(2,1)} %param.24) | copy-start | bytes 2162692
  22.1 1.7 collective-permute-start
  27.3 345.7 %reduce-scatter.4.cloned.1.call-start = ((), (), s32[]{:S(2)}) async-start(), calls=%async_computation.3 | async-start | bytes 12976128 | tf_op jit(solution)/shard_map/reduce_scatter | solution.py:881
  27.4 10.2 %collective-permute-start.1 = (bf16[2,64,1152]{2,1,0:T(8,128)(2,1)S(1)}, bf16[2,64,1152]{2,1,0:T(8,128)(2,1)S(1)}, u32[]{:S(2)}, u32[]{:S(2)}) collective-permute-start(bf16[2,64,1152]{2,1,0:T(8,128)(2,1)S(1)} %get-tuple-element.405), channel_id=1, source_target_pairs={{0,8},{4,12},{8,0},{12,4},{16,24},{20,28},{24,16},{28,20},{1,9},{5... | collective-permute-start | bytes 884744 | tf_op jit(solution)/shard_map/ppermute | solution.py:500
  37.9 14.1 %collective-permute-start.2 = (bf16[2,64,1152]{2,1,0:T(8,128)(2,1)S(1)}, bf16[2,64,1152]{2,1,0:T(8,128)(2,1)S(1)}, u32[]{:S(2)}, u32[]{:S(2)}) collective-permute-start(bf16[2,64,1152]{2,1,0:T(8,128)(2,1)S(1)} %get-tuple-element.410), channel_id=1, source_target_pairs={{0,16},{4,20},{8,24},{12,28},{16,0},{20,4},{24,8},{28,12},{1,17},{... | collective-permute-start | bytes 884744 | tf_op jit(solution)/shard_map/ppermute | solution.py:500
  57.5 22.5 %collective-permute-start.3 = (bf16[256,2048]{1,0:T(8,128)(2,1)S(1)}, bf16[256,2048]{1,0:T(8,128)(2,1)S(1)}, u32[]{:S(2)}, u32[]{:S(2)}) collective-permute-start(bf16[256,2048]{1,0:T(8,128)(2,1)S(1)} %get-tuple-element.417.refs_0_), channel_id=1, source_target_pairs={{0,1},{3,2},{4,5},{7,6},{8,9},{11,10},{12,13},{15,14},{16,17},{19,... | collective-permute-start | bytes 3145736 | tf_op jit(solution)/shard_map/ppermute | solution.py:582
  80.1 23.9 %collective-permute-start.4 = (bf16[256,2048]{1,0:T(8,128)(2,1)S(1)}, bf16[256,2048]{1,0:T(8,128)(2,1)S(1)}, u32[]{:S(2)}, u32[]{:S(2)}) collective-permute-start(bf16[256,2048]{1,0:T(8,128)(2,1)S(1)} %get-tuple-element.421), channel_id=1, source_target_pairs={{0,1},{3,2},{4,5},{7,6},{8,9},{11,10},{12,13},{15,14},{16,17},{19,... | collective-permute-start | bytes 3145736 | tf_op jit(solution)/shard_map/ppermute | solution.py:582
  84.6 19.4 %collective-permute-start.5 = (bf16[256,2048]{1,0:T(8,128)(2,1)S(1)}, bf16[256,2048]{1,0:T(8,128)(2,1)S(1)}, u32[]{:S(2)}, u32[]{:S(2)}) collective-permute-start(bf16[256,2048]{1,0:T(8,128)(2,1)S(1)} %get-tuple-element.422.refs_2_), channel_id=1, source_target_pairs={{1,2},{2,1},{5,6},{6,5},{9,10},{10,9},{13,14},{14,13},{17,18},{18,... | collective-permute-start | bytes 3145736 | tf_op jit(solution)/shard_map/ppermute | solution.py:585
  104.1 22.1 %collective-permute-start.6 = (bf16[256,2048]{1,0:T(8,128)(2,1)S(1)}, bf16[256,2048]{1,0:T(8,128)(2,1)S(1)}, u32[]{:S(2)}, u32[]{:S(2)}) collective-permute-start(bf16[256,2048]{1,0:T(8,128)(2,1)S(1)} %get-tuple-element.430.refs_4_), channel_id=1, source_target_pairs={{0,1},{3,2},{1,0},{2,3},{4,5},{7,6},{5,4},{6,7},{8,9},{11,10},{9,8... | collective-permute-start | bytes 3145736 | tf_op jit(solution)/shard_map/ppermute | solution.py:582
  107.1 19.1 %collective-permute-start.7 = (bf16[256,2048]{1,0:T(8,128)(2,1)S(1)}, bf16[256,2048]{1,0:T(8,128)(2,1)S(1)}, u32[]{:S(2)}, u32[]{:S(2)}) collective-permute-start(bf16[256,2048]{1,0:T(8,128)(2,1)S(1)} %get-tuple-element.431.refs_2_), channel_id=1, source_target_pairs={{1,2},{2,1},{5,6},{6,5},{9,10},{10,9},{13,14},{14,13},{17,18},{18,... | collective-permute-start | bytes 3145736 | tf_op jit(solution)/shard_map/ppermute | solution.py:585
  126.2 6.1 %copy-start.36 = (f32[2048]{0:T(1024)S(1)}, f32[2048]{0:T(1024)}, u32[]{:S(2)}) copy-start(f32[2048]{0:T(1024)} %param.21) | copy-start | bytes 24580
  127.3 25.7 %collective-permute-start.8 = (bf16[256,2048]{1,0:T(8,128)(2,1)S(1)}, bf16[256,2048]{1,0:T(8,128)(2,1)}, u32[]{:S(2)}, u32[]{:S(2)}) collective-permute-start(bf16[256,2048]{1,0:T(8,128)(2,1)S(1)} %get-tuple-element.435.refs_4_), channel_id=1, source_target_pairs={{0,1},{3,2},{1,0},{2,3},{4,5},{7,6},{5,4},{6,7},{8,9},{11,10},{9,8... | collective-permute-start | bytes 3145736 | tf_op jit(solution)/shard_map/ppermute | solution.py:582
  130.3 22.7 %collective-permute-start.9 = (bf16[256,2048]{1,0:T(8,128)(2,1)S(1)}, bf16[256,2048]{1,0:T(8,128)(2,1)}, u32[]{:S(2)}, u32[]{:S(2)}) collective-permute-start(bf16[256,2048]{1,0:T(8,128)(2,1)S(1)} %get-tuple-element.436.refs_2_), channel_id=1, source_target_pairs={{1,2},{2,1},{5,6},{6,5},{9,10},{10,9},{13,14},{14,13},{17,18},{18,... | collective-permute-start | bytes 3145736 | tf_op jit(solution)/shard_map/ppermute | solution.py:585
  154.7 23.0 %collective-permute-start.10 = (bf16[256,2048]{1,0:T(8,128)(2,1)S(1)}, bf16[256,2048]{1,0:T(8,128)(2,1)S(1)}, u32[]{:S(2)}, u32[]{:S(2)}) collective-permute-start(bf16[256,2048]{1,0:T(8,128)(2,1)S(1)} %get-tuple-element.452.refs_4_), channel_id=1, source_target_pairs={{0,1},{3,2},{1,0},{2,3},{4,5},{7,6},{5,4},{6,7},{8,9},{11,10},{9,8... | collective-permute-start | bytes 3145736 | tf_op jit(solution)/shard_map/ppermute | solution.py:582
  156.9 20.8 %collective-permute-start.11 = (bf16[256,2048]{1,0:T(8,128)(2,1)S(1)}, bf16[256,2048]{1,0:T(8,128)(2,1)S(1)}, u32[]{:S(2)}, u32[]{:S(2)}) collective-permute-start(bf16[256,2048]{1,0:T(8,128)(2,1)S(1)} %get-tuple-element.453.refs_2_), channel_id=1, source_target_pairs={{1,2},{2,1},{5,6},{6,5},{9,10},{10,9},{13,14},{14,13},{17,18},{18,... | collective-permute-start | bytes 3145736 | tf_op jit(solution)/shard_map/ppermute | solution.py:585
  177.9 23.4 %collective-permute-start.12 = (bf16[256,2048]{1,0:T(8,128)(2,1)S(1)}, bf16[256,2048]{1,0:T(8,128)(2,1)S(1)}, u32[]{:S(2)}, u32[]{:S(2)}) collective-permute-start(bf16[256,2048]{1,0:T(8,128)(2,1)S(1)} %get-tuple-element.469.refs_4_), channel_id=1, source_target_pairs={{0,1},{3,2},{1,0},{2,3},{4,5},{7,6},{5,4},{6,7},{8,9},{11,10},{9,8... | collective-permute-start | bytes 3145736 | tf_op jit(solution)/shard_map/ppermute | solution.py:582
  180.9 20.4 %collective-permute-start.13 = (bf16[256,2048]{1,0:T(8,128)(2,1)S(1)}, bf16[256,2048]{1,0:T(8,128)(2,1)S(1)}, u32[]{:S(2)}, u32[]{:S(2)}) collective-permute-start(bf16[256,2048]{1,0:T(8,128)(2,1)S(1)} %get-tuple-element.470.refs_2_), channel_id=1, source_target_pairs={{1,2},{2,1},{5,6},{6,5},{9,10},{10,9},{13,14},{14,13},{17,18},{18,... | collective-permute-start | bytes 3145736 | tf_op jit(solution)/shard_map/ppermute | solution.py:585
  201.5 23.0 %collective-permute-start.14 = (bf16[256,2048]{1,0:T(8,128)(2,1)S(1)}, bf16[256,2048]{1,0:T(8,128)(2,1)S(1)}, u32[]{:S(2)}, u32[]{:S(2)}) collective-permute-start(bf16[256,2048]{1,0:T(8,128)(2,1)S(1)} %get-tuple-element.496.refs_4_), channel_id=1, source_target_pairs={{0,1},{3,2},{1,0},{2,3},{4,5},{7,6},{5,4},{6,7},{8,9},{11,10},{9,8... | collective-permute-start | bytes 3145736 | tf_op jit(solution)/shard_map/ppermute | solution.py:582
  204.1 20.4 %collective-permute-start.15 = (bf16[256,2048]{1,0:T(8,128)(2,1)S(1)}, bf16[256,2048]{1,0:T(8,128)(2,1)S(1)}, u32[]{:S(2)}, u32[]{:S(2)}) collective-permute-start(bf16[256,2048]{1,0:T(8,128)(2,1)S(1)} %get-tuple-element.497.refs_2_), channel_id=1, source_target_pairs={{1,2},{2,1},{5,6},{6,5},{9,10},{10,9},{13,14},{14,13},{17,18},{18,... | collective-permute-start | bytes 3145736 | tf_op jit(solution)/shard_map/ppermute | solution.py:585
  226.7 22.9 %copy-start.28 = (bf16[256,2048]{1,0:T(8,128)(2,1)}, bf16[256,2048]{1,0:T(8,128)(2,1)S(1)}, u32[]{:S(2)}) copy-start(bf16[256,2048]{1,0:T(8,128)(2,1)S(1)} %get-tuple-element.526.refs_2_) | copy-start | bytes 3145732
  226.7 22.9 %copy-start.3 = (bf16[256,2048]{1,0:T(8,128)(2,1)S(1)}, bf16[256,2048]{1,0:T(8,128)(2,1)}, u32[]{:S(2)}) copy-start(bf16[256,2048]{1,0:T(8,128)(2,1)} %get-tuple-element.527.refs_5_.refs_0_) | copy-start | bytes 3145732
  226.7 22.9 %collective-permute-start.16 = (bf16[256,2048]{1,0:T(8,128)(2,1)}, bf16[256,2048]{1,0:T(8,128)(2,1)}, u32[]{:S(2)}, u32[]{:S(2)}) collective-permute-start(bf16[256,2048]{1,0:T(8,128)(2,1)} %get-tuple-element.525.refs_4_), channel_id=1, source_target_pairs={{0,1},{3,2},{1,0},{2,3},{4,5},{7,6},{5,4},{6,7},{8,9},{11,10},{9,8... | collective-permute-start | bytes 3145736 | tf_op jit(solution)/shard_map/ppermute | solution.py:582
  228.9 20.7 %collective-permute-start.17 = (bf16[256,2048]{1,0:T(8,128)(2,1)S(1)}, bf16[256,2048]{1,0:T(8,128)(2,1)}, u32[]{:S(2)}, u32[]{:S(2)}) collective-permute-start(bf16[256,2048]{1,0:T(8,128)(2,1)S(1)} %get-tuple-element.526.refs_2_), channel_id=1, source_target_pairs={{1,2},{2,1},{5,6},{6,5},{9,10},{10,9},{13,14},{14,13},{17,18},{18,... | collective-permute-start | bytes 3145736 | tf_op jit(solution)/shard_map/ppermute | solution.py:585
  254.9 172.9 %reduce-scatter.6.cloned.1.call-start = ((), (), s32[]{:S(2)}) async-start(), calls=%async_computation.4 | async-start | bytes 6488064 | tf_op jit(solution)/shard_map/reduce_scatter | solution.py:886
  254.9 24.2 %collective-permute-start.18 = (bf16[256,2048]{1,0:T(8,128)(2,1)}, bf16[256,2048]{1,0:T(8,128)(2,1)}, u32[]{:S(2)}, u32[]{:S(2)}) collective-permute-start(bf16[256,2048]{1,0:T(8,128)(2,1)} %copy-done.22), channel_id=1, source_target_pairs={{0,1},{3,2},{1,0},{2,3},{4,5},{7,6},{5,4},{6,7},{8,9},{11,10},{9,8... | collective-permute-start | bytes 3145736 | tf_op jit(solution)/shard_map/ppermute | solution.py:582
  256.7 22.4 %collective-permute-start.19 = (bf16[256,2048]{1,0:T(8,128)(2,1)}, bf16[256,2048]{1,0:T(8,128)(2,1)}, u32[]{:S(2)}, u32[]{:S(2)}) collective-permute-start(bf16[256,2048]{1,0:T(8,128)(2,1)} %copy-done.20), channel_id=1, source_target_pairs={{1,2},{2,1},{5,6},{6,5},{9,10},{10,9},{13,14},{14,13},{17,18},{18,... | collective-permute-start | bytes 3145736 | tf_op jit(solution)/shard_map/ppermute | solution.py:585
  267.5 11.7 %copy-start.2 = (bf16[256,2048]{1,0:T(8,128)(2,1)S(1)}, bf16[256,2048]{1,0:T(8,128)(2,1)}, u32[]{:S(2)}) copy-start(bf16[256,2048]{1,0:T(8,128)(2,1)} %get-tuple-element.555.refs_5_.refs_0_) | copy-start | bytes 3145732
  285.8 224.3 %reduce-scatter.8.cloned.1.call-start = ((), (), s32[]{:S(2)}) async-start(), calls=%async_computation.5 | async-start | bytes 10653696 | tf_op jit(solution)/shard_map/reduce_scatter | solution.py:952
  285.8 19.2 %collective-permute-start.20 = (bf16[256,2048]{1,0:T(8,128)(2,1)}, bf16[256,2048]{1,0:T(8,128)(2,1)S(1)}, u32[]{:S(2)}, u32[]{:S(2)}) collective-permute-start(bf16[256,2048]{1,0:T(8,128)(2,1)} %get-tuple-element.577.refs_4_), channel_id=1, source_target_pairs={{0,1},{3,2},{1,0},{2,3},{4,5},{7,6},{5,4},{6,7},{8,9},{11,10},{9,8... | collective-permute-start | bytes 3145736 | tf_op jit(solution)/shard_map/ppermute | solution.py:582
  287.5 17.5 %collective-permute-start.21 = (bf16[256,2048]{1,0:T(8,128)(2,1)}, bf16[256,2048]{1,0:T(8,128)(2,1)S(1)}, u32[]{:S(2)}, u32[]{:S(2)}) collective-permute-start(bf16[256,2048]{1,0:T(8,128)(2,1)} %get-tuple-element.578.refs_2_), channel_id=1, source_target_pairs={{1,2},{2,1},{5,6},{6,5},{9,10},{10,9},{13,14},{14,13},{17,18},{18,... | collective-permute-start | bytes 3145736 | tf_op jit(solution)/shard_map/ppermute | solution.py:585
  288.3 8.3 %copy-start.17 = (bf16[256,2048]{1,0:T(8,128)(2,1)S(1)}, bf16[256,2048]{1,0:T(8,128)(2,1)}, u32[]{:S(2)}) copy-start(bf16[256,2048]{1,0:T(8,128)(2,1)} %copy-done.16) | copy-start | bytes 3145732
  296.6 8.5 %copy-start.1 = (bf16[256,2048]{1,0:T(8,128)(2,1)S(1)}, bf16[256,2048]{1,0:T(8,128)(2,1)}, u32[]{:S(2)}) copy-start(bf16[256,2048]{1,0:T(8,128)(2,1)} %get-tuple-element.579.refs_5_.refs_0_) | copy-start | bytes 3145732
  306.8 20.7 %collective-permute-start.23 = (bf16[256,2048]{1,0:T(8,128)(2,1)S(1)}, bf16[256,2048]{1,0:T(8,128)(2,1)S(1)}, u32[]{:S(2)}, u32[]{:S(2)}) collective-permute-start(bf16[256,2048]{1,0:T(8,128)(2,1)S(1)} %get-tuple-element.614.refs_4_), channel_id=1, source_target_pairs={{0,1},{3,2},{1,0},{2,3},{4,5},{7,6},{5,4},{6,7},{8,9},{11,10},{9,8... | collective-permute-start | bytes 3145736 | tf_op jit(solution)/shard_map/ppermute | solution.py:582
  310.3 17.3 %collective-permute-start.24 = (bf16[256,2048]{1,0:T(8,128)(2,1)S(1)}, bf16[256,2048]{1,0:T(8,128)(2,1)S(1)}, u32[]{:S(2)}, u32[]{:S(2)}) collective-permute-start(bf16[256,2048]{1,0:T(8,128)(2,1)S(1)} %get-tuple-element.615.refs_2_), channel_id=1, source_target_pairs={{1,2},{2,1},{5,6},{6,5},{9,10},{10,9},{13,14},{14,13},{17,18},{18,... | collective-permute-start | bytes 3145736 | tf_op jit(solution)/shard_map/ppermute | solution.py:585
  319.3 8.3 %copy-start = (bf16[256,2048]{1,0:T(8,128)(2,1)S(1)}, bf16[256,2048]{1,0:T(8,128)(2,1)}, u32[]{:S(2)}) copy-start(bf16[256,2048]{1,0:T(8,128)(2,1)} %get-tuple-element.613.refs_5_.refs_0_) | copy-start | bytes 3145732
  319.4 1.6 collective-permute-start.22
  328.7 40.9 %collective-permute-start.25 = (bf16[256,2048]{1,0:T(8,128)(2,1)S(1)}, bf16[256,2048]{1,0:T(8,128)(2,1)S(1)}, u32[]{:S(2)}, u32[]{:S(2)}) collective-permute-start(bf16[256,2048]{1,0:T(8,128)(2,1)S(1)} %get-tuple-element.622.refs_4_), channel_id=1, source_target_pairs={{0,1},{3,2},{1,0},{2,3},{4,5},{7,6},{5,4},{6,7},{8,9},{11,10},{9,8... | collective-permute-start | bytes 3145736 | tf_op jit(solution)/shard_map/ppermute | solution.py:582
  332.9 36.7 %collective-permute-start.26 = (bf16[256,2048]{1,0:T(8,128)(2,1)S(1)}, bf16[256,2048]{1,0:T(8,128)(2,1)S(1)}, u32[]{:S(2)}, u32[]{:S(2)}) collective-permute-start(bf16[256,2048]{1,0:T(8,128)(2,1)S(1)} %get-tuple-element.623.refs_2_), channel_id=1, source_target_pairs={{1,2},{2,1},{5,6},{6,5},{9,10},{10,9},{13,14},{14,13},{17,18},{18,... | collective-permute-start | bytes 3145736 | tf_op jit(solution)/shard_map/ppermute | solution.py:585
  333.8 13.3 %collective-permute-start.27 = (bf16[2,64,1152]{2,1,0:T(8,128)(2,1)S(1)}, bf16[2,64,1152]{2,1,0:T(8,128)(2,1)S(1)}, u32[]{:S(2)}, u32[]{:S(2)}) collective-permute-start(bf16[2,64,1152]{2,1,0:T(8,128)(2,1)S(1)} %get-tuple-element.612), channel_id=1, source_target_pairs={{0,8},{4,12},{8,0},{12,4},{16,24},{20,28},{24,16},{28,20},{1,9},{5... | collective-permute-start | bytes 884744 | tf_op jit(solution)/shard_map/ppermute | solution.py:500
  347.3 12.3 %collective-permute-start.28 = (bf16[2,64,1152]{2,1,0:T(8,128)(2,1)S(1)}, bf16[2,64,1152]{2,1,0:T(8,128)(2,1)S(1)}, u32[]{:S(2)}, u32[]{:S(2)}) collective-permute-start(bf16[2,64,1152]{2,1,0:T(8,128)(2,1)S(1)} %get-tuple-element.644), channel_id=1, source_target_pairs={{0,16},{4,20},{8,24},{12,28},{16,0},{20,4},{24,8},{28,12},{1,17},{... | collective-permute-start | bytes 884744 | tf_op jit(solution)/shard_map/ppermute | solution.py:500
  373.0 27.7 %collective-permute-start.29 = (bf16[256,2048]{1,0:T(8,128)(2,1)}, bf16[256,2048]{1,0:T(8,128)(2,1)S(1)}, u32[]{:S(2)}, u32[]{:S(2)}) collective-permute-start(bf16[256,2048]{1,0:T(8,128)(2,1)} %get-tuple-element.670.refs_4_), channel_id=1, source_target_pairs={{0,1},{3,2},{1,0},{2,3},{4,5},{7,6},{5,4},{6,7},{8,9},{11,10},{9,8... | collective-permute-start | bytes 3145736 | tf_op jit(solution)/shard_map/ppermute | solution.py:582
  374.8 25.9 %collective-permute-start.30 = (bf16[256,2048]{1,0:T(8,128)(2,1)}, bf16[256,2048]{1,0:T(8,128)(2,1)S(1)}, u32[]{:S(2)}, u32[]{:S(2)}) collective-permute-start(bf16[256,2048]{1,0:T(8,128)(2,1)} %get-tuple-element.671.refs_2_), channel_id=1, source_target_pairs={{1,2},{2,1},{5,6},{6,5},{9,10},{10,9},{13,14},{14,13},{17,18},{18,... | collective-permute-start | bytes 3145736 | tf_op jit(solution)/shard_map/ppermute | solution.py:585
  392.5 8.2 %copy-start.5 = (bf16[256,2048]{1,0:T(8,128)(2,1)S(1)}, bf16[256,2048]{1,0:T(8,128)(2,1)}, u32[]{:S(2)}) copy-start(bf16[256,2048]{1,0:T(8,128)(2,1)} %copy-done.4) | copy-start | bytes 3145732
  405.1 17.5 %collective-permute-start.31 = (bf16[256,2048]{1,0:T(8,128)(2,1)}, bf16[256,2048]{1,0:T(8,128)(2,1)}, u32[]{:S(2)}, u32[]{:S(2)}) collective-permute-start(bf16[256,2048]{1,0:T(8,128)(2,1)} %get-tuple-element.694.refs_4_), channel_id=1, source_target_pairs={{0,1},{3,2},{1,0},{2,3},{4,5},{7,6},{5,4},{6,7},{8,9},{11,10},{9,8... | collective-permute-start | bytes 3145736 | tf_op jit(solution)/shard_map/ppermute | solution.py:582
  407.2 15.4 %collective-permute-start.32 = (bf16[256,2048]{1,0:T(8,128)(2,1)}, bf16[256,2048]{1,0:T(8,128)(2,1)}, u32[]{:S(2)}, u32[]{:S(2)}) collective-permute-start(bf16[256,2048]{1,0:T(8,128)(2,1)} %get-tuple-element.695.refs_2_), channel_id=1, source_target_pairs={{1,2},{2,1},{5,6},{6,5},{9,10},{10,9},{13,14},{14,13},{17,18},{18,... | collective-permute-start | bytes 3145736 | tf_op jit(solution)/shard_map/ppermute | solution.py:585
  408.8 13.8 %copy-start.7 = (bf16[256,2048]{1,0:T(8,128)(2,1)S(1)}, bf16[256,2048]{1,0:T(8,128)(2,1)}, u32[]{:S(2)}) copy-start(bf16[256,2048]{1,0:T(8,128)(2,1)} %copy-done.6) | copy-start | bytes 3145732
  427.8 6.9 %copy-start.9 = (bf16[256,2048]{1,0:T(8,128)(2,1)S(1)}, bf16[256,2048]{1,0:T(8,128)(2,1)}, u32[]{:S(2)}) copy-start(bf16[256,2048]{1,0:T(8,128)(2,1)} %copy-done.8) | copy-start | bytes 3145732
  427.9 23.2 %collective-permute-start.33 = (bf16[256,2048]{1,0:T(8,128)(2,1)}, bf16[256,2048]{1,0:T(8,128)(2,1)S(1)}, u32[]{:S(2)}, u32[]{:S(2)}) collective-permute-start(bf16[256,2048]{1,0:T(8,128)(2,1)} %copy-done.26), channel_id=1, source_target_pairs={{0,1},{3,2},{1,0},{2,3},{4,5},{7,6},{5,4},{6,7},{8,9},{11,10},{9,8... | collective-permute-start | bytes 3145736 | tf_op jit(solution)/shard_map/ppermute | solution.py:582
  431.7 19.4 %collective-permute-start.34 = (bf16[256,2048]{1,0:T(8,128)(2,1)}, bf16[256,2048]{1,0:T(8,128)(2,1)S(1)}, u32[]{:S(2)}, u32[]{:S(2)}) collective-permute-start(bf16[256,2048]{1,0:T(8,128)(2,1)} %copy-done.24), channel_id=1, source_target_pairs={{1,2},{2,1},{5,6},{6,5},{9,10},{10,9},{13,14},{14,13},{17,18},{18,... | collective-permute-start | bytes 3145736 | tf_op jit(solution)/shard_map/ppermute | solution.py:585
  434.8 16.3 %copy-start.25 = (bf16[256,2048]{1,0:T(8,128)(2,1)S(1)}, bf16[256,2048]{1,0:T(8,128)(2,1)}, u32[]{:S(2)}) copy-start(bf16[256,2048]{1,0:T(8,128)(2,1)} %copy-done.24) | copy-start | bytes 3145732
  434.8 16.3 %copy-start.27 = (bf16[256,2048]{1,0:T(8,128)(2,1)S(1)}, bf16[256,2048]{1,0:T(8,128)(2,1)}, u32[]{:S(2)}) copy-start(bf16[256,2048]{1,0:T(8,128)(2,1)} %copy-done.26) | copy-start | bytes 3145732
  451.2 7.9 %copy-start.11 = (bf16[256,2048]{1,0:T(8,128)(2,1)S(1)}, bf16[256,2048]{1,0:T(8,128)(2,1)}, u32[]{:S(2)}) copy-start(bf16[256,2048]{1,0:T(8,128)(2,1)} %copy-done.10) | copy-start | bytes 3145732
  451.3 20.8 %collective-permute-start.35 = (bf16[256,2048]{1,0:T(8,128)(2,1)S(1)}, bf16[256,2048]{1,0:T(8,128)(2,1)S(1)}, u32[]{:S(2)}, u32[]{:S(2)}) collective-permute-start(bf16[256,2048]{1,0:T(8,128)(2,1)S(1)} %get-tuple-element.749.refs_4_), channel_id=1, source_target_pairs={{0,1},{3,2},{1,0},{2,3},{4,5},{7,6},{5,4},{6,7},{8,9},{11,10},{9,8... | collective-permute-start | bytes 3145736 | tf_op jit(solution)/shard_map/ppermute | solution.py:582
  455.2 16.8 %collective-permute-start.36 = (bf16[256,2048]{1,0:T(8,128)(2,1)S(1)}, bf16[256,2048]{1,0:T(8,128)(2,1)S(1)}, u32[]{:S(2)}, u32[]{:S(2)}) collective-permute-start(bf16[256,2048]{1,0:T(8,128)(2,1)S(1)} %get-tuple-element.750.refs_2_), channel_id=1, source_target_pairs={{1,2},{2,1},{5,6},{6,5},{9,10},{10,9},{13,14},{14,13},{17,18},{18,... | collective-permute-start | bytes 3145736 | tf_op jit(solution)/shard_map/ppermute | solution.py:585
  463.5 12.8 %copy-start.40 = (bf16[1,2,256,1408]{3,2,1,0:T(8,128)(2,1)S(1)}, bf16[1,2,256,1408]{3,2,1,0:T(8,128)(2,1)}, u32[]{:S(2)}) copy-start(bf16[1,2,256,1408]{3,2,1,0:T(8,128)(2,1)} %reduce-scatter.4.cloned.1.call-done) | copy-start | bytes 4325380
  473.2 4.9 copy-start.42
  473.2 18.2 %collective-permute-start.37 = (bf16[256,2048]{1,0:T(8,128)(2,1)S(1)}, bf16[256,2048]{1,0:T(8,128)(2,1)S(1)}, u32[]{:S(2)}, u32[]{:S(2)}) collective-permute-start(bf16[256,2048]{1,0:T(8,128)(2,1)S(1)} %get-tuple-element.760.refs_3_), channel_id=1, source_target_pairs={{1,0},{2,3},{5,4},{6,7},{9,8},{10,11},{13,12},{14,15},{17,16},{18,... | collective-permute-start | bytes 3145736 | tf_op jit(solution)/shard_map/ppermute | solution.py:582
  474.6 17.8 %collective-permute-start.38 = (bf16[256,2048]{1,0:T(8,128)(2,1)S(1)}, bf16[256,2048]{1,0:T(8,128)(2,1)}, u32[]{:S(2)}, u32[]{:S(2)}) collective-permute-start(bf16[256,2048]{1,0:T(8,128)(2,1)S(1)} %get-tuple-element.761.refs_1_), channel_id=1, source_target_pairs={{1,2},{2,1},{5,6},{6,5},{9,10},{10,9},{13,14},{14,13},{17,18},{18,... | collective-permute-start | bytes 3145736 | tf_op jit(solution)/shard_map/ppermute | solution.py:585
  510.0 9.7 %copy-start.39 = (bf16[1,272,2176]{2,1,0:T(8,128)(2,1)S(1)}, bf16[1,272,2176]{2,1,0:T(8,128)(2,1)}, u32[]{:S(2)}) copy-start(bf16[1,272,2176]{2,1,0:T(8,128)(2,1)} %reduce-scatter.8.cloned.1.call-done) | copy-start | bytes 3551236
  510.0 27.6 %collective-permute-start.39 = (bf16[256,2048]{1,0:T(8,128)(2,1)S(1)}, bf16[256,2048]{1,0:T(8,128)(2,1)S(1)}, u32[]{:S(2)}, u32[]{:S(2)}) collective-permute-start(bf16[256,2048]{1,0:T(8,128)(2,1)S(1)} %get-tuple-element.769.refs_1_), channel_id=1, source_target_pairs={{1,0},{2,3},{5,4},{6,7},{9,8},{10,11},{13,12},{14,15},{17,16},{18,... | collective-permute-start | bytes 3145736 | tf_op jit(solution)/shard_map/ppermute | solution.py:582
  513.6 13.7 %collective-permute-start.42 = (f32[256]{0:T(256)S(1)}, f32[256]{0:T(256)S(1)}, u32[]{:S(2)}, u32[]{:S(2)}) collective-permute-start(f32[256]{0:T(256)S(1)} %get-tuple-element.815), channel_id=1, source_target_pairs={{0,3},{1,2},{2,1},{3,0},{4,7},{5,6},{6,5},{7,4},{8,11},{9,10},{10,... | collective-permute-start | bytes 3080 | tf_op jit(solution)/shard_map/ppermute | solution.py:972
  517.0 10.3 %collective-permute-start.41 = (f32[256]{0:T(256)S(1)}, f32[256]{0:T(256)S(1)}, u32[]{:S(2)}, u32[]{:S(2)}) collective-permute-start(f32[256]{0:T(256)S(1)} %get-tuple-element.815), channel_id=1, source_target_pairs={{0,2},{1,3},{2,0},{3,1},{4,6},{5,7},{6,4},{7,5},{8,10},{9,11},{10,... | collective-permute-start | bytes 3080 | tf_op jit(solution)/shard_map/ppermute | solution.py:972
  518.2 18.8 %collective-permute-start.40 = (f32[256]{0:T(256)S(1)}, f32[256]{0:T(256)S(1)}, u32[]{:S(2)}, u32[]{:S(2)}) collective-permute-start(f32[256]{0:T(256)S(1)} %get-tuple-element.815), channel_id=1, source_target_pairs={{0,1},{1,0},{2,3},{3,2},{4,5},{5,4},{6,7},{7,6},{8,9},{9,8},{10,11... | collective-permute-start | bytes 3080 | tf_op jit(solution)/shard_map/ppermute | solution.py:972
  (26 other events, 41.3 us)
Sparse Core Ops, SparseCore 0:
  27.4 99.9 all-gather.2
  255.0 93.6 reduce-scatter.3
  352.8 59.1 reduce-scatter.5
  428.0 81.9 reduce-scatter.7

commit v7 on v6

--- a/solution.py
+++ b/solution.py
@@ -368,17 +368,39 @@
         out_ref[:, i] = block.reshape(blocks, width, units)
 
 
-def query_grad_kernel(count, *refs):
-    xn_ref, out_ref = refs[0], refs[-1]
+def query_grad_kernel(count, first_column, *refs):
+    xn_ref, out_ref, block, sems = refs[0], refs[-3], refs[-2], refs[-1]
     datt, dq, o = (refs[1 + i * count : 1 + (i + 1) * count] for i in range(3))
     rows, width = dq[0].shape
+    _, groups, span, columns = block.shape
+    step, steps = pl.program_id(0), pl.num_programs(0)
+
+    def copy(at):
+        slot = lax.rem(at, 2)
+        return pltpu.make_async_copy(
+            block.at[slot], out_ref.at[pl.ds(at * groups, groups), :, pl.ds(first_column, columns)], sems.at[slot]
+        )
+
+    @pl.when(step >= 2)
+    def _():
+        copy(step - 2).wait()
+
     xn = [xn_ref[i * rows : (i + 1) * rows, :] for i in range(count)]
-    out_ref[:, :width] = summed([(x, g[...]) for x, g in zip(xn, dq)])
-    out_ref[:, width:] = summed([(d[...], r[...]) for d, r in zip(datt, o)])
+    slot = lax.rem(step, 2)
+    query = summed([(x, g[...]) for x, g in zip(xn, dq)])
+    block[slot, :, :, :width] = query.reshape(groups, span, width)
+    output = summed([(d[...], r[...]) for d, r in zip(datt, o)])
+    block[slot, :, :, width:] = output.reshape(groups, span, width)
+    copy(step).start()
+
+    @pl.when(step == steps - 1)
+    def _():
+        copy(step - 1).wait()
+        copy(step).wait()
 
 
 def state_grad_kernel(count, *refs):
-    xn_ref, query_ref, out_ref = refs[0], refs[-2], refs[-1]
+    xn_ref, out_ref = refs[0], refs[-1]
     dk, dv, dz, bias, gain1, gain2 = (refs[1 + i * count : 1 + (i + 1) * count] for i in range(6))
     rows, width = dk[0].shape
     slots = dz[0].shape[1]
@@ -387,8 +409,7 @@
     xn = [xn_ref[i * rows : (i + 1) * rows, :] for i in range(count)]
     for i, grads in enumerate((dk, dv)):
         block = summed([(x, g[...]) for x, g in zip(xn, grads)])
-        out_ref[:, :span, (2 + i) * width : (3 + i) * width] = block.reshape(groups, span, width)
-    out_ref[:, :span, : 2 * width] = query_ref[...].reshape(groups, span, 2 * width)
+        out_ref[:, :span, i * width : (i + 1) * width] = block.reshape(groups, span, width)
     forget = tn(xn[0], dz[0][...])
     for x, g in zip(xn[1:], dz[1:]):
         forget = forget + tn(x, g[...])
@@ -406,7 +427,7 @@
     small = padded(forget)
     lane = lax.broadcasted_iota(jnp.int32, small.shape, 1)
     small = jnp.where(lane == slots, column(gain2), jnp.where(lane == slots + 1, column(gain1), small))
-    out_ref[:, :span, 4 * width :] = small.astype(bf16).reshape(groups, span, slots + pad)
+    out_ref[:, :span, 2 * width :] = small.astype(bf16).reshape(groups, span, slots + pad)
     total = bias[0][...]
     for part in bias[1:]:
         total = total + part[...]
@@ -415,8 +436,8 @@
     row = lax.broadcasted_iota(jnp.int32, total.shape, 0)
     tail = jnp.where(row == 0, upper, jnp.where(row == 1, total - upper, 0.0)).astype(bf16)
     for g in range(groups):
-        out_ref[g, span:, : 4 * width] = jnp.zeros((16, 4 * width), bf16)
-        out_ref[g, span:, 4 * width :] = tail
+        out_ref[g, span:, : 2 * width] = jnp.zeros((16, 2 * width), bf16)
+        out_ref[g, span:, 2 * width :] = tail
 
 
 def pack(ref, m, decay, state):
@@ -493,7 +514,7 @@
     )(*operands)
 
 
-def scan_states(n, state, decay, sent, after, own=(), pieces=1, tie=None, last_tie=None):
+def scan_states(n, state, decay, sent, after, own=(), pieces=1, ties=()):
     parts, slots, width = state.shape
     part, bit, hops = [], 1, 0
     while bit < n:
@@ -502,8 +523,8 @@
         shapes = [shaped(state.shape, f32), shaped(decay.shape, f32)] * 2 + [shaped(sent.shape, bf16)]
         if final:
             shapes = [shaped((parts * pieces, slots, width), f32)]
-        if final and last_tie is not None:
-            state = behind_of(state, *last_tie)
+        if hops < len(ties) and ties[hops] is not None:
+            state = ties[hops](state, got)
         results = in_vmem(
             "hop",
             functools.partial(hop_kernel, bit, after, not part, final, parts, pieces),
@@ -513,8 +534,6 @@
         if final:
             return results[0]
         state, decay, *part, sent = results
-        if tie is not None and not hops:
-            sent = tie(sent)
         bit, hops = 2 * bit, hops + 1
 
 
@@ -586,8 +605,10 @@
         self.waiting = (piece, outer, pair, middle, payload if returns else None)
         return values
 
-    def join(self, coming=None):
+    def join(self, coming=None, after=()):
         piece, outer, pair, middle, total = self.waiting
+        if after:
+            outer = behind_of(outer, *after)
         if piece is None and total is None:
             outer = None
         operands = [piece, outer, pair, middle, total, coming]
@@ -656,12 +677,12 @@
     )(xn, w_query)
     stacked = []
 
-    def stack_weights(sent):
-        gate, down, sent = lax.optimization_barrier((w_gate, w_down, sent))
+    def stack_weights(state, got):
+        gate, down, _ = lax.optimization_barrier((w_gate, w_down, got))
         stacked.append(jnp.stack([gate, w_up, down.T]))
-        return sent
-
-    entering = scan_states(n_seq, local, decay, sent, False, tie=stack_weights)
+        return state
+
+    entering = scan_states(n_seq, local, decay, sent, False, ties=[stack_weights])
     full = lax.all_gather(stacked[0], "seq")
 
     def chunk_rows(m, t, columns, back):
@@ -729,7 +750,7 @@
             (width // columns // 2,),
             [pl.BlockSpec((rows, 2 * columns), lambda j: (0, j))] + [fixed((TILE, units))] * len(acts),
             pl.BlockSpec((2 * group, span, units), lambda j: (j, 0, 0)),
-            shaped((n_seq, span, units), bf16),
+            shaped((n_seq, span, units + 2 * head), bf16),
             cost=cost(2 * rows * width * units, 2 * (rows * width + rows * units + width * units)),
         )(cot, *acts)
 
@@ -798,8 +819,8 @@
         names = list(live)
         live.update(zip(names, line.step([live[n] for n in names])))
 
-    def end(coming=None, done=None):
-        total = line.join(coming)
+    def end(coming=None, done=None, after=()):
+        total = line.join(coming, after)
         if done is not None:
             live[done] = total
 
@@ -880,11 +901,9 @@
     start()
     wide_shares = lax.psum_scatter(live.pop("wide_grads"), "seq", scatter_dimension=0)
     go_back(0, 0)
-    live["down_grads"] = down_grads(taken("act"))
+    go_back(0, 1)
     end(live.pop(("ffn_part", 0, 1)), ("dhn", 1, 0))
     start()
-    down_shares = lax.psum_scatter(live.pop("down_grads"), "seq", scatter_dimension=0)
-    go_back(0, 1)
     go_back(1, 0)
     end(live.pop(("ffn_part", 1, 0)), ("dhn", 1, 1))
     start()
@@ -903,29 +922,43 @@
     piece_whole = [fixed((TILE, head))] * len(every)
     made = []
 
-    def next_step(sent):
+    def beside_first(state, got):
         live["xn"] = xn
-        end(behind_of(live.pop(("ffn_part", 1, 1)), sent), ("ffn", 0, 0))
+        end(behind_of(live.pop(("ffn_part", 1, 1)), got), ("ffn", 0, 0))
         start()
-        made.append(query_gradients(live.pop("xn")))
-        return sent
-
-    query_gradients = lambda xn: call(
-        "query_grads",
-        functools.partial(query_grad_kernel, len(every)),
-        (width // TILE,),
-        xn_columns + piece_columns + piece_whole * 2,
-        pl.BlockSpec((TILE, 2 * head), lambda j: (j, 0)),
-        shaped((width, 2 * head), bf16),
-        cost=cost(4 * rows * width * head, 4 * rows * width + 4 * rows * head + 4 * width * head),
-    )(xn, *[backs[key][0] for key in every], *[backs[key][1] for key in every],
-      *[reads[key][0] for key in every])
-    live["leaving"] = scan_states(n_seq, *folded, True, own, pieces, next_step, made)
-    live["query_grads"], live["wide"] = made[0], wide_shares
+        made.append(live.pop("xn"))
+        return state
+
+    def beside_second(state, got):
+        acts = taken("act")
+        acts[0] = behind_of(acts[0], state)
+        made.append(down_grads(acts))
+        return behind_of(state, made[1])
+
+    def beside_third(state, got):
+        grads = call(
+            "query_grads",
+            functools.partial(query_grad_kernel, len(every), units),
+            (width // columns,),
+            xn_columns + piece_columns + piece_whole * 2 + [anywhere],
+            anywhere,
+            shaped((n_seq, span, units + 2 * head), bf16),
+            [pltpu.VMEM((2, group, span, 2 * head), bf16), pltpu.SemaphoreType.DMA((2,))],
+            cost=cost(4 * rows * width * head, 4 * rows * width + 4 * rows * head + 4 * width * head),
+            aliases={1 + 3 * len(every): 0},
+        )(behind_of(made[0], state), *[backs[key][0] for key in every], *[backs[key][1] for key in every],
+          *[reads[key][0] for key in every], made[1])
+        made.append(grads)
+        return behind_of(state, grads)
+
+    ties = [beside_first, beside_second, beside_third]
+    live["leaving"] = scan_states(n_seq, *folded, True, own, pieces, ties)
+    live["query_grads"], live["wide"] = made[2], wide_shares
     go_last(0, 0)
     end(live.pop(("dxn_part", 0, 0)), ("ffn", 0, 1))
     start()
     wide_shares = live.pop("wide")
+    down_shares = lax.psum_scatter(live.pop("query_grads"), "seq", scatter_dimension=0)
     go_last(0, 1)
     go_last(1, 0)
     go_last(1, 1)
@@ -938,24 +971,20 @@
         "state_grads",
         functools.partial(state_grad_kernel, len(every)),
         (width // TILE,),
-        xn_columns + piece_whole * 2 + [fixed((TILE, slots))] * len(every) + [fixed((8, slots))] * len(every) + few * 2
-        + [pl.BlockSpec((TILE, 2 * head), lambda j: (j, 0))],
-        pl.BlockSpec((group, span + 16, 4 * head + 128), lambda j: (j, 0, 0)),
-        shaped((n_seq, span + 16, 4 * head + 128), bf16),
+        xn_columns + piece_whole * 2 + [fixed((TILE, slots))] * len(every) + [fixed((8, slots))] * len(every) + few * 2,
+        pl.BlockSpec((group, span + 16, 2 * head + 128), lambda j: (j, 0, 0)),
+        shaped((n_seq, span + 16, 2 * head + 128), bf16),
         cost=cost(4 * rows * width * head, 2 * rows * width + 4 * rows * head + 4 * width * head),
-    )(live.pop("xn"), *[lasts[key][i] for i in (0, 1, 2, 4, 5) for key in every], *[backs[key][9] for key in every],
-      live.pop("query_grads"))
-    live["down"] = down_shares
+    )(live.pop("xn"), *[lasts[key][i] for i in (0, 1, 2, 4, 5) for key in every], *[backs[key][9] for key in every])
     end(live.pop(("dxn_part", 1, 0)), ("ffn", 1, 1))
     start()
-    down_shares = live.pop("down")
     attn_shares = lax.psum_scatter(live.pop("state_grads"), "seq", scatter_dimension=0)
     finish_out(0, 0)
     finish_out(0, 1)
-    live["out"] = outs[0]
+    live["out"], live["down"] = outs[0], down_shares
     end(live.pop(("dxn_part", 1, 1)), ("dxn", 0, 0))
     start()
-    outs[0] = live.pop("out")
+    outs[0], down_shares = live.pop("out"), live.pop("down")
     finish_out(1, 0)
     finish_out(1, 1)
     finish_grad(0, 0)
@@ -964,32 +993,34 @@
     start()
     in_grads[0] = live.pop("in_grad")
     finish_grad(0, 1)
-    live["in_grad"], live["attn"] = in_grads[0], attn_shares
+    live["in_grad"] = in_grads[0]
     end(None, ("dxn", 1, 0))
     start()
-    in_grads[0], late = live.pop("in_grad"), live.pop("attn").astype(f32)
-    gain1_total = late[:span, 4 * head + slots + 1]
+    in_grads[0] = live.pop("in_grad")
+    late = behind_of(attn_shares, in_grads[0]).astype(f32)
+    gain1_total = late[:span, 2 * head + slots + 1]
     others = [lax.ppermute(gain1_total, "head", [(i, i ^ d) for i in range(n_head)]) for d in (1, 2, 3)]
     gain1_total = (gain1_total + others[0]) + (others[1] + others[2])
     finish_grad(1, 0)
-    end(None, ("dxn", 1, 1))
+    end(None, ("dxn", 1, 1), (gain1_total, in_grads[0]))
     finish_grad(1, 1)
-    small_shares = late[:, 4 * head :]
+    small_shares = late[:, 2 * head :]
+    query_shares = down_shares[:, units:].astype(f32)
 
     return (
         live["out"],
         in_grads[0],
         gain1_total,
+        query_shares[:, :head],
         late[:span, :head],
-        late[:span, 2 * head : 3 * head],
-        late[:span, 3 * head : 4 * head],
+        late[:span, head : 2 * head],
         small_shares[:span, :slots],
         small_shares[span, :slots] + small_shares[span + 1, :slots],
-        late[:span, head : 2 * head].T,
+        query_shares[:, head:].T,
         small_shares[:span, slots],
         wide_shares[0].astype(f32),
         wide_shares[1].astype(f32),
-        down_shares.astype(f32).T,
+        down_shares[:, :units].astype(f32).T,
     )
 
 

time: 556 us -> 550 us (0.989)
  the two profiles are of different devices: /device:TPU:0 before, /device:TPU:2 now
where the time goes in v7:
time: 550 us; the launch traced here: 541 us
  Pallas kernels  287 us (52%)
  waiting for transfers between devices  113 us (21%)
  starting transfers between devices  83.8 us (15%)
  local copies, waits for them, and re-layouts  32.8 us (6%)
  between operations  15.1 us (3%)
  other arithmetic  10.3 us (2%)
    pallas_call x30, Pallas kernels, run(): function(*[o if i in loose or spec.memory_space == pltpu.SMEM else pltpu....  264 us
    ppermute x18, waiting for transfers between devices, step(): outer = lax.ppermute(payload, 'head', way)  89.2 us
    ppermute x18, starting transfers between devices, step(): outer = lax.ppermute(payload, 'head', way)  55.2 us
    unnamed x111, local copies, waits for them, and re-layouts  30.2 us
    pallas_call x25, Pallas kernels, in_vmem(): pl.pallas_call(kernel, name=name, in_specs=[pl.BlockSpec(memory_space=plt...  22.7 us
    ppermute x6, waiting for transfers between devices, scan_states(): got = lax.ppermute(sent, 'seq', [(i, i ^ bit) for i in range(n)])  18.3 us
    ppermute x16, starting transfers between devices, step(): middle = lax.ppermute(pair, 'head', self.MIDDLE)  16.8 us
  transfers between devices with their start and end apart: 47, of which 14 were waited for; matrix products, arithmetic and copies ran while one was open for 3% of the time, Pallas kernels for 49%

profile of v7, /device:TPU:2, one launch (start us, length us, event | category | flops | bytes accessed | tf_op | source)
XLA Modules:
  0.0 541.4 jit_solution(4416959099752243304)
XLA Ops:
  7.2 14.9 %project.1 = (bf16[1024,2048]{1,0:T(8,128)(2,1)}, bf16[1024,512]{1,0:T(8,128)(2,1)}, bf16[1024,512]{1,0:T(8,128)(2,1)}, f32[1024,64]{1,0:T(8,128)}, f32[1024,64]...) custom-call(bf16[1024,2048]{1,0:T(8,128)(2,1)} %bitcast.35, ...), custom_call_target="tpu_custom_call" | custom-call | flops 4563402752 | bytes 16777216 | tf_op jit(solution)/shard_map/project/pallas_call | solution.py:62
  24.1 2.7 pad_maximum_fusion
  27.2 9.0 %collective-permute-done.1.refs_2_ = bf16[2,64,1152]{2,1,0:T(8,128)(2,1)S(1)} collective-permute-done((bf16[2,64,1152]{2,1,0:T(8,128)(2,1)S(1)}, bf16[2,64,1152]{2,1,0:T(8,128)(2,1)S(1)}, u32[]{:S(2)}, u32[]{:S(2)}) %collective-permute-start.1) | collective-permute-done | bytes 294944 | tf_op jit(solution)/shard_map/ppermute | solution.py:521
  38.1 6.6 %query.1.q_ref = bf16[1024,512]{1,0:T(8,128)(2,1)} custom-call(bf16[1024,2048]{1,0:T(8,128)(2,1)} %get-tuple-element.731.xn_ref.refs_0_, bf16[2048,512]{1,0:T(8,128)(2,1)} %wq_ref.9), custom_call_target="tpu_custom_call" | custom-call | flops 2147483648 | bytes 7340032 | tf_op jit(solution)/shard_map/query/pallas_call | solution.py:62
  44.7 6.1 %collective-permute-done.2.refs_2_ = bf16[2,64,1152]{2,1,0:T(8,128)(2,1)S(1)} collective-permute-done((bf16[2,64,1152]{2,1,0:T(8,128)(2,1)S(1)}, bf16[2,64,1152]{2,1,0:T(8,128)(2,1)S(1)}, u32[]{:S(2)}, u32[]{:S(2)}) %collective-permute-start.2) | collective-permute-done | bytes 294944 | tf_op jit(solution)/shard_map/ppermute | solution.py:521
  51.1 5.3 read.4
  56.4 3.6 collective-permute-start.3
  60.0 5.3 read.5
  65.3 13.6 %collective-permute-done.3.refs_1_ = bf16[256,2048]{1,0:T(8,128)(2,1)S(1)} collective-permute-done((bf16[256,2048]{1,0:T(8,128)(2,1)S(1)}, bf16[256,2048]{1,0:T(8,128)(2,1)S(1)}, u32[]{:S(2)}, u32[]{:S(2)}) %collective-permute-start.3) | collective-permute-done | bytes 1048608 | tf_op jit(solution)/shard_map/ppermute | solution.py:601
  79.0 4.5 collective-permute-start.4
  84.2 5.2 read.6
  89.5 12.6 %collective-permute-done.4.refs_1_ = bf16[256,2048]{1,0:T(8,128)(2,1)S(1)} collective-permute-done((bf16[256,2048]{1,0:T(8,128)(2,1)S(1)}, bf16[256,2048]{1,0:T(8,128)(2,1)S(1)}, u32[]{:S(2)}, u32[]{:S(2)}) %collective-permute-start.4) | collective-permute-done | bytes 1048608 | tf_op jit(solution)/shard_map/ppermute | solution.py:601
  102.2 3.8 collective-permute-start.6
  106.8 5.4 read.7
  112.1 12.1 %collective-permute-done.6.refs_1_ = bf16[256,2048]{1,0:T(8,128)(2,1)S(1)} collective-permute-done((bf16[256,2048]{1,0:T(8,128)(2,1)S(1)}, bf16[256,2048]{1,0:T(8,128)(2,1)S(1)}, u32[]{:S(2)}, u32[]{:S(2)}) %collective-permute-start.6) | collective-permute-done | bytes 1048608 | tf_op jit(solution)/shard_map/ppermute | solution.py:601
  125.5 3.8 collective-permute-start.8
  132.7 19.5 %feed.4 = (bf16[256,2048]{1,0:T(8,128)(2,1)}, bf16[256,2048]{1,0:T(8,128)(2,1)}, bf16[256,1408]{1,0:T(8,128)(2,1)}, bf16[256,1408]{1,0:T(8,128)(2,1)}, bf16[256,...) custom-call(bf16[1024,2048]{1,0:T(8,128)(2,1)} %bitcast.36, ...), custom_call_target="tpu_custom_call" | custom-call | flops 8858370048 | bytes 24641536 | tf_op jit(solution)/shard_map/feed/pallas_call | solution.py:62
  153.9 2.3 collective-permute-start.10
  157.1 19.5 %feed.5 = (bf16[256,2048]{1,0:T(8,128)(2,1)}, bf16[256,2048]{1,0:T(8,128)(2,1)}, bf16[256,1408]{1,0:T(8,128)(2,1)}, bf16[256,1408]{1,0:T(8,128)(2,1)}, bf16[256,...) custom-call(bf16[1024,2048]{1,0:T(8,128)(2,1)} %bitcast.37, ...), custom_call_target="tpu_custom_call" | custom-call | flops 8858370048 | bytes 24641536 | tf_op jit(solution)/shard_map/feed/pallas_call | solution.py:62
  176.8 3.0 collective-permute-start.12
  180.7 19.5 %feed.6 = (bf16[256,2048]{1,0:T(8,128)(2,1)}, bf16[256,2048]{1,0:T(8,128)(2,1)}, bf16[256,1408]{1,0:T(8,128)(2,1)}, bf16[256,1408]{1,0:T(8,128)(2,1)}, bf16[256,...) custom-call(bf16[1024,2048]{1,0:T(8,128)(2,1)} %bitcast.38, ...), custom_call_target="tpu_custom_call" | custom-call | flops 8858370048 | bytes 24641536 | tf_op jit(solution)/shard_map/feed/pallas_call | solution.py:62
  203.6 19.5 %feed.7 = (bf16[256,2048]{1,0:T(8,128)(2,1)}, bf16[256,2048]{1,0:T(8,128)(2,1)}, bf16[256,1408]{1,0:T(8,128)(2,1)}, bf16[256,1408]{1,0:T(8,128)(2,1)}, bf16[256,...) custom-call(bf16[1024,2048]{1,0:T(8,128)(2,1)} %bitcast.39, ...), custom_call_target="tpu_custom_call" | custom-call | flops 8858370048 | bytes 24641536 | tf_op jit(solution)/shard_map/feed/pallas_call | solution.py:62
  224.6 2.7 collective-permute-start.16
  228.9 19.1 %wide_grads.1 = bf16[8,2,256,1408]{3,2,1,0:T(8,128)(2,1)} custom-call(bf16[256,2048]{1,0:T(8,128)(2,1)} %get-tuple-element.553.refs_0_, bf16[256,2048]{1,0:T(8,128)(2,1)} %get-tuple-element.554.refs_1_, bf16[256,2048]{1,0:T(8,128)(2,1)} %get-tuple-element.555.refs_2_, bf16[256,2048]{1,0:T(8,128)(2,1)} %get-tuple-element.556.refs_3_, ...), custom_call_target="tpu_custom_call" | custom-call | flops 11811160064 | bytes 21495808 | tf_op jit(solution)/shard_map/wide_grads/pallas_call | solution.py:62
  248.0 2.3 join.25
  255.6 8.4 %back.4 = (bf16[256,2048]{1,0:T(8,128)(2,1)}, bf16[256,512]{1,0:T(8,128)(2,1)}, f32[256,512]{1,0:T(8,128)}, f32[256,512]{1,0:T(8,128)}, f32[256,64]{1,0:T(8,128)...) custom-call(bf16[256,2048]{1,0:T(8,128)(2,1)S(1)} %get-tuple-element, ...), custom_call_target="tpu_custom_call" | custom-call | flops 930086912 | bytes 9961472 | tf_op jit(solution)/shard_map/back/pallas_call | solution.py:62
  264.1 9.7 %back.5 = (bf16[256,2048]{1,0:T(8,128)(2,1)}, bf16[256,512]{1,0:T(8,128)(2,1)}, f32[256,512]{1,0:T(8,128)}, f32[256,512]{1,0:T(8,128)}, f32[256,64]{1,0:T(8,128)...) custom-call(bf16[256,2048]{1,0:T(8,128)(2,1)S(1)} %copy-done.15, ...), custom_call_target="tpu_custom_call" | custom-call | flops 930086912 | bytes 9961472 | tf_op jit(solution)/shard_map/back/pallas_call | solution.py:62
  274.1 3.9 collective-permute-start.20
  278.7 8.3 %back.6 = (bf16[256,2048]{1,0:T(8,128)(2,1)}, bf16[256,512]{1,0:T(8,128)(2,1)}, f32[256,512]{1,0:T(8,128)}, f32[256,512]{1,0:T(8,128)}, f32[256,64]{1,0:T(8,128)...) custom-call(bf16[256,2048]{1,0:T(8,128)(2,1)S(1)} %get-tuple-element, ...), custom_call_target="tpu_custom_call" | custom-call | flops 930086912 | bytes 9961472 | tf_op jit(solution)/shard_map/back/pallas_call | solution.py:62
  287.0 10.5 %collective-permute-done.20.refs_1_ = bf16[256,2048]{1,0:T(8,128)(2,1)S(1)} collective-permute-done((bf16[256,2048]{1,0:T(8,128)(2,1)S(1)}, bf16[256,2048]{1,0:T(8,128)(2,1)S(1)}, u32[]{:S(2)}, u32[]{:S(2)}) %collective-permute-start.20) | collective-permute-done | bytes 1048608 | tf_op jit(solution)/shard_map/ppermute | solution.py:601
  297.6 4.0 collective-permute-start.23
  302.4 8.3 %back.7 = (bf16[256,2048]{1,0:T(8,128)(2,1)}, bf16[256,512]{1,0:T(8,128)(2,1)}, f32[256,512]{1,0:T(8,128)}, f32[256,512]{1,0:T(8,128)}, f32[256,64]{1,0:T(8,128)...) custom-call(bf16[256,2048]{1,0:T(8,128)(2,1)S(1)} %get-tuple-element, ...), custom_call_target="tpu_custom_call" | custom-call | flops 930086912 | bytes 9961472 | tf_op jit(solution)/shard_map/back/pallas_call | solution.py:62
  313.3 4.2 collective-permute-done.23.refs_1_
  320.0 3.9 collective-permute-start.25
  325.7 10.7 %down_grads.1.refs_13_ = bf16[8,256,2432]{2,1,0:T(8,128)(2,1)} custom-call(bf16[1024,2048]{1,0:T(8,128)(2,1)} %bitcast.56, bf16[256,1408]{1,0:T(8,128)(2,1)} %get-tuple-element.643.refs_1_, bf16[256,1408]{1,0:T(8,128)(2,1)} %get-tuple-element.644.refs_2_, bf16[256,1408]{1,0:T(8,128)(2,1)} %get-tuple-element.645.refs_3_, ...), custom_call_target="tpu_custom_call" | custom-call | flops 5905580032 | bytes 12845056 | tf_op jit(solution)/shard_map/down_grads/pallas_call | solution.py:62
  339.5 3.6 collective-permute-start.28
  343.1 11.1 %query_grads.1 = bf16[8,256,2432]{2,1,0:T(8,128)(2,1)} custom-call(bf16[1024,2048]{1,0:T(8,128)(2,1)} %get-tuple-element.731.xn_ref.refs_0_, bf16[256,2048]{1,0:T(8,128)(2,1)} %get-tuple-element.655.refs_1_.dhid_ref, bf16[256,2048]{1,0:T(8,128)(2,1)} %get-tuple-element.656.refs_2_.dhid_ref, ...), custom_call_target="tpu_custom_call", output_to_operand_aliasing={{}: (13, {})} | custom-call | flops 4294967296 | bytes 14680064 | tf_op jit(solution)/shard_map/query_grads/pallas_call | solution.py:62
  359.1 8.1 %last.4 = (bf16[256,512]{1,0:T(8,128)(2,1)}, bf16[256,512]{1,0:T(8,128)(2,1)}, bf16[256,64]{1,0:T(8,128)(2,1)}, bf16[256,2048]{1,0:T(8,128)(2,1)S(1)}, f32[8,64]{1,0:T(8,128)}, /*index=5*/f32[8,2048]{1,0:T(8,128)}) custom-call(f32[4,64,1024]{2,1,0:T(8,128)S(1)} %hop.11.l0_ref, bf16[1024,512]{1,0:T(8,128)(2,1)} %get-tuple-element.407.k_ref, ...), custom_call_target="tpu_custom_call" | custom-call | flops 1677721600 | bytes 13107200 | tf_op jit(solution)/shard_map/last/pallas_call | solution.py:62
  367.2 3.6 join.29
  375.4 8.7 %last.7 = (bf16[256,512]{1,0:T(8,128)(2,1)}, bf16[256,512]{1,0:T(8,128)(2,1)}, bf16[256,64]{1,0:T(8,128)(2,1)}, bf16[256,2048]{1,0:T(8,128)(2,1)S(1)}, f32[8,64]{1,0:T(8,128)}, /*index=5*/f32[8,2048]{1,0:T(8,128)}) custom-call(f32[4,64,1024]{2,1,0:T(8,128)S(1)} %hop.11.l0_ref, bf16[1024,512]{1,0:T(8,128)(2,1)} %get-tuple-element.407.k_ref, ...), custom_call_target="tpu_custom_call" | custom-call | flops 1677721600 | bytes 13107200 | tf_op jit(solution)/shard_map/last/pallas_call | solution.py:62
  384.1 9.5 %last.6 = (bf16[256,512]{1,0:T(8,128)(2,1)}, bf16[256,512]{1,0:T(8,128)(2,1)}, bf16[256,64]{1,0:T(8,128)(2,1)}, bf16[256,2048]{1,0:T(8,128)(2,1)S(1)}, f32[8,64]{1,0:T(8,128)}, /*index=5*/f32[8,2048]{1,0:T(8,128)}) custom-call(f32[4,64,1024]{2,1,0:T(8,128)S(1)} %hop.11.l0_ref, bf16[1024,512]{1,0:T(8,128)(2,1)} %get-tuple-element.407.k_ref, ...), custom_call_target="tpu_custom_call" | custom-call | flops 1677721600 | bytes 13107200 | tf_op jit(solution)/shard_map/last/pallas_call | solution.py:62
  393.6 8.4 %last.5 = (bf16[256,512]{1,0:T(8,128)(2,1)}, bf16[256,512]{1,0:T(8,128)(2,1)}, bf16[256,64]{1,0:T(8,128)(2,1)}, bf16[256,2048]{1,0:T(8,128)(2,1)S(1)}, f32[8,64]{1,0:T(8,128)}, /*index=5*/f32[8,2048]{1,0:T(8,128)}) custom-call(f32[4,64,1024]{2,1,0:T(8,128)S(1)} %hop.11.l0_ref, bf16[1024,512]{1,0:T(8,128)(2,1)} %get-tuple-element.407.k_ref, ...), custom_call_target="tpu_custom_call" | custom-call | flops 1677721600 | bytes 13107200 | tf_op jit(solution)/shard_map/last/pallas_call | solution.py:62
  402.1 3.6 join.30
  406.7 4.1 collective-permute-start.31
  412.4 11.5 %state_grads.1 = bf16[8,272,1152]{2,1,0:T(8,128)(2,1)} custom-call(bf16[1024,2048]{1,0:T(8,128)(2,1)} %get-tuple-element.731.xn_ref.refs_0_, bf16[256,512]{1,0:T(8,128)(2,1)} %get-tuple-element.732.refs_1_, bf16[256,512]{1,0:T(8,128)(2,1)} %get-tuple-element.733.refs_2_, bf16[256,512]{1,0:T(8,128)(2,1)} %get-tuple-element.734.refs_3_, ...), custom_call_target="tpu_custom_call" | custom-call | flops 4294967296 | bytes 10485760 | tf_op jit(solution)/shard_map/state_grads/pallas_call | solution.py:62
  423.9 2.2 collective-permute-done.31.refs_1_
  426.1 2.3 join.31
  431.4 3.8 collective-permute-start.33
  438.1 2.3 out.5.refs_0_
  440.4 9.1 %collective-permute-done.33.refs_1_ = bf16[256,2048]{1,0:T(8,128)(2,1)S(1)} collective-permute-done((bf16[256,2048]{1,0:T(8,128)(2,1)}, bf16[256,2048]{1,0:T(8,128)(2,1)S(1)}, u32[]{:S(2)}, u32[]{:S(2)}) %collective-permute-start.33) | collective-permute-done | bytes 1048608 | tf_op jit(solution)/shard_map/ppermute | solution.py:601
  451.6 3.9 collective-permute-start.35
  457.5 3.1 in_grad.4.refs_0_
  460.6 2.3 out.6.refs_0_
  462.9 2.3 out.7
  465.2 10.6 %collective-permute-done.35.refs_1_ = bf16[256,2048]{1,0:T(8,128)(2,1)S(1)} collective-permute-done((bf16[256,2048]{1,0:T(8,128)(2,1)}, bf16[256,2048]{1,0:T(8,128)(2,1)S(1)}, u32[]{:S(2)}, u32[]{:S(2)}) %collective-permute-start.35) | collective-permute-done | bytes 1048608 | tf_op jit(solution)/shard_map/ppermute | solution.py:601
  483.4 2.9 copy.48
  486.3 3.2 in_grad.5.refs_0_
  489.5 14.3 %collective-permute-done.37.refs_0_ = bf16[256,2048]{1,0:T(8,128)(2,1)S(1)} collective-permute-done((bf16[256,2048]{1,0:T(8,128)(2,1)}, bf16[256,2048]{1,0:T(8,128)(2,1)S(1)}, u32[]{:S(2)}, u32[]{:S(2)}) %collective-permute-start.37) | collective-permute-done | bytes 1048608 | tf_op jit(solution)/shard_map/ppermute | solution.py:601
  507.7 2.2 slice_convert_fusion
  511.9 3.3 collective-permute-start.42
  515.2 2.2 collective-permute-start.41
  522.3 3.2 in_grad.6.refs_0_
  525.5 5.1 collective-permute-done.40
  531.3 3.2 in_grad.7
  (211 shorter events, 78.9 us)
Async XLA Ops:
  7.2 124.3 %all-gather.3.cloned.1.call-start = ((), (), s32[]{:S(2)}) async-start(), calls=%async_computation.6 | async-start | bytes 19464192 | tf_op jit(solution)/shard_map/all_gather | solution.py:686
  7.2 16.5 %copy-start.52 = (bf16[1408,256]{1,0:T(8,128)(2,1)S(1)}, bf16[1408,256]{1,0:T(8,128)(2,1)}, u32[]{:S(2)}) copy-start(bf16[1408,256]{1,0:T(8,128)(2,1)} %param.24) | copy-start | bytes 2162692
  7.2 16.8 %copy-start.53 = (bf16[256,1408]{1,0:T(8,128)(2,1)S(1)}, bf16[256,1408]{1,0:T(8,128)(2,1)}, u32[]{:S(2)}) copy-start(bf16[256,1408]{1,0:T(8,128)(2,1)} %param.23) | copy-start | bytes 2162692
  22.1 1.6 collective-permute-start
  26.8 346.0 %reduce-scatter.4.cloned.1.call-start = ((), (), s32[]{:S(2)}) async-start(), calls=%async_computation.3 | async-start | bytes 12976128 | tf_op jit(solution)/shard_map/reduce_scatter | solution.py:902
  27.1 9.1 %collective-permute-start.1 = (bf16[2,64,1152]{2,1,0:T(8,128)(2,1)S(1)}, bf16[2,64,1152]{2,1,0:T(8,128)(2,1)S(1)}, u32[]{:S(2)}, u32[]{:S(2)}) collective-permute-start(bf16[2,64,1152]{2,1,0:T(8,128)(2,1)S(1)} %get-tuple-element.416), channel_id=1, source_target_pairs={{0,8},{4,12},{8,0},{12,4},{16,24},{20,28},{24,16},{28,20},{1,9},{5... | collective-permute-start | bytes 884744 | tf_op jit(solution)/shard_map/ppermute | solution.py:521
  36.5 14.3 %collective-permute-start.2 = (bf16[2,64,1152]{2,1,0:T(8,128)(2,1)S(1)}, bf16[2,64,1152]{2,1,0:T(8,128)(2,1)S(1)}, u32[]{:S(2)}, u32[]{:S(2)}) collective-permute-start(bf16[2,64,1152]{2,1,0:T(8,128)(2,1)S(1)} %get-tuple-element.421), channel_id=1, source_target_pairs={{0,16},{4,20},{8,24},{12,28},{16,0},{20,4},{24,8},{28,12},{1,17},{... | collective-permute-start | bytes 884744 | tf_op jit(solution)/shard_map/ppermute | solution.py:521
  56.4 22.5 %collective-permute-start.3 = (bf16[256,2048]{1,0:T(8,128)(2,1)S(1)}, bf16[256,2048]{1,0:T(8,128)(2,1)S(1)}, u32[]{:S(2)}, u32[]{:S(2)}) collective-permute-start(bf16[256,2048]{1,0:T(8,128)(2,1)S(1)} %get-tuple-element.428.refs_0_), channel_id=1, source_target_pairs={{0,1},{3,2},{4,5},{7,6},{8,9},{11,10},{12,13},{15,14},{16,17},{19,... | collective-permute-start | bytes 3145736 | tf_op jit(solution)/shard_map/ppermute | solution.py:601
  79.0 23.1 %collective-permute-start.4 = (bf16[256,2048]{1,0:T(8,128)(2,1)S(1)}, bf16[256,2048]{1,0:T(8,128)(2,1)S(1)}, u32[]{:S(2)}, u32[]{:S(2)}) collective-permute-start(bf16[256,2048]{1,0:T(8,128)(2,1)S(1)} %get-tuple-element.432), channel_id=1, source_target_pairs={{0,1},{3,2},{4,5},{7,6},{8,9},{11,10},{12,13},{15,14},{16,17},{19,... | collective-permute-start | bytes 3145736 | tf_op jit(solution)/shard_map/ppermute | solution.py:601
  83.5 18.6 %collective-permute-start.5 = (bf16[256,2048]{1,0:T(8,128)(2,1)S(1)}, bf16[256,2048]{1,0:T(8,128)(2,1)S(1)}, u32[]{:S(2)}, u32[]{:S(2)}) collective-permute-start(bf16[256,2048]{1,0:T(8,128)(2,1)S(1)} %get-tuple-element.433.refs_2_), channel_id=1, source_target_pairs={{1,2},{2,1},{5,6},{6,5},{9,10},{10,9},{13,14},{14,13},{17,18},{18,... | collective-permute-start | bytes 3145736 | tf_op jit(solution)/shard_map/ppermute | solution.py:604
  102.2 22.1 %collective-permute-start.6 = (bf16[256,2048]{1,0:T(8,128)(2,1)S(1)}, bf16[256,2048]{1,0:T(8,128)(2,1)S(1)}, u32[]{:S(2)}, u32[]{:S(2)}) collective-permute-start(bf16[256,2048]{1,0:T(8,128)(2,1)S(1)} %get-tuple-element.441.refs_4_), channel_id=1, source_target_pairs={{0,1},{3,2},{1,0},{2,3},{4,5},{7,6},{5,4},{6,7},{8,9},{11,10},{9,8... | collective-permute-start | bytes 3145736 | tf_op jit(solution)/shard_map/ppermute | solution.py:601
  106.0 18.3 %collective-permute-start.7 = (bf16[256,2048]{1,0:T(8,128)(2,1)S(1)}, bf16[256,2048]{1,0:T(8,128)(2,1)S(1)}, u32[]{:S(2)}, u32[]{:S(2)}) collective-permute-start(bf16[256,2048]{1,0:T(8,128)(2,1)S(1)} %get-tuple-element.442.refs_2_), channel_id=1, source_target_pairs={{1,2},{2,1},{5,6},{6,5},{9,10},{10,9},{13,14},{14,13},{17,18},{18,... | collective-permute-start | bytes 3145736 | tf_op jit(solution)/shard_map/ppermute | solution.py:604
  125.5 26.7 %collective-permute-start.8 = (bf16[256,2048]{1,0:T(8,128)(2,1)S(1)}, bf16[256,2048]{1,0:T(8,128)(2,1)}, u32[]{:S(2)}, u32[]{:S(2)}) collective-permute-start(bf16[256,2048]{1,0:T(8,128)(2,1)S(1)} %get-tuple-element.446.refs_4_), channel_id=1, source_target_pairs={{0,1},{3,2},{1,0},{2,3},{4,5},{7,6},{5,4},{6,7},{8,9},{11,10},{9,8... | collective-permute-start | bytes 3145736 | tf_op jit(solution)/shard_map/ppermute | solution.py:601
  129.3 22.9 %collective-permute-start.9 = (bf16[256,2048]{1,0:T(8,128)(2,1)S(1)}, bf16[256,2048]{1,0:T(8,128)(2,1)}, u32[]{:S(2)}, u32[]{:S(2)}) collective-permute-start(bf16[256,2048]{1,0:T(8,128)(2,1)S(1)} %get-tuple-element.447.refs_2_), channel_id=1, source_target_pairs={{1,2},{2,1},{5,6},{6,5},{9,10},{10,9},{13,14},{14,13},{17,18},{18,... | collective-permute-start | bytes 3145736 | tf_op jit(solution)/shard_map/ppermute | solution.py:604
  153.9 22.7 %collective-permute-start.10 = (bf16[256,2048]{1,0:T(8,128)(2,1)S(1)}, bf16[256,2048]{1,0:T(8,128)(2,1)S(1)}, u32[]{:S(2)}, u32[]{:S(2)}) collective-permute-start(bf16[256,2048]{1,0:T(8,128)(2,1)S(1)} %get-tuple-element.463.refs_4_), channel_id=1, source_target_pairs={{0,1},{3,2},{1,0},{2,3},{4,5},{7,6},{5,4},{6,7},{8,9},{11,10},{9,8... | collective-permute-start | bytes 3145736 | tf_op jit(solution)/shard_map/ppermute | solution.py:601
  156.2 20.4 %collective-permute-start.11 = (bf16[256,2048]{1,0:T(8,128)(2,1)S(1)}, bf16[256,2048]{1,0:T(8,128)(2,1)S(1)}, u32[]{:S(2)}, u32[]{:S(2)}) collective-permute-start(bf16[256,2048]{1,0:T(8,128)(2,1)S(1)} %get-tuple-element.464.refs_2_), channel_id=1, source_target_pairs={{1,2},{2,1},{5,6},{6,5},{9,10},{10,9},{13,14},{14,13},{17,18},{18,... | collective-permute-start | bytes 3145736 | tf_op jit(solution)/shard_map/ppermute | solution.py:604
  176.8 23.4 %collective-permute-start.12 = (bf16[256,2048]{1,0:T(8,128)(2,1)S(1)}, bf16[256,2048]{1,0:T(8,128)(2,1)S(1)}, u32[]{:S(2)}, u32[]{:S(2)}) collective-permute-start(bf16[256,2048]{1,0:T(8,128)(2,1)S(1)} %get-tuple-element.480.refs_4_), channel_id=1, source_target_pairs={{0,1},{3,2},{1,0},{2,3},{4,5},{7,6},{5,4},{6,7},{8,9},{11,10},{9,8... | collective-permute-start | bytes 3145736 | tf_op jit(solution)/shard_map/ppermute | solution.py:601
  179.8 20.4 %collective-permute-start.13 = (bf16[256,2048]{1,0:T(8,128)(2,1)S(1)}, bf16[256,2048]{1,0:T(8,128)(2,1)S(1)}, u32[]{:S(2)}, u32[]{:S(2)}) collective-permute-start(bf16[256,2048]{1,0:T(8,128)(2,1)S(1)} %get-tuple-element.481.refs_2_), channel_id=1, source_target_pairs={{1,2},{2,1},{5,6},{6,5},{9,10},{10,9},{13,14},{14,13},{17,18},{18,... | collective-permute-start | bytes 3145736 | tf_op jit(solution)/shard_map/ppermute | solution.py:604
  200.4 22.7 %collective-permute-start.14 = (bf16[256,2048]{1,0:T(8,128)(2,1)S(1)}, bf16[256,2048]{1,0:T(8,128)(2,1)S(1)}, u32[]{:S(2)}, u32[]{:S(2)}) collective-permute-start(bf16[256,2048]{1,0:T(8,128)(2,1)S(1)} %get-tuple-element.507.refs_4_), channel_id=1, source_target_pairs={{0,1},{3,2},{1,0},{2,3},{4,5},{7,6},{5,4},{6,7},{8,9},{11,10},{9,8... | collective-permute-start | bytes 3145736 | tf_op jit(solution)/shard_map/ppermute | solution.py:601
  202.5 20.6 %collective-permute-start.15 = (bf16[256,2048]{1,0:T(8,128)(2,1)S(1)}, bf16[256,2048]{1,0:T(8,128)(2,1)S(1)}, u32[]{:S(2)}, u32[]{:S(2)}) collective-permute-start(bf16[256,2048]{1,0:T(8,128)(2,1)S(1)} %get-tuple-element.508.refs_2_), channel_id=1, source_target_pairs={{1,2},{2,1},{5,6},{6,5},{9,10},{10,9},{13,14},{14,13},{17,18},{18,... | collective-permute-start | bytes 3145736 | tf_op jit(solution)/shard_map/ppermute | solution.py:604
  224.6 23.4 %copy-start.3 = (bf16[256,2048]{1,0:T(8,128)(2,1)S(1)}, bf16[256,2048]{1,0:T(8,128)(2,1)}, u32[]{:S(2)}) copy-start(bf16[256,2048]{1,0:T(8,128)(2,1)} %get-tuple-element.538.refs_5_.refs_0_) | copy-start | bytes 3145732
  224.6 23.4 %collective-permute-start.16 = (bf16[256,2048]{1,0:T(8,128)(2,1)}, bf16[256,2048]{1,0:T(8,128)(2,1)}, u32[]{:S(2)}, u32[]{:S(2)}) collective-permute-start(bf16[256,2048]{1,0:T(8,128)(2,1)} %get-tuple-element.536.refs_4_), channel_id=1, source_target_pairs={{0,1},{3,2},{1,0},{2,3},{4,5},{7,6},{5,4},{6,7},{8,9},{11,10},{9,8... | collective-permute-start | bytes 3145736 | tf_op jit(solution)/shard_map/ppermute | solution.py:601
  227.3 20.7 %collective-permute-start.17 = (bf16[256,2048]{1,0:T(8,128)(2,1)}, bf16[256,2048]{1,0:T(8,128)(2,1)}, u32[]{:S(2)}, u32[]{:S(2)}) collective-permute-start(bf16[256,2048]{1,0:T(8,128)(2,1)} %get-tuple-element.537.refs_2_), channel_id=1, source_target_pairs={{1,2},{2,1},{5,6},{6,5},{9,10},{10,9},{13,14},{14,13},{17,18},{18,... | collective-permute-start | bytes 3145736 | tf_op jit(solution)/shard_map/ppermute | solution.py:604
  253.4 198.3 %reduce-scatter.6.cloned.1.call-start = ((), (), s32[]{:S(2)}) async-start(), calls=%async_computation.4 | async-start | bytes 11206656 | tf_op jit(solution)/shard_map/reduce_scatter | solution.py:961
  253.4 20.4 %collective-permute-start.18 = (bf16[256,2048]{1,0:T(8,128)(2,1)}, bf16[256,2048]{1,0:T(8,128)(2,1)S(1)}, u32[]{:S(2)}, u32[]{:S(2)}) collective-permute-start(bf16[256,2048]{1,0:T(8,128)(2,1)} %copy-done.25), channel_id=1, source_target_pairs={{0,1},{3,2},{1,0},{2,3},{4,5},{7,6},{5,4},{6,7},{8,9},{11,10},{9,8... | collective-permute-start | bytes 3145736 | tf_op jit(solution)/shard_map/ppermute | solution.py:601
  254.7 19.1 %collective-permute-start.19 = (bf16[256,2048]{1,0:T(8,128)(2,1)S(1)}, bf16[256,2048]{1,0:T(8,128)(2,1)S(1)}, u32[]{:S(2)}, u32[]{:S(2)}) collective-permute-start(bf16[256,2048]{1,0:T(8,128)(2,1)S(1)} %copy-done.23), channel_id=1, source_target_pairs={{1,2},{2,1},{5,6},{6,5},{9,10},{10,9},{13,14},{14,13},{17,18},{18,... | collective-permute-start | bytes 3145736 | tf_op jit(solution)/shard_map/ppermute | solution.py:604
  255.6 8.4 %copy-start.15 = (bf16[256,2048]{1,0:T(8,128)(2,1)S(1)}, bf16[256,2048]{1,0:T(8,128)(2,1)}, u32[]{:S(2)}) copy-start(bf16[256,2048]{1,0:T(8,128)(2,1)} %copy-done.14) | copy-start | bytes 3145732
  264.1 9.8 %copy-start.2 = (bf16[256,2048]{1,0:T(8,128)(2,1)S(1)}, bf16[256,2048]{1,0:T(8,128)(2,1)}, u32[]{:S(2)}) copy-start(bf16[256,2048]{1,0:T(8,128)(2,1)} %get-tuple-element.566.refs_5_.refs_0_) | copy-start | bytes 3145732
  264.1 9.8 %copy-start.24 = (bf16[256,2048]{1,0:T(8,128)(2,1)S(1)}, bf16[256,2048]{1,0:T(8,128)(2,1)}, u32[]{:S(2)}) copy-start(bf16[256,2048]{1,0:T(8,128)(2,1)} %copy-done.22) | copy-start | bytes 3145732
  264.1 9.8 %copy-start.26 = (bf16[256,2048]{1,0:T(8,128)(2,1)S(1)}, bf16[256,2048]{1,0:T(8,128)(2,1)}, u32[]{:S(2)}) copy-start(bf16[256,2048]{1,0:T(8,128)(2,1)} %copy-done.25) | copy-start | bytes 3145732
  274.1 23.4 %collective-permute-start.20 = (bf16[256,2048]{1,0:T(8,128)(2,1)S(1)}, bf16[256,2048]{1,0:T(8,128)(2,1)S(1)}, u32[]{:S(2)}, u32[]{:S(2)}) collective-permute-start(bf16[256,2048]{1,0:T(8,128)(2,1)S(1)} %get-tuple-element.592.refs_4_), channel_id=1, source_target_pairs={{0,1},{3,2},{1,0},{2,3},{4,5},{7,6},{5,4},{6,7},{8,9},{11,10},{9,8... | collective-permute-start | bytes 3145736 | tf_op jit(solution)/shard_map/ppermute | solution.py:601
  277.9 19.5 %collective-permute-start.21 = (bf16[256,2048]{1,0:T(8,128)(2,1)S(1)}, bf16[256,2048]{1,0:T(8,128)(2,1)S(1)}, u32[]{:S(2)}, u32[]{:S(2)}) collective-permute-start(bf16[256,2048]{1,0:T(8,128)(2,1)S(1)} %get-tuple-element.593.refs_2_), channel_id=1, source_target_pairs={{1,2},{2,1},{5,6},{6,5},{9,10},{10,9},{13,14},{14,13},{17,18},{18,... | collective-permute-start | bytes 3145736 | tf_op jit(solution)/shard_map/ppermute | solution.py:604
  278.7 18.8 %copy-start.1 = (bf16[256,2048]{1,0:T(8,128)(2,1)S(1)}, bf16[256,2048]{1,0:T(8,128)(2,1)}, u32[]{:S(2)}) copy-start(bf16[256,2048]{1,0:T(8,128)(2,1)} %get-tuple-element.594.refs_5_.refs_0_) | copy-start | bytes 3145732
  297.6 19.9 %collective-permute-start.23 = (bf16[256,2048]{1,0:T(8,128)(2,1)S(1)}, bf16[256,2048]{1,0:T(8,128)(2,1)S(1)}, u32[]{:S(2)}, u32[]{:S(2)}) collective-permute-start(bf16[256,2048]{1,0:T(8,128)(2,1)S(1)} %get-tuple-element.625.refs_4_), channel_id=1, source_target_pairs={{0,1},{3,2},{1,0},{2,3},{4,5},{7,6},{5,4},{6,7},{8,9},{11,10},{9,8... | collective-permute-start | bytes 3145736 | tf_op jit(solution)/shard_map/ppermute | solution.py:601
  301.7 15.9 %collective-permute-start.24 = (bf16[256,2048]{1,0:T(8,128)(2,1)S(1)}, bf16[256,2048]{1,0:T(8,128)(2,1)S(1)}, u32[]{:S(2)}, u32[]{:S(2)}) collective-permute-start(bf16[256,2048]{1,0:T(8,128)(2,1)S(1)} %get-tuple-element.626.refs_2_), channel_id=1, source_target_pairs={{1,2},{2,1},{5,6},{6,5},{9,10},{10,9},{13,14},{14,13},{17,18},{18,... | collective-permute-start | bytes 3145736 | tf_op jit(solution)/shard_map/ppermute | solution.py:604
  310.7 8.4 %copy-start.39 = (f32[64,128]{1,0:T(8,128)}, f32[64,128]{1,0:T(8,128)S(1)}, u32[]{:S(2)}) copy-start(f32[64,128]{1,0:T(8,128)S(1)} %get-tuple-element.622.refs_7_.refs_12_) | copy-start | bytes 98308
  310.8 1.6 collective-permute-start.22
  312.7 23.7 %collective-permute-start.27 = (bf16[2,64,1152]{2,1,0:T(8,128)(2,1)S(1)}, bf16[2,64,1152]{2,1,0:T(8,128)(2,1)S(1)}, u32[]{:S(2)}, u32[]{:S(2)}) collective-permute-start(bf16[2,64,1152]{2,1,0:T(8,128)(2,1)S(1)} %get-tuple-element.649), channel_id=1, source_target_pairs={{0,8},{4,12},{8,0},{12,4},{16,24},{20,28},{24,16},{28,20},{1,9},{5... | collective-permute-start | bytes 884744 | tf_op jit(solution)/shard_map/ppermute | solution.py:521
  320.0 47.1 %collective-permute-start.25 = (bf16[256,2048]{1,0:T(8,128)(2,1)}, bf16[256,2048]{1,0:T(8,128)(2,1)}, u32[]{:S(2)}, u32[]{:S(2)}) collective-permute-start(bf16[256,2048]{1,0:T(8,128)(2,1)} %get-tuple-element.637.refs_4_), channel_id=1, source_target_pairs={{0,1},{3,2},{1,0},{2,3},{4,5},{7,6},{5,4},{6,7},{8,9},{11,10},{9,8... | collective-permute-start | bytes 3145736 | tf_op jit(solution)/shard_map/ppermute | solution.py:601
  323.9 43.3 %collective-permute-start.26 = (bf16[256,2048]{1,0:T(8,128)(2,1)}, bf16[256,2048]{1,0:T(8,128)(2,1)}, u32[]{:S(2)}, u32[]{:S(2)}) collective-permute-start(bf16[256,2048]{1,0:T(8,128)(2,1)} %get-tuple-element.638.refs_2_), channel_id=1, source_target_pairs={{1,2},{2,1},{5,6},{6,5},{9,10},{10,9},{13,14},{14,13},{17,18},{18,... | collective-permute-start | bytes 3145736 | tf_op jit(solution)/shard_map/ppermute | solution.py:604
  339.5 14.7 %collective-permute-start.28 = (bf16[2,64,1152]{2,1,0:T(8,128)(2,1)S(1)}, bf16[2,64,1152]{2,1,0:T(8,128)(2,1)S(1)}, u32[]{:S(2)}, u32[]{:S(2)}) collective-permute-start(bf16[2,64,1152]{2,1,0:T(8,128)(2,1)S(1)} %get-tuple-element.669), channel_id=1, source_target_pairs={{0,16},{4,20},{8,24},{12,28},{16,0},{20,4},{24,8},{28,12},{1,17},{... | collective-permute-start | bytes 884744 | tf_op jit(solution)/shard_map/ppermute | solution.py:521
  372.8 137.0 %reduce-scatter.8.cloned.1.call-start = ((), (), s32[]{:S(2)}) async-start(), calls=%async_computation.5 | async-start | bytes 5640192 | tf_op jit(solution)/shard_map/reduce_scatter | solution.py:981
  372.9 29.2 %collective-permute-start.29 = (bf16[256,2048]{1,0:T(8,128)(2,1)}, bf16[256,2048]{1,0:T(8,128)(2,1)S(1)}, u32[]{:S(2)}, u32[]{:S(2)}) collective-permute-start(bf16[256,2048]{1,0:T(8,128)(2,1)} %get-tuple-element.695.refs_4_), channel_id=1, source_target_pairs={{0,1},{3,2},{1,0},{2,3},{4,5},{7,6},{5,4},{6,7},{8,9},{11,10},{9,8... | collective-permute-start | bytes 3145736 | tf_op jit(solution)/shard_map/ppermute | solution.py:601
  374.7 27.4 %collective-permute-start.30 = (bf16[256,2048]{1,0:T(8,128)(2,1)}, bf16[256,2048]{1,0:T(8,128)(2,1)S(1)}, u32[]{:S(2)}, u32[]{:S(2)}) collective-permute-start(bf16[256,2048]{1,0:T(8,128)(2,1)} %get-tuple-element.696.refs_2_), channel_id=1, source_target_pairs={{1,2},{2,1},{5,6},{6,5},{9,10},{10,9},{13,14},{14,13},{17,18},{18,... | collective-permute-start | bytes 3145736 | tf_op jit(solution)/shard_map/ppermute | solution.py:604
  393.6 8.4 %copy-start.5 = (bf16[256,2048]{1,0:T(8,128)(2,1)S(1)}, bf16[256,2048]{1,0:T(8,128)(2,1)}, u32[]{:S(2)}) copy-start(bf16[256,2048]{1,0:T(8,128)(2,1)} %copy-done.4) | copy-start | bytes 3145732
  406.7 19.4 %collective-permute-start.31 = (bf16[256,2048]{1,0:T(8,128)(2,1)}, bf16[256,2048]{1,0:T(8,128)(2,1)}, u32[]{:S(2)}, u32[]{:S(2)}) collective-permute-start(bf16[256,2048]{1,0:T(8,128)(2,1)} %get-tuple-element.718.refs_4_), channel_id=1, source_target_pairs={{0,1},{3,2},{1,0},{2,3},{4,5},{7,6},{5,4},{6,7},{8,9},{11,10},{9,8... | collective-permute-start | bytes 3145736 | tf_op jit(solution)/shard_map/ppermute | solution.py:601
  410.7 15.3 %collective-permute-start.32 = (bf16[256,2048]{1,0:T(8,128)(2,1)}, bf16[256,2048]{1,0:T(8,128)(2,1)}, u32[]{:S(2)}, u32[]{:S(2)}) collective-permute-start(bf16[256,2048]{1,0:T(8,128)(2,1)} %get-tuple-element.719.refs_2_), channel_id=1, source_target_pairs={{1,2},{2,1},{5,6},{6,5},{9,10},{10,9},{13,14},{14,13},{17,18},{18,... | collective-permute-start | bytes 3145736 | tf_op jit(solution)/shard_map/ppermute | solution.py:604
  412.4 13.7 %copy-start.7 = (bf16[256,2048]{1,0:T(8,128)(2,1)S(1)}, bf16[256,2048]{1,0:T(8,128)(2,1)}, u32[]{:S(2)}) copy-start(bf16[256,2048]{1,0:T(8,128)(2,1)} %copy-done.6) | copy-start | bytes 3145732
  431.4 18.1 %collective-permute-start.33 = (bf16[256,2048]{1,0:T(8,128)(2,1)}, bf16[256,2048]{1,0:T(8,128)(2,1)S(1)}, u32[]{:S(2)}, u32[]{:S(2)}) collective-permute-start(bf16[256,2048]{1,0:T(8,128)(2,1)} %copy-done.29), channel_id=1, source_target_pairs={{0,1},{3,2},{1,0},{2,3},{4,5},{7,6},{5,4},{6,7},{8,9},{11,10},{9,8... | collective-permute-start | bytes 3145736 | tf_op jit(solution)/shard_map/ppermute | solution.py:601
  435.2 14.3 %collective-permute-start.34 = (bf16[256,2048]{1,0:T(8,128)(2,1)}, bf16[256,2048]{1,0:T(8,128)(2,1)S(1)}, u32[]{:S(2)}, u32[]{:S(2)}) collective-permute-start(bf16[256,2048]{1,0:T(8,128)(2,1)} %copy-done.27), channel_id=1, source_target_pairs={{1,2},{2,1},{5,6},{6,5},{9,10},{10,9},{13,14},{14,13},{17,18},{18,... | collective-permute-start | bytes 3145736 | tf_op jit(solution)/shard_map/ppermute | solution.py:604
  438.1 11.4 %copy-start.28 = (bf16[256,2048]{1,0:T(8,128)(2,1)S(1)}, bf16[256,2048]{1,0:T(8,128)(2,1)}, u32[]{:S(2)}) copy-start(bf16[256,2048]{1,0:T(8,128)(2,1)} %copy-done.27) | copy-start | bytes 3145732
  438.1 11.4 %copy-start.30 = (bf16[256,2048]{1,0:T(8,128)(2,1)S(1)}, bf16[256,2048]{1,0:T(8,128)(2,1)}, u32[]{:S(2)}) copy-start(bf16[256,2048]{1,0:T(8,128)(2,1)} %copy-done.29) | copy-start | bytes 3145732
  451.6 9.0 %copy-start.11 = (bf16[256,2048]{1,0:T(8,128)(2,1)S(1)}, bf16[256,2048]{1,0:T(8,128)(2,1)}, u32[]{:S(2)}) copy-start(bf16[256,2048]{1,0:T(8,128)(2,1)} %copy-done.10) | copy-start | bytes 3145732
  451.6 24.1 %collective-permute-start.35 = (bf16[256,2048]{1,0:T(8,128)(2,1)}, bf16[256,2048]{1,0:T(8,128)(2,1)S(1)}, u32[]{:S(2)}, u32[]{:S(2)}) collective-permute-start(bf16[256,2048]{1,0:T(8,128)(2,1)} %copy-done.16), channel_id=1, source_target_pairs={{0,1},{3,2},{1,0},{2,3},{4,5},{7,6},{5,4},{6,7},{8,9},{11,10},{9,8... | collective-permute-start | bytes 3145736 | tf_op jit(solution)/shard_map/ppermute | solution.py:601
  455.5 20.2 %collective-permute-start.36 = (bf16[256,2048]{1,0:T(8,128)(2,1)S(1)}, bf16[256,2048]{1,0:T(8,128)(2,1)S(1)}, u32[]{:S(2)}, u32[]{:S(2)}) collective-permute-start(bf16[256,2048]{1,0:T(8,128)(2,1)S(1)} %get-tuple-element.773.refs_2_), channel_id=1, source_target_pairs={{1,2},{2,1},{5,6},{6,5},{9,10},{10,9},{13,14},{14,13},{17,18},{18,... | collective-permute-start | bytes 3145736 | tf_op jit(solution)/shard_map/ppermute | solution.py:604
  462.9 12.8 %copy-start.17 = (bf16[256,2048]{1,0:T(8,128)(2,1)S(1)}, bf16[256,2048]{1,0:T(8,128)(2,1)}, u32[]{:S(2)}) copy-start(bf16[256,2048]{1,0:T(8,128)(2,1)} %copy-done.16) | copy-start | bytes 3145732
  465.2 15.2 %copy-start.50 = (bf16[1,2,256,1408]{3,2,1,0:T(8,128)(2,1)S(1)}, bf16[1,2,256,1408]{3,2,1,0:T(8,128)(2,1)}, u32[]{:S(2)}) copy-start(bf16[1,2,256,1408]{3,2,1,0:T(8,128)(2,1)} %reduce-scatter.4.cloned.1.call-done) | copy-start | bytes 4325380
  478.2 25.6 %collective-permute-start.37 = (bf16[256,2048]{1,0:T(8,128)(2,1)}, bf16[256,2048]{1,0:T(8,128)(2,1)S(1)}, u32[]{:S(2)}, u32[]{:S(2)}) collective-permute-start(bf16[256,2048]{1,0:T(8,128)(2,1)} %get-tuple-element.783.refs_3_), channel_id=1, source_target_pairs={{1,0},{2,3},{5,4},{6,7},{9,8},{10,11},{13,12},{14,15},{17,16},{18,... | collective-permute-start | bytes 3145736 | tf_op jit(solution)/shard_map/ppermute | solution.py:601
  479.6 24.1 %collective-permute-start.38 = (bf16[256,2048]{1,0:T(8,128)(2,1)}, bf16[256,2048]{1,0:T(8,128)(2,1)S(1)}, u32[]{:S(2)}, u32[]{:S(2)}) collective-permute-start(bf16[256,2048]{1,0:T(8,128)(2,1)} %get-tuple-element.784.refs_1_), channel_id=1, source_target_pairs={{1,2},{2,1},{5,6},{6,5},{9,10},{10,9},{13,14},{14,13},{17,18},{18,... | collective-permute-start | bytes 3145736 | tf_op jit(solution)/shard_map/ppermute | solution.py:604
  506.4 24.8 %collective-permute-start.39 = (bf16[256,2048]{1,0:T(8,128)(2,1)S(1)}, bf16[256,2048]{1,0:T(8,128)(2,1)S(1)}, u32[]{:S(2)}, u32[]{:S(2)}) collective-permute-start(bf16[256,2048]{1,0:T(8,128)(2,1)S(1)} %get-tuple-element.791.refs_1_), channel_id=1, source_target_pairs={{1,0},{2,3},{5,4},{6,7},{9,8},{10,11},{13,12},{14,15},{17,16},{18,... | collective-permute-start | bytes 3145736 | tf_op jit(solution)/shard_map/ppermute | solution.py:601
  511.9 10.4 %copy-start.32 = (bf16[256,2048]{1,0:T(8,128)(2,1)S(1)}, bf16[256,2048]{1,0:T(8,128)(2,1)}, u32[]{:S(2)}) copy-start(bf16[256,2048]{1,0:T(8,128)(2,1)} %copy-done.31) | copy-start | bytes 3145732
  511.9 13.6 %collective-permute-start.42 = (f32[256]{0:T(256)S(1)}, f32[256]{0:T(256)S(1)}, u32[]{:S(2)}, u32[]{:S(2)}) collective-permute-start(f32[256]{0:T(256)S(1)} %get-tuple-element.839), channel_id=1, source_target_pairs={{0,3},{1,2},{2,1},{3,0},{4,7},{5,6},{6,5},{7,4},{8,11},{9,10},{10,... | collective-permute-start | bytes 3080 | tf_op jit(solution)/shard_map/ppermute | solution.py:1002
  515.2 10.3 %collective-permute-start.41 = (f32[256]{0:T(256)S(1)}, f32[256]{0:T(256)S(1)}, u32[]{:S(2)}, u32[]{:S(2)}) collective-permute-start(f32[256]{0:T(256)S(1)} %get-tuple-element.839), channel_id=1, source_target_pairs={{0,2},{1,3},{2,0},{3,1},{4,6},{5,7},{6,4},{7,5},{8,10},{9,11},{10,... | collective-permute-start | bytes 3080 | tf_op jit(solution)/shard_map/ppermute | solution.py:1002
  517.4 13.2 %collective-permute-start.40 = (f32[256]{0:T(256)S(1)}, f32[256]{0:T(256)S(1)}, u32[]{:S(2)}, u32[]{:S(2)}) collective-permute-start(f32[256]{0:T(256)S(1)} %get-tuple-element.839), channel_id=1, source_target_pairs={{0,1},{1,0},{2,3},{3,2},{4,5},{5,4},{6,7},{7,6},{8,9},{9,8},{10,11... | collective-permute-start | bytes 3080 | tf_op jit(solution)/shard_map/ppermute | solution.py:1002
  (37 other events, 80.9 us)
Sparse Core Ops, SparseCore 0:
  27.0 98.8 all-gather.2
  253.5 89.9 reduce-scatter.3
  372.9 77.6 reduce-scatter.5
  454.0 55.7 reduce-scatter.7

commit v8 on v7

--- a/solution.py
+++ b/solution.py
@@ -108,8 +108,20 @@
     return both[:, :width] + both[:, width:]
 
 
-def project_kernel(per_part, x_ref, gain_ref, wk_ref, wv_ref, wf_ref, bias_ref,
-                   xn_ref, k_ref, v_ref, z_ref, cum_ref, in_ref, s_ref, d_ref, sent_ref, state, decay):
+def project_kernel(per_part, x_ref, gain_ref, wk_ref, wv_ref, wf_ref, bias_ref, gate_ref, up_ref, down_ref,
+                   xn_ref, k_ref, v_ref, z_ref, cum_ref, in_ref, s_ref, d_ref, sent_ref, stacked_ref,
+                   state, decay, down_rows, sems):
+    step = pl.program_id(0)
+    copies = [pltpu.make_async_copy(source, stacked_ref.at[i], sems.at[i])
+              for i, source in enumerate((gate_ref, up_ref, down_rows))]
+
+    @pl.when(step == 0)
+    def _():
+        copies[0].start()
+        copies[1].start()
+        down_rows[...] = down_ref[...].astype(f32).T.astype(bf16)
+        copies[2].start()
+
     @pl.when(lax.rem(pl.program_id(0), per_part) == 0)
     def _():
         state[...] = jnp.zeros_like(state)
@@ -137,6 +149,11 @@
     s_ref[0] = state[...]
     d_ref[0] = jnp.exp(decay[...])
     pack(sent_ref, 0, jnp.exp(decay[...]), state[...])
+
+    @pl.when(step == pl.num_programs(0) - 1)
+    def _():
+        for copy in copies:
+            copy.wait()
 
 
 def query_kernel(xn_ref, wq_ref, q_ref):
@@ -652,20 +669,21 @@
     all_rows = lambda c: pl.BlockSpec((TILE, c), lambda i: (i, 0))
     by_part = lambda c: pl.BlockSpec((1, slots, c), lambda i: (i // per_part, 0, 0))
     forget_rows = w_forget.T
-    xn, k, v, z, cum, inflow, local, decay, sent = call(
+    xn, k, v, z, cum, inflow, local, decay, sent, stacked = call(
         "project",
         functools.partial(project_kernel, per_part),
         (rows // TILE,),
-        [all_rows(width), fixed((1, width))] + [fixed((width, head))] * 2 + [fixed((slots, width)), fixed((1, slots))],
+        [all_rows(width), fixed((1, width))] + [fixed((width, head))] * 2 + [fixed((slots, width)), fixed((1, slots)), anywhere, anywhere,
+                                                                        fixed((units, span))],
         [all_rows(width), all_rows(head), all_rows(head)] + [all_rows(slots)] * 3
-        + [by_part(2 * head), by_part(128), by_part(2 * head + 128)],
+        + [by_part(2 * head), by_part(128), by_part(2 * head + 128), anywhere],
         [shaped((rows, width), bf16)] + [shaped((rows, head), bf16)] * 2
         + [shaped((rows, slots), f32)] * 3 + [shaped((parts, slots, 2 * head), f32), shaped((parts, slots, 128), f32),
-                                             shaped((parts, slots, 2 * head + 128), bf16)],
-        [state_scratch, decay_scratch],
+                                             shaped((parts, slots, 2 * head + 128), bf16), shaped((3, span, units), bf16)],
+        [state_scratch, decay_scratch, pltpu.VMEM((span, units), bf16), pltpu.SemaphoreType.DMA((3,))],
         cost=cost(2 * rows * width * (2 * head + slots), 2 * rows * width * 3 + 2 * width * 2 * head),
         loose_out=(6, 7, 8),
-    )(x, gain1, w_key, w_value, forget_rows, forget_bias.reshape(1, slots))
+    )(x, gain1, w_key, w_value, forget_rows, forget_bias.reshape(1, slots), w_gate, w_up, w_down)
     q = call(
         "query",
         query_kernel,
@@ -675,15 +693,8 @@
         shaped((rows, head), bf16),
         cost=cost(2 * rows * width * head, 2 * rows * (width + head) + 2 * width * head),
     )(xn, w_query)
-    stacked = []
-
-    def stack_weights(state, got):
-        gate, down, _ = lax.optimization_barrier((w_gate, w_down, got))
-        stacked.append(jnp.stack([gate, w_up, down.T]))
-        return state
-
-    entering = scan_states(n_seq, local, decay, sent, False, ties=[stack_weights])
-    full = lax.all_gather(stacked[0], "seq")
+    full = lax.all_gather(stacked, "seq")
+    entering = scan_states(n_seq, local, decay, sent, False)
 
     def chunk_rows(m, t, columns, back):
         start = (m * pieces + t) * chunks
@@ -905,6 +916,7 @@
     end(live.pop(("ffn_part", 0, 1)), ("dhn", 1, 0))
     start()
     go_back(1, 0)
+    live["down"] = down_grads(taken("act"))
     end(live.pop(("ffn_part", 1, 0)), ("dhn", 1, 1))
     start()
     go_back(1, 1)
@@ -926,14 +938,8 @@
         live["xn"] = xn
         end(behind_of(live.pop(("ffn_part", 1, 1)), got), ("ffn", 0, 0))
         start()
-        made.append(live.pop("xn"))
+        made.extend((live.pop("xn"), live.pop("down")))
         return state
-
-    def beside_second(state, got):
-        acts = taken("act")
-        acts[0] = behind_of(acts[0], state)
-        made.append(down_grads(acts))
-        return behind_of(state, made[1])
 
     def beside_third(state, got):
         grads = call(
@@ -951,7 +957,7 @@
         made.append(grads)
         return behind_of(state, grads)
 
-    ties = [beside_first, beside_second, beside_third]
+    ties = [beside_first, None, beside_third]
     live["leaving"] = scan_states(n_seq, *folded, True, own, pieces, ties)
     live["query_grads"], live["wide"] = made[2], wide_shares
     go_last(0, 0)
@@ -961,10 +967,10 @@
     down_shares = lax.psum_scatter(live.pop("query_grads"), "seq", scatter_dimension=0)
     go_last(0, 1)
     go_last(1, 0)
-    go_last(1, 1)
     live["xn"] = xn
     end(live.pop(("dxn_part", 0, 1)), ("ffn", 1, 0))
     start()
+    go_last(1, 1)
     live.pop("leaving")
     few = [pl.BlockSpec((8, TILE), lambda j: (0, j))] * len(every)
     live["state_grads"] = call(

time: 550 us -> 594 us (1.080)
  the two profiles are of different devices: /device:TPU:2 before, /device:TPU:0 now
where the time goes in v8:
time: 594 us; the launch traced here: 585 us
  Pallas kernels  321 us (54%)
  waiting for transfers between devices  129 us (22%)
  starting transfers between devices  79.6 us (13%)
  local copies, waits for them, and re-layouts  33.7 us (6%)
  between operations  14.9 us (3%)
  other arithmetic  7.54 us (1%)
    pallas_call x30, Pallas kernels, run(): function(*[o if i in loose or spec.memory_space == pltpu.SMEM else pltpu....  299 us
    ppermute x18, waiting for transfers between devices, step(): outer = lax.ppermute(payload, 'head', way)  86.7 us
    ppermute x18, starting transfers between devices, step(): outer = lax.ppermute(payload, 'head', way)  49.1 us
    unnamed x109, local copies, waits for them, and re-layouts  31.5 us
    ppermute x6, waiting for transfers between devices, scan_states(): got = lax.ppermute(sent, 'seq', [(i, i ^ bit) for i in range(n)])  29 us
    pallas_call x25, Pallas kernels, in_vmem(): pl.pallas_call(kernel, name=name, in_specs=[pl.BlockSpec(memory_space=plt...  22.1 us
    ppermute x16, starting transfers between devices, step(): middle = lax.ppermute(pair, 'head', self.MIDDLE)  16.9 us
  transfers between devices with their start and end apart: 47, of which 14 were waited for; matrix products, arithmetic and copies ran while one was open for 3% of the time, Pallas kernels for 45%

profile of v8, /device:TPU:0, one launch (start us, length us, event | category | flops | bytes accessed | tf_op | source)
XLA Modules:
  0.0 585.5 jit_solution(15688373427851262785)
XLA Ops:
  7.2 48.9 %project.1 = (bf16[1024,2048]{1,0:T(8,128)(2,1)}, bf16[1024,512]{1,0:T(8,128)(2,1)}, bf16[1024,512]{1,0:T(8,128)(2,1)}, f32[1024,64]{1,0:T(8,128)}, f32[1024,64]...) custom-call(bf16[1024,2048]{1,0:T(8,128)(2,1)} %bitcast.30, ...), custom_call_target="tpu_custom_call" | custom-call | flops 4563402752 | bytes 16777216 | tf_op jit(solution)/shard_map/project/pallas_call | solution.py:62
  58.2 2.9 collective-permute-start.1
  61.1 7.3 %collective-permute-done.1.refs_2_ = bf16[2,64,1152]{2,1,0:T(8,128)(2,1)S(1)} collective-permute-done((bf16[2,64,1152]{2,1,0:T(8,128)(2,1)S(1)}, bf16[2,64,1152]{2,1,0:T(8,128)(2,1)S(1)}, u32[]{:S(2)}, u32[]{:S(2)}) %collective-permute-start.1) | collective-permute-done | bytes 294944 | tf_op jit(solution)/shard_map/ppermute | solution.py:538
  70.5 6.2 %query.1.q_ref = bf16[1024,512]{1,0:T(8,128)(2,1)} custom-call(bf16[1024,2048]{1,0:T(8,128)(2,1)} %get-tuple-element.713.xn_ref.refs_0_, bf16[2048,512]{1,0:T(8,128)(2,1)} %wq_ref.9), custom_call_target="tpu_custom_call" | custom-call | flops 2147483648 | bytes 7340032 | tf_op jit(solution)/shard_map/query/pallas_call | solution.py:62
  76.7 7.2 %collective-permute-done.2.refs_2_ = bf16[2,64,1152]{2,1,0:T(8,128)(2,1)S(1)} collective-permute-done((bf16[2,64,1152]{2,1,0:T(8,128)(2,1)S(1)}, bf16[2,64,1152]{2,1,0:T(8,128)(2,1)S(1)}, u32[]{:S(2)}, u32[]{:S(2)}) %collective-permute-start.2) | collective-permute-done | bytes 294944 | tf_op jit(solution)/shard_map/ppermute | solution.py:538
  84.2 5.3 read.4
  89.5 3.8 collective-permute-start.3
  93.3 5.3 read.5
  98.6 15.4 %collective-permute-done.3.refs_1_ = bf16[256,2048]{1,0:T(8,128)(2,1)S(1)} collective-permute-done((bf16[256,2048]{1,0:T(8,128)(2,1)S(1)}, bf16[256,2048]{1,0:T(8,128)(2,1)S(1)}, u32[]{:S(2)}, u32[]{:S(2)}) %collective-permute-start.3) | collective-permute-done | bytes 1048608 | tf_op jit(solution)/shard_map/ppermute | solution.py:618
  114.1 4.5 collective-permute-start.4
  119.3 5.2 read.6
  124.6 13.9 %collective-permute-done.4.refs_1_ = bf16[256,2048]{1,0:T(8,128)(2,1)S(1)} collective-permute-done((bf16[256,2048]{1,0:T(8,128)(2,1)S(1)}, bf16[256,2048]{1,0:T(8,128)(2,1)S(1)}, u32[]{:S(2)}, u32[]{:S(2)}) %collective-permute-start.4) | collective-permute-done | bytes 1048608 | tf_op jit(solution)/shard_map/ppermute | solution.py:618
  138.6 4.3 collective-permute-start.6
  143.6 5.6 read.7
  149.2 13.8 %collective-permute-done.6.refs_1_ = bf16[256,2048]{1,0:T(8,128)(2,1)S(1)} collective-permute-done((bf16[256,2048]{1,0:T(8,128)(2,1)S(1)}, bf16[256,2048]{1,0:T(8,128)(2,1)S(1)}, u32[]{:S(2)}, u32[]{:S(2)}) %collective-permute-start.6) | collective-permute-done | bytes 1048608 | tf_op jit(solution)/shard_map/ppermute | solution.py:618
  164.2 3.8 collective-permute-start.8
  168.0 1.9 collective-permute-start.9
  171.2 19.4 %feed.4 = (bf16[256,2048]{1,0:T(8,128)(2,1)}, bf16[256,2048]{1,0:T(8,128)(2,1)}, bf16[256,1408]{1,0:T(8,128)(2,1)}, bf16[256,1408]{1,0:T(8,128)(2,1)}, bf16[256,...) custom-call(bf16[1024,2048]{1,0:T(8,128)(2,1)} %bitcast.31, ...), custom_call_target="tpu_custom_call" | custom-call | flops 8858370048 | bytes 24641536 | tf_op jit(solution)/shard_map/feed/pallas_call | solution.py:62
  192.3 2.1 collective-permute-start.10
  195.7 19.4 %feed.5 = (bf16[256,2048]{1,0:T(8,128)(2,1)}, bf16[256,2048]{1,0:T(8,128)(2,1)}, bf16[256,1408]{1,0:T(8,128)(2,1)}, bf16[256,1408]{1,0:T(8,128)(2,1)}, bf16[256,...) custom-call(bf16[1024,2048]{1,0:T(8,128)(2,1)} %bitcast.32, ...), custom_call_target="tpu_custom_call" | custom-call | flops 8858370048 | bytes 24641536 | tf_op jit(solution)/shard_map/feed/pallas_call | solution.py:62
  215.4 3.0 collective-permute-start.12
  219.3 19.5 %feed.6 = (bf16[256,2048]{1,0:T(8,128)(2,1)}, bf16[256,2048]{1,0:T(8,128)(2,1)}, bf16[256,1408]{1,0:T(8,128)(2,1)}, bf16[256,1408]{1,0:T(8,128)(2,1)}, bf16[256,...) custom-call(bf16[1024,2048]{1,0:T(8,128)(2,1)} %bitcast.33, ...), custom_call_target="tpu_custom_call" | custom-call | flops 8858370048 | bytes 24641536 | tf_op jit(solution)/shard_map/feed/pallas_call | solution.py:62
  241.8 19.5 %feed.7 = (bf16[256,2048]{1,0:T(8,128)(2,1)}, bf16[256,2048]{1,0:T(8,128)(2,1)}, bf16[256,1408]{1,0:T(8,128)(2,1)}, bf16[256,1408]{1,0:T(8,128)(2,1)}, bf16[256,...) custom-call(bf16[1024,2048]{1,0:T(8,128)(2,1)} %bitcast.34, ...), custom_call_target="tpu_custom_call" | custom-call | flops 8858370048 | bytes 24641536 | tf_op jit(solution)/shard_map/feed/pallas_call | solution.py:62
  262.8 3.0 collective-permute-start.16
  267.4 19.1 %wide_grads.1 = bf16[8,2,256,1408]{3,2,1,0:T(8,128)(2,1)} custom-call(bf16[256,2048]{1,0:T(8,128)(2,1)} %get-tuple-element.543.refs_0_, bf16[256,2048]{1,0:T(8,128)(2,1)} %get-tuple-element.544.refs_1_, bf16[256,2048]{1,0:T(8,128)(2,1)} %get-tuple-element.545.refs_2_, bf16[256,2048]{1,0:T(8,128)(2,1)} %get-tuple-element.546.refs_3_, ...), custom_call_target="tpu_custom_call" | custom-call | flops 11811160064 | bytes 21495808 | tf_op jit(solution)/shard_map/wide_grads/pallas_call | solution.py:62
  286.5 2.3 join.25
  294.3 8.7 %back.4 = (bf16[256,2048]{1,0:T(8,128)(2,1)}, bf16[256,512]{1,0:T(8,128)(2,1)}, f32[256,512]{1,0:T(8,128)}, f32[256,512]{1,0:T(8,128)}, f32[256,64]{1,0:T(8,128)...) custom-call(bf16[256,2048]{1,0:T(8,128)(2,1)S(1)} %get-tuple-element, ...), custom_call_target="tpu_custom_call" | custom-call | flops 930086912 | bytes 9961472 | tf_op jit(solution)/shard_map/back/pallas_call | solution.py:62
  303.1 9.5 %back.5 = (bf16[256,2048]{1,0:T(8,128)(2,1)}, bf16[256,512]{1,0:T(8,128)(2,1)}, f32[256,512]{1,0:T(8,128)}, f32[256,512]{1,0:T(8,128)}, f32[256,64]{1,0:T(8,128)...) custom-call(bf16[256,2048]{1,0:T(8,128)(2,1)S(1)} %copy-done.15, ...), custom_call_target="tpu_custom_call" | custom-call | flops 930086912 | bytes 9961472 | tf_op jit(solution)/shard_map/back/pallas_call | solution.py:62
  312.9 4.2 collective-permute-start.20
  317.8 9.1 %back.6 = (bf16[256,2048]{1,0:T(8,128)(2,1)}, bf16[256,512]{1,0:T(8,128)(2,1)}, f32[256,512]{1,0:T(8,128)}, f32[256,512]{1,0:T(8,128)}, f32[256,64]{1,0:T(8,128)...) custom-call(bf16[256,2048]{1,0:T(8,128)(2,1)S(1)} %get-tuple-element, ...), custom_call_target="tpu_custom_call" | custom-call | flops 930086912 | bytes 9961472 | tf_op jit(solution)/shard_map/back/pallas_call | solution.py:62
  326.9 10.7 %down_grads.1.refs_13_ = bf16[8,256,2432]{2,1,0:T(8,128)(2,1)} custom-call(bf16[1024,2048]{1,0:T(8,128)(2,1)} %bitcast.50, bf16[256,1408]{1,0:T(8,128)(2,1)} %get-tuple-element.597.refs_1_, bf16[256,1408]{1,0:T(8,128)(2,1)} %get-tuple-element.598.refs_2_, bf16[256,1408]{1,0:T(8,128)(2,1)} %get-tuple-element.599.refs_3_, ...), custom_call_target="tpu_custom_call" | custom-call | flops 5905580032 | bytes 12845056 | tf_op jit(solution)/shard_map/down_grads/pallas_call | solution.py:62
  337.9 2.4 collective-permute-start.23
  341.0 8.4 %back.7 = (bf16[256,2048]{1,0:T(8,128)(2,1)}, bf16[256,512]{1,0:T(8,128)(2,1)}, f32[256,512]{1,0:T(8,128)}, f32[256,512]{1,0:T(8,128)}, f32[256,64]{1,0:T(8,128)...) custom-call(bf16[256,2048]{1,0:T(8,128)(2,1)S(1)} %get-tuple-element, ...), custom_call_target="tpu_custom_call" | custom-call | flops 930086912 | bytes 9961472 | tf_op jit(solution)/shard_map/back/pallas_call | solution.py:62
  351.2 5.1 collective-permute-done.23.refs_1_
  358.8 4.2 collective-permute-start.25
  366.7 11.7 %collective-permute-done.27.refs_2_ = bf16[2,64,1152]{2,1,0:T(8,128)(2,1)S(1)} collective-permute-done((bf16[2,64,1152]{2,1,0:T(8,128)(2,1)S(1)}, bf16[2,64,1152]{2,1,0:T(8,128)(2,1)S(1)}, u32[]{:S(2)}, u32[]{:S(2)}) %collective-permute-start.27) | collective-permute-done | bytes 294944 | tf_op jit(solution)/shard_map/ppermute | solution.py:538
  382.7 11.1 %query_grads.1 = bf16[8,256,2432]{2,1,0:T(8,128)(2,1)} custom-call(bf16[1024,2048]{1,0:T(8,128)(2,1)} %get-tuple-element.713.xn_ref.refs_0_, bf16[256,2048]{1,0:T(8,128)(2,1)} %get-tuple-element.636.refs_1_.dhid_ref, bf16[256,2048]{1,0:T(8,128)(2,1)} %get-tuple-element.637.refs_2_.dhid_ref, ...), custom_call_target="tpu_custom_call", output_to_operand_aliasing={{}: (13, {})} | custom-call | flops 4294967296 | bytes 14680064 | tf_op jit(solution)/shard_map/query_grads/pallas_call | solution.py:62
  398.7 8.1 %last.4 = (bf16[256,512]{1,0:T(8,128)(2,1)}, bf16[256,512]{1,0:T(8,128)(2,1)}, bf16[256,64]{1,0:T(8,128)(2,1)}, bf16[256,2048]{1,0:T(8,128)(2,1)S(1)}, f32[8,64]{1,0:T(8,128)}, /*index=5*/f32[8,2048]{1,0:T(8,128)}) custom-call(f32[4,64,1024]{2,1,0:T(8,128)S(1)} %hop.11.l0_ref, bf16[1024,512]{1,0:T(8,128)(2,1)} %get-tuple-element.398.k_ref, ...), custom_call_target="tpu_custom_call" | custom-call | flops 1677721600 | bytes 13107200 | tf_op jit(solution)/shard_map/last/pallas_call | solution.py:62
  406.8 3.6 join.29
  414.8 8.6 %last.6 = (bf16[256,512]{1,0:T(8,128)(2,1)}, bf16[256,512]{1,0:T(8,128)(2,1)}, bf16[256,64]{1,0:T(8,128)(2,1)}, bf16[256,2048]{1,0:T(8,128)(2,1)S(1)}, f32[8,64]{1,0:T(8,128)}, /*index=5*/f32[8,2048]{1,0:T(8,128)}) custom-call(f32[4,64,1024]{2,1,0:T(8,128)S(1)} %hop.11.l0_ref, bf16[1024,512]{1,0:T(8,128)(2,1)} %get-tuple-element.398.k_ref, ...), custom_call_target="tpu_custom_call" | custom-call | flops 1677721600 | bytes 13107200 | tf_op jit(solution)/shard_map/last/pallas_call | solution.py:62
  423.5 9.5 %last.5 = (bf16[256,512]{1,0:T(8,128)(2,1)}, bf16[256,512]{1,0:T(8,128)(2,1)}, bf16[256,64]{1,0:T(8,128)(2,1)}, bf16[256,2048]{1,0:T(8,128)(2,1)S(1)}, f32[8,64]{1,0:T(8,128)}, /*index=5*/f32[8,2048]{1,0:T(8,128)}) custom-call(f32[4,64,1024]{2,1,0:T(8,128)S(1)} %hop.11.l0_ref, bf16[1024,512]{1,0:T(8,128)(2,1)} %get-tuple-element.398.k_ref, ...), custom_call_target="tpu_custom_call" | custom-call | flops 1677721600 | bytes 13107200 | tf_op jit(solution)/shard_map/last/pallas_call | solution.py:62
  433.0 3.4 join.30
  437.4 4.0 collective-permute-start.31
  443.0 8.1 %last.7 = (bf16[256,512]{1,0:T(8,128)(2,1)}, bf16[256,512]{1,0:T(8,128)(2,1)}, bf16[256,64]{1,0:T(8,128)(2,1)}, bf16[256,2048]{1,0:T(8,128)(2,1)S(1)}, f32[8,64]{1,0:T(8,128)}, /*index=5*/f32[8,2048]{1,0:T(8,128)}) custom-call(f32[4,64,1024]{2,1,0:T(8,128)S(1)} %hop.11.l0_ref, bf16[1024,512]{1,0:T(8,128)(2,1)} %get-tuple-element.398.k_ref, ...), custom_call_target="tpu_custom_call" | custom-call | flops 1677721600 | bytes 13107200 | tf_op jit(solution)/shard_map/last/pallas_call | solution.py:62
  451.1 11.8 %state_grads.1 = bf16[8,272,1152]{2,1,0:T(8,128)(2,1)} custom-call(bf16[1024,2048]{1,0:T(8,128)(2,1)} %get-tuple-element.713.xn_ref.refs_0_, bf16[256,512]{1,0:T(8,128)(2,1)} %get-tuple-element.714.refs_1_, bf16[256,512]{1,0:T(8,128)(2,1)} %get-tuple-element.715.refs_2_, bf16[256,512]{1,0:T(8,128)(2,1)} %get-tuple-element.716.refs_3_, ...), custom_call_target="tpu_custom_call" | custom-call | flops 4294967296 | bytes 10485760 | tf_op jit(solution)/shard_map/state_grads/pallas_call | solution.py:62
  463.0 2.6 join.31
  470.2 2.1 out.4.refs_0_
  472.4 2.5 out.5.refs_0_
  474.9 8.7 %collective-permute-done.33.refs_1_ = bf16[256,2048]{1,0:T(8,128)(2,1)S(1)} collective-permute-done((bf16[256,2048]{1,0:T(8,128)(2,1)}, bf16[256,2048]{1,0:T(8,128)(2,1)S(1)}, u32[]{:S(2)}, u32[]{:S(2)}) %collective-permute-start.33) | collective-permute-done | bytes 1048608 | tf_op jit(solution)/shard_map/ppermute | solution.py:618
  485.7 4.9 reduce-scatter.6.cloned.1.call-done
  494.1 3.1 in_grad.4.refs_0_
  497.2 2.2 out.6.refs_0_
  499.4 2.2 out.7
  501.7 14.1 %collective-permute-done.35.refs_1_ = bf16[256,2048]{1,0:T(8,128)(2,1)S(1)} collective-permute-done((bf16[256,2048]{1,0:T(8,128)(2,1)}, bf16[256,2048]{1,0:T(8,128)(2,1)S(1)}, u32[]{:S(2)}, u32[]{:S(2)}) %collective-permute-start.35) | collective-permute-done | bytes 1048608 | tf_op jit(solution)/shard_map/ppermute | solution.py:618
  523.1 2.9 copy.41
  527.2 3.2 in_grad.5.refs_0_
  530.4 15.6 %collective-permute-done.37.refs_0_ = bf16[256,2048]{1,0:T(8,128)(2,1)S(1)} collective-permute-done((bf16[256,2048]{1,0:T(8,128)(2,1)}, bf16[256,2048]{1,0:T(8,128)(2,1)S(1)}, u32[]{:S(2)}, u32[]{:S(2)}) %collective-permute-start.37) | collective-permute-done | bytes 1048608 | tf_op jit(solution)/shard_map/ppermute | solution.py:618
  549.7 2.2 slice_convert_fusion
  553.9 2.3 collective-permute-start.42
  556.2 2.8 collective-permute-start.41
  561.7 2.0 copy.40
  563.7 3.2 in_grad.6.refs_0_
  566.9 8.0 %collective-permute-done.40 = f32[256]{0:T(256)S(1)} collective-permute-done((f32[256]{0:T(256)S(1)}, f32[256]{0:T(256)S(1)}, u32[]{:S(2)}, u32[]{:S(2)}) %collective-permute-start.40) | collective-permute-done | bytes 1056 | tf_op jit(solution)/shard_map/ppermute | solution.py:1008
  575.5 3.2 in_grad.7
  (207 shorter events, 77.7 us)
Async XLA Ops:
  7.2 162.8 %all-gather.3.cloned.1.call-start = ((), (), s32[]{:S(2)}) async-start(), calls=%async_computation.6 | async-start | bytes 19464192 | tf_op jit(solution)/shard_map/all_gather | solution.py:696
  56.2 356.3 %reduce-scatter.4.cloned.1.call-start = ((), (), s32[]{:S(2)}) async-start(), calls=%async_computation.3 | async-start | bytes 12976128 | tf_op jit(solution)/shard_map/reduce_scatter | solution.py:913
  56.2 1.7 collective-permute-start
  58.2 10.2 %collective-permute-start.1 = (bf16[2,64,1152]{2,1,0:T(8,128)(2,1)S(1)}, bf16[2,64,1152]{2,1,0:T(8,128)(2,1)S(1)}, u32[]{:S(2)}, u32[]{:S(2)}) collective-permute-start(bf16[2,64,1152]{2,1,0:T(8,128)(2,1)S(1)} %get-tuple-element.407), channel_id=1, source_target_pairs={{0,8},{4,12},{8,0},{12,4},{16,24},{20,28},{24,16},{28,20},{1,9},{5... | collective-permute-start | bytes 884744 | tf_op jit(solution)/shard_map/ppermute | solution.py:538
  68.7 15.3 %collective-permute-start.2 = (bf16[2,64,1152]{2,1,0:T(8,128)(2,1)S(1)}, bf16[2,64,1152]{2,1,0:T(8,128)(2,1)S(1)}, u32[]{:S(2)}, u32[]{:S(2)}) collective-permute-start(bf16[2,64,1152]{2,1,0:T(8,128)(2,1)S(1)} %get-tuple-element.412), channel_id=1, source_target_pairs={{0,16},{4,20},{8,24},{12,28},{16,0},{20,4},{24,8},{28,12},{1,17},{... | collective-permute-start | bytes 884744 | tf_op jit(solution)/shard_map/ppermute | solution.py:538
  89.5 24.5 %collective-permute-start.3 = (bf16[256,2048]{1,0:T(8,128)(2,1)S(1)}, bf16[256,2048]{1,0:T(8,128)(2,1)S(1)}, u32[]{:S(2)}, u32[]{:S(2)}) collective-permute-start(bf16[256,2048]{1,0:T(8,128)(2,1)S(1)} %get-tuple-element.419.refs_0_), channel_id=1, source_target_pairs={{0,1},{3,2},{4,5},{7,6},{8,9},{11,10},{12,13},{15,14},{16,17},{19,... | collective-permute-start | bytes 3145736 | tf_op jit(solution)/shard_map/ppermute | solution.py:618
  114.1 24.4 %collective-permute-start.4 = (bf16[256,2048]{1,0:T(8,128)(2,1)S(1)}, bf16[256,2048]{1,0:T(8,128)(2,1)S(1)}, u32[]{:S(2)}, u32[]{:S(2)}) collective-permute-start(bf16[256,2048]{1,0:T(8,128)(2,1)S(1)} %get-tuple-element.423), channel_id=1, source_target_pairs={{0,1},{3,2},{4,5},{7,6},{8,9},{11,10},{12,13},{15,14},{16,17},{19,... | collective-permute-start | bytes 3145736 | tf_op jit(solution)/shard_map/ppermute | solution.py:618
  118.6 19.9 %collective-permute-start.5 = (bf16[256,2048]{1,0:T(8,128)(2,1)S(1)}, bf16[256,2048]{1,0:T(8,128)(2,1)S(1)}, u32[]{:S(2)}, u32[]{:S(2)}) collective-permute-start(bf16[256,2048]{1,0:T(8,128)(2,1)S(1)} %get-tuple-element.424.refs_2_), channel_id=1, source_target_pairs={{1,2},{2,1},{5,6},{6,5},{9,10},{10,9},{13,14},{14,13},{17,18},{18,... | collective-permute-start | bytes 3145736 | tf_op jit(solution)/shard_map/ppermute | solution.py:621
  138.6 24.4 %collective-permute-start.6 = (bf16[256,2048]{1,0:T(8,128)(2,1)S(1)}, bf16[256,2048]{1,0:T(8,128)(2,1)S(1)}, u32[]{:S(2)}, u32[]{:S(2)}) collective-permute-start(bf16[256,2048]{1,0:T(8,128)(2,1)S(1)} %get-tuple-element.432.refs_4_), channel_id=1, source_target_pairs={{0,1},{3,2},{1,0},{2,3},{4,5},{7,6},{5,4},{6,7},{8,9},{11,10},{9,8... | collective-permute-start | bytes 3145736 | tf_op jit(solution)/shard_map/ppermute | solution.py:618
  142.9 20.2 %collective-permute-start.7 = (bf16[256,2048]{1,0:T(8,128)(2,1)S(1)}, bf16[256,2048]{1,0:T(8,128)(2,1)S(1)}, u32[]{:S(2)}, u32[]{:S(2)}) collective-permute-start(bf16[256,2048]{1,0:T(8,128)(2,1)S(1)} %get-tuple-element.433.refs_2_), channel_id=1, source_target_pairs={{1,2},{2,1},{5,6},{6,5},{9,10},{10,9},{13,14},{14,13},{17,18},{18,... | collective-permute-start | bytes 3145736 | tf_op jit(solution)/shard_map/ppermute | solution.py:621
  164.2 26.4 %collective-permute-start.8 = (bf16[256,2048]{1,0:T(8,128)(2,1)S(1)}, bf16[256,2048]{1,0:T(8,128)(2,1)}, u32[]{:S(2)}, u32[]{:S(2)}) collective-permute-start(bf16[256,2048]{1,0:T(8,128)(2,1)S(1)} %get-tuple-element.437.refs_4_), channel_id=1, source_target_pairs={{0,1},{3,2},{1,0},{2,3},{4,5},{7,6},{5,4},{6,7},{8,9},{11,10},{9,8... | collective-permute-start | bytes 3145736 | tf_op jit(solution)/shard_map/ppermute | solution.py:618
  168.0 22.6 %collective-permute-start.9 = (bf16[256,2048]{1,0:T(8,128)(2,1)S(1)}, bf16[256,2048]{1,0:T(8,128)(2,1)}, u32[]{:S(2)}, u32[]{:S(2)}) collective-permute-start(bf16[256,2048]{1,0:T(8,128)(2,1)S(1)} %get-tuple-element.438.refs_2_), channel_id=1, source_target_pairs={{1,2},{2,1},{5,6},{6,5},{9,10},{10,9},{13,14},{14,13},{17,18},{18,... | collective-permute-start | bytes 3145736 | tf_op jit(solution)/shard_map/ppermute | solution.py:621
  192.3 22.8 %collective-permute-start.10 = (bf16[256,2048]{1,0:T(8,128)(2,1)S(1)}, bf16[256,2048]{1,0:T(8,128)(2,1)S(1)}, u32[]{:S(2)}, u32[]{:S(2)}) collective-permute-start(bf16[256,2048]{1,0:T(8,128)(2,1)S(1)} %get-tuple-element.453.refs_4_), channel_id=1, source_target_pairs={{0,1},{3,2},{1,0},{2,3},{4,5},{7,6},{5,4},{6,7},{8,9},{11,10},{9,8... | collective-permute-start | bytes 3145736 | tf_op jit(solution)/shard_map/ppermute | solution.py:618
  194.5 20.7 %collective-permute-start.11 = (bf16[256,2048]{1,0:T(8,128)(2,1)S(1)}, bf16[256,2048]{1,0:T(8,128)(2,1)S(1)}, u32[]{:S(2)}, u32[]{:S(2)}) collective-permute-start(bf16[256,2048]{1,0:T(8,128)(2,1)S(1)} %get-tuple-element.454.refs_2_), channel_id=1, source_target_pairs={{1,2},{2,1},{5,6},{6,5},{9,10},{10,9},{13,14},{14,13},{17,18},{18,... | collective-permute-start | bytes 3145736 | tf_op jit(solution)/shard_map/ppermute | solution.py:621
  215.4 23.4 %collective-permute-start.12 = (bf16[256,2048]{1,0:T(8,128)(2,1)S(1)}, bf16[256,2048]{1,0:T(8,128)(2,1)S(1)}, u32[]{:S(2)}, u32[]{:S(2)}) collective-permute-start(bf16[256,2048]{1,0:T(8,128)(2,1)S(1)} %get-tuple-element.470.refs_4_), channel_id=1, source_target_pairs={{0,1},{3,2},{1,0},{2,3},{4,5},{7,6},{5,4},{6,7},{8,9},{11,10},{9,8... | collective-permute-start | bytes 3145736 | tf_op jit(solution)/shard_map/ppermute | solution.py:618
  218.4 20.4 %collective-permute-start.13 = (bf16[256,2048]{1,0:T(8,128)(2,1)S(1)}, bf16[256,2048]{1,0:T(8,128)(2,1)S(1)}, u32[]{:S(2)}, u32[]{:S(2)}) collective-permute-start(bf16[256,2048]{1,0:T(8,128)(2,1)S(1)} %get-tuple-element.471.refs_2_), channel_id=1, source_target_pairs={{1,2},{2,1},{5,6},{6,5},{9,10},{10,9},{13,14},{14,13},{17,18},{18,... | collective-permute-start | bytes 3145736 | tf_op jit(solution)/shard_map/ppermute | solution.py:621
  239.0 22.3 %collective-permute-start.14 = (bf16[256,2048]{1,0:T(8,128)(2,1)S(1)}, bf16[256,2048]{1,0:T(8,128)(2,1)S(1)}, u32[]{:S(2)}, u32[]{:S(2)}) collective-permute-start(bf16[256,2048]{1,0:T(8,128)(2,1)S(1)} %get-tuple-element.497.refs_4_), channel_id=1, source_target_pairs={{0,1},{3,2},{1,0},{2,3},{4,5},{7,6},{5,4},{6,7},{8,9},{11,10},{9,8... | collective-permute-start | bytes 3145736 | tf_op jit(solution)/shard_map/ppermute | solution.py:618
  240.9 20.4 %collective-permute-start.15 = (bf16[256,2048]{1,0:T(8,128)(2,1)S(1)}, bf16[256,2048]{1,0:T(8,128)(2,1)S(1)}, u32[]{:S(2)}, u32[]{:S(2)}) collective-permute-start(bf16[256,2048]{1,0:T(8,128)(2,1)S(1)} %get-tuple-element.498.refs_2_), channel_id=1, source_target_pairs={{1,2},{2,1},{5,6},{6,5},{9,10},{10,9},{13,14},{14,13},{17,18},{18,... | collective-permute-start | bytes 3145736 | tf_op jit(solution)/shard_map/ppermute | solution.py:621
  262.8 23.7 %copy-start.3 = (bf16[256,2048]{1,0:T(8,128)(2,1)S(1)}, bf16[256,2048]{1,0:T(8,128)(2,1)}, u32[]{:S(2)}) copy-start(bf16[256,2048]{1,0:T(8,128)(2,1)} %get-tuple-element.528.refs_5_.refs_0_) | copy-start | bytes 3145732
  262.8 23.7 %collective-permute-start.16 = (bf16[256,2048]{1,0:T(8,128)(2,1)}, bf16[256,2048]{1,0:T(8,128)(2,1)}, u32[]{:S(2)}, u32[]{:S(2)}) collective-permute-start(bf16[256,2048]{1,0:T(8,128)(2,1)} %get-tuple-element.526.refs_4_), channel_id=1, source_target_pairs={{0,1},{3,2},{1,0},{2,3},{4,5},{7,6},{5,4},{6,7},{8,9},{11,10},{9,8... | collective-permute-start | bytes 3145736 | tf_op jit(solution)/shard_map/ppermute | solution.py:618
  265.8 20.7 %collective-permute-start.17 = (bf16[256,2048]{1,0:T(8,128)(2,1)}, bf16[256,2048]{1,0:T(8,128)(2,1)}, u32[]{:S(2)}, u32[]{:S(2)}) collective-permute-start(bf16[256,2048]{1,0:T(8,128)(2,1)} %get-tuple-element.527.refs_2_), channel_id=1, source_target_pairs={{1,2},{2,1},{5,6},{6,5},{9,10},{10,9},{13,14},{14,13},{17,18},{18,... | collective-permute-start | bytes 3145736 | tf_op jit(solution)/shard_map/ppermute | solution.py:621
  291.9 198.8 %reduce-scatter.6.cloned.1.call-start = ((), (), s32[]{:S(2)}) async-start(), calls=%async_computation.4 | async-start | bytes 11206656 | tf_op jit(solution)/shard_map/reduce_scatter | solution.py:967
  291.9 20.7 %collective-permute-start.18 = (bf16[256,2048]{1,0:T(8,128)(2,1)}, bf16[256,2048]{1,0:T(8,128)(2,1)S(1)}, u32[]{:S(2)}, u32[]{:S(2)}) collective-permute-start(bf16[256,2048]{1,0:T(8,128)(2,1)} %copy-done.24), channel_id=1, source_target_pairs={{0,1},{3,2},{1,0},{2,3},{4,5},{7,6},{5,4},{6,7},{8,9},{11,10},{9,8... | collective-permute-start | bytes 3145736 | tf_op jit(solution)/shard_map/ppermute | solution.py:618
  293.2 19.5 %collective-permute-start.19 = (bf16[256,2048]{1,0:T(8,128)(2,1)S(1)}, bf16[256,2048]{1,0:T(8,128)(2,1)S(1)}, u32[]{:S(2)}, u32[]{:S(2)}) collective-permute-start(bf16[256,2048]{1,0:T(8,128)(2,1)S(1)} %copy-done.23), channel_id=1, source_target_pairs={{1,2},{2,1},{5,6},{6,5},{9,10},{10,9},{13,14},{14,13},{17,18},{18,... | collective-permute-start | bytes 3145736 | tf_op jit(solution)/shard_map/ppermute | solution.py:621
  294.3 8.8 %copy-start.15 = (bf16[256,2048]{1,0:T(8,128)(2,1)S(1)}, bf16[256,2048]{1,0:T(8,128)(2,1)}, u32[]{:S(2)}) copy-start(bf16[256,2048]{1,0:T(8,128)(2,1)} %copy-done.14) | copy-start | bytes 3145732
  303.1 9.6 %copy-start.2 = (bf16[256,2048]{1,0:T(8,128)(2,1)S(1)}, bf16[256,2048]{1,0:T(8,128)(2,1)}, u32[]{:S(2)}) copy-start(bf16[256,2048]{1,0:T(8,128)(2,1)} %get-tuple-element.556.refs_5_.refs_0_) | copy-start | bytes 3145732
  303.1 9.6 %copy-start.25 = (bf16[256,2048]{1,0:T(8,128)(2,1)S(1)}, bf16[256,2048]{1,0:T(8,128)(2,1)}, u32[]{:S(2)}) copy-start(bf16[256,2048]{1,0:T(8,128)(2,1)} %copy-done.24) | copy-start | bytes 3145732
  312.9 24.8 %collective-permute-start.20 = (bf16[256,2048]{1,0:T(8,128)(2,1)S(1)}, bf16[256,2048]{1,0:T(8,128)(2,1)S(1)}, u32[]{:S(2)}, u32[]{:S(2)}) collective-permute-start(bf16[256,2048]{1,0:T(8,128)(2,1)S(1)} %get-tuple-element.582.refs_4_), channel_id=1, source_target_pairs={{0,1},{3,2},{1,0},{2,3},{4,5},{7,6},{5,4},{6,7},{8,9},{11,10},{9,8... | collective-permute-start | bytes 3145736 | tf_op jit(solution)/shard_map/ppermute | solution.py:618
  317.1 20.6 %collective-permute-start.21 = (bf16[256,2048]{1,0:T(8,128)(2,1)S(1)}, bf16[256,2048]{1,0:T(8,128)(2,1)S(1)}, u32[]{:S(2)}, u32[]{:S(2)}) collective-permute-start(bf16[256,2048]{1,0:T(8,128)(2,1)S(1)} %get-tuple-element.583.refs_2_), channel_id=1, source_target_pairs={{1,2},{2,1},{5,6},{6,5},{9,10},{10,9},{13,14},{14,13},{17,18},{18,... | collective-permute-start | bytes 3145736 | tf_op jit(solution)/shard_map/ppermute | solution.py:621
  326.9 10.7 %copy-start.1 = (bf16[256,2048]{1,0:T(8,128)(2,1)S(1)}, bf16[256,2048]{1,0:T(8,128)(2,1)}, u32[]{:S(2)}) copy-start(bf16[256,2048]{1,0:T(8,128)(2,1)} %get-tuple-element.584.refs_5_.refs_0_) | copy-start | bytes 3145732
  337.9 18.5 %collective-permute-start.23 = (bf16[256,2048]{1,0:T(8,128)(2,1)S(1)}, bf16[256,2048]{1,0:T(8,128)(2,1)S(1)}, u32[]{:S(2)}, u32[]{:S(2)}) collective-permute-start(bf16[256,2048]{1,0:T(8,128)(2,1)S(1)} %get-tuple-element.615.refs_4_), channel_id=1, source_target_pairs={{0,1},{3,2},{1,0},{2,3},{4,5},{7,6},{5,4},{6,7},{8,9},{11,10},{9,8... | collective-permute-start | bytes 3145736 | tf_op jit(solution)/shard_map/ppermute | solution.py:618
  340.2 16.1 %collective-permute-start.24 = (bf16[256,2048]{1,0:T(8,128)(2,1)S(1)}, bf16[256,2048]{1,0:T(8,128)(2,1)S(1)}, u32[]{:S(2)}, u32[]{:S(2)}) collective-permute-start(bf16[256,2048]{1,0:T(8,128)(2,1)S(1)} %get-tuple-element.616.refs_2_), channel_id=1, source_target_pairs={{1,2},{2,1},{5,6},{6,5},{9,10},{10,9},{13,14},{14,13},{17,18},{18,... | collective-permute-start | bytes 3145736 | tf_op jit(solution)/shard_map/ppermute | solution.py:621
  340.9 15.4 %copy-start = (bf16[256,2048]{1,0:T(8,128)(2,1)S(1)}, bf16[256,2048]{1,0:T(8,128)(2,1)}, u32[]{:S(2)}) copy-start(bf16[256,2048]{1,0:T(8,128)(2,1)} %get-tuple-element.614.refs_5_.refs_0_) | copy-start | bytes 3145732
  349.4 8.4 %copy-start.40 = (f32[64,128]{1,0:T(8,128)}, f32[64,128]{1,0:T(8,128)S(1)}, u32[]{:S(2)}) copy-start(f32[64,128]{1,0:T(8,128)S(1)} %get-tuple-element.612.refs_7_.refs_12_) | copy-start | bytes 98308
  349.5 1.6 collective-permute-start.22
  358.8 48.0 %collective-permute-start.25 = (bf16[256,2048]{1,0:T(8,128)(2,1)}, bf16[256,2048]{1,0:T(8,128)(2,1)}, u32[]{:S(2)}, u32[]{:S(2)}) collective-permute-start(bf16[256,2048]{1,0:T(8,128)(2,1)} %get-tuple-element.624.refs_4_), channel_id=1, source_target_pairs={{0,1},{3,2},{1,0},{2,3},{4,5},{7,6},{5,4},{6,7},{8,9},{11,10},{9,8... | collective-permute-start | bytes 3145736 | tf_op jit(solution)/shard_map/ppermute | solution.py:618
  363.0 43.8 %collective-permute-start.26 = (bf16[256,2048]{1,0:T(8,128)(2,1)}, bf16[256,2048]{1,0:T(8,128)(2,1)}, u32[]{:S(2)}, u32[]{:S(2)}) collective-permute-start(bf16[256,2048]{1,0:T(8,128)(2,1)} %get-tuple-element.625.refs_2_), channel_id=1, source_target_pairs={{1,2},{2,1},{5,6},{6,5},{9,10},{10,9},{13,14},{14,13},{17,18},{18,... | collective-permute-start | bytes 3145736 | tf_op jit(solution)/shard_map/ppermute | solution.py:621
  365.0 13.3 %collective-permute-start.27 = (bf16[2,64,1152]{2,1,0:T(8,128)(2,1)S(1)}, bf16[2,64,1152]{2,1,0:T(8,128)(2,1)S(1)}, u32[]{:S(2)}, u32[]{:S(2)}) collective-permute-start(bf16[2,64,1152]{2,1,0:T(8,128)(2,1)S(1)} %get-tuple-element.630), channel_id=1, source_target_pairs={{0,8},{4,12},{8,0},{12,4},{16,24},{20,28},{24,16},{28,20},{1,9},{5... | collective-permute-start | bytes 884744 | tf_op jit(solution)/shard_map/ppermute | solution.py:538
  381.5 12.3 %collective-permute-start.28 = (bf16[2,64,1152]{2,1,0:T(8,128)(2,1)S(1)}, bf16[2,64,1152]{2,1,0:T(8,128)(2,1)S(1)}, u32[]{:S(2)}, u32[]{:S(2)}) collective-permute-start(bf16[2,64,1152]{2,1,0:T(8,128)(2,1)S(1)} %get-tuple-element.651), channel_id=1, source_target_pairs={{0,16},{4,20},{8,24},{12,28},{16,0},{20,4},{24,8},{28,12},{1,17},{... | collective-permute-start | bytes 884744 | tf_op jit(solution)/shard_map/ppermute | solution.py:538
  412.5 139.4 %reduce-scatter.8.cloned.1.call-start = ((), (), s32[]{:S(2)}) async-start(), calls=%async_computation.5 | async-start | bytes 5640192 | tf_op jit(solution)/shard_map/reduce_scatter | solution.py:987
  412.5 20.5 %collective-permute-start.29 = (bf16[256,2048]{1,0:T(8,128)(2,1)}, bf16[256,2048]{1,0:T(8,128)(2,1)S(1)}, u32[]{:S(2)}, u32[]{:S(2)}) collective-permute-start(bf16[256,2048]{1,0:T(8,128)(2,1)} %get-tuple-element.677.refs_4_), channel_id=1, source_target_pairs={{0,1},{3,2},{1,0},{2,3},{4,5},{7,6},{5,4},{6,7},{8,9},{11,10},{9,8... | collective-permute-start | bytes 3145736 | tf_op jit(solution)/shard_map/ppermute | solution.py:618
  414.1 18.9 %collective-permute-start.30 = (bf16[256,2048]{1,0:T(8,128)(2,1)}, bf16[256,2048]{1,0:T(8,128)(2,1)S(1)}, u32[]{:S(2)}, u32[]{:S(2)}) collective-permute-start(bf16[256,2048]{1,0:T(8,128)(2,1)} %get-tuple-element.678.refs_2_), channel_id=1, source_target_pairs={{1,2},{2,1},{5,6},{6,5},{9,10},{10,9},{13,14},{14,13},{17,18},{18,... | collective-permute-start | bytes 3145736 | tf_op jit(solution)/shard_map/ppermute | solution.py:621
  423.5 9.6 %copy-start.7 = (bf16[256,2048]{1,0:T(8,128)(2,1)S(1)}, bf16[256,2048]{1,0:T(8,128)(2,1)}, u32[]{:S(2)}) copy-start(bf16[256,2048]{1,0:T(8,128)(2,1)} %copy-done.6) | copy-start | bytes 3145732
  437.4 25.6 %collective-permute-start.31 = (bf16[256,2048]{1,0:T(8,128)(2,1)}, bf16[256,2048]{1,0:T(8,128)(2,1)}, u32[]{:S(2)}, u32[]{:S(2)}) collective-permute-start(bf16[256,2048]{1,0:T(8,128)(2,1)} %get-tuple-element.694.refs_4_), channel_id=1, source_target_pairs={{0,1},{3,2},{1,0},{2,3},{4,5},{7,6},{5,4},{6,7},{8,9},{11,10},{9,8... | collective-permute-start | bytes 3145736 | tf_op jit(solution)/shard_map/ppermute | solution.py:618
  441.3 21.6 %collective-permute-start.32 = (bf16[256,2048]{1,0:T(8,128)(2,1)}, bf16[256,2048]{1,0:T(8,128)(2,1)}, u32[]{:S(2)}, u32[]{:S(2)}) collective-permute-start(bf16[256,2048]{1,0:T(8,128)(2,1)} %get-tuple-element.695.refs_2_), channel_id=1, source_target_pairs={{1,2},{2,1},{5,6},{6,5},{9,10},{10,9},{13,14},{14,13},{17,18},{18,... | collective-permute-start | bytes 3145736 | tf_op jit(solution)/shard_map/ppermute | solution.py:621
  451.1 11.9 %copy-start.5 = (bf16[256,2048]{1,0:T(8,128)(2,1)S(1)}, bf16[256,2048]{1,0:T(8,128)(2,1)}, u32[]{:S(2)}) copy-start(bf16[256,2048]{1,0:T(8,128)(2,1)} %copy-done.4) | copy-start | bytes 3145732
  468.5 15.1 %collective-permute-start.33 = (bf16[256,2048]{1,0:T(8,128)(2,1)}, bf16[256,2048]{1,0:T(8,128)(2,1)S(1)}, u32[]{:S(2)}, u32[]{:S(2)}) collective-permute-start(bf16[256,2048]{1,0:T(8,128)(2,1)} %copy-done.28), channel_id=1, source_target_pairs={{0,1},{3,2},{1,0},{2,3},{4,5},{7,6},{5,4},{6,7},{8,9},{11,10},{9,8... | collective-permute-start | bytes 3145736 | tf_op jit(solution)/shard_map/ppermute | solution.py:618
  469.5 14.1 %collective-permute-start.34 = (bf16[256,2048]{1,0:T(8,128)(2,1)}, bf16[256,2048]{1,0:T(8,128)(2,1)S(1)}, u32[]{:S(2)}, u32[]{:S(2)}) collective-permute-start(bf16[256,2048]{1,0:T(8,128)(2,1)} %copy-done.26), channel_id=1, source_target_pairs={{1,2},{2,1},{5,6},{6,5},{9,10},{10,9},{13,14},{14,13},{17,18},{18,... | collective-permute-start | bytes 3145736 | tf_op jit(solution)/shard_map/ppermute | solution.py:621
  472.4 11.2 %copy-start.27 = (bf16[256,2048]{1,0:T(8,128)(2,1)S(1)}, bf16[256,2048]{1,0:T(8,128)(2,1)}, u32[]{:S(2)}) copy-start(bf16[256,2048]{1,0:T(8,128)(2,1)} %copy-done.26) | copy-start | bytes 3145732
  472.4 11.2 %copy-start.29 = (bf16[256,2048]{1,0:T(8,128)(2,1)S(1)}, bf16[256,2048]{1,0:T(8,128)(2,1)}, u32[]{:S(2)}) copy-start(bf16[256,2048]{1,0:T(8,128)(2,1)} %copy-done.28) | copy-start | bytes 3145732
  490.6 25.1 %collective-permute-start.35 = (bf16[256,2048]{1,0:T(8,128)(2,1)}, bf16[256,2048]{1,0:T(8,128)(2,1)S(1)}, u32[]{:S(2)}, u32[]{:S(2)}) collective-permute-start(bf16[256,2048]{1,0:T(8,128)(2,1)} %copy-done.16), channel_id=1, source_target_pairs={{0,1},{3,2},{1,0},{2,3},{4,5},{7,6},{5,4},{6,7},{8,9},{11,10},{9,8... | collective-permute-start | bytes 3145736 | tf_op jit(solution)/shard_map/ppermute | solution.py:618
  492.1 23.6 %collective-permute-start.36 = (bf16[256,2048]{1,0:T(8,128)(2,1)S(1)}, bf16[256,2048]{1,0:T(8,128)(2,1)S(1)}, u32[]{:S(2)}, u32[]{:S(2)}) collective-permute-start(bf16[256,2048]{1,0:T(8,128)(2,1)S(1)} %get-tuple-element.755.refs_2_), channel_id=1, source_target_pairs={{1,2},{2,1},{5,6},{6,5},{9,10},{10,9},{13,14},{14,13},{17,18},{18,... | collective-permute-start | bytes 3145736 | tf_op jit(solution)/shard_map/ppermute | solution.py:621
  499.4 16.3 %copy-start.17 = (bf16[256,2048]{1,0:T(8,128)(2,1)S(1)}, bf16[256,2048]{1,0:T(8,128)(2,1)}, u32[]{:S(2)}) copy-start(bf16[256,2048]{1,0:T(8,128)(2,1)} %copy-done.16) | copy-start | bytes 3145732
  501.7 18.4 %copy-start.51 = (bf16[1,2,256,1408]{3,2,1,0:T(8,128)(2,1)S(1)}, bf16[1,2,256,1408]{3,2,1,0:T(8,128)(2,1)}, u32[]{:S(2)}) copy-start(bf16[1,2,256,1408]{3,2,1,0:T(8,128)(2,1)} %reduce-scatter.4.cloned.1.call-done) | copy-start | bytes 4325380
  517.9 28.2 %collective-permute-start.37 = (bf16[256,2048]{1,0:T(8,128)(2,1)}, bf16[256,2048]{1,0:T(8,128)(2,1)S(1)}, u32[]{:S(2)}, u32[]{:S(2)}) collective-permute-start(bf16[256,2048]{1,0:T(8,128)(2,1)} %get-tuple-element.765.refs_3_), channel_id=1, source_target_pairs={{1,0},{2,3},{5,4},{6,7},{9,8},{10,11},{13,12},{14,15},{17,16},{18,... | collective-permute-start | bytes 3145736 | tf_op jit(solution)/shard_map/ppermute | solution.py:618
  519.3 26.8 %collective-permute-start.38 = (bf16[256,2048]{1,0:T(8,128)(2,1)S(1)}, bf16[256,2048]{1,0:T(8,128)(2,1)S(1)}, u32[]{:S(2)}, u32[]{:S(2)}) collective-permute-start(bf16[256,2048]{1,0:T(8,128)(2,1)S(1)} %get-tuple-element.766.refs_1_), channel_id=1, source_target_pairs={{1,2},{2,1},{5,6},{6,5},{9,10},{10,9},{13,14},{14,13},{17,18},{18,... | collective-permute-start | bytes 3145736 | tf_op jit(solution)/shard_map/ppermute | solution.py:621
  527.2 18.9 %copy-start.31 = (bf16[256,2048]{1,0:T(8,128)(2,1)S(1)}, bf16[256,2048]{1,0:T(8,128)(2,1)}, u32[]{:S(2)}) copy-start(bf16[256,2048]{1,0:T(8,128)(2,1)} %copy-done.30) | copy-start | bytes 3145732
  548.4 27.0 %collective-permute-start.39 = (bf16[256,2048]{1,0:T(8,128)(2,1)S(1)}, bf16[256,2048]{1,0:T(8,128)(2,1)S(1)}, u32[]{:S(2)}, u32[]{:S(2)}) collective-permute-start(bf16[256,2048]{1,0:T(8,128)(2,1)S(1)} %get-tuple-element.773.refs_1_), channel_id=1, source_target_pairs={{1,0},{2,3},{5,4},{6,7},{9,8},{10,11},{13,12},{14,15},{17,16},{18,... | collective-permute-start | bytes 3145736 | tf_op jit(solution)/shard_map/ppermute | solution.py:618
  551.8 7.2 %copy-start.49 = (bf16[1,272,1152]{2,1,0:T(8,128)(2,1)S(1)}, bf16[1,272,1152]{2,1,0:T(8,128)(2,1)}, u32[]{:S(2)}) copy-start(bf16[1,272,1152]{2,1,0:T(8,128)(2,1)} %reduce-scatter.8.cloned.1.call-done) | copy-start | bytes 1880068
  551.8 7.2 %copy-start.50 = (f32[256,1024]{1,0:T(8,128)S(1)}, f32[256,1024]{1,0:T(8,128)}, u32[]{:S(2)}) copy-start(f32[256,1024]{1,0:T(8,128)} %slice_convert_fusion) | copy-start | bytes 3145732
  553.9 9.8 %copy-start.33 = (bf16[256,2048]{1,0:T(8,128)(2,1)S(1)}, bf16[256,2048]{1,0:T(8,128)(2,1)}, u32[]{:S(2)}) copy-start(bf16[256,2048]{1,0:T(8,128)(2,1)} %copy-done.32) | copy-start | bytes 3145732
  553.9 13.0 %collective-permute-start.42 = (f32[256]{0:T(256)S(1)}, f32[256]{0:T(256)S(1)}, u32[]{:S(2)}, u32[]{:S(2)}) collective-permute-start(f32[256]{0:T(256)S(1)} %get-tuple-element.821), channel_id=1, source_target_pairs={{0,3},{1,2},{2,1},{3,0},{4,7},{5,6},{6,5},{7,4},{8,11},{9,10},{10,... | collective-permute-start | bytes 3080 | tf_op jit(solution)/shard_map/ppermute | solution.py:1008
  556.2 10.6 %collective-permute-start.41 = (f32[256]{0:T(256)S(1)}, f32[256]{0:T(256)S(1)}, u32[]{:S(2)}, u32[]{:S(2)}) collective-permute-start(f32[256]{0:T(256)S(1)} %get-tuple-element.821), channel_id=1, source_target_pairs={{0,2},{1,3},{2,0},{3,1},{4,6},{5,7},{6,4},{7,5},{8,10},{9,11},{10,... | collective-permute-start | bytes 3080 | tf_op jit(solution)/shard_map/ppermute | solution.py:1008
  559.1 15.8 %collective-permute-start.40 = (f32[256]{0:T(256)S(1)}, f32[256]{0:T(256)S(1)}, u32[]{:S(2)}, u32[]{:S(2)}) collective-permute-start(f32[256]{0:T(256)S(1)} %get-tuple-element.821), channel_id=1, source_target_pairs={{0,1},{1,0},{2,3},{3,2},{4,5},{5,4},{6,7},{7,6},{8,9},{9,8},{10,11... | collective-permute-start | bytes 3080 | tf_op jit(solution)/shard_map/ppermute | solution.py:1008
  (36 other events, 59.9 us)
Sparse Core Ops, SparseCore 0:
  56.3 101.0 all-gather.2
  292.0 91.9 reduce-scatter.3
  412.6 77.9 reduce-scatter.5
  494.0 55.7 reduce-scatter.7

commit v9 on v7

--- a/solution.py
+++ b/solution.py
@@ -905,6 +905,7 @@
     end(live.pop(("ffn_part", 0, 1)), ("dhn", 1, 0))
     start()
     go_back(1, 0)
+    live["down"] = down_grads(taken("act"))
     end(live.pop(("ffn_part", 1, 0)), ("dhn", 1, 1))
     start()
     go_back(1, 1)
@@ -926,16 +927,10 @@
         live["xn"] = xn
         end(behind_of(live.pop(("ffn_part", 1, 1)), got), ("ffn", 0, 0))
         start()
-        made.append(live.pop("xn"))
+        made.extend((live.pop("xn"), live.pop("down")))
         return state
 
     def beside_second(state, got):
-        acts = taken("act")
-        acts[0] = behind_of(acts[0], state)
-        made.append(down_grads(acts))
-        return behind_of(state, made[1])
-
-    def beside_third(state, got):
         grads = call(
             "query_grads",
             functools.partial(query_grad_kernel, len(every), units),
@@ -944,14 +939,14 @@
             anywhere,
             shaped((n_seq, span, units + 2 * head), bf16),
             [pltpu.VMEM((2, group, span, 2 * head), bf16), pltpu.SemaphoreType.DMA((2,))],
-            cost=cost(4 * rows * width * head, 4 * rows * width + 4 * rows * head + 4 * width * head),
+            cost=cost(12 * rows * width * head, 3 * (4 * rows * width + 4 * rows * head + 4 * width * head)),
             aliases={1 + 3 * len(every): 0},
         )(behind_of(made[0], state), *[backs[key][0] for key in every], *[backs[key][1] for key in every],
           *[reads[key][0] for key in every], made[1])
         made.append(grads)
         return behind_of(state, grads)
 
-    ties = [beside_first, beside_second, beside_third]
+    ties = [beside_first, beside_second]
     live["leaving"] = scan_states(n_seq, *folded, True, own, pieces, ties)
     live["query_grads"], live["wide"] = made[2], wide_shares
     go_last(0, 0)
@@ -961,10 +956,10 @@
     down_shares = lax.psum_scatter(live.pop("query_grads"), "seq", scatter_dimension=0)
     go_last(0, 1)
     go_last(1, 0)
-    go_last(1, 1)
     live["xn"] = xn
     end(live.pop(("dxn_part", 0, 1)), ("ffn", 1, 0))
     start()
+    go_last(1, 1)
     live.pop("leaving")
     few = [pl.BlockSpec((8, TILE), lambda j: (0, j))] * len(every)
     live["state_grads"] = call(

time: 550 us -> 540 us (0.982)
  the two profiles are of different devices: /device:TPU:2 before, /device:TPU:4 now
where the time goes in v9:
time: 540 us; the launch traced here: 532 us
  Pallas kernels  288 us (53%)
  waiting for transfers between devices  110 us (20%)
  starting transfers between devices  78.1 us (14%)
  local copies, waits for them, and re-layouts  30.3 us (6%)
  between operations  14.9 us (3%)
  other arithmetic  10.3 us (2%)
    pallas_call x30, Pallas kernels, run(): function(*[o if i in loose or spec.memory_space == pltpu.SMEM else pltpu....  266 us
    ppermute x18, waiting for transfers between devices, step(): outer = lax.ppermute(payload, 'head', way)  78.8 us
    ppermute x18, starting transfers between devices, step(): outer = lax.ppermute(payload, 'head', way)  52 us
    unnamed x105, local copies, waits for them, and re-layouts  27.8 us
    ppermute x6, waiting for transfers between devices, scan_states(): got = lax.ppermute(sent, 'seq', [(i, i ^ bit) for i in range(n)])  25.3 us
    pallas_call x25, Pallas kernels, in_vmem(): pl.pallas_call(kernel, name=name, in_specs=[pl.BlockSpec(memory_space=plt...  22.3 us
    ppermute x16, starting transfers between devices, step(): middle = lax.ppermute(pair, 'head', self.MIDDLE)  17.1 us
  transfers between devices with their start and end apart: 47, of which 15 were waited for; matrix products, arithmetic and copies ran while one was open for 3% of the time, Pallas kernels for 50%

profile of v9, /device:TPU:4, one launch (start us, length us, event | category | flops | bytes accessed | tf_op | source)
XLA Modules:
  0.0 531.9 jit_solution(7152569794984314183)
XLA Ops:
  7.2 14.9 %project.1 = (bf16[1024,2048]{1,0:T(8,128)(2,1)}, bf16[1024,512]{1,0:T(8,128)(2,1)}, bf16[1024,512]{1,0:T(8,128)(2,1)}, f32[1024,64]{1,0:T(8,128)}, f32[1024,64]...) custom-call(bf16[1024,2048]{1,0:T(8,128)(2,1)} %bitcast.35, ...), custom_call_target="tpu_custom_call" | custom-call | flops 4563402752 | bytes 16777216 | tf_op jit(solution)/shard_map/project/pallas_call | solution.py:62
  24.1 2.7 pad_maximum_fusion
  28.7 7.6 %collective-permute-done.1.refs_2_ = bf16[2,64,1152]{2,1,0:T(8,128)(2,1)S(1)} collective-permute-done((bf16[2,64,1152]{2,1,0:T(8,128)(2,1)S(1)}, bf16[2,64,1152]{2,1,0:T(8,128)(2,1)S(1)}, u32[]{:S(2)}, u32[]{:S(2)}) %collective-permute-start.1) | collective-permute-done | bytes 294944 | tf_op jit(solution)/shard_map/ppermute | solution.py:521
  36.8 6.6 %query.1.q_ref = bf16[1024,512]{1,0:T(8,128)(2,1)} custom-call(bf16[1024,2048]{1,0:T(8,128)(2,1)} %get-tuple-element.715.xn_ref.refs_0_, bf16[2048,512]{1,0:T(8,128)(2,1)} %wq_ref.9), custom_call_target="tpu_custom_call" | custom-call | flops 2147483648 | bytes 7340032 | tf_op jit(solution)/shard_map/query/pallas_call | solution.py:62
  43.4 7.9 %collective-permute-done.2.refs_2_ = bf16[2,64,1152]{2,1,0:T(8,128)(2,1)S(1)} collective-permute-done((bf16[2,64,1152]{2,1,0:T(8,128)(2,1)S(1)}, bf16[2,64,1152]{2,1,0:T(8,128)(2,1)S(1)}, u32[]{:S(2)}, u32[]{:S(2)}) %collective-permute-start.2) | collective-permute-done | bytes 294944 | tf_op jit(solution)/shard_map/ppermute | solution.py:521
  51.6 5.3 read.4
  56.9 3.4 collective-permute-start.3
  60.3 5.3 %read.5 = (bf16[256,512]{1,0:T(8,128)(2,1)}, f32[256,64]{1,0:T(8,128)}, f32[256,64]{1,0:T(8,128)}, f32[2,64,1024]{2,1,0:T(8,128)}, f32[1,64,1024]{2,1,0:T(8,128)}, /*index=5*/bf16[256,2048]{1,0:T(8,128)(2,1)S(1)}) custom-call(bf16[1024,512]{1,0:T(8,128)(2,1)} %query.1.q_ref, bf16[1024,512]{1,0:T(8,128)(2,1)} %get-tuple-element.399.k_ref, ...), custom_call_target="tpu_custom_call" | custom-call | flops 694157312 | bytes 4194304 | tf_op jit(solution)/shard_map/read/pallas_call | solution.py:62
  65.6 14.3 %collective-permute-done.3.refs_1_ = bf16[256,2048]{1,0:T(8,128)(2,1)S(1)} collective-permute-done((bf16[256,2048]{1,0:T(8,128)(2,1)S(1)}, bf16[256,2048]{1,0:T(8,128)(2,1)S(1)}, u32[]{:S(2)}, u32[]{:S(2)}) %collective-permute-start.3) | collective-permute-done | bytes 1048608 | tf_op jit(solution)/shard_map/ppermute | solution.py:601
  80.0 4.5 collective-permute-start.4
  85.2 5.2 read.6
  90.5 12.9 %collective-permute-done.4.refs_1_ = bf16[256,2048]{1,0:T(8,128)(2,1)S(1)} collective-permute-done((bf16[256,2048]{1,0:T(8,128)(2,1)S(1)}, bf16[256,2048]{1,0:T(8,128)(2,1)S(1)}, u32[]{:S(2)}, u32[]{:S(2)}) %collective-permute-start.4) | collective-permute-done | bytes 1048608 | tf_op jit(solution)/shard_map/ppermute | solution.py:601
  103.4 4.3 collective-permute-start.6
  108.5 5.3 %read.7 = (bf16[256,512]{1,0:T(8,128)(2,1)}, f32[256,64]{1,0:T(8,128)}, f32[256,64]{1,0:T(8,128)}, f32[2,64,1024]{2,1,0:T(8,128)}, f32[1,64,1024]{2,1,0:T(8,128)}, /*index=5*/bf16[256,2048]{1,0:T(8,128)(2,1)S(1)}) custom-call(bf16[1024,512]{1,0:T(8,128)(2,1)} %query.1.q_ref, bf16[1024,512]{1,0:T(8,128)(2,1)} %get-tuple-element.399.k_ref, ...), custom_call_target="tpu_custom_call" | custom-call | flops 694157312 | bytes 4194304 | tf_op jit(solution)/shard_map/read/pallas_call | solution.py:62
  113.8 13.1 %collective-permute-done.6.refs_1_ = bf16[256,2048]{1,0:T(8,128)(2,1)S(1)} collective-permute-done((bf16[256,2048]{1,0:T(8,128)(2,1)S(1)}, bf16[256,2048]{1,0:T(8,128)(2,1)S(1)}, u32[]{:S(2)}, u32[]{:S(2)}) %collective-permute-start.6) | collective-permute-done | bytes 1048608 | tf_op jit(solution)/shard_map/ppermute | solution.py:601
  128.1 3.8 collective-permute-start.8
  131.9 1.9 collective-permute-start.9
  135.0 19.4 %feed.4 = (bf16[256,2048]{1,0:T(8,128)(2,1)}, bf16[256,2048]{1,0:T(8,128)(2,1)}, bf16[256,1408]{1,0:T(8,128)(2,1)}, bf16[256,1408]{1,0:T(8,128)(2,1)}, bf16[256,...) custom-call(bf16[1024,2048]{1,0:T(8,128)(2,1)} %bitcast.36, ...), custom_call_target="tpu_custom_call" | custom-call | flops 8858370048 | bytes 24641536 | tf_op jit(solution)/shard_map/feed/pallas_call | solution.py:62
  156.2 2.1 collective-permute-start.10
  159.6 19.4 %feed.5 = (bf16[256,2048]{1,0:T(8,128)(2,1)}, bf16[256,2048]{1,0:T(8,128)(2,1)}, bf16[256,1408]{1,0:T(8,128)(2,1)}, bf16[256,1408]{1,0:T(8,128)(2,1)}, bf16[256,...) custom-call(bf16[1024,2048]{1,0:T(8,128)(2,1)} %bitcast.37, ...), custom_call_target="tpu_custom_call" | custom-call | flops 8858370048 | bytes 24641536 | tf_op jit(solution)/shard_map/feed/pallas_call | solution.py:62
  179.2 3.0 collective-permute-start.12
  183.1 19.4 %feed.6 = (bf16[256,2048]{1,0:T(8,128)(2,1)}, bf16[256,2048]{1,0:T(8,128)(2,1)}, bf16[256,1408]{1,0:T(8,128)(2,1)}, bf16[256,1408]{1,0:T(8,128)(2,1)}, bf16[256,...) custom-call(bf16[1024,2048]{1,0:T(8,128)(2,1)} %bitcast.38, ...), custom_call_target="tpu_custom_call" | custom-call | flops 8858370048 | bytes 24641536 | tf_op jit(solution)/shard_map/feed/pallas_call | solution.py:62
  202.8 1.9 collective-permute-start.14
  205.6 19.5 %feed.7 = (bf16[256,2048]{1,0:T(8,128)(2,1)}, bf16[256,2048]{1,0:T(8,128)(2,1)}, bf16[256,1408]{1,0:T(8,128)(2,1)}, bf16[256,1408]{1,0:T(8,128)(2,1)}, bf16[256,...) custom-call(bf16[1024,2048]{1,0:T(8,128)(2,1)} %bitcast.39, ...), custom_call_target="tpu_custom_call" | custom-call | flops 8858370048 | bytes 24641536 | tf_op jit(solution)/shard_map/feed/pallas_call | solution.py:62
  226.6 3.0 collective-permute-start.16
  231.3 19.0 %wide_grads.1 = bf16[8,2,256,1408]{3,2,1,0:T(8,128)(2,1)} custom-call(bf16[256,2048]{1,0:T(8,128)(2,1)} %get-tuple-element.545.refs_0_, bf16[256,2048]{1,0:T(8,128)(2,1)} %get-tuple-element.546.refs_1_, bf16[256,2048]{1,0:T(8,128)(2,1)} %get-tuple-element.547.refs_2_, bf16[256,2048]{1,0:T(8,128)(2,1)} %get-tuple-element.548.refs_3_, ...), custom_call_target="tpu_custom_call" | custom-call | flops 11811160064 | bytes 21495808 | tf_op jit(solution)/shard_map/wide_grads/pallas_call | solution.py:62
  250.3 2.3 join.25
  258.1 8.4 %back.4 = (bf16[256,2048]{1,0:T(8,128)(2,1)}, bf16[256,512]{1,0:T(8,128)(2,1)}, f32[256,512]{1,0:T(8,128)}, f32[256,512]{1,0:T(8,128)}, f32[256,64]{1,0:T(8,128)...) custom-call(bf16[256,2048]{1,0:T(8,128)(2,1)S(1)} %get-tuple-element, ...), custom_call_target="tpu_custom_call" | custom-call | flops 930086912 | bytes 9961472 | tf_op jit(solution)/shard_map/back/pallas_call | solution.py:62
  266.6 9.6 %back.5 = (bf16[256,2048]{1,0:T(8,128)(2,1)}, bf16[256,512]{1,0:T(8,128)(2,1)}, f32[256,512]{1,0:T(8,128)}, f32[256,512]{1,0:T(8,128)}, f32[256,64]{1,0:T(8,128)...) custom-call(bf16[256,2048]{1,0:T(8,128)(2,1)S(1)} %copy-done.15, ...), custom_call_target="tpu_custom_call" | custom-call | flops 930086912 | bytes 9961472 | tf_op jit(solution)/shard_map/back/pallas_call | solution.py:62
  276.4 4.8 collective-permute-start.20
  281.9 9.2 %back.6 = (bf16[256,2048]{1,0:T(8,128)(2,1)}, bf16[256,512]{1,0:T(8,128)(2,1)}, f32[256,512]{1,0:T(8,128)}, f32[256,512]{1,0:T(8,128)}, f32[256,64]{1,0:T(8,128)...) custom-call(bf16[256,2048]{1,0:T(8,128)(2,1)S(1)} %get-tuple-element, ...), custom_call_target="tpu_custom_call" | custom-call | flops 930086912 | bytes 9961472 | tf_op jit(solution)/shard_map/back/pallas_call | solution.py:62
  291.1 10.8 %down_grads.1.refs_13_ = bf16[8,256,2432]{2,1,0:T(8,128)(2,1)} custom-call(bf16[1024,2048]{1,0:T(8,128)(2,1)} %bitcast.55, bf16[256,1408]{1,0:T(8,128)(2,1)} %get-tuple-element.599.refs_1_, bf16[256,1408]{1,0:T(8,128)(2,1)} %get-tuple-element.600.refs_2_, bf16[256,1408]{1,0:T(8,128)(2,1)} %get-tuple-element.601.refs_3_, ...), custom_call_target="tpu_custom_call" | custom-call | flops 5905580032 | bytes 12845056 | tf_op jit(solution)/shard_map/down_grads/pallas_call | solution.py:62
  302.0 2.1 collective-permute-start.23
  304.8 8.4 %back.7 = (bf16[256,2048]{1,0:T(8,128)(2,1)}, bf16[256,512]{1,0:T(8,128)(2,1)}, f32[256,512]{1,0:T(8,128)}, f32[256,512]{1,0:T(8,128)}, f32[256,64]{1,0:T(8,128)...) custom-call(bf16[256,2048]{1,0:T(8,128)(2,1)S(1)} %get-tuple-element, ...), custom_call_target="tpu_custom_call" | custom-call | flops 930086912 | bytes 9961472 | tf_op jit(solution)/shard_map/back/pallas_call | solution.py:62
  321.7 4.2 collective-permute-start.25
  327.6 11.1 %query_grads.1 = bf16[8,256,2432]{2,1,0:T(8,128)(2,1)} custom-call(bf16[1024,2048]{1,0:T(8,128)(2,1)} %get-tuple-element.715.xn_ref.refs_0_, bf16[256,2048]{1,0:T(8,128)(2,1)} %get-tuple-element.633.refs_1_.dhid_ref, bf16[256,2048]{1,0:T(8,128)(2,1)} %get-tuple-element.634.refs_2_.dhid_ref, ...), custom_call_target="tpu_custom_call", output_to_operand_aliasing={{}: (13, {})} | custom-call | flops 12884901888 | bytes 44040192 | tf_op jit(solution)/shard_map/query_grads/pallas_call | solution.py:62
  340.8 6.7 %collective-permute-done.28.refs_2_ = bf16[2,64,1152]{2,1,0:T(8,128)(2,1)S(1)} collective-permute-done((bf16[2,64,1152]{2,1,0:T(8,128)(2,1)S(1)}, bf16[2,64,1152]{2,1,0:T(8,128)(2,1)S(1)}, u32[]{:S(2)}, u32[]{:S(2)}) %collective-permute-start.28) | collective-permute-done | bytes 294944 | tf_op jit(solution)/shard_map/ppermute | solution.py:521
  348.6 8.1 %last.4 = (bf16[256,512]{1,0:T(8,128)(2,1)}, bf16[256,512]{1,0:T(8,128)(2,1)}, bf16[256,64]{1,0:T(8,128)(2,1)}, bf16[256,2048]{1,0:T(8,128)(2,1)S(1)}, f32[8,64]{1,0:T(8,128)}, /*index=5*/f32[8,2048]{1,0:T(8,128)}) custom-call(f32[4,64,1024]{2,1,0:T(8,128)S(1)} %hop.11.l0_ref, bf16[1024,512]{1,0:T(8,128)(2,1)} %get-tuple-element.399.k_ref, ...), custom_call_target="tpu_custom_call" | custom-call | flops 1677721600 | bytes 13107200 | tf_op jit(solution)/shard_map/last/pallas_call | solution.py:62
  356.7 3.7 join.29
  365.0 9.0 %last.6 = (bf16[256,512]{1,0:T(8,128)(2,1)}, bf16[256,512]{1,0:T(8,128)(2,1)}, bf16[256,64]{1,0:T(8,128)(2,1)}, bf16[256,2048]{1,0:T(8,128)(2,1)S(1)}, f32[8,64]{1,0:T(8,128)}, /*index=5*/f32[8,2048]{1,0:T(8,128)}) custom-call(f32[4,64,1024]{2,1,0:T(8,128)S(1)} %hop.11.l0_ref, bf16[1024,512]{1,0:T(8,128)(2,1)} %get-tuple-element.399.k_ref, ...), custom_call_target="tpu_custom_call" | custom-call | flops 1677721600 | bytes 13107200 | tf_op jit(solution)/shard_map/last/pallas_call | solution.py:62
  374.0 9.8 %last.5 = (bf16[256,512]{1,0:T(8,128)(2,1)}, bf16[256,512]{1,0:T(8,128)(2,1)}, bf16[256,64]{1,0:T(8,128)(2,1)}, bf16[256,2048]{1,0:T(8,128)(2,1)S(1)}, f32[8,64]{1,0:T(8,128)}, /*index=5*/f32[8,2048]{1,0:T(8,128)}) custom-call(f32[4,64,1024]{2,1,0:T(8,128)S(1)} %hop.11.l0_ref, bf16[1024,512]{1,0:T(8,128)(2,1)} %get-tuple-element.399.k_ref, ...), custom_call_target="tpu_custom_call" | custom-call | flops 1677721600 | bytes 13107200 | tf_op jit(solution)/shard_map/last/pallas_call | solution.py:62
  384.7 3.0 join.30
  388.7 3.8 collective-permute-start.31
  394.1 8.4 %last.7 = (bf16[256,512]{1,0:T(8,128)(2,1)}, bf16[256,512]{1,0:T(8,128)(2,1)}, bf16[256,64]{1,0:T(8,128)(2,1)}, bf16[256,2048]{1,0:T(8,128)(2,1)S(1)}, f32[8,64]{1,0:T(8,128)}, /*index=5*/f32[8,2048]{1,0:T(8,128)}) custom-call(f32[4,64,1024]{2,1,0:T(8,128)S(1)} %hop.11.l0_ref, bf16[1024,512]{1,0:T(8,128)(2,1)} %get-tuple-element.399.k_ref, ...), custom_call_target="tpu_custom_call" | custom-call | flops 1677721600 | bytes 13107200 | tf_op jit(solution)/shard_map/last/pallas_call | solution.py:62
  402.5 11.5 %state_grads.1 = bf16[8,272,1152]{2,1,0:T(8,128)(2,1)} custom-call(bf16[1024,2048]{1,0:T(8,128)(2,1)} %get-tuple-element.715.xn_ref.refs_0_, bf16[256,512]{1,0:T(8,128)(2,1)} %get-tuple-element.716.refs_1_, bf16[256,512]{1,0:T(8,128)(2,1)} %get-tuple-element.717.refs_2_, bf16[256,512]{1,0:T(8,128)(2,1)} %get-tuple-element.718.refs_3_, ...), custom_call_target="tpu_custom_call" | custom-call | flops 4294967296 | bytes 10485760 | tf_op jit(solution)/shard_map/state_grads/pallas_call | solution.py:62
  414.0 2.4 join.31
  421.9 2.1 out.4.refs_0_
  424.1 2.6 out.5.refs_0_
  426.7 13.4 %collective-permute-done.33.refs_1_ = bf16[256,2048]{1,0:T(8,128)(2,1)S(1)} collective-permute-done((bf16[256,2048]{1,0:T(8,128)(2,1)}, bf16[256,2048]{1,0:T(8,128)(2,1)S(1)}, u32[]{:S(2)}, u32[]{:S(2)}) %collective-permute-start.33) | collective-permute-done | bytes 1048608 | tf_op jit(solution)/shard_map/ppermute | solution.py:601
  442.3 3.9 collective-permute-start.35
  448.1 3.1 in_grad.4.refs_0_
  451.2 2.3 out.6.refs_0_
  453.5 2.3 out.7
  455.8 10.6 %collective-permute-done.35.refs_1_ = bf16[256,2048]{1,0:T(8,128)(2,1)S(1)} collective-permute-done((bf16[256,2048]{1,0:T(8,128)(2,1)}, bf16[256,2048]{1,0:T(8,128)(2,1)S(1)}, u32[]{:S(2)}, u32[]{:S(2)}) %collective-permute-start.35) | collective-permute-done | bytes 1048608 | tf_op jit(solution)/shard_map/ppermute | solution.py:601
  473.7 2.9 copy.48
  477.8 3.2 in_grad.5.refs_0_
  481.1 13.1 %collective-permute-done.37.refs_0_ = bf16[256,2048]{1,0:T(8,128)(2,1)S(1)} collective-permute-done((bf16[256,2048]{1,0:T(8,128)(2,1)}, bf16[256,2048]{1,0:T(8,128)(2,1)S(1)}, u32[]{:S(2)}, u32[]{:S(2)}) %collective-permute-start.37) | collective-permute-done | bytes 1048608 | tf_op jit(solution)/shard_map/ppermute | solution.py:601
  497.8 2.2 slice_convert_fusion
  502.5 3.3 collective-permute-start.42
  505.8 1.8 collective-permute-start.41
  510.5 2.0 copy.47
  512.5 3.2 in_grad.6.refs_0_
  515.7 5.6 %collective-permute-done.40 = f32[256]{0:T(256)S(1)} collective-permute-done((f32[256]{0:T(256)S(1)}, f32[256]{0:T(256)S(1)}, u32[]{:S(2)}, u32[]{:S(2)}) %collective-permute-start.40) | collective-permute-done | bytes 1056 | tf_op jit(solution)/shard_map/ppermute | solution.py:997
  522.0 3.2 in_grad.7
  (205 shorter events, 73.2 us)
Async XLA Ops:
  7.2 126.6 %all-gather.3.cloned.1.call-start = ((), (), s32[]{:S(2)}) async-start(), calls=%async_computation.6 | async-start | bytes 19464192 | tf_op jit(solution)/shard_map/all_gather | solution.py:686
  7.2 16.5 %copy-start.49 = (bf16[1408,256]{1,0:T(8,128)(2,1)S(1)}, bf16[1408,256]{1,0:T(8,128)(2,1)}, u32[]{:S(2)}) copy-start(bf16[1408,256]{1,0:T(8,128)(2,1)} %param.24) | copy-start | bytes 2162692
  7.2 16.8 %copy-start.50 = (bf16[256,1408]{1,0:T(8,128)(2,1)S(1)}, bf16[256,1408]{1,0:T(8,128)(2,1)}, u32[]{:S(2)}) copy-start(bf16[256,1408]{1,0:T(8,128)(2,1)} %param.23) | copy-start | bytes 2162692
  22.1 1.6 collective-permute-start
  26.8 335.5 %reduce-scatter.4.cloned.1.call-start = ((), (), s32[]{:S(2)}) async-start(), calls=%async_computation.3 | async-start | bytes 12976128 | tf_op jit(solution)/shard_map/reduce_scatter | solution.py:902
  27.1 9.1 %collective-permute-start.1 = (bf16[2,64,1152]{2,1,0:T(8,128)(2,1)S(1)}, bf16[2,64,1152]{2,1,0:T(8,128)(2,1)S(1)}, u32[]{:S(2)}, u32[]{:S(2)}) collective-permute-start(bf16[2,64,1152]{2,1,0:T(8,128)(2,1)S(1)} %get-tuple-element.408), channel_id=1, source_target_pairs={{0,8},{4,12},{8,0},{12,4},{16,24},{20,28},{24,16},{28,20},{1,9},{5... | collective-permute-start | bytes 884744 | tf_op jit(solution)/shard_map/ppermute | solution.py:521
  36.5 14.8 %collective-permute-start.2 = (bf16[2,64,1152]{2,1,0:T(8,128)(2,1)S(1)}, bf16[2,64,1152]{2,1,0:T(8,128)(2,1)S(1)}, u32[]{:S(2)}, u32[]{:S(2)}) collective-permute-start(bf16[2,64,1152]{2,1,0:T(8,128)(2,1)S(1)} %get-tuple-element.413), channel_id=1, source_target_pairs={{0,16},{4,20},{8,24},{12,28},{16,0},{20,4},{24,8},{28,12},{1,17},{... | collective-permute-start | bytes 884744 | tf_op jit(solution)/shard_map/ppermute | solution.py:521
  56.9 23.0 %collective-permute-start.3 = (bf16[256,2048]{1,0:T(8,128)(2,1)S(1)}, bf16[256,2048]{1,0:T(8,128)(2,1)S(1)}, u32[]{:S(2)}, u32[]{:S(2)}) collective-permute-start(bf16[256,2048]{1,0:T(8,128)(2,1)S(1)} %get-tuple-element.420.refs_0_), channel_id=1, source_target_pairs={{0,1},{3,2},{4,5},{7,6},{8,9},{11,10},{12,13},{15,14},{16,17},{19,... | collective-permute-start | bytes 3145736 | tf_op jit(solution)/shard_map/ppermute | solution.py:601
  80.0 23.3 %collective-permute-start.4 = (bf16[256,2048]{1,0:T(8,128)(2,1)S(1)}, bf16[256,2048]{1,0:T(8,128)(2,1)S(1)}, u32[]{:S(2)}, u32[]{:S(2)}) collective-permute-start(bf16[256,2048]{1,0:T(8,128)(2,1)S(1)} %get-tuple-element.424), channel_id=1, source_target_pairs={{0,1},{3,2},{4,5},{7,6},{8,9},{11,10},{12,13},{15,14},{16,17},{19,... | collective-permute-start | bytes 3145736 | tf_op jit(solution)/shard_map/ppermute | solution.py:601
  84.5 18.8 %collective-permute-start.5 = (bf16[256,2048]{1,0:T(8,128)(2,1)S(1)}, bf16[256,2048]{1,0:T(8,128)(2,1)S(1)}, u32[]{:S(2)}, u32[]{:S(2)}) collective-permute-start(bf16[256,2048]{1,0:T(8,128)(2,1)S(1)} %get-tuple-element.425.refs_2_), channel_id=1, source_target_pairs={{1,2},{2,1},{5,6},{6,5},{9,10},{10,9},{13,14},{14,13},{17,18},{18,... | collective-permute-start | bytes 3145736 | tf_op jit(solution)/shard_map/ppermute | solution.py:604
  103.4 23.4 %collective-permute-start.6 = (bf16[256,2048]{1,0:T(8,128)(2,1)S(1)}, bf16[256,2048]{1,0:T(8,128)(2,1)S(1)}, u32[]{:S(2)}, u32[]{:S(2)}) collective-permute-start(bf16[256,2048]{1,0:T(8,128)(2,1)S(1)} %get-tuple-element.433.refs_4_), channel_id=1, source_target_pairs={{0,1},{3,2},{1,0},{2,3},{4,5},{7,6},{5,4},{6,7},{8,9},{11,10},{9,8... | collective-permute-start | bytes 3145736 | tf_op jit(solution)/shard_map/ppermute | solution.py:601
  107.7 19.1 %collective-permute-start.7 = (bf16[256,2048]{1,0:T(8,128)(2,1)S(1)}, bf16[256,2048]{1,0:T(8,128)(2,1)S(1)}, u32[]{:S(2)}, u32[]{:S(2)}) collective-permute-start(bf16[256,2048]{1,0:T(8,128)(2,1)S(1)} %get-tuple-element.434.refs_2_), channel_id=1, source_target_pairs={{1,2},{2,1},{5,6},{6,5},{9,10},{10,9},{13,14},{14,13},{17,18},{18,... | collective-permute-start | bytes 3145736 | tf_op jit(solution)/shard_map/ppermute | solution.py:604
  128.1 26.4 %collective-permute-start.8 = (bf16[256,2048]{1,0:T(8,128)(2,1)S(1)}, bf16[256,2048]{1,0:T(8,128)(2,1)}, u32[]{:S(2)}, u32[]{:S(2)}) collective-permute-start(bf16[256,2048]{1,0:T(8,128)(2,1)S(1)} %get-tuple-element.438.refs_4_), channel_id=1, source_target_pairs={{0,1},{3,2},{1,0},{2,3},{4,5},{7,6},{5,4},{6,7},{8,9},{11,10},{9,8... | collective-permute-start | bytes 3145736 | tf_op jit(solution)/shard_map/ppermute | solution.py:601
  131.9 22.6 %collective-permute-start.9 = (bf16[256,2048]{1,0:T(8,128)(2,1)S(1)}, bf16[256,2048]{1,0:T(8,128)(2,1)}, u32[]{:S(2)}, u32[]{:S(2)}) collective-permute-start(bf16[256,2048]{1,0:T(8,128)(2,1)S(1)} %get-tuple-element.439.refs_2_), channel_id=1, source_target_pairs={{1,2},{2,1},{5,6},{6,5},{9,10},{10,9},{13,14},{14,13},{17,18},{18,... | collective-permute-start | bytes 3145736 | tf_op jit(solution)/shard_map/ppermute | solution.py:604
  156.2 22.8 %collective-permute-start.10 = (bf16[256,2048]{1,0:T(8,128)(2,1)S(1)}, bf16[256,2048]{1,0:T(8,128)(2,1)S(1)}, u32[]{:S(2)}, u32[]{:S(2)}) collective-permute-start(bf16[256,2048]{1,0:T(8,128)(2,1)S(1)} %get-tuple-element.455.refs_4_), channel_id=1, source_target_pairs={{0,1},{3,2},{1,0},{2,3},{4,5},{7,6},{5,4},{6,7},{8,9},{11,10},{9,8... | collective-permute-start | bytes 3145736 | tf_op jit(solution)/shard_map/ppermute | solution.py:601
  158.3 20.7 %collective-permute-start.11 = (bf16[256,2048]{1,0:T(8,128)(2,1)S(1)}, bf16[256,2048]{1,0:T(8,128)(2,1)S(1)}, u32[]{:S(2)}, u32[]{:S(2)}) collective-permute-start(bf16[256,2048]{1,0:T(8,128)(2,1)S(1)} %get-tuple-element.456.refs_2_), channel_id=1, source_target_pairs={{1,2},{2,1},{5,6},{6,5},{9,10},{10,9},{13,14},{14,13},{17,18},{18,... | collective-permute-start | bytes 3145736 | tf_op jit(solution)/shard_map/ppermute | solution.py:604
  179.2 23.3 %collective-permute-start.12 = (bf16[256,2048]{1,0:T(8,128)(2,1)S(1)}, bf16[256,2048]{1,0:T(8,128)(2,1)S(1)}, u32[]{:S(2)}, u32[]{:S(2)}) collective-permute-start(bf16[256,2048]{1,0:T(8,128)(2,1)S(1)} %get-tuple-element.472.refs_4_), channel_id=1, source_target_pairs={{0,1},{3,2},{1,0},{2,3},{4,5},{7,6},{5,4},{6,7},{8,9},{11,10},{9,8... | collective-permute-start | bytes 3145736 | tf_op jit(solution)/shard_map/ppermute | solution.py:601
  182.2 20.4 %collective-permute-start.13 = (bf16[256,2048]{1,0:T(8,128)(2,1)S(1)}, bf16[256,2048]{1,0:T(8,128)(2,1)S(1)}, u32[]{:S(2)}, u32[]{:S(2)}) collective-permute-start(bf16[256,2048]{1,0:T(8,128)(2,1)S(1)} %get-tuple-element.473.refs_2_), channel_id=1, source_target_pairs={{1,2},{2,1},{5,6},{6,5},{9,10},{10,9},{13,14},{14,13},{17,18},{18,... | collective-permute-start | bytes 3145736 | tf_op jit(solution)/shard_map/ppermute | solution.py:604
  202.8 22.4 %collective-permute-start.14 = (bf16[256,2048]{1,0:T(8,128)(2,1)S(1)}, bf16[256,2048]{1,0:T(8,128)(2,1)S(1)}, u32[]{:S(2)}, u32[]{:S(2)}) collective-permute-start(bf16[256,2048]{1,0:T(8,128)(2,1)S(1)} %get-tuple-element.499.refs_4_), channel_id=1, source_target_pairs={{0,1},{3,2},{1,0},{2,3},{4,5},{7,6},{5,4},{6,7},{8,9},{11,10},{9,8... | collective-permute-start | bytes 3145736 | tf_op jit(solution)/shard_map/ppermute | solution.py:601
  204.7 20.5 %collective-permute-start.15 = (bf16[256,2048]{1,0:T(8,128)(2,1)S(1)}, bf16[256,2048]{1,0:T(8,128)(2,1)S(1)}, u32[]{:S(2)}, u32[]{:S(2)}) collective-permute-start(bf16[256,2048]{1,0:T(8,128)(2,1)S(1)} %get-tuple-element.500.refs_2_), channel_id=1, source_target_pairs={{1,2},{2,1},{5,6},{6,5},{9,10},{10,9},{13,14},{14,13},{17,18},{18,... | collective-permute-start | bytes 3145736 | tf_op jit(solution)/shard_map/ppermute | solution.py:604
  226.6 23.7 %copy-start.3 = (bf16[256,2048]{1,0:T(8,128)(2,1)S(1)}, bf16[256,2048]{1,0:T(8,128)(2,1)}, u32[]{:S(2)}) copy-start(bf16[256,2048]{1,0:T(8,128)(2,1)} %get-tuple-element.530.refs_5_.refs_0_) | copy-start | bytes 3145732
  226.6 23.7 %collective-permute-start.16 = (bf16[256,2048]{1,0:T(8,128)(2,1)}, bf16[256,2048]{1,0:T(8,128)(2,1)}, u32[]{:S(2)}, u32[]{:S(2)}) collective-permute-start(bf16[256,2048]{1,0:T(8,128)(2,1)} %get-tuple-element.528.refs_4_), channel_id=1, source_target_pairs={{0,1},{3,2},{1,0},{2,3},{4,5},{7,6},{5,4},{6,7},{8,9},{11,10},{9,8... | collective-permute-start | bytes 3145736 | tf_op jit(solution)/shard_map/ppermute | solution.py:601
  229.6 20.7 %collective-permute-start.17 = (bf16[256,2048]{1,0:T(8,128)(2,1)}, bf16[256,2048]{1,0:T(8,128)(2,1)}, u32[]{:S(2)}, u32[]{:S(2)}) collective-permute-start(bf16[256,2048]{1,0:T(8,128)(2,1)} %get-tuple-element.529.refs_2_), channel_id=1, source_target_pairs={{1,2},{2,1},{5,6},{6,5},{9,10},{10,9},{13,14},{14,13},{17,18},{18,... | collective-permute-start | bytes 3145736 | tf_op jit(solution)/shard_map/ppermute | solution.py:604
  255.7 186.5 %reduce-scatter.6.cloned.1.call-start = ((), (), s32[]{:S(2)}) async-start(), calls=%async_computation.4 | async-start | bytes 11206656 | tf_op jit(solution)/shard_map/reduce_scatter | solution.py:956
  255.8 20.4 %collective-permute-start.18 = (bf16[256,2048]{1,0:T(8,128)(2,1)}, bf16[256,2048]{1,0:T(8,128)(2,1)S(1)}, u32[]{:S(2)}, u32[]{:S(2)}) collective-permute-start(bf16[256,2048]{1,0:T(8,128)(2,1)} %copy-done.24), channel_id=1, source_target_pairs={{0,1},{3,2},{1,0},{2,3},{4,5},{7,6},{5,4},{6,7},{8,9},{11,10},{9,8... | collective-permute-start | bytes 3145736 | tf_op jit(solution)/shard_map/ppermute | solution.py:601
  257.0 19.2 %collective-permute-start.19 = (bf16[256,2048]{1,0:T(8,128)(2,1)S(1)}, bf16[256,2048]{1,0:T(8,128)(2,1)S(1)}, u32[]{:S(2)}, u32[]{:S(2)}) collective-permute-start(bf16[256,2048]{1,0:T(8,128)(2,1)S(1)} %copy-done.23), channel_id=1, source_target_pairs={{1,2},{2,1},{5,6},{6,5},{9,10},{10,9},{13,14},{14,13},{17,18},{18,... | collective-permute-start | bytes 3145736 | tf_op jit(solution)/shard_map/ppermute | solution.py:604
  258.1 8.4 %copy-start.15 = (bf16[256,2048]{1,0:T(8,128)(2,1)S(1)}, bf16[256,2048]{1,0:T(8,128)(2,1)}, u32[]{:S(2)}) copy-start(bf16[256,2048]{1,0:T(8,128)(2,1)} %copy-done.14) | copy-start | bytes 3145732
  266.6 9.6 %copy-start.2 = (bf16[256,2048]{1,0:T(8,128)(2,1)S(1)}, bf16[256,2048]{1,0:T(8,128)(2,1)}, u32[]{:S(2)}) copy-start(bf16[256,2048]{1,0:T(8,128)(2,1)} %get-tuple-element.558.refs_5_.refs_0_) | copy-start | bytes 3145732
  266.6 9.6 %copy-start.25 = (bf16[256,2048]{1,0:T(8,128)(2,1)S(1)}, bf16[256,2048]{1,0:T(8,128)(2,1)}, u32[]{:S(2)}) copy-start(bf16[256,2048]{1,0:T(8,128)(2,1)} %copy-done.24) | copy-start | bytes 3145732
  276.4 25.5 %collective-permute-start.20 = (bf16[256,2048]{1,0:T(8,128)(2,1)S(1)}, bf16[256,2048]{1,0:T(8,128)(2,1)S(1)}, u32[]{:S(2)}, u32[]{:S(2)}) collective-permute-start(bf16[256,2048]{1,0:T(8,128)(2,1)S(1)} %get-tuple-element.584.refs_4_), channel_id=1, source_target_pairs={{0,1},{3,2},{1,0},{2,3},{4,5},{7,6},{5,4},{6,7},{8,9},{11,10},{9,8... | collective-permute-start | bytes 3145736 | tf_op jit(solution)/shard_map/ppermute | solution.py:601
  281.2 20.7 %collective-permute-start.21 = (bf16[256,2048]{1,0:T(8,128)(2,1)S(1)}, bf16[256,2048]{1,0:T(8,128)(2,1)S(1)}, u32[]{:S(2)}, u32[]{:S(2)}) collective-permute-start(bf16[256,2048]{1,0:T(8,128)(2,1)S(1)} %get-tuple-element.585.refs_2_), channel_id=1, source_target_pairs={{1,2},{2,1},{5,6},{6,5},{9,10},{10,9},{13,14},{14,13},{17,18},{18,... | collective-permute-start | bytes 3145736 | tf_op jit(solution)/shard_map/ppermute | solution.py:604
  291.1 10.8 %copy-start.1 = (bf16[256,2048]{1,0:T(8,128)(2,1)S(1)}, bf16[256,2048]{1,0:T(8,128)(2,1)}, u32[]{:S(2)}) copy-start(bf16[256,2048]{1,0:T(8,128)(2,1)} %get-tuple-element.586.refs_5_.refs_0_) | copy-start | bytes 3145732
  302.0 17.1 %collective-permute-start.23 = (bf16[256,2048]{1,0:T(8,128)(2,1)S(1)}, bf16[256,2048]{1,0:T(8,128)(2,1)S(1)}, u32[]{:S(2)}, u32[]{:S(2)}) collective-permute-start(bf16[256,2048]{1,0:T(8,128)(2,1)S(1)} %get-tuple-element.617.refs_4_), channel_id=1, source_target_pairs={{0,1},{3,2},{1,0},{2,3},{4,5},{7,6},{5,4},{6,7},{8,9},{11,10},{9,8... | collective-permute-start | bytes 3145736 | tf_op jit(solution)/shard_map/ppermute | solution.py:601
  304.1 15.0 %collective-permute-start.24 = (bf16[256,2048]{1,0:T(8,128)(2,1)S(1)}, bf16[256,2048]{1,0:T(8,128)(2,1)S(1)}, u32[]{:S(2)}, u32[]{:S(2)}) collective-permute-start(bf16[256,2048]{1,0:T(8,128)(2,1)S(1)} %get-tuple-element.618.refs_2_), channel_id=1, source_target_pairs={{1,2},{2,1},{5,6},{6,5},{9,10},{10,9},{13,14},{14,13},{17,18},{18,... | collective-permute-start | bytes 3145736 | tf_op jit(solution)/shard_map/ppermute | solution.py:604
  313.4 1.6 collective-permute-start.22
  317.3 21.5 %collective-permute-start.27 = (bf16[2,64,1152]{2,1,0:T(8,128)(2,1)}, bf16[2,64,1152]{2,1,0:T(8,128)(2,1)S(1)}, u32[]{:S(2)}, u32[]{:S(2)}) collective-permute-start(bf16[2,64,1152]{2,1,0:T(8,128)(2,1)} %get-tuple-element.648), channel_id=1, source_target_pairs={{0,8},{4,12},{8,0},{12,4},{16,24},{20,28},{24,16},{28,20},{1,9},{5... | collective-permute-start | bytes 884744 | tf_op jit(solution)/shard_map/ppermute | solution.py:521
  321.7 35.0 %collective-permute-start.25 = (bf16[256,2048]{1,0:T(8,128)(2,1)}, bf16[256,2048]{1,0:T(8,128)(2,1)}, u32[]{:S(2)}, u32[]{:S(2)}) collective-permute-start(bf16[256,2048]{1,0:T(8,128)(2,1)} %get-tuple-element.626.refs_4_), channel_id=1, source_target_pairs={{0,1},{3,2},{1,0},{2,3},{4,5},{7,6},{5,4},{6,7},{8,9},{11,10},{9,8... | collective-permute-start | bytes 3145736 | tf_op jit(solution)/shard_map/ppermute | solution.py:601
  325.8 30.9 %collective-permute-start.26 = (bf16[256,2048]{1,0:T(8,128)(2,1)}, bf16[256,2048]{1,0:T(8,128)(2,1)}, u32[]{:S(2)}, u32[]{:S(2)}) collective-permute-start(bf16[256,2048]{1,0:T(8,128)(2,1)} %get-tuple-element.627.refs_2_), channel_id=1, source_target_pairs={{1,2},{2,1},{5,6},{6,5},{9,10},{10,9},{13,14},{14,13},{17,18},{18,... | collective-permute-start | bytes 3145736 | tf_op jit(solution)/shard_map/ppermute | solution.py:604
  340.7 6.8 %collective-permute-start.28 = (bf16[2,64,1152]{2,1,0:T(8,128)(2,1)S(1)}, bf16[2,64,1152]{2,1,0:T(8,128)(2,1)S(1)}, u32[]{:S(2)}, u32[]{:S(2)}) collective-permute-start(bf16[2,64,1152]{2,1,0:T(8,128)(2,1)S(1)} %get-tuple-element.653), channel_id=1, source_target_pairs={{0,16},{4,20},{8,24},{12,28},{16,0},{20,4},{24,8},{28,12},{1,17},{... | collective-permute-start | bytes 884744 | tf_op jit(solution)/shard_map/ppermute | solution.py:521
  362.4 138.0 %reduce-scatter.8.cloned.1.call-start = ((), (), s32[]{:S(2)}) async-start(), calls=%async_computation.5 | async-start | bytes 5640192 | tf_op jit(solution)/shard_map/reduce_scatter | solution.py:976
  362.4 22.2 %collective-permute-start.29 = (bf16[256,2048]{1,0:T(8,128)(2,1)}, bf16[256,2048]{1,0:T(8,128)(2,1)S(1)}, u32[]{:S(2)}, u32[]{:S(2)}) collective-permute-start(bf16[256,2048]{1,0:T(8,128)(2,1)} %get-tuple-element.679.refs_4_), channel_id=1, source_target_pairs={{0,1},{3,2},{1,0},{2,3},{4,5},{7,6},{5,4},{6,7},{8,9},{11,10},{9,8... | collective-permute-start | bytes 3145736 | tf_op jit(solution)/shard_map/ppermute | solution.py:601
  364.2 20.4 %collective-permute-start.30 = (bf16[256,2048]{1,0:T(8,128)(2,1)}, bf16[256,2048]{1,0:T(8,128)(2,1)S(1)}, u32[]{:S(2)}, u32[]{:S(2)}) collective-permute-start(bf16[256,2048]{1,0:T(8,128)(2,1)} %get-tuple-element.680.refs_2_), channel_id=1, source_target_pairs={{1,2},{2,1},{5,6},{6,5},{9,10},{10,9},{13,14},{14,13},{17,18},{18,... | collective-permute-start | bytes 3145736 | tf_op jit(solution)/shard_map/ppermute | solution.py:604
  374.0 10.7 %copy-start.7 = (bf16[256,2048]{1,0:T(8,128)(2,1)S(1)}, bf16[256,2048]{1,0:T(8,128)(2,1)}, u32[]{:S(2)}) copy-start(bf16[256,2048]{1,0:T(8,128)(2,1)} %copy-done.6) | copy-start | bytes 3145732
  388.7 25.3 %collective-permute-start.31 = (bf16[256,2048]{1,0:T(8,128)(2,1)}, bf16[256,2048]{1,0:T(8,128)(2,1)}, u32[]{:S(2)}, u32[]{:S(2)}) collective-permute-start(bf16[256,2048]{1,0:T(8,128)(2,1)} %get-tuple-element.696.refs_4_), channel_id=1, source_target_pairs={{0,1},{3,2},{1,0},{2,3},{4,5},{7,6},{5,4},{6,7},{8,9},{11,10},{9,8... | collective-permute-start | bytes 3145736 | tf_op jit(solution)/shard_map/ppermute | solution.py:601
  392.4 21.6 %collective-permute-start.32 = (bf16[256,2048]{1,0:T(8,128)(2,1)}, bf16[256,2048]{1,0:T(8,128)(2,1)}, u32[]{:S(2)}, u32[]{:S(2)}) collective-permute-start(bf16[256,2048]{1,0:T(8,128)(2,1)} %get-tuple-element.697.refs_2_), channel_id=1, source_target_pairs={{1,2},{2,1},{5,6},{6,5},{9,10},{10,9},{13,14},{14,13},{17,18},{18,... | collective-permute-start | bytes 3145736 | tf_op jit(solution)/shard_map/ppermute | solution.py:604
  402.5 11.6 %copy-start.5 = (bf16[256,2048]{1,0:T(8,128)(2,1)S(1)}, bf16[256,2048]{1,0:T(8,128)(2,1)}, u32[]{:S(2)}) copy-start(bf16[256,2048]{1,0:T(8,128)(2,1)} %copy-done.4) | copy-start | bytes 3145732
  419.4 20.7 %collective-permute-start.33 = (bf16[256,2048]{1,0:T(8,128)(2,1)}, bf16[256,2048]{1,0:T(8,128)(2,1)S(1)}, u32[]{:S(2)}, u32[]{:S(2)}) collective-permute-start(bf16[256,2048]{1,0:T(8,128)(2,1)} %copy-done.28), channel_id=1, source_target_pairs={{0,1},{3,2},{1,0},{2,3},{4,5},{7,6},{5,4},{6,7},{8,9},{11,10},{9,8... | collective-permute-start | bytes 3145736 | tf_op jit(solution)/shard_map/ppermute | solution.py:601
  421.0 19.1 %collective-permute-start.34 = (bf16[256,2048]{1,0:T(8,128)(2,1)}, bf16[256,2048]{1,0:T(8,128)(2,1)S(1)}, u32[]{:S(2)}, u32[]{:S(2)}) collective-permute-start(bf16[256,2048]{1,0:T(8,128)(2,1)} %copy-done.26), channel_id=1, source_target_pairs={{1,2},{2,1},{5,6},{6,5},{9,10},{10,9},{13,14},{14,13},{17,18},{18,... | collective-permute-start | bytes 3145736 | tf_op jit(solution)/shard_map/ppermute | solution.py:604
  424.1 16.1 %copy-start.27 = (bf16[256,2048]{1,0:T(8,128)(2,1)S(1)}, bf16[256,2048]{1,0:T(8,128)(2,1)}, u32[]{:S(2)}) copy-start(bf16[256,2048]{1,0:T(8,128)(2,1)} %copy-done.26) | copy-start | bytes 3145732
  424.1 16.1 %copy-start.29 = (bf16[256,2048]{1,0:T(8,128)(2,1)S(1)}, bf16[256,2048]{1,0:T(8,128)(2,1)}, u32[]{:S(2)}) copy-start(bf16[256,2048]{1,0:T(8,128)(2,1)} %copy-done.28) | copy-start | bytes 3145732
  442.3 9.0 %copy-start.11 = (bf16[256,2048]{1,0:T(8,128)(2,1)S(1)}, bf16[256,2048]{1,0:T(8,128)(2,1)}, u32[]{:S(2)}) copy-start(bf16[256,2048]{1,0:T(8,128)(2,1)} %copy-done.10) | copy-start | bytes 3145732
  442.3 24.1 %collective-permute-start.35 = (bf16[256,2048]{1,0:T(8,128)(2,1)}, bf16[256,2048]{1,0:T(8,128)(2,1)S(1)}, u32[]{:S(2)}, u32[]{:S(2)}) collective-permute-start(bf16[256,2048]{1,0:T(8,128)(2,1)} %copy-done.16), channel_id=1, source_target_pairs={{0,1},{3,2},{1,0},{2,3},{4,5},{7,6},{5,4},{6,7},{8,9},{11,10},{9,8... | collective-permute-start | bytes 3145736 | tf_op jit(solution)/shard_map/ppermute | solution.py:601
  446.1 20.2 %collective-permute-start.36 = (bf16[256,2048]{1,0:T(8,128)(2,1)S(1)}, bf16[256,2048]{1,0:T(8,128)(2,1)S(1)}, u32[]{:S(2)}, u32[]{:S(2)}) collective-permute-start(bf16[256,2048]{1,0:T(8,128)(2,1)S(1)} %get-tuple-element.757.refs_2_), channel_id=1, source_target_pairs={{1,2},{2,1},{5,6},{6,5},{9,10},{10,9},{13,14},{14,13},{17,18},{18,... | collective-permute-start | bytes 3145736 | tf_op jit(solution)/shard_map/ppermute | solution.py:604
  453.5 12.9 %copy-start.17 = (bf16[256,2048]{1,0:T(8,128)(2,1)S(1)}, bf16[256,2048]{1,0:T(8,128)(2,1)}, u32[]{:S(2)}) copy-start(bf16[256,2048]{1,0:T(8,128)(2,1)} %copy-done.16) | copy-start | bytes 3145732
  455.8 14.9 %copy-start.47 = (bf16[1,2,256,1408]{3,2,1,0:T(8,128)(2,1)S(1)}, bf16[1,2,256,1408]{3,2,1,0:T(8,128)(2,1)}, u32[]{:S(2)}) copy-start(bf16[1,2,256,1408]{3,2,1,0:T(8,128)(2,1)} %reduce-scatter.4.cloned.1.call-done) | copy-start | bytes 4325380
  468.5 25.7 %collective-permute-start.37 = (bf16[256,2048]{1,0:T(8,128)(2,1)}, bf16[256,2048]{1,0:T(8,128)(2,1)S(1)}, u32[]{:S(2)}, u32[]{:S(2)}) collective-permute-start(bf16[256,2048]{1,0:T(8,128)(2,1)} %get-tuple-element.767.refs_3_), channel_id=1, source_target_pairs={{1,0},{2,3},{5,4},{6,7},{9,8},{10,11},{13,12},{14,15},{17,16},{18,... | collective-permute-start | bytes 3145736 | tf_op jit(solution)/shard_map/ppermute | solution.py:601
  469.9 24.3 %collective-permute-start.38 = (bf16[256,2048]{1,0:T(8,128)(2,1)S(1)}, bf16[256,2048]{1,0:T(8,128)(2,1)S(1)}, u32[]{:S(2)}, u32[]{:S(2)}) collective-permute-start(bf16[256,2048]{1,0:T(8,128)(2,1)S(1)} %get-tuple-element.768.refs_1_), channel_id=1, source_target_pairs={{1,2},{2,1},{5,6},{6,5},{9,10},{10,9},{13,14},{14,13},{17,18},{18,... | collective-permute-start | bytes 3145736 | tf_op jit(solution)/shard_map/ppermute | solution.py:604
  477.8 16.4 %copy-start.31 = (bf16[256,2048]{1,0:T(8,128)(2,1)S(1)}, bf16[256,2048]{1,0:T(8,128)(2,1)}, u32[]{:S(2)}) copy-start(bf16[256,2048]{1,0:T(8,128)(2,1)} %copy-done.30) | copy-start | bytes 3145732
  496.5 25.4 %collective-permute-start.39 = (bf16[256,2048]{1,0:T(8,128)(2,1)S(1)}, bf16[256,2048]{1,0:T(8,128)(2,1)S(1)}, u32[]{:S(2)}, u32[]{:S(2)}) collective-permute-start(bf16[256,2048]{1,0:T(8,128)(2,1)S(1)} %get-tuple-element.775.refs_1_), channel_id=1, source_target_pairs={{1,0},{2,3},{5,4},{6,7},{9,8},{10,11},{13,12},{14,15},{17,16},{18,... | collective-permute-start | bytes 3145736 | tf_op jit(solution)/shard_map/ppermute | solution.py:601
  500.4 7.5 %copy-start.46 = (f32[256,1024]{1,0:T(8,128)S(1)}, f32[256,1024]{1,0:T(8,128)}, u32[]{:S(2)}) copy-start(f32[256,1024]{1,0:T(8,128)} %slice_convert_fusion) | copy-start | bytes 3145732
  502.5 10.0 %copy-start.33 = (bf16[256,2048]{1,0:T(8,128)(2,1)S(1)}, bf16[256,2048]{1,0:T(8,128)(2,1)}, u32[]{:S(2)}) copy-start(bf16[256,2048]{1,0:T(8,128)(2,1)} %copy-done.32) | copy-start | bytes 3145732
  502.5 13.2 %collective-permute-start.42 = (f32[256]{0:T(256)S(1)}, f32[256]{0:T(256)S(1)}, u32[]{:S(2)}, u32[]{:S(2)}) collective-permute-start(f32[256]{0:T(256)S(1)} %get-tuple-element.823), channel_id=1, source_target_pairs={{0,3},{1,2},{2,1},{3,0},{4,7},{5,6},{6,5},{7,4},{8,11},{9,10},{10,... | collective-permute-start | bytes 3080 | tf_op jit(solution)/shard_map/ppermute | solution.py:997
  505.8 9.9 %collective-permute-start.41 = (f32[256]{0:T(256)S(1)}, f32[256]{0:T(256)S(1)}, u32[]{:S(2)}, u32[]{:S(2)}) collective-permute-start(f32[256]{0:T(256)S(1)} %get-tuple-element.823), channel_id=1, source_target_pairs={{0,2},{1,3},{2,0},{3,1},{4,6},{5,7},{6,4},{7,5},{8,10},{9,11},{10,... | collective-permute-start | bytes 3080 | tf_op jit(solution)/shard_map/ppermute | solution.py:997
  507.6 13.7 %collective-permute-start.40 = (f32[256]{0:T(256)S(1)}, f32[256]{0:T(256)S(1)}, u32[]{:S(2)}, u32[]{:S(2)}) collective-permute-start(f32[256]{0:T(256)S(1)} %get-tuple-element.823), channel_id=1, source_target_pairs={{0,1},{1,0},{2,3},{3,2},{4,5},{5,4},{6,7},{7,6},{8,9},{9,8},{10,11... | collective-permute-start | bytes 3080 | tf_op jit(solution)/shard_map/ppermute | solution.py:997
  (34 other events, 66.9 us)
Sparse Core Ops, SparseCore 0:
  27.0 98.0 all-gather.2
  255.8 87.7 reduce-scatter.3
  362.5 78.6 reduce-scatter.5
  444.6 55.7 reduce-scatter.7

commit v10 on v9

--- a/solution.py
+++ b/solution.py
@@ -109,7 +109,15 @@
 
 
 def project_kernel(per_part, x_ref, gain_ref, wk_ref, wv_ref, wf_ref, bias_ref,
-                   xn_ref, k_ref, v_ref, z_ref, cum_ref, in_ref, s_ref, d_ref, sent_ref, state, decay):
+                   xn_ref, k_ref, v_ref, z_ref, cum_ref, in_ref, s_ref, d_ref, sent_ref, state, decay, wk, wv, sems):
+    first = pl.program_id(0) == 0
+    loads = [pltpu.make_async_copy(wk_ref, wk, sems.at[0]), pltpu.make_async_copy(wv_ref, wv, sems.at[1])]
+
+    @pl.when(first)
+    def _():
+        for load in loads:
+            load.start()
+
     @pl.when(lax.rem(pl.program_id(0), per_part) == 0)
     def _():
         state[...] = jnp.zeros_like(state)
@@ -119,8 +127,14 @@
     r1 = lax.rsqrt(jnp.mean(x * x, axis=-1, keepdims=True) + EPS)
     xn = (x * r1 * gain_ref[...]).astype(bf16)
     xn_ref[...] = xn
-    k_ref[...] = nn(xn, wk_ref[...]).astype(bf16)
-    v_ref[...] = nn(xn, wv_ref[...]).astype(bf16)
+
+    @pl.when(first)
+    def _():
+        for load in loads:
+            load.wait()
+
+    k_ref[...] = nn(xn, wk[...]).astype(bf16)
+    v_ref[...] = nn(xn, wv[...]).astype(bf16)
     z_ref[...] = nt(xn, wf_ref[...]) + bias_ref[...]
     width = k_ref.shape[1]
     for c in range(x_ref.shape[0] // CHUNK):
@@ -143,9 +157,14 @@
     q_ref[...] = nn(xn_ref[...], wq_ref[...]).astype(bf16)
 
 
-def read_kernel(q_ref, k_ref, v_ref, cum_ref, in_ref, e0_ref, wo_ref, o_ref, p_ref, sc_ref, e_ref, left_ref, att_ref, state):
-    @pl.when(pl.program_id(0) == 0)
-    def _():
+def read_kernel(q_ref, k_ref, v_ref, cum_ref, in_ref, e0_ref, wo_ref, o_ref, p_ref, sc_ref, e_ref, left_ref, att_ref,
+                state, wo, sem):
+    first = pl.program_id(0) == 0
+    load = pltpu.make_async_copy(wo_ref, wo, sem.at[0])
+
+    @pl.when(first)
+    def _():
+        load.start()
         state[...] = e0_ref[...]
 
     width = q_ref.shape[1]
@@ -165,7 +184,12 @@
     mixing = jnp.where(lower, nt(w, i_hi), 0.0).astype(bf16)
     o = (nn(w, state[:, width:].astype(bf16)) + nn(mixing, v)).astype(bf16)
     o_ref[...] = o
-    att_ref[...] = nn(o, wo_ref[...]).astype(bf16)
+
+    @pl.when(first)
+    def _():
+        load.wait()
+
+    att_ref[...] = nn(o, wo[...]).astype(bf16)
     p_ref[...] = p
     sc_ref[...] = scores
     keep = jnp.exp(total[:, :1])
@@ -175,11 +199,14 @@
 
 
 def back_kernel(dhn_ref, hid_ref, cot_ref, gain_ref, wo_ref, q_ref, k_ref, v_ref, cum_ref, in_ref, p_ref, sc_ref,
-                e_ref, datt_ref, dq_ref, dkl_ref, dvl_ref, h_ref, x1_ref, g_ref, s_ref, d_ref, gg_ref, state, decay):
+                e_ref, datt_ref, dq_ref, dkl_ref, dvl_ref, h_ref, x1_ref, g_ref, s_ref, d_ref, gg_ref, state, decay,
+                wo, sem):
     step = pl.program_id(0)
+    load = pltpu.make_async_copy(wo_ref, wo, sem.at[0])
 
     @pl.when(step == 0)
     def _():
+        load.start()
         state[...] = jnp.zeros_like(state)
         decay[...] = jnp.zeros_like(decay)
         gg_ref[...] = jnp.zeros_like(gg_ref)
@@ -197,7 +224,12 @@
     datt = dhid.astype(bf16)
     datt_ref[...] = datt
     width = q_ref.shape[1]
-    do = nt(datt, wo_ref[...]).astype(bf16)
+
+    @pl.when(step == 0)
+    def _():
+        load.wait()
+
+    do = nt(datt, wo[...]).astype(bf16)
     lower, upper = triangle(True), triangle(False)
     q, k, v = q_ref[...], k_ref[...], v_ref[...]
     cum, inflow = cum_ref[...], in_ref[...]
@@ -656,13 +688,13 @@
         "project",
         functools.partial(project_kernel, per_part),
         (rows // TILE,),
-        [all_rows(width), fixed((1, width))] + [fixed((width, head))] * 2 + [fixed((slots, width)), fixed((1, slots))],
+        [all_rows(width), fixed((1, width))] + [anywhere] * 2 + [fixed((slots, width)), fixed((1, slots))],
         [all_rows(width), all_rows(head), all_rows(head)] + [all_rows(slots)] * 3
         + [by_part(2 * head), by_part(128), by_part(2 * head + 128)],
         [shaped((rows, width), bf16)] + [shaped((rows, head), bf16)] * 2
         + [shaped((rows, slots), f32)] * 3 + [shaped((parts, slots, 2 * head), f32), shaped((parts, slots, 128), f32),
                                              shaped((parts, slots, 2 * head + 128), bf16)],
-        [state_scratch, decay_scratch],
+        [state_scratch, decay_scratch] + [pltpu.VMEM((width, head), bf16)] * 2 + [pltpu.SemaphoreType.DMA((2,))],
         cost=cost(2 * rows * width * (2 * head + slots), 2 * rows * width * 3 + 2 * width * 2 * head),
         loose_out=(6, 7, 8),
     )(x, gain1, w_key, w_value, forget_rows, forget_bias.reshape(1, slots))
@@ -709,12 +741,12 @@
             read_kernel,
             (chunks,),
             [chunk_rows(m, t, head, False)] * 3 + [chunk_rows(m, t, slots, False)] * 2
-            + [state_of(which), fixed((head, width))],
+            + [state_of(which), anywhere],
             [own_rows(head, False), own_rows(slots, False), own_rows(slots, False), chunk_state(False),
              pl.BlockSpec((None, slots, 2 * head), lambda i: (0, 0, 0)), own_rows(width, False)],
             [shaped((TILE, head), bf16), shaped((TILE, slots), f32), shaped((TILE, slots), f32), states_shape,
              shaped((1, slots, 2 * head), f32), shaped((TILE, width), bf16)],
-            [state_scratch],
+            [state_scratch, pltpu.VMEM((head, width), bf16), pltpu.SemaphoreType.DMA((1,))],
             cost=cost(2 * TILE * head * (600 + width), 2 * TILE * (head * 4 + width) + 2 * head * width),
             loose=(5,),
             loose_out=(4, 5),
@@ -774,7 +806,7 @@
             back_kernel,
             (chunks,),
             [own_rows(width, True), own_rows(width, True), chunk_rows(m, t, width, True), fixed((1, width)),
-             fixed((head, width))]
+             anywhere]
             + [chunk_rows(m, t, head, True)] * 3 + [chunk_rows(m, t, slots, True)] * 2 + [own_rows(slots, True)] * 2
             + [chunk_state(True)],
             [own_rows(width, True)] + [own_rows(head, True)] * 3 + [own_rows(slots, True)] * 2
@@ -783,7 +815,7 @@
              shaped((TILE, head), f32), shaped((TILE, head), f32), shaped((TILE, slots), f32),
              shaped((TILE, slots), f32), states_shape, shaped((slots, 2 * head), f32), shaped((slots, 128), f32),
              shaped((8, width), f32)],
-            [state_scratch, decay_scratch],
+            [state_scratch, decay_scratch, pltpu.VMEM((head, width), bf16), pltpu.SemaphoreType.DMA((1,))],
             cost=cost(2 * TILE * width * head + 2 * TILE * head * 1500, TILE * width * 14 + TILE * head * 20),
             loose=(0,),
             loose_out=(7, 8),
@@ -826,15 +858,16 @@
 
     reads, backs, lasts = {}, {}, {}
     outs, in_grads = [None], [None]
-    eighth = TILE // 2
+    blocks = 4
+    eighth = TILE // blocks
 
     def into(name, kernel, m, t, kept, dtype, inputs, specs):
-        spec = pl.BlockSpec((1, eighth, width), lambda i: (m, 2 * t + i, 0))
+        spec = pl.BlockSpec((1, eighth, width), lambda i: (m, blocks * t + i, 0))
         old = [] if kept[0] is None else [kept[0]]
         kept[0] = call(
             name,
             kernel,
-            (2,),
+            (blocks,),
             specs + [anywhere] * len(old),
             spec,
             shaped(tokens.shape, dtype),
@@ -850,7 +883,7 @@
              [piece_spec, piece_spec])
 
     def finish_grad(m, t):
-        x_rows = pl.BlockSpec((eighth, width), lambda i: (2 * (m * pieces + t) + i, 0))
+        x_rows = pl.BlockSpec((eighth, width), lambda i: (blocks * (m * pieces + t) + i, 0))
         into("in_grad", in_grad_kernel, m, t, in_grads, f32, [backs[m, t][0], live.pop(("dxn", m, t)), x, gain1],
              [piece_spec, piece_spec, x_rows, pl.BlockSpec((1, width), lambda i: (0, 0))])
 

time: 540 us -> 547 us (1.013)
  the two profiles are of different devices: /device:TPU:4 before, /device:TPU:0 now
where the time goes in v10:
time: 547 us; the launch traced here: 536 us
  Pallas kernels  303 us (55%)
  waiting for transfers between devices  93.3 us (17%)
  starting transfers between devices  84.4 us (15%)
  local copies, waits for them, and re-layouts  30.6 us (6%)
  between operations  14.9 us (3%)
  other arithmetic  10.3 us (2%)
    pallas_call x30, Pallas kernels, run(): function(*[o if i in loose or spec.memory_space == pltpu.SMEM else pltpu....  280 us
    ppermute x18, waiting for transfers between devices, step(): outer = lax.ppermute(payload, 'head', way)  68.7 us
    ppermute x18, starting transfers between devices, step(): outer = lax.ppermute(payload, 'head', way)  52.6 us
    unnamed x105, local copies, waits for them, and re-layouts  28.1 us
    pallas_call x25, Pallas kernels, in_vmem(): pl.pallas_call(kernel, name=name, in_specs=[pl.BlockSpec(memory_space=plt...  22.4 us
    ppermute x6, waiting for transfers between devices, scan_states(): got = lax.ppermute(sent, 'seq', [(i, i ^ bit) for i in range(n)])  22.3 us
    ppermute x16, starting transfers between devices, step(): middle = lax.ppermute(pair, 'head', self.MIDDLE)  16.9 us
  transfers between devices with their start and end apart: 47, of which 13 were waited for; matrix products, arithmetic and copies ran while one was open for 3% of the time, Pallas kernels for 52%

profile of v10, /device:TPU:0, one launch (start us, length us, event | category | flops | bytes accessed | tf_op | source)
XLA Modules:
  0.0 536.0 jit_solution(16440581616483977180)
XLA Ops:
  7.2 16.3 %project.1 = (bf16[1024,2048]{1,0:T(8,128)(2,1)}, bf16[1024,512]{1,0:T(8,128)(2,1)}, bf16[1024,512]{1,0:T(8,128)(2,1)}, f32[1024,64]{1,0:T(8,128)}, f32[1024,64]...) custom-call(bf16[1024,2048]{1,0:T(8,128)(2,1)} %bitcast.35, ...), custom_call_target="tpu_custom_call" | custom-call | flops 4563402752 | bytes 16777216 | tf_op jit(solution)/shard_map/project/pallas_call | solution.py:62
  25.7 2.7 pad_maximum_fusion
  28.7 2.9 collective-permute-start.1
  31.6 7.3 %collective-permute-done.1.refs_2_ = bf16[2,64,1152]{2,1,0:T(8,128)(2,1)S(1)} collective-permute-done((bf16[2,64,1152]{2,1,0:T(8,128)(2,1)S(1)}, bf16[2,64,1152]{2,1,0:T(8,128)(2,1)S(1)}, u32[]{:S(2)}, u32[]{:S(2)}) %collective-permute-start.1) | collective-permute-done | bytes 294944 | tf_op jit(solution)/shard_map/ppermute | solution.py:553
  41.1 6.7 %query.1.q_ref = bf16[1024,512]{1,0:T(8,128)(2,1)} custom-call(bf16[1024,2048]{1,0:T(8,128)(2,1)} %get-tuple-element.715.xn_ref.refs_0_, bf16[2048,512]{1,0:T(8,128)(2,1)} %wq_ref.9), custom_call_target="tpu_custom_call" | custom-call | flops 2147483648 | bytes 7340032 | tf_op jit(solution)/shard_map/query/pallas_call | solution.py:62
  47.8 5.8 %collective-permute-done.2.refs_2_ = bf16[2,64,1152]{2,1,0:T(8,128)(2,1)S(1)} collective-permute-done((bf16[2,64,1152]{2,1,0:T(8,128)(2,1)S(1)}, bf16[2,64,1152]{2,1,0:T(8,128)(2,1)S(1)}, u32[]{:S(2)}, u32[]{:S(2)}) %collective-permute-start.2) | collective-permute-done | bytes 294944 | tf_op jit(solution)/shard_map/ppermute | solution.py:553
  53.8 5.0 read.4
  58.9 3.8 collective-permute-start.3
  62.7 5.4 read.5
  68.1 13.5 %collective-permute-done.3.refs_1_ = bf16[256,2048]{1,0:T(8,128)(2,1)S(1)} collective-permute-done((bf16[256,2048]{1,0:T(8,128)(2,1)S(1)}, bf16[256,2048]{1,0:T(8,128)(2,1)S(1)}, u32[]{:S(2)}, u32[]{:S(2)}) %collective-permute-start.3) | collective-permute-done | bytes 1048608 | tf_op jit(solution)/shard_map/ppermute | solution.py:633
  81.6 4.5 collective-permute-start.4
  86.9 4.9 read.6
  91.8 12.8 %collective-permute-done.4.refs_1_ = bf16[256,2048]{1,0:T(8,128)(2,1)S(1)} collective-permute-done((bf16[256,2048]{1,0:T(8,128)(2,1)S(1)}, bf16[256,2048]{1,0:T(8,128)(2,1)S(1)}, u32[]{:S(2)}, u32[]{:S(2)}) %collective-permute-start.4) | collective-permute-done | bytes 1048608 | tf_op jit(solution)/shard_map/ppermute | solution.py:633
  104.7 4.0 collective-permute-start.6
  109.4 5.5 %read.7 = (bf16[256,512]{1,0:T(8,128)(2,1)}, f32[256,64]{1,0:T(8,128)}, f32[256,64]{1,0:T(8,128)}, f32[2,64,1024]{2,1,0:T(8,128)}, f32[1,64,1024]{2,1,0:T(8,128)}, /*index=5*/bf16[256,2048]{1,0:T(8,128)(2,1)S(1)}) custom-call(bf16[1024,512]{1,0:T(8,128)(2,1)} %query.1.q_ref, bf16[1024,512]{1,0:T(8,128)(2,1)} %get-tuple-element.399.k_ref, ...), custom_call_target="tpu_custom_call" | custom-call | flops 694157312 | bytes 4194304 | tf_op jit(solution)/shard_map/read/pallas_call | solution.py:62
  114.9 11.9 %collective-permute-done.6.refs_1_ = bf16[256,2048]{1,0:T(8,128)(2,1)S(1)} collective-permute-done((bf16[256,2048]{1,0:T(8,128)(2,1)S(1)}, bf16[256,2048]{1,0:T(8,128)(2,1)S(1)}, u32[]{:S(2)}, u32[]{:S(2)}) %collective-permute-start.6) | collective-permute-done | bytes 1048608 | tf_op jit(solution)/shard_map/ppermute | solution.py:633
  128.0 4.0 collective-permute-start.8
  135.1 19.5 %feed.4 = (bf16[256,2048]{1,0:T(8,128)(2,1)}, bf16[256,2048]{1,0:T(8,128)(2,1)}, bf16[256,1408]{1,0:T(8,128)(2,1)}, bf16[256,1408]{1,0:T(8,128)(2,1)}, bf16[256,...) custom-call(bf16[1024,2048]{1,0:T(8,128)(2,1)} %bitcast.36, ...), custom_call_target="tpu_custom_call" | custom-call | flops 8858370048 | bytes 24641536 | tf_op jit(solution)/shard_map/feed/pallas_call | solution.py:62
  156.2 2.3 collective-permute-start.10
  159.7 19.5 %feed.5 = (bf16[256,2048]{1,0:T(8,128)(2,1)}, bf16[256,2048]{1,0:T(8,128)(2,1)}, bf16[256,1408]{1,0:T(8,128)(2,1)}, bf16[256,1408]{1,0:T(8,128)(2,1)}, bf16[256,...) custom-call(bf16[1024,2048]{1,0:T(8,128)(2,1)} %bitcast.37, ...), custom_call_target="tpu_custom_call" | custom-call | flops 8858370048 | bytes 24641536 | tf_op jit(solution)/shard_map/feed/pallas_call | solution.py:62
  179.3 3.0 collective-permute-start.12
  183.2 19.4 %feed.6 = (bf16[256,2048]{1,0:T(8,128)(2,1)}, bf16[256,2048]{1,0:T(8,128)(2,1)}, bf16[256,1408]{1,0:T(8,128)(2,1)}, bf16[256,1408]{1,0:T(8,128)(2,1)}, bf16[256,...) custom-call(bf16[1024,2048]{1,0:T(8,128)(2,1)} %bitcast.38, ...), custom_call_target="tpu_custom_call" | custom-call | flops 8858370048 | bytes 24641536 | tf_op jit(solution)/shard_map/feed/pallas_call | solution.py:62
  202.9 2.5 collective-permute-start.14
  206.3 19.5 %feed.7 = (bf16[256,2048]{1,0:T(8,128)(2,1)}, bf16[256,2048]{1,0:T(8,128)(2,1)}, bf16[256,1408]{1,0:T(8,128)(2,1)}, bf16[256,1408]{1,0:T(8,128)(2,1)}, bf16[256,...) custom-call(bf16[1024,2048]{1,0:T(8,128)(2,1)} %bitcast.39, ...), custom_call_target="tpu_custom_call" | custom-call | flops 8858370048 | bytes 24641536 | tf_op jit(solution)/shard_map/feed/pallas_call | solution.py:62
  227.3 2.4 collective-permute-start.16
  231.4 19.0 %wide_grads.1 = bf16[8,2,256,1408]{3,2,1,0:T(8,128)(2,1)} custom-call(bf16[256,2048]{1,0:T(8,128)(2,1)} %get-tuple-element.545.refs_0_, bf16[256,2048]{1,0:T(8,128)(2,1)} %get-tuple-element.546.refs_1_, bf16[256,2048]{1,0:T(8,128)(2,1)} %get-tuple-element.547.refs_2_, bf16[256,2048]{1,0:T(8,128)(2,1)} %get-tuple-element.548.refs_3_, ...), custom_call_target="tpu_custom_call" | custom-call | flops 11811160064 | bytes 21495808 | tf_op jit(solution)/shard_map/wide_grads/pallas_call | solution.py:62
  250.4 2.3 join.25
  258.6 9.4 %back.4 = (bf16[256,2048]{1,0:T(8,128)(2,1)}, bf16[256,512]{1,0:T(8,128)(2,1)}, f32[256,512]{1,0:T(8,128)}, f32[256,512]{1,0:T(8,128)}, f32[256,64]{1,0:T(8,128)...) custom-call(bf16[256,2048]{1,0:T(8,128)(2,1)S(1)} %get-tuple-element, ...), custom_call_target="tpu_custom_call" | custom-call | flops 930086912 | bytes 9961472 | tf_op jit(solution)/shard_map/back/pallas_call | solution.py:62
  268.1 11.4 %back.5 = (bf16[256,2048]{1,0:T(8,128)(2,1)}, bf16[256,512]{1,0:T(8,128)(2,1)}, f32[256,512]{1,0:T(8,128)}, f32[256,512]{1,0:T(8,128)}, f32[256,64]{1,0:T(8,128)...) custom-call(bf16[256,2048]{1,0:T(8,128)(2,1)S(1)} %copy-done.15, ...), custom_call_target="tpu_custom_call" | custom-call | flops 930086912 | bytes 9961472 | tf_op jit(solution)/shard_map/back/pallas_call | solution.py:62
  279.7 3.6 collective-permute-start.20
  284.0 9.8 %back.6 = (bf16[256,2048]{1,0:T(8,128)(2,1)}, bf16[256,512]{1,0:T(8,128)(2,1)}, f32[256,512]{1,0:T(8,128)}, f32[256,512]{1,0:T(8,128)}, f32[256,64]{1,0:T(8,128)...) custom-call(bf16[256,2048]{1,0:T(8,128)(2,1)S(1)} %get-tuple-element, ...), custom_call_target="tpu_custom_call" | custom-call | flops 930086912 | bytes 9961472 | tf_op jit(solution)/shard_map/back/pallas_call | solution.py:62
  293.8 10.8 %down_grads.1.refs_13_ = bf16[8,256,2432]{2,1,0:T(8,128)(2,1)} custom-call(bf16[1024,2048]{1,0:T(8,128)(2,1)} %bitcast.55, bf16[256,1408]{1,0:T(8,128)(2,1)} %get-tuple-element.599.refs_1_, bf16[256,1408]{1,0:T(8,128)(2,1)} %get-tuple-element.600.refs_2_, bf16[256,1408]{1,0:T(8,128)(2,1)} %get-tuple-element.601.refs_3_, ...), custom_call_target="tpu_custom_call" | custom-call | flops 5905580032 | bytes 12845056 | tf_op jit(solution)/shard_map/down_grads/pallas_call | solution.py:62
  304.7 2.3 collective-permute-start.23
  307.8 9.4 %back.7 = (bf16[256,2048]{1,0:T(8,128)(2,1)}, bf16[256,512]{1,0:T(8,128)(2,1)}, f32[256,512]{1,0:T(8,128)}, f32[256,512]{1,0:T(8,128)}, f32[256,64]{1,0:T(8,128)...) custom-call(bf16[256,2048]{1,0:T(8,128)(2,1)S(1)} %get-tuple-element, ...), custom_call_target="tpu_custom_call" | custom-call | flops 930086912 | bytes 9961472 | tf_op jit(solution)/shard_map/back/pallas_call | solution.py:62
  325.2 3.9 collective-permute-start.25
  330.9 11.1 %query_grads.1 = bf16[8,256,2432]{2,1,0:T(8,128)(2,1)} custom-call(bf16[1024,2048]{1,0:T(8,128)(2,1)} %get-tuple-element.715.xn_ref.refs_0_, bf16[256,2048]{1,0:T(8,128)(2,1)} %get-tuple-element.633.refs_1_.dhid_ref, bf16[256,2048]{1,0:T(8,128)(2,1)} %get-tuple-element.634.refs_2_.dhid_ref, ...), custom_call_target="tpu_custom_call", output_to_operand_aliasing={{}: (13, {})} | custom-call | flops 12884901888 | bytes 44040192 | tf_op jit(solution)/shard_map/query_grads/pallas_call | solution.py:62
  343.9 2.7 collective-permute-start.28
  346.6 6.4 %collective-permute-done.28.refs_2_ = bf16[2,64,1152]{2,1,0:T(8,128)(2,1)S(1)} collective-permute-done((bf16[2,64,1152]{2,1,0:T(8,128)(2,1)S(1)}, bf16[2,64,1152]{2,1,0:T(8,128)(2,1)S(1)}, u32[]{:S(2)}, u32[]{:S(2)}) %collective-permute-start.28) | collective-permute-done | bytes 294944 | tf_op jit(solution)/shard_map/ppermute | solution.py:553
  354.2 8.1 %last.4 = (bf16[256,512]{1,0:T(8,128)(2,1)}, bf16[256,512]{1,0:T(8,128)(2,1)}, bf16[256,64]{1,0:T(8,128)(2,1)}, bf16[256,2048]{1,0:T(8,128)(2,1)S(1)}, f32[8,64]{1,0:T(8,128)}, /*index=5*/f32[8,2048]{1,0:T(8,128)}) custom-call(f32[4,64,1024]{2,1,0:T(8,128)S(1)} %hop.11.l0_ref, bf16[1024,512]{1,0:T(8,128)(2,1)} %get-tuple-element.399.k_ref, ...), custom_call_target="tpu_custom_call" | custom-call | flops 1677721600 | bytes 13107200 | tf_op jit(solution)/shard_map/last/pallas_call | solution.py:62
  362.3 3.7 join.29
  369.9 8.8 %last.6 = (bf16[256,512]{1,0:T(8,128)(2,1)}, bf16[256,512]{1,0:T(8,128)(2,1)}, bf16[256,64]{1,0:T(8,128)(2,1)}, bf16[256,2048]{1,0:T(8,128)(2,1)S(1)}, f32[8,64]{1,0:T(8,128)}, /*index=5*/f32[8,2048]{1,0:T(8,128)}) custom-call(f32[4,64,1024]{2,1,0:T(8,128)S(1)} %hop.11.l0_ref, bf16[1024,512]{1,0:T(8,128)(2,1)} %get-tuple-element.399.k_ref, ...), custom_call_target="tpu_custom_call" | custom-call | flops 1677721600 | bytes 13107200 | tf_op jit(solution)/shard_map/last/pallas_call | solution.py:62
  378.7 9.7 %last.5 = (bf16[256,512]{1,0:T(8,128)(2,1)}, bf16[256,512]{1,0:T(8,128)(2,1)}, bf16[256,64]{1,0:T(8,128)(2,1)}, bf16[256,2048]{1,0:T(8,128)(2,1)S(1)}, f32[8,64]{1,0:T(8,128)}, /*index=5*/f32[8,2048]{1,0:T(8,128)}) custom-call(f32[4,64,1024]{2,1,0:T(8,128)S(1)} %hop.11.l0_ref, bf16[1024,512]{1,0:T(8,128)(2,1)} %get-tuple-element.399.k_ref, ...), custom_call_target="tpu_custom_call" | custom-call | flops 1677721600 | bytes 13107200 | tf_op jit(solution)/shard_map/last/pallas_call | solution.py:62
  388.5 3.5 collective-permute-done.29.refs_1_
  391.9 3.1 join.30
  396.0 3.7 collective-permute-start.31
  401.4 8.2 %last.7 = (bf16[256,512]{1,0:T(8,128)(2,1)}, bf16[256,512]{1,0:T(8,128)(2,1)}, bf16[256,64]{1,0:T(8,128)(2,1)}, bf16[256,2048]{1,0:T(8,128)(2,1)S(1)}, f32[8,64]{1,0:T(8,128)}, /*index=5*/f32[8,2048]{1,0:T(8,128)}) custom-call(f32[4,64,1024]{2,1,0:T(8,128)S(1)} %hop.11.l0_ref, bf16[1024,512]{1,0:T(8,128)(2,1)} %get-tuple-element.399.k_ref, ...), custom_call_target="tpu_custom_call" | custom-call | flops 1677721600 | bytes 13107200 | tf_op jit(solution)/shard_map/last/pallas_call | solution.py:62
  409.6 11.8 %state_grads.1 = bf16[8,272,1152]{2,1,0:T(8,128)(2,1)} custom-call(bf16[1024,2048]{1,0:T(8,128)(2,1)} %get-tuple-element.715.xn_ref.refs_0_, bf16[256,512]{1,0:T(8,128)(2,1)} %get-tuple-element.716.refs_1_, bf16[256,512]{1,0:T(8,128)(2,1)} %get-tuple-element.717.refs_2_, bf16[256,512]{1,0:T(8,128)(2,1)} %get-tuple-element.718.refs_3_, ...), custom_call_target="tpu_custom_call" | custom-call | flops 4294967296 | bytes 10485760 | tf_op jit(solution)/shard_map/state_grads/pallas_call | solution.py:62
  421.5 2.3 join.31
  426.8 3.2 collective-permute-start.33
  430.9 3.5 out.4.refs_0_
  434.4 3.6 out.5.refs_0_
  438.0 12.0 %collective-permute-done.33.refs_1_ = bf16[256,2048]{1,0:T(8,128)(2,1)S(1)} collective-permute-done((bf16[256,2048]{1,0:T(8,128)(2,1)}, bf16[256,2048]{1,0:T(8,128)(2,1)S(1)}, u32[]{:S(2)}, u32[]{:S(2)}) %collective-permute-start.33) | collective-permute-done | bytes 1048608 | tf_op jit(solution)/shard_map/ppermute | solution.py:633
  452.1 3.9 collective-permute-start.35
  458.2 4.2 in_grad.4.refs_0_
  462.4 3.6 out.6.refs_0_
  466.0 3.5 out.7
  469.5 5.4 %collective-permute-done.35.refs_1_ = bf16[256,2048]{1,0:T(8,128)(2,1)S(1)} collective-permute-done((bf16[256,2048]{1,0:T(8,128)(2,1)}, bf16[256,2048]{1,0:T(8,128)(2,1)S(1)}, u32[]{:S(2)}, u32[]{:S(2)}) %collective-permute-start.35) | collective-permute-done | bytes 1048608 | tf_op jit(solution)/shard_map/ppermute | solution.py:633
  482.3 2.9 copy.48
  486.4 4.3 in_grad.5.refs_0_
  490.7 9.6 %collective-permute-done.37.refs_0_ = bf16[256,2048]{1,0:T(8,128)(2,1)S(1)} collective-permute-done((bf16[256,2048]{1,0:T(8,128)(2,1)}, bf16[256,2048]{1,0:T(8,128)(2,1)S(1)}, u32[]{:S(2)}, u32[]{:S(2)}) %collective-permute-start.37) | collective-permute-done | bytes 1048608 | tf_op jit(solution)/shard_map/ppermute | solution.py:633
  508.1 2.6 collective-permute-start.42
  510.7 2.5 collective-permute-start.41
  518.0 4.2 in_grad.6.refs_0_
  525.0 4.2 in_grad.7
  (205 shorter events, 77.8 us)
Async XLA Ops:
  7.2 126.6 %all-gather.3.cloned.1.call-start = ((), (), s32[]{:S(2)}) async-start(), calls=%async_computation.6 | async-start | bytes 19464192 | tf_op jit(solution)/shard_map/all_gather | solution.py:718
  7.2 18.1 %copy-start.49 = (bf16[1408,256]{1,0:T(8,128)(2,1)S(1)}, bf16[1408,256]{1,0:T(8,128)(2,1)}, u32[]{:S(2)}) copy-start(bf16[1408,256]{1,0:T(8,128)(2,1)} %param.24) | copy-start | bytes 2162692
  7.2 18.4 %copy-start.50 = (bf16[256,1408]{1,0:T(8,128)(2,1)S(1)}, bf16[256,1408]{1,0:T(8,128)(2,1)}, u32[]{:S(2)}) copy-start(bf16[256,1408]{1,0:T(8,128)(2,1)} %param.23) | copy-start | bytes 2162692
  23.6 1.7 collective-permute-start
  28.4 339.5 %reduce-scatter.4.cloned.1.call-start = ((), (), s32[]{:S(2)}) async-start(), calls=%async_computation.3 | async-start | bytes 12976128 | tf_op jit(solution)/shard_map/reduce_scatter | solution.py:935
  28.7 10.2 %collective-permute-start.1 = (bf16[2,64,1152]{2,1,0:T(8,128)(2,1)S(1)}, bf16[2,64,1152]{2,1,0:T(8,128)(2,1)S(1)}, u32[]{:S(2)}, u32[]{:S(2)}) collective-permute-start(bf16[2,64,1152]{2,1,0:T(8,128)(2,1)S(1)} %get-tuple-element.408), channel_id=1, source_target_pairs={{0,8},{4,12},{8,0},{12,4},{16,24},{20,28},{24,16},{28,20},{1,9},{5... | collective-permute-start | bytes 884744 | tf_op jit(solution)/shard_map/ppermute | solution.py:553
  39.2 14.3 %collective-permute-start.2 = (bf16[2,64,1152]{2,1,0:T(8,128)(2,1)S(1)}, bf16[2,64,1152]{2,1,0:T(8,128)(2,1)S(1)}, u32[]{:S(2)}, u32[]{:S(2)}) collective-permute-start(bf16[2,64,1152]{2,1,0:T(8,128)(2,1)S(1)} %get-tuple-element.413), channel_id=1, source_target_pairs={{0,16},{4,20},{8,24},{12,28},{16,0},{20,4},{24,8},{28,12},{1,17},{... | collective-permute-start | bytes 884744 | tf_op jit(solution)/shard_map/ppermute | solution.py:553
  58.9 22.7 %collective-permute-start.3 = (bf16[256,2048]{1,0:T(8,128)(2,1)S(1)}, bf16[256,2048]{1,0:T(8,128)(2,1)S(1)}, u32[]{:S(2)}, u32[]{:S(2)}) collective-permute-start(bf16[256,2048]{1,0:T(8,128)(2,1)S(1)} %get-tuple-element.420.refs_0_), channel_id=1, source_target_pairs={{0,1},{3,2},{4,5},{7,6},{8,9},{11,10},{12,13},{15,14},{16,17},{19,... | collective-permute-start | bytes 3145736 | tf_op jit(solution)/shard_map/ppermute | solution.py:633
  81.6 23.0 %collective-permute-start.4 = (bf16[256,2048]{1,0:T(8,128)(2,1)S(1)}, bf16[256,2048]{1,0:T(8,128)(2,1)S(1)}, u32[]{:S(2)}, u32[]{:S(2)}) collective-permute-start(bf16[256,2048]{1,0:T(8,128)(2,1)S(1)} %get-tuple-element.424), channel_id=1, source_target_pairs={{0,1},{3,2},{4,5},{7,6},{8,9},{11,10},{12,13},{15,14},{16,17},{19,... | collective-permute-start | bytes 3145736 | tf_op jit(solution)/shard_map/ppermute | solution.py:633
  86.1 18.5 %collective-permute-start.5 = (bf16[256,2048]{1,0:T(8,128)(2,1)S(1)}, bf16[256,2048]{1,0:T(8,128)(2,1)S(1)}, u32[]{:S(2)}, u32[]{:S(2)}) collective-permute-start(bf16[256,2048]{1,0:T(8,128)(2,1)S(1)} %get-tuple-element.425.refs_2_), channel_id=1, source_target_pairs={{1,2},{2,1},{5,6},{6,5},{9,10},{10,9},{13,14},{14,13},{17,18},{18,... | collective-permute-start | bytes 3145736 | tf_op jit(solution)/shard_map/ppermute | solution.py:636
  104.7 22.1 %collective-permute-start.6 = (bf16[256,2048]{1,0:T(8,128)(2,1)S(1)}, bf16[256,2048]{1,0:T(8,128)(2,1)S(1)}, u32[]{:S(2)}, u32[]{:S(2)}) collective-permute-start(bf16[256,2048]{1,0:T(8,128)(2,1)S(1)} %get-tuple-element.433.refs_4_), channel_id=1, source_target_pairs={{0,1},{3,2},{1,0},{2,3},{4,5},{7,6},{5,4},{6,7},{8,9},{11,10},{9,8... | collective-permute-start | bytes 3145736 | tf_op jit(solution)/shard_map/ppermute | solution.py:633
  108.7 18.1 %collective-permute-start.7 = (bf16[256,2048]{1,0:T(8,128)(2,1)S(1)}, bf16[256,2048]{1,0:T(8,128)(2,1)S(1)}, u32[]{:S(2)}, u32[]{:S(2)}) collective-permute-start(bf16[256,2048]{1,0:T(8,128)(2,1)S(1)} %get-tuple-element.434.refs_2_), channel_id=1, source_target_pairs={{1,2},{2,1},{5,6},{6,5},{9,10},{10,9},{13,14},{14,13},{17,18},{18,... | collective-permute-start | bytes 3145736 | tf_op jit(solution)/shard_map/ppermute | solution.py:636
  128.0 26.5 %collective-permute-start.8 = (bf16[256,2048]{1,0:T(8,128)(2,1)S(1)}, bf16[256,2048]{1,0:T(8,128)(2,1)}, u32[]{:S(2)}, u32[]{:S(2)}) collective-permute-start(bf16[256,2048]{1,0:T(8,128)(2,1)S(1)} %get-tuple-element.438.refs_4_), channel_id=1, source_target_pairs={{0,1},{3,2},{1,0},{2,3},{4,5},{7,6},{5,4},{6,7},{8,9},{11,10},{9,8... | collective-permute-start | bytes 3145736 | tf_op jit(solution)/shard_map/ppermute | solution.py:633
  132.0 22.6 %collective-permute-start.9 = (bf16[256,2048]{1,0:T(8,128)(2,1)S(1)}, bf16[256,2048]{1,0:T(8,128)(2,1)}, u32[]{:S(2)}, u32[]{:S(2)}) collective-permute-start(bf16[256,2048]{1,0:T(8,128)(2,1)S(1)} %get-tuple-element.439.refs_2_), channel_id=1, source_target_pairs={{1,2},{2,1},{5,6},{6,5},{9,10},{10,9},{13,14},{14,13},{17,18},{18,... | collective-permute-start | bytes 3145736 | tf_op jit(solution)/shard_map/ppermute | solution.py:636
  156.2 22.9 %collective-permute-start.10 = (bf16[256,2048]{1,0:T(8,128)(2,1)S(1)}, bf16[256,2048]{1,0:T(8,128)(2,1)S(1)}, u32[]{:S(2)}, u32[]{:S(2)}) collective-permute-start(bf16[256,2048]{1,0:T(8,128)(2,1)S(1)} %get-tuple-element.455.refs_4_), channel_id=1, source_target_pairs={{0,1},{3,2},{1,0},{2,3},{4,5},{7,6},{5,4},{6,7},{8,9},{11,10},{9,8... | collective-permute-start | bytes 3145736 | tf_op jit(solution)/shard_map/ppermute | solution.py:633
  158.5 20.6 %collective-permute-start.11 = (bf16[256,2048]{1,0:T(8,128)(2,1)S(1)}, bf16[256,2048]{1,0:T(8,128)(2,1)S(1)}, u32[]{:S(2)}, u32[]{:S(2)}) collective-permute-start(bf16[256,2048]{1,0:T(8,128)(2,1)S(1)} %get-tuple-element.456.refs_2_), channel_id=1, source_target_pairs={{1,2},{2,1},{5,6},{6,5},{9,10},{10,9},{13,14},{14,13},{17,18},{18,... | collective-permute-start | bytes 3145736 | tf_op jit(solution)/shard_map/ppermute | solution.py:636
  179.3 23.3 %collective-permute-start.12 = (bf16[256,2048]{1,0:T(8,128)(2,1)S(1)}, bf16[256,2048]{1,0:T(8,128)(2,1)S(1)}, u32[]{:S(2)}, u32[]{:S(2)}) collective-permute-start(bf16[256,2048]{1,0:T(8,128)(2,1)S(1)} %get-tuple-element.472.refs_4_), channel_id=1, source_target_pairs={{0,1},{3,2},{1,0},{2,3},{4,5},{7,6},{5,4},{6,7},{8,9},{11,10},{9,8... | collective-permute-start | bytes 3145736 | tf_op jit(solution)/shard_map/ppermute | solution.py:633
  182.3 20.4 %collective-permute-start.13 = (bf16[256,2048]{1,0:T(8,128)(2,1)S(1)}, bf16[256,2048]{1,0:T(8,128)(2,1)S(1)}, u32[]{:S(2)}, u32[]{:S(2)}) collective-permute-start(bf16[256,2048]{1,0:T(8,128)(2,1)S(1)} %get-tuple-element.473.refs_2_), channel_id=1, source_target_pairs={{1,2},{2,1},{5,6},{6,5},{9,10},{10,9},{13,14},{14,13},{17,18},{18,... | collective-permute-start | bytes 3145736 | tf_op jit(solution)/shard_map/ppermute | solution.py:636
  202.9 22.9 %collective-permute-start.14 = (bf16[256,2048]{1,0:T(8,128)(2,1)S(1)}, bf16[256,2048]{1,0:T(8,128)(2,1)S(1)}, u32[]{:S(2)}, u32[]{:S(2)}) collective-permute-start(bf16[256,2048]{1,0:T(8,128)(2,1)S(1)} %get-tuple-element.499.refs_4_), channel_id=1, source_target_pairs={{0,1},{3,2},{1,0},{2,3},{4,5},{7,6},{5,4},{6,7},{8,9},{11,10},{9,8... | collective-permute-start | bytes 3145736 | tf_op jit(solution)/shard_map/ppermute | solution.py:633
  205.4 20.4 %collective-permute-start.15 = (bf16[256,2048]{1,0:T(8,128)(2,1)S(1)}, bf16[256,2048]{1,0:T(8,128)(2,1)S(1)}, u32[]{:S(2)}, u32[]{:S(2)}) collective-permute-start(bf16[256,2048]{1,0:T(8,128)(2,1)S(1)} %get-tuple-element.500.refs_2_), channel_id=1, source_target_pairs={{1,2},{2,1},{5,6},{6,5},{9,10},{10,9},{13,14},{14,13},{17,18},{18,... | collective-permute-start | bytes 3145736 | tf_op jit(solution)/shard_map/ppermute | solution.py:636
  227.3 23.1 %copy-start.3 = (bf16[256,2048]{1,0:T(8,128)(2,1)S(1)}, bf16[256,2048]{1,0:T(8,128)(2,1)}, u32[]{:S(2)}) copy-start(bf16[256,2048]{1,0:T(8,128)(2,1)} %get-tuple-element.530.refs_5_.refs_0_) | copy-start | bytes 3145732
  227.3 23.1 %collective-permute-start.16 = (bf16[256,2048]{1,0:T(8,128)(2,1)}, bf16[256,2048]{1,0:T(8,128)(2,1)}, u32[]{:S(2)}, u32[]{:S(2)}) collective-permute-start(bf16[256,2048]{1,0:T(8,128)(2,1)} %get-tuple-element.528.refs_4_), channel_id=1, source_target_pairs={{0,1},{3,2},{1,0},{2,3},{4,5},{7,6},{5,4},{6,7},{8,9},{11,10},{9,8... | collective-permute-start | bytes 3145736 | tf_op jit(solution)/shard_map/ppermute | solution.py:633
  229.7 20.7 %collective-permute-start.17 = (bf16[256,2048]{1,0:T(8,128)(2,1)}, bf16[256,2048]{1,0:T(8,128)(2,1)}, u32[]{:S(2)}, u32[]{:S(2)}) collective-permute-start(bf16[256,2048]{1,0:T(8,128)(2,1)} %get-tuple-element.529.refs_2_), channel_id=1, source_target_pairs={{1,2},{2,1},{5,6},{6,5},{9,10},{10,9},{13,14},{14,13},{17,18},{18,... | collective-permute-start | bytes 3145736 | tf_op jit(solution)/shard_map/ppermute | solution.py:636
  255.8 196.3 %reduce-scatter.6.cloned.1.call-start = ((), (), s32[]{:S(2)}) async-start(), calls=%async_computation.4 | async-start | bytes 11206656 | tf_op jit(solution)/shard_map/reduce_scatter | solution.py:989
  255.8 23.6 %collective-permute-start.18 = (bf16[256,2048]{1,0:T(8,128)(2,1)}, bf16[256,2048]{1,0:T(8,128)(2,1)S(1)}, u32[]{:S(2)}, u32[]{:S(2)}) collective-permute-start(bf16[256,2048]{1,0:T(8,128)(2,1)} %copy-done.24), channel_id=1, source_target_pairs={{0,1},{3,2},{1,0},{2,3},{4,5},{7,6},{5,4},{6,7},{8,9},{11,10},{9,8... | collective-permute-start | bytes 3145736 | tf_op jit(solution)/shard_map/ppermute | solution.py:633
  257.5 22.0 %collective-permute-start.19 = (bf16[256,2048]{1,0:T(8,128)(2,1)S(1)}, bf16[256,2048]{1,0:T(8,128)(2,1)S(1)}, u32[]{:S(2)}, u32[]{:S(2)}) collective-permute-start(bf16[256,2048]{1,0:T(8,128)(2,1)S(1)} %copy-done.23), channel_id=1, source_target_pairs={{1,2},{2,1},{5,6},{6,5},{9,10},{10,9},{13,14},{14,13},{17,18},{18,... | collective-permute-start | bytes 3145736 | tf_op jit(solution)/shard_map/ppermute | solution.py:636
  258.6 9.4 %copy-start.15 = (bf16[256,2048]{1,0:T(8,128)(2,1)S(1)}, bf16[256,2048]{1,0:T(8,128)(2,1)}, u32[]{:S(2)}) copy-start(bf16[256,2048]{1,0:T(8,128)(2,1)} %copy-done.14) | copy-start | bytes 3145732
  268.0 11.5 %copy-start.2 = (bf16[256,2048]{1,0:T(8,128)(2,1)S(1)}, bf16[256,2048]{1,0:T(8,128)(2,1)}, u32[]{:S(2)}) copy-start(bf16[256,2048]{1,0:T(8,128)(2,1)} %get-tuple-element.558.refs_5_.refs_0_) | copy-start | bytes 3145732
  268.0 11.5 %copy-start.25 = (bf16[256,2048]{1,0:T(8,128)(2,1)S(1)}, bf16[256,2048]{1,0:T(8,128)(2,1)}, u32[]{:S(2)}) copy-start(bf16[256,2048]{1,0:T(8,128)(2,1)} %copy-done.24) | copy-start | bytes 3145732
  279.7 24.9 %collective-permute-start.20 = (bf16[256,2048]{1,0:T(8,128)(2,1)S(1)}, bf16[256,2048]{1,0:T(8,128)(2,1)S(1)}, u32[]{:S(2)}, u32[]{:S(2)}) collective-permute-start(bf16[256,2048]{1,0:T(8,128)(2,1)S(1)} %get-tuple-element.584.refs_4_), channel_id=1, source_target_pairs={{0,1},{3,2},{1,0},{2,3},{4,5},{7,6},{5,4},{6,7},{8,9},{11,10},{9,8... | collective-permute-start | bytes 3145736 | tf_op jit(solution)/shard_map/ppermute | solution.py:633
  283.3 21.3 %collective-permute-start.21 = (bf16[256,2048]{1,0:T(8,128)(2,1)S(1)}, bf16[256,2048]{1,0:T(8,128)(2,1)S(1)}, u32[]{:S(2)}, u32[]{:S(2)}) collective-permute-start(bf16[256,2048]{1,0:T(8,128)(2,1)S(1)} %get-tuple-element.585.refs_2_), channel_id=1, source_target_pairs={{1,2},{2,1},{5,6},{6,5},{9,10},{10,9},{13,14},{14,13},{17,18},{18,... | collective-permute-start | bytes 3145736 | tf_op jit(solution)/shard_map/ppermute | solution.py:636
  293.8 10.8 %copy-start.1 = (bf16[256,2048]{1,0:T(8,128)(2,1)S(1)}, bf16[256,2048]{1,0:T(8,128)(2,1)}, u32[]{:S(2)}) copy-start(bf16[256,2048]{1,0:T(8,128)(2,1)} %get-tuple-element.586.refs_5_.refs_0_) | copy-start | bytes 3145732
  304.7 18.0 %collective-permute-start.23 = (bf16[256,2048]{1,0:T(8,128)(2,1)S(1)}, bf16[256,2048]{1,0:T(8,128)(2,1)S(1)}, u32[]{:S(2)}, u32[]{:S(2)}) collective-permute-start(bf16[256,2048]{1,0:T(8,128)(2,1)S(1)} %get-tuple-element.617.refs_4_), channel_id=1, source_target_pairs={{0,1},{3,2},{1,0},{2,3},{4,5},{7,6},{5,4},{6,7},{8,9},{11,10},{9,8... | collective-permute-start | bytes 3145736 | tf_op jit(solution)/shard_map/ppermute | solution.py:633
  307.1 15.6 %collective-permute-start.24 = (bf16[256,2048]{1,0:T(8,128)(2,1)S(1)}, bf16[256,2048]{1,0:T(8,128)(2,1)S(1)}, u32[]{:S(2)}, u32[]{:S(2)}) collective-permute-start(bf16[256,2048]{1,0:T(8,128)(2,1)S(1)} %get-tuple-element.618.refs_2_), channel_id=1, source_target_pairs={{1,2},{2,1},{5,6},{6,5},{9,10},{10,9},{13,14},{14,13},{17,18},{18,... | collective-permute-start | bytes 3145736 | tf_op jit(solution)/shard_map/ppermute | solution.py:636
  317.4 1.6 collective-permute-start.22
  321.2 20.8 %collective-permute-start.27 = (bf16[2,64,1152]{2,1,0:T(8,128)(2,1)}, bf16[2,64,1152]{2,1,0:T(8,128)(2,1)S(1)}, u32[]{:S(2)}, u32[]{:S(2)}) collective-permute-start(bf16[2,64,1152]{2,1,0:T(8,128)(2,1)} %get-tuple-element.648), channel_id=1, source_target_pairs={{0,8},{4,12},{8,0},{12,4},{16,24},{20,28},{24,16},{28,20},{1,9},{5... | collective-permute-start | bytes 884744 | tf_op jit(solution)/shard_map/ppermute | solution.py:553
  325.2 37.1 %collective-permute-start.25 = (bf16[256,2048]{1,0:T(8,128)(2,1)}, bf16[256,2048]{1,0:T(8,128)(2,1)}, u32[]{:S(2)}, u32[]{:S(2)}) collective-permute-start(bf16[256,2048]{1,0:T(8,128)(2,1)} %get-tuple-element.626.refs_4_), channel_id=1, source_target_pairs={{0,1},{3,2},{1,0},{2,3},{4,5},{7,6},{5,4},{6,7},{8,9},{11,10},{9,8... | collective-permute-start | bytes 3145736 | tf_op jit(solution)/shard_map/ppermute | solution.py:633
  329.1 33.2 %collective-permute-start.26 = (bf16[256,2048]{1,0:T(8,128)(2,1)}, bf16[256,2048]{1,0:T(8,128)(2,1)}, u32[]{:S(2)}, u32[]{:S(2)}) collective-permute-start(bf16[256,2048]{1,0:T(8,128)(2,1)} %get-tuple-element.627.refs_2_), channel_id=1, source_target_pairs={{1,2},{2,1},{5,6},{6,5},{9,10},{10,9},{13,14},{14,13},{17,18},{18,... | collective-permute-start | bytes 3145736 | tf_op jit(solution)/shard_map/ppermute | solution.py:636
  343.9 9.1 %collective-permute-start.28 = (bf16[2,64,1152]{2,1,0:T(8,128)(2,1)S(1)}, bf16[2,64,1152]{2,1,0:T(8,128)(2,1)S(1)}, u32[]{:S(2)}, u32[]{:S(2)}) collective-permute-start(bf16[2,64,1152]{2,1,0:T(8,128)(2,1)S(1)} %get-tuple-element.653), channel_id=1, source_target_pairs={{0,16},{4,20},{8,24},{12,28},{16,0},{20,4},{24,8},{28,12},{1,17},{... | collective-permute-start | bytes 884744 | tf_op jit(solution)/shard_map/ppermute | solution.py:553
  368.0 138.1 %reduce-scatter.8.cloned.1.call-start = ((), (), s32[]{:S(2)}) async-start(), calls=%async_computation.5 | async-start | bytes 5640192 | tf_op jit(solution)/shard_map/reduce_scatter | solution.py:1009
  368.0 23.9 %collective-permute-start.29 = (bf16[256,2048]{1,0:T(8,128)(2,1)}, bf16[256,2048]{1,0:T(8,128)(2,1)S(1)}, u32[]{:S(2)}, u32[]{:S(2)}) collective-permute-start(bf16[256,2048]{1,0:T(8,128)(2,1)} %get-tuple-element.679.refs_4_), channel_id=1, source_target_pairs={{0,1},{3,2},{1,0},{2,3},{4,5},{7,6},{5,4},{6,7},{8,9},{11,10},{9,8... | collective-permute-start | bytes 3145736 | tf_op jit(solution)/shard_map/ppermute | solution.py:633
  369.2 22.8 %collective-permute-start.30 = (bf16[256,2048]{1,0:T(8,128)(2,1)}, bf16[256,2048]{1,0:T(8,128)(2,1)S(1)}, u32[]{:S(2)}, u32[]{:S(2)}) collective-permute-start(bf16[256,2048]{1,0:T(8,128)(2,1)} %get-tuple-element.680.refs_2_), channel_id=1, source_target_pairs={{1,2},{2,1},{5,6},{6,5},{9,10},{10,9},{13,14},{14,13},{17,18},{18,... | collective-permute-start | bytes 3145736 | tf_op jit(solution)/shard_map/ppermute | solution.py:636
  378.7 13.2 %copy-start.7 = (bf16[256,2048]{1,0:T(8,128)(2,1)S(1)}, bf16[256,2048]{1,0:T(8,128)(2,1)}, u32[]{:S(2)}) copy-start(bf16[256,2048]{1,0:T(8,128)(2,1)} %copy-done.6) | copy-start | bytes 3145732
  396.0 25.4 %collective-permute-start.31 = (bf16[256,2048]{1,0:T(8,128)(2,1)}, bf16[256,2048]{1,0:T(8,128)(2,1)}, u32[]{:S(2)}, u32[]{:S(2)}) collective-permute-start(bf16[256,2048]{1,0:T(8,128)(2,1)} %get-tuple-element.696.refs_4_), channel_id=1, source_target_pairs={{0,1},{3,2},{1,0},{2,3},{4,5},{7,6},{5,4},{6,7},{8,9},{11,10},{9,8... | collective-permute-start | bytes 3145736 | tf_op jit(solution)/shard_map/ppermute | solution.py:633
  399.7 21.7 %collective-permute-start.32 = (bf16[256,2048]{1,0:T(8,128)(2,1)}, bf16[256,2048]{1,0:T(8,128)(2,1)}, u32[]{:S(2)}, u32[]{:S(2)}) collective-permute-start(bf16[256,2048]{1,0:T(8,128)(2,1)} %get-tuple-element.697.refs_2_), channel_id=1, source_target_pairs={{1,2},{2,1},{5,6},{6,5},{9,10},{10,9},{13,14},{14,13},{17,18},{18,... | collective-permute-start | bytes 3145736 | tf_op jit(solution)/shard_map/ppermute | solution.py:636
  409.6 11.8 %copy-start.5 = (bf16[256,2048]{1,0:T(8,128)(2,1)S(1)}, bf16[256,2048]{1,0:T(8,128)(2,1)}, u32[]{:S(2)}) copy-start(bf16[256,2048]{1,0:T(8,128)(2,1)} %copy-done.4) | copy-start | bytes 3145732
  426.8 7.6 %copy-start.9 = (bf16[256,2048]{1,0:T(8,128)(2,1)S(1)}, bf16[256,2048]{1,0:T(8,128)(2,1)}, u32[]{:S(2)}) copy-start(bf16[256,2048]{1,0:T(8,128)(2,1)} %copy-done.8) | copy-start | bytes 3145732
  426.8 23.2 %collective-permute-start.33 = (bf16[256,2048]{1,0:T(8,128)(2,1)}, bf16[256,2048]{1,0:T(8,128)(2,1)S(1)}, u32[]{:S(2)}, u32[]{:S(2)}) collective-permute-start(bf16[256,2048]{1,0:T(8,128)(2,1)} %copy-done.28), channel_id=1, source_target_pairs={{0,1},{3,2},{1,0},{2,3},{4,5},{7,6},{5,4},{6,7},{8,9},{11,10},{9,8... | collective-permute-start | bytes 3145736 | tf_op jit(solution)/shard_map/ppermute | solution.py:633
  430.0 20.0 %collective-permute-start.34 = (bf16[256,2048]{1,0:T(8,128)(2,1)}, bf16[256,2048]{1,0:T(8,128)(2,1)S(1)}, u32[]{:S(2)}, u32[]{:S(2)}) collective-permute-start(bf16[256,2048]{1,0:T(8,128)(2,1)} %copy-done.26), channel_id=1, source_target_pairs={{1,2},{2,1},{5,6},{6,5},{9,10},{10,9},{13,14},{14,13},{17,18},{18,... | collective-permute-start | bytes 3145736 | tf_op jit(solution)/shard_map/ppermute | solution.py:636
  434.4 15.6 %copy-start.27 = (bf16[256,2048]{1,0:T(8,128)(2,1)S(1)}, bf16[256,2048]{1,0:T(8,128)(2,1)}, u32[]{:S(2)}) copy-start(bf16[256,2048]{1,0:T(8,128)(2,1)} %copy-done.26) | copy-start | bytes 3145732
  434.4 15.6 %copy-start.29 = (bf16[256,2048]{1,0:T(8,128)(2,1)S(1)}, bf16[256,2048]{1,0:T(8,128)(2,1)}, u32[]{:S(2)}) copy-start(bf16[256,2048]{1,0:T(8,128)(2,1)} %copy-done.28) | copy-start | bytes 3145732
  452.1 10.3 %copy-start.11 = (bf16[256,2048]{1,0:T(8,128)(2,1)S(1)}, bf16[256,2048]{1,0:T(8,128)(2,1)}, u32[]{:S(2)}) copy-start(bf16[256,2048]{1,0:T(8,128)(2,1)} %copy-done.10) | copy-start | bytes 3145732
  452.1 22.8 %collective-permute-start.35 = (bf16[256,2048]{1,0:T(8,128)(2,1)}, bf16[256,2048]{1,0:T(8,128)(2,1)S(1)}, u32[]{:S(2)}, u32[]{:S(2)}) collective-permute-start(bf16[256,2048]{1,0:T(8,128)(2,1)} %copy-done.16), channel_id=1, source_target_pairs={{0,1},{3,2},{1,0},{2,3},{4,5},{7,6},{5,4},{6,7},{8,9},{11,10},{9,8... | collective-permute-start | bytes 3145736 | tf_op jit(solution)/shard_map/ppermute | solution.py:633
  456.0 18.9 %collective-permute-start.36 = (bf16[256,2048]{1,0:T(8,128)(2,1)S(1)}, bf16[256,2048]{1,0:T(8,128)(2,1)S(1)}, u32[]{:S(2)}, u32[]{:S(2)}) collective-permute-start(bf16[256,2048]{1,0:T(8,128)(2,1)S(1)} %get-tuple-element.757.refs_2_), channel_id=1, source_target_pairs={{1,2},{2,1},{5,6},{6,5},{9,10},{10,9},{13,14},{14,13},{17,18},{18,... | collective-permute-start | bytes 3145736 | tf_op jit(solution)/shard_map/ppermute | solution.py:636
  466.0 9.0 %copy-start.17 = (bf16[256,2048]{1,0:T(8,128)(2,1)S(1)}, bf16[256,2048]{1,0:T(8,128)(2,1)}, u32[]{:S(2)}) copy-start(bf16[256,2048]{1,0:T(8,128)(2,1)} %copy-done.16) | copy-start | bytes 3145732
  469.5 9.7 %copy-start.47 = (bf16[1,2,256,1408]{3,2,1,0:T(8,128)(2,1)S(1)}, bf16[1,2,256,1408]{3,2,1,0:T(8,128)(2,1)}, u32[]{:S(2)}) copy-start(bf16[1,2,256,1408]{3,2,1,0:T(8,128)(2,1)} %reduce-scatter.4.cloned.1.call-done) | copy-start | bytes 4325380
  477.1 23.2 %collective-permute-start.37 = (bf16[256,2048]{1,0:T(8,128)(2,1)}, bf16[256,2048]{1,0:T(8,128)(2,1)S(1)}, u32[]{:S(2)}, u32[]{:S(2)}) collective-permute-start(bf16[256,2048]{1,0:T(8,128)(2,1)} %get-tuple-element.767.refs_3_), channel_id=1, source_target_pairs={{1,0},{2,3},{5,4},{6,7},{9,8},{10,11},{13,12},{14,15},{17,16},{18,... | collective-permute-start | bytes 3145736 | tf_op jit(solution)/shard_map/ppermute | solution.py:633
  478.5 21.8 %collective-permute-start.38 = (bf16[256,2048]{1,0:T(8,128)(2,1)S(1)}, bf16[256,2048]{1,0:T(8,128)(2,1)S(1)}, u32[]{:S(2)}, u32[]{:S(2)}) collective-permute-start(bf16[256,2048]{1,0:T(8,128)(2,1)S(1)} %get-tuple-element.768.refs_1_), channel_id=1, source_target_pairs={{1,2},{2,1},{5,6},{6,5},{9,10},{10,9},{13,14},{14,13},{17,18},{18,... | collective-permute-start | bytes 3145736 | tf_op jit(solution)/shard_map/ppermute | solution.py:636
  486.4 13.9 %copy-start.31 = (bf16[256,2048]{1,0:T(8,128)(2,1)S(1)}, bf16[256,2048]{1,0:T(8,128)(2,1)}, u32[]{:S(2)}) copy-start(bf16[256,2048]{1,0:T(8,128)(2,1)} %copy-done.30) | copy-start | bytes 3145732
  502.6 22.3 %collective-permute-start.39 = (bf16[256,2048]{1,0:T(8,128)(2,1)S(1)}, bf16[256,2048]{1,0:T(8,128)(2,1)S(1)}, u32[]{:S(2)}, u32[]{:S(2)}) collective-permute-start(bf16[256,2048]{1,0:T(8,128)(2,1)S(1)} %get-tuple-element.775.refs_1_), channel_id=1, source_target_pairs={{1,0},{2,3},{5,4},{6,7},{9,8},{10,11},{13,12},{14,15},{17,16},{18,... | collective-permute-start | bytes 3145736 | tf_op jit(solution)/shard_map/ppermute | solution.py:633
  508.1 9.9 %copy-start.33 = (bf16[256,2048]{1,0:T(8,128)(2,1)S(1)}, bf16[256,2048]{1,0:T(8,128)(2,1)}, u32[]{:S(2)}) copy-start(bf16[256,2048]{1,0:T(8,128)(2,1)} %copy-done.32) | copy-start | bytes 3145732
  508.1 14.1 %collective-permute-start.42 = (f32[256]{0:T(256)S(1)}, f32[256]{0:T(256)S(1)}, u32[]{:S(2)}, u32[]{:S(2)}) collective-permute-start(f32[256]{0:T(256)S(1)} %get-tuple-element.823), channel_id=1, source_target_pairs={{0,3},{1,2},{2,1},{3,0},{4,7},{5,6},{6,5},{7,4},{8,11},{9,10},{10,... | collective-permute-start | bytes 3080 | tf_op jit(solution)/shard_map/ppermute | solution.py:1030
  510.7 11.5 %collective-permute-start.41 = (f32[256]{0:T(256)S(1)}, f32[256]{0:T(256)S(1)}, u32[]{:S(2)}, u32[]{:S(2)}) collective-permute-start(f32[256]{0:T(256)S(1)} %get-tuple-element.823), channel_id=1, source_target_pairs={{0,2},{1,3},{2,0},{3,1},{4,6},{5,7},{6,4},{7,5},{8,10},{9,11},{10,... | collective-permute-start | bytes 3080 | tf_op jit(solution)/shard_map/ppermute | solution.py:1030
  513.3 11.1 %collective-permute-start.40 = (f32[256]{0:T(256)S(1)}, f32[256]{0:T(256)S(1)}, u32[]{:S(2)}, u32[]{:S(2)}) collective-permute-start(f32[256]{0:T(256)S(1)} %get-tuple-element.823), channel_id=1, source_target_pairs={{0,1},{1,0},{2,3},{3,2},{4,5},{5,4},{6,7},{7,6},{8,9},{9,8},{10,11... | collective-permute-start | bytes 3080 | tf_op jit(solution)/shard_map/ppermute | solution.py:1030
  (34 other events, 75.3 us)
Sparse Core Ops, SparseCore 0:
  28.5 100.1 all-gather.2
  255.9 91.6 reduce-scatter.3
  368.1 78.0 reduce-scatter.5
  449.5 55.7 reduce-scatter.7

commit v11 on v9

--- a/solution.py
+++ b/solution.py
@@ -918,8 +918,8 @@
         [shaped(local.shape, f32), shaped(decay.shape, f32), shaped(sent.shape, bf16)],
     )
 
-    xn_columns = [pl.BlockSpec((rows, TILE), lambda j: (0, j))]
-    piece_columns = [pl.BlockSpec((TILE, TILE), lambda j: (0, j))] * len(every)
+    xn_columns = [pl.BlockSpec((rows, 2 * columns), lambda j: (0, j))]
+    piece_columns = [pl.BlockSpec((TILE, 2 * columns), lambda j: (0, j))] * len(every)
     piece_whole = [fixed((TILE, head))] * len(every)
     made = []
 
@@ -934,11 +934,11 @@
         grads = call(
             "query_grads",
             functools.partial(query_grad_kernel, len(every), units),
-            (width // columns,),
+            (width // columns // 2,),
             xn_columns + piece_columns + piece_whole * 2 + [anywhere],
             anywhere,
             shaped((n_seq, span, units + 2 * head), bf16),
-            [pltpu.VMEM((2, group, span, 2 * head), bf16), pltpu.SemaphoreType.DMA((2,))],
+            [pltpu.VMEM((2, 2 * group, span, 2 * head), bf16), pltpu.SemaphoreType.DMA((2,))],
             cost=cost(12 * rows * width * head, 3 * (4 * rows * width + 4 * rows * head + 4 * width * head)),
             aliases={1 + 3 * len(every): 0},
         )(behind_of(made[0], state), *[backs[key][0] for key in every], *[backs[key][1] for key in every],
@@ -961,13 +961,13 @@
     start()
     go_last(1, 1)
     live.pop("leaving")
-    few = [pl.BlockSpec((8, TILE), lambda j: (0, j))] * len(every)
+    few = [pl.BlockSpec((8, 2 * columns), lambda j: (0, j))] * len(every)
     live["state_grads"] = call(
         "state_grads",
         functools.partial(state_grad_kernel, len(every)),
-        (width // TILE,),
+        (width // columns // 2,),
         xn_columns + piece_whole * 2 + [fixed((TILE, slots))] * len(every) + [fixed((8, slots))] * len(every) + few * 2,
-        pl.BlockSpec((group, span + 16, 2 * head + 128), lambda j: (j, 0, 0)),
+        pl.BlockSpec((2 * group, span + 16, 2 * head + 128), lambda j: (j, 0, 0)),
         shaped((n_seq, span + 16, 2 * head + 128), bf16),
         cost=cost(4 * rows * width * head, 2 * rows * width + 4 * rows * head + 4 * width * head),
     )(live.pop("xn"), *[lasts[key][i] for i in (0, 1, 2, 4, 5) for key in every], *[backs[key][9] for key in every])

time: 540 us -> 543 us (level)
  the two profiles are of different devices: /device:TPU:4 before, /device:TPU:0 now
where the time goes in v11:
time: 543 us; the launch traced here: 535 us
  Pallas kernels  283 us (52%)
  waiting for transfers between devices  107 us (20%)
  starting transfers between devices  89.5 us (16%)
  local copies, waits for them, and re-layouts  30.6 us (6%)
  between operations  15.1 us (3%)
  other arithmetic  10.3 us (2%)
    pallas_call x30, Pallas kernels, run(): function(*[o if i in loose or spec.memory_space == pltpu.SMEM else pltpu....  261 us
    ppermute x18, waiting for transfers between devices, step(): outer = lax.ppermute(payload, 'head', way)  80 us
    ppermute x18, starting transfers between devices, step(): outer = lax.ppermute(payload, 'head', way)  56.7 us
    unnamed x105, local copies, waits for them, and re-layouts  28.1 us
    ppermute x6, waiting for transfers between devices, scan_states(): got = lax.ppermute(sent, 'seq', [(i, i ^ bit) for i in range(n)])  22.3 us
    pallas_call x25, Pallas kernels, in_vmem(): pl.pallas_call(kernel, name=name, in_specs=[pl.BlockSpec(memory_space=plt...  22.2 us
    ppermute x16, starting transfers between devices, step(): middle = lax.ppermute(pair, 'head', self.MIDDLE)  17 us
  transfers between devices with their start and end apart: 47, of which 15 were waited for; matrix products, arithmetic and copies ran while one was open for 3% of the time, Pallas kernels for 48%

profile of v11, /device:TPU:0, one launch (start us, length us, event | category | flops | bytes accessed | tf_op | source)
XLA Modules:
  0.0 535.4 jit_solution(3918391655016892754)
XLA Ops:
  7.2 14.9 %project.1 = (bf16[1024,2048]{1,0:T(8,128)(2,1)}, bf16[1024,512]{1,0:T(8,128)(2,1)}, bf16[1024,512]{1,0:T(8,128)(2,1)}, f32[1024,64]{1,0:T(8,128)}, f32[1024,64]...) custom-call(bf16[1024,2048]{1,0:T(8,128)(2,1)} %bitcast.35, ...), custom_call_target="tpu_custom_call" | custom-call | flops 4563402752 | bytes 16777216 | tf_op jit(solution)/shard_map/project/pallas_call | solution.py:62
  24.2 2.7 pad_maximum_fusion
  27.2 2.9 collective-permute-start.1
  30.1 7.3 %collective-permute-done.1.refs_2_ = bf16[2,64,1152]{2,1,0:T(8,128)(2,1)S(1)} collective-permute-done((bf16[2,64,1152]{2,1,0:T(8,128)(2,1)S(1)}, bf16[2,64,1152]{2,1,0:T(8,128)(2,1)S(1)}, u32[]{:S(2)}, u32[]{:S(2)}) %collective-permute-start.1) | collective-permute-done | bytes 294944 | tf_op jit(solution)/shard_map/ppermute | solution.py:521
  39.5 6.7 %query.1.q_ref = bf16[1024,512]{1,0:T(8,128)(2,1)} custom-call(bf16[1024,2048]{1,0:T(8,128)(2,1)} %get-tuple-element.715.xn_ref.refs_0_, bf16[2048,512]{1,0:T(8,128)(2,1)} %wq_ref.9), custom_call_target="tpu_custom_call" | custom-call | flops 2147483648 | bytes 7340032 | tf_op jit(solution)/shard_map/query/pallas_call | solution.py:62
  46.2 5.8 %collective-permute-done.2.refs_2_ = bf16[2,64,1152]{2,1,0:T(8,128)(2,1)S(1)} collective-permute-done((bf16[2,64,1152]{2,1,0:T(8,128)(2,1)S(1)}, bf16[2,64,1152]{2,1,0:T(8,128)(2,1)S(1)}, u32[]{:S(2)}, u32[]{:S(2)}) %collective-permute-start.2) | collective-permute-done | bytes 294944 | tf_op jit(solution)/shard_map/ppermute | solution.py:521
  52.3 5.3 read.4
  57.6 3.8 collective-permute-start.3
  61.5 5.3 read.5
  66.8 13.5 %collective-permute-done.3.refs_1_ = bf16[256,2048]{1,0:T(8,128)(2,1)S(1)} collective-permute-done((bf16[256,2048]{1,0:T(8,128)(2,1)S(1)}, bf16[256,2048]{1,0:T(8,128)(2,1)S(1)}, u32[]{:S(2)}, u32[]{:S(2)}) %collective-permute-start.3) | collective-permute-done | bytes 1048608 | tf_op jit(solution)/shard_map/ppermute | solution.py:601
  80.4 4.5 collective-permute-start.4
  85.6 5.2 read.6
  90.9 12.5 %collective-permute-done.4.refs_1_ = bf16[256,2048]{1,0:T(8,128)(2,1)S(1)} collective-permute-done((bf16[256,2048]{1,0:T(8,128)(2,1)S(1)}, bf16[256,2048]{1,0:T(8,128)(2,1)S(1)}, u32[]{:S(2)}, u32[]{:S(2)}) %collective-permute-start.4) | collective-permute-done | bytes 1048608 | tf_op jit(solution)/shard_map/ppermute | solution.py:601
  103.5 3.9 collective-permute-start.6
  108.2 5.4 %read.7 = (bf16[256,512]{1,0:T(8,128)(2,1)}, f32[256,64]{1,0:T(8,128)}, f32[256,64]{1,0:T(8,128)}, f32[2,64,1024]{2,1,0:T(8,128)}, f32[1,64,1024]{2,1,0:T(8,128)}, /*index=5*/bf16[256,2048]{1,0:T(8,128)(2,1)S(1)}) custom-call(bf16[1024,512]{1,0:T(8,128)(2,1)} %query.1.q_ref, bf16[1024,512]{1,0:T(8,128)(2,1)} %get-tuple-element.399.k_ref, ...), custom_call_target="tpu_custom_call" | custom-call | flops 694157312 | bytes 4194304 | tf_op jit(solution)/shard_map/read/pallas_call | solution.py:62
  113.5 12.0 %collective-permute-done.6.refs_1_ = bf16[256,2048]{1,0:T(8,128)(2,1)S(1)} collective-permute-done((bf16[256,2048]{1,0:T(8,128)(2,1)S(1)}, bf16[256,2048]{1,0:T(8,128)(2,1)S(1)}, u32[]{:S(2)}, u32[]{:S(2)}) %collective-permute-start.6) | collective-permute-done | bytes 1048608 | tf_op jit(solution)/shard_map/ppermute | solution.py:601
  126.8 3.9 collective-permute-start.8
  134.1 19.4 %feed.4 = (bf16[256,2048]{1,0:T(8,128)(2,1)}, bf16[256,2048]{1,0:T(8,128)(2,1)}, bf16[256,1408]{1,0:T(8,128)(2,1)}, bf16[256,1408]{1,0:T(8,128)(2,1)}, bf16[256,...) custom-call(bf16[1024,2048]{1,0:T(8,128)(2,1)} %bitcast.36, ...), custom_call_target="tpu_custom_call" | custom-call | flops 8858370048 | bytes 24641536 | tf_op jit(solution)/shard_map/feed/pallas_call | solution.py:62
  155.2 2.3 collective-permute-start.10
  158.4 19.5 %feed.5 = (bf16[256,2048]{1,0:T(8,128)(2,1)}, bf16[256,2048]{1,0:T(8,128)(2,1)}, bf16[256,1408]{1,0:T(8,128)(2,1)}, bf16[256,1408]{1,0:T(8,128)(2,1)}, bf16[256,...) custom-call(bf16[1024,2048]{1,0:T(8,128)(2,1)} %bitcast.37, ...), custom_call_target="tpu_custom_call" | custom-call | flops 8858370048 | bytes 24641536 | tf_op jit(solution)/shard_map/feed/pallas_call | solution.py:62
  178.1 3.0 collective-permute-start.12
  182.0 19.5 %feed.6 = (bf16[256,2048]{1,0:T(8,128)(2,1)}, bf16[256,2048]{1,0:T(8,128)(2,1)}, bf16[256,1408]{1,0:T(8,128)(2,1)}, bf16[256,1408]{1,0:T(8,128)(2,1)}, bf16[256,...) custom-call(bf16[1024,2048]{1,0:T(8,128)(2,1)} %bitcast.38, ...), custom_call_target="tpu_custom_call" | custom-call | flops 8858370048 | bytes 24641536 | tf_op jit(solution)/shard_map/feed/pallas_call | solution.py:62
  201.7 2.3 collective-permute-start.14
  205.1 19.5 %feed.7 = (bf16[256,2048]{1,0:T(8,128)(2,1)}, bf16[256,2048]{1,0:T(8,128)(2,1)}, bf16[256,1408]{1,0:T(8,128)(2,1)}, bf16[256,1408]{1,0:T(8,128)(2,1)}, bf16[256,...) custom-call(bf16[1024,2048]{1,0:T(8,128)(2,1)} %bitcast.39, ...), custom_call_target="tpu_custom_call" | custom-call | flops 8858370048 | bytes 24641536 | tf_op jit(solution)/shard_map/feed/pallas_call | solution.py:62
  226.1 2.6 collective-permute-start.16
  230.3 19.0 %wide_grads.1 = bf16[8,2,256,1408]{3,2,1,0:T(8,128)(2,1)} custom-call(bf16[256,2048]{1,0:T(8,128)(2,1)} %get-tuple-element.545.refs_0_, bf16[256,2048]{1,0:T(8,128)(2,1)} %get-tuple-element.546.refs_1_, bf16[256,2048]{1,0:T(8,128)(2,1)} %get-tuple-element.547.refs_2_, bf16[256,2048]{1,0:T(8,128)(2,1)} %get-tuple-element.548.refs_3_, ...), custom_call_target="tpu_custom_call" | custom-call | flops 11811160064 | bytes 21495808 | tf_op jit(solution)/shard_map/wide_grads/pallas_call | solution.py:62
  249.4 2.3 join.25
  257.2 8.4 %back.4 = (bf16[256,2048]{1,0:T(8,128)(2,1)}, bf16[256,512]{1,0:T(8,128)(2,1)}, f32[256,512]{1,0:T(8,128)}, f32[256,512]{1,0:T(8,128)}, f32[256,64]{1,0:T(8,128)...) custom-call(bf16[256,2048]{1,0:T(8,128)(2,1)S(1)} %get-tuple-element, ...), custom_call_target="tpu_custom_call" | custom-call | flops 930086912 | bytes 9961472 | tf_op jit(solution)/shard_map/back/pallas_call | solution.py:62
  265.7 9.6 %back.5 = (bf16[256,2048]{1,0:T(8,128)(2,1)}, bf16[256,512]{1,0:T(8,128)(2,1)}, f32[256,512]{1,0:T(8,128)}, f32[256,512]{1,0:T(8,128)}, f32[256,64]{1,0:T(8,128)...) custom-call(bf16[256,2048]{1,0:T(8,128)(2,1)S(1)} %copy-done.15, ...), custom_call_target="tpu_custom_call" | custom-call | flops 930086912 | bytes 9961472 | tf_op jit(solution)/shard_map/back/pallas_call | solution.py:62
  275.5 3.9 collective-permute-start.20
  280.1 8.2 %back.6 = (bf16[256,2048]{1,0:T(8,128)(2,1)}, bf16[256,512]{1,0:T(8,128)(2,1)}, f32[256,512]{1,0:T(8,128)}, f32[256,512]{1,0:T(8,128)}, f32[256,64]{1,0:T(8,128)...) custom-call(bf16[256,2048]{1,0:T(8,128)(2,1)S(1)} %get-tuple-element, ...), custom_call_target="tpu_custom_call" | custom-call | flops 930086912 | bytes 9961472 | tf_op jit(solution)/shard_map/back/pallas_call | solution.py:62
  288.3 10.8 %down_grads.1.refs_13_ = bf16[8,256,2432]{2,1,0:T(8,128)(2,1)} custom-call(bf16[1024,2048]{1,0:T(8,128)(2,1)} %bitcast.55, bf16[256,1408]{1,0:T(8,128)(2,1)} %get-tuple-element.599.refs_1_, bf16[256,1408]{1,0:T(8,128)(2,1)} %get-tuple-element.600.refs_2_, bf16[256,1408]{1,0:T(8,128)(2,1)} %get-tuple-element.601.refs_3_, ...), custom_call_target="tpu_custom_call" | custom-call | flops 5905580032 | bytes 12845056 | tf_op jit(solution)/shard_map/down_grads/pallas_call | solution.py:62
  299.3 4.1 collective-permute-start.23
  304.1 8.4 %back.7 = (bf16[256,2048]{1,0:T(8,128)(2,1)}, bf16[256,512]{1,0:T(8,128)(2,1)}, f32[256,512]{1,0:T(8,128)}, f32[256,512]{1,0:T(8,128)}, f32[256,64]{1,0:T(8,128)...) custom-call(bf16[256,2048]{1,0:T(8,128)(2,1)S(1)} %get-tuple-element, ...), custom_call_target="tpu_custom_call" | custom-call | flops 930086912 | bytes 9961472 | tf_op jit(solution)/shard_map/back/pallas_call | solution.py:62
  321.6 3.8 collective-permute-start.25
  327.2 9.3 %query_grads.1 = bf16[8,256,2432]{2,1,0:T(8,128)(2,1)} custom-call(bf16[1024,2048]{1,0:T(8,128)(2,1)} %get-tuple-element.715.xn_ref.refs_0_, bf16[256,2048]{1,0:T(8,128)(2,1)} %get-tuple-element.633.refs_1_.dhid_ref, bf16[256,2048]{1,0:T(8,128)(2,1)} %get-tuple-element.634.refs_2_.dhid_ref, ...), custom_call_target="tpu_custom_call", output_to_operand_aliasing={{}: (13, {})} | custom-call | flops 12884901888 | bytes 44040192 | tf_op jit(solution)/shard_map/query_grads/pallas_call | solution.py:62
  338.5 3.6 collective-permute-start.28
  342.0 6.4 %collective-permute-done.28.refs_2_ = bf16[2,64,1152]{2,1,0:T(8,128)(2,1)S(1)} collective-permute-done((bf16[2,64,1152]{2,1,0:T(8,128)(2,1)S(1)}, bf16[2,64,1152]{2,1,0:T(8,128)(2,1)S(1)}, u32[]{:S(2)}, u32[]{:S(2)}) %collective-permute-start.28) | collective-permute-done | bytes 294944 | tf_op jit(solution)/shard_map/ppermute | solution.py:521
  349.6 8.1 %last.4 = (bf16[256,512]{1,0:T(8,128)(2,1)}, bf16[256,512]{1,0:T(8,128)(2,1)}, bf16[256,64]{1,0:T(8,128)(2,1)}, bf16[256,2048]{1,0:T(8,128)(2,1)S(1)}, f32[8,64]{1,0:T(8,128)}, /*index=5*/f32[8,2048]{1,0:T(8,128)}) custom-call(f32[4,64,1024]{2,1,0:T(8,128)S(1)} %hop.11.l0_ref, bf16[1024,512]{1,0:T(8,128)(2,1)} %get-tuple-element.399.k_ref, ...), custom_call_target="tpu_custom_call" | custom-call | flops 1677721600 | bytes 13107200 | tf_op jit(solution)/shard_map/last/pallas_call | solution.py:62
  357.7 3.7 join.29
  365.8 9.0 %last.6 = (bf16[256,512]{1,0:T(8,128)(2,1)}, bf16[256,512]{1,0:T(8,128)(2,1)}, bf16[256,64]{1,0:T(8,128)(2,1)}, bf16[256,2048]{1,0:T(8,128)(2,1)S(1)}, f32[8,64]{1,0:T(8,128)}, /*index=5*/f32[8,2048]{1,0:T(8,128)}) custom-call(f32[4,64,1024]{2,1,0:T(8,128)S(1)} %hop.11.l0_ref, bf16[1024,512]{1,0:T(8,128)(2,1)} %get-tuple-element.399.k_ref, ...), custom_call_target="tpu_custom_call" | custom-call | flops 1677721600 | bytes 13107200 | tf_op jit(solution)/shard_map/last/pallas_call | solution.py:62
  374.8 9.8 %last.5 = (bf16[256,512]{1,0:T(8,128)(2,1)}, bf16[256,512]{1,0:T(8,128)(2,1)}, bf16[256,64]{1,0:T(8,128)(2,1)}, bf16[256,2048]{1,0:T(8,128)(2,1)S(1)}, f32[8,64]{1,0:T(8,128)}, /*index=5*/f32[8,2048]{1,0:T(8,128)}) custom-call(f32[4,64,1024]{2,1,0:T(8,128)S(1)} %hop.11.l0_ref, bf16[1024,512]{1,0:T(8,128)(2,1)} %get-tuple-element.399.k_ref, ...), custom_call_target="tpu_custom_call" | custom-call | flops 1677721600 | bytes 13107200 | tf_op jit(solution)/shard_map/last/pallas_call | solution.py:62
  384.6 2.7 collective-permute-done.29.refs_1_
  387.4 3.0 join.30
  391.3 4.9 collective-permute-start.31
  398.1 8.1 %last.7 = (bf16[256,512]{1,0:T(8,128)(2,1)}, bf16[256,512]{1,0:T(8,128)(2,1)}, bf16[256,64]{1,0:T(8,128)(2,1)}, bf16[256,2048]{1,0:T(8,128)(2,1)S(1)}, f32[8,64]{1,0:T(8,128)}, /*index=5*/f32[8,2048]{1,0:T(8,128)}) custom-call(f32[4,64,1024]{2,1,0:T(8,128)S(1)} %hop.11.l0_ref, bf16[1024,512]{1,0:T(8,128)(2,1)} %get-tuple-element.399.k_ref, ...), custom_call_target="tpu_custom_call" | custom-call | flops 1677721600 | bytes 13107200 | tf_op jit(solution)/shard_map/last/pallas_call | solution.py:62
  406.2 10.0 %state_grads.1 = bf16[8,272,1152]{2,1,0:T(8,128)(2,1)} custom-call(bf16[1024,2048]{1,0:T(8,128)(2,1)} %get-tuple-element.715.xn_ref.refs_0_, bf16[256,512]{1,0:T(8,128)(2,1)} %get-tuple-element.716.refs_1_, bf16[256,512]{1,0:T(8,128)(2,1)} %get-tuple-element.717.refs_2_, bf16[256,512]{1,0:T(8,128)(2,1)} %get-tuple-element.718.refs_3_, ...), custom_call_target="tpu_custom_call" | custom-call | flops 4294967296 | bytes 10485760 | tf_op jit(solution)/shard_map/state_grads/pallas_call | solution.py:62
  418.0 2.4 join.31
  423.3 3.8 collective-permute-start.33
  430.0 2.3 out.5.refs_0_
  432.2 15.5 %collective-permute-done.33.refs_1_ = bf16[256,2048]{1,0:T(8,128)(2,1)S(1)} collective-permute-done((bf16[256,2048]{1,0:T(8,128)(2,1)}, bf16[256,2048]{1,0:T(8,128)(2,1)S(1)}, u32[]{:S(2)}, u32[]{:S(2)}) %collective-permute-start.33) | collective-permute-done | bytes 1048608 | tf_op jit(solution)/shard_map/ppermute | solution.py:601
  449.9 3.9 collective-permute-start.35
  455.9 3.3 in_grad.4.refs_0_
  459.2 2.3 out.6.refs_0_
  461.5 2.2 out.7
  463.7 9.8 %collective-permute-done.35.refs_1_ = bf16[256,2048]{1,0:T(8,128)(2,1)S(1)} collective-permute-done((bf16[256,2048]{1,0:T(8,128)(2,1)}, bf16[256,2048]{1,0:T(8,128)(2,1)S(1)}, u32[]{:S(2)}, u32[]{:S(2)}) %collective-permute-start.35) | collective-permute-done | bytes 1048608 | tf_op jit(solution)/shard_map/ppermute | solution.py:601
  480.9 3.0 copy.48
  485.1 3.3 in_grad.5.refs_0_
  488.5 11.1 %collective-permute-done.37.refs_0_ = bf16[256,2048]{1,0:T(8,128)(2,1)S(1)} collective-permute-done((bf16[256,2048]{1,0:T(8,128)(2,1)}, bf16[256,2048]{1,0:T(8,128)(2,1)S(1)}, u32[]{:S(2)}, u32[]{:S(2)}) %collective-permute-start.37) | collective-permute-done | bytes 1048608 | tf_op jit(solution)/shard_map/ppermute | solution.py:601
  503.1 2.2 slice_convert_fusion
  508.8 3.6 collective-permute-start.41
  517.1 3.2 in_grad.6.refs_0_
  520.3 4.3 collective-permute-done.40
  525.2 3.2 in_grad.7
  (205 shorter events, 80.4 us)
Async XLA Ops:
  7.2 125.6 %all-gather.3.cloned.1.call-start = ((), (), s32[]{:S(2)}) async-start(), calls=%async_computation.6 | async-start | bytes 19464192 | tf_op jit(solution)/shard_map/all_gather | solution.py:686
  7.2 16.6 %copy-start.49 = (bf16[1408,256]{1,0:T(8,128)(2,1)S(1)}, bf16[1408,256]{1,0:T(8,128)(2,1)}, u32[]{:S(2)}) copy-start(bf16[1408,256]{1,0:T(8,128)(2,1)} %param.24) | copy-start | bytes 2162692
  7.2 16.9 %copy-start.50 = (bf16[256,1408]{1,0:T(8,128)(2,1)S(1)}, bf16[256,1408]{1,0:T(8,128)(2,1)}, u32[]{:S(2)}) copy-start(bf16[256,1408]{1,0:T(8,128)(2,1)} %param.23) | copy-start | bytes 2162692
  22.1 1.7 collective-permute-start
  26.9 336.4 %reduce-scatter.4.cloned.1.call-start = ((), (), s32[]{:S(2)}) async-start(), calls=%async_computation.3 | async-start | bytes 12976128 | tf_op jit(solution)/shard_map/reduce_scatter | solution.py:902
  27.2 10.2 %collective-permute-start.1 = (bf16[2,64,1152]{2,1,0:T(8,128)(2,1)S(1)}, bf16[2,64,1152]{2,1,0:T(8,128)(2,1)S(1)}, u32[]{:S(2)}, u32[]{:S(2)}) collective-permute-start(bf16[2,64,1152]{2,1,0:T(8,128)(2,1)S(1)} %get-tuple-element.408), channel_id=1, source_target_pairs={{0,8},{4,12},{8,0},{12,4},{16,24},{20,28},{24,16},{28,20},{1,9},{5... | collective-permute-start | bytes 884744 | tf_op jit(solution)/shard_map/ppermute | solution.py:521
  37.7 14.3 %collective-permute-start.2 = (bf16[2,64,1152]{2,1,0:T(8,128)(2,1)S(1)}, bf16[2,64,1152]{2,1,0:T(8,128)(2,1)S(1)}, u32[]{:S(2)}, u32[]{:S(2)}) collective-permute-start(bf16[2,64,1152]{2,1,0:T(8,128)(2,1)S(1)} %get-tuple-element.413), channel_id=1, source_target_pairs={{0,16},{4,20},{8,24},{12,28},{16,0},{20,4},{24,8},{28,12},{1,17},{... | collective-permute-start | bytes 884744 | tf_op jit(solution)/shard_map/ppermute | solution.py:521
  57.6 22.7 %collective-permute-start.3 = (bf16[256,2048]{1,0:T(8,128)(2,1)S(1)}, bf16[256,2048]{1,0:T(8,128)(2,1)S(1)}, u32[]{:S(2)}, u32[]{:S(2)}) collective-permute-start(bf16[256,2048]{1,0:T(8,128)(2,1)S(1)} %get-tuple-element.420.refs_0_), channel_id=1, source_target_pairs={{0,1},{3,2},{4,5},{7,6},{8,9},{11,10},{12,13},{15,14},{16,17},{19,... | collective-permute-start | bytes 3145736 | tf_op jit(solution)/shard_map/ppermute | solution.py:601
  80.4 23.0 %collective-permute-start.4 = (bf16[256,2048]{1,0:T(8,128)(2,1)S(1)}, bf16[256,2048]{1,0:T(8,128)(2,1)S(1)}, u32[]{:S(2)}, u32[]{:S(2)}) collective-permute-start(bf16[256,2048]{1,0:T(8,128)(2,1)S(1)} %get-tuple-element.424), channel_id=1, source_target_pairs={{0,1},{3,2},{4,5},{7,6},{8,9},{11,10},{12,13},{15,14},{16,17},{19,... | collective-permute-start | bytes 3145736 | tf_op jit(solution)/shard_map/ppermute | solution.py:601
  84.9 18.5 %collective-permute-start.5 = (bf16[256,2048]{1,0:T(8,128)(2,1)S(1)}, bf16[256,2048]{1,0:T(8,128)(2,1)S(1)}, u32[]{:S(2)}, u32[]{:S(2)}) collective-permute-start(bf16[256,2048]{1,0:T(8,128)(2,1)S(1)} %get-tuple-element.425.refs_2_), channel_id=1, source_target_pairs={{1,2},{2,1},{5,6},{6,5},{9,10},{10,9},{13,14},{14,13},{17,18},{18,... | collective-permute-start | bytes 3145736 | tf_op jit(solution)/shard_map/ppermute | solution.py:604
  103.5 22.1 %collective-permute-start.6 = (bf16[256,2048]{1,0:T(8,128)(2,1)S(1)}, bf16[256,2048]{1,0:T(8,128)(2,1)S(1)}, u32[]{:S(2)}, u32[]{:S(2)}) collective-permute-start(bf16[256,2048]{1,0:T(8,128)(2,1)S(1)} %get-tuple-element.433.refs_4_), channel_id=1, source_target_pairs={{0,1},{3,2},{1,0},{2,3},{4,5},{7,6},{5,4},{6,7},{8,9},{11,10},{9,8... | collective-permute-start | bytes 3145736 | tf_op jit(solution)/shard_map/ppermute | solution.py:601
  107.4 18.1 %collective-permute-start.7 = (bf16[256,2048]{1,0:T(8,128)(2,1)S(1)}, bf16[256,2048]{1,0:T(8,128)(2,1)S(1)}, u32[]{:S(2)}, u32[]{:S(2)}) collective-permute-start(bf16[256,2048]{1,0:T(8,128)(2,1)S(1)} %get-tuple-element.434.refs_2_), channel_id=1, source_target_pairs={{1,2},{2,1},{5,6},{6,5},{9,10},{10,9},{13,14},{14,13},{17,18},{18,... | collective-permute-start | bytes 3145736 | tf_op jit(solution)/shard_map/ppermute | solution.py:604
  125.6 7.2 %copy-start.38 = (f32[2048]{0:T(1024)S(1)}, f32[2048]{0:T(1024)}, u32[]{:S(2)}) copy-start(f32[2048]{0:T(1024)} %param.21) | copy-start | bytes 24580
  126.8 26.7 %collective-permute-start.8 = (bf16[256,2048]{1,0:T(8,128)(2,1)S(1)}, bf16[256,2048]{1,0:T(8,128)(2,1)}, u32[]{:S(2)}, u32[]{:S(2)}) collective-permute-start(bf16[256,2048]{1,0:T(8,128)(2,1)S(1)} %get-tuple-element.438.refs_4_), channel_id=1, source_target_pairs={{0,1},{3,2},{1,0},{2,3},{4,5},{7,6},{5,4},{6,7},{8,9},{11,10},{9,8... | collective-permute-start | bytes 3145736 | tf_op jit(solution)/shard_map/ppermute | solution.py:601
  130.7 22.8 %collective-permute-start.9 = (bf16[256,2048]{1,0:T(8,128)(2,1)S(1)}, bf16[256,2048]{1,0:T(8,128)(2,1)}, u32[]{:S(2)}, u32[]{:S(2)}) collective-permute-start(bf16[256,2048]{1,0:T(8,128)(2,1)S(1)} %get-tuple-element.439.refs_2_), channel_id=1, source_target_pairs={{1,2},{2,1},{5,6},{6,5},{9,10},{10,9},{13,14},{14,13},{17,18},{18,... | collective-permute-start | bytes 3145736 | tf_op jit(solution)/shard_map/ppermute | solution.py:604
  155.2 22.7 %collective-permute-start.10 = (bf16[256,2048]{1,0:T(8,128)(2,1)S(1)}, bf16[256,2048]{1,0:T(8,128)(2,1)S(1)}, u32[]{:S(2)}, u32[]{:S(2)}) collective-permute-start(bf16[256,2048]{1,0:T(8,128)(2,1)S(1)} %get-tuple-element.455.refs_4_), channel_id=1, source_target_pairs={{0,1},{3,2},{1,0},{2,3},{4,5},{7,6},{5,4},{6,7},{8,9},{11,10},{9,8... | collective-permute-start | bytes 3145736 | tf_op jit(solution)/shard_map/ppermute | solution.py:601
  157.5 20.4 %collective-permute-start.11 = (bf16[256,2048]{1,0:T(8,128)(2,1)S(1)}, bf16[256,2048]{1,0:T(8,128)(2,1)S(1)}, u32[]{:S(2)}, u32[]{:S(2)}) collective-permute-start(bf16[256,2048]{1,0:T(8,128)(2,1)S(1)} %get-tuple-element.456.refs_2_), channel_id=1, source_target_pairs={{1,2},{2,1},{5,6},{6,5},{9,10},{10,9},{13,14},{14,13},{17,18},{18,... | collective-permute-start | bytes 3145736 | tf_op jit(solution)/shard_map/ppermute | solution.py:604
  178.1 23.4 %collective-permute-start.12 = (bf16[256,2048]{1,0:T(8,128)(2,1)S(1)}, bf16[256,2048]{1,0:T(8,128)(2,1)S(1)}, u32[]{:S(2)}, u32[]{:S(2)}) collective-permute-start(bf16[256,2048]{1,0:T(8,128)(2,1)S(1)} %get-tuple-element.472.refs_4_), channel_id=1, source_target_pairs={{0,1},{3,2},{1,0},{2,3},{4,5},{7,6},{5,4},{6,7},{8,9},{11,10},{9,8... | collective-permute-start | bytes 3145736 | tf_op jit(solution)/shard_map/ppermute | solution.py:601
  181.1 20.4 %collective-permute-start.13 = (bf16[256,2048]{1,0:T(8,128)(2,1)S(1)}, bf16[256,2048]{1,0:T(8,128)(2,1)S(1)}, u32[]{:S(2)}, u32[]{:S(2)}) collective-permute-start(bf16[256,2048]{1,0:T(8,128)(2,1)S(1)} %get-tuple-element.473.refs_2_), channel_id=1, source_target_pairs={{1,2},{2,1},{5,6},{6,5},{9,10},{10,9},{13,14},{14,13},{17,18},{18,... | collective-permute-start | bytes 3145736 | tf_op jit(solution)/shard_map/ppermute | solution.py:604
  201.7 22.9 %collective-permute-start.14 = (bf16[256,2048]{1,0:T(8,128)(2,1)S(1)}, bf16[256,2048]{1,0:T(8,128)(2,1)S(1)}, u32[]{:S(2)}, u32[]{:S(2)}) collective-permute-start(bf16[256,2048]{1,0:T(8,128)(2,1)S(1)} %get-tuple-element.499.refs_4_), channel_id=1, source_target_pairs={{0,1},{3,2},{1,0},{2,3},{4,5},{7,6},{5,4},{6,7},{8,9},{11,10},{9,8... | collective-permute-start | bytes 3145736 | tf_op jit(solution)/shard_map/ppermute | solution.py:601
  204.0 20.6 %collective-permute-start.15 = (bf16[256,2048]{1,0:T(8,128)(2,1)S(1)}, bf16[256,2048]{1,0:T(8,128)(2,1)S(1)}, u32[]{:S(2)}, u32[]{:S(2)}) collective-permute-start(bf16[256,2048]{1,0:T(8,128)(2,1)S(1)} %get-tuple-element.500.refs_2_), channel_id=1, source_target_pairs={{1,2},{2,1},{5,6},{6,5},{9,10},{10,9},{13,14},{14,13},{17,18},{18,... | collective-permute-start | bytes 3145736 | tf_op jit(solution)/shard_map/ppermute | solution.py:604
  226.1 23.3 %copy-start.3 = (bf16[256,2048]{1,0:T(8,128)(2,1)S(1)}, bf16[256,2048]{1,0:T(8,128)(2,1)}, u32[]{:S(2)}) copy-start(bf16[256,2048]{1,0:T(8,128)(2,1)} %get-tuple-element.530.refs_5_.refs_0_) | copy-start | bytes 3145732
  226.1 23.3 %collective-permute-start.16 = (bf16[256,2048]{1,0:T(8,128)(2,1)}, bf16[256,2048]{1,0:T(8,128)(2,1)}, u32[]{:S(2)}, u32[]{:S(2)}) collective-permute-start(bf16[256,2048]{1,0:T(8,128)(2,1)} %get-tuple-element.528.refs_4_), channel_id=1, source_target_pairs={{0,1},{3,2},{1,0},{2,3},{4,5},{7,6},{5,4},{6,7},{8,9},{11,10},{9,8... | collective-permute-start | bytes 3145736 | tf_op jit(solution)/shard_map/ppermute | solution.py:601
  228.7 20.7 %collective-permute-start.17 = (bf16[256,2048]{1,0:T(8,128)(2,1)}, bf16[256,2048]{1,0:T(8,128)(2,1)}, u32[]{:S(2)}, u32[]{:S(2)}) collective-permute-start(bf16[256,2048]{1,0:T(8,128)(2,1)} %get-tuple-element.529.refs_2_), channel_id=1, source_target_pairs={{1,2},{2,1},{5,6},{6,5},{9,10},{10,9},{13,14},{14,13},{17,18},{18,... | collective-permute-start | bytes 3145736 | tf_op jit(solution)/shard_map/ppermute | solution.py:604
  254.8 195.1 %reduce-scatter.6.cloned.1.call-start = ((), (), s32[]{:S(2)}) async-start(), calls=%async_computation.4 | async-start | bytes 11206656 | tf_op jit(solution)/shard_map/reduce_scatter | solution.py:956
  254.8 20.4 %collective-permute-start.18 = (bf16[256,2048]{1,0:T(8,128)(2,1)}, bf16[256,2048]{1,0:T(8,128)(2,1)S(1)}, u32[]{:S(2)}, u32[]{:S(2)}) collective-permute-start(bf16[256,2048]{1,0:T(8,128)(2,1)} %copy-done.24), channel_id=1, source_target_pairs={{0,1},{3,2},{1,0},{2,3},{4,5},{7,6},{5,4},{6,7},{8,9},{11,10},{9,8... | collective-permute-start | bytes 3145736 | tf_op jit(solution)/shard_map/ppermute | solution.py:601
  256.3 18.9 %collective-permute-start.19 = (bf16[256,2048]{1,0:T(8,128)(2,1)S(1)}, bf16[256,2048]{1,0:T(8,128)(2,1)S(1)}, u32[]{:S(2)}, u32[]{:S(2)}) collective-permute-start(bf16[256,2048]{1,0:T(8,128)(2,1)S(1)} %copy-done.23), channel_id=1, source_target_pairs={{1,2},{2,1},{5,6},{6,5},{9,10},{10,9},{13,14},{14,13},{17,18},{18,... | collective-permute-start | bytes 3145736 | tf_op jit(solution)/shard_map/ppermute | solution.py:604
  257.2 8.4 %copy-start.15 = (bf16[256,2048]{1,0:T(8,128)(2,1)S(1)}, bf16[256,2048]{1,0:T(8,128)(2,1)}, u32[]{:S(2)}) copy-start(bf16[256,2048]{1,0:T(8,128)(2,1)} %copy-done.14) | copy-start | bytes 3145732
  265.7 9.6 %copy-start.2 = (bf16[256,2048]{1,0:T(8,128)(2,1)S(1)}, bf16[256,2048]{1,0:T(8,128)(2,1)}, u32[]{:S(2)}) copy-start(bf16[256,2048]{1,0:T(8,128)(2,1)} %get-tuple-element.558.refs_5_.refs_0_) | copy-start | bytes 3145732
  265.7 9.6 %copy-start.25 = (bf16[256,2048]{1,0:T(8,128)(2,1)S(1)}, bf16[256,2048]{1,0:T(8,128)(2,1)}, u32[]{:S(2)}) copy-start(bf16[256,2048]{1,0:T(8,128)(2,1)} %copy-done.24) | copy-start | bytes 3145732
  275.5 23.6 %collective-permute-start.20 = (bf16[256,2048]{1,0:T(8,128)(2,1)S(1)}, bf16[256,2048]{1,0:T(8,128)(2,1)S(1)}, u32[]{:S(2)}, u32[]{:S(2)}) collective-permute-start(bf16[256,2048]{1,0:T(8,128)(2,1)S(1)} %get-tuple-element.584.refs_4_), channel_id=1, source_target_pairs={{0,1},{3,2},{1,0},{2,3},{4,5},{7,6},{5,4},{6,7},{8,9},{11,10},{9,8... | collective-permute-start | bytes 3145736 | tf_op jit(solution)/shard_map/ppermute | solution.py:601
  279.4 19.7 %collective-permute-start.21 = (bf16[256,2048]{1,0:T(8,128)(2,1)S(1)}, bf16[256,2048]{1,0:T(8,128)(2,1)S(1)}, u32[]{:S(2)}, u32[]{:S(2)}) collective-permute-start(bf16[256,2048]{1,0:T(8,128)(2,1)S(1)} %get-tuple-element.585.refs_2_), channel_id=1, source_target_pairs={{1,2},{2,1},{5,6},{6,5},{9,10},{10,9},{13,14},{14,13},{17,18},{18,... | collective-permute-start | bytes 3145736 | tf_op jit(solution)/shard_map/ppermute | solution.py:604
  288.3 10.8 %copy-start.1 = (bf16[256,2048]{1,0:T(8,128)(2,1)S(1)}, bf16[256,2048]{1,0:T(8,128)(2,1)}, u32[]{:S(2)}) copy-start(bf16[256,2048]{1,0:T(8,128)(2,1)} %get-tuple-element.586.refs_5_.refs_0_) | copy-start | bytes 3145732
  299.3 19.8 %collective-permute-start.23 = (bf16[256,2048]{1,0:T(8,128)(2,1)S(1)}, bf16[256,2048]{1,0:T(8,128)(2,1)S(1)}, u32[]{:S(2)}, u32[]{:S(2)}) collective-permute-start(bf16[256,2048]{1,0:T(8,128)(2,1)S(1)} %get-tuple-element.617.refs_4_), channel_id=1, source_target_pairs={{0,1},{3,2},{1,0},{2,3},{4,5},{7,6},{5,4},{6,7},{8,9},{11,10},{9,8... | collective-permute-start | bytes 3145736 | tf_op jit(solution)/shard_map/ppermute | solution.py:601
  303.3 15.7 %collective-permute-start.24 = (bf16[256,2048]{1,0:T(8,128)(2,1)S(1)}, bf16[256,2048]{1,0:T(8,128)(2,1)S(1)}, u32[]{:S(2)}, u32[]{:S(2)}) collective-permute-start(bf16[256,2048]{1,0:T(8,128)(2,1)S(1)} %get-tuple-element.618.refs_2_), channel_id=1, source_target_pairs={{1,2},{2,1},{5,6},{6,5},{9,10},{10,9},{13,14},{14,13},{17,18},{18,... | collective-permute-start | bytes 3145736 | tf_op jit(solution)/shard_map/ppermute | solution.py:604
  312.6 1.6 collective-permute-start.22
  316.4 20.1 %collective-permute-start.27 = (bf16[2,64,1152]{2,1,0:T(8,128)(2,1)}, bf16[2,64,1152]{2,1,0:T(8,128)(2,1)S(1)}, u32[]{:S(2)}, u32[]{:S(2)}) collective-permute-start(bf16[2,64,1152]{2,1,0:T(8,128)(2,1)} %get-tuple-element.648), channel_id=1, source_target_pairs={{0,8},{4,12},{8,0},{12,4},{16,24},{20,28},{24,16},{28,20},{1,9},{5... | collective-permute-start | bytes 884744 | tf_op jit(solution)/shard_map/ppermute | solution.py:521
  321.6 36.1 %collective-permute-start.25 = (bf16[256,2048]{1,0:T(8,128)(2,1)}, bf16[256,2048]{1,0:T(8,128)(2,1)}, u32[]{:S(2)}, u32[]{:S(2)}) collective-permute-start(bf16[256,2048]{1,0:T(8,128)(2,1)} %get-tuple-element.626.refs_4_), channel_id=1, source_target_pairs={{0,1},{3,2},{1,0},{2,3},{4,5},{7,6},{5,4},{6,7},{8,9},{11,10},{9,8... | collective-permute-start | bytes 3145736 | tf_op jit(solution)/shard_map/ppermute | solution.py:601
  325.4 32.3 %collective-permute-start.26 = (bf16[256,2048]{1,0:T(8,128)(2,1)}, bf16[256,2048]{1,0:T(8,128)(2,1)}, u32[]{:S(2)}, u32[]{:S(2)}) collective-permute-start(bf16[256,2048]{1,0:T(8,128)(2,1)} %get-tuple-element.627.refs_2_), channel_id=1, source_target_pairs={{1,2},{2,1},{5,6},{6,5},{9,10},{10,9},{13,14},{14,13},{17,18},{18,... | collective-permute-start | bytes 3145736 | tf_op jit(solution)/shard_map/ppermute | solution.py:604
  338.5 10.0 %collective-permute-start.28 = (bf16[2,64,1152]{2,1,0:T(8,128)(2,1)S(1)}, bf16[2,64,1152]{2,1,0:T(8,128)(2,1)S(1)}, u32[]{:S(2)}, u32[]{:S(2)}) collective-permute-start(bf16[2,64,1152]{2,1,0:T(8,128)(2,1)S(1)} %get-tuple-element.653), channel_id=1, source_target_pairs={{0,16},{4,20},{8,24},{12,28},{16,0},{20,4},{24,8},{28,12},{1,17},{... | collective-permute-start | bytes 884744 | tf_op jit(solution)/shard_map/ppermute | solution.py:521
  363.4 141.9 %reduce-scatter.8.cloned.1.call-start = ((), (), s32[]{:S(2)}) async-start(), calls=%async_computation.5 | async-start | bytes 5640192 | tf_op jit(solution)/shard_map/reduce_scatter | solution.py:976
  363.4 24.0 %collective-permute-start.29 = (bf16[256,2048]{1,0:T(8,128)(2,1)}, bf16[256,2048]{1,0:T(8,128)(2,1)S(1)}, u32[]{:S(2)}, u32[]{:S(2)}) collective-permute-start(bf16[256,2048]{1,0:T(8,128)(2,1)} %get-tuple-element.679.refs_4_), channel_id=1, source_target_pairs={{0,1},{3,2},{1,0},{2,3},{4,5},{7,6},{5,4},{6,7},{8,9},{11,10},{9,8... | collective-permute-start | bytes 3145736 | tf_op jit(solution)/shard_map/ppermute | solution.py:601
  365.1 22.3 %collective-permute-start.30 = (bf16[256,2048]{1,0:T(8,128)(2,1)}, bf16[256,2048]{1,0:T(8,128)(2,1)S(1)}, u32[]{:S(2)}, u32[]{:S(2)}) collective-permute-start(bf16[256,2048]{1,0:T(8,128)(2,1)} %get-tuple-element.680.refs_2_), channel_id=1, source_target_pairs={{1,2},{2,1},{5,6},{6,5},{9,10},{10,9},{13,14},{14,13},{17,18},{18,... | collective-permute-start | bytes 3145736 | tf_op jit(solution)/shard_map/ppermute | solution.py:604
  374.8 12.6 %copy-start.7 = (bf16[256,2048]{1,0:T(8,128)(2,1)S(1)}, bf16[256,2048]{1,0:T(8,128)(2,1)}, u32[]{:S(2)}) copy-start(bf16[256,2048]{1,0:T(8,128)(2,1)} %copy-done.6) | copy-start | bytes 3145732
  391.3 26.6 %collective-permute-start.31 = (bf16[256,2048]{1,0:T(8,128)(2,1)}, bf16[256,2048]{1,0:T(8,128)(2,1)}, u32[]{:S(2)}, u32[]{:S(2)}) collective-permute-start(bf16[256,2048]{1,0:T(8,128)(2,1)} %get-tuple-element.696.refs_4_), channel_id=1, source_target_pairs={{0,1},{3,2},{1,0},{2,3},{4,5},{7,6},{5,4},{6,7},{8,9},{11,10},{9,8... | collective-permute-start | bytes 3145736 | tf_op jit(solution)/shard_map/ppermute | solution.py:601
  396.2 21.7 %collective-permute-start.32 = (bf16[256,2048]{1,0:T(8,128)(2,1)}, bf16[256,2048]{1,0:T(8,128)(2,1)}, u32[]{:S(2)}, u32[]{:S(2)}) collective-permute-start(bf16[256,2048]{1,0:T(8,128)(2,1)} %get-tuple-element.697.refs_2_), channel_id=1, source_target_pairs={{1,2},{2,1},{5,6},{6,5},{9,10},{10,9},{13,14},{14,13},{17,18},{18,... | collective-permute-start | bytes 3145736 | tf_op jit(solution)/shard_map/ppermute | solution.py:604
  406.2 11.8 %copy-start.5 = (bf16[256,2048]{1,0:T(8,128)(2,1)S(1)}, bf16[256,2048]{1,0:T(8,128)(2,1)}, u32[]{:S(2)}) copy-start(bf16[256,2048]{1,0:T(8,128)(2,1)} %copy-done.4) | copy-start | bytes 3145732
  423.3 24.5 %collective-permute-start.33 = (bf16[256,2048]{1,0:T(8,128)(2,1)}, bf16[256,2048]{1,0:T(8,128)(2,1)S(1)}, u32[]{:S(2)}, u32[]{:S(2)}) collective-permute-start(bf16[256,2048]{1,0:T(8,128)(2,1)} %copy-done.28), channel_id=1, source_target_pairs={{0,1},{3,2},{1,0},{2,3},{4,5},{7,6},{5,4},{6,7},{8,9},{11,10},{9,8... | collective-permute-start | bytes 3145736 | tf_op jit(solution)/shard_map/ppermute | solution.py:601
  427.1 20.7 %collective-permute-start.34 = (bf16[256,2048]{1,0:T(8,128)(2,1)}, bf16[256,2048]{1,0:T(8,128)(2,1)S(1)}, u32[]{:S(2)}, u32[]{:S(2)}) collective-permute-start(bf16[256,2048]{1,0:T(8,128)(2,1)} %copy-done.26), channel_id=1, source_target_pairs={{1,2},{2,1},{5,6},{6,5},{9,10},{10,9},{13,14},{14,13},{17,18},{18,... | collective-permute-start | bytes 3145736 | tf_op jit(solution)/shard_map/ppermute | solution.py:604
  429.9 17.8 %copy-start.27 = (bf16[256,2048]{1,0:T(8,128)(2,1)S(1)}, bf16[256,2048]{1,0:T(8,128)(2,1)}, u32[]{:S(2)}) copy-start(bf16[256,2048]{1,0:T(8,128)(2,1)} %copy-done.26) | copy-start | bytes 3145732
  429.9 17.8 %copy-start.29 = (bf16[256,2048]{1,0:T(8,128)(2,1)S(1)}, bf16[256,2048]{1,0:T(8,128)(2,1)}, u32[]{:S(2)}) copy-start(bf16[256,2048]{1,0:T(8,128)(2,1)} %copy-done.28) | copy-start | bytes 3145732
  449.9 9.3 %copy-start.11 = (bf16[256,2048]{1,0:T(8,128)(2,1)S(1)}, bf16[256,2048]{1,0:T(8,128)(2,1)}, u32[]{:S(2)}) copy-start(bf16[256,2048]{1,0:T(8,128)(2,1)} %copy-done.10) | copy-start | bytes 3145732
  449.9 23.6 %collective-permute-start.35 = (bf16[256,2048]{1,0:T(8,128)(2,1)}, bf16[256,2048]{1,0:T(8,128)(2,1)S(1)}, u32[]{:S(2)}, u32[]{:S(2)}) collective-permute-start(bf16[256,2048]{1,0:T(8,128)(2,1)} %copy-done.16), channel_id=1, source_target_pairs={{0,1},{3,2},{1,0},{2,3},{4,5},{7,6},{5,4},{6,7},{8,9},{11,10},{9,8... | collective-permute-start | bytes 3145736 | tf_op jit(solution)/shard_map/ppermute | solution.py:601
  453.8 19.7 %collective-permute-start.36 = (bf16[256,2048]{1,0:T(8,128)(2,1)S(1)}, bf16[256,2048]{1,0:T(8,128)(2,1)S(1)}, u32[]{:S(2)}, u32[]{:S(2)}) collective-permute-start(bf16[256,2048]{1,0:T(8,128)(2,1)S(1)} %get-tuple-element.757.refs_2_), channel_id=1, source_target_pairs={{1,2},{2,1},{5,6},{6,5},{9,10},{10,9},{13,14},{14,13},{17,18},{18,... | collective-permute-start | bytes 3145736 | tf_op jit(solution)/shard_map/ppermute | solution.py:604
  461.5 12.0 %copy-start.17 = (bf16[256,2048]{1,0:T(8,128)(2,1)S(1)}, bf16[256,2048]{1,0:T(8,128)(2,1)}, u32[]{:S(2)}) copy-start(bf16[256,2048]{1,0:T(8,128)(2,1)} %copy-done.16) | copy-start | bytes 3145732
  463.7 14.2 %copy-start.47 = (bf16[1,2,256,1408]{3,2,1,0:T(8,128)(2,1)S(1)}, bf16[1,2,256,1408]{3,2,1,0:T(8,128)(2,1)}, u32[]{:S(2)}) copy-start(bf16[1,2,256,1408]{3,2,1,0:T(8,128)(2,1)} %reduce-scatter.4.cloned.1.call-done) | copy-start | bytes 4325380
  475.6 23.9 %collective-permute-start.37 = (bf16[256,2048]{1,0:T(8,128)(2,1)}, bf16[256,2048]{1,0:T(8,128)(2,1)S(1)}, u32[]{:S(2)}, u32[]{:S(2)}) collective-permute-start(bf16[256,2048]{1,0:T(8,128)(2,1)} %get-tuple-element.767.refs_3_), channel_id=1, source_target_pairs={{1,0},{2,3},{5,4},{6,7},{9,8},{10,11},{13,12},{14,15},{17,16},{18,... | collective-permute-start | bytes 3145736 | tf_op jit(solution)/shard_map/ppermute | solution.py:601
  477.2 22.3 %collective-permute-start.38 = (bf16[256,2048]{1,0:T(8,128)(2,1)S(1)}, bf16[256,2048]{1,0:T(8,128)(2,1)S(1)}, u32[]{:S(2)}, u32[]{:S(2)}) collective-permute-start(bf16[256,2048]{1,0:T(8,128)(2,1)S(1)} %get-tuple-element.768.refs_1_), channel_id=1, source_target_pairs={{1,2},{2,1},{5,6},{6,5},{9,10},{10,9},{13,14},{14,13},{17,18},{18,... | collective-permute-start | bytes 3145736 | tf_op jit(solution)/shard_map/ppermute | solution.py:604
  485.1 14.4 %copy-start.31 = (bf16[256,2048]{1,0:T(8,128)(2,1)S(1)}, bf16[256,2048]{1,0:T(8,128)(2,1)}, u32[]{:S(2)}) copy-start(bf16[256,2048]{1,0:T(8,128)(2,1)} %copy-done.30) | copy-start | bytes 3145732
  501.8 23.3 %collective-permute-start.39 = (bf16[256,2048]{1,0:T(8,128)(2,1)S(1)}, bf16[256,2048]{1,0:T(8,128)(2,1)S(1)}, u32[]{:S(2)}, u32[]{:S(2)}) collective-permute-start(bf16[256,2048]{1,0:T(8,128)(2,1)S(1)} %get-tuple-element.775.refs_1_), channel_id=1, source_target_pairs={{1,0},{2,3},{5,4},{6,7},{9,8},{10,11},{13,12},{14,15},{17,16},{18,... | collective-permute-start | bytes 3145736 | tf_op jit(solution)/shard_map/ppermute | solution.py:601
  507.3 9.8 %copy-start.33 = (bf16[256,2048]{1,0:T(8,128)(2,1)S(1)}, bf16[256,2048]{1,0:T(8,128)(2,1)}, u32[]{:S(2)}) copy-start(bf16[256,2048]{1,0:T(8,128)(2,1)} %copy-done.32) | copy-start | bytes 3145732
  507.3 13.0 %collective-permute-start.42 = (f32[256]{0:T(256)S(1)}, f32[256]{0:T(256)S(1)}, u32[]{:S(2)}, u32[]{:S(2)}) collective-permute-start(f32[256]{0:T(256)S(1)} %get-tuple-element.823), channel_id=1, source_target_pairs={{0,3},{1,2},{2,1},{3,0},{4,7},{5,6},{6,5},{7,4},{8,11},{9,10},{10,... | collective-permute-start | bytes 3080 | tf_op jit(solution)/shard_map/ppermute | solution.py:997
  508.8 11.5 %collective-permute-start.41 = (f32[256]{0:T(256)S(1)}, f32[256]{0:T(256)S(1)}, u32[]{:S(2)}, u32[]{:S(2)}) collective-permute-start(f32[256]{0:T(256)S(1)} %get-tuple-element.823), channel_id=1, source_target_pairs={{0,2},{1,3},{2,0},{3,1},{4,6},{5,7},{6,4},{7,5},{8,10},{9,11},{10,... | collective-permute-start | bytes 3080 | tf_op jit(solution)/shard_map/ppermute | solution.py:997
  512.5 12.1 %collective-permute-start.40 = (f32[256]{0:T(256)S(1)}, f32[256]{0:T(256)S(1)}, u32[]{:S(2)}, u32[]{:S(2)}) collective-permute-start(f32[256]{0:T(256)S(1)} %get-tuple-element.823), channel_id=1, source_target_pairs={{0,1},{1,0},{2,3},{3,2},{4,5},{5,4},{6,7},{7,6},{8,9},{9,8},{10,11... | collective-permute-start | bytes 3080 | tf_op jit(solution)/shard_map/ppermute | solution.py:997
  (34 other events, 74.2 us)
Sparse Core Ops, SparseCore 0:
  27.0 100.2 all-gather.2
  254.9 89.8 reduce-scatter.3
  363.5 78.8 reduce-scatter.5
  445.7 55.7 reduce-scatter.7

commit v12 on v9

--- a/solution.py
+++ b/solution.py
@@ -934,11 +934,12 @@
         grads = call(
             "query_grads",
             functools.partial(query_grad_kernel, len(every), units),
-            (width // columns,),
-            xn_columns + piece_columns + piece_whole * 2 + [anywhere],
+            (width // columns // 2,),
+            [pl.BlockSpec((rows, 2 * columns), lambda j: (0, j))]
+            + [pl.BlockSpec((TILE, 2 * columns), lambda j: (0, j))] * len(every) + piece_whole * 2 + [anywhere],
             anywhere,
             shaped((n_seq, span, units + 2 * head), bf16),
-            [pltpu.VMEM((2, group, span, 2 * head), bf16), pltpu.SemaphoreType.DMA((2,))],
+            [pltpu.VMEM((2, 2 * group, span, 2 * head), bf16), pltpu.SemaphoreType.DMA((2,))],
             cost=cost(12 * rows * width * head, 3 * (4 * rows * width + 4 * rows * head + 4 * width * head)),
             aliases={1 + 3 * len(every): 0},
         )(behind_of(made[0], state), *[backs[key][0] for key in every], *[backs[key][1] for key in every],

time: 540 us -> 543 us (level)
  the two profiles are of different devices: /device:TPU:4 before, /device:TPU:0 now
where the time goes in v12:
time: 543 us; the launch traced here: 536 us
  Pallas kernels  285 us (52%)
  waiting for transfers between devices  106 us (20%)
  starting transfers between devices  88.8 us (16%)
  local copies, waits for them, and re-layouts  30.5 us (6%)
  between operations  14.8 us (3%)
  other arithmetic  10.3 us (2%)
    pallas_call x30, Pallas kernels, run(): function(*[o if i in loose or spec.memory_space == pltpu.SMEM else pltpu....  263 us
    ppermute x18, waiting for transfers between devices, step(): outer = lax.ppermute(payload, 'head', way)  79.1 us
    ppermute x18, starting transfers between devices, step(): outer = lax.ppermute(payload, 'head', way)  56.4 us
    unnamed x105, local copies, waits for them, and re-layouts  28.1 us
    pallas_call x25, Pallas kernels, in_vmem(): pl.pallas_call(kernel, name=name, in_specs=[pl.BlockSpec(memory_space=plt...  22.5 us
    ppermute x6, waiting for transfers between devices, scan_states(): got = lax.ppermute(sent, 'seq', [(i, i ^ bit) for i in range(n)])  22.3 us
    ppermute x16, starting transfers between devices, step(): middle = lax.ppermute(pair, 'head', self.MIDDLE)  16.9 us
  transfers between devices with their start and end apart: 47, of which 15 were waited for; matrix products, arithmetic and copies ran while one was open for 3% of the time, Pallas kernels for 49%

profile of v12, /device:TPU:0, one launch (start us, length us, event | category | flops | bytes accessed | tf_op | source)
XLA Modules:
  0.0 535.7 jit_solution(15339443553638540009)
XLA Ops:
  7.2 14.9 %project.1 = (bf16[1024,2048]{1,0:T(8,128)(2,1)}, bf16[1024,512]{1,0:T(8,128)(2,1)}, bf16[1024,512]{1,0:T(8,128)(2,1)}, f32[1024,64]{1,0:T(8,128)}, f32[1024,64]...) custom-call(bf16[1024,2048]{1,0:T(8,128)(2,1)} %bitcast.35, ...), custom_call_target="tpu_custom_call" | custom-call | flops 4563402752 | bytes 16777216 | tf_op jit(solution)/shard_map/project/pallas_call | solution.py:62
  24.2 2.7 pad_maximum_fusion
  27.2 2.9 collective-permute-start.1
  30.1 7.3 %collective-permute-done.1.refs_2_ = bf16[2,64,1152]{2,1,0:T(8,128)(2,1)S(1)} collective-permute-done((bf16[2,64,1152]{2,1,0:T(8,128)(2,1)S(1)}, bf16[2,64,1152]{2,1,0:T(8,128)(2,1)S(1)}, u32[]{:S(2)}, u32[]{:S(2)}) %collective-permute-start.1) | collective-permute-done | bytes 294944 | tf_op jit(solution)/shard_map/ppermute | solution.py:521
  39.5 6.7 %query.1.q_ref = bf16[1024,512]{1,0:T(8,128)(2,1)} custom-call(bf16[1024,2048]{1,0:T(8,128)(2,1)} %get-tuple-element.715.xn_ref.refs_0_, bf16[2048,512]{1,0:T(8,128)(2,1)} %wq_ref.9), custom_call_target="tpu_custom_call" | custom-call | flops 2147483648 | bytes 7340032 | tf_op jit(solution)/shard_map/query/pallas_call | solution.py:62
  46.2 5.8 %collective-permute-done.2.refs_2_ = bf16[2,64,1152]{2,1,0:T(8,128)(2,1)S(1)} collective-permute-done((bf16[2,64,1152]{2,1,0:T(8,128)(2,1)S(1)}, bf16[2,64,1152]{2,1,0:T(8,128)(2,1)S(1)}, u32[]{:S(2)}, u32[]{:S(2)}) %collective-permute-start.2) | collective-permute-done | bytes 294944 | tf_op jit(solution)/shard_map/ppermute | solution.py:521
  52.3 5.3 read.4
  57.6 3.8 collective-permute-start.3
  61.5 5.3 read.5
  66.8 13.5 %collective-permute-done.3.refs_1_ = bf16[256,2048]{1,0:T(8,128)(2,1)S(1)} collective-permute-done((bf16[256,2048]{1,0:T(8,128)(2,1)S(1)}, bf16[256,2048]{1,0:T(8,128)(2,1)S(1)}, u32[]{:S(2)}, u32[]{:S(2)}) %collective-permute-start.3) | collective-permute-done | bytes 1048608 | tf_op jit(solution)/shard_map/ppermute | solution.py:601
  80.4 4.5 collective-permute-start.4
  85.6 5.2 read.6
  90.9 12.5 %collective-permute-done.4.refs_1_ = bf16[256,2048]{1,0:T(8,128)(2,1)S(1)} collective-permute-done((bf16[256,2048]{1,0:T(8,128)(2,1)S(1)}, bf16[256,2048]{1,0:T(8,128)(2,1)S(1)}, u32[]{:S(2)}, u32[]{:S(2)}) %collective-permute-start.4) | collective-permute-done | bytes 1048608 | tf_op jit(solution)/shard_map/ppermute | solution.py:601
  103.5 3.9 collective-permute-start.6
  108.2 5.4 %read.7 = (bf16[256,512]{1,0:T(8,128)(2,1)}, f32[256,64]{1,0:T(8,128)}, f32[256,64]{1,0:T(8,128)}, f32[2,64,1024]{2,1,0:T(8,128)}, f32[1,64,1024]{2,1,0:T(8,128)}, /*index=5*/bf16[256,2048]{1,0:T(8,128)(2,1)S(1)}) custom-call(bf16[1024,512]{1,0:T(8,128)(2,1)} %query.1.q_ref, bf16[1024,512]{1,0:T(8,128)(2,1)} %get-tuple-element.399.k_ref, ...), custom_call_target="tpu_custom_call" | custom-call | flops 694157312 | bytes 4194304 | tf_op jit(solution)/shard_map/read/pallas_call | solution.py:62
  113.5 12.0 %collective-permute-done.6.refs_1_ = bf16[256,2048]{1,0:T(8,128)(2,1)S(1)} collective-permute-done((bf16[256,2048]{1,0:T(8,128)(2,1)S(1)}, bf16[256,2048]{1,0:T(8,128)(2,1)S(1)}, u32[]{:S(2)}, u32[]{:S(2)}) %collective-permute-start.6) | collective-permute-done | bytes 1048608 | tf_op jit(solution)/shard_map/ppermute | solution.py:601
  126.8 3.9 collective-permute-start.8
  133.9 19.5 %feed.4 = (bf16[256,2048]{1,0:T(8,128)(2,1)}, bf16[256,2048]{1,0:T(8,128)(2,1)}, bf16[256,1408]{1,0:T(8,128)(2,1)}, bf16[256,1408]{1,0:T(8,128)(2,1)}, bf16[256,...) custom-call(bf16[1024,2048]{1,0:T(8,128)(2,1)} %bitcast.36, ...), custom_call_target="tpu_custom_call" | custom-call | flops 8858370048 | bytes 24641536 | tf_op jit(solution)/shard_map/feed/pallas_call | solution.py:62
  155.1 2.3 collective-permute-start.10
  158.6 19.5 %feed.5 = (bf16[256,2048]{1,0:T(8,128)(2,1)}, bf16[256,2048]{1,0:T(8,128)(2,1)}, bf16[256,1408]{1,0:T(8,128)(2,1)}, bf16[256,1408]{1,0:T(8,128)(2,1)}, bf16[256,...) custom-call(bf16[1024,2048]{1,0:T(8,128)(2,1)} %bitcast.37, ...), custom_call_target="tpu_custom_call" | custom-call | flops 8858370048 | bytes 24641536 | tf_op jit(solution)/shard_map/feed/pallas_call | solution.py:62
  178.3 3.0 collective-permute-start.12
  182.2 19.4 %feed.6 = (bf16[256,2048]{1,0:T(8,128)(2,1)}, bf16[256,2048]{1,0:T(8,128)(2,1)}, bf16[256,1408]{1,0:T(8,128)(2,1)}, bf16[256,1408]{1,0:T(8,128)(2,1)}, bf16[256,...) custom-call(bf16[1024,2048]{1,0:T(8,128)(2,1)} %bitcast.38, ...), custom_call_target="tpu_custom_call" | custom-call | flops 8858370048 | bytes 24641536 | tf_op jit(solution)/shard_map/feed/pallas_call | solution.py:62
  204.9 19.5 %feed.7 = (bf16[256,2048]{1,0:T(8,128)(2,1)}, bf16[256,2048]{1,0:T(8,128)(2,1)}, bf16[256,1408]{1,0:T(8,128)(2,1)}, bf16[256,1408]{1,0:T(8,128)(2,1)}, bf16[256,...) custom-call(bf16[1024,2048]{1,0:T(8,128)(2,1)} %bitcast.39, ...), custom_call_target="tpu_custom_call" | custom-call | flops 8858370048 | bytes 24641536 | tf_op jit(solution)/shard_map/feed/pallas_call | solution.py:62
  225.9 2.7 collective-permute-start.16
  230.3 19.0 %wide_grads.1 = bf16[8,2,256,1408]{3,2,1,0:T(8,128)(2,1)} custom-call(bf16[256,2048]{1,0:T(8,128)(2,1)} %get-tuple-element.545.refs_0_, bf16[256,2048]{1,0:T(8,128)(2,1)} %get-tuple-element.546.refs_1_, bf16[256,2048]{1,0:T(8,128)(2,1)} %get-tuple-element.547.refs_2_, bf16[256,2048]{1,0:T(8,128)(2,1)} %get-tuple-element.548.refs_3_, ...), custom_call_target="tpu_custom_call" | custom-call | flops 11811160064 | bytes 21495808 | tf_op jit(solution)/shard_map/wide_grads/pallas_call | solution.py:62
  249.4 2.3 join.25
  257.2 8.4 %back.4 = (bf16[256,2048]{1,0:T(8,128)(2,1)}, bf16[256,512]{1,0:T(8,128)(2,1)}, f32[256,512]{1,0:T(8,128)}, f32[256,512]{1,0:T(8,128)}, f32[256,64]{1,0:T(8,128)...) custom-call(bf16[256,2048]{1,0:T(8,128)(2,1)S(1)} %get-tuple-element, ...), custom_call_target="tpu_custom_call" | custom-call | flops 930086912 | bytes 9961472 | tf_op jit(solution)/shard_map/back/pallas_call | solution.py:62
  265.7 9.6 %back.5 = (bf16[256,2048]{1,0:T(8,128)(2,1)}, bf16[256,512]{1,0:T(8,128)(2,1)}, f32[256,512]{1,0:T(8,128)}, f32[256,512]{1,0:T(8,128)}, f32[256,64]{1,0:T(8,128)...) custom-call(bf16[256,2048]{1,0:T(8,128)(2,1)S(1)} %copy-done.15, ...), custom_call_target="tpu_custom_call" | custom-call | flops 930086912 | bytes 9961472 | tf_op jit(solution)/shard_map/back/pallas_call | solution.py:62
  275.5 3.9 collective-permute-start.20
  280.1 8.2 %back.6 = (bf16[256,2048]{1,0:T(8,128)(2,1)}, bf16[256,512]{1,0:T(8,128)(2,1)}, f32[256,512]{1,0:T(8,128)}, f32[256,512]{1,0:T(8,128)}, f32[256,64]{1,0:T(8,128)...) custom-call(bf16[256,2048]{1,0:T(8,128)(2,1)S(1)} %get-tuple-element, ...), custom_call_target="tpu_custom_call" | custom-call | flops 930086912 | bytes 9961472 | tf_op jit(solution)/shard_map/back/pallas_call | solution.py:62
  288.4 10.8 %down_grads.1.refs_13_ = bf16[8,256,2432]{2,1,0:T(8,128)(2,1)} custom-call(bf16[1024,2048]{1,0:T(8,128)(2,1)} %bitcast.55, bf16[256,1408]{1,0:T(8,128)(2,1)} %get-tuple-element.599.refs_1_, bf16[256,1408]{1,0:T(8,128)(2,1)} %get-tuple-element.600.refs_2_, bf16[256,1408]{1,0:T(8,128)(2,1)} %get-tuple-element.601.refs_3_, ...), custom_call_target="tpu_custom_call" | custom-call | flops 5905580032 | bytes 12845056 | tf_op jit(solution)/shard_map/down_grads/pallas_call | solution.py:62
  299.3 4.0 collective-permute-start.23
  304.0 8.3 %back.7 = (bf16[256,2048]{1,0:T(8,128)(2,1)}, bf16[256,512]{1,0:T(8,128)(2,1)}, f32[256,512]{1,0:T(8,128)}, f32[256,512]{1,0:T(8,128)}, f32[256,64]{1,0:T(8,128)...) custom-call(bf16[256,2048]{1,0:T(8,128)(2,1)S(1)} %get-tuple-element, ...), custom_call_target="tpu_custom_call" | custom-call | flops 930086912 | bytes 9961472 | tf_op jit(solution)/shard_map/back/pallas_call | solution.py:62
  321.7 3.8 collective-permute-start.25
  327.3 9.3 %query_grads.1 = bf16[8,256,2432]{2,1,0:T(8,128)(2,1)} custom-call(bf16[1024,2048]{1,0:T(8,128)(2,1)} %get-tuple-element.715.xn_ref.refs_0_, bf16[256,2048]{1,0:T(8,128)(2,1)} %get-tuple-element.633.refs_1_.dhid_ref, bf16[256,2048]{1,0:T(8,128)(2,1)} %get-tuple-element.634.refs_2_.dhid_ref, ...), custom_call_target="tpu_custom_call", output_to_operand_aliasing={{}: (13, {})} | custom-call | flops 12884901888 | bytes 44040192 | tf_op jit(solution)/shard_map/query_grads/pallas_call | solution.py:62
  338.6 3.4 collective-permute-start.28
  341.9 6.4 %collective-permute-done.28.refs_2_ = bf16[2,64,1152]{2,1,0:T(8,128)(2,1)S(1)} collective-permute-done((bf16[2,64,1152]{2,1,0:T(8,128)(2,1)S(1)}, bf16[2,64,1152]{2,1,0:T(8,128)(2,1)S(1)}, u32[]{:S(2)}, u32[]{:S(2)}) %collective-permute-start.28) | collective-permute-done | bytes 294944 | tf_op jit(solution)/shard_map/ppermute | solution.py:521
  349.5 8.1 %last.4 = (bf16[256,512]{1,0:T(8,128)(2,1)}, bf16[256,512]{1,0:T(8,128)(2,1)}, bf16[256,64]{1,0:T(8,128)(2,1)}, bf16[256,2048]{1,0:T(8,128)(2,1)S(1)}, f32[8,64]{1,0:T(8,128)}, /*index=5*/f32[8,2048]{1,0:T(8,128)}) custom-call(f32[4,64,1024]{2,1,0:T(8,128)S(1)} %hop.11.l0_ref, bf16[1024,512]{1,0:T(8,128)(2,1)} %get-tuple-element.399.k_ref, ...), custom_call_target="tpu_custom_call" | custom-call | flops 1677721600 | bytes 13107200 | tf_op jit(solution)/shard_map/last/pallas_call | solution.py:62
  357.6 3.7 join.29
  365.7 9.0 %last.6 = (bf16[256,512]{1,0:T(8,128)(2,1)}, bf16[256,512]{1,0:T(8,128)(2,1)}, bf16[256,64]{1,0:T(8,128)(2,1)}, bf16[256,2048]{1,0:T(8,128)(2,1)S(1)}, f32[8,64]{1,0:T(8,128)}, /*index=5*/f32[8,2048]{1,0:T(8,128)}) custom-call(f32[4,64,1024]{2,1,0:T(8,128)S(1)} %hop.11.l0_ref, bf16[1024,512]{1,0:T(8,128)(2,1)} %get-tuple-element.399.k_ref, ...), custom_call_target="tpu_custom_call" | custom-call | flops 1677721600 | bytes 13107200 | tf_op jit(solution)/shard_map/last/pallas_call | solution.py:62
  374.7 9.8 %last.5 = (bf16[256,512]{1,0:T(8,128)(2,1)}, bf16[256,512]{1,0:T(8,128)(2,1)}, bf16[256,64]{1,0:T(8,128)(2,1)}, bf16[256,2048]{1,0:T(8,128)(2,1)S(1)}, f32[8,64]{1,0:T(8,128)}, /*index=5*/f32[8,2048]{1,0:T(8,128)}) custom-call(f32[4,64,1024]{2,1,0:T(8,128)S(1)} %hop.11.l0_ref, bf16[1024,512]{1,0:T(8,128)(2,1)} %get-tuple-element.399.k_ref, ...), custom_call_target="tpu_custom_call" | custom-call | flops 1677721600 | bytes 13107200 | tf_op jit(solution)/shard_map/last/pallas_call | solution.py:62
  384.5 2.7 collective-permute-done.29.refs_1_
  387.3 3.0 join.30
  391.3 4.9 collective-permute-start.31
  397.8 8.1 %last.7 = (bf16[256,512]{1,0:T(8,128)(2,1)}, bf16[256,512]{1,0:T(8,128)(2,1)}, bf16[256,64]{1,0:T(8,128)(2,1)}, bf16[256,2048]{1,0:T(8,128)(2,1)S(1)}, f32[8,64]{1,0:T(8,128)}, /*index=5*/f32[8,2048]{1,0:T(8,128)}) custom-call(f32[4,64,1024]{2,1,0:T(8,128)S(1)} %hop.11.l0_ref, bf16[1024,512]{1,0:T(8,128)(2,1)} %get-tuple-element.399.k_ref, ...), custom_call_target="tpu_custom_call" | custom-call | flops 1677721600 | bytes 13107200 | tf_op jit(solution)/shard_map/last/pallas_call | solution.py:62
  405.9 11.8 %state_grads.1 = bf16[8,272,1152]{2,1,0:T(8,128)(2,1)} custom-call(bf16[1024,2048]{1,0:T(8,128)(2,1)} %get-tuple-element.715.xn_ref.refs_0_, bf16[256,512]{1,0:T(8,128)(2,1)} %get-tuple-element.716.refs_1_, bf16[256,512]{1,0:T(8,128)(2,1)} %get-tuple-element.717.refs_2_, bf16[256,512]{1,0:T(8,128)(2,1)} %get-tuple-element.718.refs_3_, ...), custom_call_target="tpu_custom_call" | custom-call | flops 4294967296 | bytes 10485760 | tf_op jit(solution)/shard_map/state_grads/pallas_call | solution.py:62
  417.9 2.6 join.31
  423.4 3.8 collective-permute-start.33
  427.9 2.1 out.4.refs_0_
  430.1 2.3 out.5.refs_0_
  432.4 15.5 %collective-permute-done.33.refs_1_ = bf16[256,2048]{1,0:T(8,128)(2,1)S(1)} collective-permute-done((bf16[256,2048]{1,0:T(8,128)(2,1)}, bf16[256,2048]{1,0:T(8,128)(2,1)S(1)}, u32[]{:S(2)}, u32[]{:S(2)}) %collective-permute-start.33) | collective-permute-done | bytes 1048608 | tf_op jit(solution)/shard_map/ppermute | solution.py:601
  450.1 3.9 collective-permute-start.35
  456.1 3.2 in_grad.4.refs_0_
  459.4 2.3 out.6.refs_0_
  461.6 2.2 out.7
  463.8 9.9 %collective-permute-done.35.refs_1_ = bf16[256,2048]{1,0:T(8,128)(2,1)S(1)} collective-permute-done((bf16[256,2048]{1,0:T(8,128)(2,1)}, bf16[256,2048]{1,0:T(8,128)(2,1)S(1)}, u32[]{:S(2)}, u32[]{:S(2)}) %collective-permute-start.35) | collective-permute-done | bytes 1048608 | tf_op jit(solution)/shard_map/ppermute | solution.py:601
  481.2 2.9 copy.48
  485.4 3.3 in_grad.5.refs_0_
  488.7 11.3 %collective-permute-done.37.refs_0_ = bf16[256,2048]{1,0:T(8,128)(2,1)S(1)} collective-permute-done((bf16[256,2048]{1,0:T(8,128)(2,1)}, bf16[256,2048]{1,0:T(8,128)(2,1)S(1)}, u32[]{:S(2)}, u32[]{:S(2)}) %collective-permute-start.37) | collective-permute-done | bytes 1048608 | tf_op jit(solution)/shard_map/ppermute | solution.py:601
  503.5 2.2 slice_convert_fusion
  509.2 3.6 collective-permute-start.41
  517.5 3.2 in_grad.6.refs_0_
  520.7 4.4 collective-permute-done.40
  525.7 3.2 in_grad.7
  (205 shorter events, 78.8 us)
Async XLA Ops:
  7.2 125.5 %all-gather.3.cloned.1.call-start = ((), (), s32[]{:S(2)}) async-start(), calls=%async_computation.6 | async-start | bytes 19464192 | tf_op jit(solution)/shard_map/all_gather | solution.py:686
  7.2 16.6 %copy-start.49 = (bf16[1408,256]{1,0:T(8,128)(2,1)S(1)}, bf16[1408,256]{1,0:T(8,128)(2,1)}, u32[]{:S(2)}) copy-start(bf16[1408,256]{1,0:T(8,128)(2,1)} %param.24) | copy-start | bytes 2162692
  7.2 16.9 %copy-start.50 = (bf16[256,1408]{1,0:T(8,128)(2,1)S(1)}, bf16[256,1408]{1,0:T(8,128)(2,1)}, u32[]{:S(2)}) copy-start(bf16[256,1408]{1,0:T(8,128)(2,1)} %param.23) | copy-start | bytes 2162692
  22.1 1.7 collective-permute-start
  26.9 336.3 %reduce-scatter.4.cloned.1.call-start = ((), (), s32[]{:S(2)}) async-start(), calls=%async_computation.3 | async-start | bytes 12976128 | tf_op jit(solution)/shard_map/reduce_scatter | solution.py:902
  27.2 10.2 %collective-permute-start.1 = (bf16[2,64,1152]{2,1,0:T(8,128)(2,1)S(1)}, bf16[2,64,1152]{2,1,0:T(8,128)(2,1)S(1)}, u32[]{:S(2)}, u32[]{:S(2)}) collective-permute-start(bf16[2,64,1152]{2,1,0:T(8,128)(2,1)S(1)} %get-tuple-element.408), channel_id=1, source_target_pairs={{0,8},{4,12},{8,0},{12,4},{16,24},{20,28},{24,16},{28,20},{1,9},{5... | collective-permute-start | bytes 884744 | tf_op jit(solution)/shard_map/ppermute | solution.py:521
  37.7 14.3 %collective-permute-start.2 = (bf16[2,64,1152]{2,1,0:T(8,128)(2,1)S(1)}, bf16[2,64,1152]{2,1,0:T(8,128)(2,1)S(1)}, u32[]{:S(2)}, u32[]{:S(2)}) collective-permute-start(bf16[2,64,1152]{2,1,0:T(8,128)(2,1)S(1)} %get-tuple-element.413), channel_id=1, source_target_pairs={{0,16},{4,20},{8,24},{12,28},{16,0},{20,4},{24,8},{28,12},{1,17},{... | collective-permute-start | bytes 884744 | tf_op jit(solution)/shard_map/ppermute | solution.py:521
  57.6 22.7 %collective-permute-start.3 = (bf16[256,2048]{1,0:T(8,128)(2,1)S(1)}, bf16[256,2048]{1,0:T(8,128)(2,1)S(1)}, u32[]{:S(2)}, u32[]{:S(2)}) collective-permute-start(bf16[256,2048]{1,0:T(8,128)(2,1)S(1)} %get-tuple-element.420.refs_0_), channel_id=1, source_target_pairs={{0,1},{3,2},{4,5},{7,6},{8,9},{11,10},{12,13},{15,14},{16,17},{19,... | collective-permute-start | bytes 3145736 | tf_op jit(solution)/shard_map/ppermute | solution.py:601
  80.4 23.0 %collective-permute-start.4 = (bf16[256,2048]{1,0:T(8,128)(2,1)S(1)}, bf16[256,2048]{1,0:T(8,128)(2,1)S(1)}, u32[]{:S(2)}, u32[]{:S(2)}) collective-permute-start(bf16[256,2048]{1,0:T(8,128)(2,1)S(1)} %get-tuple-element.424), channel_id=1, source_target_pairs={{0,1},{3,2},{4,5},{7,6},{8,9},{11,10},{12,13},{15,14},{16,17},{19,... | collective-permute-start | bytes 3145736 | tf_op jit(solution)/shard_map/ppermute | solution.py:601
  84.9 18.5 %collective-permute-start.5 = (bf16[256,2048]{1,0:T(8,128)(2,1)S(1)}, bf16[256,2048]{1,0:T(8,128)(2,1)S(1)}, u32[]{:S(2)}, u32[]{:S(2)}) collective-permute-start(bf16[256,2048]{1,0:T(8,128)(2,1)S(1)} %get-tuple-element.425.refs_2_), channel_id=1, source_target_pairs={{1,2},{2,1},{5,6},{6,5},{9,10},{10,9},{13,14},{14,13},{17,18},{18,... | collective-permute-start | bytes 3145736 | tf_op jit(solution)/shard_map/ppermute | solution.py:604
  103.5 22.1 %collective-permute-start.6 = (bf16[256,2048]{1,0:T(8,128)(2,1)S(1)}, bf16[256,2048]{1,0:T(8,128)(2,1)S(1)}, u32[]{:S(2)}, u32[]{:S(2)}) collective-permute-start(bf16[256,2048]{1,0:T(8,128)(2,1)S(1)} %get-tuple-element.433.refs_4_), channel_id=1, source_target_pairs={{0,1},{3,2},{1,0},{2,3},{4,5},{7,6},{5,4},{6,7},{8,9},{11,10},{9,8... | collective-permute-start | bytes 3145736 | tf_op jit(solution)/shard_map/ppermute | solution.py:601
  107.4 18.1 %collective-permute-start.7 = (bf16[256,2048]{1,0:T(8,128)(2,1)S(1)}, bf16[256,2048]{1,0:T(8,128)(2,1)S(1)}, u32[]{:S(2)}, u32[]{:S(2)}) collective-permute-start(bf16[256,2048]{1,0:T(8,128)(2,1)S(1)} %get-tuple-element.434.refs_2_), channel_id=1, source_target_pairs={{1,2},{2,1},{5,6},{6,5},{9,10},{10,9},{13,14},{14,13},{17,18},{18,... | collective-permute-start | bytes 3145736 | tf_op jit(solution)/shard_map/ppermute | solution.py:604
  126.8 26.6 %collective-permute-start.8 = (bf16[256,2048]{1,0:T(8,128)(2,1)S(1)}, bf16[256,2048]{1,0:T(8,128)(2,1)}, u32[]{:S(2)}, u32[]{:S(2)}) collective-permute-start(bf16[256,2048]{1,0:T(8,128)(2,1)S(1)} %get-tuple-element.438.refs_4_), channel_id=1, source_target_pairs={{0,1},{3,2},{1,0},{2,3},{4,5},{7,6},{5,4},{6,7},{8,9},{11,10},{9,8... | collective-permute-start | bytes 3145736 | tf_op jit(solution)/shard_map/ppermute | solution.py:601
  130.7 22.7 %collective-permute-start.9 = (bf16[256,2048]{1,0:T(8,128)(2,1)S(1)}, bf16[256,2048]{1,0:T(8,128)(2,1)}, u32[]{:S(2)}, u32[]{:S(2)}) collective-permute-start(bf16[256,2048]{1,0:T(8,128)(2,1)S(1)} %get-tuple-element.439.refs_2_), channel_id=1, source_target_pairs={{1,2},{2,1},{5,6},{6,5},{9,10},{10,9},{13,14},{14,13},{17,18},{18,... | collective-permute-start | bytes 3145736 | tf_op jit(solution)/shard_map/ppermute | solution.py:604
  155.1 23.0 %collective-permute-start.10 = (bf16[256,2048]{1,0:T(8,128)(2,1)S(1)}, bf16[256,2048]{1,0:T(8,128)(2,1)S(1)}, u32[]{:S(2)}, u32[]{:S(2)}) collective-permute-start(bf16[256,2048]{1,0:T(8,128)(2,1)S(1)} %get-tuple-element.455.refs_4_), channel_id=1, source_target_pairs={{0,1},{3,2},{1,0},{2,3},{4,5},{7,6},{5,4},{6,7},{8,9},{11,10},{9,8... | collective-permute-start | bytes 3145736 | tf_op jit(solution)/shard_map/ppermute | solution.py:601
  157.4 20.7 %collective-permute-start.11 = (bf16[256,2048]{1,0:T(8,128)(2,1)S(1)}, bf16[256,2048]{1,0:T(8,128)(2,1)S(1)}, u32[]{:S(2)}, u32[]{:S(2)}) collective-permute-start(bf16[256,2048]{1,0:T(8,128)(2,1)S(1)} %get-tuple-element.456.refs_2_), channel_id=1, source_target_pairs={{1,2},{2,1},{5,6},{6,5},{9,10},{10,9},{13,14},{14,13},{17,18},{18,... | collective-permute-start | bytes 3145736 | tf_op jit(solution)/shard_map/ppermute | solution.py:604
  178.3 23.3 %collective-permute-start.12 = (bf16[256,2048]{1,0:T(8,128)(2,1)S(1)}, bf16[256,2048]{1,0:T(8,128)(2,1)S(1)}, u32[]{:S(2)}, u32[]{:S(2)}) collective-permute-start(bf16[256,2048]{1,0:T(8,128)(2,1)S(1)} %get-tuple-element.472.refs_4_), channel_id=1, source_target_pairs={{0,1},{3,2},{1,0},{2,3},{4,5},{7,6},{5,4},{6,7},{8,9},{11,10},{9,8... | collective-permute-start | bytes 3145736 | tf_op jit(solution)/shard_map/ppermute | solution.py:601
  181.3 20.4 %collective-permute-start.13 = (bf16[256,2048]{1,0:T(8,128)(2,1)S(1)}, bf16[256,2048]{1,0:T(8,128)(2,1)S(1)}, u32[]{:S(2)}, u32[]{:S(2)}) collective-permute-start(bf16[256,2048]{1,0:T(8,128)(2,1)S(1)} %get-tuple-element.473.refs_2_), channel_id=1, source_target_pairs={{1,2},{2,1},{5,6},{6,5},{9,10},{10,9},{13,14},{14,13},{17,18},{18,... | collective-permute-start | bytes 3145736 | tf_op jit(solution)/shard_map/ppermute | solution.py:604
  201.8 22.6 %collective-permute-start.14 = (bf16[256,2048]{1,0:T(8,128)(2,1)S(1)}, bf16[256,2048]{1,0:T(8,128)(2,1)S(1)}, u32[]{:S(2)}, u32[]{:S(2)}) collective-permute-start(bf16[256,2048]{1,0:T(8,128)(2,1)S(1)} %get-tuple-element.499.refs_4_), channel_id=1, source_target_pairs={{0,1},{3,2},{1,0},{2,3},{4,5},{7,6},{5,4},{6,7},{8,9},{11,10},{9,8... | collective-permute-start | bytes 3145736 | tf_op jit(solution)/shard_map/ppermute | solution.py:601
  204.0 20.4 %collective-permute-start.15 = (bf16[256,2048]{1,0:T(8,128)(2,1)S(1)}, bf16[256,2048]{1,0:T(8,128)(2,1)S(1)}, u32[]{:S(2)}, u32[]{:S(2)}) collective-permute-start(bf16[256,2048]{1,0:T(8,128)(2,1)S(1)} %get-tuple-element.500.refs_2_), channel_id=1, source_target_pairs={{1,2},{2,1},{5,6},{6,5},{9,10},{10,9},{13,14},{14,13},{17,18},{18,... | collective-permute-start | bytes 3145736 | tf_op jit(solution)/shard_map/ppermute | solution.py:604
  225.9 23.5 %copy-start.3 = (bf16[256,2048]{1,0:T(8,128)(2,1)S(1)}, bf16[256,2048]{1,0:T(8,128)(2,1)}, u32[]{:S(2)}) copy-start(bf16[256,2048]{1,0:T(8,128)(2,1)} %get-tuple-element.530.refs_5_.refs_0_) | copy-start | bytes 3145732
  225.9 23.4 %collective-permute-start.16 = (bf16[256,2048]{1,0:T(8,128)(2,1)}, bf16[256,2048]{1,0:T(8,128)(2,1)}, u32[]{:S(2)}, u32[]{:S(2)}) collective-permute-start(bf16[256,2048]{1,0:T(8,128)(2,1)} %get-tuple-element.528.refs_4_), channel_id=1, source_target_pairs={{0,1},{3,2},{1,0},{2,3},{4,5},{7,6},{5,4},{6,7},{8,9},{11,10},{9,8... | collective-permute-start | bytes 3145736 | tf_op jit(solution)/shard_map/ppermute | solution.py:601
  228.6 20.7 %collective-permute-start.17 = (bf16[256,2048]{1,0:T(8,128)(2,1)}, bf16[256,2048]{1,0:T(8,128)(2,1)}, u32[]{:S(2)}, u32[]{:S(2)}) collective-permute-start(bf16[256,2048]{1,0:T(8,128)(2,1)} %get-tuple-element.529.refs_2_), channel_id=1, source_target_pairs={{1,2},{2,1},{5,6},{6,5},{9,10},{10,9},{13,14},{14,13},{17,18},{18,... | collective-permute-start | bytes 3145736 | tf_op jit(solution)/shard_map/ppermute | solution.py:604
  254.7 195.3 %reduce-scatter.6.cloned.1.call-start = ((), (), s32[]{:S(2)}) async-start(), calls=%async_computation.4 | async-start | bytes 11206656 | tf_op jit(solution)/shard_map/reduce_scatter | solution.py:957
  254.8 20.5 %collective-permute-start.18 = (bf16[256,2048]{1,0:T(8,128)(2,1)}, bf16[256,2048]{1,0:T(8,128)(2,1)S(1)}, u32[]{:S(2)}, u32[]{:S(2)}) collective-permute-start(bf16[256,2048]{1,0:T(8,128)(2,1)} %copy-done.24), channel_id=1, source_target_pairs={{0,1},{3,2},{1,0},{2,3},{4,5},{7,6},{5,4},{6,7},{8,9},{11,10},{9,8... | collective-permute-start | bytes 3145736 | tf_op jit(solution)/shard_map/ppermute | solution.py:601
  256.1 19.2 %collective-permute-start.19 = (bf16[256,2048]{1,0:T(8,128)(2,1)S(1)}, bf16[256,2048]{1,0:T(8,128)(2,1)S(1)}, u32[]{:S(2)}, u32[]{:S(2)}) collective-permute-start(bf16[256,2048]{1,0:T(8,128)(2,1)S(1)} %copy-done.23), channel_id=1, source_target_pairs={{1,2},{2,1},{5,6},{6,5},{9,10},{10,9},{13,14},{14,13},{17,18},{18,... | collective-permute-start | bytes 3145736 | tf_op jit(solution)/shard_map/ppermute | solution.py:604
  257.2 8.4 %copy-start.15 = (bf16[256,2048]{1,0:T(8,128)(2,1)S(1)}, bf16[256,2048]{1,0:T(8,128)(2,1)}, u32[]{:S(2)}) copy-start(bf16[256,2048]{1,0:T(8,128)(2,1)} %copy-done.14) | copy-start | bytes 3145732
  265.7 9.6 %copy-start.2 = (bf16[256,2048]{1,0:T(8,128)(2,1)S(1)}, bf16[256,2048]{1,0:T(8,128)(2,1)}, u32[]{:S(2)}) copy-start(bf16[256,2048]{1,0:T(8,128)(2,1)} %get-tuple-element.558.refs_5_.refs_0_) | copy-start | bytes 3145732
  265.7 9.6 %copy-start.25 = (bf16[256,2048]{1,0:T(8,128)(2,1)S(1)}, bf16[256,2048]{1,0:T(8,128)(2,1)}, u32[]{:S(2)}) copy-start(bf16[256,2048]{1,0:T(8,128)(2,1)} %copy-done.24) | copy-start | bytes 3145732
  275.5 23.6 %collective-permute-start.20 = (bf16[256,2048]{1,0:T(8,128)(2,1)S(1)}, bf16[256,2048]{1,0:T(8,128)(2,1)S(1)}, u32[]{:S(2)}, u32[]{:S(2)}) collective-permute-start(bf16[256,2048]{1,0:T(8,128)(2,1)S(1)} %get-tuple-element.584.refs_4_), channel_id=1, source_target_pairs={{0,1},{3,2},{1,0},{2,3},{4,5},{7,6},{5,4},{6,7},{8,9},{11,10},{9,8... | collective-permute-start | bytes 3145736 | tf_op jit(solution)/shard_map/ppermute | solution.py:601
  279.4 19.7 %collective-permute-start.21 = (bf16[256,2048]{1,0:T(8,128)(2,1)S(1)}, bf16[256,2048]{1,0:T(8,128)(2,1)S(1)}, u32[]{:S(2)}, u32[]{:S(2)}) collective-permute-start(bf16[256,2048]{1,0:T(8,128)(2,1)S(1)} %get-tuple-element.585.refs_2_), channel_id=1, source_target_pairs={{1,2},{2,1},{5,6},{6,5},{9,10},{10,9},{13,14},{14,13},{17,18},{18,... | collective-permute-start | bytes 3145736 | tf_op jit(solution)/shard_map/ppermute | solution.py:604
  288.3 10.8 %copy-start.1 = (bf16[256,2048]{1,0:T(8,128)(2,1)S(1)}, bf16[256,2048]{1,0:T(8,128)(2,1)}, u32[]{:S(2)}) copy-start(bf16[256,2048]{1,0:T(8,128)(2,1)} %get-tuple-element.586.refs_5_.refs_0_) | copy-start | bytes 3145732
  299.3 19.9 %collective-permute-start.23 = (bf16[256,2048]{1,0:T(8,128)(2,1)S(1)}, bf16[256,2048]{1,0:T(8,128)(2,1)S(1)}, u32[]{:S(2)}, u32[]{:S(2)}) collective-permute-start(bf16[256,2048]{1,0:T(8,128)(2,1)S(1)} %get-tuple-element.617.refs_4_), channel_id=1, source_target_pairs={{0,1},{3,2},{1,0},{2,3},{4,5},{7,6},{5,4},{6,7},{8,9},{11,10},{9,8... | collective-permute-start | bytes 3145736 | tf_op jit(solution)/shard_map/ppermute | solution.py:601
  303.3 15.9 %collective-permute-start.24 = (bf16[256,2048]{1,0:T(8,128)(2,1)S(1)}, bf16[256,2048]{1,0:T(8,128)(2,1)S(1)}, u32[]{:S(2)}, u32[]{:S(2)}) collective-permute-start(bf16[256,2048]{1,0:T(8,128)(2,1)S(1)} %get-tuple-element.618.refs_2_), channel_id=1, source_target_pairs={{1,2},{2,1},{5,6},{6,5},{9,10},{10,9},{13,14},{14,13},{17,18},{18,... | collective-permute-start | bytes 3145736 | tf_op jit(solution)/shard_map/ppermute | solution.py:604
  312.5 1.6 collective-permute-start.22
  316.3 20.3 %collective-permute-start.27 = (bf16[2,64,1152]{2,1,0:T(8,128)(2,1)}, bf16[2,64,1152]{2,1,0:T(8,128)(2,1)S(1)}, u32[]{:S(2)}, u32[]{:S(2)}) collective-permute-start(bf16[2,64,1152]{2,1,0:T(8,128)(2,1)} %get-tuple-element.648), channel_id=1, source_target_pairs={{0,8},{4,12},{8,0},{12,4},{16,24},{20,28},{24,16},{28,20},{1,9},{5... | collective-permute-start | bytes 884744 | tf_op jit(solution)/shard_map/ppermute | solution.py:521
  321.7 35.9 %collective-permute-start.25 = (bf16[256,2048]{1,0:T(8,128)(2,1)}, bf16[256,2048]{1,0:T(8,128)(2,1)}, u32[]{:S(2)}, u32[]{:S(2)}) collective-permute-start(bf16[256,2048]{1,0:T(8,128)(2,1)} %get-tuple-element.626.refs_4_), channel_id=1, source_target_pairs={{0,1},{3,2},{1,0},{2,3},{4,5},{7,6},{5,4},{6,7},{8,9},{11,10},{9,8... | collective-permute-start | bytes 3145736 | tf_op jit(solution)/shard_map/ppermute | solution.py:601
  325.5 32.1 %collective-permute-start.26 = (bf16[256,2048]{1,0:T(8,128)(2,1)}, bf16[256,2048]{1,0:T(8,128)(2,1)}, u32[]{:S(2)}, u32[]{:S(2)}) collective-permute-start(bf16[256,2048]{1,0:T(8,128)(2,1)} %get-tuple-element.627.refs_2_), channel_id=1, source_target_pairs={{1,2},{2,1},{5,6},{6,5},{9,10},{10,9},{13,14},{14,13},{17,18},{18,... | collective-permute-start | bytes 3145736 | tf_op jit(solution)/shard_map/ppermute | solution.py:604
  338.6 9.8 %collective-permute-start.28 = (bf16[2,64,1152]{2,1,0:T(8,128)(2,1)S(1)}, bf16[2,64,1152]{2,1,0:T(8,128)(2,1)S(1)}, u32[]{:S(2)}, u32[]{:S(2)}) collective-permute-start(bf16[2,64,1152]{2,1,0:T(8,128)(2,1)S(1)} %get-tuple-element.653), channel_id=1, source_target_pairs={{0,16},{4,20},{8,24},{12,28},{16,0},{20,4},{24,8},{28,12},{1,17},{... | collective-permute-start | bytes 884744 | tf_op jit(solution)/shard_map/ppermute | solution.py:521
  363.3 142.4 %reduce-scatter.8.cloned.1.call-start = ((), (), s32[]{:S(2)}) async-start(), calls=%async_computation.5 | async-start | bytes 5640192 | tf_op jit(solution)/shard_map/reduce_scatter | solution.py:977
  363.3 24.0 %collective-permute-start.29 = (bf16[256,2048]{1,0:T(8,128)(2,1)}, bf16[256,2048]{1,0:T(8,128)(2,1)S(1)}, u32[]{:S(2)}, u32[]{:S(2)}) collective-permute-start(bf16[256,2048]{1,0:T(8,128)(2,1)} %get-tuple-element.679.refs_4_), channel_id=1, source_target_pairs={{0,1},{3,2},{1,0},{2,3},{4,5},{7,6},{5,4},{6,7},{8,9},{11,10},{9,8... | collective-permute-start | bytes 3145736 | tf_op jit(solution)/shard_map/ppermute | solution.py:601
  365.0 22.3 %collective-permute-start.30 = (bf16[256,2048]{1,0:T(8,128)(2,1)}, bf16[256,2048]{1,0:T(8,128)(2,1)S(1)}, u32[]{:S(2)}, u32[]{:S(2)}) collective-permute-start(bf16[256,2048]{1,0:T(8,128)(2,1)} %get-tuple-element.680.refs_2_), channel_id=1, source_target_pairs={{1,2},{2,1},{5,6},{6,5},{9,10},{10,9},{13,14},{14,13},{17,18},{18,... | collective-permute-start | bytes 3145736 | tf_op jit(solution)/shard_map/ppermute | solution.py:604
  374.7 12.6 %copy-start.7 = (bf16[256,2048]{1,0:T(8,128)(2,1)S(1)}, bf16[256,2048]{1,0:T(8,128)(2,1)}, u32[]{:S(2)}) copy-start(bf16[256,2048]{1,0:T(8,128)(2,1)} %copy-done.6) | copy-start | bytes 3145732
  391.3 26.6 %collective-permute-start.31 = (bf16[256,2048]{1,0:T(8,128)(2,1)}, bf16[256,2048]{1,0:T(8,128)(2,1)}, u32[]{:S(2)}, u32[]{:S(2)}) collective-permute-start(bf16[256,2048]{1,0:T(8,128)(2,1)} %get-tuple-element.696.refs_4_), channel_id=1, source_target_pairs={{0,1},{3,2},{1,0},{2,3},{4,5},{7,6},{5,4},{6,7},{8,9},{11,10},{9,8... | collective-permute-start | bytes 3145736 | tf_op jit(solution)/shard_map/ppermute | solution.py:601
  396.1 21.7 %collective-permute-start.32 = (bf16[256,2048]{1,0:T(8,128)(2,1)}, bf16[256,2048]{1,0:T(8,128)(2,1)}, u32[]{:S(2)}, u32[]{:S(2)}) collective-permute-start(bf16[256,2048]{1,0:T(8,128)(2,1)} %get-tuple-element.697.refs_2_), channel_id=1, source_target_pairs={{1,2},{2,1},{5,6},{6,5},{9,10},{10,9},{13,14},{14,13},{17,18},{18,... | collective-permute-start | bytes 3145736 | tf_op jit(solution)/shard_map/ppermute | solution.py:604
  405.9 11.9 %copy-start.5 = (bf16[256,2048]{1,0:T(8,128)(2,1)S(1)}, bf16[256,2048]{1,0:T(8,128)(2,1)}, u32[]{:S(2)}) copy-start(bf16[256,2048]{1,0:T(8,128)(2,1)} %copy-done.4) | copy-start | bytes 3145732
  423.4 24.5 %collective-permute-start.33 = (bf16[256,2048]{1,0:T(8,128)(2,1)}, bf16[256,2048]{1,0:T(8,128)(2,1)S(1)}, u32[]{:S(2)}, u32[]{:S(2)}) collective-permute-start(bf16[256,2048]{1,0:T(8,128)(2,1)} %copy-done.28), channel_id=1, source_target_pairs={{0,1},{3,2},{1,0},{2,3},{4,5},{7,6},{5,4},{6,7},{8,9},{11,10},{9,8... | collective-permute-start | bytes 3145736 | tf_op jit(solution)/shard_map/ppermute | solution.py:601
  427.2 20.7 %collective-permute-start.34 = (bf16[256,2048]{1,0:T(8,128)(2,1)}, bf16[256,2048]{1,0:T(8,128)(2,1)S(1)}, u32[]{:S(2)}, u32[]{:S(2)}) collective-permute-start(bf16[256,2048]{1,0:T(8,128)(2,1)} %copy-done.26), channel_id=1, source_target_pairs={{1,2},{2,1},{5,6},{6,5},{9,10},{10,9},{13,14},{14,13},{17,18},{18,... | collective-permute-start | bytes 3145736 | tf_op jit(solution)/shard_map/ppermute | solution.py:604
  430.1 17.8 %copy-start.27 = (bf16[256,2048]{1,0:T(8,128)(2,1)S(1)}, bf16[256,2048]{1,0:T(8,128)(2,1)}, u32[]{:S(2)}) copy-start(bf16[256,2048]{1,0:T(8,128)(2,1)} %copy-done.26) | copy-start | bytes 3145732
  430.1 17.8 %copy-start.29 = (bf16[256,2048]{1,0:T(8,128)(2,1)S(1)}, bf16[256,2048]{1,0:T(8,128)(2,1)}, u32[]{:S(2)}) copy-start(bf16[256,2048]{1,0:T(8,128)(2,1)} %copy-done.28) | copy-start | bytes 3145732
  450.1 9.3 %copy-start.11 = (bf16[256,2048]{1,0:T(8,128)(2,1)S(1)}, bf16[256,2048]{1,0:T(8,128)(2,1)}, u32[]{:S(2)}) copy-start(bf16[256,2048]{1,0:T(8,128)(2,1)} %copy-done.10) | copy-start | bytes 3145732
  450.1 23.7 %collective-permute-start.35 = (bf16[256,2048]{1,0:T(8,128)(2,1)}, bf16[256,2048]{1,0:T(8,128)(2,1)S(1)}, u32[]{:S(2)}, u32[]{:S(2)}) collective-permute-start(bf16[256,2048]{1,0:T(8,128)(2,1)} %copy-done.16), channel_id=1, source_target_pairs={{0,1},{3,2},{1,0},{2,3},{4,5},{7,6},{5,4},{6,7},{8,9},{11,10},{9,8... | collective-permute-start | bytes 3145736 | tf_op jit(solution)/shard_map/ppermute | solution.py:601
  454.0 19.8 %collective-permute-start.36 = (bf16[256,2048]{1,0:T(8,128)(2,1)S(1)}, bf16[256,2048]{1,0:T(8,128)(2,1)S(1)}, u32[]{:S(2)}, u32[]{:S(2)}) collective-permute-start(bf16[256,2048]{1,0:T(8,128)(2,1)S(1)} %get-tuple-element.757.refs_2_), channel_id=1, source_target_pairs={{1,2},{2,1},{5,6},{6,5},{9,10},{10,9},{13,14},{14,13},{17,18},{18,... | collective-permute-start | bytes 3145736 | tf_op jit(solution)/shard_map/ppermute | solution.py:604
  461.6 12.1 %copy-start.17 = (bf16[256,2048]{1,0:T(8,128)(2,1)S(1)}, bf16[256,2048]{1,0:T(8,128)(2,1)}, u32[]{:S(2)}) copy-start(bf16[256,2048]{1,0:T(8,128)(2,1)} %copy-done.16) | copy-start | bytes 3145732
  463.8 14.3 %copy-start.47 = (bf16[1,2,256,1408]{3,2,1,0:T(8,128)(2,1)S(1)}, bf16[1,2,256,1408]{3,2,1,0:T(8,128)(2,1)}, u32[]{:S(2)}) copy-start(bf16[1,2,256,1408]{3,2,1,0:T(8,128)(2,1)} %reduce-scatter.4.cloned.1.call-done) | copy-start | bytes 4325380
  475.9 24.0 %collective-permute-start.37 = (bf16[256,2048]{1,0:T(8,128)(2,1)}, bf16[256,2048]{1,0:T(8,128)(2,1)S(1)}, u32[]{:S(2)}, u32[]{:S(2)}) collective-permute-start(bf16[256,2048]{1,0:T(8,128)(2,1)} %get-tuple-element.767.refs_3_), channel_id=1, source_target_pairs={{1,0},{2,3},{5,4},{6,7},{9,8},{10,11},{13,12},{14,15},{17,16},{18,... | collective-permute-start | bytes 3145736 | tf_op jit(solution)/shard_map/ppermute | solution.py:601
  477.5 22.5 %collective-permute-start.38 = (bf16[256,2048]{1,0:T(8,128)(2,1)S(1)}, bf16[256,2048]{1,0:T(8,128)(2,1)S(1)}, u32[]{:S(2)}, u32[]{:S(2)}) collective-permute-start(bf16[256,2048]{1,0:T(8,128)(2,1)S(1)} %get-tuple-element.768.refs_1_), channel_id=1, source_target_pairs={{1,2},{2,1},{5,6},{6,5},{9,10},{10,9},{13,14},{14,13},{17,18},{18,... | collective-permute-start | bytes 3145736 | tf_op jit(solution)/shard_map/ppermute | solution.py:604
  485.4 14.5 %copy-start.31 = (bf16[256,2048]{1,0:T(8,128)(2,1)S(1)}, bf16[256,2048]{1,0:T(8,128)(2,1)}, u32[]{:S(2)}) copy-start(bf16[256,2048]{1,0:T(8,128)(2,1)} %copy-done.30) | copy-start | bytes 3145732
  502.2 23.4 %collective-permute-start.39 = (bf16[256,2048]{1,0:T(8,128)(2,1)S(1)}, bf16[256,2048]{1,0:T(8,128)(2,1)S(1)}, u32[]{:S(2)}, u32[]{:S(2)}) collective-permute-start(bf16[256,2048]{1,0:T(8,128)(2,1)S(1)} %get-tuple-element.775.refs_1_), channel_id=1, source_target_pairs={{1,0},{2,3},{5,4},{6,7},{9,8},{10,11},{13,12},{14,15},{17,16},{18,... | collective-permute-start | bytes 3145736 | tf_op jit(solution)/shard_map/ppermute | solution.py:601
  505.7 7.2 %copy-start.46 = (f32[256,1024]{1,0:T(8,128)S(1)}, f32[256,1024]{1,0:T(8,128)}, u32[]{:S(2)}) copy-start(f32[256,1024]{1,0:T(8,128)} %slice_convert_fusion) | copy-start | bytes 3145732
  507.7 9.8 %copy-start.33 = (bf16[256,2048]{1,0:T(8,128)(2,1)S(1)}, bf16[256,2048]{1,0:T(8,128)(2,1)}, u32[]{:S(2)}) copy-start(bf16[256,2048]{1,0:T(8,128)(2,1)} %copy-done.32) | copy-start | bytes 3145732
  507.7 13.0 %collective-permute-start.42 = (f32[256]{0:T(256)S(1)}, f32[256]{0:T(256)S(1)}, u32[]{:S(2)}, u32[]{:S(2)}) collective-permute-start(f32[256]{0:T(256)S(1)} %get-tuple-element.823), channel_id=1, source_target_pairs={{0,3},{1,2},{2,1},{3,0},{4,7},{5,6},{6,5},{7,4},{8,11},{9,10},{10,... | collective-permute-start | bytes 3080 | tf_op jit(solution)/shard_map/ppermute | solution.py:998
  509.2 11.5 %collective-permute-start.41 = (f32[256]{0:T(256)S(1)}, f32[256]{0:T(256)S(1)}, u32[]{:S(2)}, u32[]{:S(2)}) collective-permute-start(f32[256]{0:T(256)S(1)} %get-tuple-element.823), channel_id=1, source_target_pairs={{0,2},{1,3},{2,0},{3,1},{4,6},{5,7},{6,4},{7,5},{8,10},{9,11},{10,... | collective-permute-start | bytes 3080 | tf_op jit(solution)/shard_map/ppermute | solution.py:998
  512.9 12.2 %collective-permute-start.40 = (f32[256]{0:T(256)S(1)}, f32[256]{0:T(256)S(1)}, u32[]{:S(2)}, u32[]{:S(2)}) collective-permute-start(f32[256]{0:T(256)S(1)} %get-tuple-element.823), channel_id=1, source_target_pairs={{0,1},{1,0},{2,3},{3,2},{4,5},{5,4},{6,7},{7,6},{8,9},{9,8},{10,11... | collective-permute-start | bytes 3080 | tf_op jit(solution)/shard_map/ppermute | solution.py:998
  (34 other events, 74.1 us)
Sparse Core Ops, SparseCore 0:
  27.0 100.2 all-gather.2
  254.9 89.7 reduce-scatter.3
  363.4 78.9 reduce-scatter.5
  445.7 55.6 reduce-scatter.7
